TPU v7x, 32 devices: a whole 2x2x4 slice. The times are simulated.
32 devices in a mesh: member: 4 (over y, core), space: 8 (over z, x).
Axes of the slice: x: 2, y: 2, z: 4, core: 2. Of those that a mesh axis runs over, the one named last changes fastest.
Arguments:
- ensemble: float32 [96, 4, 64, 4, 256], P('member', None, 'space'), may hold values from 0 to 2
- diffusivity: float32 [64, 4, 256], P('space'), may hold values from 0.03 to 0.16
- binding: float32 [64, 4, 256], P('space'), may hold values from 0.02 to 0.2
- source: float32 [64, 4, 256], P('space'), may hold values from 0.005 to 0.05
- obs_index: int32 [4, 2048], replicated, may hold values from 0 to 8191
- owner: int32 [4], replicated, may hold values from 0 to 7
- observed: float32 [4, 2048], replicated, may hold values from -6 to 6
- obs_var: float32 [4, 2048], replicated, may hold values from 0.5 to 2
Outputs:
- analysis: float32 [96, 4, 64, 4, 256], P('member', None, 'space')
Inputs may be any that keep to these rules, and one draw needn't show every extreme that they name: owner holds space indices of devices.
All inputs are finite; a program needn't handle non-finite values.
Results may differ from a plain program's by a relative error of at most 0.0003.
Values sent between devices are 32-bit elements; how exact they have to be, the bound alone decides.
No kernel may reach another device: no remote copies, remote signals or barrier semaphores. Data moves between devices by JAX's collectives and lax.ppermute only.
A program may use at most 64 MiB of HBM per device.

v0:
```python
import jax
import jax.numpy as jnp
from jax import lax
from jax.sharding import PartitionSpec as P

SUBSTEPS = 6
BATCHES = 4
NEWTON = 16


unbind_rate = 0.05
uptake_rate = 0.1
recycle_rate = 0.02
highest = lax.Precision.HIGHEST


def padded_2(block, sides, width):
    for axis, dim in sides:
        count = lax.axis_size(axis)
        forward = [(i, i + 1) for i in range(count - 1)]
        backward = [(target, source) for source, target in forward]
        low = lax.ppermute(
            lax.slice_in_dim(block, block.shape[dim] - width, None, axis=dim), axis, forward
        )
        high = lax.ppermute(lax.slice_in_dim(block, 0, width, axis=dim), axis, backward)
        block = jnp.concatenate([low, block, high], axis=dim)
    return block


def spread_2(x, axis, root):
    mine = lax.axis_index(axis) == root
    return lax.psum(jnp.where(mine, x, jnp.zeros_like(x)), axis)


def react(free, receptor, complexed, internal, neighbours, diffusivity, binding, source):
    binding_flux = binding * free * receptor
    updated_unbound = (
        free
        + diffusivity * (neighbours - 6.0 * free)
        - binding_flux
        + unbind_rate * complexed
        + source
    )
    new_receptor = receptor - binding_flux + unbind_rate * complexed + recycle_rate * internal
    updated_bound_complex = complexed + binding_flux - (unbind_rate + uptake_rate) * complexed
    new_internal = internal + uptake_rate * complexed - recycle_rate * internal
    return jnp.stack([updated_unbound, new_receptor, updated_bound_complex, new_internal], axis=-4)


def transform(priors, observed, obs_var):
    members = priors.shape[1]
    identity_k = jnp.eye(members, dtype=priors.dtype)
    mean_prior = jnp.mean(priors, axis=1)
    spread = priors - mean_prior[:, None]
    weight_applied = spread / obs_var[:, None]
    system = identity_k + jnp.dot(spread.T, weight_applied, precision=highest) / (members - 1)
    frobenius = jnp.sqrt(jnp.sum(system * system))

    def newton(iteration, iterates):
        scaled_root, inverse_root = iterates
        factor = 1.5 * identity_k - 0.5 * jnp.dot(inverse_root, scaled_root, precision=highest)
        return (
            jnp.dot(scaled_root, factor, precision=highest),
            jnp.dot(factor, inverse_root, precision=highest),
        )

    scaled_root, inverse_root = lax.fori_loop(0, NEWTON, newton, (system / frobenius, identity_k))
    root_inv = inverse_root / jnp.sqrt(frobenius)
    innovation = jnp.dot(observed - mean_prior, weight_applied, precision=highest) / (members - 1)
    mean_weight = jnp.dot(
        root_inv, jnp.dot(root_inv, innovation, precision=highest), precision=highest
    )
    average = jnp.full((members, members), 1.0 / members, dtype=priors.dtype)
    return (
        jnp.dot(identity_k - average, root_inv + mean_weight[:, None], precision=highest) + average
    )


def advance(present_fields, diffusivity, binding, source):
    free = present_fields[:, 0]
    padded = padded_2(free, (("space", 1),), 1)
    plane_pad = jnp.pad(free, ((0, 0), (0, 0), (1, 1), (1, 1)))
    neighbours = padded[:, 2:] + padded[:, :-2]
    neighbours = neighbours + plane_pad[:, :, 2:, 1:-1] + plane_pad[:, :, :-2, 1:-1]
    neighbours = neighbours + plane_pad[:, :, 1:-1, 2:] + plane_pad[:, :, 1:-1, :-2]
    return react(
        free,
        present_fields[:, 1],
        present_fields[:, 2],
        present_fields[:, 3],
        neighbours,
        diffusivity,
        binding,
        source,
    )


def observe(present_fields, obs_index, owner, which_batch):
    local_count = present_fields.shape[0]
    totals = (present_fields[:, 2] + present_fields[:, 3]).reshape(local_count, -1)
    values = jnp.take(totals, obs_index[which_batch], axis=1).T
    values = spread_2(values, "space", owner[which_batch])
    return lax.all_gather(values, "member", axis=1, tiled=True)


def make_mixer(mixing_matrix, pieces):
    mixed = jnp.einsum("jk,jsry->ksry", mixing_matrix, pieces, precision=highest)
    return lax.all_to_all(mixed, "member", split_axis=0, concat_axis=2, tiled=True)


def local(ensemble, diffusivity, binding, source, obs_index, owner, observed, obs_var):
    present_fields = ensemble
    for substep in range(SUBSTEPS):
        present_fields = advance(present_fields, diffusivity, binding, source)
    local_count = present_fields.shape[0]
    species = present_fields.shape[1]
    width_y = present_fields.shape[4]
    for which_batch in range(BATCHES):
        priors = observe(present_fields, obs_index, owner, which_batch)
        mixing_matrix = transform(priors, observed[which_batch], obs_var[which_batch])
        row_state = present_fields.reshape(local_count, species, -1, width_y)
        blended_state = make_mixer(
            mixing_matrix,
            lax.all_to_all(row_state, "member", split_axis=2, concat_axis=0, tiled=True),
        )
        present_fields = blended_state.reshape(ensemble.shape)
    return present_fields


def solution(mesh):
    in_specs = (
        P("member", None, "space", None, None),
        P("space", None, None),
        P("space", None, None),
        P("space", None, None),
        P(),
        P(),
        P(),
        P(),
    )
    out_specs = P("member", None, "space", None, None)
    return jax.shard_map(local, mesh=mesh, in_specs=in_specs, out_specs=out_specs, check_vma=False)
```

profile of v0, /device:TPU:0, one launch (start us, length us, event | category | flops | bytes accessed | tf_op | source)
XLA Modules:
  0.0 805.4 jit_solution(2384413947980698470)
XLA Ops:
  8.0 4.8 collective-permute-start.1
  16.1 3.3 collective-permute-done
  19.4 2.7 fusion.101
  22.2 4.4 collective-permute-start.3
  29.7 3.3 collective-permute-done.2
  35.2 3.4 collective-permute-start.5
  41.8 3.3 collective-permute-done.4
  45.1 3.1 fusion.99
  49.9 4.3 collective-permute-start.7
  56.7 4.2 collective-permute-done.6
  60.9 6.3 fusion.98
  67.2 3.4 collective-permute-start.9
  72.8 4.3 collective-permute-done.8
  77.2 3.8 fusion.97
  81.8 4.4 collective-permute-start.11
  89.0 3.8 collective-permute-done.10
  92.7 5.8 fusion.96
  98.6 2.7 fusion.147
  101.3 2.7 copy.85
  104.0 7.6 gather_fusion
  123.7 4.2 pad_maximum_fusion
  127.9 3.8 all-to-all-start
  131.7 57.7 %all-reduce.11.cloned.1.call-done = f32[2048,24]{1,0:T(8,128)} async-done(((f32[2048,24]{1,0:T(8,128)}), f32[2048,24]{1,0:T(8,128)}) %all-reduce.11.cloned.1.call-update) | async-done | bytes 196624 | tf_op jit(solution)/shard_map/psum | solution.py:32
  190.9 9.5 %all_gather.12 = f32[2048,96]{0,1:T(8,128)} all-gather(f32[2048,24]{0,1:T(8,128)S(1)} %copy.86), channel_id=1, replica_groups=mesh['member'=4,'space'=8] {'member'}, dimensions={1}, use_global_device_ids=true | all-gather | bytes 983040 | tf_op jit(solution)/shard_map/all_gather | solution.py:103
  201.6 2.8 multiply_reduce_fusion.3
  205.2 11.6 %while.52 = (s32[]{:T(128)}, f32[96,96]{0,1:T(8,128)S(1)}, f32[96,96]{1,0:T(8,128)S(1)}, s32[]{:T(128)}) while((s32[]{:T(128)}, f32[96,96]{0,1:T(8,128)S(1)}, f32[96,96]{1,0:T(8,128)S(1)}, s32[]{:T(128)}) %tuple.147), condition=%wide.region_4.6_spmd.clone, body=%wide.region_3.5_spmd.clone.sunk | while | flops 31887360 | bytes 479285 | solution.py:67
  223.1 3.0 fusion.164
  226.1 3.5 copy.95
  229.6 3.7 all-to-all-start.1
  234.1 36.1 %all-to-all-done.1 = f32[96,4,8,256]{3,2,1,0:T(8,128)S(1)} async-done(((f32[96,4,8,256]{3,2,1,0:T(8,128)}), f32[96,4,8,256]{3,2,1,0:T(8,128)S(1)}, u32[]{:S(2)}, u32[]{:S(2)}) %all-to-all-start.1) | async-done | bytes 3145760 | tf_op jit(solution)/shard_map/all_to_all | solution.py:108
  273.0 3.6 copy.97
  276.6 9.8 %gather_fusion.1 = f32[2048,24]{1,0:T(8,128)} fusion(f32[24,8192]{0,1:T(8,128)} %bitcast.361, s32[2048]{0:T(1024)S(1)} %fusion.136), kind=kCustom, calls=%fused_computation.1.clone | custom fusion | bytes 401408 | tf_op jit(solution)/shard_map/jit(_take)/gather | solution.py:101
  289.5 3.7 copy.101
  293.2 3.8 all-to-all-start.2
  297.0 68.9 %all-reduce.13.cloned.1.call-done = f32[2048,24]{1,0:T(8,128)} async-done(((f32[2048,24]{1,0:T(8,128)}), f32[2048,24]{1,0:T(8,128)}) %all-reduce.13.cloned.1.call-update) | async-done | bytes 196624 | tf_op jit(solution)/shard_map/psum | solution.py:32
  367.4 9.0 %all_gather.13 = f32[2048,96]{0,1:T(8,128)} all-gather(f32[2048,24]{0,1:T(8,128)S(1)} %copy.98), channel_id=1, replica_groups=mesh['member'=4,'space'=8] {'member'}, dimensions={1}, use_global_device_ids=true | all-gather | bytes 983040 | tf_op jit(solution)/shard_map/all_gather | solution.py:103
  377.6 2.9 multiply_reduce_fusion.2
  381.3 11.6 %while.53 = (s32[]{:T(128)}, f32[96,96]{0,1:T(8,128)S(1)}, f32[96,96]{1,0:T(8,128)S(1)}, s32[]{:T(128)}) while((s32[]{:T(128)}, f32[96,96]{0,1:T(8,128)S(1)}, f32[96,96]{1,0:T(8,128)S(1)}, s32[]{:T(128)}) %tuple.148), condition=%wide.region_9.11_spmd.clone, body=%wide.region_8.10_spmd.clone.sunk | while | flops 31887360 | bytes 479285 | solution.py:67
  399.2 3.0 fusion.165
  402.2 3.5 copy.105
  405.7 3.7 all-to-all-start.3
  410.6 35.7 %all-to-all-done.3 = f32[96,4,8,256]{3,2,1,0:T(8,128)S(1)} async-done(((f32[96,4,8,256]{3,2,1,0:T(8,128)}), f32[96,4,8,256]{3,2,1,0:T(8,128)S(1)}, u32[]{:S(2)}, u32[]{:S(2)}) %all-to-all-start.3) | async-done | bytes 3145760 | tf_op jit(solution)/shard_map/all_to_all | solution.py:108
  449.1 3.6 copy.107
  452.7 9.8 %gather_fusion.2 = f32[2048,24]{1,0:T(8,128)} fusion(f32[24,8192]{0,1:T(8,128)} %bitcast.362, s32[2048]{0:T(1024)S(1)} %fusion.137), kind=kCustom, calls=%fused_computation.2.clone | custom fusion | bytes 401408 | tf_op jit(solution)/shard_map/jit(_take)/gather | solution.py:101
  465.6 3.7 copy.111
  469.3 3.8 all-to-all-start.4
  473.1 68.8 %all-reduce.15.cloned.1.call-done = f32[2048,24]{1,0:T(8,128)} async-done(((f32[2048,24]{1,0:T(8,128)}), f32[2048,24]{1,0:T(8,128)}) %all-reduce.15.cloned.1.call-update) | async-done | bytes 196624 | tf_op jit(solution)/shard_map/psum | solution.py:32
  543.4 9.0 %all_gather.14 = f32[2048,96]{0,1:T(8,128)} all-gather(f32[2048,24]{0,1:T(8,128)S(1)} %copy.108), channel_id=1, replica_groups=mesh['member'=4,'space'=8] {'member'}, dimensions={1}, use_global_device_ids=true | all-gather | bytes 983040 | tf_op jit(solution)/shard_map/all_gather | solution.py:103
  553.6 2.9 multiply_reduce_fusion.1
  557.3 11.6 %while.54 = (s32[]{:T(128)}, f32[96,96]{0,1:T(8,128)S(1)}, f32[96,96]{1,0:T(8,128)S(1)}, s32[]{:T(128)}) while((s32[]{:T(128)}, f32[96,96]{0,1:T(8,128)S(1)}, f32[96,96]{1,0:T(8,128)S(1)}, s32[]{:T(128)}) %tuple.149), condition=%wide.region_14.16_spmd.clone, body=%wide.region_13.15_spmd.clone.sunk | while | flops 31887360 | bytes 479285 | solution.py:67
  575.2 3.0 fusion.166
  578.2 3.5 copy.115
  581.7 3.7 all-to-all-start.5
  586.3 36.0 %all-to-all-done.5 = f32[96,4,8,256]{3,2,1,0:T(8,128)S(1)} async-done(((f32[96,4,8,256]{3,2,1,0:T(8,128)}), f32[96,4,8,256]{3,2,1,0:T(8,128)S(1)}, u32[]{:S(2)}, u32[]{:S(2)}) %all-to-all-start.5) | async-done | bytes 3145760 | tf_op jit(solution)/shard_map/all_to_all | solution.py:108
  625.1 3.6 copy.117
  628.7 9.8 %gather_fusion.3 = f32[2048,24]{1,0:T(8,128)} fusion(f32[24,8192]{0,1:T(8,128)} %bitcast.363, s32[2048]{0:T(1024)S(1)} %fusion.138), kind=kCustom, calls=%fused_computation.3.clone | custom fusion | bytes 401408 | tf_op jit(solution)/shard_map/jit(_take)/gather | solution.py:101
  641.5 3.7 copy.121
  645.2 3.8 all-to-all-start.6
  649.1 68.9 %all-reduce.17.cloned.1.call-done = f32[2048,24]{1,0:T(8,128)} async-done(((f32[2048,24]{1,0:T(8,128)}), f32[2048,24]{1,0:T(8,128)}) %all-reduce.17.cloned.1.call-update) | async-done | bytes 196624 | tf_op jit(solution)/shard_map/psum | solution.py:32
  719.6 9.0 %all_gather.15 = f32[2048,96]{0,1:T(8,128)} all-gather(f32[2048,24]{0,1:T(8,128)S(1)} %copy.118), channel_id=1, replica_groups=mesh['member'=4,'space'=8] {'member'}, dimensions={1}, use_global_device_ids=true | all-gather | bytes 983040 | tf_op jit(solution)/shard_map/all_gather | solution.py:103
  729.8 2.9 multiply_reduce_fusion
  733.4 11.6 %while.55 = (s32[]{:T(128)}, f32[96,96]{0,1:T(8,128)S(1)}, f32[96,96]{1,0:T(8,128)S(1)}, s32[]{:T(128)}) while((s32[]{:T(128)}, f32[96,96]{0,1:T(8,128)S(1)}, f32[96,96]{1,0:T(8,128)S(1)}, s32[]{:T(128)}) %tuple.146), condition=%wide.region_19.21_spmd.clone, body=%wide.region_18.20_spmd.clone.sunk | while | flops 31887360 | bytes 479285 | solution.py:67
  751.3 3.0 fusion.167
  756.2 39.4 %all_to_all.141 = f32[96,4,8,256]{3,2,1,0:T(8,128)S(1)} all-to-all(f32[96,4,8,256]{3,2,1,0:T(8,128)S(1)} %copy.125), channel_id=1, replica_groups=mesh['member'=4,'space'=8] {'member'}, dimensions={0} | all-to-all | bytes 6291456 | tf_op jit(solution)/shard_map/all_to_all | solution.py:108
  (491 shorter events, 137.1 us)
Async XLA Ops:
  6.5 26.5 %copy-start = (f32[24,4,8,4,256]{4,3,2,1,0:T(4,128)S(1)}, f32[24,4,8,4,256]{4,3,2,1,0:T(4,128)}, u32[]{:S(2)}) copy-start(f32[24,4,8,4,256]{4,3,2,1,0:T(4,128)} %param.18) | copy-start | bytes 9437188
  6.5 26.5 %copy-start.20 = (f32[8,4,256]{2,1,0:T(4,128)S(1)}, f32[8,4,256]{2,1,0:T(4,128)}, u32[]{:S(2)}) copy-start(f32[8,4,256]{2,1,0:T(4,128)} %param.21) | copy-start | bytes 98308
  6.5 26.5 %copy-start.21 = (f32[8,4,256]{2,1,0:T(4,128)S(1)}, f32[8,4,256]{2,1,0:T(4,128)}, u32[]{:S(2)}) copy-start(f32[8,4,256]{2,1,0:T(4,128)} %param.19) | copy-start | bytes 98308
  6.5 26.5 %copy-start.19 = (f32[8,4,256]{2,1,0:T(4,128)S(1)}, f32[8,4,256]{2,1,0:T(4,128)}, u32[]{:S(2)}) copy-start(f32[8,4,256]{2,1,0:T(4,128)} %param.20) | copy-start | bytes 98308
  6.5 21.3 %copy-start.22 = (f32[4,2048]{1,0:T(4,128)S(1)}, f32[4,2048]{1,0:T(4,128)}, u32[]{:S(2)}) copy-start(f32[4,2048]{1,0:T(4,128)} %param.25) | copy-start | bytes 98308
  6.5 182.9 %all-reduce.11.cloned.1.call-start = ((), (), s32[]{:S(2)}) async-start(), calls=%async_computation.8 | async-start | bytes 2097152 | tf_op jit(solution)/shard_map/psum | solution.py:32
  8.0 8.1 collective-permute-start.1
  12.9 6.5 collective-permute-start
  22.2 7.6 collective-permute-start.3
  26.5 6.5 collective-permute-start.2
  35.2 13.1 %copy-start.1 = (f32[24,8,4,256]{3,2,1,0:T(4,128)}, f32[24,8,4,256]{3,2,1,0:T(4,128)S(1)}, u32[]{:S(2)}) copy-start(f32[24,8,4,256]{3,2,1,0:T(4,128)S(1)} %get-tuple-element.220) | copy-start | bytes 2359300
  35.2 13.1 %copy-start.8 = (f32[24,8,4,256]{3,2,1,0:T(4,128)}, f32[24,8,4,256]{3,2,1,0:T(4,128)S(1)}, u32[]{:S(2)}) copy-start(f32[24,8,4,256]{3,2,1,0:T(4,128)S(1)} %get-tuple-element.218) | copy-start | bytes 2359300
  35.2 6.6 collective-permute-start.5
  38.6 6.5 collective-permute-start.4
  48.3 0.9 copy-start.5
  49.9 6.9 collective-permute-start.7
  54.2 6.7 collective-permute-start.6
  60.9 16.2 %copy-start.2 = (f32[24,8,4,256]{3,2,1,0:T(4,128)S(1)}, f32[24,8,4,256]{3,2,1,0:T(4,128)}, u32[]{:S(2)}) copy-start(f32[24,8,4,256]{3,2,1,0:T(4,128)} %copy-done.1) | copy-start | bytes 2359300
  60.9 16.2 %copy-start.6 = (f32[24,8,4,256]{3,2,1,0:T(4,128)S(1)}, f32[24,8,4,256]{3,2,1,0:T(4,128)}, u32[]{:S(2)}) copy-start(f32[24,8,4,256]{3,2,1,0:T(4,128)} %copy-done.5) | copy-start | bytes 2359300
  60.9 16.2 %copy-start.11 = (f32[24,8,4,256]{3,2,1,0:T(4,128)S(1)}, f32[24,8,4,256]{3,2,1,0:T(4,128)}, u32[]{:S(2)}) copy-start(f32[24,8,4,256]{3,2,1,0:T(4,128)} %get-tuple-element.217) | copy-start | bytes 2359300
  67.2 13.7 %copy-start.3 = (f32[24,8,4,256]{3,2,1,0:T(4,128)}, f32[24,8,4,256]{3,2,1,0:T(4,128)S(1)}, u32[]{:S(2)}) copy-start(f32[24,8,4,256]{3,2,1,0:T(4,128)S(1)} %get-tuple-element.214) | copy-start | bytes 2359300
  67.2 13.7 %copy-start.7 = (f32[24,8,4,256]{3,2,1,0:T(4,128)}, f32[24,8,4,256]{3,2,1,0:T(4,128)S(1)}, u32[]{:S(2)}) copy-start(f32[24,8,4,256]{3,2,1,0:T(4,128)S(1)} %get-tuple-element.212) | copy-start | bytes 2359300
  67.2 5.6 collective-permute-start.9
  70.7 6.5 collective-permute-start.8
  72.0 9.0 %copy-start.14 = (f32[96,96]{1,0:T(8,128)}, f32[96,96]{1,0:T(8,128)S(1)}, u32[]{:S(2)}) copy-start(f32[96,96]{1,0:T(8,128)S(1)} %fusion.126) | copy-start | bytes 110596
  77.2 10.5 %copy-start.23 = (s32[4]{0:T(128)S(1)}, s32[4]{0:T(128)}, u32[]{:S(2)}) copy-start(s32[4]{0:T(128)} %param.23) | copy-start | bytes 52
  81.0 0.9 copy-start.9
  81.8 7.1 collective-permute-start.11
  86.2 6.5 collective-permute-start.10
  92.7 5.8 copy-start.4
  92.7 5.9 copy-start.10
  92.7 5.9 copy-start.12
  92.7 5.9 copy-start.13
  101.3 10.3 %copy-start.28 = (pred[2048]{0:T(1024)(128)(4,1)S(1)}, pred[2048]{0:T(1024)(128)(4,1)}, u32[]{:S(2)}) copy-start(pred[2048]{0:T(1024)(128)(4,1)} %compare_and_fusion.3) | copy-start | bytes 6148
  127.9 73.8 %copy-start.27 = (f32[1,2048]{1,0:T(1,128)S(1)}, f32[1,2048]{1,0:T(1,128)}, u32[]{:S(2)}) copy-start(f32[1,2048]{1,0:T(1,128)} %get-tuple-element.236) | copy-start | bytes 24580
  127.9 91.5 %all-to-all-start = ((f32[24,4,32,256]{3,1,0,2:T(4,128)}), f32[24,4,32,256]{3,1,0,2:T(4,128)S(1)}, u32[]{:S(2)}, u32[]{:S(2)}) async-start(f32[24,4,32,256]{3,1,0,2:T(4,128)} %pad_maximum_fusion), calls=%async_computation | async-start | bytes 6291456 | tf_op jit(solution)/shard_map/all_to_all | solution.py:124
  131.7 73.5 %copy-start.16 = (f32[96,96]{1,0:T(8,128)S(1)}, f32[96,96]{1,0:T(8,128)}, u32[]{:S(2)}) copy-start(f32[96,96]{1,0:T(8,128)} %copy-done.14) | copy-start | bytes 110596
  229.6 40.6 %all-to-all-start.1 = ((f32[96,4,8,256]{3,2,1,0:T(8,128)}), f32[96,4,8,256]{3,2,1,0:T(8,128)S(1)}, u32[]{:S(2)}, u32[]{:S(2)}) async-start(f32[96,4,8,256]{3,2,1,0:T(8,128)} %copy.95), calls=%async_computation.1 | async-start | bytes 6291456 | tf_op jit(solution)/shard_map/all_to_all | solution.py:108
  233.3 132.6 %all-reduce.13.cloned.1.call-start = ((), (), s32[]{:S(2)}) async-start(), calls=%async_computation.9 | async-start | bytes 2097152 | tf_op jit(solution)/shard_map/psum | solution.py:32
  293.2 84.5 %copy-start.26 = (f32[1,2048]{1,0:T(1,128)S(1)}, f32[1,2048]{1,0:T(1,128)}, u32[]{:S(2)}) copy-start(f32[1,2048]{1,0:T(1,128)} %get-tuple-element.235) | copy-start | bytes 24580
  293.2 102.3 %all-to-all-start.2 = ((f32[24,4,32,256]{3,1,0,2:T(4,128)}), f32[24,4,32,256]{3,1,0,2:T(4,128)S(1)}, u32[]{:S(2)}, u32[]{:S(2)}) async-start(f32[24,4,32,256]{3,1,0,2:T(4,128)} %copy.101), calls=%async_computation.2 | async-start | bytes 6291456 | tf_op jit(solution)/shard_map/all_to_all | solution.py:124
  297.0 84.3 %copy-start.17 = (f32[96,96]{1,0:T(8,128)S(1)}, f32[96,96]{1,0:T(8,128)}, u32[]{:S(2)}) copy-start(f32[96,96]{1,0:T(8,128)} %copy-done.14) | copy-start | bytes 110596
  405.7 40.6 %all-to-all-start.3 = ((f32[96,4,8,256]{3,2,1,0:T(8,128)}), f32[96,4,8,256]{3,2,1,0:T(8,128)S(1)}, u32[]{:S(2)}, u32[]{:S(2)}) async-start(f32[96,4,8,256]{3,2,1,0:T(8,128)} %copy.105), calls=%async_computation.3 | async-start | bytes 6291456 | tf_op jit(solution)/shard_map/all_to_all | solution.py:108
  409.4 132.5 %all-reduce.15.cloned.1.call-start = ((), (), s32[]{:S(2)}) async-start(), calls=%async_computation.10 | async-start | bytes 2097152 | tf_op jit(solution)/shard_map/psum | solution.py:32
  469.3 84.4 %copy-start.25 = (f32[1,2048]{1,0:T(1,128)S(1)}, f32[1,2048]{1,0:T(1,128)}, u32[]{:S(2)}) copy-start(f32[1,2048]{1,0:T(1,128)} %get-tuple-element.237) | copy-start | bytes 24580
  469.3 102.2 %all-to-all-start.4 = ((f32[24,4,32,256]{3,1,0,2:T(4,128)}), f32[24,4,32,256]{3,1,0,2:T(4,128)S(1)}, u32[]{:S(2)}, u32[]{:S(2)}) async-start(f32[24,4,32,256]{3,1,0,2:T(4,128)} %copy.111), calls=%async_computation.4 | async-start | bytes 6291456 | tf_op jit(solution)/shard_map/all_to_all | solution.py:124
  473.1 84.1 %copy-start.18 = (f32[96,96]{1,0:T(8,128)S(1)}, f32[96,96]{1,0:T(8,128)}, u32[]{:S(2)}) copy-start(f32[96,96]{1,0:T(8,128)} %copy-done.14) | copy-start | bytes 110596
  581.7 40.6 %all-to-all-start.5 = ((f32[96,4,8,256]{3,2,1,0:T(8,128)}), f32[96,4,8,256]{3,2,1,0:T(8,128)S(1)}, u32[]{:S(2)}, u32[]{:S(2)}) async-start(f32[96,4,8,256]{3,2,1,0:T(8,128)} %copy.115), calls=%async_computation.5 | async-start | bytes 6291456 | tf_op jit(solution)/shard_map/all_to_all | solution.py:108
  585.4 132.7 %all-reduce.17.cloned.1.call-start = ((), (), s32[]{:S(2)}) async-start(), calls=%async_computation.11 | async-start | bytes 2097152 | tf_op jit(solution)/shard_map/psum | solution.py:32
  645.2 84.5 %copy-start.24 = (f32[1,2048]{1,0:T(1,128)S(1)}, f32[1,2048]{1,0:T(1,128)}, u32[]{:S(2)}) copy-start(f32[1,2048]{1,0:T(1,128)} %get-tuple-element.234) | copy-start | bytes 24580
  645.2 102.4 %all-to-all-start.6 = ((f32[24,4,32,256]{3,1,0,2:T(4,128)}), f32[24,4,32,256]{3,1,0,2:T(4,128)S(1)}, u32[]{:S(2)}, u32[]{:S(2)}) async-start(f32[24,4,32,256]{3,1,0,2:T(4,128)} %copy.121), calls=%async_computation.6 | async-start | bytes 6291456 | tf_op jit(solution)/shard_map/all_to_all | solution.py:124
  649.1 84.3 %copy-start.15 = (f32[96,96]{1,0:T(8,128)S(1)}, f32[96,96]{1,0:T(8,128)}, u32[]{:S(2)}) copy-start(f32[96,96]{1,0:T(8,128)} %copy-done.14) | copy-start | bytes 110596
Sparse Core Ops, SparseCore 0:
  113.1 76.2 all-reduce.10
  289.1 76.7 all-reduce.12
  465.2 76.6 all-reduce.14
  641.2 76.8 all-reduce.16
where the time goes:
time: 813 us; the launch traced here: 805 us
  waiting for transfers between devices  399 us (49%)
  local copies, waits for them, and re-layouts  123 us (15%)
  matrix products  76.2 us (9%)
  blocking collectives  76 us (9%)
  starting transfers between devices  60 us (7%)
  other arithmetic  48.1 us (6%)
  between operations  19.5 us (2%)
    psum x4, waiting for transfers between devices, spread_2(): return lax.psum(jnp.where(mine, x, jnp.zeros_like(x)), axis)  264 us
    all_to_all x3, waiting for transfers between devices, make_mixer(): lax.all_to_all(mixed, 'member', split_axis=0, concat_axis=2, tiled=True)  108 us
    all_to_all x1, blocking collectives, make_mixer(): lax.all_to_all(mixed, 'member', split_axis=0, concat_axis=2, tiled=True)  39.4 us
    gather x4, local copies, waits for them, and re-layouts, observe(): values = jnp.take(totals, obs_index[which_batch], axis=1).T  37.1 us
    all_gather x4, blocking collectives, observe(): return lax.all_gather(values, 'member', axis=1, tiled=True)  36.6 us
    ppermute x6, starting transfers between devices, padded_2(): lax.ppermute(lax.slice_in_dim(block, block.shape[dim] - width, None, axis...  24.7 us
    add x6, other arithmetic, react(): free + diffusivity * (neighbours - 6.0 * free) - binding_flux  23.8 us
    ppermute x6, waiting for transfers between devices, padded_2(): lax.ppermute(lax.slice_in_dim(block, 0, width, axis=dim), axis, backward)  22.2 us
  transfers between devices with their start and end apart: 23, of which 17 were waited for; matrix products, arithmetic and copies ran while one was open for 13% of the time, Pallas kernels for 0%

commit v1 on v0

v1 whole, which is shorter than its diff:
```python
import functools

import jax
import jax.numpy as jnp
from jax import lax
from jax.experimental import pallas as pl
from jax.experimental.pallas import tpu as pltpu
from jax.sharding import PartitionSpec as P

SUBSTEPS = 6
NEWTON = 16
LANES = 128

unbind_rate = 0.05
uptake_rate = 0.1
recycle_rate = 0.02

VMEM = pl.BlockSpec(memory_space=pltpu.VMEM)
SMEM = pl.BlockSpec(memory_space=pltpu.SMEM)
bf16 = jnp.bfloat16
f32 = jnp.float32


def split(x):
    high = x.astype(bf16)
    return high, (x - high.astype(f32)).astype(bf16)


def dot_parts(a, b, dims):
    a_high, a_low = a
    b_high, b_low = b
    mul = functools.partial(
        lax.dot_general, dimension_numbers=(dims, ((), ())), preferred_element_type=f32
    )
    return mul(a_high, b_high) + (mul(a_high, b_low) + mul(a_low, b_high))


def wide_left(x):
    return jnp.concatenate(split(x), axis=1)


def wide_right(x):
    both = jnp.concatenate(split(x), axis=1)
    return jnp.concatenate([both, both], axis=0)


def square_dot(left, right):
    out = jnp.dot(left, right, preferred_element_type=f32)
    side = out.shape[0]
    return out[:, :side] + out[:, side:]


NN = ((1,), (0,))
NT = ((1,), (1,))


def substep_kernel(
    a, r, c, i, low, high, diffusivity, binding, source, out_a, out_r, out_c, out_i, *edges, final
):
    nx, nz, members, ny = a.shape
    lane = lax.broadcasted_iota(jnp.int32, (members, ny), 1)
    at_left, at_right = lane == 0, lane == ny - 1

    def cell(x, z):
        free = a[x, z]
        neighbours = (low[z] if x == 0 else a[x - 1, z]) + (
            high[z] if x == nx - 1 else a[x + 1, z]
        )
        if z + 1 < nz:
            neighbours += a[x, z + 1]
        if z > 0:
            neighbours += a[x, z - 1]
        neighbours += jnp.where(at_right, 0.0, pltpu.roll(free, ny - 1, 1))
        neighbours += jnp.where(at_left, 0.0, pltpu.roll(free, 1, 1))
        receptor, complexed, internal = r[x, z], c[x, z], i[x, z]
        row = pl.ds(z, 1)
        flux = binding[x, row, :] * free * receptor
        back = unbind_rate * complexed - flux
        new_free = (
            free
            + diffusivity[x, row, :] * (neighbours - 6.0 * free)
            + back
            + source[x, row, :]
        )
        new_internal = internal + uptake_rate * complexed - recycle_rate * internal
        new_complexed = complexed + flux - (unbind_rate + uptake_rate) * complexed
        out_a[x, z] = new_free
        out_r[x, z] = receptor + back + recycle_rate * internal
        out_c[x, z] = new_complexed + new_internal if final else new_complexed
        out_i[x, z] = new_internal
        if not final and x == 0:
            edges[0][z] = new_free
        if not final and x == nx - 1:
            edges[1][z] = new_free

    for x in range(nx):
        for z in range(nz):
            cell(x, z)


def substep(fields, low, high, diffusivity, binding, source, final):
    nx, nz, members, ny = fields[0].shape
    whole = jax.ShapeDtypeStruct((nx, nz, members, ny), f32)
    plane = jax.ShapeDtypeStruct((nz, members, ny), f32)
    cells = nx * nz * members * ny
    return pl.pallas_call(
        functools.partial(substep_kernel, final=final),
        out_shape=[whole] * 4 + ([] if final else [plane] * 2),
        in_specs=[VMEM] * 9,
        out_specs=[VMEM] * (4 if final else 6),
        compiler_params=pltpu.CompilerParams(vmem_limit_bytes=48 * 2**20),
        cost_estimate=pl.CostEstimate(
            flops=30 * cells, bytes_accessed=32 * cells, transcendentals=0
        ),
        name="substep",
    )(*fields, low, high, diffusivity, binding, source)


def weights_kernel(place, owner, obs_index, observed, obs_var, omega, eta):
    count, rows, ny = omega.shape
    batch_size = obs_index.shape[1]
    for k in range(count):
        batch = place[0] * count + k
        mine = owner[batch] == place[1]
        line = pl.ds(batch, 1)
        voxel = obs_index[line, :]
        scale = jnp.where(mine, 1.0, 0.0) / obs_var[line, :]
        shift = ny.bit_length() - 1
        row = lax.shift_right_logical(voxel, shift)
        column = jnp.bitwise_and(voxel, ny - 1)
        at_row = lax.broadcasted_iota(jnp.int32, (rows, batch_size), 0) == row
        at_column = lax.broadcasted_iota(jnp.int32, (ny, batch_size), 0) == column
        both = jnp.concatenate(
            [jnp.where(at_row, scale, 0.0), jnp.where(at_row, scale * observed[line, :], 0.0)],
            axis=0,
        )
        one = both.astype(bf16)
        rest = both - one.astype(f32)
        two = rest.astype(bf16)
        three = (rest - two.astype(f32)).astype(bf16)
        columns = jnp.where(at_column, 1.0, 0.0).astype(bf16)
        sums = lax.dot_general(
            jnp.concatenate([one, two, three], axis=0),
            columns,
            (NT, ((), ())),
            preferred_element_type=f32,
        )
        sums = sums[: 2 * rows] + sums[2 * rows : 4 * rows] + sums[4 * rows :]
        omega[k] = sums[:rows]
        eta[k] = sums[rows:]


def voxel_weights(place, owner, obs_index, observed, obs_var, count, rows, ny):
    out = jax.ShapeDtypeStruct((count, rows, ny), f32)
    return pl.pallas_call(
        weights_kernel,
        out_shape=[out, out],
        in_specs=[SMEM, SMEM, VMEM, VMEM, VMEM],
        out_specs=[VMEM, VMEM],
        compiler_params=pltpu.CompilerParams(vmem_limit_bytes=32 * 2**20),
        name="voxel_weights",
    )(place, owner, obs_index, observed, obs_var)


def gram_kernel(place, owner, omega, eta, *refs, offsets):
    *sources, out, members_at = refs
    count = out.shape[0]
    nx, nz, rows, ny = sources[0].shape
    members = members_at.shape[0]
    for k in range(count):
        out[k] = jnp.zeros(out.shape[1:], f32)

        @pl.when(owner[place[0] * count + k] == place[1])
        def _(k=k):
            def tile(t, total):
                x, z = t // nz, t % nz
                for j, source in enumerate(sources):
                    start = pl.multiple_of(offsets(place[2], j), 8)
                    members_at[pl.ds(start, rows), :] = source[x, z]
                values = members_at[...]
                mean = jnp.sum(values, axis=0, keepdims=True) * (1.0 / members)
                spread = values - mean
                weight = omega[k, pl.ds(t, 1), :]
                shift = eta[k, pl.ds(t, 1), :] - weight * mean
                tail = lax.broadcasted_iota(jnp.int32, (LANES - members, ny), 0)
                weighted = jnp.concatenate(
                    [spread * weight, jnp.where(tail == 0, shift, 0.0)], axis=0
                )
                return total + dot_parts(split(spread), split(weighted), NT)

            out[k] = lax.fori_loop(0, nx * nz, tile, jnp.zeros(out.shape[1:], f32), unroll=4)


def gram(place, owner, omega, eta, sources, offsets):
    nx, nz, rows, ny = sources[0].shape
    members = rows * len(sources)
    count = omega.shape[0]
    return pl.pallas_call(
        functools.partial(gram_kernel, offsets=offsets),
        out_shape=jax.ShapeDtypeStruct((count, members, LANES), f32),
        in_specs=[SMEM, SMEM, VMEM, VMEM] + [VMEM] * len(sources),
        out_specs=VMEM,
        scratch_shapes=[pltpu.VMEM((members, ny), f32)],
        compiler_params=pltpu.CompilerParams(vmem_limit_bytes=32 * 2**20),
        name="gram",
    )(place, owner, omega, eta, *sources)


def batch_transform(extended, total, members):
    side = extended.shape[0]
    row = lax.broadcasted_iota(jnp.int32, (side, side), 0)
    column = lax.broadcasted_iota(jnp.int32, (side, side), 1)
    in_column = column < members
    inside = in_column & (row < members)
    last = column == members
    identity = jnp.where((row == column) & inside, 1.0, 0.0)
    matrix = jnp.where(in_column, extended, 0.0)

    mean = jnp.sum(total, axis=1, keepdims=True) * (1.0 / members)
    centred = jnp.where(in_column, total - mean, 0.0)
    product = square_dot(wide_left(matrix), wide_right(jnp.where(last, mean, centred)))
    product = jnp.where(last, extended - product, product)
    product = square_dot(wide_left(centred.T), wide_right(product)) * (1.0 / (members - 1))
    innovation = jnp.sum(jnp.where(last, product, 0.0), axis=1, keepdims=True)
    system = identity + jnp.where(in_column, product, 0.0)
    frobenius = jnp.sqrt(jnp.sum(jnp.sum(system * system, axis=1, keepdims=True), axis=0, keepdims=True))

    scaled_root = system / frobenius
    factor = 1.5 * identity - 0.5 * scaled_root
    scaled_root = square_dot(wide_left(scaled_root), wide_right(factor))
    inverse_root = factor

    def newton(iteration, iterates):
        scaled_root, inverse_root = iterates
        factor = 1.5 * identity - 0.5 * square_dot(
            wide_left(inverse_root), wide_right(scaled_root)
        )
        return (
            square_dot(wide_left(scaled_root), wide_right(factor)),
            square_dot(wide_left(factor), wide_right(inverse_root)),
        )

    scaled_root, inverse_root = lax.fori_loop(1, NEWTON, newton, (scaled_root, inverse_root))
    root_inv = inverse_root / jnp.sqrt(frobenius)
    mean_weight = jnp.sum(root_inv * innovation, axis=0, keepdims=True)
    mean_weight = jnp.sum(root_inv * mean_weight, axis=1, keepdims=True)
    mixing = jnp.where(inside, root_inv + mean_weight, 0.0)
    mixing = mixing - jnp.sum(mixing, axis=0, keepdims=True) * (1.0 / members)
    mixing = jnp.where(inside, mixing + 1.0 / members, 0.0)
    return square_dot(wide_left(total), wide_right(mixing))


def transform_kernel(place, mine, other, out, ordered, work, *, offsets, blocks, rows):
    count, members = mine.shape[0], mine.shape[1]
    half = place[0]
    for k in range(count):
        ordered[half * count + k] = mine[k]
        ordered[(1 - half) * count + k] = other[k]
    row = lax.broadcasted_iota(jnp.int32, (LANES, LANES), 0)
    column = lax.broadcasted_iota(jnp.int32, (LANES, LANES), 1)
    total = jnp.where((row == column) & (row < members), 1.0, 0.0)
    for batch in range(2 * count):
        extended = jnp.concatenate(
            [ordered[batch], jnp.zeros((LANES - members, LANES), f32)], axis=0
        )
        total = batch_transform(extended, total, members)
    work[...] = total
    if blocks == 1:
        out[...] = total.T
        return
    parts = [
        work[pl.ds(pl.multiple_of(offsets(place[2], j), 8), rows), :] for j in range(blocks)
    ]
    parts.append(jnp.zeros((LANES - members, LANES), f32))
    work[...] = jnp.concatenate(parts, axis=0).T
    out[...] = work[pl.ds(pl.multiple_of(offsets(place[2], 0), 8), rows), :]


def transforms(place, mine, other, offsets, blocks, rows):
    count, members, _ = mine.shape
    shape = (LANES, LANES) if blocks == 1 else (rows, LANES)
    return pl.pallas_call(
        functools.partial(transform_kernel, offsets=offsets, blocks=blocks, rows=rows),
        out_shape=jax.ShapeDtypeStruct(shape, f32),
        in_specs=[SMEM, VMEM, VMEM],
        out_specs=VMEM,
        scratch_shapes=[
            pltpu.VMEM((2 * count, members, LANES), f32),
            pltpu.VMEM((LANES, LANES), f32),
        ],
        compiler_params=pltpu.CompilerParams(vmem_limit_bytes=32 * 2**20),
        cost_estimate=pl.CostEstimate(
            flops=10**10, bytes_accessed=10**6, transcendentals=0
        ),
        name="transforms",
    )(place, mine, other)


def mix_kernel(weights, *refs, blocks):
    *sources, out = refs
    rows, species, _, nz, ny = out.shape
    members = blocks * sources[0].shape[2]
    high, low = split(weights[:, :members])
    both = jnp.concatenate([high.astype(f32), low.astype(f32)], axis=0).astype(bf16)
    mul = functools.partial(
        lax.dot_general, dimension_numbers=(NN, ((), ())), preferred_element_type=f32
    )
    for z in range(nz):
        mixed = []
        for kind in range(species):
            parts = [sources[kind * blocks + j][0, z] for j in range(blocks)]
            values = parts[0] if blocks == 1 else jnp.concatenate(parts, axis=0)
            value_high, value_low = split(values)
            upper = mul(both, value_high)
            mixed.append(upper[:rows] + (upper[rows:] + mul(high, value_low)))
        mixed[2] = mixed[2] - mixed[3]
        for kind in range(species):
            out[:, kind, 0, z, :] = mixed[kind]


def mix(weights, sources, blocks, rows):
    nx, nz, held, ny = sources[0].shape
    species = len(sources) // blocks
    block = pl.BlockSpec((1, nz, held, ny), lambda x: (x, 0, 0, 0))
    return pl.pallas_call(
        functools.partial(mix_kernel, blocks=blocks),
        grid=(nx,),
        out_shape=jax.ShapeDtypeStruct((rows, species, nx, nz, ny), f32),
        in_specs=[pl.BlockSpec(weights.shape, lambda x: (0, 0))] + [block] * len(sources),
        out_specs=pl.BlockSpec((rows, species, 1, nz, ny), lambda x: (0, 0, x, 0, 0)),
        compiler_params=pltpu.CompilerParams(vmem_limit_bytes=32 * 2**20),
        name="mix",
    )(weights, *sources)


def swap(x, axis, bit):
    count = lax.axis_size(axis)
    return lax.ppermute(x, axis, [(k, k ^ bit) for k in range(count)])


def local(ensemble, diffusivity, binding, source, obs_index, owner, observed, obs_var):
    rows, species, nx, nz, ny = ensemble.shape
    devices = lax.axis_size("member")
    spaces = lax.axis_size("space")
    members = rows * devices
    batches = owner.shape[0]
    member = lax.axis_index("member")
    place = jnp.stack([member & 1, lax.axis_index("space"), member]).astype(jnp.int32)

    forward = [(k, k + 1) for k in range(spaces - 1)]
    backward = [(k + 1, k) for k in range(spaces - 1)]
    fields = [jnp.transpose(ensemble[:, k], (1, 2, 0, 3)) for k in range(species)]
    first, last = fields[0][0], fields[0][-1]
    omega, eta = voxel_weights(
        place, owner, obs_index, observed, obs_var, batches // 2, nx * nz, ny
    )
    for step in range(SUBSTEPS):
        low = lax.ppermute(last, "space", forward)
        high = lax.ppermute(first, "space", backward)
        final = step == SUBSTEPS - 1
        *fields, = substep(fields, low, high, diffusivity, binding, source, final)
        if not final:
            first, last = fields[4:]
            fields = fields[:4]
    free, receptor, tracer, internal = fields

    if devices == 4 and rows % 8 == 0:
        blocks = devices

        def offsets(position, j):
            return jnp.bitwise_xor(position, j) * rows

        def collect(x):
            across = swap(x, "member", 2)
            return [x, swap(x, "member", 1), across, swap(across, "member", 1)]
    else:
        blocks = 1

        def offsets(position, j):
            return 0

        def collect(x):
            return [lax.all_gather(x, "member", axis=2, tiled=True)]

    tracers = collect(tracer)
    half = gram(place, owner, omega, eta, tracers, offsets)
    half = jnp.sum(lax.all_gather(half, "space", axis=0), axis=0)
    weights = transforms(place, half, swap(half, "member", 1), offsets, blocks, rows)
    if blocks == 1:
        weights = lax.dynamic_slice(weights, (member * rows, 0), (rows, LANES))
    sources = collect(free) + collect(receptor) + tracers + collect(internal)
    return mix(weights, sources, blocks, rows)


def solution(mesh):
    in_specs = (
        P("member", None, "space", None, None),
        P("space", None, None),
        P("space", None, None),
        P("space", None, None),
        P(),
        P(),
        P(),
        P(),
    )
    out_specs = P("member", None, "space", None, None)
    return jax.shard_map(local, mesh=mesh, in_specs=in_specs, out_specs=out_specs, check_vma=False)
```

time: 813 us -> 187 us (0.23)
  waiting for transfers between devices: 399 us -> 48.5 us
  local copies, waits for them, and re-layouts: 123 us -> 9.54 us
  matrix products: 76.2 us -> 0 us
  Pallas kernels: 0 us -> 50.3 us
  other arithmetic: 48.1 us -> 1.26 us
  blocking collectives: 76 us -> 35.8 us
  starting transfers between devices: 60 us -> 40 us
  between operations: 19.5 us -> 0.33 us
    psum x4 -> x0, waiting for transfers between devices: 264 us -> none  [spread_2(): return lax.psum(jnp.where(mine, x, jnp.zeros_like(x)), axis)]
    all_to_all x7 -> x0, waiting for transfers between devices: 108 us -> none  [the longest x3 108 us: make_mixer(): lax.all_to_all(mixed, 'member', split_axis=0, concat_axis=2, tiled=True)]
    dot_general x216 -> x0, matrix products: 76.2 us -> none  [the longest x64 16.5 us: newton(): jnp.dot(scaled_root, factor, precision=highest)]
    pallas_call x0 -> x10, Pallas kernels: none -> 50.3 us  [the longest x1 27.4 us: transforms(): pl.pallas_call(functools.partial(transform_kernel, offsets=offsets, block...]
    all_to_all x1 -> x0, blocking collectives: 39.4 us -> none  [make_mixer(): lax.all_to_all(mixed, 'member', split_axis=0, concat_axis=2, tiled=True)]
    gather x4 -> x0, local copies, waits for them, and re-layouts: 37.1 us -> none  [observe(): values = jnp.take(totals, obs_index[which_batch], axis=1).T]
    all_to_all x18 -> x0, local copies, waits for them, and re-layouts: 33 us -> none  [the longest x10 18.4 us: make_mixer(): lax.all_to_all(mixed, 'member', split_axis=0, concat_axis=2, tiled=True)]
    add x10 -> x0, other arithmetic: 29.5 us -> none  [the longest x6 23.8 us: react(): free + diffusivity * (neighbours - 6.0 * free) - binding_flux]
  transfers between devices with their start and end apart: 23 -> 25, of which waited for: 17 -> 13; matrix products, arithmetic and copies ran while one was open for 13% -> 2% of each run, Pallas kernels for 0% -> 16%
where the time goes in v1:
time: 187 us; the launch traced here: 186 us
  Pallas kernels  50.3 us (27%)
  waiting for transfers between devices  48.5 us (26%)
  starting transfers between devices  40 us (21%)
  blocking collectives  35.8 us (19%)
  local copies, waits for them, and re-layouts  9.54 us (5%)
    all_gather x1, blocking collectives, local(): half = jnp.sum(lax.all_gather(half, 'space', axis=0), axis=0)  35.8 us
    pallas_call x1, Pallas kernels, transforms(): pl.pallas_call(functools.partial(transform_kernel, offsets=offsets, block...  27.4 us
    ppermute x6, starting transfers between devices, local(): low = lax.ppermute(last, 'space', forward)  25.3 us
    ppermute x13, waiting for transfers between devices, swap(): return lax.ppermute(x, axis, [(k, k ^ bit) for k in range(count)])  20.8 us
    ppermute x6, waiting for transfers between devices, local(): high = lax.ppermute(first, 'space', backward)  20.5 us
    pallas_call x6, Pallas kernels, substep(): pl.pallas_call(functools.partial(substep_kernel, final=final), out_shape=...  12.7 us
    pallas_call x1, Pallas kernels, mix(): pl.pallas_call(functools.partial(mix_kernel, blocks=blocks), grid=(nx,),...  8.14 us
    ppermute x6, starting transfers between devices, local(): high = lax.ppermute(first, 'space', backward)  7.75 us
  transfers between devices with their start and end apart: 25, of which 13 were waited for; matrix products, arithmetic and copies ran while one was open for 2% of the time, Pallas kernels for 16%

profile of v1, /device:TPU:0, one launch (start us, length us, event | category | flops | bytes accessed | tf_op | source)
XLA Modules:
  0.0 185.7 jit_solution(16060867750562140916)
XLA Ops:
  0.0 2.4 %fusion = (f32[24,1,8,4,256]{4,3,2,1,0:T(4,128)S(1)}, f32[24,1,8,4,256]{4,3,2,1,0:T(4,128)S(1)}, f32[24,1,8,4,256]{4,3,2,1,0:T(4,128)S(1)}, f32[24,1,8,4,256]{4,3,2,1,0:T(4,128)S(1)}) fusion(f32[24,4,8,4,256]{4,3,2,1,0:T(4,128)} %param.8), kind=kLoop, calls=%fused_computation.7 | loop fusion | bytes 6291456 | tf_op jit(solution)/shard_map/slice | solution.py:352
  2.4 0.0 copy-start
  2.4 0.0 copy-start.1
  2.4 0.0 copy-start.2
  2.5 0.5 copy.26
  2.9 1.3 collective-permute-start.1
  4.2 5.5 %collective-permute-start = (f32[4,24,256]{2,1,0:T(8,128)S(1)}, f32[4,24,256]{2,1,0:T(8,128)S(1)}, u32[]{:S(2)}, u32[]{:S(2)}) collective-permute-start(f32[4,24,256]{2,1,0:T(8,128)S(1)} %get-tuple-element.82), channel_id=1, source_target_pairs={{0,1},{1,2},{2,3},{3,4},{4,5},{5,6},{6,7},{8,9},{9,10},{10,11},{11... | collective-permute-start | bytes 294920 | tf_op jit(solution)/shard_map/ppermute | solution.py:358
  9.7 1.8 copy_bitcast_fusion
  11.5 0.5 copy.25
  12.0 0.8 collective-permute-done.low
  12.8 1.9 %substep.6 = (f32[8,4,24,256]{3,2,1,0:T(8,128)S(1)}, f32[8,4,24,256]{3,2,1,0:T(8,128)S(1)}, f32[8,4,24,256]{3,2,1,0:T(8,128)S(1)}, f32[8,4,24,256]{3,2,1,0:T(8,1...) custom-call(f32[8,4,24,256]{3,2,1,0:T(8,128)S(1)} %bitcast.27, f32[8,4,24,256]{3,2,1,0:T(8,128)S(1)} %bitcast.28, ...), custom_call_target="tpu_custom_call" | custom-call | flops 5898240 | bytes 6291456 | tf_op jit(solution)/shard_map/substep/pallas_call | solution.py:106
  14.7 0.0 copy-start.3
  14.7 0.9 copy-done.3
  15.6 4.4 %collective-permute-start.2 = (f32[4,24,256]{2,1,0:T(8,128)S(1)}, f32[4,24,256]{2,1,0:T(8,128)S(1)}, u32[]{:S(2)}, u32[]{:S(2)}) collective-permute-start(f32[4,24,256]{2,1,0:T(8,128)S(1)} %get-tuple-element.47), channel_id=1, source_target_pairs={{0,1},{1,2},{2,3},{3,4},{4,5},{5,6},{6,7},{8,9},{9,10},{10,11},{11... | collective-permute-start | bytes 294920 | tf_op jit(solution)/shard_map/ppermute | solution.py:358
  20.0 1.3 collective-permute-start.3
  21.3 0.9 collective-permute-done.2.low
  22.2 5.1 %collective-permute-done.3.high = f32[4,24,256]{2,1,0:T(8,128)S(1)} collective-permute-done((f32[4,24,256]{2,1,0:T(8,128)S(1)}, f32[4,24,256]{2,1,0:T(8,128)S(1)}, u32[]{:S(2)}, u32[]{:S(2)}) %collective-permute-start.3) | collective-permute-done | bytes 98336 | tf_op jit(solution)/shard_map/ppermute | solution.py:359
  27.3 1.9 %substep.7 = (f32[8,4,24,256]{3,2,1,0:T(8,128)S(1)}, f32[8,4,24,256]{3,2,1,0:T(8,128)S(1)}, f32[8,4,24,256]{3,2,1,0:T(8,128)S(1)}, f32[8,4,24,256]{3,2,1,0:T(8,1...) custom-call(f32[8,4,24,256]{3,2,1,0:T(8,128)S(1)} %get-tuple-element.43.a, ...), custom_call_target="tpu_custom_call" | custom-call | flops 5898240 | bytes 6291456 | tf_op jit(solution)/shard_map/substep/pallas_call | solution.py:106
  29.2 0.0 copy-start.4
  29.2 0.9 copy-done.4
  30.1 4.8 %collective-permute-start.4 = (f32[4,24,256]{2,1,0:T(8,128)S(1)}, f32[4,24,256]{2,1,0:T(8,128)S(1)}, u32[]{:S(2)}, u32[]{:S(2)}) collective-permute-start(f32[4,24,256]{2,1,0:T(8,128)S(1)} %get-tuple-element.53), channel_id=1, source_target_pairs={{0,1},{1,2},{2,3},{3,4},{4,5},{5,6},{6,7},{8,9},{9,10},{10,11},{11... | collective-permute-start | bytes 294920 | tf_op jit(solution)/shard_map/ppermute | solution.py:358
  34.9 1.3 collective-permute-start.5
  36.2 1.9 %collective-permute-done.4.low = f32[4,24,256]{2,1,0:T(8,128)S(1)} collective-permute-done((f32[4,24,256]{2,1,0:T(8,128)S(1)}, f32[4,24,256]{2,1,0:T(8,128)S(1)}, u32[]{:S(2)}, u32[]{:S(2)}) %collective-permute-start.4) | collective-permute-done | bytes 98336 | tf_op jit(solution)/shard_map/ppermute | solution.py:358
  38.1 3.3 %collective-permute-done.5.high = f32[4,24,256]{2,1,0:T(8,128)S(1)} collective-permute-done((f32[4,24,256]{2,1,0:T(8,128)S(1)}, f32[4,24,256]{2,1,0:T(8,128)S(1)}, u32[]{:S(2)}, u32[]{:S(2)}) %collective-permute-start.5) | collective-permute-done | bytes 98336 | tf_op jit(solution)/shard_map/ppermute | solution.py:359
  41.4 1.9 %substep.8 = (f32[8,4,24,256]{3,2,1,0:T(8,128)S(1)}, f32[8,4,24,256]{3,2,1,0:T(8,128)S(1)}, f32[8,4,24,256]{3,2,1,0:T(8,128)S(1)}, f32[8,4,24,256]{3,2,1,0:T(8,1...) custom-call(f32[8,4,24,256]{3,2,1,0:T(8,128)S(1)} %get-tuple-element.49.a, ...), custom_call_target="tpu_custom_call" | custom-call | flops 5898240 | bytes 6291456 | tf_op jit(solution)/shard_map/substep/pallas_call | solution.py:106
  43.3 0.0 copy-start.5
  43.3 0.9 copy-done.5
  44.2 2.9 %collective-permute-start.6 = (f32[4,24,256]{2,1,0:T(8,128)S(1)}, f32[4,24,256]{2,1,0:T(8,128)S(1)}, u32[]{:S(2)}, u32[]{:S(2)}) collective-permute-start(f32[4,24,256]{2,1,0:T(8,128)S(1)} %get-tuple-element.59), channel_id=1, source_target_pairs={{0,1},{1,2},{2,3},{3,4},{4,5},{5,6},{6,7},{8,9},{9,10},{10,11},{11... | collective-permute-start | bytes 294920 | tf_op jit(solution)/shard_map/ppermute | solution.py:358
  47.1 1.3 collective-permute-start.7
  48.4 1.9 %collective-permute-done.6.low = f32[4,24,256]{2,1,0:T(8,128)S(1)} collective-permute-done((f32[4,24,256]{2,1,0:T(8,128)S(1)}, f32[4,24,256]{2,1,0:T(8,128)S(1)}, u32[]{:S(2)}, u32[]{:S(2)}) %collective-permute-start.6) | collective-permute-done | bytes 98336 | tf_op jit(solution)/shard_map/ppermute | solution.py:358
  50.3 3.3 %collective-permute-done.7.high = f32[4,24,256]{2,1,0:T(8,128)S(1)} collective-permute-done((f32[4,24,256]{2,1,0:T(8,128)S(1)}, f32[4,24,256]{2,1,0:T(8,128)S(1)}, u32[]{:S(2)}, u32[]{:S(2)}) %collective-permute-start.7) | collective-permute-done | bytes 98336 | tf_op jit(solution)/shard_map/ppermute | solution.py:359
  53.6 1.9 %substep.9 = (f32[8,4,24,256]{3,2,1,0:T(8,128)S(1)}, f32[8,4,24,256]{3,2,1,0:T(8,128)S(1)}, f32[8,4,24,256]{3,2,1,0:T(8,128)S(1)}, f32[8,4,24,256]{3,2,1,0:T(8,1...) custom-call(f32[8,4,24,256]{3,2,1,0:T(8,128)S(1)} %get-tuple-element.55.a, ...), custom_call_target="tpu_custom_call" | custom-call | flops 5898240 | bytes 6291456 | tf_op jit(solution)/shard_map/substep/pallas_call | solution.py:106
  55.5 0.9 copy-done.6
  56.4 4.8 %collective-permute-start.8 = (f32[4,24,256]{2,1,0:T(8,128)S(1)}, f32[4,24,256]{2,1,0:T(8,128)S(1)}, u32[]{:S(2)}, u32[]{:S(2)}) collective-permute-start(f32[4,24,256]{2,1,0:T(8,128)S(1)} %get-tuple-element.65), channel_id=1, source_target_pairs={{0,1},{1,2},{2,3},{3,4},{4,5},{5,6},{6,7},{8,9},{9,10},{10,11},{11... | collective-permute-start | bytes 294920 | tf_op jit(solution)/shard_map/ppermute | solution.py:358
  61.2 1.3 collective-permute-start.9
  62.5 0.9 collective-permute-done.8.low
  63.4 4.3 %collective-permute-done.9.high = f32[4,24,256]{2,1,0:T(8,128)S(1)} collective-permute-done((f32[4,24,256]{2,1,0:T(8,128)S(1)}, f32[4,24,256]{2,1,0:T(8,128)S(1)}, u32[]{:S(2)}, u32[]{:S(2)}) %collective-permute-start.9) | collective-permute-done | bytes 98336 | tf_op jit(solution)/shard_map/ppermute | solution.py:359
  67.7 1.9 %substep.10 = (f32[8,4,24,256]{3,2,1,0:T(8,128)S(1)}, f32[8,4,24,256]{3,2,1,0:T(8,128)S(1)}, f32[8,4,24,256]{3,2,1,0:T(8,128)S(1)}, f32[8,4,24,256]{3,2,1,0:T(8,...) custom-call(f32[8,4,24,256]{3,2,1,0:T(8,128)S(1)} %get-tuple-element.61.a, ...), custom_call_target="tpu_custom_call" | custom-call | flops 5898240 | bytes 6291456 | tf_op jit(solution)/shard_map/substep/pallas_call | solution.py:106
  69.6 0.0 copy-start.7
  69.6 0.9 copy-done.7
  70.5 2.9 %collective-permute-start.10 = (f32[4,24,256]{2,1,0:T(8,128)S(1)}, f32[4,24,256]{2,1,0:T(8,128)S(1)}, u32[]{:S(2)}, u32[]{:S(2)}) collective-permute-start(f32[4,24,256]{2,1,0:T(8,128)S(1)} %get-tuple-element.71), channel_id=1, source_target_pairs={{0,1},{1,2},{2,3},{3,4},{4,5},{5,6},{6,7},{8,9},{9,10},{10,11},{11... | collective-permute-start | bytes 294920 | tf_op jit(solution)/shard_map/ppermute | solution.py:358
  73.4 1.3 collective-permute-start.11
  74.7 0.9 collective-permute-done.10.low
  75.6 4.3 %collective-permute-done.11.high = f32[4,24,256]{2,1,0:T(8,128)S(1)} collective-permute-done((f32[4,24,256]{2,1,0:T(8,128)S(1)}, f32[4,24,256]{2,1,0:T(8,128)S(1)}, u32[]{:S(2)}, u32[]{:S(2)}) %collective-permute-start.11) | collective-permute-done | bytes 98336 | tf_op jit(solution)/shard_map/ppermute | solution.py:359
  79.9 3.3 %substep.11 = (f32[8,4,24,256]{3,2,1,0:T(8,128)}, f32[8,4,24,256]{3,2,1,0:T(8,128)}, f32[8,4,24,256]{3,2,1,0:T(8,128)S(1)}, f32[8,4,24,256]{3,2,1,0:T(8,128)}) custom-call(f32[8,4,24,256]{3,2,1,0:T(8,128)S(1)} %get-tuple-element.67.a, f32[8,4,24,256]{3,2,1,0:T(8,128)S(1)} %get-tuple-element.68.r, f32[8,4,24,256]{3,2,1,0:T(8,128)S(1)} %get-tuple-element.69.c, ...), custom_call_target="tpu_custom_call" | custom-call | flops 5898240 | bytes 6291456 | tf_op jit(solution)/shard_map/substep/pallas_call | solution.py:106
  83.2 1.5 collective-permute-start.13
  84.8 10.8 %collective-permute-done.13.refs_2_.refs_10_ = f32[8,4,24,256]{3,2,1,0:T(8,128)S(1)} collective-permute-done((f32[8,4,24,256]{3,2,1,0:T(8,128)S(1)}, f32[8,4,24,256]{3,2,1,0:T(8,128)S(1)}, u32[]{:S(2)}, u32[]{:S(2)}) %collective-permute-start.13) | collective-permute-done | bytes 786464 | tf_op jit(solution)/shard_map/ppermute | solution.py:338
  95.5 1.5 collective-permute-start.17
  97.1 0.2 collective-permute-start.16
  97.3 0.5 collective-permute-start.20
  97.8 1.5 collective-permute-start.23
  99.3 0.1 pad_add_fusion.place
  99.4 1.4 voxel_weights.1
  100.8 0.6 gram.1
  101.4 35.8 %all-gather = f32[16,96,128]{2,1,0:T(8,128)} all-gather(f32[2,96,128]{2,1,0:T(8,128)S(1)} %gram.1), channel_id=2, replica_groups=mesh['member'=4,'space'=8] {'space'}, dimensions={0}, use_global_device_ids=true | all-gather | bytes 884736 | tf_op jit(solution)/shard_map/all_gather | solution.py:387
  137.2 1.2 reduce_sum.9.mine
  138.4 0.1 collective-permute-start.15
  138.5 0.5 collective-permute-start.19
  139.0 0.1 collective-permute-start.22
  139.1 0.4 collective-permute-start.18
  139.5 10.0 %collective-permute-done.23.refs_14_ = f32[8,4,24,256]{3,2,1,0:T(8,128)} collective-permute-done((f32[8,4,24,256]{3,2,1,0:T(8,128)}, f32[8,4,24,256]{3,2,1,0:T(8,128)}, u32[]{:S(2)}, u32[]{:S(2)}) %collective-permute-start.23) | collective-permute-done | bytes 786464 | tf_op jit(solution)/shard_map/ppermute | solution.py:338
  149.5 0.5 collective-permute-start.24
  150.0 27.4 %transforms.1.weights = f32[24,128]{1,0:T(8,128)S(1)} custom-call(s32[3]{0:T(128)S(1)} %pad_add_fusion.place, f32[2,96,128]{2,1,0:T(8,128)S(1)} %reduce_sum.9.mine, f32[2,96,128]{2,1,0:T(8,128)S(1)} %collective-permute-done.15.other), custom_call_target="tpu_custom_call" | custom-call | flops 10000000000 | bytes 1000000 | tf_op jit(solution)/shard_map/transforms/pallas_call | solution.py:282
  177.5 8.1 %mix.1 = f32[24,4,8,4,256]{4,3,2,1,0:T(4,128)} custom-call(f32[24,128]{1,0:T(8,128)S(1)} %transforms.1.weights, f32[8,4,24,256]{3,2,1,0:T(8,128)} %get-tuple-element.74.refs_0_, f32[8,4,24,256]{3,2,1,0:T(8,128)} %collective-permute-done.16.refs_1_, f32[8,4,24,256]{3,2,1,0:T(8,128)} %collective-permute-done.17.refs_2_, ...), custom_call_target="tpu_custom_call" | custom-call | tf_op jit(solution)/shard_map/mix/pallas_call | solution.py:325
  (28 shorter events, 0.1 us)
Async XLA Ops:
  2.4 10.4 %copy-start = (f32[8,4,256]{2,1,0:T(4,128)S(1)}, f32[8,4,256]{2,1,0:T(4,128)}, u32[]{:S(2)}) copy-start(f32[8,4,256]{2,1,0:T(4,128)} %diffusivity.11) | copy-start | bytes 98308
  2.4 10.4 %copy-start.1 = (f32[8,4,256]{2,1,0:T(4,128)S(1)}, f32[8,4,256]{2,1,0:T(4,128)}, u32[]{:S(2)}) copy-start(f32[8,4,256]{2,1,0:T(4,128)} %binding.11) | copy-start | bytes 98308
  2.4 10.4 %copy-start.2 = (f32[8,4,256]{2,1,0:T(4,128)S(1)}, f32[8,4,256]{2,1,0:T(4,128)}, u32[]{:S(2)}) copy-start(f32[8,4,256]{2,1,0:T(4,128)} %source.11) | copy-start | bytes 98308
  2.9 9.0 %collective-permute-start.1 = (f32[4,24,256]{2,1,0:T(8,128)S(1)}, f32[4,24,256]{2,1,0:T(8,128)S(1)}, u32[]{:S(2)}, u32[]{:S(2)}) collective-permute-start(f32[4,24,256]{2,1,0:T(8,128)S(1)} %get-tuple-element.81), channel_id=1, source_target_pairs={{1,0},{2,1},{3,2},{4,3},{5,4},{6,5},{7,6},{9,8},{10,9},{11,10},{12... | collective-permute-start | bytes 294920 | tf_op jit(solution)/shard_map/ppermute | solution.py:359
  4.2 8.6 %collective-permute-start = (f32[4,24,256]{2,1,0:T(8,128)S(1)}, f32[4,24,256]{2,1,0:T(8,128)S(1)}, u32[]{:S(2)}, u32[]{:S(2)}) collective-permute-start(f32[4,24,256]{2,1,0:T(8,128)S(1)} %get-tuple-element.82), channel_id=1, source_target_pairs={{0,1},{1,2},{2,3},{3,4},{4,5},{5,6},{6,7},{8,9},{9,10},{10,11},{11... | collective-permute-start | bytes 294920 | tf_op jit(solution)/shard_map/ppermute | solution.py:358
  14.7 0.9 copy-start.3
  15.6 6.6 %collective-permute-start.2 = (f32[4,24,256]{2,1,0:T(8,128)S(1)}, f32[4,24,256]{2,1,0:T(8,128)S(1)}, u32[]{:S(2)}, u32[]{:S(2)}) collective-permute-start(f32[4,24,256]{2,1,0:T(8,128)S(1)} %get-tuple-element.47), channel_id=1, source_target_pairs={{0,1},{1,2},{2,3},{3,4},{4,5},{5,6},{6,7},{8,9},{9,10},{10,11},{11... | collective-permute-start | bytes 294920 | tf_op jit(solution)/shard_map/ppermute | solution.py:358
  20.0 7.3 %collective-permute-start.3 = (f32[4,24,256]{2,1,0:T(8,128)S(1)}, f32[4,24,256]{2,1,0:T(8,128)S(1)}, u32[]{:S(2)}, u32[]{:S(2)}) collective-permute-start(f32[4,24,256]{2,1,0:T(8,128)S(1)} %get-tuple-element.48), channel_id=1, source_target_pairs={{1,0},{2,1},{3,2},{4,3},{5,4},{6,5},{7,6},{9,8},{10,9},{11,10},{12... | collective-permute-start | bytes 294920 | tf_op jit(solution)/shard_map/ppermute | solution.py:359
  29.2 0.9 copy-start.4
  30.1 8.0 %collective-permute-start.4 = (f32[4,24,256]{2,1,0:T(8,128)S(1)}, f32[4,24,256]{2,1,0:T(8,128)S(1)}, u32[]{:S(2)}, u32[]{:S(2)}) collective-permute-start(f32[4,24,256]{2,1,0:T(8,128)S(1)} %get-tuple-element.53), channel_id=1, source_target_pairs={{0,1},{1,2},{2,3},{3,4},{4,5},{5,6},{6,7},{8,9},{9,10},{10,11},{11... | collective-permute-start | bytes 294920 | tf_op jit(solution)/shard_map/ppermute | solution.py:358
  34.9 6.5 %collective-permute-start.5 = (f32[4,24,256]{2,1,0:T(8,128)S(1)}, f32[4,24,256]{2,1,0:T(8,128)S(1)}, u32[]{:S(2)}, u32[]{:S(2)}) collective-permute-start(f32[4,24,256]{2,1,0:T(8,128)S(1)} %get-tuple-element.54), channel_id=1, source_target_pairs={{1,0},{2,1},{3,2},{4,3},{5,4},{6,5},{7,6},{9,8},{10,9},{11,10},{12... | collective-permute-start | bytes 294920 | tf_op jit(solution)/shard_map/ppermute | solution.py:359
  43.3 0.9 copy-start.5
  44.2 6.1 %collective-permute-start.6 = (f32[4,24,256]{2,1,0:T(8,128)S(1)}, f32[4,24,256]{2,1,0:T(8,128)S(1)}, u32[]{:S(2)}, u32[]{:S(2)}) collective-permute-start(f32[4,24,256]{2,1,0:T(8,128)S(1)} %get-tuple-element.59), channel_id=1, source_target_pairs={{0,1},{1,2},{2,3},{3,4},{4,5},{5,6},{6,7},{8,9},{9,10},{10,11},{11... | collective-permute-start | bytes 294920 | tf_op jit(solution)/shard_map/ppermute | solution.py:358
  47.1 6.5 %collective-permute-start.7 = (f32[4,24,256]{2,1,0:T(8,128)S(1)}, f32[4,24,256]{2,1,0:T(8,128)S(1)}, u32[]{:S(2)}, u32[]{:S(2)}) collective-permute-start(f32[4,24,256]{2,1,0:T(8,128)S(1)} %get-tuple-element.60), channel_id=1, source_target_pairs={{1,0},{2,1},{3,2},{4,3},{5,4},{6,5},{7,6},{9,8},{10,9},{11,10},{12... | collective-permute-start | bytes 294920 | tf_op jit(solution)/shard_map/ppermute | solution.py:359
  55.5 0.9 copy-start.6
  56.4 7.0 %collective-permute-start.8 = (f32[4,24,256]{2,1,0:T(8,128)S(1)}, f32[4,24,256]{2,1,0:T(8,128)S(1)}, u32[]{:S(2)}, u32[]{:S(2)}) collective-permute-start(f32[4,24,256]{2,1,0:T(8,128)S(1)} %get-tuple-element.65), channel_id=1, source_target_pairs={{0,1},{1,2},{2,3},{3,4},{4,5},{5,6},{6,7},{8,9},{9,10},{10,11},{11... | collective-permute-start | bytes 294920 | tf_op jit(solution)/shard_map/ppermute | solution.py:358
  61.2 6.5 %collective-permute-start.9 = (f32[4,24,256]{2,1,0:T(8,128)S(1)}, f32[4,24,256]{2,1,0:T(8,128)S(1)}, u32[]{:S(2)}, u32[]{:S(2)}) collective-permute-start(f32[4,24,256]{2,1,0:T(8,128)S(1)} %get-tuple-element.66), channel_id=1, source_target_pairs={{1,0},{2,1},{3,2},{4,3},{5,4},{6,5},{7,6},{9,8},{10,9},{11,10},{12... | collective-permute-start | bytes 294920 | tf_op jit(solution)/shard_map/ppermute | solution.py:359
  67.7 31.7 %copy-start.8 = (s32[4,2048]{1,0:T(4,128)S(1)}, s32[4,2048]{1,0:T(4,128)}, u32[]{:S(2)}) copy-start(s32[4,2048]{1,0:T(4,128)} %obs_index.1) | copy-start | bytes 98308
  67.7 31.7 %copy-start.9 = (f32[4,2048]{1,0:T(4,128)S(1)}, f32[4,2048]{1,0:T(4,128)}, u32[]{:S(2)}) copy-start(f32[4,2048]{1,0:T(4,128)} %observed.1) | copy-start | bytes 98308
  67.7 31.7 %copy-start.10 = (f32[4,2048]{1,0:T(4,128)S(1)}, f32[4,2048]{1,0:T(4,128)}, u32[]{:S(2)}) copy-start(f32[4,2048]{1,0:T(4,128)} %obs_var.1) | copy-start | bytes 98308
  67.7 31.7 %copy-start.11 = (s32[4]{0:T(128)S(1)}, s32[4]{0:T(128)}, u32[]{:S(2)}) copy-start(s32[4]{0:T(128)} %owner.3) | copy-start | bytes 52
  69.6 0.9 copy-start.7
  70.5 5.1 %collective-permute-start.10 = (f32[4,24,256]{2,1,0:T(8,128)S(1)}, f32[4,24,256]{2,1,0:T(8,128)S(1)}, u32[]{:S(2)}, u32[]{:S(2)}) collective-permute-start(f32[4,24,256]{2,1,0:T(8,128)S(1)} %get-tuple-element.71), channel_id=1, source_target_pairs={{0,1},{1,2},{2,3},{3,4},{4,5},{5,6},{6,7},{8,9},{9,10},{10,11},{11... | collective-permute-start | bytes 294920 | tf_op jit(solution)/shard_map/ppermute | solution.py:358
  73.4 6.5 %collective-permute-start.11 = (f32[4,24,256]{2,1,0:T(8,128)S(1)}, f32[4,24,256]{2,1,0:T(8,128)S(1)}, u32[]{:S(2)}, u32[]{:S(2)}) collective-permute-start(f32[4,24,256]{2,1,0:T(8,128)S(1)} %get-tuple-element.72), channel_id=1, source_target_pairs={{1,0},{2,1},{3,2},{4,3},{5,4},{6,5},{7,6},{9,8},{10,9},{11,10},{12... | collective-permute-start | bytes 294920 | tf_op jit(solution)/shard_map/ppermute | solution.py:359
  83.2 12.3 %collective-permute-start.13 = (f32[8,4,24,256]{3,2,1,0:T(8,128)S(1)}, f32[8,4,24,256]{3,2,1,0:T(8,128)S(1)}, u32[]{:S(2)}, u32[]{:S(2)}) collective-permute-start(f32[8,4,24,256]{3,2,1,0:T(8,128)S(1)} %get-tuple-element.73.refs_0_.refs_8_), channel_id=1, source_target_pairs={{0,16},{8,24},{16,0},{24,8},{1,17},{9,25},{17,1},{25,9},{2,18},{10... | collective-permute-start | bytes 2359304 | tf_op jit(solution)/shard_map/ppermute | solution.py:338
  84.8 13.0 %collective-permute-start.12 = (f32[8,4,24,256]{3,2,1,0:T(8,128)S(1)}, f32[8,4,24,256]{3,2,1,0:T(8,128)S(1)}, u32[]{:S(2)}, u32[]{:S(2)}) collective-permute-start(f32[8,4,24,256]{3,2,1,0:T(8,128)S(1)} %get-tuple-element.73.refs_0_.refs_8_), channel_id=1, source_target_pairs={{0,8},{8,0},{16,24},{24,16},{1,9},{9,1},{17,25},{25,17},{2,10},{10... | collective-permute-start | bytes 2359304 | tf_op jit(solution)/shard_map/ppermute | solution.py:338
  95.5 5.3 %collective-permute-start.14 = (f32[8,4,24,256]{3,2,1,0:T(8,128)S(1)}, f32[8,4,24,256]{3,2,1,0:T(8,128)S(1)}, u32[]{:S(2)}, u32[]{:S(2)}) collective-permute-start(f32[8,4,24,256]{3,2,1,0:T(8,128)S(1)} %collective-permute-done.13.refs_2_.refs_10_), channel_id=1, source_target_pairs={{0,8},{8,0},{16,24},{24,16},{1,9},{9,1},{17,25},{25,17},{2,10},{10... | collective-permute-start | bytes 2359304 | tf_op jit(solution)/shard_map/ppermute | solution.py:338
  95.5 43.0 %collective-permute-start.17 = (f32[8,4,24,256]{3,2,1,0:T(8,128)}, f32[8,4,24,256]{3,2,1,0:T(8,128)}, u32[]{:S(2)}, u32[]{:S(2)}) collective-permute-start(f32[8,4,24,256]{3,2,1,0:T(8,128)} %get-tuple-element.74.refs_0_), channel_id=1, source_target_pairs={{0,16},{8,24},{16,0},{24,8},{1,17},{9,25},{17,1},{25,9},{2,18},{10... | collective-permute-start | bytes 2359304 | tf_op jit(solution)/shard_map/ppermute | solution.py:338
  97.1 42.0 %collective-permute-start.16 = (f32[8,4,24,256]{3,2,1,0:T(8,128)}, f32[8,4,24,256]{3,2,1,0:T(8,128)}, u32[]{:S(2)}, u32[]{:S(2)}) collective-permute-start(f32[8,4,24,256]{3,2,1,0:T(8,128)} %get-tuple-element.74.refs_0_), channel_id=1, source_target_pairs={{0,8},{8,0},{16,24},{24,16},{1,9},{9,1},{17,25},{25,17},{2,10},{10... | collective-permute-start | bytes 2359304 | tf_op jit(solution)/shard_map/ppermute | solution.py:338
  97.3 41.8 %collective-permute-start.20 = (f32[8,4,24,256]{3,2,1,0:T(8,128)}, f32[8,4,24,256]{3,2,1,0:T(8,128)}, u32[]{:S(2)}, u32[]{:S(2)}) collective-permute-start(f32[8,4,24,256]{3,2,1,0:T(8,128)} %get-tuple-element.75.refs_4_), channel_id=1, source_target_pairs={{0,16},{8,24},{16,0},{24,8},{1,17},{9,25},{17,1},{25,9},{2,18},{10... | collective-permute-start | bytes 2359304 | tf_op jit(solution)/shard_map/ppermute | solution.py:338
  97.8 51.7 %collective-permute-start.23 = (f32[8,4,24,256]{3,2,1,0:T(8,128)}, f32[8,4,24,256]{3,2,1,0:T(8,128)}, u32[]{:S(2)}, u32[]{:S(2)}) collective-permute-start(f32[8,4,24,256]{3,2,1,0:T(8,128)} %get-tuple-element.76.refs_12_), channel_id=1, source_target_pairs={{0,16},{8,24},{16,0},{24,8},{1,17},{9,25},{17,1},{25,9},{2,18},{10... | collective-permute-start | bytes 2359304 | tf_op jit(solution)/shard_map/ppermute | solution.py:338
  138.4 11.1 %collective-permute-start.15 = (f32[2,96,128]{2,1,0:T(8,128)S(1)}, f32[2,96,128]{2,1,0:T(8,128)S(1)}, u32[]{:S(2)}, u32[]{:S(2)}) collective-permute-start(f32[2,96,128]{2,1,0:T(8,128)S(1)} %reduce_sum.9.mine), channel_id=1, source_target_pairs={{0,8},{8,0},{16,24},{24,16},{1,9},{9,1},{17,25},{25,17},{2,10},{10... | collective-permute-start | bytes 294920 | tf_op jit(solution)/shard_map/ppermute | solution.py:338
  138.5 39.0 %collective-permute-start.19 = (f32[8,4,24,256]{3,2,1,0:T(8,128)}, f32[8,4,24,256]{3,2,1,0:T(8,128)S(1)}, u32[]{:S(2)}, u32[]{:S(2)}) collective-permute-start(f32[8,4,24,256]{3,2,1,0:T(8,128)} %get-tuple-element.75.refs_4_), channel_id=1, source_target_pairs={{0,8},{8,0},{16,24},{24,16},{1,9},{9,1},{17,25},{25,17},{2,10},{10... | collective-permute-start | bytes 2359304 | tf_op jit(solution)/shard_map/ppermute | solution.py:338
  139.0 38.5 %collective-permute-start.22 = (f32[8,4,24,256]{3,2,1,0:T(8,128)}, f32[8,4,24,256]{3,2,1,0:T(8,128)S(1)}, u32[]{:S(2)}, u32[]{:S(2)}) collective-permute-start(f32[8,4,24,256]{3,2,1,0:T(8,128)} %get-tuple-element.76.refs_12_), channel_id=1, source_target_pairs={{0,8},{8,0},{16,24},{24,16},{1,9},{9,1},{17,25},{25,17},{2,10},{10... | collective-permute-start | bytes 2359304 | tf_op jit(solution)/shard_map/ppermute | solution.py:338
  139.1 38.4 %collective-permute-start.18 = (f32[8,4,24,256]{3,2,1,0:T(8,128)}, f32[8,4,24,256]{3,2,1,0:T(8,128)S(1)}, u32[]{:S(2)}, u32[]{:S(2)}) collective-permute-start(f32[8,4,24,256]{3,2,1,0:T(8,128)} %collective-permute-done.17.refs_2_), channel_id=1, source_target_pairs={{0,8},{8,0},{16,24},{24,16},{1,9},{9,1},{17,25},{25,17},{2,10},{10... | collective-permute-start | bytes 2359304 | tf_op jit(solution)/shard_map/ppermute | solution.py:338
  149.5 28.0 %collective-permute-start.21 = (f32[8,4,24,256]{3,2,1,0:T(8,128)}, f32[8,4,24,256]{3,2,1,0:T(8,128)S(1)}, u32[]{:S(2)}, u32[]{:S(2)}) collective-permute-start(f32[8,4,24,256]{3,2,1,0:T(8,128)} %collective-permute-done.20.refs_6_), channel_id=1, source_target_pairs={{0,8},{8,0},{16,24},{24,16},{1,9},{9,1},{17,25},{25,17},{2,10},{10... | collective-permute-start | bytes 2359304 | tf_op jit(solution)/shard_map/ppermute | solution.py:338
  149.5 28.0 %collective-permute-start.24 = (f32[8,4,24,256]{3,2,1,0:T(8,128)}, f32[8,4,24,256]{3,2,1,0:T(8,128)S(1)}, u32[]{:S(2)}, u32[]{:S(2)}) collective-permute-start(f32[8,4,24,256]{3,2,1,0:T(8,128)} %collective-permute-done.23.refs_14_), channel_id=1, source_target_pairs={{0,8},{8,0},{16,24},{24,16},{1,9},{9,1},{17,25},{25,17},{2,10},{10... | collective-permute-start | bytes 2359304 | tf_op jit(solution)/shard_map/ppermute | solution.py:338

commit v2 on v1

--- a/solution.py
+++ b/solution.py
@@ -10,6 +10,7 @@
 SUBSTEPS = 6
 NEWTON = 16
 LANES = 128
+SCOPED = 8 * 2**20
 
 unbind_rate = 0.05
 uptake_rate = 0.1
@@ -54,66 +55,117 @@
 NT = ((1,), (1,))
 
 
+def neighbour_sum(a, low, high, x, z, at_left, at_right):
+    nx, nz, members, ny = a.shape
+    free = a[x, z]
+    total = (low[z] if x == 0 else a[x - 1, z]) + (high[z] if x == nx - 1 else a[x + 1, z])
+    if z + 1 < nz:
+        total += a[x, z + 1]
+    if z > 0:
+        total += a[x, z - 1]
+    total += jnp.where(at_right, 0.0, pltpu.roll(free, ny - 1, 1))
+    return total + jnp.where(at_left, 0.0, pltpu.roll(free, 1, 1))
+
+
+def ends(a):
+    _, _, members, ny = a.shape
+    lane = lax.broadcasted_iota(jnp.int32, (members, ny), 1)
+    return lane == 0, lane == ny - 1
+
+
+def free_part(a, low, high, diffusivity, x, z, at):
+    free = a[x, z]
+    neighbours = neighbour_sum(a, low, high, x, z, *at)
+    return free + diffusivity[x, pl.ds(z, 1), :] * (neighbours - 6.0 * free)
+
+
+def react(free, receptor, complexed, internal, binding):
+    flux = binding * free * receptor
+    back = unbind_rate * complexed - flux
+    return (
+        back,
+        receptor + back + recycle_rate * internal,
+        complexed + flux - (unbind_rate + uptake_rate) * complexed,
+        internal + uptake_rate * complexed - recycle_rate * internal,
+    )
+
+
+def edges_kernel(a, r, c, low, high, diffusivity, binding, source, first, last):
+    nx, nz, _, _ = a.shape
+    at = ends(a)
+    for x, out in ((0, first), (nx - 1, last)):
+        for z in range(nz):
+            row = pl.ds(z, 1)
+            flux = binding[x, row, :] * a[x, z] * r[x, z]
+            out[z] = (
+                free_part(a, low, high, diffusivity, x, z, at)
+                + (unbind_rate * c[x, z] - flux)
+                + source[x, row, :]
+            )
+
+
 def substep_kernel(
-    a, r, c, i, low, high, diffusivity, binding, source, out_a, out_r, out_c, out_i, *edges, final
+    a, r, c, i, low, high, diffusivity, binding, source, out_a, out_r, out_c, out_i
 ):
-    nx, nz, members, ny = a.shape
-    lane = lax.broadcasted_iota(jnp.int32, (members, ny), 1)
-    at_left, at_right = lane == 0, lane == ny - 1
-
-    def cell(x, z):
-        free = a[x, z]
-        neighbours = (low[z] if x == 0 else a[x - 1, z]) + (
-            high[z] if x == nx - 1 else a[x + 1, z]
-        )
-        if z + 1 < nz:
-            neighbours += a[x, z + 1]
-        if z > 0:
-            neighbours += a[x, z - 1]
-        neighbours += jnp.where(at_right, 0.0, pltpu.roll(free, ny - 1, 1))
-        neighbours += jnp.where(at_left, 0.0, pltpu.roll(free, 1, 1))
-        receptor, complexed, internal = r[x, z], c[x, z], i[x, z]
-        row = pl.ds(z, 1)
-        flux = binding[x, row, :] * free * receptor
-        back = unbind_rate * complexed - flux
-        new_free = (
-            free
-            + diffusivity[x, row, :] * (neighbours - 6.0 * free)
-            + back
-            + source[x, row, :]
-        )
-        new_internal = internal + uptake_rate * complexed - recycle_rate * internal
-        new_complexed = complexed + flux - (unbind_rate + uptake_rate) * complexed
-        out_a[x, z] = new_free
-        out_r[x, z] = receptor + back + recycle_rate * internal
-        out_c[x, z] = new_complexed + new_internal if final else new_complexed
-        out_i[x, z] = new_internal
-        if not final and x == 0:
-            edges[0][z] = new_free
-        if not final and x == nx - 1:
-            edges[1][z] = new_free
-
+    nx, nz, _, _ = a.shape
+    at = ends(a)
     for x in range(nx):
         for z in range(nz):
-            cell(x, z)
-
-
-def substep(fields, low, high, diffusivity, binding, source, final):
-    nx, nz, members, ny = fields[0].shape
-    whole = jax.ShapeDtypeStruct((nx, nz, members, ny), f32)
-    plane = jax.ShapeDtypeStruct((nz, members, ny), f32)
-    cells = nx * nz * members * ny
+            row = pl.ds(z, 1)
+            back, out_r[x, z], out_c[x, z], out_i[x, z] = react(
+                a[x, z], r[x, z], c[x, z], i[x, z], binding[x, row, :]
+            )
+            out_a[x, z] = (
+                free_part(a, low, high, diffusivity, x, z, at) + back + source[x, row, :]
+            )
+
+
+def last_but_one_kernel(
+    a, r, c, i, low, high, diffusivity, binding, source, out_a, out_add, out_tracer, out_i
+):
+    nx, nz, _, _ = a.shape
+    at = ends(a)
+    for x in range(nx):
+        for z in range(nz):
+            row = pl.ds(z, 1)
+            bind = binding[x, row, :]
+            back, receptor, complexed, internal = react(
+                a[x, z], r[x, z], c[x, z], i[x, z], bind
+            )
+            free = free_part(a, low, high, diffusivity, x, z, at) + back + source[x, row, :]
+            back, _, complexed, internal = react(free, receptor, complexed, internal, bind)
+            out_a[x, z] = free
+            out_add[x, z] = back + source[x, row, :]
+            out_tracer[x, z] = complexed + internal
+            out_i[x, z] = internal
+
+
+def last_free_kernel(a, add, low, high, diffusivity, out_a):
+    nx, nz, _, _ = a.shape
+    at = ends(a)
+    for x in range(nx):
+        for z in range(nz):
+            out_a[x, z] = free_part(a, low, high, diffusivity, x, z, at) + add[x, z]
+
+
+def forecast_call(kernel, inputs, outputs, share=1.0, ready=()):
+    nx, nz, members, ny = inputs[0].shape
+    cells = int(nx * nz * members * ny * share)
+
+    def body(*refs):
+        kernel(*refs[: len(inputs)], *refs[len(inputs) + len(ready) :])
+
     return pl.pallas_call(
-        functools.partial(substep_kernel, final=final),
-        out_shape=[whole] * 4 + ([] if final else [plane] * 2),
-        in_specs=[VMEM] * 9,
-        out_specs=[VMEM] * (4 if final else 6),
-        compiler_params=pltpu.CompilerParams(vmem_limit_bytes=48 * 2**20),
+        body,
+        out_shape=[jax.ShapeDtypeStruct(shape, f32) for shape in outputs],
+        in_specs=[VMEM] * len(inputs) + [pl.BlockSpec(memory_space=pl.ANY)] * len(ready),
+        out_specs=[VMEM] * len(outputs),
+        compiler_params=pltpu.CompilerParams(vmem_limit_bytes=SCOPED),
         cost_estimate=pl.CostEstimate(
             flops=30 * cells, bytes_accessed=32 * cells, transcendentals=0
         ),
-        name="substep",
-    )(*fields, low, high, diffusivity, binding, source)
+        name=kernel.__name__.removesuffix("_kernel"),
+    )(*inputs, *ready)
 
 
 def weights_kernel(place, owner, obs_index, observed, obs_var, omega, eta):
@@ -157,13 +209,13 @@
         out_shape=[out, out],
         in_specs=[SMEM, SMEM, VMEM, VMEM, VMEM],
         out_specs=[VMEM, VMEM],
-        compiler_params=pltpu.CompilerParams(vmem_limit_bytes=32 * 2**20),
+        compiler_params=pltpu.CompilerParams(vmem_limit_bytes=SCOPED),
         name="voxel_weights",
     )(place, owner, obs_index, observed, obs_var)
 
 
 def gram_kernel(place, owner, omega, eta, *refs, offsets):
-    *sources, out, members_at = refs
+    *sources, packed, out, members_at = refs
     count = out.shape[0]
     nx, nz, rows, ny = sources[0].shape
     members = members_at.shape[0]
@@ -190,6 +242,18 @@
 
             out[k] = lax.fori_loop(0, nx * nz, tile, jnp.zeros(out.shape[1:], f32), unroll=4)
 
+    row = lax.broadcasted_iota(jnp.int32, (members, LANES), 0)
+    column = lax.broadcasted_iota(jnp.int32, (members, LANES), 1)
+    above, below = out[0], out[1]
+
+    def pick(where, x):
+        return jnp.sum(jnp.where(where, x, 0.0), axis=1, keepdims=True)
+
+    both = jnp.where(column >= row, above, below)
+    both = jnp.where(column == members, pick(column == row, below), both)
+    both = jnp.where(column == members + 1, pick(column == members, above), both)
+    packed[...] = jnp.where(column == members + 2, pick(column == members, below), both)
+
 
 def gram(place, owner, omega, eta, sources, offsets):
     nx, nz, rows, ny = sources[0].shape
@@ -197,11 +261,11 @@
     count = omega.shape[0]
     return pl.pallas_call(
         functools.partial(gram_kernel, offsets=offsets),
-        out_shape=jax.ShapeDtypeStruct((count, members, LANES), f32),
+        out_shape=jax.ShapeDtypeStruct((members, LANES), f32),
         in_specs=[SMEM, SMEM, VMEM, VMEM] + [VMEM] * len(sources),
         out_specs=VMEM,
-        scratch_shapes=[pltpu.VMEM((members, ny), f32)],
-        compiler_params=pltpu.CompilerParams(vmem_limit_bytes=32 * 2**20),
+        scratch_shapes=[pltpu.VMEM((count, members, LANES), f32), pltpu.VMEM((members, ny), f32)],
+        compiler_params=pltpu.CompilerParams(vmem_limit_bytes=SCOPED),
         name="gram",
     )(place, owner, omega, eta, *sources)
 
@@ -251,19 +315,28 @@
 
 
 def transform_kernel(place, mine, other, out, ordered, work, *, offsets, blocks, rows):
-    count, members = mine.shape[0], mine.shape[1]
-    half = place[0]
-    for k in range(count):
-        ordered[half * count + k] = mine[k]
-        ordered[(1 - half) * count + k] = other[k]
+    members = mine.shape[0]
     row = lax.broadcasted_iota(jnp.int32, (LANES, LANES), 0)
     column = lax.broadcasted_iota(jnp.int32, (LANES, LANES), 1)
+    rest = jnp.zeros((LANES - members, LANES), f32)
+
+    def pick(where, x):
+        return jnp.sum(jnp.where(where, x, 0.0), axis=1, keepdims=True)
+
+    for half, shared in ((place[0], mine), (1 - place[0], other)):
+        packed = jnp.concatenate([shared[...], rest], axis=0)
+        inside = column < members
+        above = jnp.where(inside & (column > row), packed, 0.0)
+        below = jnp.where(inside & (column < row), packed, 0.0)
+        middle = jnp.where(inside & (column == row), packed, 0.0)
+        side = jnp.where(column == members, pick(column == members + 1, packed), 0.0)
+        ordered[2 * half] = above + above.T + (middle + side)
+        middle = jnp.where(inside & (column == row), pick(column == members, packed), 0.0)
+        side = jnp.where(column == members, pick(column == members + 2, packed), 0.0)
+        ordered[2 * half + 1] = below + below.T + (middle + side)
     total = jnp.where((row == column) & (row < members), 1.0, 0.0)
-    for batch in range(2 * count):
-        extended = jnp.concatenate(
-            [ordered[batch], jnp.zeros((LANES - members, LANES), f32)], axis=0
-        )
-        total = batch_transform(extended, total, members)
+    for batch in range(ordered.shape[0]):
+        total = batch_transform(ordered[batch], total, members)
     work[...] = total
     if blocks == 1:
         out[...] = total.T
@@ -277,7 +350,7 @@
 
 
 def transforms(place, mine, other, offsets, blocks, rows):
-    count, members, _ = mine.shape
+    members = mine.shape[0]
     shape = (LANES, LANES) if blocks == 1 else (rows, LANES)
     return pl.pallas_call(
         functools.partial(transform_kernel, offsets=offsets, blocks=blocks, rows=rows),
@@ -285,10 +358,10 @@
         in_specs=[SMEM, VMEM, VMEM],
         out_specs=VMEM,
         scratch_shapes=[
-            pltpu.VMEM((2 * count, members, LANES), f32),
+            pltpu.VMEM((4, LANES, LANES), f32),
             pltpu.VMEM((LANES, LANES), f32),
         ],
-        compiler_params=pltpu.CompilerParams(vmem_limit_bytes=32 * 2**20),
+        compiler_params=pltpu.CompilerParams(vmem_limit_bytes=SCOPED),
         cost_estimate=pl.CostEstimate(
             flops=10**10, bytes_accessed=10**6, transcendentals=0
         ),
@@ -299,6 +372,7 @@
 def mix_kernel(weights, *refs, blocks):
     *sources, out = refs
     rows, species, _, nz, ny = out.shape
+    x = pl.program_id(0)
     members = blocks * sources[0].shape[2]
     high, low = split(weights[:, :members])
     both = jnp.concatenate([high.astype(f32), low.astype(f32)], axis=0).astype(bf16)
@@ -308,11 +382,12 @@
     for z in range(nz):
         mixed = []
         for kind in range(species):
-            parts = [sources[kind * blocks + j][0, z] for j in range(blocks)]
+            parts = [sources[kind * blocks + j][x, z] for j in range(blocks)]
             values = parts[0] if blocks == 1 else jnp.concatenate(parts, axis=0)
             value_high, value_low = split(values)
             upper = mul(both, value_high)
             mixed.append(upper[:rows] + (upper[rows:] + mul(high, value_low)))
+        mixed[1] = mixed[1] - mixed[2]
         mixed[2] = mixed[2] - mixed[3]
         for kind in range(species):
             out[:, kind, 0, z, :] = mixed[kind]
@@ -321,14 +396,13 @@
 def mix(weights, sources, blocks, rows):
     nx, nz, held, ny = sources[0].shape
     species = len(sources) // blocks
-    block = pl.BlockSpec((1, nz, held, ny), lambda x: (x, 0, 0, 0))
     return pl.pallas_call(
         functools.partial(mix_kernel, blocks=blocks),
         grid=(nx,),
         out_shape=jax.ShapeDtypeStruct((rows, species, nx, nz, ny), f32),
-        in_specs=[pl.BlockSpec(weights.shape, lambda x: (0, 0))] + [block] * len(sources),
+        in_specs=[VMEM] * (1 + len(sources)),
         out_specs=pl.BlockSpec((rows, species, 1, nz, ny), lambda x: (0, 0, x, 0, 0)),
-        compiler_params=pltpu.CompilerParams(vmem_limit_bytes=32 * 2**20),
+        compiler_params=pltpu.CompilerParams(vmem_limit_bytes=SCOPED),
         name="mix",
     )(weights, *sources)
 
@@ -336,6 +410,14 @@
 def swap(x, axis, bit):
     count = lax.axis_size(axis)
     return lax.ppermute(x, axis, [(k, k ^ bit) for k in range(count)])
+
+
+def total_over(x, axis):
+    bit = 1
+    while bit < lax.axis_size(axis):
+        x = x + swap(x, axis, bit)
+        bit *= 2
+    return x
 
 
 def local(ensemble, diffusivity, binding, source, obs_index, owner, observed, obs_var):
@@ -349,47 +431,79 @@
 
     forward = [(k, k + 1) for k in range(spaces - 1)]
     backward = [(k + 1, k) for k in range(spaces - 1)]
+
+    def halos(first, last):
+        return lax.ppermute(last, "space", forward), lax.ppermute(first, "space", backward)
+
+    if devices == 4 and rows % 8 == 0:
+        blocks = devices
+
+        def offsets(position, j):
+            return jnp.bitwise_xor(position, j) * rows
+
+        def collect(x):
+            return [x, swap(x, "member", 1), swap(x, "member", 2)]
+
+        def complete(held, *after):
+            return [*held, swap(lax.optimization_barrier((held[2], *after))[0], "member", 1)]
+    else:
+        blocks = 1
+
+        def offsets(position, j):
+            return 0
+
+        def collect(x):
+            return [lax.all_gather(x, "member", axis=2, tiled=True)]
+
+        def complete(held, *after):
+            return held
+
+    whole, plane = (nx, nz, rows, ny), (nz, rows, ny)
+    coefficients = (diffusivity, binding, source)
+    around = halos(
+        jnp.transpose(ensemble[:, 0, 0], (1, 0, 2)), jnp.transpose(ensemble[:, 0, -1], (1, 0, 2))
+    )
     fields = [jnp.transpose(ensemble[:, k], (1, 2, 0, 3)) for k in range(species)]
-    first, last = fields[0][0], fields[0][-1]
+    conserved = fields[1] + fields[2] + fields[3]
     omega, eta = voxel_weights(
         place, owner, obs_index, observed, obs_var, batches // 2, nx * nz, ny
     )
-    for step in range(SUBSTEPS):
-        low = lax.ppermute(last, "space", forward)
-        high = lax.ppermute(first, "space", backward)
-        final = step == SUBSTEPS - 1
-        *fields, = substep(fields, low, high, diffusivity, binding, source, final)
-        if not final:
-            first, last = fields[4:]
-            fields = fields[:4]
-    free, receptor, tracer, internal = fields
-
-    if devices == 4 and rows % 8 == 0:
-        blocks = devices
-
-        def offsets(position, j):
-            return jnp.bitwise_xor(position, j) * rows
-
-        def collect(x):
-            across = swap(x, "member", 2)
-            return [x, swap(x, "member", 1), across, swap(across, "member", 1)]
-    else:
-        blocks = 1
-
-        def offsets(position, j):
-            return 0
-
-        def collect(x):
-            return [lax.all_gather(x, "member", axis=2, tiled=True)]
-
-    tracers = collect(tracer)
-    half = gram(place, owner, omega, eta, tracers, offsets)
-    half = jnp.sum(lax.all_gather(half, "space", axis=0), axis=0)
+    for step in range(SUBSTEPS - 2):
+        if step == 1:
+            conserved = collect(lax.optimization_barrier((conserved, fields[0]))[0])
+            ready = (omega, eta)
+        elif step == 3:
+            ready = conserved[1:]
+        else:
+            ready = ()
+        next_edges = forecast_call(
+            edges_kernel, [*fields[:3], *around, *coefficients], [plane] * 2, 2 / nx
+        )
+        fields_now, around_now = fields, around
+        around = halos(*next_edges)
+        fields = forecast_call(
+            substep_kernel,
+            [*fields_now, *around_now, *coefficients],
+            [whole] * 4,
+            ready=ready,
+        )
+    conserved = complete(conserved, fields[0])
+    free, add, tracer, internal = forecast_call(
+        last_but_one_kernel, [*fields, *around, *coefficients], [whole] * 4
+    )
+    around = halos(free[0], free[-1])
+    (free,) = forecast_call(last_free_kernel, [free, add, *around, diffusivity], [whole])
+
+    tracer = complete(collect(tracer))
+    internal = collect(internal)
+    free = collect(free)
+    half = total_over(gram(place, owner, omega, eta, tracer, offsets), "space")
     weights = transforms(place, half, swap(half, "member", 1), offsets, blocks, rows)
+    internal = complete(internal, weights)
+    free = complete(free, weights)
     if blocks == 1:
         weights = lax.dynamic_slice(weights, (member * rows, 0), (rows, LANES))
-    sources = collect(free) + collect(receptor) + tracers + collect(internal)
-    return mix(weights, sources, blocks, rows)
+    return mix(weights, free + conserved + tracer + internal, blocks, rows)
 
 
 def solution(mesh):

time: 187 us -> 151 us (0.81)
  blocking collectives: 35.8 us -> 0 us
  starting transfers between devices: 40 us -> 50.9 us
  Pallas kernels: 50.3 us -> 40.7 us
    all_gather x1 -> x0, blocking collectives: 35.8 us -> none  [local(): half = jnp.sum(lax.all_gather(half, 'space', axis=0), axis=0)]
    ppermute x13 -> x16, starting transfers between devices: 6.88 us -> 16.8 us  [swap(): return lax.ppermute(x, axis, [(k, k ^ bit) for k in range(count)])]
    ppermute x12, waiting for transfers between devices: 27.7 us -> 18.3 us  [the longest x6 15.3 us: halos(): lax.ppermute(first, 'space', backward)]
    ppermute x13 -> x16, waiting for transfers between devices: 20.8 us -> 29.6 us  [swap(): return lax.ppermute(x, axis, [(k, k ^ bit) for k in range(count)])]
    pallas_call x6 -> x10, Pallas kernels: 12.7 us -> 5.85 us  [forecast_call(): pl.pallas_call(body, out_shape=[jax.ShapeDtypeStruct(shape, f32) for shap...]
    pallas_call x1, Pallas kernels: 8.14 us -> 5.15 us  [mix(): pl.pallas_call(functools.partial(mix_kernel, blocks=blocks), grid=(nx,),...]
    unnamed x26 -> x32, local copies, waits for them, and re-layouts: 5.32 us -> 3.27 us
  transfers between devices with their start and end apart: 25 -> 28, of which waited for: 13 -> 14; matrix products, arithmetic and copies ran while one was open for 2% -> 4% of each run, Pallas kernels for 16% -> 22%
where the time goes in v2:
time: 151 us; the launch traced here: 150 us
  starting transfers between devices  50.9 us (34%)
  waiting for transfers between devices  47.9 us (32%)
  Pallas kernels  40.7 us (27%)
  local copies, waits for them, and re-layouts  8.91 us (6%)
  other arithmetic  1.55 us (1%)
    ppermute x16, waiting for transfers between devices, swap(): return lax.ppermute(x, axis, [(k, k ^ bit) for k in range(count)])  29.6 us
    pallas_call x1, Pallas kernels, transforms(): pl.pallas_call(functools.partial(transform_kernel, offsets=offsets, block...  27.6 us
    ppermute x6, starting transfers between devices, halos(): lax.ppermute(last, 'space', forward)  26.2 us
    ppermute x16, starting transfers between devices, swap(): return lax.ppermute(x, axis, [(k, k ^ bit) for k in range(count)])  16.8 us
    ppermute x6, waiting for transfers between devices, halos(): lax.ppermute(first, 'space', backward)  15.3 us
    ppermute x6, starting transfers between devices, halos(): lax.ppermute(first, 'space', backward)  7.93 us
    pallas_call x10, Pallas kernels, forecast_call(): pl.pallas_call(body, out_shape=[jax.ShapeDtypeStruct(shape, f32) for shap...  5.85 us
    pallas_call x1, Pallas kernels, mix(): pl.pallas_call(functools.partial(mix_kernel, blocks=blocks), grid=(nx,),...  5.15 us
  transfers between devices with their start and end apart: 28, of which 14 were waited for; matrix products, arithmetic and copies ran while one was open for 4% of the time, Pallas kernels for 22%

profile of v2, /device:TPU:0, one launch (start us, length us, event | category | flops | bytes accessed | tf_op | source)
XLA Modules:
  0.0 150.4 jit_solution(11464879379667337848)
XLA Ops:
  0.0 1.0 fusion
  1.0 4.8 %collective-permute-start = (f32[4,24,256]{2,1,0:T(8,128)S(1)}, f32[4,24,256]{2,1,0:T(8,128)S(1)}, u32[]{:S(2)}, u32[]{:S(2)}) collective-permute-start(f32[4,24,256]{2,1,0:T(8,128)S(1)} %bitcast.39), channel_id=1, source_target_pairs={{0,1},{1,2},{2,3},{3,4},{4,5},{5,6},{6,7},{8,9},{9,10},{10,11},{11... | collective-permute-start | bytes 294920 | tf_op jit(solution)/shard_map/ppermute | solution.py:436
  5.9 1.3 collective-permute-start.1
  7.2 2.4 %fusion.1 = (f32[24,1,8,4,256]{4,3,2,1,0:T(4,128)S(1)}, f32[24,1,8,4,256]{4,3,2,1,0:T(4,128)S(1)}, f32[24,1,8,4,256]{4,3,2,1,0:T(4,128)S(1)}, f32[24,1,8,4,256]{4,3,2,1,0:T(4,128)S(1)}) fusion(f32[24,4,8,4,256]{4,3,2,1,0:T(4,128)} %param.8), kind=kLoop, calls=%fused_computation.11 | loop fusion | bytes 6291456 | tf_op jit(solution)/shard_map/slice | solution.py:466
  9.6 1.1 copy_bitcast_fusion
  10.7 0.0 copy-start
  10.7 0.0 copy-start.7
  10.7 0.0 copy-start.8
  10.8 1.4 add_add_fusion.refs_4_
  12.2 1.1 copy_bitcast_fusion.2
  13.4 0.7 substep.4
  14.1 0.9 copy-done.4
  15.1 0.0 copy-start.14
  15.1 1.6 %collective-permute-start.9 = (f32[8,4,24,256]{3,2,1,0:T(8,128)S(1)}, f32[8,4,24,256]{3,2,1,0:T(8,128)S(1)}, u32[]{:S(2)}, u32[]{:S(2)}) collective-permute-start(f32[8,4,24,256]{3,2,1,0:T(8,128)S(1)} %add_add_fusion.refs_4_), channel_id=1, source_target_pairs={{0,16},{8,24},{16,0},{24,8},{1,17},{9,25},{17,1},{25,9},{2,18},{10... | collective-permute-start | bytes 2359304 | tf_op jit(solution)/shard_map/ppermute | solution.py:412
  16.7 0.8 edges.4
  17.5 4.5 %collective-permute-start.2 = (f32[4,24,256]{2,1,0:T(8,128)}, f32[4,24,256]{2,1,0:T(8,128)S(1)}, u32[]{:S(2)}, u32[]{:S(2)}) collective-permute-start(f32[4,24,256]{2,1,0:T(8,128)} %get-tuple-element.45), channel_id=1, source_target_pairs={{0,1},{1,2},{2,3},{3,4},{4,5},{5,6},{6,7},{8,9},{9,10},{10,11},{11... | collective-permute-start | bytes 294920 | tf_op jit(solution)/shard_map/ppermute | solution.py:436
  22.0 1.3 collective-permute-start.3
  23.4 1.7 %collective-permute-done.2.refs_4_.refs_3_ = f32[4,24,256]{2,1,0:T(8,128)S(1)} collective-permute-done((f32[4,24,256]{2,1,0:T(8,128)}, f32[4,24,256]{2,1,0:T(8,128)S(1)}, u32[]{:S(2)}, u32[]{:S(2)}) %collective-permute-start.2) | collective-permute-done | bytes 98336 | tf_op jit(solution)/shard_map/ppermute | solution.py:436
  25.1 4.7 %collective-permute-done.3.refs_5_.refs_4_ = f32[4,24,256]{2,1,0:T(8,128)S(1)} collective-permute-done((f32[4,24,256]{2,1,0:T(8,128)}, f32[4,24,256]{2,1,0:T(8,128)S(1)}, u32[]{:S(2)}, u32[]{:S(2)}) %collective-permute-start.3) | collective-permute-done | bytes 98336 | tf_op jit(solution)/shard_map/ppermute | solution.py:436
  29.8 1.1 copy-done.2
  30.9 1.1 copy-done.5
  32.1 0.2 edges.5
  32.2 4.7 %collective-permute-start.4 = (f32[4,24,256]{2,1,0:T(8,128)S(1)}, f32[4,24,256]{2,1,0:T(8,128)S(1)}, u32[]{:S(2)}, u32[]{:S(2)}) collective-permute-start(f32[4,24,256]{2,1,0:T(8,128)S(1)} %get-tuple-element.51), channel_id=1, source_target_pairs={{0,1},{1,2},{2,3},{3,4},{4,5},{5,6},{6,7},{8,9},{9,10},{10,11},{11... | collective-permute-start | bytes 294920 | tf_op jit(solution)/shard_map/ppermute | solution.py:436
  36.9 1.3 collective-permute-start.5
  38.2 0.1 pad_add_fusion.place
  38.3 1.4 voxel_weights.1
  39.8 0.7 substep.5
  40.5 2.9 %collective-permute-done.5.refs_5_.refs_4_ = f32[4,24,256]{2,1,0:T(8,128)S(1)} collective-permute-done((f32[4,24,256]{2,1,0:T(8,128)S(1)}, f32[4,24,256]{2,1,0:T(8,128)S(1)}, u32[]{:S(2)}, u32[]{:S(2)}) %collective-permute-start.5) | collective-permute-done | bytes 98336 | tf_op jit(solution)/shard_map/ppermute | solution.py:436
  43.4 0.2 edges.6
  43.6 3.3 %collective-permute-start.6 = (f32[4,24,256]{2,1,0:T(8,128)S(1)}, f32[4,24,256]{2,1,0:T(8,128)S(1)}, u32[]{:S(2)}, u32[]{:S(2)}) collective-permute-start(f32[4,24,256]{2,1,0:T(8,128)S(1)} %get-tuple-element.57), channel_id=1, source_target_pairs={{0,1},{1,2},{2,3},{3,4},{4,5},{5,6},{6,7},{8,9},{9,10},{10,11},{11... | collective-permute-start | bytes 294920 | tf_op jit(solution)/shard_map/ppermute | solution.py:436
  46.9 1.3 collective-permute-start.7
  48.2 0.7 substep.6
  48.9 0.2 collective-permute-done.6.refs_4_.refs_3_
  49.1 4.3 %collective-permute-done.7.refs_5_.refs_4_ = f32[4,24,256]{2,1,0:T(8,128)S(1)} collective-permute-done((f32[4,24,256]{2,1,0:T(8,128)S(1)}, f32[4,24,256]{2,1,0:T(8,128)S(1)}, u32[]{:S(2)}, u32[]{:S(2)}) %collective-permute-start.7) | collective-permute-done | bytes 98336 | tf_op jit(solution)/shard_map/ppermute | solution.py:436
  53.4 0.2 edges.7
  53.6 4.5 %collective-permute-start.10 = (f32[4,24,256]{2,1,0:T(8,128)S(1)}, f32[4,24,256]{2,1,0:T(8,128)S(1)}, u32[]{:S(2)}, u32[]{:S(2)}) collective-permute-start(f32[4,24,256]{2,1,0:T(8,128)S(1)} %get-tuple-element.64), channel_id=1, source_target_pairs={{0,1},{1,2},{2,3},{3,4},{4,5},{5,6},{6,7},{8,9},{9,10},{10,11},{11... | collective-permute-start | bytes 294920 | tf_op jit(solution)/shard_map/ppermute | solution.py:436
  58.1 1.3 collective-permute-start.11
  59.4 0.7 substep.7
  60.1 1.1 collective-permute-done.10.refs_4_
  61.3 3.3 %collective-permute-done.11.refs_5_ = f32[4,24,256]{2,1,0:T(8,128)S(1)} collective-permute-done((f32[4,24,256]{2,1,0:T(8,128)S(1)}, f32[4,24,256]{2,1,0:T(8,128)S(1)}, u32[]{:S(2)}, u32[]{:S(2)}) %collective-permute-start.11) | collective-permute-done | bytes 98336 | tf_op jit(solution)/shard_map/ppermute | solution.py:436
  64.6 1.1 last_but_one.1
  65.7 0.6 collective-permute-start.13
  66.3 14.2 %collective-permute-done.13.refs_2_.refs_10_ = f32[8,4,24,256]{3,2,1,0:T(8,128)S(1)} collective-permute-done((f32[8,4,24,256]{3,2,1,0:T(8,128)S(1)}, f32[8,4,24,256]{3,2,1,0:T(8,128)S(1)}, u32[]{:S(2)}, u32[]{:S(2)}) %collective-permute-start.13) | collective-permute-done | bytes 786464 | tf_op jit(solution)/shard_map/ppermute | solution.py:412
  80.5 2.3 %collective-permute-done.14.refs_3_.refs_11_ = f32[8,4,24,256]{3,2,1,0:T(8,128)S(1)} collective-permute-done((f32[8,4,24,256]{3,2,1,0:T(8,128)S(1)}, f32[8,4,24,256]{3,2,1,0:T(8,128)S(1)}, u32[]{:S(2)}, u32[]{:S(2)}) %collective-permute-start.14) | collective-permute-done | bytes 786464 | tf_op jit(solution)/shard_map/ppermute | solution.py:412
  82.8 0.7 gram.1
  83.5 2.8 %collective-permute-start.15 = (f32[96,128]{1,0:T(8,128)S(1)}, f32[96,128]{1,0:T(8,128)S(1)}, u32[]{:S(2)}, u32[]{:S(2)}) collective-permute-start(f32[96,128]{1,0:T(8,128)S(1)} %gram.1), channel_id=1, source_target_pairs={{0,1},{1,0},{2,3},{3,2},{4,5},{5,4},{6,7},{7,6},{8,9},{9,8},{10,11... | collective-permute-start | bytes 147464 | tf_op jit(solution)/shard_map/ppermute | solution.py:412
  86.3 2.1 %collective-permute-done.15 = f32[96,128]{1,0:T(8,128)S(1)} collective-permute-done((f32[96,128]{1,0:T(8,128)S(1)}, f32[96,128]{1,0:T(8,128)S(1)}, u32[]{:S(2)}, u32[]{:S(2)}) %collective-permute-start.15) | collective-permute-done | bytes 49184 | tf_op jit(solution)/shard_map/ppermute | solution.py:412
  88.4 2.2 %collective-permute-start.16 = (f32[96,128]{1,0:T(8,128)S(1)}, f32[96,128]{1,0:T(8,128)S(1)}, u32[]{:S(2)}, u32[]{:S(2)}) collective-permute-start(f32[96,128]{1,0:T(8,128)S(1)} %add.17), channel_id=1, source_target_pairs={{0,2},{1,3},{2,0},{3,1},{4,6},{5,7},{6,4},{7,5},{8,10},{9,11},{10,... | collective-permute-start | bytes 147464 | tf_op jit(solution)/shard_map/ppermute | solution.py:412
  90.6 1.5 collective-permute-start.20
  92.1 4.4 %collective-permute-start.19 = (f32[4,24,256]{2,1,0:T(8,128)S(1)}, f32[4,24,256]{2,1,0:T(8,128)S(1)}, u32[]{:S(2)}, u32[]{:S(2)}) collective-permute-start(f32[4,24,256]{2,1,0:T(8,128)S(1)} %get-tuple-element.80), channel_id=1, source_target_pairs={{0,1},{1,2},{2,3},{3,4},{4,5},{5,6},{6,7},{8,9},{9,10},{10,11},{11... | collective-permute-start | bytes 294920 | tf_op jit(solution)/shard_map/ppermute | solution.py:436
  96.5 6.4 %collective-permute-start.17 = (f32[96,128]{1,0:T(8,128)S(1)}, f32[96,128]{1,0:T(8,128)S(1)}, u32[]{:S(2)}, u32[]{:S(2)}) collective-permute-start(f32[96,128]{1,0:T(8,128)S(1)} %add.18), channel_id=1, source_target_pairs={{0,4},{1,5},{2,6},{3,7},{4,0},{5,1},{6,2},{7,3},{8,12},{9,13},{10,... | collective-permute-start | bytes 147464 | tf_op jit(solution)/shard_map/ppermute | solution.py:412
  102.9 2.1 %collective-permute-done.17 = f32[96,128]{1,0:T(8,128)S(1)} collective-permute-done((f32[96,128]{1,0:T(8,128)S(1)}, f32[96,128]{1,0:T(8,128)S(1)}, u32[]{:S(2)}, u32[]{:S(2)}) %collective-permute-start.17) | collective-permute-done | bytes 49184 | tf_op jit(solution)/shard_map/ppermute | solution.py:412
  105.0 0.1 collective-permute-start.18
  105.0 0.6 collective-permute-start.26
  105.6 0.2 collective-permute-start.25
  105.8 0.3 collective-permute-start.24
  106.1 0.5 last_free.1.refs_0_
  106.6 1.6 %collective-permute-start.22 = (f32[8,4,24,256]{3,2,1,0:T(8,128)S(1)}, f32[8,4,24,256]{3,2,1,0:T(8,128)S(1)}, u32[]{:S(2)}, u32[]{:S(2)}) collective-permute-start(f32[8,4,24,256]{3,2,1,0:T(8,128)S(1)} %last_free.1.refs_0_), channel_id=1, source_target_pairs={{0,16},{8,24},{16,0},{24,8},{1,17},{9,25},{17,1},{25,9},{2,18},{10... | collective-permute-start | bytes 2359304 | tf_op jit(solution)/shard_map/ppermute | solution.py:412
  108.2 27.6 %transforms.1.weights = f32[24,128]{1,0:T(8,128)S(1)} custom-call(s32[3]{0:T(128)S(1)} %pad_add_fusion.place, f32[96,128]{1,0:T(8,128)S(1)} %add.19.mine, f32[96,128]{1,0:T(8,128)S(1)} %collective-permute-done.18.other), custom_call_target="tpu_custom_call" | custom-call | flops 10000000000 | bytes 1000000 | tf_op jit(solution)/shard_map/transforms/pallas_call | solution.py:355
  135.8 6.0 %collective-permute-done.22.refs_2_ = f32[8,4,24,256]{3,2,1,0:T(8,128)S(1)} collective-permute-done((f32[8,4,24,256]{3,2,1,0:T(8,128)S(1)}, f32[8,4,24,256]{3,2,1,0:T(8,128)S(1)}, u32[]{:S(2)}, u32[]{:S(2)}) %collective-permute-start.22) | collective-permute-done | bytes 786464 | tf_op jit(solution)/shard_map/ppermute | solution.py:412
  141.8 0.5 collective-permute-start.27
  142.4 1.8 %collective-permute-done.23.refs_3_ = f32[8,4,24,256]{3,2,1,0:T(8,128)S(1)} collective-permute-done((f32[8,4,24,256]{3,2,1,0:T(8,128)S(1)}, f32[8,4,24,256]{3,2,1,0:T(8,128)S(1)}, u32[]{:S(2)}, u32[]{:S(2)}) %collective-permute-start.23) | collective-permute-done | bytes 786464 | tf_op jit(solution)/shard_map/ppermute | solution.py:412
  144.1 1.1 collective-permute-done.27.refs_15_
  145.3 5.1 %mix.1 = f32[24,4,8,4,256]{4,3,2,1,0:T(4,128)} custom-call(f32[24,128]{1,0:T(8,128)S(1)} %transforms.1.weights, f32[8,4,24,256]{3,2,1,0:T(8,128)S(1)} %last_free.1.refs_0_, f32[8,4,24,256]{3,2,1,0:T(8,128)S(1)} %collective-permute-done.21.refs_1_, f32[8,4,24,256]{3,2,1,0:T(8,128)S(1)} %collective-permute-done.22.refs_2_, ...), custom_call_target="tpu_custom_call" | custom-call | tf_op jit(solution)/shard_map/mix/pallas_call | solution.py:399
  (48 shorter events, 0.2 us)
Async XLA Ops:
  1.0 12.4 %collective-permute-start = (f32[4,24,256]{2,1,0:T(8,128)S(1)}, f32[4,24,256]{2,1,0:T(8,128)S(1)}, u32[]{:S(2)}, u32[]{:S(2)}) collective-permute-start(f32[4,24,256]{2,1,0:T(8,128)S(1)} %bitcast.39), channel_id=1, source_target_pairs={{0,1},{1,2},{2,3},{3,4},{4,5},{5,6},{6,7},{8,9},{9,10},{10,11},{11... | collective-permute-start | bytes 294920 | tf_op jit(solution)/shard_map/ppermute | solution.py:436
  5.9 7.5 %collective-permute-start.1 = (f32[4,24,256]{2,1,0:T(8,128)S(1)}, f32[4,24,256]{2,1,0:T(8,128)S(1)}, u32[]{:S(2)}, u32[]{:S(2)}) collective-permute-start(f32[4,24,256]{2,1,0:T(8,128)S(1)} %bitcast.40), channel_id=1, source_target_pairs={{1,0},{2,1},{3,2},{4,3},{5,4},{6,5},{7,6},{9,8},{10,9},{11,10},{12... | collective-permute-start | bytes 294920 | tf_op jit(solution)/shard_map/ppermute | solution.py:436
  10.7 2.6 %copy-start = (f32[8,4,256]{2,1,0:T(4,128)S(1)}, f32[8,4,256]{2,1,0:T(4,128)}, u32[]{:S(2)}) copy-start(f32[8,4,256]{2,1,0:T(4,128)} %refs_4_.1) | copy-start | bytes 98308
  10.7 2.6 %copy-start.7 = (f32[8,4,256]{2,1,0:T(4,128)S(1)}, f32[8,4,256]{2,1,0:T(4,128)}, u32[]{:S(2)}) copy-start(f32[8,4,256]{2,1,0:T(4,128)} %refs_7_.17) | copy-start | bytes 98308
  10.7 2.6 %copy-start.8 = (f32[8,4,256]{2,1,0:T(4,128)S(1)}, f32[8,4,256]{2,1,0:T(4,128)}, u32[]{:S(2)}) copy-start(f32[8,4,256]{2,1,0:T(4,128)} %refs_8_.9) | copy-start | bytes 98308
  14.1 0.9 copy-start.4
  15.0 2.5 %copy-start.1 = (f32[8,4,24,256]{3,2,1,0:T(8,128)}, f32[8,4,24,256]{3,2,1,0:T(8,128)S(1)}, u32[]{:S(2)}) copy-start(f32[8,4,24,256]{3,2,1,0:T(8,128)S(1)} %get-tuple-element.42.refs_1_) | copy-start | bytes 2359300
  15.0 2.5 %copy-start.9 = (f32[8,4,24,256]{3,2,1,0:T(8,128)}, f32[8,4,24,256]{3,2,1,0:T(8,128)S(1)}, u32[]{:S(2)}) copy-start(f32[8,4,24,256]{3,2,1,0:T(8,128)S(1)} %get-tuple-element.44.refs_3_) | copy-start | bytes 2359300
  15.0 23.3 %copy-start.11 = (s32[4,2048]{1,0:T(4,128)S(1)}, s32[4,2048]{1,0:T(4,128)}, u32[]{:S(2)}) copy-start(s32[4,2048]{1,0:T(4,128)} %obs_index.1) | copy-start | bytes 98308
  15.0 23.3 %copy-start.12 = (f32[4,2048]{1,0:T(4,128)S(1)}, f32[4,2048]{1,0:T(4,128)}, u32[]{:S(2)}) copy-start(f32[4,2048]{1,0:T(4,128)} %observed.1) | copy-start | bytes 98308
  15.0 23.3 %copy-start.13 = (f32[4,2048]{1,0:T(4,128)S(1)}, f32[4,2048]{1,0:T(4,128)}, u32[]{:S(2)}) copy-start(f32[4,2048]{1,0:T(4,128)} %obs_var.1) | copy-start | bytes 98308
  15.1 23.3 %copy-start.14 = (s32[4]{0:T(128)S(1)}, s32[4]{0:T(128)}, u32[]{:S(2)}) copy-start(s32[4]{0:T(128)} %owner.3) | copy-start | bytes 52
  15.1 44.3 %collective-permute-start.9 = (f32[8,4,24,256]{3,2,1,0:T(8,128)S(1)}, f32[8,4,24,256]{3,2,1,0:T(8,128)S(1)}, u32[]{:S(2)}, u32[]{:S(2)}) collective-permute-start(f32[8,4,24,256]{3,2,1,0:T(8,128)S(1)} %add_add_fusion.refs_4_), channel_id=1, source_target_pairs={{0,16},{8,24},{16,0},{24,8},{1,17},{9,25},{17,1},{25,9},{2,18},{10... | collective-permute-start | bytes 2359304 | tf_op jit(solution)/shard_map/ppermute | solution.py:412
  16.7 42.8 %collective-permute-start.8 = (f32[8,4,24,256]{3,2,1,0:T(8,128)S(1)}, f32[8,4,24,256]{3,2,1,0:T(8,128)S(1)}, u32[]{:S(2)}, u32[]{:S(2)}) collective-permute-start(f32[8,4,24,256]{3,2,1,0:T(8,128)S(1)} %add_add_fusion.refs_4_), channel_id=1, source_target_pairs={{0,8},{8,0},{16,24},{24,16},{1,9},{9,1},{17,25},{25,17},{2,10},{10... | collective-permute-start | bytes 2359304 | tf_op jit(solution)/shard_map/ppermute | solution.py:412
  17.5 7.6 %collective-permute-start.2 = (f32[4,24,256]{2,1,0:T(8,128)}, f32[4,24,256]{2,1,0:T(8,128)S(1)}, u32[]{:S(2)}, u32[]{:S(2)}) collective-permute-start(f32[4,24,256]{2,1,0:T(8,128)} %get-tuple-element.45), channel_id=1, source_target_pairs={{0,1},{1,2},{2,3},{3,4},{4,5},{5,6},{6,7},{8,9},{9,10},{10,11},{11... | collective-permute-start | bytes 294920 | tf_op jit(solution)/shard_map/ppermute | solution.py:436
  22.0 7.7 %collective-permute-start.3 = (f32[4,24,256]{2,1,0:T(8,128)}, f32[4,24,256]{2,1,0:T(8,128)S(1)}, u32[]{:S(2)}, u32[]{:S(2)}) collective-permute-start(f32[4,24,256]{2,1,0:T(8,128)} %get-tuple-element.46), channel_id=1, source_target_pairs={{1,0},{2,1},{3,2},{4,3},{5,4},{6,5},{7,6},{9,8},{10,9},{11,10},{12... | collective-permute-start | bytes 294920 | tf_op jit(solution)/shard_map/ppermute | solution.py:436
  29.8 1.1 copy-start.2
  30.9 1.1 copy-start.5
  32.1 7.7 %copy-start.3 = (f32[8,4,24,256]{3,2,1,0:T(8,128)S(1)}, f32[8,4,24,256]{3,2,1,0:T(8,128)}, u32[]{:S(2)}) copy-start(f32[8,4,24,256]{3,2,1,0:T(8,128)} %copy-done.1) | copy-start | bytes 2359300
  32.1 7.7 %copy-start.6 = (f32[8,4,24,256]{3,2,1,0:T(8,128)S(1)}, f32[8,4,24,256]{3,2,1,0:T(8,128)}, u32[]{:S(2)}) copy-start(f32[8,4,24,256]{3,2,1,0:T(8,128)} %copy-done.4) | copy-start | bytes 2359300
  32.1 7.7 %copy-start.10 = (f32[8,4,24,256]{3,2,1,0:T(8,128)S(1)}, f32[8,4,24,256]{3,2,1,0:T(8,128)}, u32[]{:S(2)}) copy-start(f32[8,4,24,256]{3,2,1,0:T(8,128)} %copy-done.9) | copy-start | bytes 2359300
  32.2 8.3 %collective-permute-start.4 = (f32[4,24,256]{2,1,0:T(8,128)S(1)}, f32[4,24,256]{2,1,0:T(8,128)S(1)}, u32[]{:S(2)}, u32[]{:S(2)}) collective-permute-start(f32[4,24,256]{2,1,0:T(8,128)S(1)} %get-tuple-element.51), channel_id=1, source_target_pairs={{0,1},{1,2},{2,3},{3,4},{4,5},{5,6},{6,7},{8,9},{9,10},{10,11},{11... | collective-permute-start | bytes 294920 | tf_op jit(solution)/shard_map/ppermute | solution.py:436
  36.9 6.5 %collective-permute-start.5 = (f32[4,24,256]{2,1,0:T(8,128)S(1)}, f32[4,24,256]{2,1,0:T(8,128)S(1)}, u32[]{:S(2)}, u32[]{:S(2)}) collective-permute-start(f32[4,24,256]{2,1,0:T(8,128)S(1)} %get-tuple-element.52), channel_id=1, source_target_pairs={{1,0},{2,1},{3,2},{4,3},{5,4},{6,5},{7,6},{9,8},{10,9},{11,10},{12... | collective-permute-start | bytes 294920 | tf_op jit(solution)/shard_map/ppermute | solution.py:436
  43.6 5.5 %collective-permute-start.6 = (f32[4,24,256]{2,1,0:T(8,128)S(1)}, f32[4,24,256]{2,1,0:T(8,128)S(1)}, u32[]{:S(2)}, u32[]{:S(2)}) collective-permute-start(f32[4,24,256]{2,1,0:T(8,128)S(1)} %get-tuple-element.57), channel_id=1, source_target_pairs={{0,1},{1,2},{2,3},{3,4},{4,5},{5,6},{6,7},{8,9},{9,10},{10,11},{11... | collective-permute-start | bytes 294920 | tf_op jit(solution)/shard_map/ppermute | solution.py:436
  46.9 6.5 %collective-permute-start.7 = (f32[4,24,256]{2,1,0:T(8,128)S(1)}, f32[4,24,256]{2,1,0:T(8,128)S(1)}, u32[]{:S(2)}, u32[]{:S(2)}) collective-permute-start(f32[4,24,256]{2,1,0:T(8,128)S(1)} %get-tuple-element.58), channel_id=1, source_target_pairs={{1,0},{2,1},{3,2},{4,3},{5,4},{6,5},{7,6},{9,8},{10,9},{11,10},{12... | collective-permute-start | bytes 294920 | tf_op jit(solution)/shard_map/ppermute | solution.py:436
  53.6 7.6 %collective-permute-start.10 = (f32[4,24,256]{2,1,0:T(8,128)S(1)}, f32[4,24,256]{2,1,0:T(8,128)S(1)}, u32[]{:S(2)}, u32[]{:S(2)}) collective-permute-start(f32[4,24,256]{2,1,0:T(8,128)S(1)} %get-tuple-element.64), channel_id=1, source_target_pairs={{0,1},{1,2},{2,3},{3,4},{4,5},{5,6},{6,7},{8,9},{9,10},{10,11},{11... | collective-permute-start | bytes 294920 | tf_op jit(solution)/shard_map/ppermute | solution.py:436
  58.1 6.5 %collective-permute-start.11 = (f32[4,24,256]{2,1,0:T(8,128)S(1)}, f32[4,24,256]{2,1,0:T(8,128)S(1)}, u32[]{:S(2)}, u32[]{:S(2)}) collective-permute-start(f32[4,24,256]{2,1,0:T(8,128)S(1)} %get-tuple-element.65), channel_id=1, source_target_pairs={{1,0},{2,1},{3,2},{4,3},{5,4},{6,5},{7,6},{9,8},{10,9},{11,10},{12... | collective-permute-start | bytes 294920 | tf_op jit(solution)/shard_map/ppermute | solution.py:436
  65.7 14.8 %collective-permute-start.13 = (f32[8,4,24,256]{3,2,1,0:T(8,128)S(1)}, f32[8,4,24,256]{3,2,1,0:T(8,128)S(1)}, u32[]{:S(2)}, u32[]{:S(2)}) collective-permute-start(f32[8,4,24,256]{3,2,1,0:T(8,128)S(1)} %get-tuple-element.66.refs_0_.refs_8_), channel_id=1, source_target_pairs={{0,16},{8,24},{16,0},{24,8},{1,17},{9,25},{17,1},{25,9},{2,18},{10... | collective-permute-start | bytes 2359304 | tf_op jit(solution)/shard_map/ppermute | solution.py:412
  66.3 14.2 %collective-permute-start.12 = (f32[8,4,24,256]{3,2,1,0:T(8,128)S(1)}, f32[8,4,24,256]{3,2,1,0:T(8,128)S(1)}, u32[]{:S(2)}, u32[]{:S(2)}) collective-permute-start(f32[8,4,24,256]{3,2,1,0:T(8,128)S(1)} %get-tuple-element.66.refs_0_.refs_8_), channel_id=1, source_target_pairs={{0,8},{8,0},{16,24},{24,16},{1,9},{9,1},{17,25},{25,17},{2,10},{10... | collective-permute-start | bytes 2359304 | tf_op jit(solution)/shard_map/ppermute | solution.py:412
  80.5 2.3 %collective-permute-start.14 = (f32[8,4,24,256]{3,2,1,0:T(8,128)S(1)}, f32[8,4,24,256]{3,2,1,0:T(8,128)S(1)}, u32[]{:S(2)}, u32[]{:S(2)}) collective-permute-start(f32[8,4,24,256]{3,2,1,0:T(8,128)S(1)} %collective-permute-done.13.refs_2_.refs_10_), channel_id=1, source_target_pairs={{0,8},{8,0},{16,24},{24,16},{1,9},{9,1},{17,25},{25,17},{2,10},{10... | collective-permute-start | bytes 2359304 | tf_op jit(solution)/shard_map/ppermute | solution.py:412
  83.5 4.9 %collective-permute-start.15 = (f32[96,128]{1,0:T(8,128)S(1)}, f32[96,128]{1,0:T(8,128)S(1)}, u32[]{:S(2)}, u32[]{:S(2)}) collective-permute-start(f32[96,128]{1,0:T(8,128)S(1)} %gram.1), channel_id=1, source_target_pairs={{0,1},{1,0},{2,3},{3,2},{4,5},{5,4},{6,7},{7,6},{8,9},{9,8},{10,11... | collective-permute-start | bytes 147464 | tf_op jit(solution)/shard_map/ppermute | solution.py:412
  88.4 8.1 %collective-permute-start.16 = (f32[96,128]{1,0:T(8,128)S(1)}, f32[96,128]{1,0:T(8,128)S(1)}, u32[]{:S(2)}, u32[]{:S(2)}) collective-permute-start(f32[96,128]{1,0:T(8,128)S(1)} %add.17), channel_id=1, source_target_pairs={{0,2},{1,3},{2,0},{3,1},{4,6},{5,7},{6,4},{7,5},{8,10},{9,11},{10,... | collective-permute-start | bytes 147464 | tf_op jit(solution)/shard_map/ppermute | solution.py:412
  90.6 15.2 %collective-permute-start.20 = (f32[4,24,256]{2,1,0:T(8,128)S(1)}, f32[4,24,256]{2,1,0:T(8,128)S(1)}, u32[]{:S(2)}, u32[]{:S(2)}) collective-permute-start(f32[4,24,256]{2,1,0:T(8,128)S(1)} %get-tuple-element.79), channel_id=1, source_target_pairs={{1,0},{2,1},{3,2},{4,3},{5,4},{6,5},{7,6},{9,8},{10,9},{11,10},{12... | collective-permute-start | bytes 294920 | tf_op jit(solution)/shard_map/ppermute | solution.py:436
  92.1 14.1 %collective-permute-start.19 = (f32[4,24,256]{2,1,0:T(8,128)S(1)}, f32[4,24,256]{2,1,0:T(8,128)S(1)}, u32[]{:S(2)}, u32[]{:S(2)}) collective-permute-start(f32[4,24,256]{2,1,0:T(8,128)S(1)} %get-tuple-element.80), channel_id=1, source_target_pairs={{0,1},{1,2},{2,3},{3,4},{4,5},{5,6},{6,7},{8,9},{9,10},{10,11},{11... | collective-permute-start | bytes 294920 | tf_op jit(solution)/shard_map/ppermute | solution.py:436
  96.5 8.5 %collective-permute-start.17 = (f32[96,128]{1,0:T(8,128)S(1)}, f32[96,128]{1,0:T(8,128)S(1)}, u32[]{:S(2)}, u32[]{:S(2)}) collective-permute-start(f32[96,128]{1,0:T(8,128)S(1)} %add.18), channel_id=1, source_target_pairs={{0,4},{1,5},{2,6},{3,7},{4,0},{5,1},{6,2},{7,3},{8,12},{9,13},{10,... | collective-permute-start | bytes 147464 | tf_op jit(solution)/shard_map/ppermute | solution.py:412
  105.0 3.3 %collective-permute-start.18 = (f32[96,128]{1,0:T(8,128)S(1)}, f32[96,128]{1,0:T(8,128)S(1)}, u32[]{:S(2)}, u32[]{:S(2)}) collective-permute-start(f32[96,128]{1,0:T(8,128)S(1)} %add.19.mine), channel_id=1, source_target_pairs={{0,8},{8,0},{16,24},{24,16},{1,9},{9,1},{17,25},{25,17},{2,10},{10... | collective-permute-start | bytes 147464 | tf_op jit(solution)/shard_map/ppermute | solution.py:412
  105.0 30.8 %collective-permute-start.26 = (f32[8,4,24,256]{3,2,1,0:T(8,128)S(1)}, f32[8,4,24,256]{3,2,1,0:T(8,128)S(1)}, u32[]{:S(2)}, u32[]{:S(2)}) collective-permute-start(f32[8,4,24,256]{3,2,1,0:T(8,128)S(1)} %get-tuple-element.71.refs_12_), channel_id=1, source_target_pairs={{0,16},{8,24},{16,0},{24,8},{1,17},{9,25},{17,1},{25,9},{2,18},{10... | collective-permute-start | bytes 2359304 | tf_op jit(solution)/shard_map/ppermute | solution.py:412
  105.6 36.7 %collective-permute-start.25 = (f32[8,4,24,256]{3,2,1,0:T(8,128)S(1)}, f32[8,4,24,256]{3,2,1,0:T(8,128)S(1)}, u32[]{:S(2)}, u32[]{:S(2)}) collective-permute-start(f32[8,4,24,256]{3,2,1,0:T(8,128)S(1)} %get-tuple-element.71.refs_12_), channel_id=1, source_target_pairs={{0,8},{8,0},{16,24},{24,16},{1,9},{9,1},{17,25},{25,17},{2,10},{10... | collective-permute-start | bytes 2359304 | tf_op jit(solution)/shard_map/ppermute | solution.py:412
  105.8 36.6 %collective-permute-start.24 = (f32[8,4,24,256]{3,2,1,0:T(8,128)S(1)}, f32[8,4,24,256]{3,2,1,0:T(8,128)S(1)}, u32[]{:S(2)}, u32[]{:S(2)}) collective-permute-start(f32[8,4,24,256]{3,2,1,0:T(8,128)S(1)} %collective-permute-done.9.refs_10_.refs_6_), channel_id=1, source_target_pairs={{0,8},{8,0},{16,24},{24,16},{1,9},{9,1},{17,25},{25,17},{2,10},{10... | collective-permute-start | bytes 2359304 | tf_op jit(solution)/shard_map/ppermute | solution.py:412
  106.6 35.2 %collective-permute-start.22 = (f32[8,4,24,256]{3,2,1,0:T(8,128)S(1)}, f32[8,4,24,256]{3,2,1,0:T(8,128)S(1)}, u32[]{:S(2)}, u32[]{:S(2)}) collective-permute-start(f32[8,4,24,256]{3,2,1,0:T(8,128)S(1)} %last_free.1.refs_0_), channel_id=1, source_target_pairs={{0,16},{8,24},{16,0},{24,8},{1,17},{9,25},{17,1},{25,9},{2,18},{10... | collective-permute-start | bytes 2359304 | tf_op jit(solution)/shard_map/ppermute | solution.py:412
  108.2 34.1 %collective-permute-start.21 = (f32[8,4,24,256]{3,2,1,0:T(8,128)S(1)}, f32[8,4,24,256]{3,2,1,0:T(8,128)S(1)}, u32[]{:S(2)}, u32[]{:S(2)}) collective-permute-start(f32[8,4,24,256]{3,2,1,0:T(8,128)S(1)} %last_free.1.refs_0_), channel_id=1, source_target_pairs={{0,8},{8,0},{16,24},{24,16},{1,9},{9,1},{17,25},{25,17},{2,10},{10... | collective-permute-start | bytes 2359304 | tf_op jit(solution)/shard_map/ppermute | solution.py:412
  141.8 2.3 %collective-permute-start.23 = (f32[8,4,24,256]{3,2,1,0:T(8,128)S(1)}, f32[8,4,24,256]{3,2,1,0:T(8,128)S(1)}, u32[]{:S(2)}, u32[]{:S(2)}) collective-permute-start(f32[8,4,24,256]{3,2,1,0:T(8,128)S(1)} %collective-permute-done.22.refs_2_), channel_id=1, source_target_pairs={{0,8},{8,0},{16,24},{24,16},{1,9},{9,1},{17,25},{25,17},{2,10},{10... | collective-permute-start | bytes 2359304 | tf_op jit(solution)/shard_map/ppermute | solution.py:412
  141.8 3.4 %collective-permute-start.27 = (f32[8,4,24,256]{3,2,1,0:T(8,128)S(1)}, f32[8,4,24,256]{3,2,1,0:T(8,128)S(1)}, u32[]{:S(2)}, u32[]{:S(2)}) collective-permute-start(f32[8,4,24,256]{3,2,1,0:T(8,128)S(1)} %collective-permute-done.26.refs_14_), channel_id=1, source_target_pairs={{0,8},{8,0},{16,24},{24,16},{1,9},{9,1},{17,25},{25,17},{2,10},{10... | collective-permute-start | bytes 2359304 | tf_op jit(solution)/shard_map/ppermute | solution.py:412

commit v3 on v2

--- a/solution.py
+++ b/solution.py
@@ -10,7 +10,7 @@
 SUBSTEPS = 6
 NEWTON = 16
 LANES = 128
-SCOPED = 8 * 2**20
+SCOPED = 10 * 2**20
 
 unbind_rate = 0.05
 uptake_rate = 0.1
@@ -53,30 +53,6 @@
 
 NN = ((1,), (0,))
 NT = ((1,), (1,))
-
-
-def neighbour_sum(a, low, high, x, z, at_left, at_right):
-    nx, nz, members, ny = a.shape
-    free = a[x, z]
-    total = (low[z] if x == 0 else a[x - 1, z]) + (high[z] if x == nx - 1 else a[x + 1, z])
-    if z + 1 < nz:
-        total += a[x, z + 1]
-    if z > 0:
-        total += a[x, z - 1]
-    total += jnp.where(at_right, 0.0, pltpu.roll(free, ny - 1, 1))
-    return total + jnp.where(at_left, 0.0, pltpu.roll(free, 1, 1))
-
-
-def ends(a):
-    _, _, members, ny = a.shape
-    lane = lax.broadcasted_iota(jnp.int32, (members, ny), 1)
-    return lane == 0, lane == ny - 1
-
-
-def free_part(a, low, high, diffusivity, x, z, at):
-    free = a[x, z]
-    neighbours = neighbour_sum(a, low, high, x, z, *at)
-    return free + diffusivity[x, pl.ds(z, 1), :] * (neighbours - 6.0 * free)
 
 
 def react(free, receptor, complexed, internal, binding):
@@ -90,68 +66,106 @@
     )
 
 
-def edges_kernel(a, r, c, low, high, diffusivity, binding, source, first, last):
-    nx, nz, _, _ = a.shape
-    at = ends(a)
-    for x, out in ((0, first), (nx - 1, last)):
+def spread_free(free, planes, neighbours, diffusivity):
+    lane = lax.broadcasted_iota(jnp.int32, free.shape, 1)
+    last = free.shape[1] - 1
+    for plane in planes:
+        neighbours = plane if neighbours is None else neighbours + plane
+    neighbours += jnp.where(lane == last, 0.0, pltpu.roll(free, last, 1))
+    neighbours += jnp.where(lane == 0, 0.0, pltpu.roll(free, 1, 1))
+    return free + diffusivity * (neighbours - 6.0 * free)
+
+
+def beside(read, x, z, nx, nz, low, high):
+    around = [low if x == 0 else read(x - 1, z), high if x == nx - 1 else read(x + 1, z)]
+    around += [read(x, other) for other in (z + 1, z - 1) if 0 <= other < nz]
+    return [value for value in around if value is not None]
+
+
+def edge_free(read, rest, x, nz, nx, z, diffusivity):
+    return spread_free(read(x, z), beside(read, x, z, nx, nz, None, None), None, diffusivity) + rest
+
+
+def first_edges_kernel(below, above, diffusivity, binding, source, first, last):
+    _, _, nz, members, _ = below.shape
+    nx = diffusivity.shape[0]
+    for x, ends, out in ((0, below, first), (nx - 1, above, last)):
+        shift = 0 if x == 0 else nx - 2
+
+        def read(at, z, ends=ends, shift=shift):
+            return ends[0, at - shift, z]
+
         for z in range(nz):
             row = pl.ds(z, 1)
-            flux = binding[x, row, :] * a[x, z] * r[x, z]
-            out[z] = (
-                free_part(a, low, high, diffusivity, x, z, at)
-                + (unbind_rate * c[x, z] - flux)
-                + source[x, row, :]
-            )
-
-
-def substep_kernel(
-    a, r, c, i, low, high, diffusivity, binding, source, out_a, out_r, out_c, out_i
+            free = read(x, z)
+            flux = binding[x, row, :] * free * ends[1, x - shift, z]
+            rest = unbind_rate * ends[2, x - shift, z] - flux + source[x, row, :]
+            spread = diffusivity[x, row, :]
+            out[z, :members, :] = free
+            out[z, members : 2 * members, :] = edge_free(read, rest, x, nz, nx, z, spread)
+            out[z, 2 * members :, :] = jnp.broadcast_to(spread, (8, spread.shape[1]))
+
+
+def two_substeps_kernel(
+    a, r, c, i, low, high, low_first, high_first, diffusivity, binding, source, *refs, final
 ):
-    nx, nz, _, _ = a.shape
-    at = ends(a)
+    out_a, out_r, out_c, out_i = refs[:4]
+    middle = refs[-1]
+    nx, nz, members, _ = a.shape
+
+    def outside(x, z, later):
+        part = slice(members, 2 * members) if later else slice(0, members)
+        values = []
+        for end, halo, origin in ((0, low, low_first), (nx - 1, high, high_first)):
+            value = halo[z, part, :] if x == end else None
+            if x == end and later:
+                value += origin[z, 2 * members : 2 * members + 1, :] * a[x, z]
+            values.append(value)
+        return values
+
     for x in range(nx):
         for z in range(nz):
             row = pl.ds(z, 1)
             back, out_r[x, z], out_c[x, z], out_i[x, z] = react(
                 a[x, z], r[x, z], c[x, z], i[x, z], binding[x, row, :]
             )
-            out_a[x, z] = (
-                free_part(a, low, high, diffusivity, x, z, at) + back + source[x, row, :]
+            around = beside(lambda x, z: a[x, z], x, z, nx, nz, *outside(x, z, False))
+            middle[x, z] = (
+                spread_free(a[x, z], around, None, diffusivity[x, row, :])
+                + back
+                + source[x, row, :]
             )
-
-
-def last_but_one_kernel(
-    a, r, c, i, low, high, diffusivity, binding, source, out_a, out_add, out_tracer, out_i
-):
-    nx, nz, _, _ = a.shape
-    at = ends(a)
     for x in range(nx):
         for z in range(nz):
             row = pl.ds(z, 1)
-            bind = binding[x, row, :]
             back, receptor, complexed, internal = react(
-                a[x, z], r[x, z], c[x, z], i[x, z], bind
+                middle[x, z], out_r[x, z], out_c[x, z], out_i[x, z], binding[x, row, :]
             )
-            free = free_part(a, low, high, diffusivity, x, z, at) + back + source[x, row, :]
-            back, _, complexed, internal = react(free, receptor, complexed, internal, bind)
-            out_a[x, z] = free
-            out_add[x, z] = back + source[x, row, :]
-            out_tracer[x, z] = complexed + internal
+            around = beside(lambda x, z: middle[x, z], x, z, nx, nz, *outside(x, z, True))
+            out_a[x, z] = (
+                spread_free(middle[x, z], around, None, diffusivity[x, row, :])
+                + back
+                + source[x, row, :]
+            )
+            if not final:
+                out_r[x, z] = receptor
+            out_c[x, z] = complexed + internal if final else complexed
             out_i[x, z] = internal
-
-
-def last_free_kernel(a, add, low, high, diffusivity, out_a):
-    nx, nz, _, _ = a.shape
-    at = ends(a)
-    for x in range(nx):
+    if final:
+        return
+    for x, out in ((0, refs[4]), (nx - 1, refs[5])):
         for z in range(nz):
-            out_a[x, z] = free_part(a, low, high, diffusivity, x, z, at) + add[x, z]
-
-
-def forecast_call(kernel, inputs, outputs, share=1.0, ready=()):
-    nx, nz, members, ny = inputs[0].shape
-    cells = int(nx * nz * members * ny * share)
-
+            row = pl.ds(z, 1)
+            free = out_a[x, z]
+            flux = binding[x, row, :] * free * out_r[x, z]
+            rest = unbind_rate * out_c[x, z] - flux + source[x, row, :]
+            out[z, :members, :] = free
+            out[z, members:, :] = edge_free(
+                lambda x, z: out_a[x, z], rest, x, nz, nx, z, diffusivity[x, row, :]
+            )
+
+
+def forecast_call(kernel, name, inputs, outputs, cells, scratch=(), ready=()):
     def body(*refs):
         kernel(*refs[: len(inputs)], *refs[len(inputs) + len(ready) :])
 
@@ -160,11 +174,12 @@
         out_shape=[jax.ShapeDtypeStruct(shape, f32) for shape in outputs],
         in_specs=[VMEM] * len(inputs) + [pl.BlockSpec(memory_space=pl.ANY)] * len(ready),
         out_specs=[VMEM] * len(outputs),
+        scratch_shapes=[pltpu.VMEM(shape, f32) for shape in scratch],
         compiler_params=pltpu.CompilerParams(vmem_limit_bytes=SCOPED),
         cost_estimate=pl.CostEstimate(
             flops=30 * cells, bytes_accessed=32 * cells, transcendentals=0
         ),
-        name=kernel.__name__.removesuffix("_kernel"),
+        name=name,
     )(*inputs, *ready)
 
 
@@ -363,7 +378,7 @@
         ],
         compiler_params=pltpu.CompilerParams(vmem_limit_bytes=SCOPED),
         cost_estimate=pl.CostEstimate(
-            flops=10**10, bytes_accessed=10**6, transcendentals=0
+            flops=10**8, bytes_accessed=10**6, transcendentals=0
         ),
         name="transforms",
     )(place, mine, other)
@@ -458,48 +473,60 @@
         def complete(held, *after):
             return held
 
-    whole, plane = (nx, nz, rows, ny), (nz, rows, ny)
+    def across(held):
+        return held[min(2, blocks - 1)]
+
+    whole = (nx, nz, rows, ny)
     coefficients = (diffusivity, binding, source)
-    around = halos(
-        jnp.transpose(ensemble[:, 0, 0], (1, 0, 2)), jnp.transpose(ensemble[:, 0, -1], (1, 0, 2))
+    cells = nx * nz * rows * ny
+    ends = [
+        jnp.transpose(ensemble[:, :3, part], (1, 2, 3, 0, 4))
+        for part in (slice(0, 2), slice(nx - 2, nx))
+    ]
+    edges = forecast_call(
+        first_edges_kernel,
+        "first_edges",
+        [*ends, *coefficients],
+        [(nz, 2 * rows + 8, ny)] * 2,
+        2 * cells // nx,
     )
     fields = [jnp.transpose(ensemble[:, k], (1, 2, 0, 3)) for k in range(species)]
     conserved = fields[1] + fields[2] + fields[3]
     omega, eta = voxel_weights(
         place, owner, obs_index, observed, obs_var, batches // 2, nx * nz, ny
     )
-    for step in range(SUBSTEPS - 2):
+    around = origin = halos(*edges)
+    steps = SUBSTEPS // 2
+    for step in range(steps):
+        final = step == steps - 1
+        ready = ()
         if step == 1:
             conserved = collect(lax.optimization_barrier((conserved, fields[0]))[0])
             ready = (omega, eta)
-        elif step == 3:
+        elif step == 2:
             ready = conserved[1:]
-        else:
-            ready = ()
-        next_edges = forecast_call(
-            edges_kernel, [*fields[:3], *around, *coefficients], [plane] * 2, 2 / nx
-        )
-        fields_now, around_now = fields, around
-        around = halos(*next_edges)
-        fields = forecast_call(
-            substep_kernel,
-            [*fields_now, *around_now, *coefficients],
-            [whole] * 4,
+        *fields, = forecast_call(
+            functools.partial(two_substeps_kernel, final=final),
+            "two_substeps",
+            [*fields, *around, *origin, *coefficients],
+            [whole] * 4 + ([] if final else [(nz, 2 * rows, ny)] * 2),
+            2 * cells,
+            scratch=[whole],
             ready=ready,
         )
-    conserved = complete(conserved, fields[0])
-    free, add, tracer, internal = forecast_call(
-        last_but_one_kernel, [*fields, *around, *coefficients], [whole] * 4
-    )
-    around = halos(free[0], free[-1])
-    (free,) = forecast_call(last_free_kernel, [free, add, *around, diffusivity], [whole])
+        if not final:
+            around = halos(*fields[4:])
+            fields = fields[:4]
+    free, _, tracer, internal = fields
 
     tracer = complete(collect(tracer))
-    internal = collect(internal)
+    conserved = complete(conserved, across(tracer))
+    internal = collect(lax.optimization_barrier((internal, across(tracer)))[0])
+    half = total_over(gram(place, owner, omega, eta, tracer, offsets), "space")
+    half, free, _ = lax.optimization_barrier((half, free, across(internal)))
     free = collect(free)
-    half = total_over(gram(place, owner, omega, eta, tracer, offsets), "space")
+    internal = complete(internal, half)
     weights = transforms(place, half, swap(half, "member", 1), offsets, blocks, rows)
-    internal = complete(internal, weights)
     free = complete(free, weights)
     if blocks == 1:
         weights = lax.dynamic_slice(weights, (member * rows, 0), (rows, LANES))

time: 151 us -> 139 us (0.921)
  starting transfers between devices: 50.9 us -> 32.5 us
  local copies, waits for them, and re-layouts: 8.91 us -> 13.1 us
  waiting for transfers between devices: 47.9 us -> 49.8 us
    ppermute x6 -> x3, starting transfers between devices: 26.2 us -> 13.8 us  [halos(): lax.ppermute(last, 'space', forward)]
    ppermute x6 -> x3, waiting for transfers between devices: 2.99 us -> 8.39 us  [halos(): lax.ppermute(last, 'space', forward)]
    ppermute x6 -> x3, waiting for transfers between devices: 15.3 us -> 10.3 us  [halos(): lax.ppermute(first, 'space', backward)]
    unnamed x32, local copies, waits for them, and re-layouts: 3.27 us -> 8.14 us
    ppermute x6 -> x3, starting transfers between devices: 7.93 us -> 3.88 us  [halos(): lax.ppermute(first, 'space', backward)]
    ppermute x16, starting transfers between devices: 16.8 us -> 14.8 us  [swap(): return lax.ppermute(x, axis, [(k, k ^ bit) for k in range(count)])]
    pallas_call x10 -> x4, Pallas kernels: 5.85 us -> 6.11 us  [forecast_call(): pl.pallas_call(body, out_shape=[jax.ShapeDtypeStruct(shape, f32) for shap...]
  transfers between devices with their start and end apart: 28 -> 22, of which waited for: 14 -> 12; matrix products, arithmetic and copies ran while one was open for 4% -> 3% of each run, Pallas kernels for 22% -> 23%
where the time goes in v3:
time: 139 us
  waiting for transfers between devices  49.8 us (36%)
  Pallas kernels  41.1 us (30%)
  starting transfers between devices  32.5 us (23%)
  local copies, waits for them, and re-layouts  13.1 us (9%)
  other arithmetic  1.77 us (1%)
    ppermute x16, waiting for transfers between devices, swap(): return lax.ppermute(x, axis, [(k, k ^ bit) for k in range(count)])  31.1 us
    pallas_call x1, Pallas kernels, transforms(): pl.pallas_call(functools.partial(transform_kernel, offsets=offsets, block...  27.6 us
    ppermute x16, starting transfers between devices, swap(): return lax.ppermute(x, axis, [(k, k ^ bit) for k in range(count)])  14.8 us
    ppermute x3, starting transfers between devices, halos(): lax.ppermute(last, 'space', forward)  13.8 us
    ppermute x3, waiting for transfers between devices, halos(): lax.ppermute(first, 'space', backward)  10.3 us
    ppermute x3, waiting for transfers between devices, halos(): lax.ppermute(last, 'space', forward)  8.39 us
    unnamed x32, local copies, waits for them, and re-layouts  8.14 us
    pallas_call x4, Pallas kernels, forecast_call(): pl.pallas_call(body, out_shape=[jax.ShapeDtypeStruct(shape, f32) for shap...  6.11 us
  transfers between devices with their start and end apart: 22, of which 12 were waited for; matrix products, arithmetic and copies ran while one was open for 3% of the time, Pallas kernels for 23%

profile of v3, /device:TPU:0, one launch (start us, length us, event | category | flops | bytes accessed | tf_op | source)
XLA Modules:
  0.0 138.6 jit_solution(8717102442293700043)
XLA Ops:
  0.0 1.6 %fusion = (f32[24,3,2,4,256]{4,3,2,1,0:T(4,128)S(1)}, f32[24,3,2,4,256]{4,3,2,1,0:T(4,128)S(1)}) fusion(f32[24,4,8,4,256]{4,3,2,1,0:T(4,128)} %param.8), kind=kLoop, calls=%fused_computation.8 | loop fusion | bytes 2359296 | tf_op jit(solution)/shard_map/slice | solution.py:483
  1.6 0.4 copy_bitcast_fusion.4
  2.0 0.2 first_edges.1
  2.2 4.9 %collective-permute-start = (f32[4,56,256]{2,1,0:T(8,128)S(1)}, f32[4,56,256]{2,1,0:T(8,128)S(1)}, u32[]{:S(2)}, u32[]{:S(2)}) collective-permute-start(f32[4,56,256]{2,1,0:T(8,128)S(1)} %get-tuple-element.33), channel_id=1, source_target_pairs={{0,1},{1,2},{2,3},{3,4},{4,5},{5,6},{6,7},{8,9},{9,10},{10,11},{11... | collective-permute-start | bytes 688136 | tf_op jit(solution)/shard_map/ppermute | solution.py:451
  7.1 1.3 collective-permute-start.1
  8.4 1.0 fusion.1
  9.4 0.9 copy_bitcast_fusion
  10.3 1.7 %add_add_fusion.refs_4_ = f32[8,4,24,256]{3,2,1,0:T(8,128)S(1)} fusion(f32[24,1,8,4,256]{4,3,2,1,0:T(4,128)S(1)} %get-tuple-element.61, f32[24,1,8,4,256]{4,3,2,1,0:T(4,128)S(1)} %get-tuple-element.60, f32[24,1,8,4,256]{4,3,2,1,0:T(4,128)S(1)} %get-tuple-element.59), kind=kLoop, calls=%fused_computation.4 | loop fusion | flops 393216 | bytes 3145728 | tf_op jit(solution)/shard_map/add | solution.py:494
  12.0 0.0 copy-start.11
  12.0 0.0 copy-start.12
  12.0 0.0 copy-start.13
  12.0 0.0 copy-start.14
  12.0 1.1 copy_bitcast_fusion.2
  13.2 3.7 %collective-permute-done.refs_4_.refs_6_ = f32[4,56,256]{2,1,0:T(8,128)S(1)} collective-permute-done((f32[4,56,256]{2,1,0:T(8,128)S(1)}, f32[4,56,256]{2,1,0:T(8,128)S(1)}, u32[]{:S(2)}, u32[]{:S(2)}) %collective-permute-start) | collective-permute-done | bytes 229408 | tf_op jit(solution)/shard_map/ppermute | solution.py:451
  16.9 0.0 collective-permute-done.1.refs_5_.refs_7_
  16.9 2.3 %two_substeps.3 = (f32[8,4,24,256]{3,2,1,0:T(8,128)S(1)}, f32[8,4,24,256]{3,2,1,0:T(8,128)S(1)}, f32[8,4,24,256]{3,2,1,0:T(8,128)S(1)}, f32[8,4,24,256]{3,2,1,0:...) custom-call(f32[8,4,24,256]{3,2,1,0:T(8,128)S(1)} %get-tuple-element.66.refs_0_, ...), custom_call_target="tpu_custom_call" | custom-call | flops 11796480 | bytes 12582912 | tf_op jit(solution)/shard_map/two_substeps/pallas_call | solution.py:172
  19.1 0.9 copy-done
  20.0 0.9 copy-done.2
  20.9 0.9 copy-done.4
  21.8 0.9 copy-done.6
  22.7 1.5 %collective-permute-start.7 = (f32[8,4,24,256]{3,2,1,0:T(8,128)S(1)}, f32[8,4,24,256]{3,2,1,0:T(8,128)S(1)}, u32[]{:S(2)}, u32[]{:S(2)}) collective-permute-start(f32[8,4,24,256]{3,2,1,0:T(8,128)S(1)} %add_add_fusion.refs_4_), channel_id=1, source_target_pairs={{0,16},{8,24},{16,0},{24,8},{1,17},{9,25},{17,1},{25,9},{2,18},{10... | collective-permute-start | bytes 2359304 | tf_op jit(solution)/shard_map/ppermute | solution.py:427
  24.2 0.0 collective-permute-start.6
  24.2 4.4 %collective-permute-start.2 = (f32[4,48,256]{2,1,0:T(8,128)}, f32[4,48,256]{2,1,0:T(8,128)S(1)}, u32[]{:S(2)}, u32[]{:S(2)}) collective-permute-start(f32[4,48,256]{2,1,0:T(8,128)} %get-tuple-element.39), channel_id=1, source_target_pairs={{0,1},{1,2},{2,3},{3,4},{4,5},{5,6},{6,7},{8,9},{9,10},{10,11},{11... | collective-permute-start | bytes 589832 | tf_op jit(solution)/shard_map/ppermute | solution.py:451
  28.6 1.3 collective-permute-start.3
  29.9 0.1 pad_add_fusion.place
  30.0 1.4 %voxel_weights.1 = (f32[2,32,256]{2,1,0:T(8,128)S(1)}, f32[2,32,256]{2,1,0:T(8,128)S(1)}) custom-call(s32[3]{0:T(128)S(1)} %pad_add_fusion.place, s32[4]{0:T(128)S(1)} %copy-done.14, s32[4,2048]{1,0:T(4,128)S(1)} %copy-done.11, f32[4,2048]{1,0:T(4,128)S(1)} %copy-done.12, f32[4,2048]{1,0:T(4,128)S(1)} %copy-done.13), custom_call_target="tpu_custom_call" | custom-call | tf_op jit(solution)/shard_map/voxel_weights/pallas_call | solution.py:222
  31.4 2.3 %collective-permute-done.2.refs_4_ = f32[4,48,256]{2,1,0:T(8,128)S(1)} collective-permute-done((f32[4,48,256]{2,1,0:T(8,128)}, f32[4,48,256]{2,1,0:T(8,128)S(1)}, u32[]{:S(2)}, u32[]{:S(2)}) %collective-permute-start.2) | collective-permute-done | bytes 196640 | tf_op jit(solution)/shard_map/ppermute | solution.py:451
  33.7 4.7 %collective-permute-done.3.refs_5_ = f32[4,48,256]{2,1,0:T(8,128)S(1)} collective-permute-done((f32[4,48,256]{2,1,0:T(8,128)}, f32[4,48,256]{2,1,0:T(8,128)S(1)}, u32[]{:S(2)}, u32[]{:S(2)}) %collective-permute-start.3) | collective-permute-done | bytes 196640 | tf_op jit(solution)/shard_map/ppermute | solution.py:451
  38.5 1.1 copy-done.1
  39.6 1.1 copy-done.3
  40.7 1.1 copy-done.5
  41.9 1.1 copy-done.7
  43.0 1.6 %two_substeps.4 = (f32[8,4,24,256]{3,2,1,0:T(8,128)S(1)}, f32[8,4,24,256]{3,2,1,0:T(8,128)S(1)}, f32[8,4,24,256]{3,2,1,0:T(8,128)S(1)}, f32[8,4,24,256]{3,2,1,0:...) custom-call(f32[8,4,24,256]{3,2,1,0:T(8,128)S(1)} %copy-done.1, f32[8,4,24,256]{3,2,1,0:T(8,128)S(1)} %copy-done.3, ...), custom_call_target="tpu_custom_call" | custom-call | flops 11796480 | bytes 12582912 | tf_op jit(solution)/shard_map/two_substeps/pallas_call | solution.py:172
  44.6 4.5 %collective-permute-start.4 = (f32[4,48,256]{2,1,0:T(8,128)S(1)}, f32[4,48,256]{2,1,0:T(8,128)S(1)}, u32[]{:S(2)}, u32[]{:S(2)}) collective-permute-start(f32[4,48,256]{2,1,0:T(8,128)S(1)} %get-tuple-element.45), channel_id=1, source_target_pairs={{0,1},{1,2},{2,3},{3,4},{4,5},{5,6},{6,7},{8,9},{9,10},{10,11},{11... | collective-permute-start | bytes 589832 | tf_op jit(solution)/shard_map/ppermute | solution.py:451
  49.1 1.3 collective-permute-start.5
  50.4 2.4 %collective-permute-done.4.refs_4_ = f32[4,48,256]{2,1,0:T(8,128)S(1)} collective-permute-done((f32[4,48,256]{2,1,0:T(8,128)S(1)}, f32[4,48,256]{2,1,0:T(8,128)S(1)}, u32[]{:S(2)}, u32[]{:S(2)}) %collective-permute-start.4) | collective-permute-done | bytes 196640 | tf_op jit(solution)/shard_map/ppermute | solution.py:451
  52.8 5.6 %collective-permute-done.5.refs_5_ = f32[4,48,256]{2,1,0:T(8,128)S(1)} collective-permute-done((f32[4,48,256]{2,1,0:T(8,128)S(1)}, f32[4,48,256]{2,1,0:T(8,128)S(1)}, u32[]{:S(2)}, u32[]{:S(2)}) %collective-permute-start.5) | collective-permute-done | bytes 196640 | tf_op jit(solution)/shard_map/ppermute | solution.py:451
  58.5 2.1 %two_substeps.5 = (f32[8,4,24,256]{3,2,1,0:T(8,128)S(1)}, f32[8,4,24,256]{3,2,1,0:T(8,128)}, f32[8,4,24,256]{3,2,1,0:T(8,128)S(1)}, f32[8,4,24,256]{3,2,1,0:T(8,128)S(1)}) custom-call(f32[8,4,24,256]{3,2,1,0:T(8,128)S(1)} %get-tuple-element.41.refs_0_, f32[8,4,24,256]{3,2,1,0:T(8,128)S(1)} %get-tuple-element.42.refs_1_, ...), custom_call_target="tpu_custom_call" | custom-call | flops 11796480 | bytes 12582912 | tf_op jit(solution)/shard_map/two_substeps/pallas_call | solution.py:172
  60.5 0.5 collective-permute-start.9
  61.0 0.0 collective-permute-start.8
  61.0 18.2 %collective-permute-done.9.refs_2_.refs_10_ = f32[8,4,24,256]{3,2,1,0:T(8,128)S(1)} collective-permute-done((f32[8,4,24,256]{3,2,1,0:T(8,128)S(1)}, f32[8,4,24,256]{3,2,1,0:T(8,128)S(1)}, u32[]{:S(2)}, u32[]{:S(2)}) %collective-permute-start.9) | collective-permute-done | bytes 786464 | tf_op jit(solution)/shard_map/ppermute | solution.py:427
  79.2 0.5 collective-permute-start.14
  79.7 0.0 collective-permute-done.8.refs_1_.refs_9_
  79.7 1.8 %collective-permute-done.10.refs_3_.refs_11_ = f32[8,4,24,256]{3,2,1,0:T(8,128)S(1)} collective-permute-done((f32[8,4,24,256]{3,2,1,0:T(8,128)S(1)}, f32[8,4,24,256]{3,2,1,0:T(8,128)S(1)}, u32[]{:S(2)}, u32[]{:S(2)}) %collective-permute-start.10) | collective-permute-done | bytes 786464 | tf_op jit(solution)/shard_map/ppermute | solution.py:427
  81.5 0.9 gram.1
  82.4 2.4 %collective-permute-start.11 = (f32[96,128]{1,0:T(8,128)S(1)}, f32[96,128]{1,0:T(8,128)S(1)}, u32[]{:S(2)}, u32[]{:S(2)}) collective-permute-start(f32[96,128]{1,0:T(8,128)S(1)} %gram.1), channel_id=1, source_target_pairs={{0,1},{1,0},{2,3},{3,2},{4,5},{5,4},{6,7},{7,6},{8,9},{9,8},{10,11... | collective-permute-start | bytes 147464 | tf_op jit(solution)/shard_map/ppermute | solution.py:427
  84.8 2.1 %collective-permute-done.11 = f32[96,128]{1,0:T(8,128)S(1)} collective-permute-done((f32[96,128]{1,0:T(8,128)S(1)}, f32[96,128]{1,0:T(8,128)S(1)}, u32[]{:S(2)}, u32[]{:S(2)}) %collective-permute-start.11) | collective-permute-done | bytes 49184 | tf_op jit(solution)/shard_map/ppermute | solution.py:427
  86.8 7.5 %collective-permute-start.12 = (f32[96,128]{1,0:T(8,128)S(1)}, f32[96,128]{1,0:T(8,128)S(1)}, u32[]{:S(2)}, u32[]{:S(2)}) collective-permute-start(f32[96,128]{1,0:T(8,128)S(1)} %add.17), channel_id=1, source_target_pairs={{0,2},{1,3},{2,0},{3,1},{4,6},{5,7},{6,4},{7,5},{8,10},{9,11},{10,... | collective-permute-start | bytes 147464 | tf_op jit(solution)/shard_map/ppermute | solution.py:427
  94.4 2.1 %collective-permute-done.12 = f32[96,128]{1,0:T(8,128)S(1)} collective-permute-done((f32[96,128]{1,0:T(8,128)S(1)}, f32[96,128]{1,0:T(8,128)S(1)}, u32[]{:S(2)}, u32[]{:S(2)}) %collective-permute-start.12) | collective-permute-done | bytes 49184 | tf_op jit(solution)/shard_map/ppermute | solution.py:427
  96.4 0.2 collective-permute-start.13
  96.6 4.9 %collective-permute-done.13 = f32[96,128]{1,0:T(8,128)S(1)} collective-permute-done((f32[96,128]{1,0:T(8,128)S(1)}, f32[96,128]{1,0:T(8,128)S(1)}, u32[]{:S(2)}, u32[]{:S(2)}) %collective-permute-start.13) | collective-permute-done | bytes 49184 | tf_op jit(solution)/shard_map/ppermute | solution.py:427
  101.5 0.0 collective-permute-done.14.refs_14_
  101.5 0.6 collective-permute-start.17
  102.1 0.0 collective-permute-start.15
  102.1 0.5 collective-permute-start.20
  102.6 0.5 collective-permute-start.16
  103.1 0.2 collective-permute-done.15.other
  103.3 0.2 collective-permute-start.21
  103.5 27.6 %transforms.1.weights = f32[24,128]{1,0:T(8,128)S(1)} custom-call(s32[3]{0:T(128)S(1)} %pad_add_fusion.place, f32[96,128]{1,0:T(8,128)S(1)} %add.19.mine, f32[96,128]{1,0:T(8,128)S(1)} %collective-permute-done.15.other), custom_call_target="tpu_custom_call" | custom-call | flops 100000000 | bytes 1000000 | tf_op jit(solution)/shard_map/transforms/pallas_call | solution.py:370
  131.1 0.4 collective-permute-start.18
  131.5 0.0 collective-permute-done.20.refs_13_
  131.5 0.0 collective-permute-done.16.refs_1_
  131.5 1.9 %collective-permute-done.18.refs_3_ = f32[8,4,24,256]{3,2,1,0:T(8,128)S(1)} collective-permute-done((f32[8,4,24,256]{3,2,1,0:T(8,128)S(1)}, f32[8,4,24,256]{3,2,1,0:T(8,128)S(1)}, u32[]{:S(2)}, u32[]{:S(2)}) %collective-permute-start.18) | collective-permute-done | bytes 786464 | tf_op jit(solution)/shard_map/ppermute | solution.py:427
  133.4 5.2 %mix.1 = f32[24,4,8,4,256]{4,3,2,1,0:T(4,128)} custom-call(f32[24,128]{1,0:T(8,128)S(1)} %transforms.1.weights, f32[8,4,24,256]{3,2,1,0:T(8,128)S(1)} %get-tuple-element.53.refs_0_, f32[8,4,24,256]{3,2,1,0:T(8,128)S(1)} %collective-permute-done.16.refs_1_, f32[8,4,24,256]{3,2,1,0:T(8,128)S(1)} %collective-permute-done.17.refs_2_, ...), custom_call_target="tpu_custom_call" | custom-call | tf_op jit(solution)/shard_map/mix/pallas_call | solution.py:414
  (30 shorter events, 0.1 us)
Async XLA Ops:
  0.0 8.4 %copy-start.15 = (f32[24,4,8,4,256]{4,3,2,1,0:T(4,128)S(1)}, f32[24,4,8,4,256]{4,3,2,1,0:T(4,128)}, u32[]{:S(2)}) copy-start(f32[24,4,8,4,256]{4,3,2,1,0:T(4,128)} %param.8) | copy-start | bytes 9437188
  0.0 2.0 %copy-start.10 = (f32[8,4,256]{2,1,0:T(4,128)S(1)}, f32[8,4,256]{2,1,0:T(4,128)}, u32[]{:S(2)}) copy-start(f32[8,4,256]{2,1,0:T(4,128)} %refs_10_.5) | copy-start | bytes 98308
  0.0 2.0 %copy-start.9 = (f32[8,4,256]{2,1,0:T(4,128)S(1)}, f32[8,4,256]{2,1,0:T(4,128)}, u32[]{:S(2)}) copy-start(f32[8,4,256]{2,1,0:T(4,128)} %refs_9_.5) | copy-start | bytes 98308
  0.0 2.0 %copy-start.8 = (f32[8,4,256]{2,1,0:T(4,128)S(1)}, f32[8,4,256]{2,1,0:T(4,128)}, u32[]{:S(2)}) copy-start(f32[8,4,256]{2,1,0:T(4,128)} %refs_8_.5) | copy-start | bytes 98308
  2.2 14.6 %collective-permute-start = (f32[4,56,256]{2,1,0:T(8,128)S(1)}, f32[4,56,256]{2,1,0:T(8,128)S(1)}, u32[]{:S(2)}, u32[]{:S(2)}) collective-permute-start(f32[4,56,256]{2,1,0:T(8,128)S(1)} %get-tuple-element.33), channel_id=1, source_target_pairs={{0,1},{1,2},{2,3},{3,4},{4,5},{5,6},{6,7},{8,9},{9,10},{10,11},{11... | collective-permute-start | bytes 688136 | tf_op jit(solution)/shard_map/ppermute | solution.py:451
  7.1 9.7 %collective-permute-start.1 = (f32[4,56,256]{2,1,0:T(8,128)S(1)}, f32[4,56,256]{2,1,0:T(8,128)S(1)}, u32[]{:S(2)}, u32[]{:S(2)}) collective-permute-start(f32[4,56,256]{2,1,0:T(8,128)S(1)} %get-tuple-element.34), channel_id=1, source_target_pairs={{1,0},{2,1},{3,2},{4,3},{5,4},{6,5},{7,6},{9,8},{10,9},{11,10},{12... | collective-permute-start | bytes 688136 | tf_op jit(solution)/shard_map/ppermute | solution.py:451
  12.0 18.0 %copy-start.11 = (s32[4,2048]{1,0:T(4,128)S(1)}, s32[4,2048]{1,0:T(4,128)}, u32[]{:S(2)}) copy-start(s32[4,2048]{1,0:T(4,128)} %obs_index.1) | copy-start | bytes 98308
  12.0 18.0 %copy-start.12 = (f32[4,2048]{1,0:T(4,128)S(1)}, f32[4,2048]{1,0:T(4,128)}, u32[]{:S(2)}) copy-start(f32[4,2048]{1,0:T(4,128)} %observed.1) | copy-start | bytes 98308
  12.0 18.0 %copy-start.13 = (f32[4,2048]{1,0:T(4,128)S(1)}, f32[4,2048]{1,0:T(4,128)}, u32[]{:S(2)}) copy-start(f32[4,2048]{1,0:T(4,128)} %obs_var.1) | copy-start | bytes 98308
  12.0 18.0 %copy-start.14 = (s32[4]{0:T(128)S(1)}, s32[4]{0:T(128)}, u32[]{:S(2)}) copy-start(s32[4]{0:T(128)} %owner.3) | copy-start | bytes 52
  19.1 0.9 copy-start
  20.0 0.9 copy-start.2
  20.9 0.9 copy-start.4
  21.8 0.9 copy-start.6
  22.7 35.8 %collective-permute-start.7 = (f32[8,4,24,256]{3,2,1,0:T(8,128)S(1)}, f32[8,4,24,256]{3,2,1,0:T(8,128)S(1)}, u32[]{:S(2)}, u32[]{:S(2)}) collective-permute-start(f32[8,4,24,256]{3,2,1,0:T(8,128)S(1)} %add_add_fusion.refs_4_), channel_id=1, source_target_pairs={{0,16},{8,24},{16,0},{24,8},{1,17},{9,25},{17,1},{25,9},{2,18},{10... | collective-permute-start | bytes 2359304 | tf_op jit(solution)/shard_map/ppermute | solution.py:427
  24.2 34.2 %collective-permute-start.6 = (f32[8,4,24,256]{3,2,1,0:T(8,128)S(1)}, f32[8,4,24,256]{3,2,1,0:T(8,128)S(1)}, u32[]{:S(2)}, u32[]{:S(2)}) collective-permute-start(f32[8,4,24,256]{3,2,1,0:T(8,128)S(1)} %add_add_fusion.refs_4_), channel_id=1, source_target_pairs={{0,8},{8,0},{16,24},{24,16},{1,9},{9,1},{17,25},{25,17},{2,10},{10... | collective-permute-start | bytes 2359304 | tf_op jit(solution)/shard_map/ppermute | solution.py:427
  24.2 9.5 %collective-permute-start.2 = (f32[4,48,256]{2,1,0:T(8,128)}, f32[4,48,256]{2,1,0:T(8,128)S(1)}, u32[]{:S(2)}, u32[]{:S(2)}) collective-permute-start(f32[4,48,256]{2,1,0:T(8,128)} %get-tuple-element.39), channel_id=1, source_target_pairs={{0,1},{1,2},{2,3},{3,4},{4,5},{5,6},{6,7},{8,9},{9,10},{10,11},{11... | collective-permute-start | bytes 589832 | tf_op jit(solution)/shard_map/ppermute | solution.py:451
  28.6 9.8 %collective-permute-start.3 = (f32[4,48,256]{2,1,0:T(8,128)}, f32[4,48,256]{2,1,0:T(8,128)S(1)}, u32[]{:S(2)}, u32[]{:S(2)}) collective-permute-start(f32[4,48,256]{2,1,0:T(8,128)} %get-tuple-element.40), channel_id=1, source_target_pairs={{1,0},{2,1},{3,2},{4,3},{5,4},{6,5},{7,6},{9,8},{10,9},{11,10},{12... | collective-permute-start | bytes 589832 | tf_op jit(solution)/shard_map/ppermute | solution.py:451
  38.4 1.1 copy-start.1
  39.6 1.1 copy-start.3
  40.7 1.1 copy-start.5
  41.9 1.1 copy-start.7
  44.6 8.3 %collective-permute-start.4 = (f32[4,48,256]{2,1,0:T(8,128)S(1)}, f32[4,48,256]{2,1,0:T(8,128)S(1)}, u32[]{:S(2)}, u32[]{:S(2)}) collective-permute-start(f32[4,48,256]{2,1,0:T(8,128)S(1)} %get-tuple-element.45), channel_id=1, source_target_pairs={{0,1},{1,2},{2,3},{3,4},{4,5},{5,6},{6,7},{8,9},{9,10},{10,11},{11... | collective-permute-start | bytes 589832 | tf_op jit(solution)/shard_map/ppermute | solution.py:451
  49.1 9.3 %collective-permute-start.5 = (f32[4,48,256]{2,1,0:T(8,128)S(1)}, f32[4,48,256]{2,1,0:T(8,128)S(1)}, u32[]{:S(2)}, u32[]{:S(2)}) collective-permute-start(f32[4,48,256]{2,1,0:T(8,128)S(1)} %get-tuple-element.46), channel_id=1, source_target_pairs={{1,0},{2,1},{3,2},{4,3},{5,4},{6,5},{7,6},{9,8},{10,9},{11,10},{12... | collective-permute-start | bytes 589832 | tf_op jit(solution)/shard_map/ppermute | solution.py:451
  60.5 18.7 %collective-permute-start.9 = (f32[8,4,24,256]{3,2,1,0:T(8,128)S(1)}, f32[8,4,24,256]{3,2,1,0:T(8,128)S(1)}, u32[]{:S(2)}, u32[]{:S(2)}) collective-permute-start(f32[8,4,24,256]{3,2,1,0:T(8,128)S(1)} %get-tuple-element.48.refs_0_.refs_8_), channel_id=1, source_target_pairs={{0,16},{8,24},{16,0},{24,8},{1,17},{9,25},{17,1},{25,9},{2,18},{10... | collective-permute-start | bytes 2359304 | tf_op jit(solution)/shard_map/ppermute | solution.py:427
  61.0 18.7 %collective-permute-start.8 = (f32[8,4,24,256]{3,2,1,0:T(8,128)S(1)}, f32[8,4,24,256]{3,2,1,0:T(8,128)S(1)}, u32[]{:S(2)}, u32[]{:S(2)}) collective-permute-start(f32[8,4,24,256]{3,2,1,0:T(8,128)S(1)} %get-tuple-element.48.refs_0_.refs_8_), channel_id=1, source_target_pairs={{0,8},{8,0},{16,24},{24,16},{1,9},{9,1},{17,25},{25,17},{2,10},{10... | collective-permute-start | bytes 2359304 | tf_op jit(solution)/shard_map/ppermute | solution.py:427
  79.2 2.3 %collective-permute-start.10 = (f32[8,4,24,256]{3,2,1,0:T(8,128)S(1)}, f32[8,4,24,256]{3,2,1,0:T(8,128)S(1)}, u32[]{:S(2)}, u32[]{:S(2)}) collective-permute-start(f32[8,4,24,256]{3,2,1,0:T(8,128)S(1)} %collective-permute-done.9.refs_2_.refs_10_), channel_id=1, source_target_pairs={{0,8},{8,0},{16,24},{24,16},{1,9},{9,1},{17,25},{25,17},{2,10},{10... | collective-permute-start | bytes 2359304 | tf_op jit(solution)/shard_map/ppermute | solution.py:427
  79.2 22.3 %collective-permute-start.14 = (f32[8,4,24,256]{3,2,1,0:T(8,128)S(1)}, f32[8,4,24,256]{3,2,1,0:T(8,128)S(1)}, u32[]{:S(2)}, u32[]{:S(2)}) collective-permute-start(f32[8,4,24,256]{3,2,1,0:T(8,128)S(1)} %get-tuple-element.51.refs_12_), channel_id=1, source_target_pairs={{0,16},{8,24},{16,0},{24,8},{1,17},{9,25},{17,1},{25,9},{2,18},{10... | collective-permute-start | bytes 2359304 | tf_op jit(solution)/shard_map/ppermute | solution.py:427
  82.4 4.4 %collective-permute-start.11 = (f32[96,128]{1,0:T(8,128)S(1)}, f32[96,128]{1,0:T(8,128)S(1)}, u32[]{:S(2)}, u32[]{:S(2)}) collective-permute-start(f32[96,128]{1,0:T(8,128)S(1)} %gram.1), channel_id=1, source_target_pairs={{0,1},{1,0},{2,3},{3,2},{4,5},{5,4},{6,7},{7,6},{8,9},{9,8},{10,11... | collective-permute-start | bytes 147464 | tf_op jit(solution)/shard_map/ppermute | solution.py:427
  86.8 9.6 %collective-permute-start.12 = (f32[96,128]{1,0:T(8,128)S(1)}, f32[96,128]{1,0:T(8,128)S(1)}, u32[]{:S(2)}, u32[]{:S(2)}) collective-permute-start(f32[96,128]{1,0:T(8,128)S(1)} %add.17), channel_id=1, source_target_pairs={{0,2},{1,3},{2,0},{3,1},{4,6},{5,7},{6,4},{7,5},{8,10},{9,11},{10,... | collective-permute-start | bytes 147464 | tf_op jit(solution)/shard_map/ppermute | solution.py:427
  96.4 5.0 %collective-permute-start.13 = (f32[96,128]{1,0:T(8,128)S(1)}, f32[96,128]{1,0:T(8,128)S(1)}, u32[]{:S(2)}, u32[]{:S(2)}) collective-permute-start(f32[96,128]{1,0:T(8,128)S(1)} %add.18), channel_id=1, source_target_pairs={{0,4},{1,5},{2,6},{3,7},{4,0},{5,1},{6,2},{7,3},{8,12},{9,13},{10,... | collective-permute-start | bytes 147464 | tf_op jit(solution)/shard_map/ppermute | solution.py:427
  101.5 29.6 %collective-permute-start.17 = (f32[8,4,24,256]{3,2,1,0:T(8,128)S(1)}, f32[8,4,24,256]{3,2,1,0:T(8,128)S(1)}, u32[]{:S(2)}, u32[]{:S(2)}) collective-permute-start(f32[8,4,24,256]{3,2,1,0:T(8,128)S(1)} %get-tuple-element.53.refs_0_), channel_id=1, source_target_pairs={{0,16},{8,24},{16,0},{24,8},{1,17},{9,25},{17,1},{25,9},{2,18},{10... | collective-permute-start | bytes 2359304 | tf_op jit(solution)/shard_map/ppermute | solution.py:427
  102.1 1.2 collective-permute-start.15
  102.1 29.4 %collective-permute-start.20 = (f32[8,4,24,256]{3,2,1,0:T(8,128)S(1)}, f32[8,4,24,256]{3,2,1,0:T(8,128)S(1)}, u32[]{:S(2)}, u32[]{:S(2)}) collective-permute-start(f32[8,4,24,256]{3,2,1,0:T(8,128)S(1)} %get-tuple-element.51.refs_12_), channel_id=1, source_target_pairs={{0,8},{8,0},{16,24},{24,16},{1,9},{9,1},{17,25},{25,17},{2,10},{10... | collective-permute-start | bytes 2359304 | tf_op jit(solution)/shard_map/ppermute | solution.py:427
  102.6 28.9 %collective-permute-start.19 = (f32[8,4,24,256]{3,2,1,0:T(8,128)S(1)}, f32[8,4,24,256]{3,2,1,0:T(8,128)S(1)}, u32[]{:S(2)}, u32[]{:S(2)}) collective-permute-start(f32[8,4,24,256]{3,2,1,0:T(8,128)S(1)} %collective-permute-done.7.refs_12_.refs_6_), channel_id=1, source_target_pairs={{0,8},{8,0},{16,24},{24,16},{1,9},{9,1},{17,25},{25,17},{2,10},{10... | collective-permute-start | bytes 2359304 | tf_op jit(solution)/shard_map/ppermute | solution.py:427
  102.6 28.9 %collective-permute-start.16 = (f32[8,4,24,256]{3,2,1,0:T(8,128)S(1)}, f32[8,4,24,256]{3,2,1,0:T(8,128)S(1)}, u32[]{:S(2)}, u32[]{:S(2)}) collective-permute-start(f32[8,4,24,256]{3,2,1,0:T(8,128)S(1)} %get-tuple-element.53.refs_0_), channel_id=1, source_target_pairs={{0,8},{8,0},{16,24},{24,16},{1,9},{9,1},{17,25},{25,17},{2,10},{10... | collective-permute-start | bytes 2359304 | tf_op jit(solution)/shard_map/ppermute | solution.py:427
  103.3 28.2 %collective-permute-start.21 = (f32[8,4,24,256]{3,2,1,0:T(8,128)S(1)}, f32[8,4,24,256]{3,2,1,0:T(8,128)S(1)}, u32[]{:S(2)}, u32[]{:S(2)}) collective-permute-start(f32[8,4,24,256]{3,2,1,0:T(8,128)S(1)} %collective-permute-done.14.refs_14_), channel_id=1, source_target_pairs={{0,8},{8,0},{16,24},{24,16},{1,9},{9,1},{17,25},{25,17},{2,10},{10... | collective-permute-start | bytes 2359304 | tf_op jit(solution)/shard_map/ppermute | solution.py:427
  131.1 2.4 %collective-permute-start.18 = (f32[8,4,24,256]{3,2,1,0:T(8,128)S(1)}, f32[8,4,24,256]{3,2,1,0:T(8,128)S(1)}, u32[]{:S(2)}, u32[]{:S(2)}) collective-permute-start(f32[8,4,24,256]{3,2,1,0:T(8,128)S(1)} %collective-permute-done.17.refs_2_), channel_id=1, source_target_pairs={{0,8},{8,0},{16,24},{24,16},{1,9},{9,1},{17,25},{25,17},{2,10},{10... | collective-permute-start | bytes 2359304 | tf_op jit(solution)/shard_map/ppermute | solution.py:427

commit v4 on v3

--- a/solution.py
+++ b/solution.py
@@ -9,6 +9,7 @@
 
 SUBSTEPS = 6
 NEWTON = 16
+UNROLL = 5
 LANES = 128
 SCOPED = 10 * 2**20
 
@@ -42,12 +43,15 @@
 
 def wide_right(x):
     both = jnp.concatenate(split(x), axis=1)
+    rows, lanes = both.shape
+    if rows < lanes // 2:
+        both = jnp.concatenate([both, jnp.zeros((lanes // 2 - rows, lanes), bf16)], axis=0)
     return jnp.concatenate([both, both], axis=0)
 
 
-def square_dot(left, right):
+def wide_dot(left, right):
     out = jnp.dot(left, right, preferred_element_type=f32)
-    side = out.shape[0]
+    side = out.shape[1] // 2
     return out[:, :side] + out[:, side:]
 
 
@@ -285,73 +289,77 @@
     )(place, owner, omega, eta, *sources)
 
 
+def turned(x):
+    rows = x.shape[0]
+    whole = jnp.concatenate([x, jnp.zeros((LANES - rows, LANES), f32)], axis=0)
+    return whole.T[:rows]
+
+
 def batch_transform(extended, total, members):
-    side = extended.shape[0]
-    row = lax.broadcasted_iota(jnp.int32, (side, side), 0)
-    column = lax.broadcasted_iota(jnp.int32, (side, side), 1)
-    in_column = column < members
-    inside = in_column & (row < members)
+    row = lax.broadcasted_iota(jnp.int32, extended.shape, 0)
+    column = lax.broadcasted_iota(jnp.int32, extended.shape, 1)
+    inside = column < members
     last = column == members
-    identity = jnp.where((row == column) & inside, 1.0, 0.0)
-    matrix = jnp.where(in_column, extended, 0.0)
+    identity = jnp.where(row == column, 1.0, 0.0)
+    matrix = jnp.where(inside, extended, 0.0)
 
     mean = jnp.sum(total, axis=1, keepdims=True) * (1.0 / members)
-    centred = jnp.where(in_column, total - mean, 0.0)
-    product = square_dot(wide_left(matrix), wide_right(jnp.where(last, mean, centred)))
+    centred = jnp.where(inside, total - mean, 0.0)
+    product = wide_dot(wide_left(matrix), wide_right(jnp.where(last, mean, centred)))
     product = jnp.where(last, extended - product, product)
-    product = square_dot(wide_left(centred.T), wide_right(product)) * (1.0 / (members - 1))
+    product = wide_dot(wide_left(turned(centred)), wide_right(product)) * (1.0 / (members - 1))
     innovation = jnp.sum(jnp.where(last, product, 0.0), axis=1, keepdims=True)
-    system = identity + jnp.where(in_column, product, 0.0)
+    system = identity + jnp.where(inside, product, 0.0)
     frobenius = jnp.sqrt(jnp.sum(jnp.sum(system * system, axis=1, keepdims=True), axis=0, keepdims=True))
 
     scaled_root = system / frobenius
     factor = 1.5 * identity - 0.5 * scaled_root
-    scaled_root = square_dot(wide_left(scaled_root), wide_right(factor))
+    scaled_root = wide_dot(wide_left(scaled_root), wide_right(factor))
     inverse_root = factor
 
     def newton(iteration, iterates):
         scaled_root, inverse_root = iterates
-        factor = 1.5 * identity - 0.5 * square_dot(
+        factor = 1.5 * identity - 0.5 * wide_dot(
             wide_left(inverse_root), wide_right(scaled_root)
         )
         return (
-            square_dot(wide_left(scaled_root), wide_right(factor)),
-            square_dot(wide_left(factor), wide_right(inverse_root)),
+            wide_dot(wide_left(scaled_root), wide_right(factor)),
+            wide_dot(wide_left(factor), wide_right(inverse_root)),
         )
 
-    scaled_root, inverse_root = lax.fori_loop(1, NEWTON, newton, (scaled_root, inverse_root))
+    scaled_root, inverse_root = lax.fori_loop(1, NEWTON, newton, (scaled_root, inverse_root), unroll=UNROLL)
     root_inv = inverse_root / jnp.sqrt(frobenius)
     mean_weight = jnp.sum(root_inv * innovation, axis=0, keepdims=True)
     mean_weight = jnp.sum(root_inv * mean_weight, axis=1, keepdims=True)
     mixing = jnp.where(inside, root_inv + mean_weight, 0.0)
     mixing = mixing - jnp.sum(mixing, axis=0, keepdims=True) * (1.0 / members)
     mixing = jnp.where(inside, mixing + 1.0 / members, 0.0)
-    return square_dot(wide_left(total), wide_right(mixing))
+    return wide_dot(wide_left(total), wide_right(mixing))
 
 
 def transform_kernel(place, mine, other, out, ordered, work, *, offsets, blocks, rows):
     members = mine.shape[0]
-    row = lax.broadcasted_iota(jnp.int32, (LANES, LANES), 0)
-    column = lax.broadcasted_iota(jnp.int32, (LANES, LANES), 1)
-    rest = jnp.zeros((LANES - members, LANES), f32)
+    row = lax.broadcasted_iota(jnp.int32, (members, LANES), 0)
+    column = lax.broadcasted_iota(jnp.int32, (members, LANES), 1)
+    inside = column < members
 
     def pick(where, x):
         return jnp.sum(jnp.where(where, x, 0.0), axis=1, keepdims=True)
 
     for half, shared in ((place[0], mine), (1 - place[0], other)):
-        packed = jnp.concatenate([shared[...], rest], axis=0)
-        inside = column < members
+        packed = shared[...]
         above = jnp.where(inside & (column > row), packed, 0.0)
         below = jnp.where(inside & (column < row), packed, 0.0)
-        middle = jnp.where(inside & (column == row), packed, 0.0)
+        middle = jnp.where(column == row, packed, 0.0)
         side = jnp.where(column == members, pick(column == members + 1, packed), 0.0)
-        ordered[2 * half] = above + above.T + (middle + side)
-        middle = jnp.where(inside & (column == row), pick(column == members, packed), 0.0)
+        ordered[2 * half] = above + turned(above) + (middle + side)
+        middle = jnp.where(column == row, pick(column == members, packed), 0.0)
         side = jnp.where(column == members, pick(column == members + 2, packed), 0.0)
-        ordered[2 * half + 1] = below + below.T + (middle + side)
-    total = jnp.where((row == column) & (row < members), 1.0, 0.0)
+        ordered[2 * half + 1] = below + turned(below) + (middle + side)
+    total = jnp.where(row == column, 1.0, 0.0)
     for batch in range(ordered.shape[0]):
         total = batch_transform(ordered[batch], total, members)
+    total = jnp.concatenate([total, jnp.zeros((LANES - members, LANES), f32)], axis=0)
     work[...] = total
     if blocks == 1:
         out[...] = total.T
@@ -373,7 +381,7 @@
         in_specs=[SMEM, VMEM, VMEM],
         out_specs=VMEM,
         scratch_shapes=[
-            pltpu.VMEM((4, LANES, LANES), f32),
+            pltpu.VMEM((4, members, LANES), f32),
             pltpu.VMEM((LANES, LANES), f32),
         ],
         compiler_params=pltpu.CompilerParams(vmem_limit_bytes=SCOPED),
@@ -384,9 +392,9 @@
     )(place, mine, other)
 
 
-def mix_kernel(weights, *refs, blocks):
+def mix_kernel(weights, *refs, blocks, kinds, begin):
     *sources, out = refs
-    rows, species, _, nz, ny = out.shape
+    rows, _, _, nz, _ = out.shape
     x = pl.program_id(0)
     members = blocks * sources[0].shape[2]
     high, low = split(weights[:, :members])
@@ -396,30 +404,40 @@
     )
     for z in range(nz):
         mixed = []
-        for kind in range(species):
+        for kind in range(kinds):
             parts = [sources[kind * blocks + j][x, z] for j in range(blocks)]
             values = parts[0] if blocks == 1 else jnp.concatenate(parts, axis=0)
             value_high, value_low = split(values)
             upper = mul(both, value_high)
             mixed.append(upper[:rows] + (upper[rows:] + mul(high, value_low)))
-        mixed[1] = mixed[1] - mixed[2]
-        mixed[2] = mixed[2] - mixed[3]
-        for kind in range(species):
-            out[:, kind, 0, z, :] = mixed[kind]
-
-
-def mix(weights, sources, blocks, rows):
-    nx, nz, held, ny = sources[0].shape
-    species = len(sources) // blocks
+        for kind in range(kinds - 1):
+            mixed[kind] = mixed[kind] - mixed[kind + 1]
+        for kind in range(kinds):
+            out[:, begin + kind, 0, z, :] = mixed[kind]
+
+
+def mix(weights, sources, blocks, shape, kinds, begin, result=None):
+    rows, _, nx, nz, ny = shape
+    count = len(sources)
+    before = [] if result is None else [result]
+    cells = nx * nz * ny * rows * kinds
+
+    def body(*refs):
+        mix_kernel(*refs[: 1 + count], refs[-1], blocks=blocks, kinds=kinds, begin=begin)
+
     return pl.pallas_call(
-        functools.partial(mix_kernel, blocks=blocks),
+        body,
         grid=(nx,),
-        out_shape=jax.ShapeDtypeStruct((rows, species, nx, nz, ny), f32),
-        in_specs=[VMEM] * (1 + len(sources)),
-        out_specs=pl.BlockSpec((rows, species, 1, nz, ny), lambda x: (0, 0, x, 0, 0)),
+        out_shape=jax.ShapeDtypeStruct(shape, f32),
+        in_specs=[VMEM] * (1 + count) + [pl.BlockSpec(memory_space=pl.ANY)] * len(before),
+        out_specs=pl.BlockSpec((rows, begin + kinds, 1, nz, ny), lambda x: (0, 0, x, 0, 0)),
+        input_output_aliases={} if result is None else {1 + count: 0},
         compiler_params=pltpu.CompilerParams(vmem_limit_bytes=SCOPED),
+        cost_estimate=pl.CostEstimate(
+            flops=1000 * cells, bytes_accessed=4 * cells, transcendentals=0
+        ),
         name="mix",
-    )(weights, *sources)
+    )(weights, *sources, *before)
 
 
 def swap(x, axis, bit):
@@ -500,9 +518,10 @@
     for step in range(steps):
         final = step == steps - 1
         ready = ()
-        if step == 1:
+        if step == 0:
+            ready = (omega, eta)
+        elif step == 1:
             conserved = collect(lax.optimization_barrier((conserved, fields[0]))[0])
-            ready = (omega, eta)
         elif step == 2:
             ready = conserved[1:]
         *fields, = forecast_call(
@@ -530,7 +549,9 @@
     free = complete(free, weights)
     if blocks == 1:
         weights = lax.dynamic_slice(weights, (member * rows, 0), (rows, LANES))
-    return mix(weights, free + conserved + tracer + internal, blocks, rows)
+    bound = conserved + tracer + internal
+    result = mix(weights, bound, blocks, ensemble.shape, species - 1, 1)
+    return mix(weights, free, blocks, ensemble.shape, 1, 0, result)
 
 
 def solution(mesh):

time: 139 us -> 130 us (0.935)
  starting transfers between devices: 32.5 us -> 26.2 us
  local copies, waits for them, and re-layouts: 13.1 us -> 8.42 us
  Pallas kernels: 41.1 us -> 43.9 us
  waiting for transfers between devices: 49.8 us -> 47 us
    unnamed x32 -> x22, local copies, waits for them, and re-layouts: 8.14 us -> 0.05 us
    ppermute x16, starting transfers between devices: 14.8 us -> 8.36 us  [swap(): return lax.ppermute(x, axis, [(k, k ^ bit) for k in range(count)])]
    pallas_call x1, Pallas kernels: 0.86 us -> 4.08 us  [gram(): pl.pallas_call(functools.partial(gram_kernel, offsets=offsets), out_shape...]
    pallas_call x1 -> x2, Pallas kernels: 5.16 us -> 8.35 us  [mix(): pl.pallas_call(body, grid=(nx,), out_shape=jax.ShapeDtypeStruct(shape, f3...]
    pallas_call x1, Pallas kernels: 27.6 us -> 24.6 us  [transforms(): pl.pallas_call(functools.partial(transform_kernel, offsets=offsets, block...]
    transpose x2, local copies, waits for them, and re-layouts: 2.04 us -> 4.64 us  [local(): jnp.transpose(ensemble[:, k], (1, 2, 0, 3))]
    ppermute x3, waiting for transfers between devices: 8.39 us -> 5.91 us  [halos(): lax.ppermute(last, 'space', forward)]
  transfers between devices with their start and end apart: 22 -> 22, of which waited for: 12 -> 10; matrix products, arithmetic and copies ran while one was open for 3% -> 7% of each run, Pallas kernels for 23% -> 28%
where the time goes in v4:
time: 130 us; the launch traced here: 128 us
  waiting for transfers between devices  47 us (36%)
  Pallas kernels  43.9 us (34%)
  starting transfers between devices  26.2 us (20%)
  local copies, waits for them, and re-layouts  8.42 us (6%)
  other arithmetic  2.5 us (2%)
    ppermute x16, waiting for transfers between devices, swap(): return lax.ppermute(x, axis, [(k, k ^ bit) for k in range(count)])  30.7 us
    pallas_call x1, Pallas kernels, transforms(): pl.pallas_call(functools.partial(transform_kernel, offsets=offsets, block...  24.6 us
    ppermute x3, starting transfers between devices, halos(): lax.ppermute(last, 'space', forward)  14 us
    ppermute x3, waiting for transfers between devices, halos(): lax.ppermute(first, 'space', backward)  10.4 us
    ppermute x16, starting transfers between devices, swap(): return lax.ppermute(x, axis, [(k, k ^ bit) for k in range(count)])  8.36 us
    pallas_call x2, Pallas kernels, mix(): pl.pallas_call(body, grid=(nx,), out_shape=jax.ShapeDtypeStruct(shape, f3...  8.35 us
    ppermute x3, waiting for transfers between devices, halos(): lax.ppermute(last, 'space', forward)  5.91 us
    pallas_call x4, Pallas kernels, forecast_call(): pl.pallas_call(body, out_shape=[jax.ShapeDtypeStruct(shape, f32) for shap...  5.48 us
  transfers between devices with their start and end apart: 22, of which 10 were waited for; matrix products, arithmetic and copies ran while one was open for 7% of the time, Pallas kernels for 28%

profile of v4, /device:TPU:0, one launch (start us, length us, event | category | flops | bytes accessed | tf_op | source)
XLA Modules:
  0.0 128.3 jit_solution(15158003351288044988)
XLA Ops:
  0.0 1.6 %fusion = (f32[24,3,2,4,256]{4,3,2,1,0:T(4,128)S(1)}, f32[24,3,2,4,256]{4,3,2,1,0:T(4,128)S(1)}) fusion(f32[24,4,8,4,256]{4,3,2,1,0:T(4,128)} %param.8), kind=kLoop, calls=%fused_computation.8 | loop fusion | bytes 2359296 | tf_op jit(solution)/shard_map/slice | solution.py:501
  1.6 0.4 copy_bitcast_fusion.4
  2.0 0.0 copy-done.2
  2.0 0.2 first_edges.1
  2.2 4.9 %collective-permute-start = (f32[4,56,256]{2,1,0:T(8,128)S(1)}, f32[4,56,256]{2,1,0:T(8,128)S(1)}, u32[]{:S(2)}, u32[]{:S(2)}) collective-permute-start(f32[4,56,256]{2,1,0:T(8,128)S(1)} %get-tuple-element.33), channel_id=1, source_target_pairs={{0,1},{1,2},{2,3},{3,4},{4,5},{5,6},{6,7},{8,9},{9,10},{10,11},{11... | collective-permute-start | bytes 688136 | tf_op jit(solution)/shard_map/ppermute | solution.py:469
  7.1 1.3 %collective-permute-start.1 = (f32[4,56,256]{2,1,0:T(8,128)S(1)}, f32[4,56,256]{2,1,0:T(8,128)S(1)}, u32[]{:S(2)}, u32[]{:S(2)}) collective-permute-start(f32[4,56,256]{2,1,0:T(8,128)S(1)} %get-tuple-element.34), channel_id=1, source_target_pairs={{1,0},{2,1},{3,2},{4,3},{5,4},{6,5},{7,6},{9,8},{10,9},{11,10},{12... | collective-permute-start | bytes 688136 | tf_op jit(solution)/shard_map/ppermute | solution.py:469
  8.4 1.8 %fusion.1 = (f32[24,1,8,4,256]{4,3,2,1,0:T(4,128)S(1)}, f32[24,1,8,4,256]{4,3,2,1,0:T(4,128)}, f32[24,1,8,4,256]{4,3,2,1,0:T(4,128)}, f32[24,1,8,4,256]{4,3,2,1,0:T(4,128)}) fusion(f32[24,4,8,4,256]{4,3,2,1,0:T(4,128)S(1)} %copy-done.10), kind=kLoop, calls=%fused_computation.9 | loop fusion | bytes 6291456 | tf_op jit(solution)/shard_map/slice | solution.py:511
  10.2 0.0 copy-start.4
  10.2 0.0 copy-start.5
  10.2 0.0 copy-start.6
  10.2 2.4 %copy_bitcast_fusion = (f32[8,4,24,256]{3,2,1,0:T(8,128)S(1)}, f32[8,4,24,256]{3,2,1,0:T(8,128)S(1)}) fusion(f32[24,1,8,4,256]{4,3,2,1,0:T(4,128)S(1)} %get-tuple-element.59, f32[24,1,8,4,256]{4,3,2,1,0:T(4,128)} %get-tuple-element.60), kind=kLoop, calls=%fused_computation | loop fusion | bytes 3145728 | tf_op jit(solution)/shard_map/transpose | solution.py:511
  12.6 2.4 %add_add_fusion.refs_1_ = f32[8,4,24,256]{3,2,1,0:T(8,128)S(1)} fusion(f32[24,1,8,4,256]{4,3,2,1,0:T(4,128)S(1)} %copy-done.7, f32[24,1,8,4,256]{4,3,2,1,0:T(4,128)S(1)} %copy-done.9, f32[24,1,8,4,256]{4,3,2,1,0:T(4,128)} %copy-done.8), kind=kLoop, calls=%fused_computation.4 | loop fusion | flops 393216 | bytes 3145728 | tf_op jit(solution)/shard_map/add | solution.py:512
  15.0 0.1 pad_add_fusion.place
  15.1 1.4 %voxel_weights.1 = (f32[2,32,256]{2,1,0:T(8,128)S(1)}, f32[2,32,256]{2,1,0:T(8,128)S(1)}) custom-call(s32[3]{0:T(128)S(1)} %pad_add_fusion.place, s32[4]{0:T(128)S(1)} %copy-done.6, s32[4,2048]{1,0:T(4,128)S(1)} %copy-done.3, f32[4,2048]{1,0:T(4,128)S(1)} %copy-done.4, f32[4,2048]{1,0:T(4,128)S(1)} %copy-done.5), custom_call_target="tpu_custom_call" | custom-call | tf_op jit(solution)/shard_map/voxel_weights/pallas_call | solution.py:226
  16.6 2.3 %copy_bitcast_fusion.2 = (f32[8,4,24,256]{3,2,1,0:T(8,128)S(1)}, f32[8,4,24,256]{3,2,1,0:T(8,128)S(1)}) fusion(f32[24,1,8,4,256]{4,3,2,1,0:T(4,128)} %get-tuple-element.61, f32[24,1,8,4,256]{4,3,2,1,0:T(4,128)} %get-tuple-element.62), kind=kLoop, calls=%fused_computation.2 | loop fusion | bytes 3145728 | tf_op jit(solution)/shard_map/transpose | solution.py:511
  18.8 0.0 collective-permute-done.refs_4_.refs_6_
  18.9 0.0 collective-permute-done.1.refs_5_.refs_7_
  18.9 1.6 %two_substeps.3 = (f32[8,4,24,256]{3,2,1,0:T(8,128)S(1)}, f32[8,4,24,256]{3,2,1,0:T(8,128)S(1)}, f32[8,4,24,256]{3,2,1,0:T(8,128)S(1)}, f32[8,4,24,256]{3,2,1,0:...) custom-call(f32[8,4,24,256]{3,2,1,0:T(8,128)S(1)} %get-tuple-element.66.refs_0_, ...), custom_call_target="tpu_custom_call" | custom-call | flops 11796480 | bytes 12582912 | tf_op jit(solution)/shard_map/two_substeps/pallas_call | solution.py:176
  20.4 1.6 %collective-permute-start.7 = (f32[8,4,24,256]{3,2,1,0:T(8,128)S(1)}, f32[8,4,24,256]{3,2,1,0:T(8,128)S(1)}, u32[]{:S(2)}, u32[]{:S(2)}) collective-permute-start(f32[8,4,24,256]{3,2,1,0:T(8,128)S(1)} %add_add_fusion.refs_1_), channel_id=1, source_target_pairs={{0,16},{8,24},{16,0},{24,8},{1,17},{9,25},{17,1},{25,9},{2,18},{10... | collective-permute-start | bytes 2359304 | tf_op jit(solution)/shard_map/ppermute | solution.py:445
  22.0 0.0 collective-permute-start.6
  22.0 4.5 %collective-permute-start.2 = (f32[4,48,256]{2,1,0:T(8,128)S(1)}, f32[4,48,256]{2,1,0:T(8,128)S(1)}, u32[]{:S(2)}, u32[]{:S(2)}) collective-permute-start(f32[4,48,256]{2,1,0:T(8,128)S(1)} %get-tuple-element.39), channel_id=1, source_target_pairs={{0,1},{1,2},{2,3},{3,4},{4,5},{5,6},{6,7},{8,9},{9,10},{10,11},{11... | collective-permute-start | bytes 589832 | tf_op jit(solution)/shard_map/ppermute | solution.py:469
  26.6 1.3 %collective-permute-start.3 = (f32[4,48,256]{2,1,0:T(8,128)S(1)}, f32[4,48,256]{2,1,0:T(8,128)S(1)}, u32[]{:S(2)}, u32[]{:S(2)}) collective-permute-start(f32[4,48,256]{2,1,0:T(8,128)S(1)} %get-tuple-element.40), channel_id=1, source_target_pairs={{1,0},{2,1},{3,2},{4,3},{5,4},{6,5},{7,6},{9,8},{10,9},{11,10},{12... | collective-permute-start | bytes 589832 | tf_op jit(solution)/shard_map/ppermute | solution.py:469
  27.9 3.5 %collective-permute-done.2.refs_4_ = f32[4,48,256]{2,1,0:T(8,128)S(1)} collective-permute-done((f32[4,48,256]{2,1,0:T(8,128)S(1)}, f32[4,48,256]{2,1,0:T(8,128)S(1)}, u32[]{:S(2)}, u32[]{:S(2)}) %collective-permute-start.2) | collective-permute-done | bytes 196640 | tf_op jit(solution)/shard_map/ppermute | solution.py:469
  31.4 4.8 %collective-permute-done.3.refs_5_ = f32[4,48,256]{2,1,0:T(8,128)S(1)} collective-permute-done((f32[4,48,256]{2,1,0:T(8,128)S(1)}, f32[4,48,256]{2,1,0:T(8,128)S(1)}, u32[]{:S(2)}, u32[]{:S(2)}) %collective-permute-start.3) | collective-permute-done | bytes 196640 | tf_op jit(solution)/shard_map/ppermute | solution.py:469
  36.2 1.6 %two_substeps.4 = (f32[8,4,24,256]{3,2,1,0:T(8,128)S(1)}, f32[8,4,24,256]{3,2,1,0:T(8,128)S(1)}, f32[8,4,24,256]{3,2,1,0:T(8,128)S(1)}, f32[8,4,24,256]{3,2,1,0:...) custom-call(f32[8,4,24,256]{3,2,1,0:T(8,128)S(1)} %get-tuple-element.35.refs_0_, ...), custom_call_target="tpu_custom_call" | custom-call | flops 11796480 | bytes 12582912 | tf_op jit(solution)/shard_map/two_substeps/pallas_call | solution.py:176
  37.8 4.5 %collective-permute-start.4 = (f32[4,48,256]{2,1,0:T(8,128)S(1)}, f32[4,48,256]{2,1,0:T(8,128)S(1)}, u32[]{:S(2)}, u32[]{:S(2)}) collective-permute-start(f32[4,48,256]{2,1,0:T(8,128)S(1)} %get-tuple-element.45), channel_id=1, source_target_pairs={{0,1},{1,2},{2,3},{3,4},{4,5},{5,6},{6,7},{8,9},{9,10},{10,11},{11... | collective-permute-start | bytes 589832 | tf_op jit(solution)/shard_map/ppermute | solution.py:469
  42.4 1.3 %collective-permute-start.5 = (f32[4,48,256]{2,1,0:T(8,128)S(1)}, f32[4,48,256]{2,1,0:T(8,128)S(1)}, u32[]{:S(2)}, u32[]{:S(2)}) collective-permute-start(f32[4,48,256]{2,1,0:T(8,128)S(1)} %get-tuple-element.46), channel_id=1, source_target_pairs={{1,0},{2,1},{3,2},{4,3},{5,4},{6,5},{7,6},{9,8},{10,9},{11,10},{12... | collective-permute-start | bytes 589832 | tf_op jit(solution)/shard_map/ppermute | solution.py:469
  43.7 2.4 %collective-permute-done.4.refs_4_ = f32[4,48,256]{2,1,0:T(8,128)S(1)} collective-permute-done((f32[4,48,256]{2,1,0:T(8,128)S(1)}, f32[4,48,256]{2,1,0:T(8,128)S(1)}, u32[]{:S(2)}, u32[]{:S(2)}) %collective-permute-start.4) | collective-permute-done | bytes 196640 | tf_op jit(solution)/shard_map/ppermute | solution.py:469
  46.1 5.6 %collective-permute-done.5.refs_5_ = f32[4,48,256]{2,1,0:T(8,128)S(1)} collective-permute-done((f32[4,48,256]{2,1,0:T(8,128)S(1)}, f32[4,48,256]{2,1,0:T(8,128)S(1)}, u32[]{:S(2)}, u32[]{:S(2)}) %collective-permute-start.5) | collective-permute-done | bytes 196640 | tf_op jit(solution)/shard_map/ppermute | solution.py:469
  51.7 0.0 collective-permute-done.7.refs_12_.refs_3_
  51.7 0.0 collective-permute-done.6.refs_11_.refs_2_
  51.7 2.1 %two_substeps.5 = (f32[8,4,24,256]{3,2,1,0:T(8,128)S(1)}, f32[8,4,24,256]{3,2,1,0:T(8,128)}, f32[8,4,24,256]{3,2,1,0:T(8,128)S(1)}, f32[8,4,24,256]{3,2,1,0:T(8,128)S(1)}) custom-call(f32[8,4,24,256]{3,2,1,0:T(8,128)S(1)} %get-tuple-element.41.refs_0_, f32[8,4,24,256]{3,2,1,0:T(8,128)S(1)} %get-tuple-element.42.refs_1_, ...), custom_call_target="tpu_custom_call" | custom-call | flops 11796480 | bytes 12582912 | tf_op jit(solution)/shard_map/two_substeps/pallas_call | solution.py:176
  53.8 0.5 collective-permute-start.9
  54.3 0.0 collective-permute-start.8
  54.3 18.2 %collective-permute-done.9.refs_2_.refs_7_ = f32[8,4,24,256]{3,2,1,0:T(8,128)S(1)} collective-permute-done((f32[8,4,24,256]{3,2,1,0:T(8,128)S(1)}, f32[8,4,24,256]{3,2,1,0:T(8,128)S(1)}, u32[]{:S(2)}, u32[]{:S(2)}) %collective-permute-start.9) | collective-permute-done | bytes 786464 | tf_op jit(solution)/shard_map/ppermute | solution.py:445
  72.5 0.0 collective-permute-start.10
  72.5 0.5 collective-permute-start.14
  73.0 0.0 collective-permute-done.8.refs_1_.refs_6_
  73.0 1.8 %collective-permute-done.10.refs_3_.refs_8_ = f32[8,4,24,256]{3,2,1,0:T(8,128)S(1)} collective-permute-done((f32[8,4,24,256]{3,2,1,0:T(8,128)S(1)}, f32[8,4,24,256]{3,2,1,0:T(8,128)S(1)}, u32[]{:S(2)}, u32[]{:S(2)}) %collective-permute-start.10) | collective-permute-done | bytes 786464 | tf_op jit(solution)/shard_map/ppermute | solution.py:445
  74.8 4.1 %gram.1 = f32[96,128]{1,0:T(8,128)S(1)} custom-call(s32[3]{0:T(128)S(1)} %pad_add_fusion.place, s32[4]{0:T(128)S(1)} %copy-done.6, f32[2,32,256]{2,1,0:T(8,128)S(1)} %get-tuple-element.31.refs_11_.omega, f32[2,32,256]{2,1,0:T(8,128)S(1)} %get-tuple-element.32.refs_12_.eta, f32[8,4,24,256]{3,2,1,0:T(8,128)S(1)} %get-tuple-element.48.refs_0_.refs_5_, ...), custom_call_target="tpu_custom_call" | custom-call | tf_op jit(solution)/shard_map/gram/pallas_call | solution.py:281
  78.9 0.1 collective-permute-start.11
  78.9 4.4 %collective-permute-done.11 = f32[96,128]{1,0:T(8,128)S(1)} collective-permute-done((f32[96,128]{1,0:T(8,128)S(1)}, f32[96,128]{1,0:T(8,128)S(1)}, u32[]{:S(2)}, u32[]{:S(2)}) %collective-permute-start.11) | collective-permute-done | bytes 49184 | tf_op jit(solution)/shard_map/ppermute | solution.py:445
  83.3 1.1 collective-permute-start.12
  84.4 3.0 %collective-permute-done.12 = f32[96,128]{1,0:T(8,128)S(1)} collective-permute-done((f32[96,128]{1,0:T(8,128)S(1)}, f32[96,128]{1,0:T(8,128)S(1)}, u32[]{:S(2)}, u32[]{:S(2)}) %collective-permute-start.12) | collective-permute-done | bytes 49184 | tf_op jit(solution)/shard_map/ppermute | solution.py:445
  87.5 2.4 %collective-permute-start.13 = (f32[96,128]{1,0:T(8,128)S(1)}, f32[96,128]{1,0:T(8,128)S(1)}, u32[]{:S(2)}, u32[]{:S(2)}) collective-permute-start(f32[96,128]{1,0:T(8,128)S(1)} %add.18), channel_id=1, source_target_pairs={{0,4},{1,5},{2,6},{3,7},{4,0},{5,1},{6,2},{7,3},{8,12},{9,13},{10,... | collective-permute-start | bytes 147464 | tf_op jit(solution)/shard_map/ppermute | solution.py:445
  89.9 3.1 %collective-permute-done.13 = f32[96,128]{1,0:T(8,128)S(1)} collective-permute-done((f32[96,128]{1,0:T(8,128)S(1)}, f32[96,128]{1,0:T(8,128)S(1)}, u32[]{:S(2)}, u32[]{:S(2)}) %collective-permute-start.13) | collective-permute-done | bytes 49184 | tf_op jit(solution)/shard_map/ppermute | solution.py:445
  93.0 0.0 collective-permute-done.14.refs_11_
  93.0 0.6 collective-permute-start.17
  93.6 0.0 collective-permute-start.15
  93.6 0.5 collective-permute-start.20
  94.1 0.0 collective-permute-start.19
  94.1 0.5 collective-permute-start.21
  94.6 0.2 collective-permute-done.15.other
  94.8 0.2 collective-permute-start.16
  95.0 24.6 %transforms.1.refs_0_ = f32[24,128]{1,0:T(8,128)S(1)} custom-call(s32[3]{0:T(128)S(1)} %pad_add_fusion.place, f32[96,128]{1,0:T(8,128)S(1)} %add.19.mine, f32[96,128]{1,0:T(8,128)S(1)} %collective-permute-done.15.other), custom_call_target="tpu_custom_call" | custom-call | flops 100000000 | bytes 1000000 | tf_op jit(solution)/shard_map/transforms/pallas_call | solution.py:378
  119.5 0.0 collective-permute-done.17.refs_3_
  119.6 0.4 collective-permute-start.18
  120.0 0.0 collective-permute-done.20.refs_10_
  120.0 0.0 collective-permute-done.19.refs_4_
  120.0 0.0 collective-permute-done.21.refs_12_
  120.0 4.7 %mix.2.refs_5_ = f32[24,4,8,4,256]{4,3,2,1,0:T(4,128)} custom-call(f32[24,128]{1,0:T(8,128)S(1)} %transforms.1.refs_0_, f32[8,4,24,256]{3,2,1,0:T(8,128)S(1)} %add_add_fusion.refs_1_, f32[8,4,24,256]{3,2,1,0:T(8,128)S(1)} %collective-permute-done.6.refs_11_.refs_2_, f32[8,4,24,256]{3,2,1,0:T(8,128)S(1)} %collective-permute-done.7.refs_12_.refs_3_, ...), custom_call_target="tpu_custom_call" | custom-call | flops 589824000 | bytes 2359296 | tf_op jit(solution)/shard_map/mix/pallas_call | solution.py:428
  124.7 0.0 collective-permute-done.16.refs_2_
  124.7 0.0 collective-permute-done.18.refs_4_
  124.7 3.6 %mix.3 = f32[24,4,8,4,256]{4,3,2,1,0:T(4,128)} custom-call(f32[24,128]{1,0:T(8,128)S(1)} %transforms.1.refs_0_, f32[8,4,24,256]{3,2,1,0:T(8,128)S(1)} %get-tuple-element.53.refs_1_, f32[8,4,24,256]{3,2,1,0:T(8,128)S(1)} %collective-permute-done.16.refs_2_, f32[8,4,24,256]{3,2,1,0:T(8,128)S(1)} %collective-permute-done.17.refs_3_, ...), custom_call_target="tpu_custom_call", output_to_operand_aliasing={{}: (5, {})} | custom-call | flops 196608000 | bytes 786432 | tf_op jit(solution)/shard_map/mix/pallas_call | solution.py:428
  (21 shorter events, 0.1 us)
Async XLA Ops:
  0.0 8.4 %copy-start.10 = (f32[24,4,8,4,256]{4,3,2,1,0:T(4,128)S(1)}, f32[24,4,8,4,256]{4,3,2,1,0:T(4,128)}, u32[]{:S(2)}) copy-start(f32[24,4,8,4,256]{4,3,2,1,0:T(4,128)} %param.8) | copy-start | bytes 9437188
  0.0 2.0 %copy-start.2 = (f32[8,4,256]{2,1,0:T(4,128)S(1)}, f32[8,4,256]{2,1,0:T(4,128)}, u32[]{:S(2)}) copy-start(f32[8,4,256]{2,1,0:T(4,128)} %refs_10_.5) | copy-start | bytes 98308
  0.0 2.0 %copy-start.1 = (f32[8,4,256]{2,1,0:T(4,128)S(1)}, f32[8,4,256]{2,1,0:T(4,128)}, u32[]{:S(2)}) copy-start(f32[8,4,256]{2,1,0:T(4,128)} %refs_9_.5) | copy-start | bytes 98308
  0.0 2.0 %copy-start = (f32[8,4,256]{2,1,0:T(4,128)S(1)}, f32[8,4,256]{2,1,0:T(4,128)}, u32[]{:S(2)}) copy-start(f32[8,4,256]{2,1,0:T(4,128)} %refs_8_.5) | copy-start | bytes 98308
  2.2 16.6 %collective-permute-start = (f32[4,56,256]{2,1,0:T(8,128)S(1)}, f32[4,56,256]{2,1,0:T(8,128)S(1)}, u32[]{:S(2)}, u32[]{:S(2)}) collective-permute-start(f32[4,56,256]{2,1,0:T(8,128)S(1)} %get-tuple-element.33), channel_id=1, source_target_pairs={{0,1},{1,2},{2,3},{3,4},{4,5},{5,6},{6,7},{8,9},{9,10},{10,11},{11... | collective-permute-start | bytes 688136 | tf_op jit(solution)/shard_map/ppermute | solution.py:469
  7.1 11.7 %collective-permute-start.1 = (f32[4,56,256]{2,1,0:T(8,128)S(1)}, f32[4,56,256]{2,1,0:T(8,128)S(1)}, u32[]{:S(2)}, u32[]{:S(2)}) collective-permute-start(f32[4,56,256]{2,1,0:T(8,128)S(1)} %get-tuple-element.34), channel_id=1, source_target_pairs={{1,0},{2,1},{3,2},{4,3},{5,4},{6,5},{7,6},{9,8},{10,9},{11,10},{12... | collective-permute-start | bytes 688136 | tf_op jit(solution)/shard_map/ppermute | solution.py:469
  10.2 2.4 %copy-start.8 = (f32[24,1,8,4,256]{4,3,2,1,0:T(4,128)}, f32[24,1,8,4,256]{4,3,2,1,0:T(4,128)S(1)}, u32[]{:S(2)}) copy-start(f32[24,1,8,4,256]{4,3,2,1,0:T(4,128)S(1)} %get-tuple-element.59) | copy-start | bytes 2359300
  10.2 2.4 %copy-start.7 = (f32[24,1,8,4,256]{4,3,2,1,0:T(4,128)S(1)}, f32[24,1,8,4,256]{4,3,2,1,0:T(4,128)}, u32[]{:S(2)}) copy-start(f32[24,1,8,4,256]{4,3,2,1,0:T(4,128)} %get-tuple-element.61) | copy-start | bytes 2359300
  10.2 2.4 %copy-start.9 = (f32[24,1,8,4,256]{4,3,2,1,0:T(4,128)S(1)}, f32[24,1,8,4,256]{4,3,2,1,0:T(4,128)}, u32[]{:S(2)}) copy-start(f32[24,1,8,4,256]{4,3,2,1,0:T(4,128)} %get-tuple-element.60) | copy-start | bytes 2359300
  10.2 4.9 %copy-start.3 = (s32[4,2048]{1,0:T(4,128)S(1)}, s32[4,2048]{1,0:T(4,128)}, u32[]{:S(2)}) copy-start(s32[4,2048]{1,0:T(4,128)} %obs_index.1) | copy-start | bytes 98308
  10.2 4.9 %copy-start.4 = (f32[4,2048]{1,0:T(4,128)S(1)}, f32[4,2048]{1,0:T(4,128)}, u32[]{:S(2)}) copy-start(f32[4,2048]{1,0:T(4,128)} %observed.1) | copy-start | bytes 98308
  10.2 4.9 %copy-start.5 = (f32[4,2048]{1,0:T(4,128)S(1)}, f32[4,2048]{1,0:T(4,128)}, u32[]{:S(2)}) copy-start(f32[4,2048]{1,0:T(4,128)} %obs_var.1) | copy-start | bytes 98308
  10.2 4.9 %copy-start.6 = (s32[4]{0:T(128)S(1)}, s32[4]{0:T(128)}, u32[]{:S(2)}) copy-start(s32[4]{0:T(128)} %owner.3) | copy-start | bytes 52
  20.4 31.3 %collective-permute-start.7 = (f32[8,4,24,256]{3,2,1,0:T(8,128)S(1)}, f32[8,4,24,256]{3,2,1,0:T(8,128)S(1)}, u32[]{:S(2)}, u32[]{:S(2)}) collective-permute-start(f32[8,4,24,256]{3,2,1,0:T(8,128)S(1)} %add_add_fusion.refs_1_), channel_id=1, source_target_pairs={{0,16},{8,24},{16,0},{24,8},{1,17},{9,25},{17,1},{25,9},{2,18},{10... | collective-permute-start | bytes 2359304 | tf_op jit(solution)/shard_map/ppermute | solution.py:445
  22.0 29.7 %collective-permute-start.6 = (f32[8,4,24,256]{3,2,1,0:T(8,128)S(1)}, f32[8,4,24,256]{3,2,1,0:T(8,128)S(1)}, u32[]{:S(2)}, u32[]{:S(2)}) collective-permute-start(f32[8,4,24,256]{3,2,1,0:T(8,128)S(1)} %add_add_fusion.refs_1_), channel_id=1, source_target_pairs={{0,8},{8,0},{16,24},{24,16},{1,9},{9,1},{17,25},{25,17},{2,10},{10... | collective-permute-start | bytes 2359304 | tf_op jit(solution)/shard_map/ppermute | solution.py:445
  22.0 9.4 %collective-permute-start.2 = (f32[4,48,256]{2,1,0:T(8,128)S(1)}, f32[4,48,256]{2,1,0:T(8,128)S(1)}, u32[]{:S(2)}, u32[]{:S(2)}) collective-permute-start(f32[4,48,256]{2,1,0:T(8,128)S(1)} %get-tuple-element.39), channel_id=1, source_target_pairs={{0,1},{1,2},{2,3},{3,4},{4,5},{5,6},{6,7},{8,9},{9,10},{10,11},{11... | collective-permute-start | bytes 589832 | tf_op jit(solution)/shard_map/ppermute | solution.py:469
  26.6 9.6 %collective-permute-start.3 = (f32[4,48,256]{2,1,0:T(8,128)S(1)}, f32[4,48,256]{2,1,0:T(8,128)S(1)}, u32[]{:S(2)}, u32[]{:S(2)}) collective-permute-start(f32[4,48,256]{2,1,0:T(8,128)S(1)} %get-tuple-element.40), channel_id=1, source_target_pairs={{1,0},{2,1},{3,2},{4,3},{5,4},{6,5},{7,6},{9,8},{10,9},{11,10},{12... | collective-permute-start | bytes 589832 | tf_op jit(solution)/shard_map/ppermute | solution.py:469
  37.8 8.3 %collective-permute-start.4 = (f32[4,48,256]{2,1,0:T(8,128)S(1)}, f32[4,48,256]{2,1,0:T(8,128)S(1)}, u32[]{:S(2)}, u32[]{:S(2)}) collective-permute-start(f32[4,48,256]{2,1,0:T(8,128)S(1)} %get-tuple-element.45), channel_id=1, source_target_pairs={{0,1},{1,2},{2,3},{3,4},{4,5},{5,6},{6,7},{8,9},{9,10},{10,11},{11... | collective-permute-start | bytes 589832 | tf_op jit(solution)/shard_map/ppermute | solution.py:469
  42.4 9.3 %collective-permute-start.5 = (f32[4,48,256]{2,1,0:T(8,128)S(1)}, f32[4,48,256]{2,1,0:T(8,128)S(1)}, u32[]{:S(2)}, u32[]{:S(2)}) collective-permute-start(f32[4,48,256]{2,1,0:T(8,128)S(1)} %get-tuple-element.46), channel_id=1, source_target_pairs={{1,0},{2,1},{3,2},{4,3},{5,4},{6,5},{7,6},{9,8},{10,9},{11,10},{12... | collective-permute-start | bytes 589832 | tf_op jit(solution)/shard_map/ppermute | solution.py:469
  53.8 18.7 %collective-permute-start.9 = (f32[8,4,24,256]{3,2,1,0:T(8,128)S(1)}, f32[8,4,24,256]{3,2,1,0:T(8,128)S(1)}, u32[]{:S(2)}, u32[]{:S(2)}) collective-permute-start(f32[8,4,24,256]{3,2,1,0:T(8,128)S(1)} %get-tuple-element.48.refs_0_.refs_5_), channel_id=1, source_target_pairs={{0,16},{8,24},{16,0},{24,8},{1,17},{9,25},{17,1},{25,9},{2,18},{10... | collective-permute-start | bytes 2359304 | tf_op jit(solution)/shard_map/ppermute | solution.py:445
  54.3 18.7 %collective-permute-start.8 = (f32[8,4,24,256]{3,2,1,0:T(8,128)S(1)}, f32[8,4,24,256]{3,2,1,0:T(8,128)S(1)}, u32[]{:S(2)}, u32[]{:S(2)}) collective-permute-start(f32[8,4,24,256]{3,2,1,0:T(8,128)S(1)} %get-tuple-element.48.refs_0_.refs_5_), channel_id=1, source_target_pairs={{0,8},{8,0},{16,24},{24,16},{1,9},{9,1},{17,25},{25,17},{2,10},{10... | collective-permute-start | bytes 2359304 | tf_op jit(solution)/shard_map/ppermute | solution.py:445
  72.5 2.3 %collective-permute-start.10 = (f32[8,4,24,256]{3,2,1,0:T(8,128)S(1)}, f32[8,4,24,256]{3,2,1,0:T(8,128)S(1)}, u32[]{:S(2)}, u32[]{:S(2)}) collective-permute-start(f32[8,4,24,256]{3,2,1,0:T(8,128)S(1)} %collective-permute-done.9.refs_2_.refs_7_), channel_id=1, source_target_pairs={{0,8},{8,0},{16,24},{24,16},{1,9},{9,1},{17,25},{25,17},{2,10},{10... | collective-permute-start | bytes 2359304 | tf_op jit(solution)/shard_map/ppermute | solution.py:445
  72.5 20.5 %collective-permute-start.14 = (f32[8,4,24,256]{3,2,1,0:T(8,128)S(1)}, f32[8,4,24,256]{3,2,1,0:T(8,128)S(1)}, u32[]{:S(2)}, u32[]{:S(2)}) collective-permute-start(f32[8,4,24,256]{3,2,1,0:T(8,128)S(1)} %get-tuple-element.51.refs_9_), channel_id=1, source_target_pairs={{0,16},{8,24},{16,0},{24,8},{1,17},{9,25},{17,1},{25,9},{2,18},{10... | collective-permute-start | bytes 2359304 | tf_op jit(solution)/shard_map/ppermute | solution.py:445
  78.9 4.4 %collective-permute-start.11 = (f32[96,128]{1,0:T(8,128)S(1)}, f32[96,128]{1,0:T(8,128)S(1)}, u32[]{:S(2)}, u32[]{:S(2)}) collective-permute-start(f32[96,128]{1,0:T(8,128)S(1)} %gram.1), channel_id=1, source_target_pairs={{0,1},{1,0},{2,3},{3,2},{4,5},{5,4},{6,7},{7,6},{8,9},{9,8},{10,11... | collective-permute-start | bytes 147464 | tf_op jit(solution)/shard_map/ppermute | solution.py:445
  83.3 4.2 %collective-permute-start.12 = (f32[96,128]{1,0:T(8,128)S(1)}, f32[96,128]{1,0:T(8,128)S(1)}, u32[]{:S(2)}, u32[]{:S(2)}) collective-permute-start(f32[96,128]{1,0:T(8,128)S(1)} %add.17), channel_id=1, source_target_pairs={{0,2},{1,3},{2,0},{3,1},{4,6},{5,7},{6,4},{7,5},{8,10},{9,11},{10,... | collective-permute-start | bytes 147464 | tf_op jit(solution)/shard_map/ppermute | solution.py:445
  87.5 5.5 %collective-permute-start.13 = (f32[96,128]{1,0:T(8,128)S(1)}, f32[96,128]{1,0:T(8,128)S(1)}, u32[]{:S(2)}, u32[]{:S(2)}) collective-permute-start(f32[96,128]{1,0:T(8,128)S(1)} %add.18), channel_id=1, source_target_pairs={{0,4},{1,5},{2,6},{3,7},{4,0},{5,1},{6,2},{7,3},{8,12},{9,13},{10,... | collective-permute-start | bytes 147464 | tf_op jit(solution)/shard_map/ppermute | solution.py:445
  93.0 26.6 %collective-permute-start.17 = (f32[8,4,24,256]{3,2,1,0:T(8,128)S(1)}, f32[8,4,24,256]{3,2,1,0:T(8,128)S(1)}, u32[]{:S(2)}, u32[]{:S(2)}) collective-permute-start(f32[8,4,24,256]{3,2,1,0:T(8,128)S(1)} %get-tuple-element.53.refs_1_), channel_id=1, source_target_pairs={{0,16},{8,24},{16,0},{24,8},{1,17},{9,25},{17,1},{25,9},{2,18},{10... | collective-permute-start | bytes 2359304 | tf_op jit(solution)/shard_map/ppermute | solution.py:445
  93.6 1.2 collective-permute-start.15
  93.6 26.4 %collective-permute-start.20 = (f32[8,4,24,256]{3,2,1,0:T(8,128)S(1)}, f32[8,4,24,256]{3,2,1,0:T(8,128)S(1)}, u32[]{:S(2)}, u32[]{:S(2)}) collective-permute-start(f32[8,4,24,256]{3,2,1,0:T(8,128)S(1)} %get-tuple-element.51.refs_9_), channel_id=1, source_target_pairs={{0,8},{8,0},{16,24},{24,16},{1,9},{9,1},{17,25},{25,17},{2,10},{10... | collective-permute-start | bytes 2359304 | tf_op jit(solution)/shard_map/ppermute | solution.py:445
  94.1 25.9 %collective-permute-start.19 = (f32[8,4,24,256]{3,2,1,0:T(8,128)S(1)}, f32[8,4,24,256]{3,2,1,0:T(8,128)S(1)}, u32[]{:S(2)}, u32[]{:S(2)}) collective-permute-start(f32[8,4,24,256]{3,2,1,0:T(8,128)S(1)} %collective-permute-done.7.refs_12_.refs_3_), channel_id=1, source_target_pairs={{0,8},{8,0},{16,24},{24,16},{1,9},{9,1},{17,25},{25,17},{2,10},{10... | collective-permute-start | bytes 2359304 | tf_op jit(solution)/shard_map/ppermute | solution.py:445
  94.1 25.9 %collective-permute-start.21 = (f32[8,4,24,256]{3,2,1,0:T(8,128)S(1)}, f32[8,4,24,256]{3,2,1,0:T(8,128)S(1)}, u32[]{:S(2)}, u32[]{:S(2)}) collective-permute-start(f32[8,4,24,256]{3,2,1,0:T(8,128)S(1)} %collective-permute-done.14.refs_11_), channel_id=1, source_target_pairs={{0,8},{8,0},{16,24},{24,16},{1,9},{9,1},{17,25},{25,17},{2,10},{10... | collective-permute-start | bytes 2359304 | tf_op jit(solution)/shard_map/ppermute | solution.py:445
  94.8 29.9 %collective-permute-start.16 = (f32[8,4,24,256]{3,2,1,0:T(8,128)S(1)}, f32[8,4,24,256]{3,2,1,0:T(8,128)S(1)}, u32[]{:S(2)}, u32[]{:S(2)}) collective-permute-start(f32[8,4,24,256]{3,2,1,0:T(8,128)S(1)} %get-tuple-element.53.refs_1_), channel_id=1, source_target_pairs={{0,8},{8,0},{16,24},{24,16},{1,9},{9,1},{17,25},{25,17},{2,10},{10... | collective-permute-start | bytes 2359304 | tf_op jit(solution)/shard_map/ppermute | solution.py:445
  119.6 5.2 %collective-permute-start.18 = (f32[8,4,24,256]{3,2,1,0:T(8,128)S(1)}, f32[8,4,24,256]{3,2,1,0:T(8,128)S(1)}, u32[]{:S(2)}, u32[]{:S(2)}) collective-permute-start(f32[8,4,24,256]{3,2,1,0:T(8,128)S(1)} %collective-permute-done.17.refs_3_), channel_id=1, source_target_pairs={{0,8},{8,0},{16,24},{24,16},{1,9},{9,1},{17,25},{25,17},{2,10},{10... | collective-permute-start | bytes 2359304 | tf_op jit(solution)/shard_map/ppermute | solution.py:445

commit v5 on v4

--- a/solution.py
+++ b/solution.py
@@ -110,73 +110,142 @@
             out[z, 2 * members :, :] = jnp.broadcast_to(spread, (8, spread.shape[1]))
 
 
-def two_substeps_kernel(
-    a, r, c, i, low, high, low_first, high_first, diffusivity, binding, source, *refs, final
+def first_substep(
+    a, r, c, i, low, high, diffusivity, binding, source, out_a, out_r, out_c, out_i
 ):
-    out_a, out_r, out_c, out_i = refs[:4]
-    middle = refs[-1]
-    nx, nz, members, _ = a.shape
-
-    def outside(x, z, later):
-        part = slice(members, 2 * members) if later else slice(0, members)
-        values = []
-        for end, halo, origin in ((0, low, low_first), (nx - 1, high, high_first)):
-            value = halo[z, part, :] if x == end else None
-            if x == end and later:
-                value += origin[z, 2 * members : 2 * members + 1, :] * a[x, z]
-            values.append(value)
-        return values
-
+    nx, nz, _, _ = a.shape
     for x in range(nx):
         for z in range(nz):
             row = pl.ds(z, 1)
             back, out_r[x, z], out_c[x, z], out_i[x, z] = react(
                 a[x, z], r[x, z], c[x, z], i[x, z], binding[x, row, :]
             )
-            around = beside(lambda x, z: a[x, z], x, z, nx, nz, *outside(x, z, False))
-            middle[x, z] = (
+            around = beside(lambda x, z: a[x, z], x, z, nx, nz, low(z), high(z))
+            out_a[x, z] = (
                 spread_free(a[x, z], around, None, diffusivity[x, row, :])
                 + back
                 + source[x, row, :]
             )
+
+
+def two_substeps_kernel(
+    a, r, c, i, low, high, low_first, high_first, diffusivity, binding, source, *refs, lean
+):
+    out_a, out_r, out_c, out_i, first, last, middle = refs
+    nx, nz, members, _ = a.shape
+    first_substep(
+        a,
+        r,
+        c,
+        i,
+        lambda z: low[z, :members, :],
+        lambda z: high[z, :members, :],
+        diffusivity,
+        binding,
+        source,
+        middle,
+        out_r,
+        out_c,
+        out_i,
+    )
+
+    def outside(halo, origin, x, z):
+        later = halo[z, members : 2 * members, :]
+        return later + origin[z, 2 * members : 2 * members + 1, :] * a[x, z]
+
     for x in range(nx):
         for z in range(nz):
             row = pl.ds(z, 1)
-            back, receptor, complexed, internal = react(
+            back, out_r[x, z], out_c[x, z], out_i[x, z] = react(
                 middle[x, z], out_r[x, z], out_c[x, z], out_i[x, z], binding[x, row, :]
             )
-            around = beside(lambda x, z: middle[x, z], x, z, nx, nz, *outside(x, z, True))
+            around = beside(
+                lambda x, z: middle[x, z],
+                x,
+                z,
+                nx,
+                nz,
+                outside(low, low_first, x, z) if x == 0 else None,
+                outside(high, high_first, x, z) if x == nx - 1 else None,
+            )
             out_a[x, z] = (
                 spread_free(middle[x, z], around, None, diffusivity[x, row, :])
                 + back
                 + source[x, row, :]
             )
-            if not final:
-                out_r[x, z] = receptor
-            out_c[x, z] = complexed + internal if final else complexed
-            out_i[x, z] = internal
-    if final:
-        return
-    for x, out in ((0, refs[4]), (nx - 1, refs[5])):
+    for x, out in ((0, first), (nx - 1, last)):
         for z in range(nz):
             row = pl.ds(z, 1)
             free = out_a[x, z]
+            out[z, :members, :] = free
+            if lean:
+                continue
             flux = binding[x, row, :] * free * out_r[x, z]
             rest = unbind_rate * out_c[x, z] - flux + source[x, row, :]
-            out[z, :members, :] = free
             out[z, members:, :] = edge_free(
                 lambda x, z: out_a[x, z], rest, x, nz, nx, z, diffusivity[x, row, :]
             )
 
 
-def forecast_call(kernel, name, inputs, outputs, cells, scratch=(), ready=()):
+def last_but_one_kernel(
+    place, a, r, c, i, low, high, diffusivity, binding, source, *refs, halves
+):
+    *tracers, out_i, out_a, out_add, first, last, mid_r, mid_c, mid_i = refs
+    nx, nz, _, _ = a.shape
+    first_substep(
+        a,
+        r,
+        c,
+        i,
+        lambda z: low[z],
+        lambda z: high[z],
+        diffusivity,
+        binding,
+        source,
+        out_a,
+        mid_r,
+        mid_c,
+        mid_i,
+    )
+    span = nx // halves
+    for part, tracer in enumerate(tracers):
+        begin = jnp.bitwise_xor(part, lax.shift_right_logical(place[2], 1)) * span
+        for j in range(span):
+            x = j if halves == 1 else begin + j
+            for z in range(nz):
+                row = pl.ds(z, 1)
+                back, _, complexed, internal = react(
+                    out_a[x, z], mid_r[x, z], mid_c[x, z], mid_i[x, z], binding[x, row, :]
+                )
+                tracer[j, z] = complexed + internal
+                out_i[x, z] = internal
+                out_add[x, z] = back + source[x, row, :]
+    for x, out in ((0, first), (nx - 1, last)):
+        for z in range(nz):
+            out[z] = out_a[x, z]
+
+
+def last_free_kernel(a, add, low, high, diffusivity, out_a):
+    nx, nz, _, _ = a.shape
+    for x in range(nx):
+        for z in range(nz):
+            around = beside(lambda x, z: a[x, z], x, z, nx, nz, low[z], high[z])
+            out_a[x, z] = (
+                spread_free(a[x, z], around, None, diffusivity[x, pl.ds(z, 1), :]) + add[x, z]
+            )
+
+
+def forecast_call(kernel, name, inputs, outputs, cells, scratch=(), ready=(), scalars=()):
     def body(*refs):
-        kernel(*refs[: len(inputs)], *refs[len(inputs) + len(ready) :])
+        count = len(scalars) + len(inputs)
+        kernel(*refs[:count], *refs[count + len(ready) :])
 
     return pl.pallas_call(
         body,
         out_shape=[jax.ShapeDtypeStruct(shape, f32) for shape in outputs],
-        in_specs=[VMEM] * len(inputs) + [pl.BlockSpec(memory_space=pl.ANY)] * len(ready),
+        in_specs=[SMEM] * len(scalars)
+        + [VMEM] * len(inputs)
+        + [pl.BlockSpec(memory_space=pl.ANY)] * len(ready),
         out_specs=[VMEM] * len(outputs),
         scratch_shapes=[pltpu.VMEM(shape, f32) for shape in scratch],
         compiler_params=pltpu.CompilerParams(vmem_limit_bytes=SCOPED),
@@ -184,7 +253,7 @@
             flops=30 * cells, bytes_accessed=32 * cells, transcendentals=0
         ),
         name=name,
-    )(*inputs, *ready)
+    )(*scalars, *inputs, *ready)
 
 
 def weights_kernel(place, owner, obs_index, observed, obs_var, omega, eta):
@@ -233,11 +302,12 @@
     )(place, owner, obs_index, observed, obs_var)
 
 
-def gram_kernel(place, owner, omega, eta, *refs, offsets):
+def gram_kernel(place, owner, omega, eta, *refs, offsets, halves):
     *sources, packed, out, members_at = refs
     count = out.shape[0]
-    nx, nz, rows, ny = sources[0].shape
+    span, nz, rows, ny = sources[0].shape
     members = members_at.shape[0]
+    begin = 0 if halves == 1 else lax.shift_right_logical(place[2], 1) * (span * nz)
     for k in range(count):
         out[k] = jnp.zeros(out.shape[1:], f32)
 
@@ -251,15 +321,15 @@
                 values = members_at[...]
                 mean = jnp.sum(values, axis=0, keepdims=True) * (1.0 / members)
                 spread = values - mean
-                weight = omega[k, pl.ds(t, 1), :]
-                shift = eta[k, pl.ds(t, 1), :] - weight * mean
+                weight = omega[k, pl.ds(begin + t, 1), :]
+                shift = eta[k, pl.ds(begin + t, 1), :] - weight * mean
                 tail = lax.broadcasted_iota(jnp.int32, (LANES - members, ny), 0)
                 weighted = jnp.concatenate(
                     [spread * weight, jnp.where(tail == 0, shift, 0.0)], axis=0
                 )
                 return total + dot_parts(split(spread), split(weighted), NT)
 
-            out[k] = lax.fori_loop(0, nx * nz, tile, jnp.zeros(out.shape[1:], f32), unroll=4)
+            out[k] = lax.fori_loop(0, span * nz, tile, jnp.zeros(out.shape[1:], f32), unroll=4)
 
     row = lax.broadcasted_iota(jnp.int32, (members, LANES), 0)
     column = lax.broadcasted_iota(jnp.int32, (members, LANES), 1)
@@ -274,19 +344,28 @@
     packed[...] = jnp.where(column == members + 2, pick(column == members, below), both)
 
 
-def gram(place, owner, omega, eta, sources, offsets):
-    nx, nz, rows, ny = sources[0].shape
+def gram(place, owner, omega, eta, sources, offsets, halves, ready):
+    _, _, rows, ny = sources[0].shape
     members = rows * len(sources)
     count = omega.shape[0]
+
+    def body(*refs):
+        inputs = 4 + len(sources)
+        gram_kernel(
+            *refs[:inputs], *refs[inputs + len(ready) :], offsets=offsets, halves=halves
+        )
+
     return pl.pallas_call(
-        functools.partial(gram_kernel, offsets=offsets),
+        body,
         out_shape=jax.ShapeDtypeStruct((members, LANES), f32),
-        in_specs=[SMEM, SMEM, VMEM, VMEM] + [VMEM] * len(sources),
+        in_specs=[SMEM, SMEM, VMEM, VMEM]
+        + [VMEM] * len(sources)
+        + [pl.BlockSpec(memory_space=pl.ANY)] * len(ready),
         out_specs=VMEM,
         scratch_shapes=[pltpu.VMEM((count, members, LANES), f32), pltpu.VMEM((members, ny), f32)],
         compiler_params=pltpu.CompilerParams(vmem_limit_bytes=SCOPED),
         name="gram",
-    )(place, owner, omega, eta, *sources)
+    )(place, owner, omega, eta, *sources, *ready)
 
 
 def turned(x):
@@ -337,8 +416,8 @@
     return wide_dot(wide_left(total), wide_right(mixing))
 
 
-def transform_kernel(place, mine, other, out, ordered, work, *, offsets, blocks, rows):
-    members = mine.shape[0]
+def unpack(place, shares, groups, ordered):
+    members = ordered.shape[1]
     row = lax.broadcasted_iota(jnp.int32, (members, LANES), 0)
     column = lax.broadcasted_iota(jnp.int32, (members, LANES), 1)
     inside = column < members
@@ -346,8 +425,8 @@
     def pick(where, x):
         return jnp.sum(jnp.where(where, x, 0.0), axis=1, keepdims=True)
 
-    for half, shared in ((place[0], mine), (1 - place[0], other)):
-        packed = shared[...]
+    for half, group in zip((place[0], 1 - place[0]), groups(place[2])):
+        packed = sum(shares[k] for k in group)
         above = jnp.where(inside & (column > row), packed, 0.0)
         below = jnp.where(inside & (column < row), packed, 0.0)
         middle = jnp.where(column == row, packed, 0.0)
@@ -356,88 +435,113 @@
         middle = jnp.where(column == row, pick(column == members, packed), 0.0)
         side = jnp.where(column == members, pick(column == members + 2, packed), 0.0)
         ordered[2 * half + 1] = below + turned(below) + (middle + side)
-    total = jnp.where(row == column, 1.0, 0.0)
-    for batch in range(ordered.shape[0]):
-        total = batch_transform(ordered[batch], total, members)
-    total = jnp.concatenate([total, jnp.zeros((LANES - members, LANES), f32)], axis=0)
-    work[...] = total
+
+
+def early_kernel(place, shares, total, last, ordered, *, groups):
+    unpack(place, shares, groups, ordered)
+    batches, members, _ = ordered.shape
+    row = lax.broadcasted_iota(jnp.int32, (members, LANES), 0)
+    column = lax.broadcasted_iota(jnp.int32, (members, LANES), 1)
+    product = jnp.where(row == column, 1.0, 0.0)
+    for batch in range(batches - 1):
+        product = batch_transform(ordered[batch], product, members)
+    total[...] = product
+    last[...] = ordered[batches - 1]
+
+
+def late_kernel(place, total, last, out, work, *, offsets, blocks, rows):
+    members = total.shape[0]
+    product = batch_transform(last[...], total[...], members)
+    rest = jnp.zeros((LANES - members, LANES), f32)
+    work[...] = jnp.concatenate([product, rest], axis=0)
     if blocks == 1:
-        out[...] = total.T
+        out[...] = work[...].T
         return
     parts = [
         work[pl.ds(pl.multiple_of(offsets(place[2], j), 8), rows), :] for j in range(blocks)
     ]
-    parts.append(jnp.zeros((LANES - members, LANES), f32))
-    work[...] = jnp.concatenate(parts, axis=0).T
+    work[...] = jnp.concatenate([*parts, rest], axis=0).T
     out[...] = work[pl.ds(pl.multiple_of(offsets(place[2], 0), 8), rows), :]
 
 
-def transforms(place, mine, other, offsets, blocks, rows):
-    members = mine.shape[0]
-    shape = (LANES, LANES) if blocks == 1 else (rows, LANES)
+def transform_call(kernel, name, out_shape, scratch, inputs):
+    many = isinstance(out_shape, list)
     return pl.pallas_call(
-        functools.partial(transform_kernel, offsets=offsets, blocks=blocks, rows=rows),
-        out_shape=jax.ShapeDtypeStruct(shape, f32),
-        in_specs=[SMEM, VMEM, VMEM],
-        out_specs=VMEM,
-        scratch_shapes=[
-            pltpu.VMEM((4, members, LANES), f32),
-            pltpu.VMEM((LANES, LANES), f32),
-        ],
+        kernel,
+        out_shape=out_shape,
+        in_specs=[SMEM] + [VMEM] * (len(inputs) - 1),
+        out_specs=[VMEM] * len(out_shape) if many else VMEM,
+        scratch_shapes=[pltpu.VMEM(shape, f32) for shape in scratch],
         compiler_params=pltpu.CompilerParams(vmem_limit_bytes=SCOPED),
         cost_estimate=pl.CostEstimate(
             flops=10**8, bytes_accessed=10**6, transcendentals=0
         ),
-        name="transforms",
-    )(place, mine, other)
-
-
-def mix_kernel(weights, *refs, blocks, kinds, begin):
+        name=name,
+    )(*inputs)
+
+
+def mix_kernel(place, weights, *refs, blocks, halves):
     *sources, out = refs
-    rows, _, _, nz, _ = out.shape
-    x = pl.program_id(0)
-    members = blocks * sources[0].shape[2]
+    rows, species, _, nz, _ = out.shape
+    step = pl.program_id(0)
+    span = pl.num_programs(0) // halves
+    free, conserved, internal, *tracers = [
+        sources[k : k + blocks] for k in range(0, len(sources), blocks)
+    ]
+    members = blocks * free[0].shape[2]
     high, low = split(weights[:, :members])
     both = jnp.concatenate([high.astype(f32), low.astype(f32)], axis=0).astype(bf16)
     mul = functools.partial(
         lax.dot_general, dimension_numbers=(NN, ((), ())), preferred_element_type=f32
     )
-    for z in range(nz):
-        mixed = []
-        for kind in range(kinds):
-            parts = [sources[kind * blocks + j][x, z] for j in range(blocks)]
-            values = parts[0] if blocks == 1 else jnp.concatenate(parts, axis=0)
-            value_high, value_low = split(values)
-            upper = mul(both, value_high)
-            mixed.append(upper[:rows] + (upper[rows:] + mul(high, value_low)))
-        for kind in range(kinds - 1):
-            mixed[kind] = mixed[kind] - mixed[kind + 1]
-        for kind in range(kinds):
-            out[:, begin + kind, 0, z, :] = mixed[kind]
-
-
-def mix(weights, sources, blocks, shape, kinds, begin, result=None):
-    rows, _, nx, nz, ny = shape
-    count = len(sources)
-    before = [] if result is None else [result]
-    cells = nx * nz * ny * rows * kinds
-
-    def body(*refs):
-        mix_kernel(*refs[: 1 + count], refs[-1], blocks=blocks, kinds=kinds, begin=begin)
+
+    def mixed(held, x, z):
+        parts = [array[x, z] for array in held]
+        values = parts[0] if blocks == 1 else jnp.concatenate(parts, axis=0)
+        value_high, value_low = split(values)
+        upper = mul(both, value_high)
+        return upper[:rows] + (upper[rows:] + mul(high, value_low))
+
+    for part in range(halves):
+
+        @pl.when(step // span == part)
+        def _(part=part):
+            at = step % span
+            x = at if halves == 1 else half_begin(place, part, span) + at
+            for z in range(nz):
+                tracer = mixed(tracers[part], at, z)
+                inside = mixed(internal, x, z)
+                out[:, 0, 0, z, :] = mixed(free, x, z)
+                out[:, 1, 0, z, :] = mixed(conserved, x, z) - tracer
+                out[:, 2, 0, z, :] = tracer - inside
+                out[:, 3, 0, z, :] = inside
+
+
+def half_begin(place, part, span):
+    return jnp.bitwise_xor(part, lax.shift_right_logical(place[2], 1)) * span
+
+
+def mix(place, weights, sources, blocks, halves, shape):
+    rows, species, nx, nz, ny = shape
+    span = nx // halves
+
+    def at(step, place):
+        if halves == 1:
+            return (0, 0, step, 0, 0)
+        return (0, 0, half_begin(place, step // span, span) + step % span, 0, 0)
 
     return pl.pallas_call(
-        body,
-        grid=(nx,),
+        functools.partial(mix_kernel, blocks=blocks, halves=halves),
+        grid_spec=pltpu.PrefetchScalarGridSpec(
+            num_scalar_prefetch=1,
+            grid=(nx,),
+            in_specs=[VMEM] * (1 + len(sources)),
+            out_specs=pl.BlockSpec((rows, species, 1, nz, ny), at),
+        ),
         out_shape=jax.ShapeDtypeStruct(shape, f32),
-        in_specs=[VMEM] * (1 + count) + [pl.BlockSpec(memory_space=pl.ANY)] * len(before),
-        out_specs=pl.BlockSpec((rows, begin + kinds, 1, nz, ny), lambda x: (0, 0, x, 0, 0)),
-        input_output_aliases={} if result is None else {1 + count: 0},
         compiler_params=pltpu.CompilerParams(vmem_limit_bytes=SCOPED),
-        cost_estimate=pl.CostEstimate(
-            flops=1000 * cells, bytes_accessed=4 * cells, transcendentals=0
-        ),
         name="mix",
-    )(weights, *sources, *before)
+    )(place, weights, *sources)
 
 
 def swap(x, axis, bit):
@@ -468,23 +572,30 @@
     def halos(first, last):
         return lax.ppermute(last, "space", forward), lax.ppermute(first, "space", backward)
 
-    if devices == 4 and rows % 8 == 0:
-        blocks = devices
+    if devices == 4 and rows % 8 == 0 and nx % 2 == 0:
+        blocks, halves = devices, 2
 
         def offsets(position, j):
             return jnp.bitwise_xor(position, j) * rows
 
-        def collect(x):
-            return [x, swap(x, "member", 1), swap(x, "member", 2)]
+        def groups(position):
+            flip = functools.partial(jnp.bitwise_xor, position)
+            return (position, flip(2)), (flip(1), flip(3))
+
+        def collect(x, sent=None):
+            return [x, swap(x, "member", 1), swap(x if sent is None else sent, "member", 2)]
 
         def complete(held, *after):
             return [*held, swap(lax.optimization_barrier((held[2], *after))[0], "member", 1)]
     else:
-        blocks = 1
+        blocks, halves = 1, 1
 
         def offsets(position, j):
             return 0
 
+        def groups(position):
+            return (0,), (1,)
+
         def collect(x):
             return [lax.all_gather(x, "member", axis=2, tiled=True)]
 
@@ -494,7 +605,10 @@
     def across(held):
         return held[min(2, blocks - 1)]
 
-    whole = (nx, nz, rows, ny)
+    def tie(x, *after):
+        return lax.optimization_barrier((x, *after))[0]
+
+    whole, plane = (nx, nz, rows, ny), (nz, rows, ny)
     coefficients = (diffusivity, binding, source)
     cells = nx * nz * rows * ny
     ends = [
@@ -514,44 +628,79 @@
         place, owner, obs_index, observed, obs_var, batches // 2, nx * nz, ny
     )
     around = origin = halos(*edges)
-    steps = SUBSTEPS // 2
+    steps = SUBSTEPS // 2 - 1
     for step in range(steps):
-        final = step == steps - 1
-        ready = ()
-        if step == 0:
-            ready = (omega, eta)
-        elif step == 1:
-            conserved = collect(lax.optimization_barrier((conserved, fields[0]))[0])
-        elif step == 2:
-            ready = conserved[1:]
-        *fields, = forecast_call(
-            functools.partial(two_substeps_kernel, final=final),
+        lean = step == steps - 1
+        *fields, first, last = forecast_call(
+            functools.partial(two_substeps_kernel, lean=lean),
             "two_substeps",
             [*fields, *around, *origin, *coefficients],
-            [whole] * 4 + ([] if final else [(nz, 2 * rows, ny)] * 2),
+            [whole] * 4 + [plane if lean else (nz, 2 * rows, ny)] * 2,
             2 * cells,
             scratch=[whole],
-            ready=ready,
+            ready=(omega, eta) if step == 0 else (),
         )
-        if not final:
-            around = halos(*fields[4:])
-            fields = fields[:4]
-    free, _, tracer, internal = fields
-
-    tracer = complete(collect(tracer))
-    conserved = complete(conserved, across(tracer))
-    internal = collect(lax.optimization_barrier((internal, across(tracer)))[0])
-    half = total_over(gram(place, owner, omega, eta, tracer, offsets), "space")
-    half, free, _ = lax.optimization_barrier((half, free, across(internal)))
-    free = collect(free)
+        around = halos(first, last)
+        if step == 0:
+            conserved = collect(tie(conserved, fields[0]))
+    *tracers, internal, free, add, first, last = forecast_call(
+        functools.partial(last_but_one_kernel, halves=halves),
+        "last_but_one",
+        [*fields, *around, *coefficients],
+        [(nx // halves, nz, rows, ny)] * halves + [whole] * 3 + [plane] * 2,
+        2 * cells,
+        scratch=[whole] * 3,
+        ready=conserved[1:],
+        scalars=[place],
+    )
+    if halves == 2:
+        near, far = tracers
+        near = complete(collect(near, far))
+    else:
+        near = collect(tracers[0])
+    (free,) = forecast_call(
+        last_free_kernel,
+        "last_free",
+        [free, add, *halos(first, last), diffusivity],
+        [whole],
+        cells,
+    )
+    conserved = complete(conserved, across(near), free)
+    internal = collect(tie(internal, across(near), free))
+    half = total_over(gram(place, owner, omega, eta, near, offsets, halves, [free]), "space")
+    if halves == 2:
+        half = tie(half, across(internal))
+        shares = lax.all_to_all(
+            jnp.broadcast_to(half, (devices, *half.shape)), "member", 0, 0
+        )
+        far = collect(tie(far, shares), tie(tracers[0], shares))
+        free = collect(tie(free, shares))
+    else:
+        free = collect(free)
+        shares = jnp.stack([half, swap(half, "member", 1)])
     internal = complete(internal, half)
-    weights = transforms(place, half, swap(half, "member", 1), offsets, blocks, rows)
-    free = complete(free, weights)
+    square = jax.ShapeDtypeStruct((members, LANES), f32)
+    total, extended = transform_call(
+        functools.partial(early_kernel, groups=groups),
+        "transforms_early",
+        [square, square],
+        [(batches, members, LANES)],
+        [place, shares],
+    )
+    if halves == 2:
+        far = complete(far, total)
+    free = complete(free, total)
+    weights = transform_call(
+        functools.partial(late_kernel, offsets=offsets, blocks=blocks, rows=rows),
+        "transforms_late",
+        jax.ShapeDtypeStruct((LANES, LANES) if blocks == 1 else (rows, LANES), f32),
+        [(LANES, LANES)],
+        [place, total, extended],
+    )
     if blocks == 1:
         weights = lax.dynamic_slice(weights, (member * rows, 0), (rows, LANES))
-    bound = conserved + tracer + internal
-    result = mix(weights, bound, blocks, ensemble.shape, species - 1, 1)
-    return mix(weights, free, blocks, ensemble.shape, 1, 0, result)
+    sources = free + conserved + internal + near + (far if halves == 2 else [])
+    return mix(place, weights, sources, blocks, halves, ensemble.shape)
 
 
 def solution(mesh):

time: 130 us -> 132 us (1.015); the launches traced: 128 us -> 132 us
  starting transfers between devices: 26.2 us -> 38.8 us
  waiting for transfers between devices: 47 us -> 35.2 us
  blocking collectives: 0 us -> 7.7 us
  Pallas kernels: 43.9 us -> 38.9 us
    ppermute x16 -> x18, waiting for transfers between devices: 30.7 us -> 15.7 us  [swap(): return lax.ppermute(x, axis, [(k, k ^ bit) for k in range(count)])]
    all_to_all x0 -> x1, blocking collectives: none -> 7.7 us  [local(): lax.all_to_all(jnp.broadcast_to(half, (devices, *half.shape)), 'member',...]
    ppermute x16 -> x18, starting transfers between devices: 8.36 us -> 15 us  [swap(): return lax.ppermute(x, axis, [(k, k ^ bit) for k in range(count)])]
    pallas_call x4, Pallas kernels: 37 us -> 31.8 us  [the longest x2 25.1 us: transform_call(): pl.pallas_call(kernel, out_shape=out_shape, in_specs=[SMEM] + [VMEM] * (l...]
    ppermute x3 -> x4, starting transfers between devices: 14 us -> 18.6 us  [halos(): lax.ppermute(last, 'space', forward)]
    ppermute x3 -> x4, waiting for transfers between devices: 10.4 us -> 14.2 us  [halos(): lax.ppermute(first, 'space', backward)]
    ppermute x3 -> x4, starting transfers between devices: 3.88 us -> 5.17 us  [halos(): lax.ppermute(first, 'space', backward)]
    ppermute x3 -> x4, waiting for transfers between devices: 5.91 us -> 5.29 us  [halos(): lax.ppermute(last, 'space', forward)]
  transfers between devices with their start and end apart: 22 -> 26, of which waited for: 10 -> 12; matrix products, arithmetic and copies ran while one was open for 7% -> 7% of each run, Pallas kernels for 28% -> 22%
where the time goes in v5:
time: 132 us
  Pallas kernels  38.9 us (29%)
  starting transfers between devices  38.8 us (29%)
  waiting for transfers between devices  35.2 us (27%)
  local copies, waits for them, and re-layouts  8.44 us (6%)
  blocking collectives  7.7 us (6%)
  other arithmetic  2.5 us (2%)
    pallas_call x2, Pallas kernels, transform_call(): pl.pallas_call(kernel, out_shape=out_shape, in_specs=[SMEM] + [VMEM] * (l...  25.1 us
    ppermute x4, starting transfers between devices, halos(): lax.ppermute(last, 'space', forward)  18.6 us
    ppermute x18, waiting for transfers between devices, swap(): return lax.ppermute(x, axis, [(k, k ^ bit) for k in range(count)])  15.7 us
    ppermute x18, starting transfers between devices, swap(): return lax.ppermute(x, axis, [(k, k ^ bit) for k in range(count)])  15 us
    ppermute x4, waiting for transfers between devices, halos(): lax.ppermute(first, 'space', backward)  14.2 us
    all_to_all x1, blocking collectives, local(): lax.all_to_all(jnp.broadcast_to(half, (devices, *half.shape)), 'member',...  7.7 us
    pallas_call x1, Pallas kernels, mix(): pl.pallas_call(functools.partial(mix_kernel, blocks=blocks, halves=halves...  5.87 us
    pallas_call x5, Pallas kernels, forecast_call(): pl.pallas_call(body, out_shape=[jax.ShapeDtypeStruct(shape, f32) for shap...  5.69 us
  transfers between devices with their start and end apart: 26, of which 12 were waited for; matrix products, arithmetic and copies ran while one was open for 7% of the time, Pallas kernels for 22%

profile of v5, /device:TPU:0, one launch (start us, length us, event | category | flops | bytes accessed | tf_op | source)
XLA Modules:
  0.0 131.9 jit_solution(1400023535350296913)
XLA Ops:
  0.0 1.6 %fusion = (f32[24,3,2,4,256]{4,3,2,1,0:T(4,128)S(1)}, f32[24,3,2,4,256]{4,3,2,1,0:T(4,128)S(1)}) fusion(f32[24,4,8,4,256]{4,3,2,1,0:T(4,128)} %param.8), kind=kLoop, calls=%fused_computation.8 | loop fusion | bytes 2359296 | tf_op jit(solution)/shard_map/slice | solution.py:615
  1.6 0.4 copy_bitcast_fusion.4
  2.0 0.2 first_edges.1
  2.2 4.9 %collective-permute-start = (f32[4,56,256]{2,1,0:T(8,128)S(1)}, f32[4,56,256]{2,1,0:T(8,128)S(1)}, u32[]{:S(2)}, u32[]{:S(2)}) collective-permute-start(f32[4,56,256]{2,1,0:T(8,128)S(1)} %get-tuple-element.42), channel_id=1, source_target_pairs={{0,1},{1,2},{2,3},{3,4},{4,5},{5,6},{6,7},{8,9},{9,10},{10,11},{11... | collective-permute-start | bytes 688136 | tf_op jit(solution)/shard_map/ppermute | solution.py:573
  7.1 1.3 collective-permute-start.1
  8.4 1.8 %fusion.1 = (f32[24,1,8,4,256]{4,3,2,1,0:T(4,128)S(1)}, f32[24,1,8,4,256]{4,3,2,1,0:T(4,128)}, f32[24,1,8,4,256]{4,3,2,1,0:T(4,128)}, f32[24,1,8,4,256]{4,3,2,1,0:T(4,128)}) fusion(f32[24,4,8,4,256]{4,3,2,1,0:T(4,128)S(1)} %copy-done.10), kind=kLoop, calls=%fused_computation.9 | loop fusion | bytes 6291456 | tf_op jit(solution)/shard_map/slice | solution.py:625
  10.2 0.0 copy-start.4
  10.2 0.0 copy-start.5
  10.2 0.0 copy-start.6
  10.2 2.4 %copy_bitcast_fusion = (f32[8,4,24,256]{3,2,1,0:T(8,128)S(1)}, f32[8,4,24,256]{3,2,1,0:T(8,128)S(1)}) fusion(f32[24,1,8,4,256]{4,3,2,1,0:T(4,128)S(1)} %get-tuple-element.77, f32[24,1,8,4,256]{4,3,2,1,0:T(4,128)} %get-tuple-element.78), kind=kLoop, calls=%fused_computation | loop fusion | bytes 3145728 | tf_op jit(solution)/shard_map/transpose | solution.py:625
  12.6 2.4 %add_add_fusion.refs_4_ = f32[8,4,24,256]{3,2,1,0:T(8,128)S(1)} fusion(f32[24,1,8,4,256]{4,3,2,1,0:T(4,128)S(1)} %copy-done.7, f32[24,1,8,4,256]{4,3,2,1,0:T(4,128)S(1)} %copy-done.9, f32[24,1,8,4,256]{4,3,2,1,0:T(4,128)} %copy-done.8), kind=kLoop, calls=%fused_computation.4 | loop fusion | flops 393216 | bytes 3145728 | tf_op jit(solution)/shard_map/add | solution.py:626
  15.0 0.1 pad_add_fusion.place.refs_0_
  15.1 1.4 %voxel_weights.1 = (f32[2,32,256]{2,1,0:T(8,128)S(1)}, f32[2,32,256]{2,1,0:T(8,128)S(1)}) custom-call(s32[3]{0:T(128)S(1)} %pad_add_fusion.place.refs_0_, s32[4]{0:T(128)S(1)} %copy-done.6, s32[4,2048]{1,0:T(4,128)S(1)} %copy-done.3, f32[4,2048]{1,0:T(4,128)S(1)} %copy-done.4, f32[4,2048]{1,0:T(4,128)S(1)} %copy-done.5), custom_call_target="tpu_custom_call" | custom-call | tf_op jit(solution)/shard_map/voxel_weights/pallas_call | solution.py:295
  16.5 2.3 %copy_bitcast_fusion.2 = (f32[8,4,24,256]{3,2,1,0:T(8,128)S(1)}, f32[8,4,24,256]{3,2,1,0:T(8,128)S(1)}) fusion(f32[24,1,8,4,256]{4,3,2,1,0:T(4,128)} %get-tuple-element.79, f32[24,1,8,4,256]{4,3,2,1,0:T(4,128)} %get-tuple-element.80), kind=kLoop, calls=%fused_computation.2 | loop fusion | bytes 3145728 | tf_op jit(solution)/shard_map/transpose | solution.py:625
  18.8 0.0 collective-permute-done.1.refs_5_.refs_7_
  18.9 1.7 %two_substeps.2 = (f32[8,4,24,256]{3,2,1,0:T(8,128)S(1)}, f32[8,4,24,256]{3,2,1,0:T(8,128)S(1)}, f32[8,4,24,256]{3,2,1,0:T(8,128)S(1)}, f32[8,4,24,256]{3,2,1,0:...) custom-call(f32[8,4,24,256]{3,2,1,0:T(8,128)S(1)} %get-tuple-element.84.refs_0_, ...), custom_call_target="tpu_custom_call" | custom-call | flops 11796480 | bytes 12582912 | tf_op jit(solution)/shard_map/two_substeps/pallas_call | solution.py:243
  20.6 1.6 %collective-permute-start.7 = (f32[8,4,24,256]{3,2,1,0:T(8,128)S(1)}, f32[8,4,24,256]{3,2,1,0:T(8,128)S(1)}, u32[]{:S(2)}, u32[]{:S(2)}) collective-permute-start(f32[8,4,24,256]{3,2,1,0:T(8,128)S(1)} %add_add_fusion.refs_4_), channel_id=1, source_target_pairs={{0,16},{8,24},{16,0},{24,8},{1,17},{9,25},{17,1},{25,9},{2,18},{10... | collective-permute-start | bytes 2359304 | tf_op jit(solution)/shard_map/ppermute | solution.py:549
  22.2 0.0 collective-permute-start.6
  22.2 4.5 %collective-permute-start.2 = (f32[4,48,256]{2,1,0:T(8,128)S(1)}, f32[4,48,256]{2,1,0:T(8,128)S(1)}, u32[]{:S(2)}, u32[]{:S(2)}) collective-permute-start(f32[4,48,256]{2,1,0:T(8,128)S(1)} %get-tuple-element.48), channel_id=1, source_target_pairs={{0,1},{1,2},{2,3},{3,4},{4,5},{5,6},{6,7},{8,9},{9,10},{10,11},{11... | collective-permute-start | bytes 589832 | tf_op jit(solution)/shard_map/ppermute | solution.py:573
  26.7 1.3 collective-permute-start.3
  28.0 3.5 %collective-permute-done.2.refs_4_ = f32[4,48,256]{2,1,0:T(8,128)S(1)} collective-permute-done((f32[4,48,256]{2,1,0:T(8,128)S(1)}, f32[4,48,256]{2,1,0:T(8,128)S(1)}, u32[]{:S(2)}, u32[]{:S(2)}) %collective-permute-start.2) | collective-permute-done | bytes 196640 | tf_op jit(solution)/shard_map/ppermute | solution.py:573
  31.5 4.8 %collective-permute-done.3.refs_5_ = f32[4,48,256]{2,1,0:T(8,128)S(1)} collective-permute-done((f32[4,48,256]{2,1,0:T(8,128)S(1)}, f32[4,48,256]{2,1,0:T(8,128)S(1)}, u32[]{:S(2)}, u32[]{:S(2)}) %collective-permute-start.3) | collective-permute-done | bytes 196640 | tf_op jit(solution)/shard_map/ppermute | solution.py:573
  36.4 1.6 %two_substeps.3 = (f32[8,4,24,256]{3,2,1,0:T(8,128)S(1)}, f32[8,4,24,256]{3,2,1,0:T(8,128)S(1)}, f32[8,4,24,256]{3,2,1,0:T(8,128)S(1)}, f32[8,4,24,256]{3,2,1,0:...) custom-call(f32[8,4,24,256]{3,2,1,0:T(8,128)S(1)} %get-tuple-element.44.refs_0_, ...), custom_call_target="tpu_custom_call" | custom-call | flops 11796480 | bytes 12582912 | tf_op jit(solution)/shard_map/two_substeps/pallas_call | solution.py:243
  38.0 4.5 %collective-permute-start.4 = (f32[4,24,256]{2,1,0:T(8,128)S(1)}, f32[4,24,256]{2,1,0:T(8,128)S(1)}, u32[]{:S(2)}, u32[]{:S(2)}) collective-permute-start(f32[4,24,256]{2,1,0:T(8,128)S(1)} %get-tuple-element.54), channel_id=1, source_target_pairs={{0,1},{1,2},{2,3},{3,4},{4,5},{5,6},{6,7},{8,9},{9,10},{10,11},{11... | collective-permute-start | bytes 294920 | tf_op jit(solution)/shard_map/ppermute | solution.py:573
  42.5 1.3 collective-permute-start.5
  43.8 0.9 collective-permute-done.4.refs_5_
  44.7 5.0 %collective-permute-done.5.refs_6_ = f32[4,24,256]{2,1,0:T(8,128)S(1)} collective-permute-done((f32[4,24,256]{2,1,0:T(8,128)S(1)}, f32[4,24,256]{2,1,0:T(8,128)S(1)}, u32[]{:S(2)}, u32[]{:S(2)}) %collective-permute-start.5) | collective-permute-done | bytes 98336 | tf_op jit(solution)/shard_map/ppermute | solution.py:573
  49.8 0.0 collective-permute-done.7.refs_11_.refs_6_
  49.8 0.0 collective-permute-done.6.refs_10_.refs_5_
  49.8 1.7 %last_but_one.1 = (f32[4,4,24,256]{3,2,1,0:T(8,128)S(1)}, f32[4,4,24,256]{3,2,1,0:T(8,128)S(1)}, f32[8,4,24,256]{3,2,1,0:T(8,128)S(1)}, f32[8,4,24,256]{3,2,1,0:...) custom-call(s32[3]{0:T(128)S(1)} %pad_add_fusion.place.refs_0_, ...), custom_call_target="tpu_custom_call" | custom-call | flops 11796480 | bytes 12582912 | tf_op jit(solution)/shard_map/last_but_one/pallas_call | solution.py:243
  51.4 0.6 collective-permute-start.9
  52.0 4.7 %collective-permute-start.11 = (f32[4,24,256]{2,1,0:T(8,128)S(1)}, f32[4,24,256]{2,1,0:T(8,128)S(1)}, u32[]{:S(2)}, u32[]{:S(2)}) collective-permute-start(f32[4,24,256]{2,1,0:T(8,128)S(1)} %get-tuple-element.61), channel_id=1, source_target_pairs={{0,1},{1,2},{2,3},{3,4},{4,5},{5,6},{6,7},{8,9},{9,10},{10,11},{11... | collective-permute-start | bytes 294920 | tf_op jit(solution)/shard_map/ppermute | solution.py:573
  56.7 1.3 collective-permute-start.12
  58.0 0.9 collective-permute-done.11.refs_2_
  58.9 4.3 %collective-permute-done.12.refs_3_ = f32[4,24,256]{2,1,0:T(8,128)S(1)} collective-permute-done((f32[4,24,256]{2,1,0:T(8,128)S(1)}, f32[4,24,256]{2,1,0:T(8,128)S(1)}, u32[]{:S(2)}, u32[]{:S(2)}) %collective-permute-start.12) | collective-permute-done | bytes 98336 | tf_op jit(solution)/shard_map/ppermute | solution.py:573
  63.2 0.5 last_free.1.refs_8_.refs_0_
  63.7 0.0 collective-permute-done.9.refs_6_.refs_14_
  63.7 1.6 %collective-permute-start.16 = (f32[8,4,24,256]{3,2,1,0:T(8,128)S(1)}, f32[8,4,24,256]{3,2,1,0:T(8,128)S(1)}, u32[]{:S(2)}, u32[]{:S(2)}) collective-permute-start(f32[8,4,24,256]{3,2,1,0:T(8,128)S(1)} %get-tuple-element.64.refs_8_), channel_id=1, source_target_pairs={{0,16},{8,24},{16,0},{24,8},{1,17},{9,25},{17,1},{25,9},{2,18},{10... | collective-permute-start | bytes 2359304 | tf_op jit(solution)/shard_map/ppermute | solution.py:549
  65.3 0.0 collective-permute-start.8
  65.3 0.5 collective-permute-start.10
  65.8 1.2 collective-permute-done.8.refs_5_.refs_13_
  67.0 0.6 collective-permute-done.10.refs_7_.refs_15_
  67.6 0.9 gram.1
  68.4 1.3 collective-permute-start.13
  69.7 2.8 %collective-permute-done.13 = f32[96,128]{1,0:T(8,128)S(1)} collective-permute-done((f32[96,128]{1,0:T(8,128)S(1)}, f32[96,128]{1,0:T(8,128)S(1)}, u32[]{:S(2)}, u32[]{:S(2)}) %collective-permute-start.13) | collective-permute-done | bytes 49184 | tf_op jit(solution)/shard_map/ppermute | solution.py:549
  72.6 1.6 %collective-permute-start.14 = (f32[96,128]{1,0:T(8,128)S(1)}, f32[96,128]{1,0:T(8,128)S(1)}, u32[]{:S(2)}, u32[]{:S(2)}) collective-permute-start(f32[96,128]{1,0:T(8,128)S(1)} %add.17), channel_id=1, source_target_pairs={{0,2},{1,3},{2,0},{3,1},{4,6},{5,7},{6,4},{7,5},{8,10},{9,11},{10,... | collective-permute-start | bytes 147464 | tf_op jit(solution)/shard_map/ppermute | solution.py:549
  74.2 3.0 %collective-permute-done.14 = f32[96,128]{1,0:T(8,128)S(1)} collective-permute-done((f32[96,128]{1,0:T(8,128)S(1)}, f32[96,128]{1,0:T(8,128)S(1)}, u32[]{:S(2)}, u32[]{:S(2)}) %collective-permute-start.14) | collective-permute-done | bytes 49184 | tf_op jit(solution)/shard_map/ppermute | solution.py:549
  77.2 4.1 %collective-permute-start.15 = (f32[96,128]{1,0:T(8,128)S(1)}, f32[96,128]{1,0:T(8,128)S(1)}, u32[]{:S(2)}, u32[]{:S(2)}) collective-permute-start(f32[96,128]{1,0:T(8,128)S(1)} %add.18), channel_id=1, source_target_pairs={{0,4},{1,5},{2,6},{3,7},{4,0},{5,1},{6,2},{7,3},{8,12},{9,13},{10,... | collective-permute-start | bytes 147464 | tf_op jit(solution)/shard_map/ppermute | solution.py:549
  81.3 2.1 %collective-permute-done.15 = f32[96,128]{1,0:T(8,128)S(1)} collective-permute-done((f32[96,128]{1,0:T(8,128)S(1)}, f32[96,128]{1,0:T(8,128)S(1)}, u32[]{:S(2)}, u32[]{:S(2)}) %collective-permute-start.15) | collective-permute-done | bytes 49184 | tf_op jit(solution)/shard_map/ppermute | solution.py:549
  83.4 0.0 collective-permute-done.16.refs_10_
  83.4 7.7 %all_to_all.5.shares = f32[4,96,128]{2,1,0:T(8,128)S(1)} all-to-all(f32[4,96,128]{2,1,0:T(8,128)S(1)} %broadcast_in_dim.3), channel_id=1, replica_groups=mesh['member'=4,'space'=8] {'member'}, dimensions={0} | all-to-all | bytes 393216 | tf_op jit(solution)/shard_map/all_to_all | solution.py:673
  91.1 0.4 collective-permute-start.18
  91.5 0.0 collective-permute-start.21
  91.5 0.5 collective-permute-start.20
  92.0 1.7 %collective-permute-start.24 = (f32[4,4,24,256]{3,2,1,0:T(8,128)S(1)}, f32[4,4,24,256]{3,2,1,0:T(8,128)S(1)}, u32[]{:S(2)}, u32[]{:S(2)}) collective-permute-start(f32[4,4,24,256]{3,2,1,0:T(8,128)S(1)} %get-tuple-element.73.refs_4_.refs_12_), channel_id=1, source_target_pairs={{0,16},{8,24},{16,0},{24,8},{1,17},{9,25},{17,1},{25,9},{2,18},{10... | collective-permute-start | bytes 1179656 | tf_op jit(solution)/shard_map/ppermute | solution.py:549
  93.7 18.5 %transforms_early.1 = (f32[96,128]{1,0:T(8,128)S(1)}, f32[96,128]{1,0:T(8,128)S(1)}) custom-call(s32[3]{0:T(128)S(1)} %pad_add_fusion.place.refs_0_, f32[4,96,128]{2,1,0:T(8,128)S(1)} %all_to_all.5.shares), custom_call_target="tpu_custom_call" | custom-call | flops 100000000 | bytes 1000000 | tf_op jit(solution)/shard_map/transforms_early/pallas_call | solution.py:469
  112.2 0.6 collective-permute-start.17
  112.8 6.0 %collective-permute-done.24.refs_18_ = f32[4,4,24,256]{3,2,1,0:T(8,128)S(1)} collective-permute-done((f32[4,4,24,256]{3,2,1,0:T(8,128)S(1)}, f32[4,4,24,256]{3,2,1,0:T(8,128)S(1)}, u32[]{:S(2)}, u32[]{:S(2)}) %collective-permute-start.24) | collective-permute-done | bytes 393248 | tf_op jit(solution)/shard_map/ppermute | solution.py:549
  118.8 0.5 collective-permute-start.23
  119.3 0.1 collective-permute-start.25
  119.3 6.6 %transforms_late.1.weights = f32[24,128]{1,0:T(8,128)S(1)} custom-call(s32[3]{0:T(128)S(1)} %pad_add_fusion.place.refs_0_, f32[96,128]{1,0:T(8,128)S(1)} %get-tuple-element.66.total, f32[96,128]{1,0:T(8,128)S(1)} %get-tuple-element.67.last), custom_call_target="tpu_custom_call" | custom-call | flops 100000000 | bytes 1000000 | tf_op jit(solution)/shard_map/transforms_late/pallas_call | solution.py:469
  125.9 0.0 collective-permute-done.23.refs_17_
  125.9 0.0 collective-permute-done.25.refs_19_
  126.0 5.9 %mix.1 = f32[24,4,8,4,256]{4,3,2,1,0:T(4,128)} custom-call(s32[3]{0:T(128)S(1)} %pad_add_fusion.place.refs_0_, f32[24,128]{1,0:T(8,128)S(1)} %transforms_late.1.weights, f32[8,4,24,256]{3,2,1,0:T(8,128)S(1)} %last_free.1.refs_8_.refs_0_, f32[8,4,24,256]{3,2,1,0:T(8,128)S(1)} %collective-permute-done.17.refs_1_, ...), custom_call_target="tpu_custom_call" | custom-call | tf_op jit(solution)/shard_map/mix/pallas_call | solution.py:533
  (32 shorter events, 0.1 us)
Async XLA Ops:
  0.0 8.4 %copy-start.10 = (f32[24,4,8,4,256]{4,3,2,1,0:T(4,128)S(1)}, f32[24,4,8,4,256]{4,3,2,1,0:T(4,128)}, u32[]{:S(2)}) copy-start(f32[24,4,8,4,256]{4,3,2,1,0:T(4,128)} %param.8) | copy-start | bytes 9437188
  0.0 2.0 %copy-start = (f32[8,4,256]{2,1,0:T(4,128)S(1)}, f32[8,4,256]{2,1,0:T(4,128)}, u32[]{:S(2)}) copy-start(f32[8,4,256]{2,1,0:T(4,128)} %refs_4_.3) | copy-start | bytes 98308
  0.0 2.0 %copy-start.2 = (f32[8,4,256]{2,1,0:T(4,128)S(1)}, f32[8,4,256]{2,1,0:T(4,128)}, u32[]{:S(2)}) copy-start(f32[8,4,256]{2,1,0:T(4,128)} %refs_9_.5) | copy-start | bytes 98308
  0.0 2.0 %copy-start.1 = (f32[8,4,256]{2,1,0:T(4,128)S(1)}, f32[8,4,256]{2,1,0:T(4,128)}, u32[]{:S(2)}) copy-start(f32[8,4,256]{2,1,0:T(4,128)} %refs_8_.5) | copy-start | bytes 98308
  2.2 16.6 %collective-permute-start = (f32[4,56,256]{2,1,0:T(8,128)S(1)}, f32[4,56,256]{2,1,0:T(8,128)S(1)}, u32[]{:S(2)}, u32[]{:S(2)}) collective-permute-start(f32[4,56,256]{2,1,0:T(8,128)S(1)} %get-tuple-element.42), channel_id=1, source_target_pairs={{0,1},{1,2},{2,3},{3,4},{4,5},{5,6},{6,7},{8,9},{9,10},{10,11},{11... | collective-permute-start | bytes 688136 | tf_op jit(solution)/shard_map/ppermute | solution.py:573
  7.1 11.7 %collective-permute-start.1 = (f32[4,56,256]{2,1,0:T(8,128)S(1)}, f32[4,56,256]{2,1,0:T(8,128)S(1)}, u32[]{:S(2)}, u32[]{:S(2)}) collective-permute-start(f32[4,56,256]{2,1,0:T(8,128)S(1)} %get-tuple-element.43), channel_id=1, source_target_pairs={{1,0},{2,1},{3,2},{4,3},{5,4},{6,5},{7,6},{9,8},{10,9},{11,10},{12... | collective-permute-start | bytes 688136 | tf_op jit(solution)/shard_map/ppermute | solution.py:573
  10.2 2.4 %copy-start.8 = (f32[24,1,8,4,256]{4,3,2,1,0:T(4,128)}, f32[24,1,8,4,256]{4,3,2,1,0:T(4,128)S(1)}, u32[]{:S(2)}) copy-start(f32[24,1,8,4,256]{4,3,2,1,0:T(4,128)S(1)} %get-tuple-element.77) | copy-start | bytes 2359300
  10.2 2.4 %copy-start.7 = (f32[24,1,8,4,256]{4,3,2,1,0:T(4,128)S(1)}, f32[24,1,8,4,256]{4,3,2,1,0:T(4,128)}, u32[]{:S(2)}) copy-start(f32[24,1,8,4,256]{4,3,2,1,0:T(4,128)} %get-tuple-element.79) | copy-start | bytes 2359300
  10.2 2.4 %copy-start.9 = (f32[24,1,8,4,256]{4,3,2,1,0:T(4,128)S(1)}, f32[24,1,8,4,256]{4,3,2,1,0:T(4,128)}, u32[]{:S(2)}) copy-start(f32[24,1,8,4,256]{4,3,2,1,0:T(4,128)} %get-tuple-element.78) | copy-start | bytes 2359300
  10.2 4.9 %copy-start.3 = (s32[4,2048]{1,0:T(4,128)S(1)}, s32[4,2048]{1,0:T(4,128)}, u32[]{:S(2)}) copy-start(s32[4,2048]{1,0:T(4,128)} %obs_index.1) | copy-start | bytes 98308
  10.2 4.9 %copy-start.4 = (f32[4,2048]{1,0:T(4,128)S(1)}, f32[4,2048]{1,0:T(4,128)}, u32[]{:S(2)}) copy-start(f32[4,2048]{1,0:T(4,128)} %observed.1) | copy-start | bytes 98308
  10.2 4.9 %copy-start.5 = (f32[4,2048]{1,0:T(4,128)S(1)}, f32[4,2048]{1,0:T(4,128)}, u32[]{:S(2)}) copy-start(f32[4,2048]{1,0:T(4,128)} %obs_var.1) | copy-start | bytes 98308
  10.2 4.9 %copy-start.6 = (s32[4]{0:T(128)S(1)}, s32[4]{0:T(128)}, u32[]{:S(2)}) copy-start(s32[4]{0:T(128)} %refs_1_.1) | copy-start | bytes 52
  20.6 29.2 %collective-permute-start.7 = (f32[8,4,24,256]{3,2,1,0:T(8,128)S(1)}, f32[8,4,24,256]{3,2,1,0:T(8,128)S(1)}, u32[]{:S(2)}, u32[]{:S(2)}) collective-permute-start(f32[8,4,24,256]{3,2,1,0:T(8,128)S(1)} %add_add_fusion.refs_4_), channel_id=1, source_target_pairs={{0,16},{8,24},{16,0},{24,8},{1,17},{9,25},{17,1},{25,9},{2,18},{10... | collective-permute-start | bytes 2359304 | tf_op jit(solution)/shard_map/ppermute | solution.py:549
  22.2 27.6 %collective-permute-start.6 = (f32[8,4,24,256]{3,2,1,0:T(8,128)S(1)}, f32[8,4,24,256]{3,2,1,0:T(8,128)S(1)}, u32[]{:S(2)}, u32[]{:S(2)}) collective-permute-start(f32[8,4,24,256]{3,2,1,0:T(8,128)S(1)} %add_add_fusion.refs_4_), channel_id=1, source_target_pairs={{0,8},{8,0},{16,24},{24,16},{1,9},{9,1},{17,25},{25,17},{2,10},{10... | collective-permute-start | bytes 2359304 | tf_op jit(solution)/shard_map/ppermute | solution.py:549
  22.2 9.4 %collective-permute-start.2 = (f32[4,48,256]{2,1,0:T(8,128)S(1)}, f32[4,48,256]{2,1,0:T(8,128)S(1)}, u32[]{:S(2)}, u32[]{:S(2)}) collective-permute-start(f32[4,48,256]{2,1,0:T(8,128)S(1)} %get-tuple-element.48), channel_id=1, source_target_pairs={{0,1},{1,2},{2,3},{3,4},{4,5},{5,6},{6,7},{8,9},{9,10},{10,11},{11... | collective-permute-start | bytes 589832 | tf_op jit(solution)/shard_map/ppermute | solution.py:573
  26.7 9.6 %collective-permute-start.3 = (f32[4,48,256]{2,1,0:T(8,128)S(1)}, f32[4,48,256]{2,1,0:T(8,128)S(1)}, u32[]{:S(2)}, u32[]{:S(2)}) collective-permute-start(f32[4,48,256]{2,1,0:T(8,128)S(1)} %get-tuple-element.49), channel_id=1, source_target_pairs={{1,0},{2,1},{3,2},{4,3},{5,4},{6,5},{7,6},{9,8},{10,9},{11,10},{12... | collective-permute-start | bytes 589832 | tf_op jit(solution)/shard_map/ppermute | solution.py:573
  38.0 6.7 %collective-permute-start.4 = (f32[4,24,256]{2,1,0:T(8,128)S(1)}, f32[4,24,256]{2,1,0:T(8,128)S(1)}, u32[]{:S(2)}, u32[]{:S(2)}) collective-permute-start(f32[4,24,256]{2,1,0:T(8,128)S(1)} %get-tuple-element.54), channel_id=1, source_target_pairs={{0,1},{1,2},{2,3},{3,4},{4,5},{5,6},{6,7},{8,9},{9,10},{10,11},{11... | collective-permute-start | bytes 294920 | tf_op jit(solution)/shard_map/ppermute | solution.py:573
  42.5 7.2 %collective-permute-start.5 = (f32[4,24,256]{2,1,0:T(8,128)S(1)}, f32[4,24,256]{2,1,0:T(8,128)S(1)}, u32[]{:S(2)}, u32[]{:S(2)}) collective-permute-start(f32[4,24,256]{2,1,0:T(8,128)S(1)} %get-tuple-element.55), channel_id=1, source_target_pairs={{1,0},{2,1},{3,2},{4,3},{5,4},{6,5},{7,6},{9,8},{10,9},{11,10},{12... | collective-permute-start | bytes 294920 | tf_op jit(solution)/shard_map/ppermute | solution.py:573
  51.4 12.2 %collective-permute-start.9 = (f32[4,4,24,256]{3,2,1,0:T(8,128)S(1)}, f32[4,4,24,256]{3,2,1,0:T(8,128)S(1)}, u32[]{:S(2)}, u32[]{:S(2)}) collective-permute-start(f32[4,4,24,256]{3,2,1,0:T(8,128)S(1)} %get-tuple-element.72.refs_16_), channel_id=1, source_target_pairs={{0,16},{8,24},{16,0},{24,8},{1,17},{9,25},{17,1},{25,9},{2,18},{10... | collective-permute-start | bytes 1179656 | tf_op jit(solution)/shard_map/ppermute | solution.py:549
  52.0 6.9 %collective-permute-start.11 = (f32[4,24,256]{2,1,0:T(8,128)S(1)}, f32[4,24,256]{2,1,0:T(8,128)S(1)}, u32[]{:S(2)}, u32[]{:S(2)}) collective-permute-start(f32[4,24,256]{2,1,0:T(8,128)S(1)} %get-tuple-element.61), channel_id=1, source_target_pairs={{0,1},{1,2},{2,3},{3,4},{4,5},{5,6},{6,7},{8,9},{9,10},{10,11},{11... | collective-permute-start | bytes 294920 | tf_op jit(solution)/shard_map/ppermute | solution.py:573
  56.7 6.5 %collective-permute-start.12 = (f32[4,24,256]{2,1,0:T(8,128)S(1)}, f32[4,24,256]{2,1,0:T(8,128)S(1)}, u32[]{:S(2)}, u32[]{:S(2)}) collective-permute-start(f32[4,24,256]{2,1,0:T(8,128)S(1)} %get-tuple-element.62), channel_id=1, source_target_pairs={{1,0},{2,1},{3,2},{4,3},{5,4},{6,5},{7,6},{9,8},{10,9},{11,10},{12... | collective-permute-start | bytes 294920 | tf_op jit(solution)/shard_map/ppermute | solution.py:573
  63.7 19.7 %collective-permute-start.16 = (f32[8,4,24,256]{3,2,1,0:T(8,128)S(1)}, f32[8,4,24,256]{3,2,1,0:T(8,128)S(1)}, u32[]{:S(2)}, u32[]{:S(2)}) collective-permute-start(f32[8,4,24,256]{3,2,1,0:T(8,128)S(1)} %get-tuple-element.64.refs_8_), channel_id=1, source_target_pairs={{0,16},{8,24},{16,0},{24,8},{1,17},{9,25},{17,1},{25,9},{2,18},{10... | collective-permute-start | bytes 2359304 | tf_op jit(solution)/shard_map/ppermute | solution.py:549
  65.3 1.7 %collective-permute-start.8 = (f32[4,4,24,256]{3,2,1,0:T(8,128)S(1)}, f32[4,4,24,256]{3,2,1,0:T(8,128)S(1)}, u32[]{:S(2)}, u32[]{:S(2)}) collective-permute-start(f32[4,4,24,256]{3,2,1,0:T(8,128)S(1)} %get-tuple-element.73.refs_4_.refs_12_), channel_id=1, source_target_pairs={{0,8},{8,0},{16,24},{24,16},{1,9},{9,1},{17,25},{25,17},{2,10},{10... | collective-permute-start | bytes 1179656 | tf_op jit(solution)/shard_map/ppermute | solution.py:549
  65.3 2.3 %collective-permute-start.10 = (f32[4,4,24,256]{3,2,1,0:T(8,128)S(1)}, f32[4,4,24,256]{3,2,1,0:T(8,128)S(1)}, u32[]{:S(2)}, u32[]{:S(2)}) collective-permute-start(f32[4,4,24,256]{3,2,1,0:T(8,128)S(1)} %collective-permute-done.9.refs_6_.refs_14_), channel_id=1, source_target_pairs={{0,8},{8,0},{16,24},{24,16},{1,9},{9,1},{17,25},{25,17},{2,10},{10... | collective-permute-start | bytes 1179656 | tf_op jit(solution)/shard_map/ppermute | solution.py:549
  68.4 4.2 %collective-permute-start.13 = (f32[96,128]{1,0:T(8,128)S(1)}, f32[96,128]{1,0:T(8,128)S(1)}, u32[]{:S(2)}, u32[]{:S(2)}) collective-permute-start(f32[96,128]{1,0:T(8,128)S(1)} %gram.1), channel_id=1, source_target_pairs={{0,1},{1,0},{2,3},{3,2},{4,5},{5,4},{6,7},{7,6},{8,9},{9,8},{10,11... | collective-permute-start | bytes 147464 | tf_op jit(solution)/shard_map/ppermute | solution.py:549
  72.6 4.6 %collective-permute-start.14 = (f32[96,128]{1,0:T(8,128)S(1)}, f32[96,128]{1,0:T(8,128)S(1)}, u32[]{:S(2)}, u32[]{:S(2)}) collective-permute-start(f32[96,128]{1,0:T(8,128)S(1)} %add.17), channel_id=1, source_target_pairs={{0,2},{1,3},{2,0},{3,1},{4,6},{5,7},{6,4},{7,5},{8,10},{9,11},{10,... | collective-permute-start | bytes 147464 | tf_op jit(solution)/shard_map/ppermute | solution.py:549
  77.2 6.2 %collective-permute-start.15 = (f32[96,128]{1,0:T(8,128)S(1)}, f32[96,128]{1,0:T(8,128)S(1)}, u32[]{:S(2)}, u32[]{:S(2)}) collective-permute-start(f32[96,128]{1,0:T(8,128)S(1)} %add.18), channel_id=1, source_target_pairs={{0,4},{1,5},{2,6},{3,7},{4,0},{5,1},{6,2},{7,3},{8,12},{9,13},{10,... | collective-permute-start | bytes 147464 | tf_op jit(solution)/shard_map/ppermute | solution.py:549
  91.1 21.1 %collective-permute-start.18 = (f32[8,4,24,256]{3,2,1,0:T(8,128)S(1)}, f32[8,4,24,256]{3,2,1,0:T(8,128)S(1)}, u32[]{:S(2)}, u32[]{:S(2)}) collective-permute-start(f32[8,4,24,256]{3,2,1,0:T(8,128)S(1)} %last_free.1.refs_8_.refs_0_), channel_id=1, source_target_pairs={{0,16},{8,24},{16,0},{24,8},{1,17},{9,25},{17,1},{25,9},{2,18},{10... | collective-permute-start | bytes 2359304 | tf_op jit(solution)/shard_map/ppermute | solution.py:549
  91.5 27.3 %collective-permute-start.21 = (f32[8,4,24,256]{3,2,1,0:T(8,128)S(1)}, f32[8,4,24,256]{3,2,1,0:T(8,128)S(1)}, u32[]{:S(2)}, u32[]{:S(2)}) collective-permute-start(f32[8,4,24,256]{3,2,1,0:T(8,128)S(1)} %get-tuple-element.64.refs_8_), channel_id=1, source_target_pairs={{0,8},{8,0},{16,24},{24,16},{1,9},{9,1},{17,25},{25,17},{2,10},{10... | collective-permute-start | bytes 2359304 | tf_op jit(solution)/shard_map/ppermute | solution.py:549
  91.5 27.8 %collective-permute-start.20 = (f32[8,4,24,256]{3,2,1,0:T(8,128)S(1)}, f32[8,4,24,256]{3,2,1,0:T(8,128)S(1)}, u32[]{:S(2)}, u32[]{:S(2)}) collective-permute-start(f32[8,4,24,256]{3,2,1,0:T(8,128)S(1)} %collective-permute-done.7.refs_11_.refs_6_), channel_id=1, source_target_pairs={{0,8},{8,0},{16,24},{24,16},{1,9},{9,1},{17,25},{25,17},{2,10},{10... | collective-permute-start | bytes 2359304 | tf_op jit(solution)/shard_map/ppermute | solution.py:549
  92.0 26.8 %collective-permute-start.24 = (f32[4,4,24,256]{3,2,1,0:T(8,128)S(1)}, f32[4,4,24,256]{3,2,1,0:T(8,128)S(1)}, u32[]{:S(2)}, u32[]{:S(2)}) collective-permute-start(f32[4,4,24,256]{3,2,1,0:T(8,128)S(1)} %get-tuple-element.73.refs_4_.refs_12_), channel_id=1, source_target_pairs={{0,16},{8,24},{16,0},{24,8},{1,17},{9,25},{17,1},{25,9},{2,18},{10... | collective-permute-start | bytes 1179656 | tf_op jit(solution)/shard_map/ppermute | solution.py:549
  93.7 32.3 %collective-permute-start.22 = (f32[8,4,24,256]{3,2,1,0:T(8,128)S(1)}, f32[8,4,24,256]{3,2,1,0:T(8,128)S(1)}, u32[]{:S(2)}, u32[]{:S(2)}) collective-permute-start(f32[8,4,24,256]{3,2,1,0:T(8,128)S(1)} %collective-permute-done.16.refs_10_), channel_id=1, source_target_pairs={{0,8},{8,0},{16,24},{24,16},{1,9},{9,1},{17,25},{25,17},{2,10},{10... | collective-permute-start | bytes 2359304 | tf_op jit(solution)/shard_map/ppermute | solution.py:549
  112.2 13.8 %collective-permute-start.17 = (f32[8,4,24,256]{3,2,1,0:T(8,128)S(1)}, f32[8,4,24,256]{3,2,1,0:T(8,128)S(1)}, u32[]{:S(2)}, u32[]{:S(2)}) collective-permute-start(f32[8,4,24,256]{3,2,1,0:T(8,128)S(1)} %last_free.1.refs_8_.refs_0_), channel_id=1, source_target_pairs={{0,8},{8,0},{16,24},{24,16},{1,9},{9,1},{17,25},{25,17},{2,10},{10... | collective-permute-start | bytes 2359304 | tf_op jit(solution)/shard_map/ppermute | solution.py:549
  118.8 7.2 %collective-permute-start.19 = (f32[8,4,24,256]{3,2,1,0:T(8,128)S(1)}, f32[8,4,24,256]{3,2,1,0:T(8,128)S(1)}, u32[]{:S(2)}, u32[]{:S(2)}) collective-permute-start(f32[8,4,24,256]{3,2,1,0:T(8,128)S(1)} %collective-permute-done.18.refs_2_), channel_id=1, source_target_pairs={{0,8},{8,0},{16,24},{24,16},{1,9},{9,1},{17,25},{25,17},{2,10},{10... | collective-permute-start | bytes 2359304 | tf_op jit(solution)/shard_map/ppermute | solution.py:549
  118.8 7.2 %collective-permute-start.23 = (f32[4,4,24,256]{3,2,1,0:T(8,128)S(1)}, f32[4,4,24,256]{3,2,1,0:T(8,128)S(1)}, u32[]{:S(2)}, u32[]{:S(2)}) collective-permute-start(f32[4,4,24,256]{3,2,1,0:T(8,128)S(1)} %get-tuple-element.72.refs_16_), channel_id=1, source_target_pairs={{0,8},{8,0},{16,24},{24,16},{1,9},{9,1},{17,25},{25,17},{2,10},{10... | collective-permute-start | bytes 1179656 | tf_op jit(solution)/shard_map/ppermute | solution.py:549
  119.3 6.7 %collective-permute-start.25 = (f32[4,4,24,256]{3,2,1,0:T(8,128)S(1)}, f32[4,4,24,256]{3,2,1,0:T(8,128)S(1)}, u32[]{:S(2)}, u32[]{:S(2)}) collective-permute-start(f32[4,4,24,256]{3,2,1,0:T(8,128)S(1)} %collective-permute-done.24.refs_18_), channel_id=1, source_target_pairs={{0,8},{8,0},{16,24},{24,16},{1,9},{9,1},{17,25},{25,17},{2,10},{10... | collective-permute-start | bytes 1179656 | tf_op jit(solution)/shard_map/ppermute | solution.py:549

commit v6 on v5

--- a/solution.py
+++ b/solution.py
@@ -9,9 +9,9 @@
 
 SUBSTEPS = 6
 NEWTON = 16
-UNROLL = 5
+UNROLL = 15
 LANES = 128
-SCOPED = 10 * 2**20
+SCOPED = 5 * 2**20
 
 unbind_rate = 0.05
 uptake_rate = 0.1
@@ -129,9 +129,13 @@
 
 
 def two_substeps_kernel(
-    a, r, c, i, low, high, low_first, high_first, diffusivity, binding, source, *refs, lean
+    place, a, r, c, i, low, high, low_first, high_first, diffusivity, binding, source, *refs, halves
 ):
-    out_a, out_r, out_c, out_i, first, last, middle = refs
+    if halves is None:
+        out_a, out_r, out_c, out_i, first, last, middle = refs
+        mid_r, mid_c, mid_i = out_r, out_c, out_i
+    else:
+        *tracers, out_i, out_a, middle, mid_r, mid_c, mid_i = refs
     nx, nz, members, _ = a.shape
     first_substep(
         a,
@@ -144,10 +148,22 @@
         binding,
         source,
         middle,
-        out_r,
-        out_c,
-        out_i,
+        mid_r,
+        mid_c,
+        mid_i,
     )
+    if halves is not None:
+        span = nx // halves
+        for part, tracer in enumerate(tracers):
+            begin = half_begin(place, part, span)
+            for j in range(span):
+                x = j if halves == 1 else begin + j
+                for z in range(nz):
+                    _, _, complexed, internal = react(
+                        middle[x, z], mid_r[x, z], mid_c[x, z], mid_i[x, z], binding[x, pl.ds(z, 1), :]
+                    )
+                    tracer[j, z] = complexed + internal
+                    out_i[x, z] = internal
 
     def outside(halo, origin, x, z):
         later = halo[z, members : 2 * members, :]
@@ -156,9 +172,12 @@
     for x in range(nx):
         for z in range(nz):
             row = pl.ds(z, 1)
-            back, out_r[x, z], out_c[x, z], out_i[x, z] = react(
-                middle[x, z], out_r[x, z], out_c[x, z], out_i[x, z], binding[x, row, :]
-            )
+            if halves is None:
+                back, out_r[x, z], out_c[x, z], out_i[x, z] = react(
+                    middle[x, z], out_r[x, z], out_c[x, z], out_i[x, z], binding[x, row, :]
+                )
+            else:
+                back = react(middle[x, z], mid_r[x, z], mid_c[x, z], 0.0, binding[x, row, :])[0]
             around = beside(
                 lambda x, z: middle[x, z],
                 x,
@@ -173,66 +192,22 @@
                 + back
                 + source[x, row, :]
             )
+    if halves is not None:
+        return
     for x, out in ((0, first), (nx - 1, last)):
         for z in range(nz):
             row = pl.ds(z, 1)
             free = out_a[x, z]
-            out[z, :members, :] = free
-            if lean:
-                continue
             flux = binding[x, row, :] * free * out_r[x, z]
             rest = unbind_rate * out_c[x, z] - flux + source[x, row, :]
+            out[z, :members, :] = free
             out[z, members:, :] = edge_free(
                 lambda x, z: out_a[x, z], rest, x, nz, nx, z, diffusivity[x, row, :]
             )
 
 
-def last_but_one_kernel(
-    place, a, r, c, i, low, high, diffusivity, binding, source, *refs, halves
-):
-    *tracers, out_i, out_a, out_add, first, last, mid_r, mid_c, mid_i = refs
-    nx, nz, _, _ = a.shape
-    first_substep(
-        a,
-        r,
-        c,
-        i,
-        lambda z: low[z],
-        lambda z: high[z],
-        diffusivity,
-        binding,
-        source,
-        out_a,
-        mid_r,
-        mid_c,
-        mid_i,
-    )
-    span = nx // halves
-    for part, tracer in enumerate(tracers):
-        begin = jnp.bitwise_xor(part, lax.shift_right_logical(place[2], 1)) * span
-        for j in range(span):
-            x = j if halves == 1 else begin + j
-            for z in range(nz):
-                row = pl.ds(z, 1)
-                back, _, complexed, internal = react(
-                    out_a[x, z], mid_r[x, z], mid_c[x, z], mid_i[x, z], binding[x, row, :]
-                )
-                tracer[j, z] = complexed + internal
-                out_i[x, z] = internal
-                out_add[x, z] = back + source[x, row, :]
-    for x, out in ((0, first), (nx - 1, last)):
-        for z in range(nz):
-            out[z] = out_a[x, z]
-
-
-def last_free_kernel(a, add, low, high, diffusivity, out_a):
-    nx, nz, _, _ = a.shape
-    for x in range(nx):
-        for z in range(nz):
-            around = beside(lambda x, z: a[x, z], x, z, nx, nz, low[z], high[z])
-            out_a[x, z] = (
-                spread_free(a[x, z], around, None, diffusivity[x, pl.ds(z, 1), :]) + add[x, z]
-            )
+def half_begin(place, part, span):
+    return jnp.bitwise_xor(part, lax.shift_right_logical(place[2], 1)) * span
 
 
 def forecast_call(kernel, name, inputs, outputs, cells, scratch=(), ready=(), scalars=()):
@@ -416,8 +391,8 @@
     return wide_dot(wide_left(total), wide_right(mixing))
 
 
-def unpack(place, shares, groups, ordered):
-    members = ordered.shape[1]
+def transform_kernel(place, mine, other, out, ordered, work, *, offsets, blocks, rows):
+    members = mine.shape[0]
     row = lax.broadcasted_iota(jnp.int32, (members, LANES), 0)
     column = lax.broadcasted_iota(jnp.int32, (members, LANES), 1)
     inside = column < members
@@ -425,8 +400,8 @@
     def pick(where, x):
         return jnp.sum(jnp.where(where, x, 0.0), axis=1, keepdims=True)
 
-    for half, group in zip((place[0], 1 - place[0]), groups(place[2])):
-        packed = sum(shares[k] for k in group)
+    for half, shared in ((place[0], mine), (1 - place[0], other)):
+        packed = shared[...]
         above = jnp.where(inside & (column > row), packed, 0.0)
         below = jnp.where(inside & (column < row), packed, 0.0)
         middle = jnp.where(column == row, packed, 0.0)
@@ -435,25 +410,11 @@
         middle = jnp.where(column == row, pick(column == members, packed), 0.0)
         side = jnp.where(column == members, pick(column == members + 2, packed), 0.0)
         ordered[2 * half + 1] = below + turned(below) + (middle + side)
-
-
-def early_kernel(place, shares, total, last, ordered, *, groups):
-    unpack(place, shares, groups, ordered)
-    batches, members, _ = ordered.shape
-    row = lax.broadcasted_iota(jnp.int32, (members, LANES), 0)
-    column = lax.broadcasted_iota(jnp.int32, (members, LANES), 1)
-    product = jnp.where(row == column, 1.0, 0.0)
-    for batch in range(batches - 1):
-        product = batch_transform(ordered[batch], product, members)
-    total[...] = product
-    last[...] = ordered[batches - 1]
-
-
-def late_kernel(place, total, last, out, work, *, offsets, blocks, rows):
-    members = total.shape[0]
-    product = batch_transform(last[...], total[...], members)
+    total = jnp.where(row == column, 1.0, 0.0)
+    for batch in range(ordered.shape[0]):
+        total = batch_transform(ordered[batch], total, members)
     rest = jnp.zeros((LANES - members, LANES), f32)
-    work[...] = jnp.concatenate([product, rest], axis=0)
+    work[...] = jnp.concatenate([total, rest], axis=0)
     if blocks == 1:
         out[...] = work[...].T
         return
@@ -464,20 +425,24 @@
     out[...] = work[pl.ds(pl.multiple_of(offsets(place[2], 0), 8), rows), :]
 
 
-def transform_call(kernel, name, out_shape, scratch, inputs):
-    many = isinstance(out_shape, list)
+def transforms(place, mine, other, offsets, blocks, rows):
+    members = mine.shape[0]
+    shape = (LANES, LANES) if blocks == 1 else (rows, LANES)
     return pl.pallas_call(
-        kernel,
-        out_shape=out_shape,
-        in_specs=[SMEM] + [VMEM] * (len(inputs) - 1),
-        out_specs=[VMEM] * len(out_shape) if many else VMEM,
-        scratch_shapes=[pltpu.VMEM(shape, f32) for shape in scratch],
+        functools.partial(transform_kernel, offsets=offsets, blocks=blocks, rows=rows),
+        out_shape=jax.ShapeDtypeStruct(shape, f32),
+        in_specs=[SMEM, VMEM, VMEM],
+        out_specs=VMEM,
+        scratch_shapes=[
+            pltpu.VMEM((4, members, LANES), f32),
+            pltpu.VMEM((LANES, LANES), f32),
+        ],
         compiler_params=pltpu.CompilerParams(vmem_limit_bytes=SCOPED),
         cost_estimate=pl.CostEstimate(
             flops=10**8, bytes_accessed=10**6, transcendentals=0
         ),
-        name=name,
-    )(*inputs)
+        name="transforms",
+    )(place, mine, other)
 
 
 def mix_kernel(place, weights, *refs, blocks, halves):
@@ -517,10 +482,6 @@
                 out[:, 3, 0, z, :] = inside
 
 
-def half_begin(place, part, span):
-    return jnp.bitwise_xor(part, lax.shift_right_logical(place[2], 1)) * span
-
-
 def mix(place, weights, sources, blocks, halves, shape):
     rows, species, nx, nz, ny = shape
     span = nx // halves
@@ -578,10 +539,6 @@
         def offsets(position, j):
             return jnp.bitwise_xor(position, j) * rows
 
-        def groups(position):
-            flip = functools.partial(jnp.bitwise_xor, position)
-            return (position, flip(2)), (flip(1), flip(3))
-
         def collect(x, sent=None):
             return [x, swap(x, "member", 1), swap(x if sent is None else sent, "member", 2)]
 
@@ -593,9 +550,6 @@
         def offsets(position, j):
             return 0
 
-        def groups(position):
-            return (0,), (1,)
-
         def collect(x):
             return [lax.all_gather(x, "member", axis=2, tiled=True)]
 
@@ -608,7 +562,7 @@
     def tie(x, *after):
         return lax.optimization_barrier((x, *after))[0]
 
-    whole, plane = (nx, nz, rows, ny), (nz, rows, ny)
+    whole = (nx, nz, rows, ny)
     coefficients = (diffusivity, binding, source)
     cells = nx * nz * rows * ny
     ends = [
@@ -628,75 +582,42 @@
         place, owner, obs_index, observed, obs_var, batches // 2, nx * nz, ny
     )
     around = origin = halos(*edges)
-    steps = SUBSTEPS // 2 - 1
+    steps = SUBSTEPS // 2
     for step in range(steps):
-        lean = step == steps - 1
-        *fields, first, last = forecast_call(
-            functools.partial(two_substeps_kernel, lean=lean),
+        final = step == steps - 1
+        outputs = [whole] * 4 + [(nz, 2 * rows, ny)] * 2
+        if final:
+            outputs = [(nx // halves, nz, rows, ny)] * halves + [whole] * 2
+        *fields, = forecast_call(
+            functools.partial(two_substeps_kernel, halves=halves if final else None),
             "two_substeps",
             [*fields, *around, *origin, *coefficients],
-            [whole] * 4 + [plane if lean else (nz, 2 * rows, ny)] * 2,
+            outputs,
             2 * cells,
-            scratch=[whole],
-            ready=(omega, eta) if step == 0 else (),
+            scratch=[whole] * (4 if final else 1),
+            ready=(omega, eta) if step == 0 else conserved[1:] if final else (),
+            scalars=[place],
         )
-        around = halos(first, last)
+        if not final:
+            around = halos(*fields[4:])
+            fields = fields[:4]
         if step == 0:
             conserved = collect(tie(conserved, fields[0]))
-    *tracers, internal, free, add, first, last = forecast_call(
-        functools.partial(last_but_one_kernel, halves=halves),
-        "last_but_one",
-        [*fields, *around, *coefficients],
-        [(nx // halves, nz, rows, ny)] * halves + [whole] * 3 + [plane] * 2,
-        2 * cells,
-        scratch=[whole] * 3,
-        ready=conserved[1:],
-        scalars=[place],
-    )
+    *tracers, internal, free = fields
+    near = complete(collect(*tracers))
+    conserved = complete(conserved, across(near))
+    internal = collect(tie(internal, across(near)))
+    half = total_over(gram(place, owner, omega, eta, near, offsets, halves, ()), "space")
+    half = tie(half, across(internal))
     if halves == 2:
-        near, far = tracers
-        near = complete(collect(near, far))
-    else:
-        near = collect(tracers[0])
-    (free,) = forecast_call(
-        last_free_kernel,
-        "last_free",
-        [free, add, *halos(first, last), diffusivity],
-        [whole],
-        cells,
-    )
-    conserved = complete(conserved, across(near), free)
-    internal = collect(tie(internal, across(near), free))
-    half = total_over(gram(place, owner, omega, eta, near, offsets, halves, [free]), "space")
+        half = half + swap(half, "member", 2)
+        far = collect(tie(tracers[1], half), tie(tracers[0], half))
+    free = collect(tie(free, half))
+    internal = complete(internal, half)
+    weights = transforms(place, half, swap(half, "member", 1), offsets, blocks, rows)
+    free = complete(free, weights)
     if halves == 2:
-        half = tie(half, across(internal))
-        shares = lax.all_to_all(
-            jnp.broadcast_to(half, (devices, *half.shape)), "member", 0, 0
-        )
-        far = collect(tie(far, shares), tie(tracers[0], shares))
-        free = collect(tie(free, shares))
-    else:
-        free = collect(free)
-        shares = jnp.stack([half, swap(half, "member", 1)])
-    internal = complete(internal, half)
-    square = jax.ShapeDtypeStruct((members, LANES), f32)
-    total, extended = transform_call(
-        functools.partial(early_kernel, groups=groups),
-        "transforms_early",
-        [square, square],
-        [(batches, members, LANES)],
-        [place, shares],
-    )
-    if halves == 2:
-        far = complete(far, total)
-    free = complete(free, total)
-    weights = transform_call(
-        functools.partial(late_kernel, offsets=offsets, blocks=blocks, rows=rows),
-        "transforms_late",
-        jax.ShapeDtypeStruct((LANES, LANES) if blocks == 1 else (rows, LANES), f32),
-        [(LANES, LANES)],
-        [place, total, extended],
-    )
+        far = complete(far, weights)
     if blocks == 1:
         weights = lax.dynamic_slice(weights, (member * rows, 0), (rows, LANES))
     sources = free + conserved + internal + near + (far if halves == 2 else [])

time: 132 us -> 131 us (level)
  waiting for transfers between devices: 35.2 us -> 43.3 us
  blocking collectives: 7.7 us -> 0 us
    ppermute x18 -> x20, waiting for transfers between devices: 15.7 us -> 27 us  [swap(): return lax.ppermute(x, axis, [(k, k ^ bit) for k in range(count)])]
    all_to_all x1 -> x0, blocking collectives: 7.7 us -> none  [local(): lax.all_to_all(jnp.broadcast_to(half, (devices, *half.shape)), 'member',...]
    ppermute x18 -> x20, starting transfers between devices: 15 us -> 20.3 us  [swap(): return lax.ppermute(x, axis, [(k, k ^ bit) for k in range(count)])]
    ppermute x4 -> x3, starting transfers between devices: 18.6 us -> 14 us  [halos(): lax.ppermute(last, 'space', forward)]
    ppermute x4 -> x3, waiting for transfers between devices: 14.2 us -> 10.4 us  [halos(): lax.ppermute(first, 'space', backward)]
    ppermute x4 -> x3, starting transfers between devices: 5.17 us -> 3.88 us  [halos(): lax.ppermute(first, 'space', backward)]
    pallas_call x5 -> x4, Pallas kernels: 5.69 us -> 6.72 us  [forecast_call(): pl.pallas_call(body, out_shape=[jax.ShapeDtypeStruct(shape, f32) for shap...]
    pallas_call x2 -> x1, Pallas kernels: 25.1 us -> 24.1 us  [transforms(): pl.pallas_call(functools.partial(transform_kernel, offsets=offsets, block...]
  transfers between devices with their start and end apart: 26 -> 26, of which waited for: 12 -> 14; matrix products, arithmetic and copies ran while one was open for 7% -> 7% of each run, Pallas kernels for 22% -> 22%
where the time goes in v6:
time: 131 us; the launch traced here: 132 us
  waiting for transfers between devices  43.3 us (33%)
  Pallas kernels  38.9 us (30%)
  starting transfers between devices  38.1 us (29%)
  local copies, waits for them, and re-layouts  8.41 us (6%)
  other arithmetic  2.51 us (2%)
    ppermute x20, waiting for transfers between devices, swap(): return lax.ppermute(x, axis, [(k, k ^ bit) for k in range(count)])  27 us
    pallas_call x1, Pallas kernels, transforms(): pl.pallas_call(functools.partial(transform_kernel, offsets=offsets, block...  24.1 us
    ppermute x20, starting transfers between devices, swap(): return lax.ppermute(x, axis, [(k, k ^ bit) for k in range(count)])  20.3 us
    ppermute x3, starting transfers between devices, halos(): lax.ppermute(last, 'space', forward)  14 us
    ppermute x3, waiting for transfers between devices, halos(): lax.ppermute(first, 'space', backward)  10.4 us
    pallas_call x4, Pallas kernels, forecast_call(): pl.pallas_call(body, out_shape=[jax.ShapeDtypeStruct(shape, f32) for shap...  6.72 us
    ppermute x3, waiting for transfers between devices, halos(): lax.ppermute(last, 'space', forward)  5.91 us
    pallas_call x1, Pallas kernels, mix(): pl.pallas_call(functools.partial(mix_kernel, blocks=blocks, halves=halves...  5.84 us
  transfers between devices with their start and end apart: 26, of which 14 were waited for; matrix products, arithmetic and copies ran while one was open for 7% of the time, Pallas kernels for 22%

profile of v6, /device:TPU:0, one launch (start us, length us, event | category | flops | bytes accessed | tf_op | source)
XLA Modules:
  0.0 131.6 jit_solution(7258871563833194666)
XLA Ops:
  0.0 1.6 %fusion = (f32[24,3,2,4,256]{4,3,2,1,0:T(4,128)S(1)}, f32[24,3,2,4,256]{4,3,2,1,0:T(4,128)S(1)}) fusion(f32[24,4,8,4,256]{4,3,2,1,0:T(4,128)} %param.8), kind=kLoop, calls=%fused_computation.8 | loop fusion | bytes 2359296 | tf_op jit(solution)/shard_map/slice | solution.py:569
  1.6 0.4 copy_bitcast_fusion.4
  2.0 0.2 first_edges.1
  2.2 4.9 %collective-permute-start = (f32[4,56,256]{2,1,0:T(8,128)S(1)}, f32[4,56,256]{2,1,0:T(8,128)S(1)}, u32[]{:S(2)}, u32[]{:S(2)}) collective-permute-start(f32[4,56,256]{2,1,0:T(8,128)S(1)} %get-tuple-element.37), channel_id=1, source_target_pairs={{0,1},{1,2},{2,3},{3,4},{4,5},{5,6},{6,7},{8,9},{9,10},{10,11},{11... | collective-permute-start | bytes 688136 | tf_op jit(solution)/shard_map/ppermute | solution.py:534
  7.1 1.3 collective-permute-start.1
  8.4 1.7 %fusion.1 = (f32[24,1,8,4,256]{4,3,2,1,0:T(4,128)S(1)}, f32[24,1,8,4,256]{4,3,2,1,0:T(4,128)}, f32[24,1,8,4,256]{4,3,2,1,0:T(4,128)}, f32[24,1,8,4,256]{4,3,2,1,0:T(4,128)}) fusion(f32[24,4,8,4,256]{4,3,2,1,0:T(4,128)S(1)} %copy-done.10), kind=kLoop, calls=%fused_computation.9 | loop fusion | bytes 6291456 | tf_op jit(solution)/shard_map/slice | solution.py:579
  10.2 0.0 copy-start.4
  10.2 0.0 copy-start.5
  10.2 0.0 copy-start.6
  10.2 2.4 %copy_bitcast_fusion = (f32[8,4,24,256]{3,2,1,0:T(8,128)S(1)}, f32[8,4,24,256]{3,2,1,0:T(8,128)S(1)}) fusion(f32[24,1,8,4,256]{4,3,2,1,0:T(4,128)S(1)} %get-tuple-element.67, f32[24,1,8,4,256]{4,3,2,1,0:T(4,128)} %get-tuple-element.68), kind=kLoop, calls=%fused_computation | loop fusion | bytes 3145728 | tf_op jit(solution)/shard_map/transpose | solution.py:579
  12.6 2.4 %add_add_fusion.refs_4_ = f32[8,4,24,256]{3,2,1,0:T(8,128)S(1)} fusion(f32[24,1,8,4,256]{4,3,2,1,0:T(4,128)S(1)} %copy-done.7, f32[24,1,8,4,256]{4,3,2,1,0:T(4,128)S(1)} %copy-done.9, f32[24,1,8,4,256]{4,3,2,1,0:T(4,128)} %copy-done.8), kind=kLoop, calls=%fused_computation.4 | loop fusion | flops 393216 | bytes 3145728 | tf_op jit(solution)/shard_map/add | solution.py:580
  15.0 0.1 pad_add_fusion.place.refs_0_
  15.1 1.4 %voxel_weights.1 = (f32[2,32,256]{2,1,0:T(8,128)S(1)}, f32[2,32,256]{2,1,0:T(8,128)S(1)}) custom-call(s32[3]{0:T(128)S(1)} %pad_add_fusion.place.refs_0_, s32[4]{0:T(128)S(1)} %copy-done.6, s32[4,2048]{1,0:T(4,128)S(1)} %copy-done.3, f32[4,2048]{1,0:T(4,128)S(1)} %copy-done.4, f32[4,2048]{1,0:T(4,128)S(1)} %copy-done.5), custom_call_target="tpu_custom_call" | custom-call | tf_op jit(solution)/shard_map/voxel_weights/pallas_call | solution.py:270
  16.5 2.3 %copy_bitcast_fusion.2 = (f32[8,4,24,256]{3,2,1,0:T(8,128)S(1)}, f32[8,4,24,256]{3,2,1,0:T(8,128)S(1)}) fusion(f32[24,1,8,4,256]{4,3,2,1,0:T(4,128)} %get-tuple-element.69, f32[24,1,8,4,256]{4,3,2,1,0:T(4,128)} %get-tuple-element.70), kind=kLoop, calls=%fused_computation.2 | loop fusion | bytes 3145728 | tf_op jit(solution)/shard_map/transpose | solution.py:579
  18.8 0.0 collective-permute-done.refs_5_.refs_7_
  18.8 0.0 collective-permute-done.1.refs_6_.refs_8_
  18.8 2.3 %two_substeps.3 = (f32[8,4,24,256]{3,2,1,0:T(8,128)S(1)}, f32[8,4,24,256]{3,2,1,0:T(8,128)S(1)}, f32[8,4,24,256]{3,2,1,0:T(8,128)S(1)}, f32[8,4,24,256]{3,2,1,0:...) custom-call(s32[3]{0:T(128)S(1)} %pad_add_fusion.place.refs_0_, ...), custom_call_target="tpu_custom_call" | custom-call | flops 11796480 | bytes 12582912 | tf_op jit(solution)/shard_map/two_substeps/pallas_call | solution.py:218
  21.1 1.6 %collective-permute-start.7 = (f32[8,4,24,256]{3,2,1,0:T(8,128)S(1)}, f32[8,4,24,256]{3,2,1,0:T(8,128)S(1)}, u32[]{:S(2)}, u32[]{:S(2)}) collective-permute-start(f32[8,4,24,256]{3,2,1,0:T(8,128)S(1)} %add_add_fusion.refs_4_), channel_id=1, source_target_pairs={{0,16},{8,24},{16,0},{24,8},{1,17},{9,25},{17,1},{25,9},{2,18},{10... | collective-permute-start | bytes 2359304 | tf_op jit(solution)/shard_map/ppermute | solution.py:510
  22.7 0.0 collective-permute-start.6
  22.7 4.5 %collective-permute-start.2 = (f32[4,48,256]{2,1,0:T(8,128)S(1)}, f32[4,48,256]{2,1,0:T(8,128)S(1)}, u32[]{:S(2)}, u32[]{:S(2)}) collective-permute-start(f32[4,48,256]{2,1,0:T(8,128)S(1)} %get-tuple-element.43), channel_id=1, source_target_pairs={{0,1},{1,2},{2,3},{3,4},{4,5},{5,6},{6,7},{8,9},{9,10},{10,11},{11... | collective-permute-start | bytes 589832 | tf_op jit(solution)/shard_map/ppermute | solution.py:534
  27.3 1.3 collective-permute-start.3
  28.6 3.5 %collective-permute-done.2.refs_5_ = f32[4,48,256]{2,1,0:T(8,128)S(1)} collective-permute-done((f32[4,48,256]{2,1,0:T(8,128)S(1)}, f32[4,48,256]{2,1,0:T(8,128)S(1)}, u32[]{:S(2)}, u32[]{:S(2)}) %collective-permute-start.2) | collective-permute-done | bytes 196640 | tf_op jit(solution)/shard_map/ppermute | solution.py:534
  32.1 4.8 %collective-permute-done.3.refs_6_ = f32[4,48,256]{2,1,0:T(8,128)S(1)} collective-permute-done((f32[4,48,256]{2,1,0:T(8,128)S(1)}, f32[4,48,256]{2,1,0:T(8,128)S(1)}, u32[]{:S(2)}, u32[]{:S(2)}) %collective-permute-start.3) | collective-permute-done | bytes 196640 | tf_op jit(solution)/shard_map/ppermute | solution.py:534
  36.9 2.2 %two_substeps.4 = (f32[8,4,24,256]{3,2,1,0:T(8,128)S(1)}, f32[8,4,24,256]{3,2,1,0:T(8,128)S(1)}, f32[8,4,24,256]{3,2,1,0:T(8,128)S(1)}, f32[8,4,24,256]{3,2,1,0:...) custom-call(s32[3]{0:T(128)S(1)} %pad_add_fusion.place.refs_0_, ...), custom_call_target="tpu_custom_call" | custom-call | flops 11796480 | bytes 12582912 | tf_op jit(solution)/shard_map/two_substeps/pallas_call | solution.py:218
  39.1 4.5 %collective-permute-start.4 = (f32[4,48,256]{2,1,0:T(8,128)S(1)}, f32[4,48,256]{2,1,0:T(8,128)S(1)}, u32[]{:S(2)}, u32[]{:S(2)}) collective-permute-start(f32[4,48,256]{2,1,0:T(8,128)S(1)} %get-tuple-element.49), channel_id=1, source_target_pairs={{0,1},{1,2},{2,3},{3,4},{4,5},{5,6},{6,7},{8,9},{9,10},{10,11},{11... | collective-permute-start | bytes 589832 | tf_op jit(solution)/shard_map/ppermute | solution.py:534
  43.7 1.3 collective-permute-start.5
  45.0 2.4 %collective-permute-done.4.refs_5_ = f32[4,48,256]{2,1,0:T(8,128)S(1)} collective-permute-done((f32[4,48,256]{2,1,0:T(8,128)S(1)}, f32[4,48,256]{2,1,0:T(8,128)S(1)}, u32[]{:S(2)}, u32[]{:S(2)}) %collective-permute-start.4) | collective-permute-done | bytes 196640 | tf_op jit(solution)/shard_map/ppermute | solution.py:534
  47.4 5.6 %collective-permute-done.5.refs_6_ = f32[4,48,256]{2,1,0:T(8,128)S(1)} collective-permute-done((f32[4,48,256]{2,1,0:T(8,128)S(1)}, f32[4,48,256]{2,1,0:T(8,128)S(1)}, u32[]{:S(2)}, u32[]{:S(2)}) %collective-permute-start.5) | collective-permute-done | bytes 196640 | tf_op jit(solution)/shard_map/ppermute | solution.py:534
  53.0 0.0 collective-permute-done.7.refs_13_.refs_6_
  53.0 0.0 collective-permute-done.6.refs_12_.refs_5_
  53.0 2.0 %two_substeps.5 = (f32[4,4,24,256]{3,2,1,0:T(8,128)S(1)}, f32[4,4,24,256]{3,2,1,0:T(8,128)S(1)}, f32[8,4,24,256]{3,2,1,0:T(8,128)S(1)}, f32[8,4,24,256]{3,2,1,0:T(8,128)S(1)}) custom-call(s32[3]{0:T(128)S(1)} %pad_add_fusion.place.refs_0_, f32[8,4,24,256]{3,2,1,0:T(8,128)S(1)} %get-tuple-element.45.refs_1_, f32[8,4,24,256]{3,2,1,0:T(8,128)S(1)} %get-tuple-element.46.refs_2_, ...), custom_call_target="tpu_custom_call" | custom-call | flops 11796480 | bytes 12582912 | tf_op jit(solution)/shard_map/two_substeps/pallas_call | solution.py:218
  55.0 0.6 collective-permute-start.9
  55.6 9.7 %collective-permute-done.9.refs_6_.refs_14_ = f32[4,4,24,256]{3,2,1,0:T(8,128)S(1)} collective-permute-done((f32[4,4,24,256]{3,2,1,0:T(8,128)S(1)}, f32[4,4,24,256]{3,2,1,0:T(8,128)S(1)}, u32[]{:S(2)}, u32[]{:S(2)}) %collective-permute-start.9) | collective-permute-done | bytes 393248 | tf_op jit(solution)/shard_map/ppermute | solution.py:510
  65.4 0.5 collective-permute-start.14
  65.9 0.5 collective-permute-start.10
  66.4 1.2 collective-permute-done.8.refs_5_.refs_13_
  67.6 0.6 collective-permute-done.10.refs_7_.refs_15_
  68.2 0.9 gram.1
  69.0 2.4 %collective-permute-start.11 = (f32[96,128]{1,0:T(8,128)S(1)}, f32[96,128]{1,0:T(8,128)S(1)}, u32[]{:S(2)}, u32[]{:S(2)}) collective-permute-start(f32[96,128]{1,0:T(8,128)S(1)} %gram.1), channel_id=1, source_target_pairs={{0,1},{1,0},{2,3},{3,2},{4,5},{5,4},{6,7},{7,6},{8,9},{9,8},{10,11... | collective-permute-start | bytes 147464 | tf_op jit(solution)/shard_map/ppermute | solution.py:510
  71.4 2.2 %collective-permute-done.11 = f32[96,128]{1,0:T(8,128)S(1)} collective-permute-done((f32[96,128]{1,0:T(8,128)S(1)}, f32[96,128]{1,0:T(8,128)S(1)}, u32[]{:S(2)}, u32[]{:S(2)}) %collective-permute-start.11) | collective-permute-done | bytes 49184 | tf_op jit(solution)/shard_map/ppermute | solution.py:510
  73.6 5.8 %collective-permute-start.12 = (f32[96,128]{1,0:T(8,128)S(1)}, f32[96,128]{1,0:T(8,128)S(1)}, u32[]{:S(2)}, u32[]{:S(2)}) collective-permute-start(f32[96,128]{1,0:T(8,128)S(1)} %add.20), channel_id=1, source_target_pairs={{0,2},{1,3},{2,0},{3,1},{4,6},{5,7},{6,4},{7,5},{8,10},{9,11},{10,... | collective-permute-start | bytes 147464 | tf_op jit(solution)/shard_map/ppermute | solution.py:510
  79.4 2.1 %collective-permute-done.12 = f32[96,128]{1,0:T(8,128)S(1)} collective-permute-done((f32[96,128]{1,0:T(8,128)S(1)}, f32[96,128]{1,0:T(8,128)S(1)}, u32[]{:S(2)}, u32[]{:S(2)}) %collective-permute-start.12) | collective-permute-done | bytes 49184 | tf_op jit(solution)/shard_map/ppermute | solution.py:510
  81.5 3.5 %collective-permute-start.13 = (f32[96,128]{1,0:T(8,128)S(1)}, f32[96,128]{1,0:T(8,128)S(1)}, u32[]{:S(2)}, u32[]{:S(2)}) collective-permute-start(f32[96,128]{1,0:T(8,128)S(1)} %add.21), channel_id=1, source_target_pairs={{0,4},{1,5},{2,6},{3,7},{4,0},{5,1},{6,2},{7,3},{8,12},{9,13},{10,... | collective-permute-start | bytes 147464 | tf_op jit(solution)/shard_map/ppermute | solution.py:510
  85.0 2.1 %collective-permute-done.13 = f32[96,128]{1,0:T(8,128)S(1)} collective-permute-done((f32[96,128]{1,0:T(8,128)S(1)}, f32[96,128]{1,0:T(8,128)S(1)}, u32[]{:S(2)}, u32[]{:S(2)}) %collective-permute-start.13) | collective-permute-done | bytes 49184 | tf_op jit(solution)/shard_map/ppermute | solution.py:510
  87.1 0.0 collective-permute-done.14.refs_10_
  87.1 1.6 %collective-permute-start.15 = (f32[96,128]{1,0:T(8,128)S(1)}, f32[96,128]{1,0:T(8,128)S(1)}, u32[]{:S(2)}, u32[]{:S(2)}) collective-permute-start(f32[96,128]{1,0:T(8,128)S(1)} %add.22), channel_id=1, source_target_pairs={{0,16},{8,24},{16,0},{24,8},{1,17},{9,25},{17,1},{25,9},{2,18},{10... | collective-permute-start | bytes 147464 | tf_op jit(solution)/shard_map/ppermute | solution.py:510
  88.7 3.2 %collective-permute-done.15 = f32[96,128]{1,0:T(8,128)S(1)} collective-permute-done((f32[96,128]{1,0:T(8,128)S(1)}, f32[96,128]{1,0:T(8,128)S(1)}, u32[]{:S(2)}, u32[]{:S(2)}) %collective-permute-start.15) | collective-permute-done | bytes 49184 | tf_op jit(solution)/shard_map/ppermute | solution.py:510
  91.8 1.6 %collective-permute-start.18 = (f32[8,4,24,256]{3,2,1,0:T(8,128)S(1)}, f32[8,4,24,256]{3,2,1,0:T(8,128)S(1)}, u32[]{:S(2)}, u32[]{:S(2)}) collective-permute-start(f32[8,4,24,256]{3,2,1,0:T(8,128)S(1)} %get-tuple-element.58.refs_0_), channel_id=1, source_target_pairs={{0,16},{8,24},{16,0},{24,8},{1,17},{9,25},{17,1},{25,9},{2,18},{10... | collective-permute-start | bytes 2359304 | tf_op jit(solution)/shard_map/ppermute | solution.py:510
  93.4 0.5 collective-permute-start.20
  93.9 0.5 collective-permute-start.24
  94.4 0.0 collective-permute-start.16
  94.4 2.5 %collective-permute-done.16.other = f32[96,128]{1,0:T(8,128)S(1)} collective-permute-done((f32[96,128]{1,0:T(8,128)S(1)}, f32[96,128]{1,0:T(8,128)S(1)}, u32[]{:S(2)}, u32[]{:S(2)}) %collective-permute-start.16) | collective-permute-done | bytes 49184 | tf_op jit(solution)/shard_map/ppermute | solution.py:510
  96.9 0.1 collective-permute-start.17
  97.0 24.1 %transforms.1.weights = f32[24,128]{1,0:T(8,128)S(1)} custom-call(s32[3]{0:T(128)S(1)} %pad_add_fusion.place.refs_0_, f32[96,128]{1,0:T(8,128)S(1)} %add.23.mine, f32[96,128]{1,0:T(8,128)S(1)} %collective-permute-done.16.other), custom_call_target="tpu_custom_call" | custom-call | flops 100000000 | bytes 1000000 | tf_op jit(solution)/shard_map/transforms/pallas_call | solution.py:431
  121.1 0.0 collective-permute-done.18.refs_2_
  121.1 0.4 collective-permute-start.22
  121.6 0.1 collective-permute-start.19
  121.7 0.0 collective-permute-done.21.refs_9_
  121.7 0.4 collective-permute-start.23
  122.1 0.1 collective-permute-start.25
  122.2 2.9 %collective-permute-done.23.refs_17_ = f32[4,4,24,256]{3,2,1,0:T(8,128)S(1)} collective-permute-done((f32[4,4,24,256]{3,2,1,0:T(8,128)S(1)}, f32[4,4,24,256]{3,2,1,0:T(8,128)S(1)}, u32[]{:S(2)}, u32[]{:S(2)}) %collective-permute-start.23) | collective-permute-done | bytes 393248 | tf_op jit(solution)/shard_map/ppermute | solution.py:510
  125.2 0.6 collective-permute-done.25.refs_19_
  125.7 0.0 collective-permute-done.17.refs_1_
  125.7 5.8 %mix.1 = f32[24,4,8,4,256]{4,3,2,1,0:T(4,128)} custom-call(s32[3]{0:T(128)S(1)} %pad_add_fusion.place.refs_0_, f32[24,128]{1,0:T(8,128)S(1)} %transforms.1.weights, f32[8,4,24,256]{3,2,1,0:T(8,128)S(1)} %get-tuple-element.58.refs_0_, f32[8,4,24,256]{3,2,1,0:T(8,128)S(1)} %collective-permute-done.17.refs_1_, ...), custom_call_target="tpu_custom_call" | custom-call | tf_op jit(solution)/shard_map/mix/pallas_call | solution.py:494
  (29 shorter events, 0.1 us)
Async XLA Ops:
  0.0 8.4 %copy-start.10 = (f32[24,4,8,4,256]{4,3,2,1,0:T(4,128)S(1)}, f32[24,4,8,4,256]{4,3,2,1,0:T(4,128)}, u32[]{:S(2)}) copy-start(f32[24,4,8,4,256]{4,3,2,1,0:T(4,128)} %param.8) | copy-start | bytes 9437188
  0.0 2.0 %copy-start.2 = (f32[8,4,256]{2,1,0:T(4,128)S(1)}, f32[8,4,256]{2,1,0:T(4,128)}, u32[]{:S(2)}) copy-start(f32[8,4,256]{2,1,0:T(4,128)} %refs_11_.5) | copy-start | bytes 98308
  0.0 2.0 %copy-start.1 = (f32[8,4,256]{2,1,0:T(4,128)S(1)}, f32[8,4,256]{2,1,0:T(4,128)}, u32[]{:S(2)}) copy-start(f32[8,4,256]{2,1,0:T(4,128)} %refs_10_.5) | copy-start | bytes 98308
  0.0 2.0 %copy-start = (f32[8,4,256]{2,1,0:T(4,128)S(1)}, f32[8,4,256]{2,1,0:T(4,128)}, u32[]{:S(2)}) copy-start(f32[8,4,256]{2,1,0:T(4,128)} %refs_9_.5) | copy-start | bytes 98308
  2.2 16.6 %collective-permute-start = (f32[4,56,256]{2,1,0:T(8,128)S(1)}, f32[4,56,256]{2,1,0:T(8,128)S(1)}, u32[]{:S(2)}, u32[]{:S(2)}) collective-permute-start(f32[4,56,256]{2,1,0:T(8,128)S(1)} %get-tuple-element.37), channel_id=1, source_target_pairs={{0,1},{1,2},{2,3},{3,4},{4,5},{5,6},{6,7},{8,9},{9,10},{10,11},{11... | collective-permute-start | bytes 688136 | tf_op jit(solution)/shard_map/ppermute | solution.py:534
  7.1 11.7 %collective-permute-start.1 = (f32[4,56,256]{2,1,0:T(8,128)S(1)}, f32[4,56,256]{2,1,0:T(8,128)S(1)}, u32[]{:S(2)}, u32[]{:S(2)}) collective-permute-start(f32[4,56,256]{2,1,0:T(8,128)S(1)} %get-tuple-element.38), channel_id=1, source_target_pairs={{1,0},{2,1},{3,2},{4,3},{5,4},{6,5},{7,6},{9,8},{10,9},{11,10},{12... | collective-permute-start | bytes 688136 | tf_op jit(solution)/shard_map/ppermute | solution.py:534
  10.2 2.4 %copy-start.8 = (f32[24,1,8,4,256]{4,3,2,1,0:T(4,128)}, f32[24,1,8,4,256]{4,3,2,1,0:T(4,128)S(1)}, u32[]{:S(2)}) copy-start(f32[24,1,8,4,256]{4,3,2,1,0:T(4,128)S(1)} %get-tuple-element.67) | copy-start | bytes 2359300
  10.2 2.4 %copy-start.7 = (f32[24,1,8,4,256]{4,3,2,1,0:T(4,128)S(1)}, f32[24,1,8,4,256]{4,3,2,1,0:T(4,128)}, u32[]{:S(2)}) copy-start(f32[24,1,8,4,256]{4,3,2,1,0:T(4,128)} %get-tuple-element.69) | copy-start | bytes 2359300
  10.2 2.4 %copy-start.9 = (f32[24,1,8,4,256]{4,3,2,1,0:T(4,128)S(1)}, f32[24,1,8,4,256]{4,3,2,1,0:T(4,128)}, u32[]{:S(2)}) copy-start(f32[24,1,8,4,256]{4,3,2,1,0:T(4,128)} %get-tuple-element.68) | copy-start | bytes 2359300
  10.2 4.9 %copy-start.3 = (s32[4,2048]{1,0:T(4,128)S(1)}, s32[4,2048]{1,0:T(4,128)}, u32[]{:S(2)}) copy-start(s32[4,2048]{1,0:T(4,128)} %obs_index.1) | copy-start | bytes 98308
  10.2 4.9 %copy-start.4 = (f32[4,2048]{1,0:T(4,128)S(1)}, f32[4,2048]{1,0:T(4,128)}, u32[]{:S(2)}) copy-start(f32[4,2048]{1,0:T(4,128)} %observed.1) | copy-start | bytes 98308
  10.2 4.9 %copy-start.5 = (f32[4,2048]{1,0:T(4,128)S(1)}, f32[4,2048]{1,0:T(4,128)}, u32[]{:S(2)}) copy-start(f32[4,2048]{1,0:T(4,128)} %obs_var.1) | copy-start | bytes 98308
  10.2 4.9 %copy-start.6 = (s32[4]{0:T(128)S(1)}, s32[4]{0:T(128)}, u32[]{:S(2)}) copy-start(s32[4]{0:T(128)} %refs_1_.1) | copy-start | bytes 52
  21.1 31.9 %collective-permute-start.7 = (f32[8,4,24,256]{3,2,1,0:T(8,128)S(1)}, f32[8,4,24,256]{3,2,1,0:T(8,128)S(1)}, u32[]{:S(2)}, u32[]{:S(2)}) collective-permute-start(f32[8,4,24,256]{3,2,1,0:T(8,128)S(1)} %add_add_fusion.refs_4_), channel_id=1, source_target_pairs={{0,16},{8,24},{16,0},{24,8},{1,17},{9,25},{17,1},{25,9},{2,18},{10... | collective-permute-start | bytes 2359304 | tf_op jit(solution)/shard_map/ppermute | solution.py:510
  22.7 30.3 %collective-permute-start.6 = (f32[8,4,24,256]{3,2,1,0:T(8,128)S(1)}, f32[8,4,24,256]{3,2,1,0:T(8,128)S(1)}, u32[]{:S(2)}, u32[]{:S(2)}) collective-permute-start(f32[8,4,24,256]{3,2,1,0:T(8,128)S(1)} %add_add_fusion.refs_4_), channel_id=1, source_target_pairs={{0,8},{8,0},{16,24},{24,16},{1,9},{9,1},{17,25},{25,17},{2,10},{10... | collective-permute-start | bytes 2359304 | tf_op jit(solution)/shard_map/ppermute | solution.py:510
  22.7 9.4 %collective-permute-start.2 = (f32[4,48,256]{2,1,0:T(8,128)S(1)}, f32[4,48,256]{2,1,0:T(8,128)S(1)}, u32[]{:S(2)}, u32[]{:S(2)}) collective-permute-start(f32[4,48,256]{2,1,0:T(8,128)S(1)} %get-tuple-element.43), channel_id=1, source_target_pairs={{0,1},{1,2},{2,3},{3,4},{4,5},{5,6},{6,7},{8,9},{9,10},{10,11},{11... | collective-permute-start | bytes 589832 | tf_op jit(solution)/shard_map/ppermute | solution.py:534
  27.3 9.6 %collective-permute-start.3 = (f32[4,48,256]{2,1,0:T(8,128)S(1)}, f32[4,48,256]{2,1,0:T(8,128)S(1)}, u32[]{:S(2)}, u32[]{:S(2)}) collective-permute-start(f32[4,48,256]{2,1,0:T(8,128)S(1)} %get-tuple-element.44), channel_id=1, source_target_pairs={{1,0},{2,1},{3,2},{4,3},{5,4},{6,5},{7,6},{9,8},{10,9},{11,10},{12... | collective-permute-start | bytes 589832 | tf_op jit(solution)/shard_map/ppermute | solution.py:534
  39.1 8.3 %collective-permute-start.4 = (f32[4,48,256]{2,1,0:T(8,128)S(1)}, f32[4,48,256]{2,1,0:T(8,128)S(1)}, u32[]{:S(2)}, u32[]{:S(2)}) collective-permute-start(f32[4,48,256]{2,1,0:T(8,128)S(1)} %get-tuple-element.49), channel_id=1, source_target_pairs={{0,1},{1,2},{2,3},{3,4},{4,5},{5,6},{6,7},{8,9},{9,10},{10,11},{11... | collective-permute-start | bytes 589832 | tf_op jit(solution)/shard_map/ppermute | solution.py:534
  43.7 9.3 %collective-permute-start.5 = (f32[4,48,256]{2,1,0:T(8,128)S(1)}, f32[4,48,256]{2,1,0:T(8,128)S(1)}, u32[]{:S(2)}, u32[]{:S(2)}) collective-permute-start(f32[4,48,256]{2,1,0:T(8,128)S(1)} %get-tuple-element.50), channel_id=1, source_target_pairs={{1,0},{2,1},{3,2},{4,3},{5,4},{6,5},{7,6},{9,8},{10,9},{11,10},{12... | collective-permute-start | bytes 589832 | tf_op jit(solution)/shard_map/ppermute | solution.py:534
  55.0 10.3 %collective-permute-start.9 = (f32[4,4,24,256]{3,2,1,0:T(8,128)S(1)}, f32[4,4,24,256]{3,2,1,0:T(8,128)S(1)}, u32[]{:S(2)}, u32[]{:S(2)}) collective-permute-start(f32[4,4,24,256]{3,2,1,0:T(8,128)S(1)} %get-tuple-element.62.refs_16_), channel_id=1, source_target_pairs={{0,16},{8,24},{16,0},{24,8},{1,17},{9,25},{17,1},{25,9},{2,18},{10... | collective-permute-start | bytes 1179656 | tf_op jit(solution)/shard_map/ppermute | solution.py:510
  65.4 21.7 %collective-permute-start.14 = (f32[8,4,24,256]{3,2,1,0:T(8,128)S(1)}, f32[8,4,24,256]{3,2,1,0:T(8,128)S(1)}, u32[]{:S(2)}, u32[]{:S(2)}) collective-permute-start(f32[8,4,24,256]{3,2,1,0:T(8,128)S(1)} %get-tuple-element.55.refs_8_), channel_id=1, source_target_pairs={{0,16},{8,24},{16,0},{24,8},{1,17},{9,25},{17,1},{25,9},{2,18},{10... | collective-permute-start | bytes 2359304 | tf_op jit(solution)/shard_map/ppermute | solution.py:510
  65.9 1.7 %collective-permute-start.8 = (f32[4,4,24,256]{3,2,1,0:T(8,128)S(1)}, f32[4,4,24,256]{3,2,1,0:T(8,128)S(1)}, u32[]{:S(2)}, u32[]{:S(2)}) collective-permute-start(f32[4,4,24,256]{3,2,1,0:T(8,128)S(1)} %get-tuple-element.63.refs_4_.refs_12_), channel_id=1, source_target_pairs={{0,8},{8,0},{16,24},{24,16},{1,9},{9,1},{17,25},{25,17},{2,10},{10... | collective-permute-start | bytes 1179656 | tf_op jit(solution)/shard_map/ppermute | solution.py:510
  65.9 2.3 %collective-permute-start.10 = (f32[4,4,24,256]{3,2,1,0:T(8,128)S(1)}, f32[4,4,24,256]{3,2,1,0:T(8,128)S(1)}, u32[]{:S(2)}, u32[]{:S(2)}) collective-permute-start(f32[4,4,24,256]{3,2,1,0:T(8,128)S(1)} %collective-permute-done.9.refs_6_.refs_14_), channel_id=1, source_target_pairs={{0,8},{8,0},{16,24},{24,16},{1,9},{9,1},{17,25},{25,17},{2,10},{10... | collective-permute-start | bytes 1179656 | tf_op jit(solution)/shard_map/ppermute | solution.py:510
  69.0 4.6 %collective-permute-start.11 = (f32[96,128]{1,0:T(8,128)S(1)}, f32[96,128]{1,0:T(8,128)S(1)}, u32[]{:S(2)}, u32[]{:S(2)}) collective-permute-start(f32[96,128]{1,0:T(8,128)S(1)} %gram.1), channel_id=1, source_target_pairs={{0,1},{1,0},{2,3},{3,2},{4,5},{5,4},{6,7},{7,6},{8,9},{9,8},{10,11... | collective-permute-start | bytes 147464 | tf_op jit(solution)/shard_map/ppermute | solution.py:510
  73.6 7.9 %collective-permute-start.12 = (f32[96,128]{1,0:T(8,128)S(1)}, f32[96,128]{1,0:T(8,128)S(1)}, u32[]{:S(2)}, u32[]{:S(2)}) collective-permute-start(f32[96,128]{1,0:T(8,128)S(1)} %add.20), channel_id=1, source_target_pairs={{0,2},{1,3},{2,0},{3,1},{4,6},{5,7},{6,4},{7,5},{8,10},{9,11},{10,... | collective-permute-start | bytes 147464 | tf_op jit(solution)/shard_map/ppermute | solution.py:510
  81.5 5.6 %collective-permute-start.13 = (f32[96,128]{1,0:T(8,128)S(1)}, f32[96,128]{1,0:T(8,128)S(1)}, u32[]{:S(2)}, u32[]{:S(2)}) collective-permute-start(f32[96,128]{1,0:T(8,128)S(1)} %add.21), channel_id=1, source_target_pairs={{0,4},{1,5},{2,6},{3,7},{4,0},{5,1},{6,2},{7,3},{8,12},{9,13},{10,... | collective-permute-start | bytes 147464 | tf_op jit(solution)/shard_map/ppermute | solution.py:510
  87.1 4.7 %collective-permute-start.15 = (f32[96,128]{1,0:T(8,128)S(1)}, f32[96,128]{1,0:T(8,128)S(1)}, u32[]{:S(2)}, u32[]{:S(2)}) collective-permute-start(f32[96,128]{1,0:T(8,128)S(1)} %add.22), channel_id=1, source_target_pairs={{0,16},{8,24},{16,0},{24,8},{1,17},{9,25},{17,1},{25,9},{2,18},{10... | collective-permute-start | bytes 147464 | tf_op jit(solution)/shard_map/ppermute | solution.py:510
  91.8 29.3 %collective-permute-start.18 = (f32[8,4,24,256]{3,2,1,0:T(8,128)S(1)}, f32[8,4,24,256]{3,2,1,0:T(8,128)S(1)}, u32[]{:S(2)}, u32[]{:S(2)}) collective-permute-start(f32[8,4,24,256]{3,2,1,0:T(8,128)S(1)} %get-tuple-element.58.refs_0_), channel_id=1, source_target_pairs={{0,16},{8,24},{16,0},{24,8},{1,17},{9,25},{17,1},{25,9},{2,18},{10... | collective-permute-start | bytes 2359304 | tf_op jit(solution)/shard_map/ppermute | solution.py:510
  93.4 28.3 %collective-permute-start.21 = (f32[8,4,24,256]{3,2,1,0:T(8,128)S(1)}, f32[8,4,24,256]{3,2,1,0:T(8,128)S(1)}, u32[]{:S(2)}, u32[]{:S(2)}) collective-permute-start(f32[8,4,24,256]{3,2,1,0:T(8,128)S(1)} %get-tuple-element.55.refs_8_), channel_id=1, source_target_pairs={{0,8},{8,0},{16,24},{24,16},{1,9},{9,1},{17,25},{25,17},{2,10},{10... | collective-permute-start | bytes 2359304 | tf_op jit(solution)/shard_map/ppermute | solution.py:510
  93.4 28.7 %collective-permute-start.20 = (f32[8,4,24,256]{3,2,1,0:T(8,128)S(1)}, f32[8,4,24,256]{3,2,1,0:T(8,128)S(1)}, u32[]{:S(2)}, u32[]{:S(2)}) collective-permute-start(f32[8,4,24,256]{3,2,1,0:T(8,128)S(1)} %collective-permute-done.7.refs_13_.refs_6_), channel_id=1, source_target_pairs={{0,8},{8,0},{16,24},{24,16},{1,9},{9,1},{17,25},{25,17},{2,10},{10... | collective-permute-start | bytes 2359304 | tf_op jit(solution)/shard_map/ppermute | solution.py:510
  93.9 27.6 %collective-permute-start.24 = (f32[4,4,24,256]{3,2,1,0:T(8,128)S(1)}, f32[4,4,24,256]{3,2,1,0:T(8,128)S(1)}, u32[]{:S(2)}, u32[]{:S(2)}) collective-permute-start(f32[4,4,24,256]{3,2,1,0:T(8,128)S(1)} %get-tuple-element.63.refs_4_.refs_12_), channel_id=1, source_target_pairs={{0,16},{8,24},{16,0},{24,8},{1,17},{9,25},{17,1},{25,9},{2,18},{10... | collective-permute-start | bytes 1179656 | tf_op jit(solution)/shard_map/ppermute | solution.py:510
  94.4 2.5 %collective-permute-start.16 = (f32[96,128]{1,0:T(8,128)S(1)}, f32[96,128]{1,0:T(8,128)S(1)}, u32[]{:S(2)}, u32[]{:S(2)}) collective-permute-start(f32[96,128]{1,0:T(8,128)S(1)} %add.23.mine), channel_id=1, source_target_pairs={{0,8},{8,0},{16,24},{24,16},{1,9},{9,1},{17,25},{25,17},{2,10},{10... | collective-permute-start | bytes 147464 | tf_op jit(solution)/shard_map/ppermute | solution.py:510
  96.9 28.8 %collective-permute-start.17 = (f32[8,4,24,256]{3,2,1,0:T(8,128)S(1)}, f32[8,4,24,256]{3,2,1,0:T(8,128)S(1)}, u32[]{:S(2)}, u32[]{:S(2)}) collective-permute-start(f32[8,4,24,256]{3,2,1,0:T(8,128)S(1)} %get-tuple-element.58.refs_0_), channel_id=1, source_target_pairs={{0,8},{8,0},{16,24},{24,16},{1,9},{9,1},{17,25},{25,17},{2,10},{10... | collective-permute-start | bytes 2359304 | tf_op jit(solution)/shard_map/ppermute | solution.py:510
  121.1 4.6 %collective-permute-start.22 = (f32[8,4,24,256]{3,2,1,0:T(8,128)S(1)}, f32[8,4,24,256]{3,2,1,0:T(8,128)S(1)}, u32[]{:S(2)}, u32[]{:S(2)}) collective-permute-start(f32[8,4,24,256]{3,2,1,0:T(8,128)S(1)} %collective-permute-done.14.refs_10_), channel_id=1, source_target_pairs={{0,8},{8,0},{16,24},{24,16},{1,9},{9,1},{17,25},{25,17},{2,10},{10... | collective-permute-start | bytes 2359304 | tf_op jit(solution)/shard_map/ppermute | solution.py:510
  121.6 4.2 %collective-permute-start.19 = (f32[8,4,24,256]{3,2,1,0:T(8,128)S(1)}, f32[8,4,24,256]{3,2,1,0:T(8,128)S(1)}, u32[]{:S(2)}, u32[]{:S(2)}) collective-permute-start(f32[8,4,24,256]{3,2,1,0:T(8,128)S(1)} %collective-permute-done.18.refs_2_), channel_id=1, source_target_pairs={{0,8},{8,0},{16,24},{24,16},{1,9},{9,1},{17,25},{25,17},{2,10},{10... | collective-permute-start | bytes 2359304 | tf_op jit(solution)/shard_map/ppermute | solution.py:510
  121.7 3.5 %collective-permute-start.23 = (f32[4,4,24,256]{3,2,1,0:T(8,128)S(1)}, f32[4,4,24,256]{3,2,1,0:T(8,128)S(1)}, u32[]{:S(2)}, u32[]{:S(2)}) collective-permute-start(f32[4,4,24,256]{3,2,1,0:T(8,128)S(1)} %get-tuple-element.62.refs_16_), channel_id=1, source_target_pairs={{0,8},{8,0},{16,24},{24,16},{1,9},{9,1},{17,25},{25,17},{2,10},{10... | collective-permute-start | bytes 1179656 | tf_op jit(solution)/shard_map/ppermute | solution.py:510
  122.1 3.6 %collective-permute-start.25 = (f32[4,4,24,256]{3,2,1,0:T(8,128)S(1)}, f32[4,4,24,256]{3,2,1,0:T(8,128)S(1)}, u32[]{:S(2)}, u32[]{:S(2)}) collective-permute-start(f32[4,4,24,256]{3,2,1,0:T(8,128)S(1)} %collective-permute-done.24.refs_18_), channel_id=1, source_target_pairs={{0,8},{8,0},{16,24},{24,16},{1,9},{9,1},{17,25},{25,17},{2,10},{10... | collective-permute-start | bytes 1179656 | tf_op jit(solution)/shard_map/ppermute | solution.py:510

commit v7 on v5

--- a/solution.py
+++ b/solution.py
@@ -110,106 +110,137 @@
             out[z, 2 * members :, :] = jnp.broadcast_to(spread, (8, spread.shape[1]))
 
 
-def first_substep(
-    a, r, c, i, low, high, diffusivity, binding, source, out_a, out_r, out_c, out_i
-):
+def step_planes(planes, a, r, c, i, outside, diffusivity, binding, source, out_a, outs, keep):
     nx, nz, _, _ = a.shape
-    for x in range(nx):
+    for x in planes:
         for z in range(nz):
             row = pl.ds(z, 1)
-            back, out_r[x, z], out_c[x, z], out_i[x, z] = react(
-                a[x, z], r[x, z], c[x, z], i[x, z], binding[x, row, :]
-            )
-            around = beside(lambda x, z: a[x, z], x, z, nx, nz, low(z), high(z))
+            back, *others = react(a[x, z], r[x, z], c[x, z], i[x, z], binding[x, row, :])
+            around = beside(lambda x, z: a[x, z], x, z, nx, nz, *outside(x, z))
             out_a[x, z] = (
                 spread_free(a[x, z], around, None, diffusivity[x, row, :])
                 + back
                 + source[x, row, :]
             )
+            if x in keep:
+                for out, value in zip(outs, others):
+                    out[x, z] = value
+
+
+def before_last(a, low, high):
+    nx, _, members, _ = a.shape
+
+    def outside(x, z):
+        return (
+            low[z, :members, :] if x == 0 else None,
+            high[z, :members, :] if x == nx - 1 else None,
+        )
+
+    return outside
+
+
+def after_first(a, low, high, low_first, high_first):
+    nx, _, members, _ = a.shape
+
+    def completed(halo, origin, x, z):
+        later = halo[z, members : 2 * members, :]
+        return later + origin[z, 2 * members : 2 * members + 1, :] * a[x, z]
+
+    def outside(x, z):
+        return (
+            completed(low, low_first, x, z) if x == 0 else None,
+            completed(high, high_first, x, z) if x == nx - 1 else None,
+        )
+
+    return outside
+
+
+def next_edges_kernel(
+    a, r, c, i, low, high, low_first, high_first, diffusivity, binding, source, *refs
+):
+    first, last, *kept = refs
+    middle, later = kept[:4], kept[4:]
+    nx, nz, members, _ = a.shape
+    coefficients = (diffusivity, binding, source)
+
+    def near(depth):
+        return [x for x in range(nx) if min(x, nx - 1 - x) < depth]
+
+    step_planes(
+        near(3), a, r, c, i, before_last(a, low, high), *coefficients, middle[0], middle[1:], near(2)
+    )
+    step_planes(
+        near(2),
+        *middle,
+        after_first(a, low, high, low_first, high_first),
+        *coefficients,
+        later[0],
+        later[1:],
+        near(1),
+    )
+    free, receptor, complexed = later[:3]
+    for x, out in ((0, first), (nx - 1, last)):
+        for z in range(nz):
+            row = pl.ds(z, 1)
+            flux = binding[x, row, :] * free[x, z] * receptor[x, z]
+            rest = unbind_rate * complexed[x, z] - flux + source[x, row, :]
+            out[z, :members, :] = free[x, z]
+            out[z, members:, :] = edge_free(
+                lambda x, z: free[x, z], rest, x, nz, nx, z, diffusivity[x, row, :]
+            )
 
 
 def two_substeps_kernel(
-    a, r, c, i, low, high, low_first, high_first, diffusivity, binding, source, *refs, lean
+    a, r, c, i, low, high, low_first, high_first, diffusivity, binding, source, *refs
 ):
-    out_a, out_r, out_c, out_i, first, last, middle = refs
-    nx, nz, members, _ = a.shape
-    first_substep(
+    outs, middle = refs[:4], refs[4:]
+    everywhere = range(a.shape[0])
+    coefficients = (diffusivity, binding, source)
+    step_planes(
+        everywhere,
         a,
         r,
         c,
         i,
-        lambda z: low[z, :members, :],
-        lambda z: high[z, :members, :],
-        diffusivity,
-        binding,
-        source,
-        middle,
-        out_r,
-        out_c,
-        out_i,
-    )
-
-    def outside(halo, origin, x, z):
-        later = halo[z, members : 2 * members, :]
-        return later + origin[z, 2 * members : 2 * members + 1, :] * a[x, z]
-
-    for x in range(nx):
-        for z in range(nz):
-            row = pl.ds(z, 1)
-            back, out_r[x, z], out_c[x, z], out_i[x, z] = react(
-                middle[x, z], out_r[x, z], out_c[x, z], out_i[x, z], binding[x, row, :]
-            )
-            around = beside(
-                lambda x, z: middle[x, z],
-                x,
-                z,
-                nx,
-                nz,
-                outside(low, low_first, x, z) if x == 0 else None,
-                outside(high, high_first, x, z) if x == nx - 1 else None,
-            )
-            out_a[x, z] = (
-                spread_free(middle[x, z], around, None, diffusivity[x, row, :])
-                + back
-                + source[x, row, :]
-            )
-    for x, out in ((0, first), (nx - 1, last)):
-        for z in range(nz):
-            row = pl.ds(z, 1)
-            free = out_a[x, z]
-            out[z, :members, :] = free
-            if lean:
-                continue
-            flux = binding[x, row, :] * free * out_r[x, z]
-            rest = unbind_rate * out_c[x, z] - flux + source[x, row, :]
-            out[z, members:, :] = edge_free(
-                lambda x, z: out_a[x, z], rest, x, nz, nx, z, diffusivity[x, row, :]
-            )
+        before_last(a, low, high),
+        *coefficients,
+        middle[0],
+        middle[1:],
+        everywhere,
+    )
+    step_planes(
+        everywhere,
+        *middle,
+        after_first(a, low, high, low_first, high_first),
+        *coefficients,
+        outs[0],
+        outs[1:],
+        everywhere,
+    )
 
 
 def last_but_one_kernel(
     place, a, r, c, i, low, high, diffusivity, binding, source, *refs, halves
 ):
-    *tracers, out_i, out_a, out_add, first, last, mid_r, mid_c, mid_i = refs
+    *tracers, out_i, out_a, out_add, mid_r, mid_c, mid_i = refs
     nx, nz, _, _ = a.shape
-    first_substep(
+    step_planes(
+        range(nx),
         a,
         r,
         c,
         i,
-        lambda z: low[z],
-        lambda z: high[z],
+        before_last(a, low, high),
         diffusivity,
         binding,
         source,
         out_a,
-        mid_r,
-        mid_c,
-        mid_i,
+        (mid_r, mid_c, mid_i),
+        range(nx),
     )
     span = nx // halves
     for part, tracer in enumerate(tracers):
-        begin = jnp.bitwise_xor(part, lax.shift_right_logical(place[2], 1)) * span
+        begin = half_begin(place, part, span)
         for j in range(span):
             x = j if halves == 1 else begin + j
             for z in range(nz):
@@ -220,19 +251,23 @@
                 tracer[j, z] = complexed + internal
                 out_i[x, z] = internal
                 out_add[x, z] = back + source[x, row, :]
-    for x, out in ((0, first), (nx - 1, last)):
-        for z in range(nz):
-            out[z] = out_a[x, z]
-
-
-def last_free_kernel(a, add, low, high, diffusivity, out_a):
+
+
+def last_free_kernel(
+    before, a, add, low, high, low_first, high_first, diffusivity, out_a
+):
     nx, nz, _, _ = a.shape
+    outside = after_first(before, low, high, low_first, high_first)
     for x in range(nx):
         for z in range(nz):
-            around = beside(lambda x, z: a[x, z], x, z, nx, nz, low[z], high[z])
+            around = beside(lambda x, z: a[x, z], x, z, nx, nz, *outside(x, z))
             out_a[x, z] = (
                 spread_free(a[x, z], around, None, diffusivity[x, pl.ds(z, 1), :]) + add[x, z]
             )
+
+
+def half_begin(place, part, span):
+    return jnp.bitwise_xor(part, lax.shift_right_logical(place[2], 1)) * span
 
 
 def forecast_call(kernel, name, inputs, outputs, cells, scratch=(), ready=(), scalars=()):
@@ -416,8 +451,8 @@
     return wide_dot(wide_left(total), wide_right(mixing))
 
 
-def unpack(place, shares, groups, ordered):
-    members = ordered.shape[1]
+def early_kernel(place, mine, other, total, last, ordered):
+    members = mine.shape[0]
     row = lax.broadcasted_iota(jnp.int32, (members, LANES), 0)
     column = lax.broadcasted_iota(jnp.int32, (members, LANES), 1)
     inside = column < members
@@ -425,8 +460,8 @@
     def pick(where, x):
         return jnp.sum(jnp.where(where, x, 0.0), axis=1, keepdims=True)
 
-    for half, group in zip((place[0], 1 - place[0]), groups(place[2])):
-        packed = sum(shares[k] for k in group)
+    for half, shared in ((place[0], mine), (1 - place[0], other)):
+        packed = shared[...]
         above = jnp.where(inside & (column > row), packed, 0.0)
         below = jnp.where(inside & (column < row), packed, 0.0)
         middle = jnp.where(column == row, packed, 0.0)
@@ -435,13 +470,7 @@
         middle = jnp.where(column == row, pick(column == members, packed), 0.0)
         side = jnp.where(column == members, pick(column == members + 2, packed), 0.0)
         ordered[2 * half + 1] = below + turned(below) + (middle + side)
-
-
-def early_kernel(place, shares, total, last, ordered, *, groups):
-    unpack(place, shares, groups, ordered)
-    batches, members, _ = ordered.shape
-    row = lax.broadcasted_iota(jnp.int32, (members, LANES), 0)
-    column = lax.broadcasted_iota(jnp.int32, (members, LANES), 1)
+    batches = ordered.shape[0]
     product = jnp.where(row == column, 1.0, 0.0)
     for batch in range(batches - 1):
         product = batch_transform(ordered[batch], product, members)
@@ -464,13 +493,12 @@
     out[...] = work[pl.ds(pl.multiple_of(offsets(place[2], 0), 8), rows), :]
 
 
-def transform_call(kernel, name, out_shape, scratch, inputs):
-    many = isinstance(out_shape, list)
+def transform_call(kernel, name, outputs, scratch, inputs):
     return pl.pallas_call(
         kernel,
-        out_shape=out_shape,
+        out_shape=[jax.ShapeDtypeStruct(shape, f32) for shape in outputs],
         in_specs=[SMEM] + [VMEM] * (len(inputs) - 1),
-        out_specs=[VMEM] * len(out_shape) if many else VMEM,
+        out_specs=[VMEM] * len(outputs),
         scratch_shapes=[pltpu.VMEM(shape, f32) for shape in scratch],
         compiler_params=pltpu.CompilerParams(vmem_limit_bytes=SCOPED),
         cost_estimate=pl.CostEstimate(
@@ -517,10 +545,6 @@
                 out[:, 3, 0, z, :] = inside
 
 
-def half_begin(place, part, span):
-    return jnp.bitwise_xor(part, lax.shift_right_logical(place[2], 1)) * span
-
-
 def mix(place, weights, sources, blocks, halves, shape):
     rows, species, nx, nz, ny = shape
     span = nx // halves
@@ -578,10 +602,6 @@
         def offsets(position, j):
             return jnp.bitwise_xor(position, j) * rows
 
-        def groups(position):
-            flip = functools.partial(jnp.bitwise_xor, position)
-            return (position, flip(2)), (flip(1), flip(3))
-
         def collect(x, sent=None):
             return [x, swap(x, "member", 1), swap(x if sent is None else sent, "member", 2)]
 
@@ -593,10 +613,7 @@
         def offsets(position, j):
             return 0
 
-        def groups(position):
-            return (0,), (1,)
-
-        def collect(x):
+        def collect(x, sent=None):
             return [lax.all_gather(x, "member", axis=2, tiled=True)]
 
         def complete(held, *after):
@@ -608,7 +625,7 @@
     def tie(x, *after):
         return lax.optimization_barrier((x, *after))[0]
 
-    whole, plane = (nx, nz, rows, ny), (nz, rows, ny)
+    whole = (nx, nz, rows, ny)
     coefficients = (diffusivity, binding, source)
     cells = nx * nz * rows * ny
     ends = [
@@ -624,76 +641,70 @@
     )
     fields = [jnp.transpose(ensemble[:, k], (1, 2, 0, 3)) for k in range(species)]
     conserved = fields[1] + fields[2] + fields[3]
+    around = origin = halos(*edges)
+    for step in range(SUBSTEPS // 2 - 1):
+        inputs = [*fields, *around, *origin, *coefficients]
+        if step == 1:
+            conserved = collect(tie(conserved, fields[0]))
+        around = halos(
+            *forecast_call(
+                next_edges_kernel,
+                "next_edges",
+                inputs,
+                [(nz, 2 * rows, ny)] * 2,
+                cells,
+                scratch=[whole] * 8,
+            )
+        )
+        fields = forecast_call(
+            two_substeps_kernel, "two_substeps", inputs, [whole] * 4, 2 * cells, scratch=[whole] * 4
+        )
     omega, eta = voxel_weights(
         place, owner, obs_index, observed, obs_var, batches // 2, nx * nz, ny
     )
-    around = origin = halos(*edges)
-    steps = SUBSTEPS // 2 - 1
-    for step in range(steps):
-        lean = step == steps - 1
-        *fields, first, last = forecast_call(
-            functools.partial(two_substeps_kernel, lean=lean),
-            "two_substeps",
-            [*fields, *around, *origin, *coefficients],
-            [whole] * 4 + [plane if lean else (nz, 2 * rows, ny)] * 2,
-            2 * cells,
-            scratch=[whole],
-            ready=(omega, eta) if step == 0 else (),
-        )
-        around = halos(first, last)
-        if step == 0:
-            conserved = collect(tie(conserved, fields[0]))
-    *tracers, internal, free, add, first, last = forecast_call(
+    *tracers, internal, middle, add = forecast_call(
         functools.partial(last_but_one_kernel, halves=halves),
         "last_but_one",
         [*fields, *around, *coefficients],
-        [(nx // halves, nz, rows, ny)] * halves + [whole] * 3 + [plane] * 2,
+        [(nx // halves, nz, rows, ny)] * halves + [whole] * 3,
         2 * cells,
         scratch=[whole] * 3,
-        ready=conserved[1:],
+        ready=[*conserved[1:], omega, eta],
         scalars=[place],
     )
-    if halves == 2:
-        near, far = tracers
-        near = complete(collect(near, far))
-    else:
-        near = collect(tracers[0])
     (free,) = forecast_call(
         last_free_kernel,
         "last_free",
-        [free, add, *halos(first, last), diffusivity],
+        [fields[0], middle, add, *around, *origin, diffusivity],
         [whole],
         cells,
     )
-    conserved = complete(conserved, across(near), free)
-    internal = collect(tie(internal, across(near), free))
-    half = total_over(gram(place, owner, omega, eta, near, offsets, halves, [free]), "space")
+    near = collect(*tracers)
+    conserved = complete(conserved, tracers[0])
+    near = complete(near)
+    far = collect(tracers[1], tie(tracers[0], across(near))) if halves == 2 else []
+    half = gram(place, owner, omega, eta, near, offsets, halves, [*conserved[3:], *far[1:2]])
     if halves == 2:
-        half = tie(half, across(internal))
-        shares = lax.all_to_all(
-            jnp.broadcast_to(half, (devices, *half.shape)), "member", 0, 0
-        )
-        far = collect(tie(far, shares), tie(tracers[0], shares))
-        free = collect(tie(free, shares))
-    else:
-        free = collect(free)
-        shares = jnp.stack([half, swap(half, "member", 1)])
+        half = tie(half + swap(half, "member", 2), across(far))
+        far = complete(far, half)
+    internal = collect(internal, tie(internal, half))
+    free = collect(free, tie(free, half))
+    half = total_over(half, "space")
+    other = swap(half, "member", 1)
     internal = complete(internal, half)
-    square = jax.ShapeDtypeStruct((members, LANES), f32)
+    square = (members, LANES)
     total, extended = transform_call(
-        functools.partial(early_kernel, groups=groups),
+        early_kernel,
         "transforms_early",
         [square, square],
         [(batches, members, LANES)],
-        [place, shares],
-    )
-    if halves == 2:
-        far = complete(far, total)
+        [place, half, other],
+    )
     free = complete(free, total)
-    weights = transform_call(
+    (weights,) = transform_call(
         functools.partial(late_kernel, offsets=offsets, blocks=blocks, rows=rows),
         "transforms_late",
-        jax.ShapeDtypeStruct((LANES, LANES) if blocks == 1 else (rows, LANES), f32),
+        [(LANES, LANES) if blocks == 1 else (rows, LANES)],
         [(LANES, LANES)],
         [place, total, extended],
     )

time: 132 us -> 129 us (0.977)
  blocking collectives: 7.7 us -> 0 us
  local copies, waits for them, and re-layouts: 8.44 us -> 12 us
  starting transfers between devices: 38.8 us -> 35.3 us
  waiting for transfers between devices: 35.2 us -> 38.4 us
  Pallas kernels: 38.9 us -> 40.8 us
    ppermute x18 -> x20, waiting for transfers between devices: 15.7 us -> 26.3 us  [swap(): return lax.ppermute(x, axis, [(k, k ^ bit) for k in range(count)])]
    ppermute x4 -> x3, waiting for transfers between devices: 14.2 us -> 4.83 us  [halos(): lax.ppermute(first, 'space', backward)]
    all_to_all x1 -> x0, blocking collectives: 7.7 us -> none  [local(): lax.all_to_all(jnp.broadcast_to(half, (devices, *half.shape)), 'member',...]
    unnamed x22 -> x36, local copies, waits for them, and re-layouts: 0.05 us -> 7.02 us
    ppermute x4 -> x3, starting transfers between devices: 18.6 us -> 13.8 us  [halos(): lax.ppermute(last, 'space', forward)]
    transpose x2, local copies, waits for them, and re-layouts: 4.64 us -> 2.04 us  [local(): jnp.transpose(ensemble[:, k], (1, 2, 0, 3))]
    ppermute x18 -> x20, starting transfers between devices: 15 us -> 17.4 us  [swap(): return lax.ppermute(x, axis, [(k, k ^ bit) for k in range(count)])]
    pallas_call x5 -> x7, Pallas kernels: 5.69 us -> 7.83 us  [forecast_call(): pl.pallas_call(body, out_shape=[jax.ShapeDtypeStruct(shape, f32) for shap...]
  transfers between devices with their start and end apart: 26 -> 26, of which waited for: 12 -> 10; matrix products, arithmetic and copies ran while one was open for 7% -> 4% of each run, Pallas kernels for 22% -> 25%
where the time goes in v7:
time: 129 us
  Pallas kernels  40.8 us (32%)
  waiting for transfers between devices  38.4 us (30%)
  starting transfers between devices  35.3 us (27%)
  local copies, waits for them, and re-layouts  12 us (9%)
  other arithmetic  1.78 us (1%)
    ppermute x20, waiting for transfers between devices, swap(): return lax.ppermute(x, axis, [(k, k ^ bit) for k in range(count)])  26.3 us
    pallas_call x2, Pallas kernels, transform_call(): pl.pallas_call(kernel, out_shape=[jax.ShapeDtypeStruct(shape, f32) for sh...  25.1 us
    ppermute x20, starting transfers between devices, swap(): return lax.ppermute(x, axis, [(k, k ^ bit) for k in range(count)])  17.4 us
    ppermute x3, starting transfers between devices, halos(): lax.ppermute(last, 'space', forward)  13.8 us
    pallas_call x7, Pallas kernels, forecast_call(): pl.pallas_call(body, out_shape=[jax.ShapeDtypeStruct(shape, f32) for shap...  7.83 us
    ppermute x3, waiting for transfers between devices, halos(): lax.ppermute(last, 'space', forward)  7.25 us
    unnamed x36, local copies, waits for them, and re-layouts  7.02 us
    pallas_call x1, Pallas kernels, mix(): pl.pallas_call(functools.partial(mix_kernel, blocks=blocks, halves=halves...  5.81 us
  transfers between devices with their start and end apart: 26, of which 10 were waited for; matrix products, arithmetic and copies ran while one was open for 4% of the time, Pallas kernels for 25%

profile of v7, /device:TPU:0, one launch (start us, length us, event | category | flops | bytes accessed | tf_op | source)
XLA Modules:
  0.0 128.7 jit_solution(6704342423536191370)
XLA Ops:
  0.0 1.6 %fusion = (f32[24,3,2,4,256]{4,3,2,1,0:T(4,128)S(1)}, f32[24,3,2,4,256]{4,3,2,1,0:T(4,128)S(1)}) fusion(f32[24,4,8,4,256]{4,3,2,1,0:T(4,128)} %param.8), kind=kLoop, calls=%fused_computation.8 | loop fusion | bytes 2359296 | tf_op jit(solution)/shard_map/slice | solution.py:632
  1.6 0.4 copy_bitcast_fusion.4
  2.0 0.2 first_edges.1
  2.2 4.9 %collective-permute-start = (f32[4,56,256]{2,1,0:T(8,128)S(1)}, f32[4,56,256]{2,1,0:T(8,128)S(1)}, u32[]{:S(2)}, u32[]{:S(2)}) collective-permute-start(f32[4,56,256]{2,1,0:T(8,128)S(1)} %get-tuple-element.39), channel_id=1, source_target_pairs={{0,1},{1,2},{2,3},{3,4},{4,5},{5,6},{6,7},{8,9},{9,10},{10,11},{11... | collective-permute-start | bytes 688136 | tf_op jit(solution)/shard_map/ppermute | solution.py:597
  7.1 1.3 %collective-permute-start.1 = (f32[4,56,256]{2,1,0:T(8,128)S(1)}, f32[4,56,256]{2,1,0:T(8,128)S(1)}, u32[]{:S(2)}, u32[]{:S(2)}) collective-permute-start(f32[4,56,256]{2,1,0:T(8,128)S(1)} %get-tuple-element.40), channel_id=1, source_target_pairs={{1,0},{2,1},{3,2},{4,3},{5,4},{6,5},{7,6},{9,8},{10,9},{11,10},{12... | collective-permute-start | bytes 688136 | tf_op jit(solution)/shard_map/ppermute | solution.py:597
  8.4 1.0 fusion.1
  9.4 0.9 copy_bitcast_fusion
  10.3 1.7 %add_add_fusion.refs_4_ = f32[8,4,24,256]{3,2,1,0:T(8,128)S(1)} fusion(f32[24,1,8,4,256]{4,3,2,1,0:T(4,128)S(1)} %get-tuple-element.73, f32[24,1,8,4,256]{4,3,2,1,0:T(4,128)S(1)} %get-tuple-element.72, f32[24,1,8,4,256]{4,3,2,1,0:T(4,128)S(1)} %get-tuple-element.71), kind=kLoop, calls=%fused_computation.4 | loop fusion | flops 393216 | bytes 3145728 | tf_op jit(solution)/shard_map/add | solution.py:643
  12.0 1.1 copy_bitcast_fusion.2
  13.1 3.7 %collective-permute-done.refs_4_.refs_6_.refs_5_ = f32[4,56,256]{2,1,0:T(8,128)S(1)} collective-permute-done((f32[4,56,256]{2,1,0:T(8,128)S(1)}, f32[4,56,256]{2,1,0:T(8,128)S(1)}, u32[]{:S(2)}, u32[]{:S(2)}) %collective-permute-start) | collective-permute-done | bytes 229408 | tf_op jit(solution)/shard_map/ppermute | solution.py:597
  16.9 0.0 collective-permute-done.1.refs_5_.refs_7_.refs_6_
  16.9 1.5 %two_substeps.2 = (f32[8,4,24,256]{3,2,1,0:T(8,128)S(1)}, f32[8,4,24,256]{3,2,1,0:T(8,128)S(1)}, f32[8,4,24,256]{3,2,1,0:T(8,128)S(1)}, f32[8,4,24,256]{3,2,1,0:T(8,128)S(1)}) custom-call(f32[8,4,24,256]{3,2,1,0:T(8,128)S(1)} %get-tuple-element.78.refs_0_, f32[8,4,24,256]{3,2,1,0:T(8,128)S(1)} %get-tuple-element.77.refs_1_, ...), custom_call_target="tpu_custom_call" | custom-call | flops 11796480 | bytes 12582912 | tf_op jit(solution)/shard_map/two_substeps/pallas_call | solution.py:278
  18.3 0.0 copy-start
  18.4 0.0 copy-start.13
  18.4 0.0 copy-start.16
  18.4 1.6 %collective-permute-start.7 = (f32[8,4,24,256]{3,2,1,0:T(8,128)S(1)}, f32[8,4,24,256]{3,2,1,0:T(8,128)S(1)}, u32[]{:S(2)}, u32[]{:S(2)}) collective-permute-start(f32[8,4,24,256]{3,2,1,0:T(8,128)S(1)} %add_add_fusion.refs_4_), channel_id=1, source_target_pairs={{0,16},{8,24},{16,0},{24,8},{1,17},{9,25},{17,1},{25,9},{2,18},{10... | collective-permute-start | bytes 2359304 | tf_op jit(solution)/shard_map/ppermute | solution.py:573
  20.0 0.9 next_edges.2
  20.9 4.4 %collective-permute-start.2 = (f32[4,48,256]{2,1,0:T(8,128)S(1)}, f32[4,48,256]{2,1,0:T(8,128)S(1)}, u32[]{:S(2)}, u32[]{:S(2)}) collective-permute-start(f32[4,48,256]{2,1,0:T(8,128)S(1)} %get-tuple-element.45), channel_id=1, source_target_pairs={{0,1},{1,2},{2,3},{3,4},{4,5},{5,6},{6,7},{8,9},{9,10},{10,11},{11... | collective-permute-start | bytes 589832 | tf_op jit(solution)/shard_map/ppermute | solution.py:597
  25.3 1.3 %collective-permute-start.3 = (f32[4,48,256]{2,1,0:T(8,128)S(1)}, f32[4,48,256]{2,1,0:T(8,128)S(1)}, u32[]{:S(2)}, u32[]{:S(2)}) collective-permute-start(f32[4,48,256]{2,1,0:T(8,128)S(1)} %get-tuple-element.46), channel_id=1, source_target_pairs={{1,0},{2,1},{3,2},{4,3},{5,4},{6,5},{7,6},{9,8},{10,9},{11,10},{12... | collective-permute-start | bytes 589832 | tf_op jit(solution)/shard_map/ppermute | solution.py:597
  26.6 3.5 %collective-permute-done.2.refs_4_ = f32[4,48,256]{2,1,0:T(8,128)S(1)} collective-permute-done((f32[4,48,256]{2,1,0:T(8,128)S(1)}, f32[4,48,256]{2,1,0:T(8,128)S(1)}, u32[]{:S(2)}, u32[]{:S(2)}) %collective-permute-start.2) | collective-permute-done | bytes 196640 | tf_op jit(solution)/shard_map/ppermute | solution.py:597
  30.1 4.8 %collective-permute-done.3.refs_5_ = f32[4,48,256]{2,1,0:T(8,128)S(1)} collective-permute-done((f32[4,48,256]{2,1,0:T(8,128)S(1)}, f32[4,48,256]{2,1,0:T(8,128)S(1)}, u32[]{:S(2)}, u32[]{:S(2)}) %collective-permute-start.3) | collective-permute-done | bytes 196640 | tf_op jit(solution)/shard_map/ppermute | solution.py:597
  34.9 1.6 %next_edges.3 = (f32[4,48,256]{2,1,0:T(8,128)}, f32[4,48,256]{2,1,0:T(8,128)}) custom-call(f32[8,4,24,256]{3,2,1,0:T(8,128)S(1)} %get-tuple-element.41.refs_0_, f32[8,4,24,256]{3,2,1,0:T(8,128)S(1)} %get-tuple-element.42.refs_1_, f32[8,4,24,256]{3,2,1,0:T(8,128)S(1)} %get-tuple-element.43.refs_2_, f32[8,4,24,256]{3,2,1,0:T(8,128)S(1)} %get-tuple-element.44.refs_3_, ...), custom_call_target="tpu_custom_call" | custom-call | flops 5898240 | bytes 6291456 | tf_op jit(solution)/shard_map/next_edges/pallas_call | solution.py:278
  36.5 4.5 %collective-permute-start.4 = (f32[4,48,256]{2,1,0:T(8,128)}, f32[4,48,256]{2,1,0:T(8,128)S(1)}, u32[]{:S(2)}, u32[]{:S(2)}) collective-permute-start(f32[4,48,256]{2,1,0:T(8,128)} %get-tuple-element.51), channel_id=1, source_target_pairs={{0,1},{1,2},{2,3},{3,4},{4,5},{5,6},{6,7},{8,9},{9,10},{10,11},{11... | collective-permute-start | bytes 589832 | tf_op jit(solution)/shard_map/ppermute | solution.py:597
  41.1 1.5 %collective-permute-start.5 = (f32[4,48,256]{2,1,0:T(8,128)}, f32[4,48,256]{2,1,0:T(8,128)S(1)}, u32[]{:S(2)}, u32[]{:S(2)}) collective-permute-start(f32[4,48,256]{2,1,0:T(8,128)} %get-tuple-element.52), channel_id=1, source_target_pairs={{1,0},{2,1},{3,2},{4,3},{5,4},{6,5},{7,6},{9,8},{10,9},{11,10},{12... | collective-permute-start | bytes 589832 | tf_op jit(solution)/shard_map/ppermute | solution.py:597
  42.6 0.1 pad_add_fusion.place.refs_0_
  42.7 0.8 copy-done.14
  43.4 0.8 copy-done.15
  44.2 1.4 %voxel_weights.1 = (f32[2,32,256]{2,1,0:T(8,128)S(1)}, f32[2,32,256]{2,1,0:T(8,128)S(1)}) custom-call(s32[3]{0:T(128)S(1)} %pad_add_fusion.place.refs_0_, s32[4]{0:T(128)S(1)} %copy-done.16, s32[4,2048]{1,0:T(4,128)S(1)} %copy-done.13, f32[4,2048]{1,0:T(4,128)S(1)} %copy-done.14, f32[4,2048]{1,0:T(4,128)S(1)} %copy-done.15), custom_call_target="tpu_custom_call" | custom-call | tf_op jit(solution)/shard_map/voxel_weights/pallas_call | solution.py:330
  45.6 0.0 copy-start.1
  45.6 1.1 copy-done.1
  46.7 1.1 copy-done.3
  47.9 1.1 copy-done.5
  49.0 1.1 copy-done.7
  50.1 0.9 copy-done.12
  51.1 1.5 %two_substeps.3 = (f32[8,4,24,256]{3,2,1,0:T(8,128)S(1)}, f32[8,4,24,256]{3,2,1,0:T(8,128)S(1)}, f32[8,4,24,256]{3,2,1,0:T(8,128)S(1)}, f32[8,4,24,256]{3,2,1,0:T(8,128)S(1)}) custom-call(f32[8,4,24,256]{3,2,1,0:T(8,128)S(1)} %copy-done.1, f32[8,4,24,256]{3,2,1,0:T(8,128)S(1)} %copy-done.3, f32[8,4,24,256]{3,2,1,0:T(8,128)S(1)} %copy-done.5, ...), custom_call_target="tpu_custom_call" | custom-call | flops 11796480 | bytes 12582912 | tf_op jit(solution)/shard_map/two_substeps/pallas_call | solution.py:278
  52.6 0.0 collective-permute-done.7.refs_11_.refs_6_
  52.6 1.7 %last_but_one.1 = (f32[4,4,24,256]{3,2,1,0:T(8,128)S(1)}, f32[4,4,24,256]{3,2,1,0:T(8,128)S(1)}, f32[8,4,24,256]{3,2,1,0:T(8,128)S(1)}, f32[8,4,24,256]{3,2,1,0:T(8,128)S(1)}, f32[8,4,24,256]{3,2,1,0:T(8,128)S(1)}) custom-call(s32[3]{0:T(128)S(1)} %pad_add_fusion.place.refs_0_, f32[8,4,24,256]{3,2,1,0:T(8,128)S(1)} %get-tuple-element.47.refs_1_.refs_0_, ...), custom_call_target="tpu_custom_call" | custom-call | flops 11796480 | bytes 12582912 | tf_op jit(solution)/shard_map/last_but_one/pallas_call | solution.py:278
  54.3 0.6 collective-permute-start.9
  54.9 0.5 collective-permute-start.12
  55.4 9.1 %collective-permute-done.9.refs_6_.refs_14_ = f32[4,4,24,256]{3,2,1,0:T(8,128)S(1)} collective-permute-done((f32[4,4,24,256]{3,2,1,0:T(8,128)S(1)}, f32[4,4,24,256]{3,2,1,0:T(8,128)S(1)}, u32[]{:S(2)}, u32[]{:S(2)}) %collective-permute-start.9) | collective-permute-done | bytes 393248 | tf_op jit(solution)/shard_map/ppermute | solution.py:573
  64.5 0.5 collective-permute-start.14
  65.0 1.2 collective-permute-done.10.refs_7_.refs_15_
  66.2 0.7 gram.1
  66.9 0.6 collective-permute-start.13
  67.5 0.5 last_free.1.refs_0_
  68.0 9.1 %collective-permute-done.13 = f32[96,128]{1,0:T(8,128)S(1)} collective-permute-done((f32[96,128]{1,0:T(8,128)S(1)}, f32[96,128]{1,0:T(8,128)S(1)}, u32[]{:S(2)}, u32[]{:S(2)}) %collective-permute-start.13) | collective-permute-done | bytes 49184 | tf_op jit(solution)/shard_map/ppermute | solution.py:573
  77.1 0.6 collective-permute-start.20
  77.7 1.5 %collective-permute-start.23 = (f32[8,4,24,256]{3,2,1,0:T(8,128)S(1)}, f32[8,4,24,256]{3,2,1,0:T(8,128)S(1)}, u32[]{:S(2)}, u32[]{:S(2)}) collective-permute-start(f32[8,4,24,256]{3,2,1,0:T(8,128)S(1)} %get-tuple-element.66.refs_8_), channel_id=1, source_target_pairs={{0,16},{8,24},{16,0},{24,8},{1,17},{9,25},{17,1},{25,9},{2,18},{10... | collective-permute-start | bytes 2359304 | tf_op jit(solution)/shard_map/ppermute | solution.py:573
  79.2 3.9 %collective-permute-start.15 = (f32[96,128]{1,0:T(8,128)S(1)}, f32[96,128]{1,0:T(8,128)S(1)}, u32[]{:S(2)}, u32[]{:S(2)}) collective-permute-start(f32[96,128]{1,0:T(8,128)S(1)} %add.20), channel_id=1, source_target_pairs={{0,1},{1,0},{2,3},{3,2},{4,5},{5,4},{6,7},{7,6},{8,9},{9,8},{10,11... | collective-permute-start | bytes 147464 | tf_op jit(solution)/shard_map/ppermute | solution.py:573
  83.1 2.1 %collective-permute-done.15 = f32[96,128]{1,0:T(8,128)S(1)} collective-permute-done((f32[96,128]{1,0:T(8,128)S(1)}, f32[96,128]{1,0:T(8,128)S(1)}, u32[]{:S(2)}, u32[]{:S(2)}) %collective-permute-start.15) | collective-permute-done | bytes 49184 | tf_op jit(solution)/shard_map/ppermute | solution.py:573
  85.1 3.3 %collective-permute-start.16 = (f32[96,128]{1,0:T(8,128)S(1)}, f32[96,128]{1,0:T(8,128)S(1)}, u32[]{:S(2)}, u32[]{:S(2)}) collective-permute-start(f32[96,128]{1,0:T(8,128)S(1)} %add.21), channel_id=1, source_target_pairs={{0,2},{1,3},{2,0},{3,1},{4,6},{5,7},{6,4},{7,5},{8,10},{9,11},{10,... | collective-permute-start | bytes 147464 | tf_op jit(solution)/shard_map/ppermute | solution.py:573
  88.4 2.1 %collective-permute-done.16 = f32[96,128]{1,0:T(8,128)S(1)} collective-permute-done((f32[96,128]{1,0:T(8,128)S(1)}, f32[96,128]{1,0:T(8,128)S(1)}, u32[]{:S(2)}, u32[]{:S(2)}) %collective-permute-start.16) | collective-permute-done | bytes 49184 | tf_op jit(solution)/shard_map/ppermute | solution.py:573
  90.5 3.1 %collective-permute-start.17 = (f32[96,128]{1,0:T(8,128)S(1)}, f32[96,128]{1,0:T(8,128)S(1)}, u32[]{:S(2)}, u32[]{:S(2)}) collective-permute-start(f32[96,128]{1,0:T(8,128)S(1)} %add.22), channel_id=1, source_target_pairs={{0,4},{1,5},{2,6},{3,7},{4,0},{5,1},{6,2},{7,3},{8,12},{9,13},{10,... | collective-permute-start | bytes 147464 | tf_op jit(solution)/shard_map/ppermute | solution.py:573
  93.6 2.1 %collective-permute-done.17 = f32[96,128]{1,0:T(8,128)S(1)} collective-permute-done((f32[96,128]{1,0:T(8,128)S(1)}, f32[96,128]{1,0:T(8,128)S(1)}, u32[]{:S(2)}, u32[]{:S(2)}) %collective-permute-start.17) | collective-permute-done | bytes 49184 | tf_op jit(solution)/shard_map/ppermute | solution.py:573
  95.6 0.1 collective-permute-start.18
  95.7 0.5 collective-permute-start.19
  96.2 0.1 collective-permute-start.22
  96.3 0.6 collective-permute-done.18.other
  96.9 18.5 %transforms_early.1 = (f32[96,128]{1,0:T(8,128)S(1)}, f32[96,128]{1,0:T(8,128)S(1)}) custom-call(s32[3]{0:T(128)S(1)} %pad_add_fusion.place.refs_0_, f32[96,128]{1,0:T(8,128)S(1)} %add.23.mine, f32[96,128]{1,0:T(8,128)S(1)} %collective-permute-done.18.other), custom_call_target="tpu_custom_call" | custom-call | flops 100000000 | bytes 1000000 | tf_op jit(solution)/shard_map/transforms_early/pallas_call | solution.py:497
  115.5 0.2 collective-permute-start.21
  115.7 0.3 collective-permute-start.24
  116.0 0.2 collective-permute-start.25
  116.2 6.6 %transforms_late.1.weights = f32[24,128]{1,0:T(8,128)S(1)} custom-call(s32[3]{0:T(128)S(1)} %pad_add_fusion.place.refs_0_, f32[96,128]{1,0:T(8,128)S(1)} %get-tuple-element.59.total, f32[96,128]{1,0:T(8,128)S(1)} %get-tuple-element.60.last), custom_call_target="tpu_custom_call" | custom-call | flops 100000000 | bytes 1000000 | tf_op jit(solution)/shard_map/transforms_late/pallas_call | solution.py:497
  122.8 5.8 %mix.1 = f32[24,4,8,4,256]{4,3,2,1,0:T(4,128)} custom-call(s32[3]{0:T(128)S(1)} %pad_add_fusion.place.refs_0_, f32[24,128]{1,0:T(8,128)S(1)} %transforms_late.1.weights, f32[8,4,24,256]{3,2,1,0:T(8,128)S(1)} %last_free.1.refs_0_, f32[8,4,24,256]{3,2,1,0:T(8,128)S(1)} %collective-permute-done.19.refs_1_, ...), custom_call_target="tpu_custom_call" | custom-call | tf_op jit(solution)/shard_map/mix/pallas_call | solution.py:557
  (47 shorter events, 0.1 us)
Async XLA Ops:
  0.0 8.4 %copy-start.17 = (f32[24,4,8,4,256]{4,3,2,1,0:T(4,128)S(1)}, f32[24,4,8,4,256]{4,3,2,1,0:T(4,128)}, u32[]{:S(2)}) copy-start(f32[24,4,8,4,256]{4,3,2,1,0:T(4,128)} %param.8) | copy-start | bytes 9437188
  0.0 2.0 %copy-start.8 = (f32[8,4,256]{2,1,0:T(4,128)S(1)}, f32[8,4,256]{2,1,0:T(4,128)}, u32[]{:S(2)}) copy-start(f32[8,4,256]{2,1,0:T(4,128)} %refs_7_.3) | copy-start | bytes 98308
  0.0 2.0 %copy-start.10 = (f32[8,4,256]{2,1,0:T(4,128)S(1)}, f32[8,4,256]{2,1,0:T(4,128)}, u32[]{:S(2)}) copy-start(f32[8,4,256]{2,1,0:T(4,128)} %refs_9_.9) | copy-start | bytes 98308
  0.0 2.0 %copy-start.9 = (f32[8,4,256]{2,1,0:T(4,128)S(1)}, f32[8,4,256]{2,1,0:T(4,128)}, u32[]{:S(2)}) copy-start(f32[8,4,256]{2,1,0:T(4,128)} %refs_8_.9) | copy-start | bytes 98308
  2.2 14.6 %collective-permute-start = (f32[4,56,256]{2,1,0:T(8,128)S(1)}, f32[4,56,256]{2,1,0:T(8,128)S(1)}, u32[]{:S(2)}, u32[]{:S(2)}) collective-permute-start(f32[4,56,256]{2,1,0:T(8,128)S(1)} %get-tuple-element.39), channel_id=1, source_target_pairs={{0,1},{1,2},{2,3},{3,4},{4,5},{5,6},{6,7},{8,9},{9,10},{10,11},{11... | collective-permute-start | bytes 688136 | tf_op jit(solution)/shard_map/ppermute | solution.py:597
  7.1 9.7 %collective-permute-start.1 = (f32[4,56,256]{2,1,0:T(8,128)S(1)}, f32[4,56,256]{2,1,0:T(8,128)S(1)}, u32[]{:S(2)}, u32[]{:S(2)}) collective-permute-start(f32[4,56,256]{2,1,0:T(8,128)S(1)} %get-tuple-element.40), channel_id=1, source_target_pairs={{1,0},{2,1},{3,2},{4,3},{5,4},{6,5},{7,6},{9,8},{10,9},{11,10},{12... | collective-permute-start | bytes 688136 | tf_op jit(solution)/shard_map/ppermute | solution.py:597
  18.3 18.2 %copy-start = (f32[8,4,24,256]{3,2,1,0:T(8,128)}, f32[8,4,24,256]{3,2,1,0:T(8,128)S(1)}, u32[]{:S(2)}) copy-start(f32[8,4,24,256]{3,2,1,0:T(8,128)S(1)} %get-tuple-element.41.refs_0_) | copy-start | bytes 2359300
  18.3 18.2 %copy-start.2 = (f32[8,4,24,256]{3,2,1,0:T(8,128)}, f32[8,4,24,256]{3,2,1,0:T(8,128)S(1)}, u32[]{:S(2)}) copy-start(f32[8,4,24,256]{3,2,1,0:T(8,128)S(1)} %get-tuple-element.42.refs_1_) | copy-start | bytes 2359300
  18.3 18.2 %copy-start.4 = (f32[8,4,24,256]{3,2,1,0:T(8,128)}, f32[8,4,24,256]{3,2,1,0:T(8,128)S(1)}, u32[]{:S(2)}) copy-start(f32[8,4,24,256]{3,2,1,0:T(8,128)S(1)} %get-tuple-element.43.refs_2_) | copy-start | bytes 2359300
  18.4 18.2 %copy-start.6 = (f32[8,4,24,256]{3,2,1,0:T(8,128)}, f32[8,4,24,256]{3,2,1,0:T(8,128)S(1)}, u32[]{:S(2)}) copy-start(f32[8,4,24,256]{3,2,1,0:T(8,128)S(1)} %get-tuple-element.44.refs_3_) | copy-start | bytes 2359300
  18.4 24.3 %copy-start.13 = (s32[4,2048]{1,0:T(4,128)S(1)}, s32[4,2048]{1,0:T(4,128)}, u32[]{:S(2)}) copy-start(s32[4,2048]{1,0:T(4,128)} %obs_index.1) | copy-start | bytes 98308
  18.4 24.3 %copy-start.16 = (s32[4]{0:T(128)S(1)}, s32[4]{0:T(128)}, u32[]{:S(2)}) copy-start(s32[4]{0:T(128)} %refs_1_.1) | copy-start | bytes 52
  18.4 34.2 %collective-permute-start.7 = (f32[8,4,24,256]{3,2,1,0:T(8,128)S(1)}, f32[8,4,24,256]{3,2,1,0:T(8,128)S(1)}, u32[]{:S(2)}, u32[]{:S(2)}) collective-permute-start(f32[8,4,24,256]{3,2,1,0:T(8,128)S(1)} %add_add_fusion.refs_4_), channel_id=1, source_target_pairs={{0,16},{8,24},{16,0},{24,8},{1,17},{9,25},{17,1},{25,9},{2,18},{10... | collective-permute-start | bytes 2359304 | tf_op jit(solution)/shard_map/ppermute | solution.py:573
  20.0 32.6 %collective-permute-start.6 = (f32[8,4,24,256]{3,2,1,0:T(8,128)S(1)}, f32[8,4,24,256]{3,2,1,0:T(8,128)S(1)}, u32[]{:S(2)}, u32[]{:S(2)}) collective-permute-start(f32[8,4,24,256]{3,2,1,0:T(8,128)S(1)} %add_add_fusion.refs_4_), channel_id=1, source_target_pairs={{0,8},{8,0},{16,24},{24,16},{1,9},{9,1},{17,25},{25,17},{2,10},{10... | collective-permute-start | bytes 2359304 | tf_op jit(solution)/shard_map/ppermute | solution.py:573
  20.9 9.2 %collective-permute-start.2 = (f32[4,48,256]{2,1,0:T(8,128)S(1)}, f32[4,48,256]{2,1,0:T(8,128)S(1)}, u32[]{:S(2)}, u32[]{:S(2)}) collective-permute-start(f32[4,48,256]{2,1,0:T(8,128)S(1)} %get-tuple-element.45), channel_id=1, source_target_pairs={{0,1},{1,2},{2,3},{3,4},{4,5},{5,6},{6,7},{8,9},{9,10},{10,11},{11... | collective-permute-start | bytes 589832 | tf_op jit(solution)/shard_map/ppermute | solution.py:597
  25.3 9.6 %collective-permute-start.3 = (f32[4,48,256]{2,1,0:T(8,128)S(1)}, f32[4,48,256]{2,1,0:T(8,128)S(1)}, u32[]{:S(2)}, u32[]{:S(2)}) collective-permute-start(f32[4,48,256]{2,1,0:T(8,128)S(1)} %get-tuple-element.46), channel_id=1, source_target_pairs={{1,0},{2,1},{3,2},{4,3},{5,4},{6,5},{7,6},{9,8},{10,9},{11,10},{12... | collective-permute-start | bytes 589832 | tf_op jit(solution)/shard_map/ppermute | solution.py:597
  34.9 1.6 %copy-start.11 = (f32[4,48,256]{2,1,0:T(8,128)}, f32[4,48,256]{2,1,0:T(8,128)S(1)}, u32[]{:S(2)}) copy-start(f32[4,48,256]{2,1,0:T(8,128)S(1)} %collective-permute-done.3.refs_5_) | copy-start | bytes 589828
  36.5 16.0 %collective-permute-start.4 = (f32[4,48,256]{2,1,0:T(8,128)}, f32[4,48,256]{2,1,0:T(8,128)S(1)}, u32[]{:S(2)}, u32[]{:S(2)}) collective-permute-start(f32[4,48,256]{2,1,0:T(8,128)} %get-tuple-element.51), channel_id=1, source_target_pairs={{0,1},{1,2},{2,3},{3,4},{4,5},{5,6},{6,7},{8,9},{9,10},{10,11},{11... | collective-permute-start | bytes 589832 | tf_op jit(solution)/shard_map/ppermute | solution.py:597
  41.1 11.5 %collective-permute-start.5 = (f32[4,48,256]{2,1,0:T(8,128)}, f32[4,48,256]{2,1,0:T(8,128)S(1)}, u32[]{:S(2)}, u32[]{:S(2)}) collective-permute-start(f32[4,48,256]{2,1,0:T(8,128)} %get-tuple-element.52), channel_id=1, source_target_pairs={{1,0},{2,1},{3,2},{4,3},{5,4},{6,5},{7,6},{9,8},{10,9},{11,10},{12... | collective-permute-start | bytes 589832 | tf_op jit(solution)/shard_map/ppermute | solution.py:597
  42.7 0.8 copy-start.14
  43.4 0.8 copy-start.15
  45.6 1.1 copy-start.1
  46.7 1.1 copy-start.3
  47.9 1.1 copy-start.5
  49.0 1.1 copy-start.7
  50.1 0.9 copy-start.12
  54.3 10.2 %collective-permute-start.9 = (f32[4,4,24,256]{3,2,1,0:T(8,128)S(1)}, f32[4,4,24,256]{3,2,1,0:T(8,128)S(1)}, u32[]{:S(2)}, u32[]{:S(2)}) collective-permute-start(f32[4,4,24,256]{3,2,1,0:T(8,128)S(1)} %get-tuple-element.55.refs_16_), channel_id=1, source_target_pairs={{0,16},{8,24},{16,0},{24,8},{1,17},{9,25},{17,1},{25,9},{2,18},{10... | collective-permute-start | bytes 1179656 | tf_op jit(solution)/shard_map/ppermute | solution.py:573
  54.9 11.4 %collective-permute-start.11 = (f32[8,4,24,256]{3,2,1,0:T(8,128)S(1)}, f32[8,4,24,256]{3,2,1,0:T(8,128)S(1)}, u32[]{:S(2)}, u32[]{:S(2)}) collective-permute-start(f32[8,4,24,256]{3,2,1,0:T(8,128)S(1)} %collective-permute-done.7.refs_11_.refs_6_), channel_id=1, source_target_pairs={{0,8},{8,0},{16,24},{24,16},{1,9},{9,1},{17,25},{25,17},{2,10},{10... | collective-permute-start | bytes 2359304 | tf_op jit(solution)/shard_map/ppermute | solution.py:573
  54.9 10.1 %collective-permute-start.12 = (f32[4,4,24,256]{3,2,1,0:T(8,128)S(1)}, f32[4,4,24,256]{3,2,1,0:T(8,128)S(1)}, u32[]{:S(2)}, u32[]{:S(2)}) collective-permute-start(f32[4,4,24,256]{3,2,1,0:T(8,128)S(1)} %get-tuple-element.55.refs_16_), channel_id=1, source_target_pairs={{0,8},{8,0},{16,24},{24,16},{1,9},{9,1},{17,25},{25,17},{2,10},{10... | collective-permute-start | bytes 1179656 | tf_op jit(solution)/shard_map/ppermute | solution.py:573
  55.4 9.6 %collective-permute-start.8 = (f32[4,4,24,256]{3,2,1,0:T(8,128)S(1)}, f32[4,4,24,256]{3,2,1,0:T(8,128)S(1)}, u32[]{:S(2)}, u32[]{:S(2)}) collective-permute-start(f32[4,4,24,256]{3,2,1,0:T(8,128)S(1)} %get-tuple-element.57.refs_4_.refs_12_), channel_id=1, source_target_pairs={{0,8},{8,0},{16,24},{24,16},{1,9},{9,1},{17,25},{25,17},{2,10},{10... | collective-permute-start | bytes 1179656 | tf_op jit(solution)/shard_map/ppermute | solution.py:573
  64.5 1.7 %collective-permute-start.10 = (f32[4,4,24,256]{3,2,1,0:T(8,128)S(1)}, f32[4,4,24,256]{3,2,1,0:T(8,128)S(1)}, u32[]{:S(2)}, u32[]{:S(2)}) collective-permute-start(f32[4,4,24,256]{3,2,1,0:T(8,128)S(1)} %collective-permute-done.9.refs_6_.refs_14_), channel_id=1, source_target_pairs={{0,8},{8,0},{16,24},{24,16},{1,9},{9,1},{17,25},{25,17},{2,10},{10... | collective-permute-start | bytes 1179656 | tf_op jit(solution)/shard_map/ppermute | solution.py:573
  64.5 12.6 %collective-permute-start.14 = (f32[4,4,24,256]{3,2,1,0:T(8,128)S(1)}, f32[4,4,24,256]{3,2,1,0:T(8,128)S(1)}, u32[]{:S(2)}, u32[]{:S(2)}) collective-permute-start(f32[4,4,24,256]{3,2,1,0:T(8,128)S(1)} %get-tuple-element.57.refs_4_.refs_12_), channel_id=1, source_target_pairs={{0,16},{8,24},{16,0},{24,8},{1,17},{9,25},{17,1},{25,9},{2,18},{10... | collective-permute-start | bytes 1179656 | tf_op jit(solution)/shard_map/ppermute | solution.py:573
  66.9 10.2 %collective-permute-start.13 = (f32[96,128]{1,0:T(8,128)S(1)}, f32[96,128]{1,0:T(8,128)S(1)}, u32[]{:S(2)}, u32[]{:S(2)}) collective-permute-start(f32[96,128]{1,0:T(8,128)S(1)} %gram.1), channel_id=1, source_target_pairs={{0,16},{8,24},{16,0},{24,8},{1,17},{9,25},{17,1},{25,9},{2,18},{10... | collective-permute-start | bytes 147464 | tf_op jit(solution)/shard_map/ppermute | solution.py:573
  77.1 38.3 %collective-permute-start.20 = (f32[8,4,24,256]{3,2,1,0:T(8,128)S(1)}, f32[8,4,24,256]{3,2,1,0:T(8,128)S(1)}, u32[]{:S(2)}, u32[]{:S(2)}) collective-permute-start(f32[8,4,24,256]{3,2,1,0:T(8,128)S(1)} %last_free.1.refs_0_), channel_id=1, source_target_pairs={{0,16},{8,24},{16,0},{24,8},{1,17},{9,25},{17,1},{25,9},{2,18},{10... | collective-permute-start | bytes 2359304 | tf_op jit(solution)/shard_map/ppermute | solution.py:573
  77.7 38.0 %collective-permute-start.23 = (f32[8,4,24,256]{3,2,1,0:T(8,128)S(1)}, f32[8,4,24,256]{3,2,1,0:T(8,128)S(1)}, u32[]{:S(2)}, u32[]{:S(2)}) collective-permute-start(f32[8,4,24,256]{3,2,1,0:T(8,128)S(1)} %get-tuple-element.66.refs_8_), channel_id=1, source_target_pairs={{0,16},{8,24},{16,0},{24,8},{1,17},{9,25},{17,1},{25,9},{2,18},{10... | collective-permute-start | bytes 2359304 | tf_op jit(solution)/shard_map/ppermute | solution.py:573
  79.2 5.9 %collective-permute-start.15 = (f32[96,128]{1,0:T(8,128)S(1)}, f32[96,128]{1,0:T(8,128)S(1)}, u32[]{:S(2)}, u32[]{:S(2)}) collective-permute-start(f32[96,128]{1,0:T(8,128)S(1)} %add.20), channel_id=1, source_target_pairs={{0,1},{1,0},{2,3},{3,2},{4,5},{5,4},{6,7},{7,6},{8,9},{9,8},{10,11... | collective-permute-start | bytes 147464 | tf_op jit(solution)/shard_map/ppermute | solution.py:573
  85.1 5.3 %collective-permute-start.16 = (f32[96,128]{1,0:T(8,128)S(1)}, f32[96,128]{1,0:T(8,128)S(1)}, u32[]{:S(2)}, u32[]{:S(2)}) collective-permute-start(f32[96,128]{1,0:T(8,128)S(1)} %add.21), channel_id=1, source_target_pairs={{0,2},{1,3},{2,0},{3,1},{4,6},{5,7},{6,4},{7,5},{8,10},{9,11},{10,... | collective-permute-start | bytes 147464 | tf_op jit(solution)/shard_map/ppermute | solution.py:573
  90.5 5.2 %collective-permute-start.17 = (f32[96,128]{1,0:T(8,128)S(1)}, f32[96,128]{1,0:T(8,128)S(1)}, u32[]{:S(2)}, u32[]{:S(2)}) collective-permute-start(f32[96,128]{1,0:T(8,128)S(1)} %add.22), channel_id=1, source_target_pairs={{0,4},{1,5},{2,6},{3,7},{4,0},{5,1},{6,2},{7,3},{8,12},{9,13},{10,... | collective-permute-start | bytes 147464 | tf_op jit(solution)/shard_map/ppermute | solution.py:573
  95.6 1.3 %collective-permute-start.18 = (f32[96,128]{1,0:T(8,128)S(1)}, f32[96,128]{1,0:T(8,128)S(1)}, u32[]{:S(2)}, u32[]{:S(2)}) collective-permute-start(f32[96,128]{1,0:T(8,128)S(1)} %add.23.mine), channel_id=1, source_target_pairs={{0,8},{8,0},{16,24},{24,16},{1,9},{9,1},{17,25},{25,17},{2,10},{10... | collective-permute-start | bytes 147464 | tf_op jit(solution)/shard_map/ppermute | solution.py:573
  95.7 27.1 %collective-permute-start.19 = (f32[8,4,24,256]{3,2,1,0:T(8,128)S(1)}, f32[8,4,24,256]{3,2,1,0:T(8,128)S(1)}, u32[]{:S(2)}, u32[]{:S(2)}) collective-permute-start(f32[8,4,24,256]{3,2,1,0:T(8,128)S(1)} %last_free.1.refs_0_), channel_id=1, source_target_pairs={{0,8},{8,0},{16,24},{24,16},{1,9},{9,1},{17,25},{25,17},{2,10},{10... | collective-permute-start | bytes 2359304 | tf_op jit(solution)/shard_map/ppermute | solution.py:573
  96.2 26.6 %collective-permute-start.22 = (f32[8,4,24,256]{3,2,1,0:T(8,128)S(1)}, f32[8,4,24,256]{3,2,1,0:T(8,128)S(1)}, u32[]{:S(2)}, u32[]{:S(2)}) collective-permute-start(f32[8,4,24,256]{3,2,1,0:T(8,128)S(1)} %get-tuple-element.66.refs_8_), channel_id=1, source_target_pairs={{0,8},{8,0},{16,24},{24,16},{1,9},{9,1},{17,25},{25,17},{2,10},{10... | collective-permute-start | bytes 2359304 | tf_op jit(solution)/shard_map/ppermute | solution.py:573
  115.5 7.4 %collective-permute-start.21 = (f32[8,4,24,256]{3,2,1,0:T(8,128)S(1)}, f32[8,4,24,256]{3,2,1,0:T(8,128)S(1)}, u32[]{:S(2)}, u32[]{:S(2)}) collective-permute-start(f32[8,4,24,256]{3,2,1,0:T(8,128)S(1)} %collective-permute-done.20.refs_2_), channel_id=1, source_target_pairs={{0,8},{8,0},{16,24},{24,16},{1,9},{9,1},{17,25},{25,17},{2,10},{10... | collective-permute-start | bytes 2359304 | tf_op jit(solution)/shard_map/ppermute | solution.py:573
  115.7 7.1 %collective-permute-start.24 = (f32[8,4,24,256]{3,2,1,0:T(8,128)S(1)}, f32[8,4,24,256]{3,2,1,0:T(8,128)S(1)}, u32[]{:S(2)}, u32[]{:S(2)}) collective-permute-start(f32[8,4,24,256]{3,2,1,0:T(8,128)S(1)} %collective-permute-done.23.refs_10_), channel_id=1, source_target_pairs={{0,8},{8,0},{16,24},{24,16},{1,9},{9,1},{17,25},{25,17},{2,10},{10... | collective-permute-start | bytes 2359304 | tf_op jit(solution)/shard_map/ppermute | solution.py:573
  116.0 6.8 %collective-permute-start.25 = (f32[4,4,24,256]{3,2,1,0:T(8,128)S(1)}, f32[4,4,24,256]{3,2,1,0:T(8,128)S(1)}, u32[]{:S(2)}, u32[]{:S(2)}) collective-permute-start(f32[4,4,24,256]{3,2,1,0:T(8,128)S(1)} %collective-permute-done.14.refs_18_), channel_id=1, source_target_pairs={{0,8},{8,0},{16,24},{24,16},{1,9},{9,1},{17,25},{25,17},{2,10},{10... | collective-permute-start | bytes 1179656 | tf_op jit(solution)/shard_map/ppermute | solution.py:573

commit v8 on v7

--- a/solution.py
+++ b/solution.py
@@ -42,17 +42,18 @@
 
 
 def wide_right(x):
-    both = jnp.concatenate(split(x), axis=1)
-    rows, lanes = both.shape
-    if rows < lanes // 2:
-        both = jnp.concatenate([both, jnp.zeros((lanes // 2 - rows, lanes), bf16)], axis=0)
-    return jnp.concatenate([both, both], axis=0)
+    rows, lanes = x.shape
+    parts = []
+    for part in split(x):
+        if rows < lanes:
+            part = jnp.concatenate([part, jnp.zeros((lanes - rows, lanes), bf16)], axis=0)
+        parts.append(jnp.concatenate([part, part], axis=0))
+    return parts
 
 
 def wide_dot(left, right):
-    out = jnp.dot(left, right, preferred_element_type=f32)
-    side = out.shape[1] // 2
-    return out[:, :side] + out[:, side:]
+    high, low = [jnp.dot(left, part, preferred_element_type=f32) for part in right]
+    return high + low
 
 
 NN = ((1,), (0,))
@@ -190,9 +191,15 @@
             )
 
 
-def two_substeps_kernel(
-    a, r, c, i, low, high, low_first, high_first, diffusivity, binding, source, *refs
-):
+def two_substeps_kernel(*refs, weigh):
+    if weigh:
+        place, owner, *refs = refs
+    a, r, c, i, low, high, low_first, high_first, diffusivity, binding, source, *refs = refs
+    if weigh:
+        obs_index, observed, obs_var, *refs = refs
+        *refs, omega, eta, m0, m1, m2, m3 = refs
+        refs = [*refs, m0, m1, m2, m3]
+        voxel_weights(place, owner, obs_index, observed, obs_var, omega, eta)
     outs, middle = refs[:4], refs[4:]
     everywhere = range(a.shape[0])
     coefficients = (diffusivity, binding, source)
@@ -291,7 +298,7 @@
     )(*scalars, *inputs, *ready)
 
 
-def weights_kernel(place, owner, obs_index, observed, obs_var, omega, eta):
+def voxel_weights(place, owner, obs_index, observed, obs_var, omega, eta):
     count, rows, ny = omega.shape
     batch_size = obs_index.shape[1]
     for k in range(count):
@@ -323,18 +330,6 @@
         sums = sums[: 2 * rows] + sums[2 * rows : 4 * rows] + sums[4 * rows :]
         omega[k] = sums[:rows]
         eta[k] = sums[rows:]
-
-
-def voxel_weights(place, owner, obs_index, observed, obs_var, count, rows, ny):
-    out = jax.ShapeDtypeStruct((count, rows, ny), f32)
-    return pl.pallas_call(
-        weights_kernel,
-        out_shape=[out, out],
-        in_specs=[SMEM, SMEM, VMEM, VMEM, VMEM],
-        out_specs=[VMEM, VMEM],
-        compiler_params=pltpu.CompilerParams(vmem_limit_bytes=SCOPED),
-        name="voxel_weights",
-    )(place, owner, obs_index, observed, obs_var)
 
 
 def gram_kernel(place, owner, omega, eta, *refs, offsets, halves):
@@ -451,7 +446,7 @@
     return wide_dot(wide_left(total), wide_right(mixing))
 
 
-def early_kernel(place, mine, other, total, last, ordered):
+def transform_kernel(place, mine, other, out, ordered, work, *, offsets, blocks, rows):
     members = mine.shape[0]
     row = lax.broadcasted_iota(jnp.int32, (members, LANES), 0)
     column = lax.broadcasted_iota(jnp.int32, (members, LANES), 1)
@@ -470,17 +465,9 @@
         middle = jnp.where(column == row, pick(column == members, packed), 0.0)
         side = jnp.where(column == members, pick(column == members + 2, packed), 0.0)
         ordered[2 * half + 1] = below + turned(below) + (middle + side)
-    batches = ordered.shape[0]
     product = jnp.where(row == column, 1.0, 0.0)
-    for batch in range(batches - 1):
+    for batch in range(ordered.shape[0]):
         product = batch_transform(ordered[batch], product, members)
-    total[...] = product
-    last[...] = ordered[batches - 1]
-
-
-def late_kernel(place, total, last, out, work, *, offsets, blocks, rows):
-    members = total.shape[0]
-    product = batch_transform(last[...], total[...], members)
     rest = jnp.zeros((LANES - members, LANES), f32)
     work[...] = jnp.concatenate([product, rest], axis=0)
     if blocks == 1:
@@ -493,19 +480,24 @@
     out[...] = work[pl.ds(pl.multiple_of(offsets(place[2], 0), 8), rows), :]
 
 
-def transform_call(kernel, name, outputs, scratch, inputs):
+def transforms(place, mine, other, offsets, blocks, rows):
+    members = mine.shape[0]
+    shape = (LANES, LANES) if blocks == 1 else (rows, LANES)
     return pl.pallas_call(
-        kernel,
-        out_shape=[jax.ShapeDtypeStruct(shape, f32) for shape in outputs],
-        in_specs=[SMEM] + [VMEM] * (len(inputs) - 1),
-        out_specs=[VMEM] * len(outputs),
-        scratch_shapes=[pltpu.VMEM(shape, f32) for shape in scratch],
+        functools.partial(transform_kernel, offsets=offsets, blocks=blocks, rows=rows),
+        out_shape=jax.ShapeDtypeStruct(shape, f32),
+        in_specs=[SMEM, VMEM, VMEM],
+        out_specs=VMEM,
+        scratch_shapes=[
+            pltpu.VMEM((4, members, LANES), f32),
+            pltpu.VMEM((LANES, LANES), f32),
+        ],
         compiler_params=pltpu.CompilerParams(vmem_limit_bytes=SCOPED),
         cost_estimate=pl.CostEstimate(
             flops=10**8, bytes_accessed=10**6, transcendentals=0
         ),
-        name=name,
-    )(*inputs)
+        name="transforms",
+    )(place, mine, other)
 
 
 def mix_kernel(place, weights, *refs, blocks, halves):
@@ -656,12 +648,17 @@
                 scratch=[whole] * 8,
             )
         )
+        weigh = step == 1
         fields = forecast_call(
-            two_substeps_kernel, "two_substeps", inputs, [whole] * 4, 2 * cells, scratch=[whole] * 4
-        )
-    omega, eta = voxel_weights(
-        place, owner, obs_index, observed, obs_var, batches // 2, nx * nz, ny
-    )
+            functools.partial(two_substeps_kernel, weigh=weigh),
+            "two_substeps",
+            [*inputs, obs_index, observed, obs_var] if weigh else inputs,
+            [whole] * 4 + ([(batches // 2, nx * nz, ny)] * 2 if weigh else []),
+            2 * cells,
+            scratch=[whole] * 4,
+            scalars=[place, owner] if weigh else (),
+        )
+    *fields, omega, eta = fields
     *tracers, internal, middle, add = forecast_call(
         functools.partial(last_but_one_kernel, halves=halves),
         "last_but_one",
@@ -669,7 +666,7 @@
         [(nx // halves, nz, rows, ny)] * halves + [whole] * 3,
         2 * cells,
         scratch=[whole] * 3,
-        ready=[*conserved[1:], omega, eta],
+        ready=conserved[1:],
         scalars=[place],
     )
     (free,) = forecast_call(
@@ -682,35 +679,21 @@
     near = collect(*tracers)
     conserved = complete(conserved, tracers[0])
     near = complete(near)
-    far = collect(tracers[1], tie(tracers[0], across(near))) if halves == 2 else []
-    half = gram(place, owner, omega, eta, near, offsets, halves, [*conserved[3:], *far[1:2]])
+    half = gram(place, owner, omega, eta, near, offsets, halves, conserved[3:])
     if halves == 2:
-        half = tie(half + swap(half, "member", 2), across(far))
-        far = complete(far, half)
+        half = half + swap(half, "member", 2)
     internal = collect(internal, tie(internal, half))
     free = collect(free, tie(free, half))
     half = total_over(half, "space")
+    far = collect(tracers[1], tie(tracers[0], half)) if halves == 2 else []
     other = swap(half, "member", 1)
-    internal = complete(internal, half)
-    square = (members, LANES)
-    total, extended = transform_call(
-        early_kernel,
-        "transforms_early",
-        [square, square],
-        [(batches, members, LANES)],
-        [place, half, other],
-    )
-    free = complete(free, total)
-    (weights,) = transform_call(
-        functools.partial(late_kernel, offsets=offsets, blocks=blocks, rows=rows),
-        "transforms_late",
-        [(LANES, LANES) if blocks == 1 else (rows, LANES)],
-        [(LANES, LANES)],
-        [place, total, extended],
-    )
+    weights = transforms(place, half, other, offsets, blocks, rows)
+    internal = complete(internal, weights)
+    free = complete(free, weights)
+    far = complete(far, weights) if halves == 2 else []
     if blocks == 1:
         weights = lax.dynamic_slice(weights, (member * rows, 0), (rows, LANES))
-    sources = free + conserved + internal + near + (far if halves == 2 else [])
+    sources = free + conserved + internal + near + far
     return mix(place, weights, sources, blocks, halves, ensemble.shape)
 
 

time: 129 us -> 133 us (1.031); the launches traced: 129 us -> 131 us
  Pallas kernels: 40.8 us -> 45.6 us
  waiting for transfers between devices: 38.4 us -> 37 us
    pallas_call x3 -> x1, Pallas kernels: 26.5 us -> 28.4 us  [transforms(): pl.pallas_call(functools.partial(transform_kernel, offsets=offsets, block...]
    pallas_call x1, Pallas kernels: 0.68 us -> 2.31 us  [gram(): pl.pallas_call(body, out_shape=jax.ShapeDtypeStruct((members, LANES), f32...]
    ppermute x20, waiting for transfers between devices: 26.3 us -> 24.9 us  [swap(): return lax.ppermute(x, axis, [(k, k ^ bit) for k in range(count)])]
  transfers between devices with their start and end apart: 26 -> 26, of which waited for: 10 -> 12; matrix products, arithmetic and copies ran while one was open for 4% -> 4% of each run, Pallas kernels for 25% -> 26%
where the time goes in v8:
time: 133 us; the launch traced here: 131 us
  Pallas kernels  45.6 us (34%)
  waiting for transfers between devices  37 us (28%)
  starting transfers between devices  34.1 us (26%)
  local copies, waits for them, and re-layouts  12 us (9%)
  other arithmetic  1.77 us (1%)
    pallas_call x1, Pallas kernels, transforms(): pl.pallas_call(functools.partial(transform_kernel, offsets=offsets, block...  28.4 us
    ppermute x20, waiting for transfers between devices, swap(): return lax.ppermute(x, axis, [(k, k ^ bit) for k in range(count)])  24.9 us
    ppermute x20, starting transfers between devices, swap(): return lax.ppermute(x, axis, [(k, k ^ bit) for k in range(count)])  16.2 us
    ppermute x3, starting transfers between devices, halos(): lax.ppermute(last, 'space', forward)  13.8 us
    pallas_call x7, Pallas kernels, forecast_call(): pl.pallas_call(body, out_shape=[jax.ShapeDtypeStruct(shape, f32) for shap...  9.07 us
    ppermute x3, waiting for transfers between devices, halos(): lax.ppermute(last, 'space', forward)  7.25 us
    unnamed x36, local copies, waits for them, and re-layouts  7.02 us
    pallas_call x1, Pallas kernels, mix(): pl.pallas_call(functools.partial(mix_kernel, blocks=blocks, halves=halves...  5.78 us
  transfers between devices with their start and end apart: 26, of which 12 were waited for; matrix products, arithmetic and copies ran while one was open for 4% of the time, Pallas kernels for 26%

profile of v8, /device:TPU:0, one launch (start us, length us, event | category | flops | bytes accessed | tf_op | source)
XLA Modules:
  0.0 130.8 jit_solution(413063425888269681)
XLA Ops:
  0.0 1.6 %fusion = (f32[24,3,2,4,256]{4,3,2,1,0:T(4,128)S(1)}, f32[24,3,2,4,256]{4,3,2,1,0:T(4,128)S(1)}) fusion(f32[24,4,8,4,256]{4,3,2,1,0:T(4,128)} %param.8), kind=kLoop, calls=%fused_computation.8 | loop fusion | bytes 2359296 | tf_op jit(solution)/shard_map/slice | solution.py:624
  1.6 0.4 copy_bitcast_fusion.4
  2.0 0.2 first_edges.1
  2.2 4.9 %collective-permute-start = (f32[4,56,256]{2,1,0:T(8,128)S(1)}, f32[4,56,256]{2,1,0:T(8,128)S(1)}, u32[]{:S(2)}, u32[]{:S(2)}) collective-permute-start(f32[4,56,256]{2,1,0:T(8,128)S(1)} %get-tuple-element.34), channel_id=1, source_target_pairs={{0,1},{1,2},{2,3},{3,4},{4,5},{5,6},{6,7},{8,9},{9,10},{10,11},{11... | collective-permute-start | bytes 688136 | tf_op jit(solution)/shard_map/ppermute | solution.py:589
  7.1 1.3 collective-permute-start.1
  8.4 1.0 fusion.1
  9.4 0.9 copy_bitcast_fusion
  10.3 1.7 %add_add_fusion.refs_4_ = f32[8,4,24,256]{3,2,1,0:T(8,128)S(1)} fusion(f32[24,1,8,4,256]{4,3,2,1,0:T(4,128)S(1)} %get-tuple-element.67, f32[24,1,8,4,256]{4,3,2,1,0:T(4,128)S(1)} %get-tuple-element.66, f32[24,1,8,4,256]{4,3,2,1,0:T(4,128)S(1)} %get-tuple-element.65), kind=kLoop, calls=%fused_computation.4 | loop fusion | flops 393216 | bytes 3145728 | tf_op jit(solution)/shard_map/add | solution.py:635
  12.0 1.1 copy_bitcast_fusion.2
  13.1 3.7 %collective-permute-done.refs_4_.refs_6_.refs_8_.refs_5_ = f32[4,56,256]{2,1,0:T(8,128)S(1)} collective-permute-done((f32[4,56,256]{2,1,0:T(8,128)S(1)}, f32[4,56,256]{2,1,0:T(8,128)S(1)}, u32[]{:S(2)}, u32[]{:S(2)}) %collective-permute-start) | collective-permute-done | bytes 229408 | tf_op jit(solution)/shard_map/ppermute | solution.py:589
  16.9 1.5 %two_substeps.2 = (f32[8,4,24,256]{3,2,1,0:T(8,128)S(1)}, f32[8,4,24,256]{3,2,1,0:T(8,128)S(1)}, f32[8,4,24,256]{3,2,1,0:T(8,128)S(1)}, f32[8,4,24,256]{3,2,1,0:T(8,128)S(1)}) custom-call(f32[8,4,24,256]{3,2,1,0:T(8,128)S(1)} %get-tuple-element.72.refs_0_, f32[8,4,24,256]{3,2,1,0:T(8,128)S(1)} %get-tuple-element.71.refs_1_, ...), custom_call_target="tpu_custom_call" | custom-call | flops 11796480 | bytes 12582912 | tf_op jit(solution)/shard_map/two_substeps/pallas_call | solution.py:285
  18.3 0.0 copy-start
  18.4 0.0 copy-start.13
  18.4 0.0 copy-start.16
  18.4 1.6 %collective-permute-start.7 = (f32[8,4,24,256]{3,2,1,0:T(8,128)S(1)}, f32[8,4,24,256]{3,2,1,0:T(8,128)S(1)}, u32[]{:S(2)}, u32[]{:S(2)}) collective-permute-start(f32[8,4,24,256]{3,2,1,0:T(8,128)S(1)} %add_add_fusion.refs_4_), channel_id=1, source_target_pairs={{0,16},{8,24},{16,0},{24,8},{1,17},{9,25},{17,1},{25,9},{2,18},{10... | collective-permute-start | bytes 2359304 | tf_op jit(solution)/shard_map/ppermute | solution.py:565
  20.0 0.0 collective-permute-start.6
  20.0 0.9 next_edges.2
  20.9 4.4 %collective-permute-start.2 = (f32[4,48,256]{2,1,0:T(8,128)S(1)}, f32[4,48,256]{2,1,0:T(8,128)S(1)}, u32[]{:S(2)}, u32[]{:S(2)}) collective-permute-start(f32[4,48,256]{2,1,0:T(8,128)S(1)} %get-tuple-element.40), channel_id=1, source_target_pairs={{0,1},{1,2},{2,3},{3,4},{4,5},{5,6},{6,7},{8,9},{9,10},{10,11},{11... | collective-permute-start | bytes 589832 | tf_op jit(solution)/shard_map/ppermute | solution.py:589
  25.3 1.3 collective-permute-start.3
  26.6 3.5 %collective-permute-done.2.refs_6_.refs_4_ = f32[4,48,256]{2,1,0:T(8,128)S(1)} collective-permute-done((f32[4,48,256]{2,1,0:T(8,128)S(1)}, f32[4,48,256]{2,1,0:T(8,128)S(1)}, u32[]{:S(2)}, u32[]{:S(2)}) %collective-permute-start.2) | collective-permute-done | bytes 196640 | tf_op jit(solution)/shard_map/ppermute | solution.py:589
  30.1 4.8 %collective-permute-done.3.refs_7_.refs_5_ = f32[4,48,256]{2,1,0:T(8,128)S(1)} collective-permute-done((f32[4,48,256]{2,1,0:T(8,128)S(1)}, f32[4,48,256]{2,1,0:T(8,128)S(1)}, u32[]{:S(2)}, u32[]{:S(2)}) %collective-permute-start.3) | collective-permute-done | bytes 196640 | tf_op jit(solution)/shard_map/ppermute | solution.py:589
  34.9 1.6 %next_edges.3 = (f32[4,48,256]{2,1,0:T(8,128)}, f32[4,48,256]{2,1,0:T(8,128)}) custom-call(f32[8,4,24,256]{3,2,1,0:T(8,128)S(1)} %get-tuple-element.36.refs_2_.refs_0_, f32[8,4,24,256]{3,2,1,0:T(8,128)S(1)} %get-tuple-element.37.refs_3_.refs_1_, f32[8,4,24,256]{3,2,1,0:T(8,128)S(1)} %get-tuple-element.38.refs_4_.refs_2_, ...), custom_call_target="tpu_custom_call" | custom-call | flops 5898240 | bytes 6291456 | tf_op jit(solution)/shard_map/next_edges/pallas_call | solution.py:285
  36.5 4.5 %collective-permute-start.4 = (f32[4,48,256]{2,1,0:T(8,128)}, f32[4,48,256]{2,1,0:T(8,128)S(1)}, u32[]{:S(2)}, u32[]{:S(2)}) collective-permute-start(f32[4,48,256]{2,1,0:T(8,128)} %get-tuple-element.48), channel_id=1, source_target_pairs={{0,1},{1,2},{2,3},{3,4},{4,5},{5,6},{6,7},{8,9},{9,10},{10,11},{11... | collective-permute-start | bytes 589832 | tf_op jit(solution)/shard_map/ppermute | solution.py:589
  41.1 1.5 %collective-permute-start.5 = (f32[4,48,256]{2,1,0:T(8,128)}, f32[4,48,256]{2,1,0:T(8,128)S(1)}, u32[]{:S(2)}, u32[]{:S(2)}) collective-permute-start(f32[4,48,256]{2,1,0:T(8,128)} %get-tuple-element.49), channel_id=1, source_target_pairs={{1,0},{2,1},{3,2},{4,3},{5,4},{6,5},{7,6},{9,8},{10,9},{11,10},{12... | collective-permute-start | bytes 589832 | tf_op jit(solution)/shard_map/ppermute | solution.py:589
  42.6 0.1 pad_add_fusion.refs_0_.place
  42.7 1.1 copy-done.1
  43.8 1.1 copy-done.3
  44.9 1.1 copy-done.5
  46.1 1.1 copy-done.7
  47.2 0.9 copy-done.12
  48.1 0.8 copy-done.14
  48.9 0.8 copy-done.15
  49.6 2.6 %two_substeps.3 = (f32[8,4,24,256]{3,2,1,0:T(8,128)S(1)}, f32[8,4,24,256]{3,2,1,0:T(8,128)S(1)}, f32[8,4,24,256]{3,2,1,0:T(8,128)S(1)}, f32[8,4,24,256]{3,2,1,0:...) custom-call(s32[3]{0:T(128)S(1)} %pad_add_fusion.refs_0_.place, s32[4]{0:T(128)S(1)} %copy-done.16, ...), custom_call_target="tpu_custom_call" | custom-call | flops 11796480 | bytes 12582912 | tf_op jit(solution)/shard_map/two_substeps/pallas_call | solution.py:285
  52.3 0.0 collective-permute-done.5.refs_6_.refs_4_
  52.3 0.0 collective-permute-done.7.refs_11_.refs_6_
  52.3 1.8 %last_but_one.1 = (f32[4,4,24,256]{3,2,1,0:T(8,128)S(1)}, f32[4,4,24,256]{3,2,1,0:T(8,128)S(1)}, f32[8,4,24,256]{3,2,1,0:T(8,128)S(1)}, f32[8,4,24,256]{3,2,1,0:T(8,128)S(1)}, f32[8,4,24,256]{3,2,1,0:T(8,128)S(1)}) custom-call(s32[3]{0:T(128)S(1)} %pad_add_fusion.refs_0_.place, f32[8,4,24,256]{3,2,1,0:T(8,128)S(1)} %get-tuple-element.44.refs_1_.refs_0_, ...), custom_call_target="tpu_custom_call" | custom-call | flops 11796480 | bytes 12582912 | tf_op jit(solution)/shard_map/last_but_one/pallas_call | solution.py:285
  54.1 0.6 collective-permute-start.9
  54.7 0.5 collective-permute-start.8
  55.2 9.1 %collective-permute-done.9.refs_6_.refs_14_ = f32[4,4,24,256]{3,2,1,0:T(8,128)S(1)} collective-permute-done((f32[4,4,24,256]{3,2,1,0:T(8,128)S(1)}, f32[4,4,24,256]{3,2,1,0:T(8,128)S(1)}, u32[]{:S(2)}, u32[]{:S(2)}) %collective-permute-start.9) | collective-permute-done | bytes 393248 | tf_op jit(solution)/shard_map/ppermute | solution.py:565
  64.3 1.7 %collective-permute-done.10.refs_7_.refs_15_ = f32[4,4,24,256]{3,2,1,0:T(8,128)S(1)} collective-permute-done((f32[4,4,24,256]{3,2,1,0:T(8,128)S(1)}, f32[4,4,24,256]{3,2,1,0:T(8,128)S(1)}, u32[]{:S(2)}, u32[]{:S(2)}) %collective-permute-start.10) | collective-permute-done | bytes 393248 | tf_op jit(solution)/shard_map/ppermute | solution.py:565
  66.1 2.3 %gram.1 = f32[96,128]{1,0:T(8,128)S(1)} custom-call(s32[3]{0:T(128)S(1)} %pad_add_fusion.refs_0_.place, s32[4]{0:T(128)S(1)} %copy-done.16, f32[2,32,256]{2,1,0:T(8,128)S(1)} %get-tuple-element.42.refs_2_, f32[2,32,256]{2,1,0:T(8,128)S(1)} %get-tuple-element.43.refs_3_, f32[4,4,24,256]{3,2,1,0:T(8,128)S(1)} %get-tuple-element.61.refs_4_.refs_12_, ...), custom_call_target="tpu_custom_call" | custom-call | tf_op jit(solution)/shard_map/gram/pallas_call | solution.py:388
  68.4 0.6 collective-permute-start.12
  69.0 0.5 last_free.1.refs_0_
  69.5 3.1 %collective-permute-done.12 = f32[96,128]{1,0:T(8,128)S(1)} collective-permute-done((f32[96,128]{1,0:T(8,128)S(1)}, f32[96,128]{1,0:T(8,128)S(1)}, u32[]{:S(2)}, u32[]{:S(2)}) %collective-permute-start.12) | collective-permute-done | bytes 49184 | tf_op jit(solution)/shard_map/ppermute | solution.py:565
  72.6 0.6 collective-permute-start.18
  73.1 1.5 %collective-permute-start.21 = (f32[8,4,24,256]{3,2,1,0:T(8,128)S(1)}, f32[8,4,24,256]{3,2,1,0:T(8,128)S(1)}, u32[]{:S(2)}, u32[]{:S(2)}) collective-permute-start(f32[8,4,24,256]{3,2,1,0:T(8,128)S(1)} %get-tuple-element.59.refs_8_), channel_id=1, source_target_pairs={{0,16},{8,24},{16,0},{24,8},{1,17},{9,25},{17,1},{25,9},{2,18},{10... | collective-permute-start | bytes 2359304 | tf_op jit(solution)/shard_map/ppermute | solution.py:565
  74.6 2.2 %collective-permute-start.13 = (f32[96,128]{1,0:T(8,128)S(1)}, f32[96,128]{1,0:T(8,128)S(1)}, u32[]{:S(2)}, u32[]{:S(2)}) collective-permute-start(f32[96,128]{1,0:T(8,128)S(1)} %add.20), channel_id=1, source_target_pairs={{0,1},{1,0},{2,3},{3,2},{4,5},{5,4},{6,7},{7,6},{8,9},{9,8},{10,11... | collective-permute-start | bytes 147464 | tf_op jit(solution)/shard_map/ppermute | solution.py:565
  76.9 2.1 %collective-permute-done.13 = f32[96,128]{1,0:T(8,128)S(1)} collective-permute-done((f32[96,128]{1,0:T(8,128)S(1)}, f32[96,128]{1,0:T(8,128)S(1)}, u32[]{:S(2)}, u32[]{:S(2)}) %collective-permute-start.13) | collective-permute-done | bytes 49184 | tf_op jit(solution)/shard_map/ppermute | solution.py:565
  78.9 3.3 %collective-permute-start.14 = (f32[96,128]{1,0:T(8,128)S(1)}, f32[96,128]{1,0:T(8,128)S(1)}, u32[]{:S(2)}, u32[]{:S(2)}) collective-permute-start(f32[96,128]{1,0:T(8,128)S(1)} %add.21), channel_id=1, source_target_pairs={{0,2},{1,3},{2,0},{3,1},{4,6},{5,7},{6,4},{7,5},{8,10},{9,11},{10,... | collective-permute-start | bytes 147464 | tf_op jit(solution)/shard_map/ppermute | solution.py:565
  82.2 2.1 %collective-permute-done.14 = f32[96,128]{1,0:T(8,128)S(1)} collective-permute-done((f32[96,128]{1,0:T(8,128)S(1)}, f32[96,128]{1,0:T(8,128)S(1)}, u32[]{:S(2)}, u32[]{:S(2)}) %collective-permute-start.14) | collective-permute-done | bytes 49184 | tf_op jit(solution)/shard_map/ppermute | solution.py:565
  84.3 3.1 %collective-permute-start.15 = (f32[96,128]{1,0:T(8,128)S(1)}, f32[96,128]{1,0:T(8,128)S(1)}, u32[]{:S(2)}, u32[]{:S(2)}) collective-permute-start(f32[96,128]{1,0:T(8,128)S(1)} %add.22), channel_id=1, source_target_pairs={{0,4},{1,5},{2,6},{3,7},{4,0},{5,1},{6,2},{7,3},{8,12},{9,13},{10,... | collective-permute-start | bytes 147464 | tf_op jit(solution)/shard_map/ppermute | solution.py:565
  87.4 2.1 %collective-permute-done.15 = f32[96,128]{1,0:T(8,128)S(1)} collective-permute-done((f32[96,128]{1,0:T(8,128)S(1)}, f32[96,128]{1,0:T(8,128)S(1)}, u32[]{:S(2)}, u32[]{:S(2)}) %collective-permute-start.15) | collective-permute-done | bytes 49184 | tf_op jit(solution)/shard_map/ppermute | solution.py:565
  89.4 0.6 collective-permute-start.24
  90.0 0.5 collective-permute-start.23
  90.5 0.7 collective-permute-done.16.other
  91.2 0.2 collective-permute-start.17
  91.4 28.4 %transforms.1.weights = f32[24,128]{1,0:T(8,128)S(1)} custom-call(s32[3]{0:T(128)S(1)} %pad_add_fusion.refs_0_.place, f32[96,128]{1,0:T(8,128)S(1)} %add.23.mine, f32[96,128]{1,0:T(8,128)S(1)} %collective-permute-done.16.other), custom_call_target="tpu_custom_call" | custom-call | flops 100000000 | bytes 1000000 | tf_op jit(solution)/shard_map/transforms/pallas_call | solution.py:486
  119.8 0.4 collective-permute-start.20
  120.2 0.2 collective-permute-start.19
  120.4 0.4 collective-permute-start.22
  120.8 0.2 collective-permute-start.25
  120.9 1.2 collective-permute-done.20.refs_9_
  122.2 2.8 %collective-permute-done.25.refs_19_ = f32[4,4,24,256]{3,2,1,0:T(8,128)S(1)} collective-permute-done((f32[4,4,24,256]{3,2,1,0:T(8,128)S(1)}, f32[4,4,24,256]{3,2,1,0:T(8,128)S(1)}, u32[]{:S(2)}, u32[]{:S(2)}) %collective-permute-start.25) | collective-permute-done | bytes 393248 | tf_op jit(solution)/shard_map/ppermute | solution.py:565
  125.0 5.8 %mix.1 = f32[24,4,8,4,256]{4,3,2,1,0:T(4,128)} custom-call(s32[3]{0:T(128)S(1)} %pad_add_fusion.refs_0_.place, f32[24,128]{1,0:T(8,128)S(1)} %transforms.1.weights, f32[8,4,24,256]{3,2,1,0:T(8,128)S(1)} %last_free.1.refs_0_, f32[8,4,24,256]{3,2,1,0:T(8,128)S(1)} %collective-permute-done.17.refs_1_, f32[8,4,24,256]{3,2,1,0:T(8,128)S(1)} %collective-permute-done.18.refs_2_, ...), custom_call_target="tpu_custom_call" | custom-call | tf_op jit(solution)/shard_map/mix/pallas_call | solution.py:549
  (45 shorter events, 0.1 us)
Async XLA Ops:
  0.0 8.4 %copy-start.17 = (f32[24,4,8,4,256]{4,3,2,1,0:T(4,128)S(1)}, f32[24,4,8,4,256]{4,3,2,1,0:T(4,128)}, u32[]{:S(2)}) copy-start(f32[24,4,8,4,256]{4,3,2,1,0:T(4,128)} %param.8) | copy-start | bytes 9437188
  0.0 2.0 %copy-start.8 = (f32[8,4,256]{2,1,0:T(4,128)S(1)}, f32[8,4,256]{2,1,0:T(4,128)}, u32[]{:S(2)}) copy-start(f32[8,4,256]{2,1,0:T(4,128)} %refs_7_.3) | copy-start | bytes 98308
  0.0 2.0 %copy-start.10 = (f32[8,4,256]{2,1,0:T(4,128)S(1)}, f32[8,4,256]{2,1,0:T(4,128)}, u32[]{:S(2)}) copy-start(f32[8,4,256]{2,1,0:T(4,128)} %refs_9_.7) | copy-start | bytes 98308
  0.0 2.0 %copy-start.9 = (f32[8,4,256]{2,1,0:T(4,128)S(1)}, f32[8,4,256]{2,1,0:T(4,128)}, u32[]{:S(2)}) copy-start(f32[8,4,256]{2,1,0:T(4,128)} %refs_8_.7) | copy-start | bytes 98308
  2.2 14.6 %collective-permute-start = (f32[4,56,256]{2,1,0:T(8,128)S(1)}, f32[4,56,256]{2,1,0:T(8,128)S(1)}, u32[]{:S(2)}, u32[]{:S(2)}) collective-permute-start(f32[4,56,256]{2,1,0:T(8,128)S(1)} %get-tuple-element.34), channel_id=1, source_target_pairs={{0,1},{1,2},{2,3},{3,4},{4,5},{5,6},{6,7},{8,9},{9,10},{10,11},{11... | collective-permute-start | bytes 688136 | tf_op jit(solution)/shard_map/ppermute | solution.py:589
  7.1 9.7 %collective-permute-start.1 = (f32[4,56,256]{2,1,0:T(8,128)S(1)}, f32[4,56,256]{2,1,0:T(8,128)S(1)}, u32[]{:S(2)}, u32[]{:S(2)}) collective-permute-start(f32[4,56,256]{2,1,0:T(8,128)S(1)} %get-tuple-element.35), channel_id=1, source_target_pairs={{1,0},{2,1},{3,2},{4,3},{5,4},{6,5},{7,6},{9,8},{10,9},{11,10},{12... | collective-permute-start | bytes 688136 | tf_op jit(solution)/shard_map/ppermute | solution.py:589
  18.3 18.2 %copy-start = (f32[8,4,24,256]{3,2,1,0:T(8,128)}, f32[8,4,24,256]{3,2,1,0:T(8,128)S(1)}, u32[]{:S(2)}) copy-start(f32[8,4,24,256]{3,2,1,0:T(8,128)S(1)} %get-tuple-element.36.refs_2_.refs_0_) | copy-start | bytes 2359300
  18.3 18.2 %copy-start.2 = (f32[8,4,24,256]{3,2,1,0:T(8,128)}, f32[8,4,24,256]{3,2,1,0:T(8,128)S(1)}, u32[]{:S(2)}) copy-start(f32[8,4,24,256]{3,2,1,0:T(8,128)S(1)} %get-tuple-element.37.refs_3_.refs_1_) | copy-start | bytes 2359300
  18.3 18.2 %copy-start.4 = (f32[8,4,24,256]{3,2,1,0:T(8,128)}, f32[8,4,24,256]{3,2,1,0:T(8,128)S(1)}, u32[]{:S(2)}) copy-start(f32[8,4,24,256]{3,2,1,0:T(8,128)S(1)} %get-tuple-element.38.refs_4_.refs_2_) | copy-start | bytes 2359300
  18.4 18.2 %copy-start.6 = (f32[8,4,24,256]{3,2,1,0:T(8,128)}, f32[8,4,24,256]{3,2,1,0:T(8,128)S(1)}, u32[]{:S(2)}) copy-start(f32[8,4,24,256]{3,2,1,0:T(8,128)S(1)} %get-tuple-element.39.refs_5_.refs_3_) | copy-start | bytes 2359300
  18.4 24.3 %copy-start.13 = (s32[4,2048]{1,0:T(4,128)S(1)}, s32[4,2048]{1,0:T(4,128)}, u32[]{:S(2)}) copy-start(s32[4,2048]{1,0:T(4,128)} %refs_13_.1) | copy-start | bytes 98308
  18.4 24.3 %copy-start.16 = (s32[4]{0:T(128)S(1)}, s32[4]{0:T(128)}, u32[]{:S(2)}) copy-start(s32[4]{0:T(128)} %refs_1_.3) | copy-start | bytes 52
  18.4 33.9 %collective-permute-start.7 = (f32[8,4,24,256]{3,2,1,0:T(8,128)S(1)}, f32[8,4,24,256]{3,2,1,0:T(8,128)S(1)}, u32[]{:S(2)}, u32[]{:S(2)}) collective-permute-start(f32[8,4,24,256]{3,2,1,0:T(8,128)S(1)} %add_add_fusion.refs_4_), channel_id=1, source_target_pairs={{0,16},{8,24},{16,0},{24,8},{1,17},{9,25},{17,1},{25,9},{2,18},{10... | collective-permute-start | bytes 2359304 | tf_op jit(solution)/shard_map/ppermute | solution.py:565
  20.0 32.3 %collective-permute-start.6 = (f32[8,4,24,256]{3,2,1,0:T(8,128)S(1)}, f32[8,4,24,256]{3,2,1,0:T(8,128)S(1)}, u32[]{:S(2)}, u32[]{:S(2)}) collective-permute-start(f32[8,4,24,256]{3,2,1,0:T(8,128)S(1)} %add_add_fusion.refs_4_), channel_id=1, source_target_pairs={{0,8},{8,0},{16,24},{24,16},{1,9},{9,1},{17,25},{25,17},{2,10},{10... | collective-permute-start | bytes 2359304 | tf_op jit(solution)/shard_map/ppermute | solution.py:565
  20.9 9.2 %collective-permute-start.2 = (f32[4,48,256]{2,1,0:T(8,128)S(1)}, f32[4,48,256]{2,1,0:T(8,128)S(1)}, u32[]{:S(2)}, u32[]{:S(2)}) collective-permute-start(f32[4,48,256]{2,1,0:T(8,128)S(1)} %get-tuple-element.40), channel_id=1, source_target_pairs={{0,1},{1,2},{2,3},{3,4},{4,5},{5,6},{6,7},{8,9},{9,10},{10,11},{11... | collective-permute-start | bytes 589832 | tf_op jit(solution)/shard_map/ppermute | solution.py:589
  25.3 9.6 %collective-permute-start.3 = (f32[4,48,256]{2,1,0:T(8,128)S(1)}, f32[4,48,256]{2,1,0:T(8,128)S(1)}, u32[]{:S(2)}, u32[]{:S(2)}) collective-permute-start(f32[4,48,256]{2,1,0:T(8,128)S(1)} %get-tuple-element.41), channel_id=1, source_target_pairs={{1,0},{2,1},{3,2},{4,3},{5,4},{6,5},{7,6},{9,8},{10,9},{11,10},{12... | collective-permute-start | bytes 589832 | tf_op jit(solution)/shard_map/ppermute | solution.py:589
  34.9 1.6 %copy-start.11 = (f32[4,48,256]{2,1,0:T(8,128)}, f32[4,48,256]{2,1,0:T(8,128)S(1)}, u32[]{:S(2)}) copy-start(f32[4,48,256]{2,1,0:T(8,128)S(1)} %collective-permute-done.3.refs_7_.refs_5_) | copy-start | bytes 589828
  36.5 15.7 %collective-permute-start.4 = (f32[4,48,256]{2,1,0:T(8,128)}, f32[4,48,256]{2,1,0:T(8,128)S(1)}, u32[]{:S(2)}, u32[]{:S(2)}) collective-permute-start(f32[4,48,256]{2,1,0:T(8,128)} %get-tuple-element.48), channel_id=1, source_target_pairs={{0,1},{1,2},{2,3},{3,4},{4,5},{5,6},{6,7},{8,9},{9,10},{10,11},{11... | collective-permute-start | bytes 589832 | tf_op jit(solution)/shard_map/ppermute | solution.py:589
  41.1 11.2 %collective-permute-start.5 = (f32[4,48,256]{2,1,0:T(8,128)}, f32[4,48,256]{2,1,0:T(8,128)S(1)}, u32[]{:S(2)}, u32[]{:S(2)}) collective-permute-start(f32[4,48,256]{2,1,0:T(8,128)} %get-tuple-element.49), channel_id=1, source_target_pairs={{1,0},{2,1},{3,2},{4,3},{5,4},{6,5},{7,6},{9,8},{10,9},{11,10},{12... | collective-permute-start | bytes 589832 | tf_op jit(solution)/shard_map/ppermute | solution.py:589
  42.7 1.1 copy-start.1
  43.8 1.1 copy-start.3
  44.9 1.1 copy-start.5
  46.1 1.1 copy-start.7
  47.2 0.9 copy-start.12
  48.1 0.8 copy-start.14
  48.9 0.8 copy-start.15
  54.1 10.2 %collective-permute-start.9 = (f32[4,4,24,256]{3,2,1,0:T(8,128)S(1)}, f32[4,4,24,256]{3,2,1,0:T(8,128)S(1)}, u32[]{:S(2)}, u32[]{:S(2)}) collective-permute-start(f32[4,4,24,256]{3,2,1,0:T(8,128)S(1)} %get-tuple-element.52.refs_16_), channel_id=1, source_target_pairs={{0,16},{8,24},{16,0},{24,8},{1,17},{9,25},{17,1},{25,9},{2,18},{10... | collective-permute-start | bytes 1179656 | tf_op jit(solution)/shard_map/ppermute | solution.py:565
  54.7 11.4 %collective-permute-start.11 = (f32[8,4,24,256]{3,2,1,0:T(8,128)S(1)}, f32[8,4,24,256]{3,2,1,0:T(8,128)S(1)}, u32[]{:S(2)}, u32[]{:S(2)}) collective-permute-start(f32[8,4,24,256]{3,2,1,0:T(8,128)S(1)} %collective-permute-done.7.refs_11_.refs_6_), channel_id=1, source_target_pairs={{0,8},{8,0},{16,24},{24,16},{1,9},{9,1},{17,25},{25,17},{2,10},{10... | collective-permute-start | bytes 2359304 | tf_op jit(solution)/shard_map/ppermute | solution.py:565
  54.7 9.6 %collective-permute-start.8 = (f32[4,4,24,256]{3,2,1,0:T(8,128)S(1)}, f32[4,4,24,256]{3,2,1,0:T(8,128)S(1)}, u32[]{:S(2)}, u32[]{:S(2)}) collective-permute-start(f32[4,4,24,256]{3,2,1,0:T(8,128)S(1)} %get-tuple-element.61.refs_4_.refs_12_), channel_id=1, source_target_pairs={{0,8},{8,0},{16,24},{24,16},{1,9},{9,1},{17,25},{25,17},{2,10},{10... | collective-permute-start | bytes 1179656 | tf_op jit(solution)/shard_map/ppermute | solution.py:565
  64.3 1.7 %collective-permute-start.10 = (f32[4,4,24,256]{3,2,1,0:T(8,128)S(1)}, f32[4,4,24,256]{3,2,1,0:T(8,128)S(1)}, u32[]{:S(2)}, u32[]{:S(2)}) collective-permute-start(f32[4,4,24,256]{3,2,1,0:T(8,128)S(1)} %collective-permute-done.9.refs_6_.refs_14_), channel_id=1, source_target_pairs={{0,8},{8,0},{16,24},{24,16},{1,9},{9,1},{17,25},{25,17},{2,10},{10... | collective-permute-start | bytes 1179656 | tf_op jit(solution)/shard_map/ppermute | solution.py:565
  68.4 4.2 %collective-permute-start.12 = (f32[96,128]{1,0:T(8,128)S(1)}, f32[96,128]{1,0:T(8,128)S(1)}, u32[]{:S(2)}, u32[]{:S(2)}) collective-permute-start(f32[96,128]{1,0:T(8,128)S(1)} %gram.1), channel_id=1, source_target_pairs={{0,16},{8,24},{16,0},{24,8},{1,17},{9,25},{17,1},{25,9},{2,18},{10... | collective-permute-start | bytes 147464 | tf_op jit(solution)/shard_map/ppermute | solution.py:565
  72.6 47.3 %collective-permute-start.18 = (f32[8,4,24,256]{3,2,1,0:T(8,128)S(1)}, f32[8,4,24,256]{3,2,1,0:T(8,128)S(1)}, u32[]{:S(2)}, u32[]{:S(2)}) collective-permute-start(f32[8,4,24,256]{3,2,1,0:T(8,128)S(1)} %last_free.1.refs_0_), channel_id=1, source_target_pairs={{0,16},{8,24},{16,0},{24,8},{1,17},{9,25},{17,1},{25,9},{2,18},{10... | collective-permute-start | bytes 2359304 | tf_op jit(solution)/shard_map/ppermute | solution.py:565
  73.1 47.1 %collective-permute-start.21 = (f32[8,4,24,256]{3,2,1,0:T(8,128)S(1)}, f32[8,4,24,256]{3,2,1,0:T(8,128)S(1)}, u32[]{:S(2)}, u32[]{:S(2)}) collective-permute-start(f32[8,4,24,256]{3,2,1,0:T(8,128)S(1)} %get-tuple-element.59.refs_8_), channel_id=1, source_target_pairs={{0,16},{8,24},{16,0},{24,8},{1,17},{9,25},{17,1},{25,9},{2,18},{10... | collective-permute-start | bytes 2359304 | tf_op jit(solution)/shard_map/ppermute | solution.py:565
  74.6 4.3 %collective-permute-start.13 = (f32[96,128]{1,0:T(8,128)S(1)}, f32[96,128]{1,0:T(8,128)S(1)}, u32[]{:S(2)}, u32[]{:S(2)}) collective-permute-start(f32[96,128]{1,0:T(8,128)S(1)} %add.20), channel_id=1, source_target_pairs={{0,1},{1,0},{2,3},{3,2},{4,5},{5,4},{6,7},{7,6},{8,9},{9,8},{10,11... | collective-permute-start | bytes 147464 | tf_op jit(solution)/shard_map/ppermute | solution.py:565
  78.9 5.3 %collective-permute-start.14 = (f32[96,128]{1,0:T(8,128)S(1)}, f32[96,128]{1,0:T(8,128)S(1)}, u32[]{:S(2)}, u32[]{:S(2)}) collective-permute-start(f32[96,128]{1,0:T(8,128)S(1)} %add.21), channel_id=1, source_target_pairs={{0,2},{1,3},{2,0},{3,1},{4,6},{5,7},{6,4},{7,5},{8,10},{9,11},{10,... | collective-permute-start | bytes 147464 | tf_op jit(solution)/shard_map/ppermute | solution.py:565
  84.3 5.2 %collective-permute-start.15 = (f32[96,128]{1,0:T(8,128)S(1)}, f32[96,128]{1,0:T(8,128)S(1)}, u32[]{:S(2)}, u32[]{:S(2)}) collective-permute-start(f32[96,128]{1,0:T(8,128)S(1)} %add.22), channel_id=1, source_target_pairs={{0,4},{1,5},{2,6},{3,7},{4,0},{5,1},{6,2},{7,3},{8,12},{9,13},{10,... | collective-permute-start | bytes 147464 | tf_op jit(solution)/shard_map/ppermute | solution.py:565
  89.4 31.0 %collective-permute-start.24 = (f32[4,4,24,256]{3,2,1,0:T(8,128)S(1)}, f32[4,4,24,256]{3,2,1,0:T(8,128)S(1)}, u32[]{:S(2)}, u32[]{:S(2)}) collective-permute-start(f32[4,4,24,256]{3,2,1,0:T(8,128)S(1)} %get-tuple-element.61.refs_4_.refs_12_), channel_id=1, source_target_pairs={{0,16},{8,24},{16,0},{24,8},{1,17},{9,25},{17,1},{25,9},{2,18},{10... | collective-permute-start | bytes 1179656 | tf_op jit(solution)/shard_map/ppermute | solution.py:565
  90.0 1.2 collective-permute-start.16
  90.0 30.7 %collective-permute-start.23 = (f32[4,4,24,256]{3,2,1,0:T(8,128)S(1)}, f32[4,4,24,256]{3,2,1,0:T(8,128)S(1)}, u32[]{:S(2)}, u32[]{:S(2)}) collective-permute-start(f32[4,4,24,256]{3,2,1,0:T(8,128)S(1)} %get-tuple-element.52.refs_16_), channel_id=1, source_target_pairs={{0,8},{8,0},{16,24},{24,16},{1,9},{9,1},{17,25},{25,17},{2,10},{10... | collective-permute-start | bytes 1179656 | tf_op jit(solution)/shard_map/ppermute | solution.py:565
  91.2 29.7 %collective-permute-start.17 = (f32[8,4,24,256]{3,2,1,0:T(8,128)S(1)}, f32[8,4,24,256]{3,2,1,0:T(8,128)S(1)}, u32[]{:S(2)}, u32[]{:S(2)}) collective-permute-start(f32[8,4,24,256]{3,2,1,0:T(8,128)S(1)} %last_free.1.refs_0_), channel_id=1, source_target_pairs={{0,8},{8,0},{16,24},{24,16},{1,9},{9,1},{17,25},{25,17},{2,10},{10... | collective-permute-start | bytes 2359304 | tf_op jit(solution)/shard_map/ppermute | solution.py:565
  119.8 2.4 %collective-permute-start.20 = (f32[8,4,24,256]{3,2,1,0:T(8,128)S(1)}, f32[8,4,24,256]{3,2,1,0:T(8,128)S(1)}, u32[]{:S(2)}, u32[]{:S(2)}) collective-permute-start(f32[8,4,24,256]{3,2,1,0:T(8,128)S(1)} %get-tuple-element.59.refs_8_), channel_id=1, source_target_pairs={{0,8},{8,0},{16,24},{24,16},{1,9},{9,1},{17,25},{25,17},{2,10},{10... | collective-permute-start | bytes 2359304 | tf_op jit(solution)/shard_map/ppermute | solution.py:565
  120.2 4.7 %collective-permute-start.19 = (f32[8,4,24,256]{3,2,1,0:T(8,128)S(1)}, f32[8,4,24,256]{3,2,1,0:T(8,128)S(1)}, u32[]{:S(2)}, u32[]{:S(2)}) collective-permute-start(f32[8,4,24,256]{3,2,1,0:T(8,128)S(1)} %collective-permute-done.18.refs_2_), channel_id=1, source_target_pairs={{0,8},{8,0},{16,24},{24,16},{1,9},{9,1},{17,25},{25,17},{2,10},{10... | collective-permute-start | bytes 2359304 | tf_op jit(solution)/shard_map/ppermute | solution.py:565
  120.4 4.6 %collective-permute-start.22 = (f32[8,4,24,256]{3,2,1,0:T(8,128)S(1)}, f32[8,4,24,256]{3,2,1,0:T(8,128)S(1)}, u32[]{:S(2)}, u32[]{:S(2)}) collective-permute-start(f32[8,4,24,256]{3,2,1,0:T(8,128)S(1)} %collective-permute-done.21.refs_10_), channel_id=1, source_target_pairs={{0,8},{8,0},{16,24},{24,16},{1,9},{9,1},{17,25},{25,17},{2,10},{10... | collective-permute-start | bytes 2359304 | tf_op jit(solution)/shard_map/ppermute | solution.py:565
  120.8 4.2 %collective-permute-start.25 = (f32[4,4,24,256]{3,2,1,0:T(8,128)S(1)}, f32[4,4,24,256]{3,2,1,0:T(8,128)S(1)}, u32[]{:S(2)}, u32[]{:S(2)}) collective-permute-start(f32[4,4,24,256]{3,2,1,0:T(8,128)S(1)} %collective-permute-done.24.refs_18_), channel_id=1, source_target_pairs={{0,8},{8,0},{16,24},{24,16},{1,9},{9,1},{17,25},{25,17},{2,10},{10... | collective-permute-start | bytes 1179656 | tf_op jit(solution)/shard_map/ppermute | solution.py:565

commit v9 on v7

--- a/solution.py
+++ b/solution.py
@@ -90,7 +90,7 @@
     return spread_free(read(x, z), beside(read, x, z, nx, nz, None, None), None, diffusivity) + rest
 
 
-def first_edges_kernel(below, above, diffusivity, binding, source, first, last):
+def first_edges_kernel(place, below, above, diffusivity, binding, source, first, last):
     _, _, nz, members, _ = below.shape
     nx = diffusivity.shape[0]
     for x, ends, out in ((0, below, first), (nx - 1, above, last)):
@@ -219,55 +219,96 @@
     )
 
 
-def last_but_one_kernel(
-    place, a, r, c, i, low, high, diffusivity, binding, source, *refs, halves
+def last_steps_kernel(
+    a, r, c, i, low, high, low_first, high_first, diffusivity, binding, source, *refs
 ):
-    *tracers, out_i, out_a, out_add, mid_r, mid_c, mid_i = refs
-    nx, nz, _, _ = a.shape
-    step_planes(
-        range(nx),
+    *outs, m0, m1, m2, m3, later_r, later_c, later_i = refs
+    before, first, last, free, tracer, inside, add, ends = outs
+    nx, nz, members, _ = a.shape
+    coefficients = (diffusivity, binding, source)
+    two_substeps_kernel(
         a,
         r,
         c,
         i,
-        before_last(a, low, high),
-        diffusivity,
-        binding,
-        source,
-        out_a,
-        (mid_r, mid_c, mid_i),
+        low,
+        high,
+        low_first,
+        high_first,
+        *coefficients,
+        before,
+        later_r,
+        later_c,
+        later_i,
+        m0,
+        m1,
+        m2,
+        m3,
+    )
+    step_planes(
         range(nx),
-    )
-    span = nx // halves
-    for part, tracer in enumerate(tracers):
-        begin = half_begin(place, part, span)
-        for j in range(span):
-            x = j if halves == 1 else begin + j
-            for z in range(nz):
-                row = pl.ds(z, 1)
-                back, _, complexed, internal = react(
-                    out_a[x, z], mid_r[x, z], mid_c[x, z], mid_i[x, z], binding[x, row, :]
-                )
-                tracer[j, z] = complexed + internal
-                out_i[x, z] = internal
-                out_add[x, z] = back + source[x, row, :]
-
-
-def last_free_kernel(
-    before, a, add, low, high, low_first, high_first, diffusivity, out_a
-):
-    nx, nz, _, _ = a.shape
-    outside = after_first(before, low, high, low_first, high_first)
+        before,
+        later_r,
+        later_c,
+        later_i,
+        lambda x, z: (None, None),
+        *coefficients,
+        free,
+        (m1, m2, m3),
+        range(nx),
+    )
     for x in range(nx):
         for z in range(nz):
-            around = beside(lambda x, z: a[x, z], x, z, nx, nz, *outside(x, z))
-            out_a[x, z] = (
-                spread_free(a[x, z], around, None, diffusivity[x, pl.ds(z, 1), :]) + add[x, z]
+            row = pl.ds(z, 1)
+            back, _, complexed, internal = react(
+                free[x, z], m1[x, z], m2[x, z], m3[x, z], binding[x, row, :]
             )
-
-
-def half_begin(place, part, span):
-    return jnp.bitwise_xor(part, lax.shift_right_logical(place[2], 1)) * span
+            inside[x, z] = internal
+            if 0 < x < nx - 1:
+                tracer[x - 1, z] = complexed + internal
+                add[x - 1, z] = back + source[x, row, :]
+                continue
+            ends[0, x // (nx - 1), z] = m1[x, z]
+            ends[1, x // (nx - 1), z] = m2[x, z]
+            ends[2, x // (nx - 1), z] = m3[x, z]
+    for x, out in ((0, first), (nx - 1, last)):
+        for z in range(nz):
+            out[z, :members, :] = before[x, z]
+            out[z, members:, :] = free[x, z]
+
+
+def last_ends_kernel(
+    free, ends, low, high, diffusivity, binding, source, tracer, out_free, add
+):
+    nx, nz, members, _ = free.shape
+    for end, (x, halo) in enumerate(((0, low), (nx - 1, high))):
+        for z in range(nz):
+            row = pl.ds(z, 1)
+            value = free[x, z] + diffusivity[x, row, :] * halo[z, :members, :]
+            back, _, complexed, internal = react(
+                value, ends[0, end, z], ends[1, end, z], ends[2, end, z], binding[x, row, :]
+            )
+            tracer[end, z] = complexed + internal
+            out_free[end, z] = value
+            add[end, z] = back + source[x, row, :]
+
+
+def last_free_kernel(
+    before, free, free_ends, add, add_ends, low, high, low_first, high_first, diffusivity, out
+):
+    nx, nz, _, _ = free.shape
+    outside = after_first(before, low, high, low_first, high_first)
+
+    def read(x, z):
+        return free[x, z] if 0 < x < nx - 1 else free_ends[x // (nx - 1), z]
+
+    for x in range(nx):
+        for z in range(nz):
+            around = beside(read, x, z, nx, nz, *outside(x, z))
+            rest = add[x - 1, z] if 0 < x < nx - 1 else add_ends[x // (nx - 1), z]
+            out[x, z] = (
+                spread_free(read(x, z), around, None, diffusivity[x, pl.ds(z, 1), :]) + rest
+            )
 
 
 def forecast_call(kernel, name, inputs, outputs, cells, scratch=(), ready=(), scalars=()):
@@ -337,35 +378,40 @@
     )(place, owner, obs_index, observed, obs_var)
 
 
-def gram_kernel(place, owner, omega, eta, *refs, offsets, halves):
-    *sources, packed, out, members_at = refs
+def gram_kernel(place, owner, omega, eta, *refs, offsets, planes, first):
+    if first:
+        *sources, out, members_at = refs
+    else:
+        begun, *sources, packed, out, members_at = refs
     count = out.shape[0]
     span, nz, rows, ny = sources[0].shape
     members = members_at.shape[0]
-    begin = 0 if halves == 1 else lax.shift_right_logical(place[2], 1) * (span * nz)
     for k in range(count):
-        out[k] = jnp.zeros(out.shape[1:], f32)
+        out[k] = jnp.zeros(out.shape[1:], f32) if first else begun[k]
 
         @pl.when(owner[place[0] * count + k] == place[1])
         def _(k=k):
             def tile(t, total):
                 x, z = t // nz, t % nz
+                voxels = pl.ds((planes[0] + x * planes[1]) * nz + z, 1)
                 for j, source in enumerate(sources):
                     start = pl.multiple_of(offsets(place[2], j), 8)
                     members_at[pl.ds(start, rows), :] = source[x, z]
                 values = members_at[...]
                 mean = jnp.sum(values, axis=0, keepdims=True) * (1.0 / members)
                 spread = values - mean
-                weight = omega[k, pl.ds(begin + t, 1), :]
-                shift = eta[k, pl.ds(begin + t, 1), :] - weight * mean
+                weight = omega[k, voxels, :]
+                shift = eta[k, voxels, :] - weight * mean
                 tail = lax.broadcasted_iota(jnp.int32, (LANES - members, ny), 0)
                 weighted = jnp.concatenate(
                     [spread * weight, jnp.where(tail == 0, shift, 0.0)], axis=0
                 )
                 return total + dot_parts(split(spread), split(weighted), NT)
 
-            out[k] = lax.fori_loop(0, span * nz, tile, jnp.zeros(out.shape[1:], f32), unroll=4)
-
+            out[k] = lax.fori_loop(0, span * nz, tile, out[k], unroll=4)
+
+    if first:
+        return
     row = lax.broadcasted_iota(jnp.int32, (members, LANES), 0)
     column = lax.broadcasted_iota(jnp.int32, (members, LANES), 1)
     above, below = out[0], out[1]
@@ -379,28 +425,21 @@
     packed[...] = jnp.where(column == members + 2, pick(column == members, below), both)
 
 
-def gram(place, owner, omega, eta, sources, offsets, halves, ready):
+def gram(place, owner, omega, eta, begun, sources, offsets, planes):
     _, _, rows, ny = sources[0].shape
     members = rows * len(sources)
-    count = omega.shape[0]
-
-    def body(*refs):
-        inputs = 4 + len(sources)
-        gram_kernel(
-            *refs[:inputs], *refs[inputs + len(ready) :], offsets=offsets, halves=halves
-        )
-
+    whole = (omega.shape[0], members, LANES)
+    work = pltpu.VMEM((members, ny), f32)
+    first = begun is None
     return pl.pallas_call(
-        body,
-        out_shape=jax.ShapeDtypeStruct((members, LANES), f32),
-        in_specs=[SMEM, SMEM, VMEM, VMEM]
-        + [VMEM] * len(sources)
-        + [pl.BlockSpec(memory_space=pl.ANY)] * len(ready),
+        functools.partial(gram_kernel, offsets=offsets, planes=planes, first=first),
+        out_shape=jax.ShapeDtypeStruct(whole if first else whole[1:], f32),
+        in_specs=[SMEM, SMEM] + [VMEM] * (2 + len(sources) + (not first)),
         out_specs=VMEM,
-        scratch_shapes=[pltpu.VMEM((count, members, LANES), f32), pltpu.VMEM((members, ny), f32)],
+        scratch_shapes=[work] if first else [pltpu.VMEM(whole, f32), work],
         compiler_params=pltpu.CompilerParams(vmem_limit_bytes=SCOPED),
         name="gram",
-    )(place, owner, omega, eta, *sources, *ready)
+    )(place, owner, omega, eta, *([] if first else [begun]), *sources)
 
 
 def turned(x):
@@ -508,12 +547,11 @@
     )(*inputs)
 
 
-def mix_kernel(place, weights, *refs, blocks, halves):
+def mix_kernel(weights, *refs, blocks):
     *sources, out = refs
-    rows, species, _, nz, _ = out.shape
-    step = pl.program_id(0)
-    span = pl.num_programs(0) // halves
-    free, conserved, internal, *tracers = [
+    rows, _, _, nz, _ = out.shape
+    x, nx = pl.program_id(0), pl.num_programs(0)
+    free, conserved, internal, tracer, tracer_ends = [
         sources[k : k + blocks] for k in range(0, len(sources), blocks)
     ]
     members = blocks * free[0].shape[2]
@@ -530,42 +568,37 @@
         upper = mul(both, value_high)
         return upper[:rows] + (upper[rows:] + mul(high, value_low))
 
-    for part in range(halves):
-
-        @pl.when(step // span == part)
-        def _(part=part):
-            at = step % span
-            x = at if halves == 1 else half_begin(place, part, span) + at
-            for z in range(nz):
-                tracer = mixed(tracers[part], at, z)
-                inside = mixed(internal, x, z)
-                out[:, 0, 0, z, :] = mixed(free, x, z)
-                out[:, 1, 0, z, :] = mixed(conserved, x, z) - tracer
-                out[:, 2, 0, z, :] = tracer - inside
-                out[:, 3, 0, z, :] = inside
-
-
-def mix(place, weights, sources, blocks, halves, shape):
+    def plane(tracer, at):
+        for z in range(nz):
+            bound = mixed(tracer, at, z)
+            inside = mixed(internal, x, z)
+            out[:, 0, 0, z, :] = mixed(free, x, z)
+            out[:, 1, 0, z, :] = mixed(conserved, x, z) - bound
+            out[:, 2, 0, z, :] = bound - inside
+            out[:, 3, 0, z, :] = inside
+
+    at_end = (x == 0) | (x == nx - 1)
+
+    @pl.when(at_end)
+    def _():
+        plane(tracer_ends, x // (nx - 1))
+
+    @pl.when(jnp.logical_not(at_end))
+    def _():
+        plane(tracer, x - 1)
+
+
+def mix(weights, sources, blocks, shape):
     rows, species, nx, nz, ny = shape
-    span = nx // halves
-
-    def at(step, place):
-        if halves == 1:
-            return (0, 0, step, 0, 0)
-        return (0, 0, half_begin(place, step // span, span) + step % span, 0, 0)
-
     return pl.pallas_call(
-        functools.partial(mix_kernel, blocks=blocks, halves=halves),
-        grid_spec=pltpu.PrefetchScalarGridSpec(
-            num_scalar_prefetch=1,
-            grid=(nx,),
-            in_specs=[VMEM] * (1 + len(sources)),
-            out_specs=pl.BlockSpec((rows, species, 1, nz, ny), at),
-        ),
+        functools.partial(mix_kernel, blocks=blocks),
+        grid=(nx,),
+        in_specs=[VMEM] * (1 + len(sources)),
+        out_specs=pl.BlockSpec((rows, species, 1, nz, ny), lambda x: (0, 0, x, 0, 0)),
         out_shape=jax.ShapeDtypeStruct(shape, f32),
         compiler_params=pltpu.CompilerParams(vmem_limit_bytes=SCOPED),
         name="mix",
-    )(place, weights, *sources)
+    )(weights, *sources)
 
 
 def swap(x, axis, bit):
@@ -573,9 +606,11 @@
     return lax.ppermute(x, axis, [(k, k ^ bit) for k in range(count)])
 
 
-def total_over(x, axis):
-    bit = 1
-    while bit < lax.axis_size(axis):
+def total_over(x, axis, *before_last):
+    bit, count = 1, lax.axis_size(axis)
+    while bit < count:
+        if before_last and 2 * bit >= count:
+            x = lax.optimization_barrier((x, *before_last))[0]
         x = x + swap(x, axis, bit)
         bit *= 2
     return x
@@ -596,24 +631,27 @@
     def halos(first, last):
         return lax.ppermute(last, "space", forward), lax.ppermute(first, "space", backward)
 
-    if devices == 4 and rows % 8 == 0 and nx % 2 == 0:
-        blocks, halves = devices, 2
+    def tie(x, *after):
+        return lax.optimization_barrier((x, *after))[0]
+
+    if devices == 4 and rows % 8 == 0:
+        blocks = devices
 
         def offsets(position, j):
             return jnp.bitwise_xor(position, j) * rows
 
-        def collect(x, sent=None):
-            return [x, swap(x, "member", 1), swap(x if sent is None else sent, "member", 2)]
+        def collect(x, *after):
+            return [x, swap(x, "member", 1), swap(tie(x, *after), "member", 2)]
 
         def complete(held, *after):
             return [*held, swap(lax.optimization_barrier((held[2], *after))[0], "member", 1)]
     else:
-        blocks, halves = 1, 1
+        blocks = 1
 
         def offsets(position, j):
             return 0
 
-        def collect(x, sent=None):
+        def collect(x, *after):
             return [lax.all_gather(x, "member", axis=2, tiled=True)]
 
         def complete(held, *after):
@@ -621,9 +659,6 @@
 
     def across(held):
         return held[min(2, blocks - 1)]
-
-    def tie(x, *after):
-        return lax.optimization_barrier((x, *after))[0]
 
     whole = (nx, nz, rows, ny)
     coefficients = (diffusivity, binding, source)
@@ -638,57 +673,61 @@
         [*ends, *coefficients],
         [(nz, 2 * rows + 8, ny)] * 2,
         2 * cells // nx,
+        scalars=[place],
     )
     fields = [jnp.transpose(ensemble[:, k], (1, 2, 0, 3)) for k in range(species)]
     conserved = fields[1] + fields[2] + fields[3]
+    omega, eta = voxel_weights(
+        place, owner, obs_index, observed, obs_var, batches // 2, nx * nz, ny
+    )
     around = origin = halos(*edges)
-    for step in range(SUBSTEPS // 2 - 1):
+    payload = (nz, 2 * rows, ny)
+    for step in range(SUBSTEPS // 2 - 2):
         inputs = [*fields, *around, *origin, *coefficients]
-        if step == 1:
-            conserved = collect(tie(conserved, fields[0]))
         around = halos(
             *forecast_call(
-                next_edges_kernel,
-                "next_edges",
-                inputs,
-                [(nz, 2 * rows, ny)] * 2,
-                cells,
-                scratch=[whole] * 8,
+                next_edges_kernel, "next_edges", inputs, [payload] * 2, cells, scratch=[whole] * 8
             )
         )
         fields = forecast_call(
             two_substeps_kernel, "two_substeps", inputs, [whole] * 4, 2 * cells, scratch=[whole] * 4
         )
-    omega, eta = voxel_weights(
-        place, owner, obs_index, observed, obs_var, batches // 2, nx * nz, ny
-    )
-    *tracers, internal, middle, add = forecast_call(
-        functools.partial(last_but_one_kernel, halves=halves),
-        "last_but_one",
-        [*fields, *around, *coefficients],
-        [(nx // halves, nz, rows, ny)] * halves + [whole] * 3,
-        2 * cells,
-        scratch=[whole] * 3,
-        ready=[*conserved[1:], omega, eta],
-        scalars=[place],
-    )
+        if step == 0:
+            conserved = collect(conserved, fields[0])
+    inner, end = (nx - 2, nz, rows, ny), (2, nz, rows, ny)
+    before, first, last, free, tracer, internal, add, ends = forecast_call(
+        last_steps_kernel,
+        "last_steps",
+        [*fields, *around, *origin, *coefficients],
+        [whole, payload, payload, whole, inner, whole, inner, (3, *end)],
+        4 * cells,
+        scratch=[whole] * 7,
+        ready=(omega, eta, *conserved[1:]),
+    )
+    tracer = collect(tracer)
+    around = halos(first, last)
+    tracer_ends, free_ends, add_ends = forecast_call(
+        last_ends_kernel,
+        "last_ends",
+        [free, ends, *around, *coefficients],
+        [end] * 3,
+        cells // nx,
+    )
+    tracer = complete(tracer, tracer_ends)
+    tracer_ends = collect(tracer_ends)
+    conserved = complete(conserved, tracer_ends[0])
+    begun = gram(place, owner, omega, eta, None, tracer, offsets, (1, 1))
+    tracer_ends = complete(tracer_ends, begun)
     (free,) = forecast_call(
         last_free_kernel,
         "last_free",
-        [fields[0], middle, add, *around, *origin, diffusivity],
+        [before, free, free_ends, add, add_ends, *around, *origin, diffusivity],
         [whole],
         cells,
     )
-    near = collect(*tracers)
-    conserved = complete(conserved, tracers[0])
-    near = complete(near)
-    far = collect(tracers[1], tie(tracers[0], across(near))) if halves == 2 else []
-    half = gram(place, owner, omega, eta, near, offsets, halves, [*conserved[3:], *far[1:2]])
-    if halves == 2:
-        half = tie(half + swap(half, "member", 2), across(far))
-        far = complete(far, half)
-    internal = collect(internal, tie(internal, half))
-    free = collect(free, tie(free, half))
+    internal = collect(internal, across(tracer_ends))
+    half = gram(place, owner, omega, eta, begun, tracer_ends, offsets, (0, nx - 1))
+    free = collect(free, half)
     half = total_over(half, "space")
     other = swap(half, "member", 1)
     internal = complete(internal, half)
@@ -710,8 +749,8 @@
     )
     if blocks == 1:
         weights = lax.dynamic_slice(weights, (member * rows, 0), (rows, LANES))
-    sources = free + conserved + internal + near + (far if halves == 2 else [])
-    return mix(place, weights, sources, blocks, halves, ensemble.shape)
+    held = free + conserved + internal + tracer + tracer_ends
+    return mix(weights, held, blocks, ensemble.shape)
 
 
 def solution(mesh):

time: 129 us -> 118 us (0.915)
  local copies, waits for them, and re-layouts: 12 us -> 6.9 us
  waiting for transfers between devices: 38.4 us -> 33.9 us
    ppermute x20 -> x19, waiting for transfers between devices: 26.3 us -> 14.9 us  [swap(): return lax.ppermute(x, axis, [(k, k ^ bit) for k in range(count)])]
    ppermute x3, waiting for transfers between devices: 4.83 us -> 12.7 us  [halos(): lax.ppermute(first, 'space', backward)]
    unnamed x36 -> x16, local copies, waits for them, and re-layouts: 7.02 us -> 0.03 us
    pallas_call x7 -> x6, Pallas kernels: 7.83 us -> 6.87 us  [forecast_call(): pl.pallas_call(body, out_shape=[jax.ShapeDtypeStruct(shape, f32) for shap...]
    ppermute x20 -> x19, starting transfers between devices: 17.4 us -> 17.8 us  [swap(): return lax.ppermute(x, axis, [(k, k ^ bit) for k in range(count)])]
    pallas_call x2 -> x3, Pallas kernels: 6.49 us -> 6.53 us  [the longest x1 5.28 us: mix(): pl.pallas_call(functools.partial(mix_kernel, blocks=blocks), grid=(nx,),...]
  transfers between devices with their start and end apart: 26 -> 25, of which waited for: 10 -> 13; matrix products, arithmetic and copies ran while one was open for 4% -> 3% of each run, Pallas kernels for 25% -> 26%
where the time goes in v9:
time: 118 us
  Pallas kernels  39.9 us (34%)
  starting transfers between devices  35.5 us (30%)
  waiting for transfers between devices  33.9 us (29%)
  local copies, waits for them, and re-layouts  6.9 us (6%)
  other arithmetic  1.37 us (1%)
    pallas_call x2, Pallas kernels, transform_call(): pl.pallas_call(kernel, out_shape=[jax.ShapeDtypeStruct(shape, f32) for sh...  25.1 us
    ppermute x19, starting transfers between devices, swap(): return lax.ppermute(x, axis, [(k, k ^ bit) for k in range(count)])  17.8 us
    ppermute x19, waiting for transfers between devices, swap(): return lax.ppermute(x, axis, [(k, k ^ bit) for k in range(count)])  14.9 us
    ppermute x3, starting transfers between devices, halos(): lax.ppermute(last, 'space', forward)  13.7 us
    ppermute x3, waiting for transfers between devices, halos(): lax.ppermute(first, 'space', backward)  12.7 us
    pallas_call x6, Pallas kernels, forecast_call(): pl.pallas_call(body, out_shape=[jax.ShapeDtypeStruct(shape, f32) for shap...  6.87 us
    ppermute x3, waiting for transfers between devices, halos(): lax.ppermute(last, 'space', forward)  6.42 us
    pallas_call x1, Pallas kernels, mix(): pl.pallas_call(functools.partial(mix_kernel, blocks=blocks), grid=(nx,),...  5.28 us
  transfers between devices with their start and end apart: 25, of which 13 were waited for; matrix products, arithmetic and copies ran while one was open for 3% of the time, Pallas kernels for 26%

profile of v9, /device:TPU:0, one launch (start us, length us, event | category | flops | bytes accessed | tf_op | source)
XLA Modules:
  0.0 118.0 jit_solution(18168928988969739103)
XLA Ops:
  0.0 2.6 %fusion = (f32[24,3,2,4,256]{4,3,2,1,0:T(4,128)}, f32[24,3,2,4,256]{4,3,2,1,0:T(4,128)}) fusion(f32[24,4,8,4,256]{4,3,2,1,0:T(4,128)} %param.8), kind=kLoop, calls=%fused_computation.8 | loop fusion | bytes 2359296 | tf_op jit(solution)/shard_map/slice | solution.py:667
  2.6 1.6 %copy_bitcast_fusion.4 = (f32[3,2,4,24,256]{4,3,2,1,0:T(8,128)S(1)}, f32[3,2,4,24,256]{4,3,2,1,0:T(8,128)S(1)}) fusion(f32[24,3,2,4,256]{4,3,2,1,0:T(4,128)} %get-tuple-element.67, f32[24,3,2,4,256]{4,3,2,1,0:T(4,128)} %get-tuple-element.68), kind=kLoop, calls=%fused_computation.5 | loop fusion | bytes 2359296 | tf_op jit(solution)/shard_map/transpose | solution.py:667
  4.2 0.1 pad_add_fusion.place.refs_0_
  4.3 0.7 first_edges.1
  5.1 4.9 %collective-permute-start = (f32[4,56,256]{2,1,0:T(8,128)S(1)}, f32[4,56,256]{2,1,0:T(8,128)S(1)}, u32[]{:S(2)}, u32[]{:S(2)}) collective-permute-start(f32[4,56,256]{2,1,0:T(8,128)S(1)} %get-tuple-element.38), channel_id=1, source_target_pairs={{0,1},{1,2},{2,3},{3,4},{4,5},{5,6},{6,7},{8,9},{9,10},{10,11},{11... | collective-permute-start | bytes 688136 | tf_op jit(solution)/shard_map/ppermute | solution.py:632
  10.0 1.3 %collective-permute-start.1 = (f32[4,56,256]{2,1,0:T(8,128)S(1)}, f32[4,56,256]{2,1,0:T(8,128)S(1)}, u32[]{:S(2)}, u32[]{:S(2)}) collective-permute-start(f32[4,56,256]{2,1,0:T(8,128)S(1)} %get-tuple-element.39), channel_id=1, source_target_pairs={{1,0},{2,1},{3,2},{4,3},{5,4},{6,5},{7,6},{9,8},{10,9},{11,10},{12... | collective-permute-start | bytes 688136 | tf_op jit(solution)/shard_map/ppermute | solution.py:632
  11.3 0.8 fusion.1
  12.1 1.3 %add_add_fusion.refs_4_ = f32[8,4,24,256]{3,2,1,0:T(8,128)S(1)} fusion(f32[24,1,8,4,256]{4,3,2,1,0:T(4,128)S(1)} %get-tuple-element.71, f32[24,1,8,4,256]{4,3,2,1,0:T(4,128)S(1)} %get-tuple-element.70, f32[24,1,8,4,256]{4,3,2,1,0:T(4,128)S(1)} %get-tuple-element.69), kind=kLoop, calls=%fused_computation.4 | loop fusion | flops 393216 | bytes 3145728 | tf_op jit(solution)/shard_map/add | solution.py:679
  13.4 0.1 collective-permute-start.4
  13.4 0.9 copy_bitcast_fusion
  14.4 0.9 copy_bitcast_fusion.2
  15.3 4.4 %collective-permute-done.refs_4_.refs_6_.refs_7_ = f32[4,56,256]{2,1,0:T(8,128)S(1)} collective-permute-done((f32[4,56,256]{2,1,0:T(8,128)S(1)}, f32[4,56,256]{2,1,0:T(8,128)S(1)}, u32[]{:S(2)}, u32[]{:S(2)}) %collective-permute-start) | collective-permute-done | bytes 229408 | tf_op jit(solution)/shard_map/ppermute | solution.py:632
  19.7 0.0 copy-start.6
  19.7 1.6 %two_substeps.1 = (f32[8,4,24,256]{3,2,1,0:T(8,128)S(1)}, f32[8,4,24,256]{3,2,1,0:T(8,128)S(1)}, f32[8,4,24,256]{3,2,1,0:T(8,128)S(1)}, f32[8,4,24,256]{3,2,1,0:T(8,128)S(1)}) custom-call(f32[8,4,24,256]{3,2,1,0:T(8,128)S(1)} %get-tuple-element.76.refs_0_, f32[8,4,24,256]{3,2,1,0:T(8,128)S(1)} %get-tuple-element.75.refs_1_, ...), custom_call_target="tpu_custom_call" | custom-call | flops 11796480 | bytes 12582912 | tf_op jit(solution)/shard_map/two_substeps/pallas_call | solution.py:319
  21.3 1.6 %collective-permute-start.5 = (f32[8,4,24,256]{3,2,1,0:T(8,128)S(1)}, f32[8,4,24,256]{3,2,1,0:T(8,128)S(1)}, u32[]{:S(2)}, u32[]{:S(2)}) collective-permute-start(f32[8,4,24,256]{3,2,1,0:T(8,128)S(1)} %add_add_fusion.refs_4_), channel_id=1, source_target_pairs={{0,16},{8,24},{16,0},{24,8},{1,17},{9,25},{17,1},{25,9},{2,18},{10... | collective-permute-start | bytes 2359304 | tf_op jit(solution)/shard_map/ppermute | solution.py:606
  22.9 1.0 next_edges.1
  24.0 4.4 %collective-permute-start.2 = (f32[4,48,256]{2,1,0:T(8,128)S(1)}, f32[4,48,256]{2,1,0:T(8,128)S(1)}, u32[]{:S(2)}, u32[]{:S(2)}) collective-permute-start(f32[4,48,256]{2,1,0:T(8,128)S(1)} %get-tuple-element.44), channel_id=1, source_target_pairs={{0,1},{1,2},{2,3},{3,4},{4,5},{5,6},{6,7},{8,9},{9,10},{10,11},{11... | collective-permute-start | bytes 589832 | tf_op jit(solution)/shard_map/ppermute | solution.py:632
  28.4 1.3 %collective-permute-start.3 = (f32[4,48,256]{2,1,0:T(8,128)S(1)}, f32[4,48,256]{2,1,0:T(8,128)S(1)}, u32[]{:S(2)}, u32[]{:S(2)}) collective-permute-start(f32[4,48,256]{2,1,0:T(8,128)S(1)} %get-tuple-element.45), channel_id=1, source_target_pairs={{1,0},{2,1},{3,2},{4,3},{5,4},{6,5},{7,6},{9,8},{10,9},{11,10},{12... | collective-permute-start | bytes 589832 | tf_op jit(solution)/shard_map/ppermute | solution.py:632
  29.7 1.4 %voxel_weights.1 = (f32[2,32,256]{2,1,0:T(8,128)S(1)}, f32[2,32,256]{2,1,0:T(8,128)S(1)}) custom-call(s32[3]{0:T(128)S(1)} %pad_add_fusion.place.refs_0_, s32[4]{0:T(128)S(1)} %copy-done.6, s32[4,2048]{1,0:T(4,128)S(1)} %copy-done.3, f32[4,2048]{1,0:T(4,128)S(1)} %copy-done.4, f32[4,2048]{1,0:T(4,128)S(1)} %copy-done.5), custom_call_target="tpu_custom_call" | custom-call | tf_op jit(solution)/shard_map/voxel_weights/pallas_call | solution.py:371
  31.1 0.4 collective-permute-done.2.refs_4_
  31.5 5.7 %collective-permute-done.3.refs_5_ = f32[4,48,256]{2,1,0:T(8,128)S(1)} collective-permute-done((f32[4,48,256]{2,1,0:T(8,128)S(1)}, f32[4,48,256]{2,1,0:T(8,128)S(1)}, u32[]{:S(2)}, u32[]{:S(2)}) %collective-permute-start.3) | collective-permute-done | bytes 196640 | tf_op jit(solution)/shard_map/ppermute | solution.py:632
  37.2 0.0 collective-permute-done.4.refs_13_.refs_5_
  37.2 1.5 %collective-permute-done.5.refs_14_.refs_6_ = f32[8,4,24,256]{3,2,1,0:T(8,128)S(1)} collective-permute-done((f32[8,4,24,256]{3,2,1,0:T(8,128)S(1)}, f32[8,4,24,256]{3,2,1,0:T(8,128)S(1)}, u32[]{:S(2)}, u32[]{:S(2)}) %collective-permute-start.5) | collective-permute-done | bytes 786464 | tf_op jit(solution)/shard_map/ppermute | solution.py:606
  38.7 2.9 %last_steps.1 = (f32[8,4,24,256]{3,2,1,0:T(8,128)S(1)}, f32[4,48,256]{2,1,0:T(8,128)S(1)}, f32[4,48,256]{2,1,0:T(8,128)S(1)}, f32[8,4,24,256]{3,2,1,0:T(8,128)S(...) custom-call(f32[8,4,24,256]{3,2,1,0:T(8,128)S(1)} %get-tuple-element, ...), custom_call_target="tpu_custom_call" | custom-call | flops 23592960 | bytes 25165824 | tf_op jit(solution)/shard_map/last_steps/pallas_call | solution.py:319
  41.6 1.6 %collective-permute-start.7 = (f32[6,4,24,256]{3,2,1,0:T(8,128)S(1)}, f32[6,4,24,256]{3,2,1,0:T(8,128)S(1)}, u32[]{:S(2)}, u32[]{:S(2)}) collective-permute-start(f32[6,4,24,256]{3,2,1,0:T(8,128)S(1)} %get-tuple-element.47.refs_0_.refs_12_), channel_id=1, source_target_pairs={{0,16},{8,24},{16,0},{24,8},{1,17},{9,25},{17,1},{25,9},{2,18},{10... | collective-permute-start | bytes 1769480 | tf_op jit(solution)/shard_map/ppermute | solution.py:606
  43.2 4.4 %collective-permute-start.8 = (f32[4,48,256]{2,1,0:T(8,128)S(1)}, f32[4,48,256]{2,1,0:T(8,128)S(1)}, u32[]{:S(2)}, u32[]{:S(2)}) collective-permute-start(f32[4,48,256]{2,1,0:T(8,128)S(1)} %get-tuple-element.50), channel_id=1, source_target_pairs={{0,1},{1,2},{2,3},{3,4},{4,5},{5,6},{6,7},{8,9},{9,10},{10,11},{11... | collective-permute-start | bytes 589832 | tf_op jit(solution)/shard_map/ppermute | solution.py:632
  47.6 1.5 %collective-permute-start.9 = (f32[4,48,256]{2,1,0:T(8,128)S(1)}, f32[4,48,256]{2,1,0:T(8,128)S(1)}, u32[]{:S(2)}, u32[]{:S(2)}) collective-permute-start(f32[4,48,256]{2,1,0:T(8,128)S(1)} %get-tuple-element.51), channel_id=1, source_target_pairs={{1,0},{2,1},{3,2},{4,3},{5,4},{6,5},{7,6},{9,8},{10,9},{11,10},{12... | collective-permute-start | bytes 589832 | tf_op jit(solution)/shard_map/ppermute | solution.py:632
  49.1 0.1 collective-permute-start.6
  49.2 1.6 %collective-permute-done.8.refs_2_.refs_5_ = f32[4,48,256]{2,1,0:T(8,128)S(1)} collective-permute-done((f32[4,48,256]{2,1,0:T(8,128)S(1)}, f32[4,48,256]{2,1,0:T(8,128)S(1)}, u32[]{:S(2)}, u32[]{:S(2)}) %collective-permute-start.8) | collective-permute-done | bytes 196640 | tf_op jit(solution)/shard_map/ppermute | solution.py:632
  50.8 7.0 %collective-permute-done.9.refs_3_.refs_6_ = f32[4,48,256]{2,1,0:T(8,128)S(1)} collective-permute-done((f32[4,48,256]{2,1,0:T(8,128)S(1)}, f32[4,48,256]{2,1,0:T(8,128)S(1)}, u32[]{:S(2)}, u32[]{:S(2)}) %collective-permute-start.9) | collective-permute-done | bytes 196640 | tf_op jit(solution)/shard_map/ppermute | solution.py:632
  57.7 0.1 last_ends.1
  57.9 0.1 collective-permute-start.10
  57.9 0.6 collective-permute-start.12
  58.5 0.2 collective-permute-start.11
  58.7 1.2 %collective-permute-done.10.refs_3_.refs_15_ = f32[6,4,24,256]{3,2,1,0:T(8,128)S(1)} collective-permute-done((f32[6,4,24,256]{3,2,1,0:T(8,128)S(1)}, f32[6,4,24,256]{3,2,1,0:T(8,128)S(1)}, u32[]{:S(2)}, u32[]{:S(2)}) %collective-permute-start.10) | collective-permute-done | bytes 589856 | tf_op jit(solution)/shard_map/ppermute | solution.py:606
  59.9 0.6 gram.2.refs_0_
  60.5 4.8 %collective-permute-done.12.refs_3_.refs_18_ = f32[2,4,24,256]{3,2,1,0:T(8,128)S(1)} collective-permute-done((f32[2,4,24,256]{3,2,1,0:T(8,128)S(1)}, f32[2,4,24,256]{3,2,1,0:T(8,128)S(1)}, u32[]{:S(2)}, u32[]{:S(2)}) %collective-permute-start.12) | collective-permute-done | bytes 196640 | tf_op jit(solution)/shard_map/ppermute | solution.py:606
  65.3 0.5 collective-permute-start.23
  65.8 0.5 last_free.1.refs_0_
  66.3 0.0 collective-permute-done.11.refs_2_.refs_17_
  66.3 0.4 collective-permute-done.13.refs_4_.refs_19_
  66.7 0.7 gram.3
  67.4 1.2 %collective-permute-start.19 = (f32[8,4,24,256]{3,2,1,0:T(8,128)S(1)}, f32[8,4,24,256]{3,2,1,0:T(8,128)S(1)}, u32[]{:S(2)}, u32[]{:S(2)}) collective-permute-start(f32[8,4,24,256]{3,2,1,0:T(8,128)S(1)} %last_free.1.refs_0_), channel_id=1, source_target_pairs={{0,16},{8,24},{16,0},{24,8},{1,17},{9,25},{17,1},{25,9},{2,18},{10... | collective-permute-start | bytes 2359304 | tf_op jit(solution)/shard_map/ppermute | solution.py:606
  68.6 3.7 %collective-permute-start.14 = (f32[96,128]{1,0:T(8,128)S(1)}, f32[96,128]{1,0:T(8,128)S(1)}, u32[]{:S(2)}, u32[]{:S(2)}) collective-permute-start(f32[96,128]{1,0:T(8,128)S(1)} %gram.3), channel_id=1, source_target_pairs={{0,1},{1,0},{2,3},{3,2},{4,5},{5,4},{6,7},{7,6},{8,9},{9,8},{10,11... | collective-permute-start | bytes 147464 | tf_op jit(solution)/shard_map/ppermute | solution.py:606
  72.3 2.1 %collective-permute-done.14 = f32[96,128]{1,0:T(8,128)S(1)} collective-permute-done((f32[96,128]{1,0:T(8,128)S(1)}, f32[96,128]{1,0:T(8,128)S(1)}, u32[]{:S(2)}, u32[]{:S(2)}) %collective-permute-start.14) | collective-permute-done | bytes 49184 | tf_op jit(solution)/shard_map/ppermute | solution.py:606
  74.3 2.5 %collective-permute-start.15 = (f32[96,128]{1,0:T(8,128)S(1)}, f32[96,128]{1,0:T(8,128)S(1)}, u32[]{:S(2)}, u32[]{:S(2)}) collective-permute-start(f32[96,128]{1,0:T(8,128)S(1)} %add.17), channel_id=1, source_target_pairs={{0,2},{1,3},{2,0},{3,1},{4,6},{5,7},{6,4},{7,5},{8,10},{9,11},{10,... | collective-permute-start | bytes 147464 | tf_op jit(solution)/shard_map/ppermute | solution.py:606
  76.9 2.1 %collective-permute-done.15 = f32[96,128]{1,0:T(8,128)S(1)} collective-permute-done((f32[96,128]{1,0:T(8,128)S(1)}, f32[96,128]{1,0:T(8,128)S(1)}, u32[]{:S(2)}, u32[]{:S(2)}) %collective-permute-start.15) | collective-permute-done | bytes 49184 | tf_op jit(solution)/shard_map/ppermute | solution.py:606
  78.9 4.1 %collective-permute-start.16 = (f32[96,128]{1,0:T(8,128)S(1)}, f32[96,128]{1,0:T(8,128)S(1)}, u32[]{:S(2)}, u32[]{:S(2)}) collective-permute-start(f32[96,128]{1,0:T(8,128)S(1)} %add.18), channel_id=1, source_target_pairs={{0,4},{1,5},{2,6},{3,7},{4,0},{5,1},{6,2},{7,3},{8,12},{9,13},{10,... | collective-permute-start | bytes 147464 | tf_op jit(solution)/shard_map/ppermute | solution.py:606
  83.0 2.6 %collective-permute-done.16 = f32[96,128]{1,0:T(8,128)S(1)} collective-permute-done((f32[96,128]{1,0:T(8,128)S(1)}, f32[96,128]{1,0:T(8,128)S(1)}, u32[]{:S(2)}, u32[]{:S(2)}) %collective-permute-start.16) | collective-permute-done | bytes 49184 | tf_op jit(solution)/shard_map/ppermute | solution.py:606
  85.6 0.1 collective-permute-start.17
  85.7 0.5 collective-permute-start.22
  86.2 0.1 collective-permute-start.18
  86.3 0.0 collective-permute-done.23.refs_10_
  86.3 0.4 collective-permute-start.21
  86.7 0.2 collective-permute-done.17.other
  86.9 0.2 collective-permute-start.24
  87.1 18.5 %transforms_early.1 = (f32[96,128]{1,0:T(8,128)S(1)}, f32[96,128]{1,0:T(8,128)S(1)}) custom-call(s32[3]{0:T(128)S(1)} %pad_add_fusion.place.refs_0_, f32[96,128]{1,0:T(8,128)S(1)} %add.19.mine, f32[96,128]{1,0:T(8,128)S(1)} %collective-permute-done.17.other), custom_call_target="tpu_custom_call" | custom-call | flops 100000000 | bytes 1000000 | tf_op jit(solution)/shard_map/transforms_early/pallas_call | solution.py:536
  105.6 0.0 collective-permute-done.19.refs_2_
  105.6 0.4 collective-permute-start.20
  106.0 6.6 %transforms_late.1.weights = f32[24,128]{1,0:T(8,128)S(1)} custom-call(s32[3]{0:T(128)S(1)} %pad_add_fusion.place.refs_0_, f32[96,128]{1,0:T(8,128)S(1)} %get-tuple-element.55.total, f32[96,128]{1,0:T(8,128)S(1)} %get-tuple-element.56.last), custom_call_target="tpu_custom_call" | custom-call | flops 100000000 | bytes 1000000 | tf_op jit(solution)/shard_map/transforms_late/pallas_call | solution.py:536
  112.6 0.0 collective-permute-done.22.refs_9_
  112.6 0.0 collective-permute-done.21.refs_7_
  112.7 0.0 collective-permute-done.20.refs_3_
  112.7 5.3 %mix.1 = f32[24,4,8,4,256]{4,3,2,1,0:T(4,128)} custom-call(f32[24,128]{1,0:T(8,128)S(1)} %transforms_late.1.weights, f32[8,4,24,256]{3,2,1,0:T(8,128)S(1)} %last_free.1.refs_0_, f32[8,4,24,256]{3,2,1,0:T(8,128)S(1)} %collective-permute-done.18.refs_1_, f32[8,4,24,256]{3,2,1,0:T(8,128)S(1)} %collective-permute-done.19.refs_2_, ...), custom_call_target="tpu_custom_call" | custom-call | tf_op jit(solution)/shard_map/mix/pallas_call | solution.py:593
  (24 shorter events, 0.1 us)
Async XLA Ops:
  0.0 11.3 %copy-start.7 = (f32[24,4,8,4,256]{4,3,2,1,0:T(4,128)S(1)}, f32[24,4,8,4,256]{4,3,2,1,0:T(4,128)}, u32[]{:S(2)}) copy-start(f32[24,4,8,4,256]{4,3,2,1,0:T(4,128)} %param.8) | copy-start | bytes 9437188
  0.0 4.3 %copy-start = (f32[8,4,256]{2,1,0:T(4,128)S(1)}, f32[8,4,256]{2,1,0:T(4,128)}, u32[]{:S(2)}) copy-start(f32[8,4,256]{2,1,0:T(4,128)} %refs_9_.7) | copy-start | bytes 98308
  0.0 4.3 %copy-start.2 = (f32[8,4,256]{2,1,0:T(4,128)S(1)}, f32[8,4,256]{2,1,0:T(4,128)}, u32[]{:S(2)}) copy-start(f32[8,4,256]{2,1,0:T(4,128)} %refs_6_.1) | copy-start | bytes 98308
  0.0 4.3 %copy-start.1 = (f32[8,4,256]{2,1,0:T(4,128)S(1)}, f32[8,4,256]{2,1,0:T(4,128)}, u32[]{:S(2)}) copy-start(f32[8,4,256]{2,1,0:T(4,128)} %refs_5_.3) | copy-start | bytes 98308
  5.1 14.6 %collective-permute-start = (f32[4,56,256]{2,1,0:T(8,128)S(1)}, f32[4,56,256]{2,1,0:T(8,128)S(1)}, u32[]{:S(2)}, u32[]{:S(2)}) collective-permute-start(f32[4,56,256]{2,1,0:T(8,128)S(1)} %get-tuple-element.38), channel_id=1, source_target_pairs={{0,1},{1,2},{2,3},{3,4},{4,5},{5,6},{6,7},{8,9},{9,10},{10,11},{11... | collective-permute-start | bytes 688136 | tf_op jit(solution)/shard_map/ppermute | solution.py:632
  10.0 9.7 %collective-permute-start.1 = (f32[4,56,256]{2,1,0:T(8,128)S(1)}, f32[4,56,256]{2,1,0:T(8,128)S(1)}, u32[]{:S(2)}, u32[]{:S(2)}) collective-permute-start(f32[4,56,256]{2,1,0:T(8,128)S(1)} %get-tuple-element.39), channel_id=1, source_target_pairs={{1,0},{2,1},{3,2},{4,3},{5,4},{6,5},{7,6},{9,8},{10,9},{11,10},{12... | collective-permute-start | bytes 688136 | tf_op jit(solution)/shard_map/ppermute | solution.py:632
  13.4 23.9 %collective-permute-start.4 = (f32[8,4,24,256]{3,2,1,0:T(8,128)S(1)}, f32[8,4,24,256]{3,2,1,0:T(8,128)S(1)}, u32[]{:S(2)}, u32[]{:S(2)}) collective-permute-start(f32[8,4,24,256]{3,2,1,0:T(8,128)S(1)} %add_add_fusion.refs_4_), channel_id=1, source_target_pairs={{0,8},{8,0},{16,24},{24,16},{1,9},{9,1},{17,25},{25,17},{2,10},{10... | collective-permute-start | bytes 2359304 | tf_op jit(solution)/shard_map/ppermute | solution.py:606
  19.7 10.0 %copy-start.3 = (s32[4,2048]{1,0:T(4,128)S(1)}, s32[4,2048]{1,0:T(4,128)}, u32[]{:S(2)}) copy-start(s32[4,2048]{1,0:T(4,128)} %obs_index.1) | copy-start | bytes 98308
  19.7 10.0 %copy-start.4 = (f32[4,2048]{1,0:T(4,128)S(1)}, f32[4,2048]{1,0:T(4,128)}, u32[]{:S(2)}) copy-start(f32[4,2048]{1,0:T(4,128)} %observed.1) | copy-start | bytes 98308
  19.7 10.0 %copy-start.5 = (f32[4,2048]{1,0:T(4,128)S(1)}, f32[4,2048]{1,0:T(4,128)}, u32[]{:S(2)}) copy-start(f32[4,2048]{1,0:T(4,128)} %obs_var.1) | copy-start | bytes 98308
  19.7 10.0 %copy-start.6 = (s32[4]{0:T(128)S(1)}, s32[4]{0:T(128)}, u32[]{:S(2)}) copy-start(s32[4]{0:T(128)} %owner.5) | copy-start | bytes 52
  21.3 17.4 %collective-permute-start.5 = (f32[8,4,24,256]{3,2,1,0:T(8,128)S(1)}, f32[8,4,24,256]{3,2,1,0:T(8,128)S(1)}, u32[]{:S(2)}, u32[]{:S(2)}) collective-permute-start(f32[8,4,24,256]{3,2,1,0:T(8,128)S(1)} %add_add_fusion.refs_4_), channel_id=1, source_target_pairs={{0,16},{8,24},{16,0},{24,8},{1,17},{9,25},{17,1},{25,9},{2,18},{10... | collective-permute-start | bytes 2359304 | tf_op jit(solution)/shard_map/ppermute | solution.py:606
  24.0 7.6 %collective-permute-start.2 = (f32[4,48,256]{2,1,0:T(8,128)S(1)}, f32[4,48,256]{2,1,0:T(8,128)S(1)}, u32[]{:S(2)}, u32[]{:S(2)}) collective-permute-start(f32[4,48,256]{2,1,0:T(8,128)S(1)} %get-tuple-element.44), channel_id=1, source_target_pairs={{0,1},{1,2},{2,3},{3,4},{4,5},{5,6},{6,7},{8,9},{9,10},{10,11},{11... | collective-permute-start | bytes 589832 | tf_op jit(solution)/shard_map/ppermute | solution.py:632
  28.4 8.8 %collective-permute-start.3 = (f32[4,48,256]{2,1,0:T(8,128)S(1)}, f32[4,48,256]{2,1,0:T(8,128)S(1)}, u32[]{:S(2)}, u32[]{:S(2)}) collective-permute-start(f32[4,48,256]{2,1,0:T(8,128)S(1)} %get-tuple-element.45), channel_id=1, source_target_pairs={{1,0},{2,1},{3,2},{4,3},{5,4},{6,5},{7,6},{9,8},{10,9},{11,10},{12... | collective-permute-start | bytes 589832 | tf_op jit(solution)/shard_map/ppermute | solution.py:632
  41.6 16.3 %collective-permute-start.7 = (f32[6,4,24,256]{3,2,1,0:T(8,128)S(1)}, f32[6,4,24,256]{3,2,1,0:T(8,128)S(1)}, u32[]{:S(2)}, u32[]{:S(2)}) collective-permute-start(f32[6,4,24,256]{3,2,1,0:T(8,128)S(1)} %get-tuple-element.47.refs_0_.refs_12_), channel_id=1, source_target_pairs={{0,16},{8,24},{16,0},{24,8},{1,17},{9,25},{17,1},{25,9},{2,18},{10... | collective-permute-start | bytes 1769480 | tf_op jit(solution)/shard_map/ppermute | solution.py:606
  43.2 7.6 %collective-permute-start.8 = (f32[4,48,256]{2,1,0:T(8,128)S(1)}, f32[4,48,256]{2,1,0:T(8,128)S(1)}, u32[]{:S(2)}, u32[]{:S(2)}) collective-permute-start(f32[4,48,256]{2,1,0:T(8,128)S(1)} %get-tuple-element.50), channel_id=1, source_target_pairs={{0,1},{1,2},{2,3},{3,4},{4,5},{5,6},{6,7},{8,9},{9,10},{10,11},{11... | collective-permute-start | bytes 589832 | tf_op jit(solution)/shard_map/ppermute | solution.py:632
  47.6 10.1 %collective-permute-start.9 = (f32[4,48,256]{2,1,0:T(8,128)S(1)}, f32[4,48,256]{2,1,0:T(8,128)S(1)}, u32[]{:S(2)}, u32[]{:S(2)}) collective-permute-start(f32[4,48,256]{2,1,0:T(8,128)S(1)} %get-tuple-element.51), channel_id=1, source_target_pairs={{1,0},{2,1},{3,2},{4,3},{5,4},{6,5},{7,6},{9,8},{10,9},{11,10},{12... | collective-permute-start | bytes 589832 | tf_op jit(solution)/shard_map/ppermute | solution.py:632
  49.1 9.6 %collective-permute-start.6 = (f32[6,4,24,256]{3,2,1,0:T(8,128)S(1)}, f32[6,4,24,256]{3,2,1,0:T(8,128)S(1)}, u32[]{:S(2)}, u32[]{:S(2)}) collective-permute-start(f32[6,4,24,256]{3,2,1,0:T(8,128)S(1)} %get-tuple-element.47.refs_0_.refs_12_), channel_id=1, source_target_pairs={{0,8},{8,0},{16,24},{24,16},{1,9},{9,1},{17,25},{25,17},{2,10},{10... | collective-permute-start | bytes 1769480 | tf_op jit(solution)/shard_map/ppermute | solution.py:606
  57.9 2.1 %collective-permute-start.10 = (f32[6,4,24,256]{3,2,1,0:T(8,128)S(1)}, f32[6,4,24,256]{3,2,1,0:T(8,128)S(1)}, u32[]{:S(2)}, u32[]{:S(2)}) collective-permute-start(f32[6,4,24,256]{3,2,1,0:T(8,128)S(1)} %collective-permute-done.7.refs_2_.refs_14_), channel_id=1, source_target_pairs={{0,8},{8,0},{16,24},{24,16},{1,9},{9,1},{17,25},{25,17},{2,10},{10... | collective-permute-start | bytes 1769480 | tf_op jit(solution)/shard_map/ppermute | solution.py:606
  57.9 7.3 %collective-permute-start.12 = (f32[2,4,24,256]{3,2,1,0:T(8,128)S(1)}, f32[2,4,24,256]{3,2,1,0:T(8,128)S(1)}, u32[]{:S(2)}, u32[]{:S(2)}) collective-permute-start(f32[2,4,24,256]{3,2,1,0:T(8,128)S(1)} %get-tuple-element.52.refs_1_.refs_16_), channel_id=1, source_target_pairs={{0,16},{8,24},{16,0},{24,8},{1,17},{9,25},{17,1},{25,9},{2,18},{10... | collective-permute-start | bytes 589832 | tf_op jit(solution)/shard_map/ppermute | solution.py:606
  58.5 7.8 %collective-permute-start.11 = (f32[2,4,24,256]{3,2,1,0:T(8,128)S(1)}, f32[2,4,24,256]{3,2,1,0:T(8,128)S(1)}, u32[]{:S(2)}, u32[]{:S(2)}) collective-permute-start(f32[2,4,24,256]{3,2,1,0:T(8,128)S(1)} %get-tuple-element.52.refs_1_.refs_16_), channel_id=1, source_target_pairs={{0,8},{8,0},{16,24},{24,16},{1,9},{9,1},{17,25},{25,17},{2,10},{10... | collective-permute-start | bytes 589832 | tf_op jit(solution)/shard_map/ppermute | solution.py:606
  65.3 1.4 %collective-permute-start.13 = (f32[2,4,24,256]{3,2,1,0:T(8,128)S(1)}, f32[2,4,24,256]{3,2,1,0:T(8,128)S(1)}, u32[]{:S(2)}, u32[]{:S(2)}) collective-permute-start(f32[2,4,24,256]{3,2,1,0:T(8,128)S(1)} %collective-permute-done.12.refs_3_.refs_18_), channel_id=1, source_target_pairs={{0,8},{8,0},{16,24},{24,16},{1,9},{9,1},{17,25},{25,17},{2,10},{10... | collective-permute-start | bytes 589832 | tf_op jit(solution)/shard_map/ppermute | solution.py:606
  65.3 21.0 %collective-permute-start.23 = (f32[8,4,24,256]{3,2,1,0:T(8,128)S(1)}, f32[8,4,24,256]{3,2,1,0:T(8,128)S(1)}, u32[]{:S(2)}, u32[]{:S(2)}) collective-permute-start(f32[8,4,24,256]{3,2,1,0:T(8,128)S(1)} %get-tuple-element.65.refs_8_), channel_id=1, source_target_pairs={{0,16},{8,24},{16,0},{24,8},{1,17},{9,25},{17,1},{25,9},{2,18},{10... | collective-permute-start | bytes 2359304 | tf_op jit(solution)/shard_map/ppermute | solution.py:606
  67.4 38.2 %collective-permute-start.19 = (f32[8,4,24,256]{3,2,1,0:T(8,128)S(1)}, f32[8,4,24,256]{3,2,1,0:T(8,128)S(1)}, u32[]{:S(2)}, u32[]{:S(2)}) collective-permute-start(f32[8,4,24,256]{3,2,1,0:T(8,128)S(1)} %last_free.1.refs_0_), channel_id=1, source_target_pairs={{0,16},{8,24},{16,0},{24,8},{1,17},{9,25},{17,1},{25,9},{2,18},{10... | collective-permute-start | bytes 2359304 | tf_op jit(solution)/shard_map/ppermute | solution.py:606
  68.6 5.8 %collective-permute-start.14 = (f32[96,128]{1,0:T(8,128)S(1)}, f32[96,128]{1,0:T(8,128)S(1)}, u32[]{:S(2)}, u32[]{:S(2)}) collective-permute-start(f32[96,128]{1,0:T(8,128)S(1)} %gram.3), channel_id=1, source_target_pairs={{0,1},{1,0},{2,3},{3,2},{4,5},{5,4},{6,7},{7,6},{8,9},{9,8},{10,11... | collective-permute-start | bytes 147464 | tf_op jit(solution)/shard_map/ppermute | solution.py:606
  74.3 4.6 %collective-permute-start.15 = (f32[96,128]{1,0:T(8,128)S(1)}, f32[96,128]{1,0:T(8,128)S(1)}, u32[]{:S(2)}, u32[]{:S(2)}) collective-permute-start(f32[96,128]{1,0:T(8,128)S(1)} %add.17), channel_id=1, source_target_pairs={{0,2},{1,3},{2,0},{3,1},{4,6},{5,7},{6,4},{7,5},{8,10},{9,11},{10,... | collective-permute-start | bytes 147464 | tf_op jit(solution)/shard_map/ppermute | solution.py:606
  78.9 6.7 %collective-permute-start.16 = (f32[96,128]{1,0:T(8,128)S(1)}, f32[96,128]{1,0:T(8,128)S(1)}, u32[]{:S(2)}, u32[]{:S(2)}) collective-permute-start(f32[96,128]{1,0:T(8,128)S(1)} %add.18), channel_id=1, source_target_pairs={{0,4},{1,5},{2,6},{3,7},{4,0},{5,1},{6,2},{7,3},{8,12},{9,13},{10,... | collective-permute-start | bytes 147464 | tf_op jit(solution)/shard_map/ppermute | solution.py:606
  85.6 1.3 %collective-permute-start.17 = (f32[96,128]{1,0:T(8,128)S(1)}, f32[96,128]{1,0:T(8,128)S(1)}, u32[]{:S(2)}, u32[]{:S(2)}) collective-permute-start(f32[96,128]{1,0:T(8,128)S(1)} %add.19.mine), channel_id=1, source_target_pairs={{0,8},{8,0},{16,24},{24,16},{1,9},{9,1},{17,25},{25,17},{2,10},{10... | collective-permute-start | bytes 147464 | tf_op jit(solution)/shard_map/ppermute | solution.py:606
  85.7 26.9 %collective-permute-start.22 = (f32[8,4,24,256]{3,2,1,0:T(8,128)S(1)}, f32[8,4,24,256]{3,2,1,0:T(8,128)S(1)}, u32[]{:S(2)}, u32[]{:S(2)}) collective-permute-start(f32[8,4,24,256]{3,2,1,0:T(8,128)S(1)} %get-tuple-element.65.refs_8_), channel_id=1, source_target_pairs={{0,8},{8,0},{16,24},{24,16},{1,9},{9,1},{17,25},{25,17},{2,10},{10... | collective-permute-start | bytes 2359304 | tf_op jit(solution)/shard_map/ppermute | solution.py:606
  86.2 26.4 %collective-permute-start.18 = (f32[8,4,24,256]{3,2,1,0:T(8,128)S(1)}, f32[8,4,24,256]{3,2,1,0:T(8,128)S(1)}, u32[]{:S(2)}, u32[]{:S(2)}) collective-permute-start(f32[8,4,24,256]{3,2,1,0:T(8,128)S(1)} %last_free.1.refs_0_), channel_id=1, source_target_pairs={{0,8},{8,0},{16,24},{24,16},{1,9},{9,1},{17,25},{25,17},{2,10},{10... | collective-permute-start | bytes 2359304 | tf_op jit(solution)/shard_map/ppermute | solution.py:606
  86.3 26.3 %collective-permute-start.21 = (f32[8,4,24,256]{3,2,1,0:T(8,128)S(1)}, f32[8,4,24,256]{3,2,1,0:T(8,128)S(1)}, u32[]{:S(2)}, u32[]{:S(2)}) collective-permute-start(f32[8,4,24,256]{3,2,1,0:T(8,128)S(1)} %collective-permute-done.5.refs_14_.refs_6_), channel_id=1, source_target_pairs={{0,8},{8,0},{16,24},{24,16},{1,9},{9,1},{17,25},{25,17},{2,10},{10... | collective-permute-start | bytes 2359304 | tf_op jit(solution)/shard_map/ppermute | solution.py:606
  86.9 25.7 %collective-permute-start.24 = (f32[8,4,24,256]{3,2,1,0:T(8,128)S(1)}, f32[8,4,24,256]{3,2,1,0:T(8,128)S(1)}, u32[]{:S(2)}, u32[]{:S(2)}) collective-permute-start(f32[8,4,24,256]{3,2,1,0:T(8,128)S(1)} %collective-permute-done.23.refs_10_), channel_id=1, source_target_pairs={{0,8},{8,0},{16,24},{24,16},{1,9},{9,1},{17,25},{25,17},{2,10},{10... | collective-permute-start | bytes 2359304 | tf_op jit(solution)/shard_map/ppermute | solution.py:606
  105.6 7.0 %collective-permute-start.20 = (f32[8,4,24,256]{3,2,1,0:T(8,128)S(1)}, f32[8,4,24,256]{3,2,1,0:T(8,128)S(1)}, u32[]{:S(2)}, u32[]{:S(2)}) collective-permute-start(f32[8,4,24,256]{3,2,1,0:T(8,128)S(1)} %collective-permute-done.19.refs_2_), channel_id=1, source_target_pairs={{0,8},{8,0},{16,24},{24,16},{1,9},{9,1},{17,25},{25,17},{2,10},{10... | collective-permute-start | bytes 2359304 | tf_op jit(solution)/shard_map/ppermute | solution.py:606

commit v10 on v9

--- a/solution.py
+++ b/solution.py
@@ -57,6 +57,11 @@
 
 NN = ((1,), (0,))
 NT = ((1,), (1,))
+
+
+def position():
+    member = lax.axis_index("member")
+    return member & 1, lax.axis_index("space"), member
 
 
 def react(free, receptor, complexed, internal, binding):
@@ -90,7 +95,7 @@
     return spread_free(read(x, z), beside(read, x, z, nx, nz, None, None), None, diffusivity) + rest
 
 
-def first_edges_kernel(place, below, above, diffusivity, binding, source, first, last):
+def first_edges_kernel(below, above, diffusivity, binding, source, first, last):
     _, _, nz, members, _ = below.shape
     nx = diffusivity.shape[0]
     for x, ends, out in ((0, below, first), (nx - 1, above, last)):
@@ -311,17 +316,14 @@
             )
 
 
-def forecast_call(kernel, name, inputs, outputs, cells, scratch=(), ready=(), scalars=()):
+def forecast_call(kernel, name, inputs, outputs, cells, scratch=(), ready=()):
     def body(*refs):
-        count = len(scalars) + len(inputs)
-        kernel(*refs[:count], *refs[count + len(ready) :])
+        kernel(*refs[: len(inputs)], *refs[len(inputs) + len(ready) :])
 
     return pl.pallas_call(
         body,
         out_shape=[jax.ShapeDtypeStruct(shape, f32) for shape in outputs],
-        in_specs=[SMEM] * len(scalars)
-        + [VMEM] * len(inputs)
-        + [pl.BlockSpec(memory_space=pl.ANY)] * len(ready),
+        in_specs=[VMEM] * len(inputs) + [pl.BlockSpec(memory_space=pl.ANY)] * len(ready),
         out_specs=[VMEM] * len(outputs),
         scratch_shapes=[pltpu.VMEM(shape, f32) for shape in scratch],
         compiler_params=pltpu.CompilerParams(vmem_limit_bytes=SCOPED),
@@ -329,10 +331,11 @@
             flops=30 * cells, bytes_accessed=32 * cells, transcendentals=0
         ),
         name=name,
-    )(*scalars, *inputs, *ready)
-
-
-def weights_kernel(place, owner, obs_index, observed, obs_var, omega, eta):
+    )(*inputs, *ready)
+
+
+def weights_kernel(owner, obs_index, observed, obs_var, omega, eta):
+    place = position()
     count, rows, ny = omega.shape
     batch_size = obs_index.shape[1]
     for k in range(count):
@@ -366,19 +369,20 @@
         eta[k] = sums[rows:]
 
 
-def voxel_weights(place, owner, obs_index, observed, obs_var, count, rows, ny):
+def voxel_weights(owner, obs_index, observed, obs_var, count, rows, ny):
     out = jax.ShapeDtypeStruct((count, rows, ny), f32)
     return pl.pallas_call(
         weights_kernel,
         out_shape=[out, out],
-        in_specs=[SMEM, SMEM, VMEM, VMEM, VMEM],
+        in_specs=[SMEM, VMEM, VMEM, VMEM],
         out_specs=[VMEM, VMEM],
         compiler_params=pltpu.CompilerParams(vmem_limit_bytes=SCOPED),
         name="voxel_weights",
-    )(place, owner, obs_index, observed, obs_var)
-
-
-def gram_kernel(place, owner, omega, eta, *refs, offsets, planes, first):
+    )(owner, obs_index, observed, obs_var)
+
+
+def gram_kernel(owner, omega, eta, *refs, offsets, planes, first):
+    place = position()
     if first:
         *sources, out, members_at = refs
     else:
@@ -425,7 +429,7 @@
     packed[...] = jnp.where(column == members + 2, pick(column == members, below), both)
 
 
-def gram(place, owner, omega, eta, begun, sources, offsets, planes):
+def gram(owner, omega, eta, begun, sources, offsets, planes):
     _, _, rows, ny = sources[0].shape
     members = rows * len(sources)
     whole = (omega.shape[0], members, LANES)
@@ -434,12 +438,12 @@
     return pl.pallas_call(
         functools.partial(gram_kernel, offsets=offsets, planes=planes, first=first),
         out_shape=jax.ShapeDtypeStruct(whole if first else whole[1:], f32),
-        in_specs=[SMEM, SMEM] + [VMEM] * (2 + len(sources) + (not first)),
+        in_specs=[SMEM] + [VMEM] * (2 + len(sources) + (not first)),
         out_specs=VMEM,
         scratch_shapes=[work] if first else [pltpu.VMEM(whole, f32), work],
         compiler_params=pltpu.CompilerParams(vmem_limit_bytes=SCOPED),
         name="gram",
-    )(place, owner, omega, eta, *([] if first else [begun]), *sources)
+    )(owner, omega, eta, *([] if first else [begun]), *sources)
 
 
 def turned(x):
@@ -490,7 +494,8 @@
     return wide_dot(wide_left(total), wide_right(mixing))
 
 
-def early_kernel(place, mine, other, total, last, ordered):
+def early_kernel(mine, other, total, last, ordered):
+    place = position()
     members = mine.shape[0]
     row = lax.broadcasted_iota(jnp.int32, (members, LANES), 0)
     column = lax.broadcasted_iota(jnp.int32, (members, LANES), 1)
@@ -517,7 +522,8 @@
     last[...] = ordered[batches - 1]
 
 
-def late_kernel(place, total, last, out, work, *, offsets, blocks, rows):
+def late_kernel(total, last, out, work, *, offsets, blocks, rows):
+    place = position()
     members = total.shape[0]
     product = batch_transform(last[...], total[...], members)
     rest = jnp.zeros((LANES - members, LANES), f32)
@@ -536,7 +542,7 @@
     return pl.pallas_call(
         kernel,
         out_shape=[jax.ShapeDtypeStruct(shape, f32) for shape in outputs],
-        in_specs=[SMEM] + [VMEM] * (len(inputs) - 1),
+        in_specs=[VMEM] * len(inputs),
         out_specs=[VMEM] * len(outputs),
         scratch_shapes=[pltpu.VMEM(shape, f32) for shape in scratch],
         compiler_params=pltpu.CompilerParams(vmem_limit_bytes=SCOPED),
@@ -556,17 +562,22 @@
     ]
     members = blocks * free[0].shape[2]
     high, low = split(weights[:, :members])
-    both = jnp.concatenate([high.astype(f32), low.astype(f32)], axis=0).astype(bf16)
-    mul = functools.partial(
-        lax.dot_general, dimension_numbers=(NN, ((), ())), preferred_element_type=f32
-    )
+    high, low = high.astype(f32), low.astype(f32)
+    both = jnp.concatenate(
+        [
+            jnp.concatenate([high, high], axis=1),
+            jnp.concatenate([low, jnp.zeros_like(low)], axis=1),
+        ],
+        axis=0,
+    ).astype(bf16)
 
     def mixed(held, x, z):
         parts = [array[x, z] for array in held]
         values = parts[0] if blocks == 1 else jnp.concatenate(parts, axis=0)
-        value_high, value_low = split(values)
-        upper = mul(both, value_high)
-        return upper[:rows] + (upper[rows:] + mul(high, value_low))
+        out = jnp.dot(
+            both, jnp.concatenate(split(values), axis=0), preferred_element_type=f32
+        )
+        return out[:rows] + out[rows:]
 
     def plane(tracer, at):
         for z in range(nz):
@@ -606,11 +617,8 @@
     return lax.ppermute(x, axis, [(k, k ^ bit) for k in range(count)])
 
 
-def total_over(x, axis, *before_last):
-    bit, count = 1, lax.axis_size(axis)
-    while bit < count:
-        if before_last and 2 * bit >= count:
-            x = lax.optimization_barrier((x, *before_last))[0]
+def total_over(x, axis, bit):
+    while bit < lax.axis_size(axis):
         x = x + swap(x, axis, bit)
         bit *= 2
     return x
@@ -623,7 +631,6 @@
     members = rows * devices
     batches = owner.shape[0]
     member = lax.axis_index("member")
-    place = jnp.stack([member & 1, lax.axis_index("space"), member]).astype(jnp.int32)
 
     forward = [(k, k + 1) for k in range(spaces - 1)]
     backward = [(k + 1, k) for k in range(spaces - 1)]
@@ -673,14 +680,14 @@
         [*ends, *coefficients],
         [(nz, 2 * rows + 8, ny)] * 2,
         2 * cells // nx,
-        scalars=[place],
     )
     fields = [jnp.transpose(ensemble[:, k], (1, 2, 0, 3)) for k in range(species)]
     conserved = fields[1] + fields[2] + fields[3]
     omega, eta = voxel_weights(
-        place, owner, obs_index, observed, obs_var, batches // 2, nx * nz, ny
+        owner, obs_index, observed, obs_var, batches // 2, nx * nz, ny
     )
     around = origin = halos(*edges)
+    conserved = collect(conserved, *around, *fields)
     payload = (nz, 2 * rows, ny)
     for step in range(SUBSTEPS // 2 - 2):
         inputs = [*fields, *around, *origin, *coefficients]
@@ -692,8 +699,6 @@
         fields = forecast_call(
             two_substeps_kernel, "two_substeps", inputs, [whole] * 4, 2 * cells, scratch=[whole] * 4
         )
-        if step == 0:
-            conserved = collect(conserved, fields[0])
     inner, end = (nx - 2, nz, rows, ny), (2, nz, rows, ny)
     before, first, last, free, tracer, internal, add, ends = forecast_call(
         last_steps_kernel,
@@ -716,7 +721,7 @@
     tracer = complete(tracer, tracer_ends)
     tracer_ends = collect(tracer_ends)
     conserved = complete(conserved, tracer_ends[0])
-    begun = gram(place, owner, omega, eta, None, tracer, offsets, (1, 1))
+    begun = gram(owner, omega, eta, None, tracer, offsets, (1, 1))
     tracer_ends = complete(tracer_ends, begun)
     (free,) = forecast_call(
         last_free_kernel,
@@ -726,9 +731,10 @@
         cells,
     )
     internal = collect(internal, across(tracer_ends))
-    half = gram(place, owner, omega, eta, begun, tracer_ends, offsets, (0, nx - 1))
+    half = gram(owner, omega, eta, begun, tracer_ends, offsets, (0, nx - 1))
+    half = half + swap(half, "space", 1)
     free = collect(free, half)
-    half = total_over(half, "space")
+    half = total_over(half, "space", 2)
     other = swap(half, "member", 1)
     internal = complete(internal, half)
     square = (members, LANES)
@@ -737,7 +743,7 @@
         "transforms_early",
         [square, square],
         [(batches, members, LANES)],
-        [place, half, other],
+        [half, other],
     )
     free = complete(free, total)
     (weights,) = transform_call(
@@ -745,7 +751,7 @@
         "transforms_late",
         [(LANES, LANES) if blocks == 1 else (rows, LANES)],
         [(LANES, LANES)],
-        [place, total, extended],
+        [total, extended],
     )
     if blocks == 1:
         weights = lax.dynamic_slice(weights, (member * rows, 0), (rows, LANES))

time: 118 us -> 117 us (level)
  local copies, waits for them, and re-layouts: 6.9 us -> 4.89 us
  Pallas kernels: 39.9 us -> 41.6 us
    pallas_call x2, Pallas kernels: 1.25 us -> 4.5 us  [gram(): pl.pallas_call(functools.partial(gram_kernel, offsets=offsets, planes=pla...]
    ppermute x19, waiting for transfers between devices: 14.9 us -> 16.5 us  [swap(): return lax.ppermute(x, axis, [(k, k ^ bit) for k in range(count)])]
    transpose x1, local copies, waits for them, and re-layouts: 1.61 us -> 0.37 us  [local(): jnp.transpose(ensemble[:, :3, part], (1, 2, 3, 0, 4))]
  transfers between devices with their start and end apart: 25 -> 25, of which waited for: 13 -> 12; matrix products, arithmetic and copies ran while one was open for 3% -> 4% of each run, Pallas kernels for 26% -> 27%
where the time goes in v10:
time: 117 us; the launch traced here: 116 us
  Pallas kernels  41.6 us (36%)
  starting transfers between devices  34.5 us (29%)
  waiting for transfers between devices  33.8 us (29%)
  local copies, waits for them, and re-layouts  4.89 us (4%)
  other arithmetic  1.29 us (1%)
    pallas_call x2, Pallas kernels, transform_call(): pl.pallas_call(kernel, out_shape=[jax.ShapeDtypeStruct(shape, f32) for sh...  24 us
    ppermute x19, starting transfers between devices, swap(): return lax.ppermute(x, axis, [(k, k ^ bit) for k in range(count)])  16.7 us
    ppermute x19, waiting for transfers between devices, swap(): return lax.ppermute(x, axis, [(k, k ^ bit) for k in range(count)])  16.5 us
    ppermute x3, starting transfers between devices, halos(): lax.ppermute(last, 'space', forward)  13.7 us
    ppermute x3, waiting for transfers between devices, halos(): lax.ppermute(first, 'space', backward)  11.5 us
    pallas_call x6, Pallas kernels, forecast_call(): pl.pallas_call(body, out_shape=[jax.ShapeDtypeStruct(shape, f32) for shap...  5.91 us
    pallas_call x1, Pallas kernels, mix(): pl.pallas_call(functools.partial(mix_kernel, blocks=blocks), grid=(nx,),...  5.86 us
    ppermute x3, waiting for transfers between devices, halos(): lax.ppermute(last, 'space', forward)  5.74 us
  transfers between devices with their start and end apart: 25, of which 12 were waited for; matrix products, arithmetic and copies ran while one was open for 4% of the time, Pallas kernels for 27%

profile of v10, /device:TPU:0, one launch (start us, length us, event | category | flops | bytes accessed | tf_op | source)
XLA Modules:
  0.0 116.5 jit_solution(14288243873099526356)
XLA Ops:
  0.0 1.6 %fusion = (f32[24,3,2,4,256]{4,3,2,1,0:T(4,128)S(1)}, f32[24,3,2,4,256]{4,3,2,1,0:T(4,128)S(1)}) fusion(f32[24,4,8,4,256]{4,3,2,1,0:T(4,128)} %param.8), kind=kLoop, calls=%fused_computation.7 | loop fusion | bytes 2359296 | tf_op jit(solution)/shard_map/slice | solution.py:674
  1.6 0.4 copy_bitcast_fusion.4
  2.0 0.2 first_edges.1
  2.2 4.9 %collective-permute-start = (f32[4,56,256]{2,1,0:T(8,128)S(1)}, f32[4,56,256]{2,1,0:T(8,128)S(1)}, u32[]{:S(2)}, u32[]{:S(2)}) collective-permute-start(f32[4,56,256]{2,1,0:T(8,128)S(1)} %get-tuple-element.38), channel_id=1, source_target_pairs={{0,1},{1,2},{2,3},{3,4},{4,5},{5,6},{6,7},{8,9},{9,10},{10,11},{11... | collective-permute-start | bytes 688136 | tf_op jit(solution)/shard_map/ppermute | solution.py:639
  7.1 1.3 %collective-permute-start.1 = (f32[4,56,256]{2,1,0:T(8,128)S(1)}, f32[4,56,256]{2,1,0:T(8,128)S(1)}, u32[]{:S(2)}, u32[]{:S(2)}) collective-permute-start(f32[4,56,256]{2,1,0:T(8,128)S(1)} %get-tuple-element.39), channel_id=1, source_target_pairs={{1,0},{2,1},{3,2},{4,3},{5,4},{6,5},{7,6},{9,8},{10,9},{11,10},{12... | collective-permute-start | bytes 688136 | tf_op jit(solution)/shard_map/ppermute | solution.py:639
  8.4 1.0 fusion.1
  9.5 1.3 %add_add_fusion.refs_4_ = f32[8,4,24,256]{3,2,1,0:T(8,128)S(1)} fusion(f32[24,1,8,4,256]{4,3,2,1,0:T(4,128)S(1)} %get-tuple-element.71, f32[24,1,8,4,256]{4,3,2,1,0:T(4,128)S(1)} %get-tuple-element.70, f32[24,1,8,4,256]{4,3,2,1,0:T(4,128)S(1)} %get-tuple-element.69), kind=kLoop, calls=%fused_computation.4 | loop fusion | flops 393216 | bytes 3145728 | tf_op jit(solution)/shard_map/add | solution.py:685
  10.7 0.1 collective-permute-start.4
  10.8 0.9 copy_bitcast_fusion
  11.8 0.0 copy-start.3
  11.8 0.0 copy-start.4
  11.8 0.0 copy-start.5
  11.8 0.0 copy-start.6
  11.8 0.9 copy_bitcast_fusion.2
  12.7 4.1 %collective-permute-done.refs_4_.refs_6_.refs_7_ = f32[4,56,256]{2,1,0:T(8,128)S(1)} collective-permute-done((f32[4,56,256]{2,1,0:T(8,128)S(1)}, f32[4,56,256]{2,1,0:T(8,128)S(1)}, u32[]{:S(2)}, u32[]{:S(2)}) %collective-permute-start) | collective-permute-done | bytes 229408 | tf_op jit(solution)/shard_map/ppermute | solution.py:639
  16.9 0.0 collective-permute-done.1.refs_5_.refs_7_.refs_8_
  16.9 1.5 %collective-permute-start.5 = (f32[8,4,24,256]{3,2,1,0:T(8,128)S(1)}, f32[8,4,24,256]{3,2,1,0:T(8,128)S(1)}, u32[]{:S(2)}, u32[]{:S(2)}) collective-permute-start(f32[8,4,24,256]{3,2,1,0:T(8,128)S(1)} %add_add_fusion.refs_4_), channel_id=1, source_target_pairs={{0,16},{8,24},{16,0},{24,8},{1,17},{9,25},{17,1},{25,9},{2,18},{10... | collective-permute-start | bytes 2359304 | tf_op jit(solution)/shard_map/ppermute | solution.py:617
  18.4 1.0 next_edges.1
  19.3 4.4 %collective-permute-start.2 = (f32[4,48,256]{2,1,0:T(8,128)S(1)}, f32[4,48,256]{2,1,0:T(8,128)S(1)}, u32[]{:S(2)}, u32[]{:S(2)}) collective-permute-start(f32[4,48,256]{2,1,0:T(8,128)S(1)} %get-tuple-element.44), channel_id=1, source_target_pairs={{0,1},{1,2},{2,3},{3,4},{4,5},{5,6},{6,7},{8,9},{9,10},{10,11},{11... | collective-permute-start | bytes 589832 | tf_op jit(solution)/shard_map/ppermute | solution.py:639
  23.7 1.3 %collective-permute-start.3 = (f32[4,48,256]{2,1,0:T(8,128)S(1)}, f32[4,48,256]{2,1,0:T(8,128)S(1)}, u32[]{:S(2)}, u32[]{:S(2)}) collective-permute-start(f32[4,48,256]{2,1,0:T(8,128)S(1)} %get-tuple-element.45), channel_id=1, source_target_pairs={{1,0},{2,1},{3,2},{4,3},{5,4},{6,5},{7,6},{9,8},{10,9},{11,10},{12... | collective-permute-start | bytes 589832 | tf_op jit(solution)/shard_map/ppermute | solution.py:639
  25.1 1.4 %voxel_weights.1 = (f32[2,32,256]{2,1,0:T(8,128)S(1)}, f32[2,32,256]{2,1,0:T(8,128)S(1)}) custom-call(s32[4]{0:T(128)S(1)} %copy-done.6, s32[4,2048]{1,0:T(4,128)S(1)} %copy-done.3, f32[4,2048]{1,0:T(4,128)S(1)} %copy-done.4, f32[4,2048]{1,0:T(4,128)S(1)} %copy-done.5), custom_call_target="tpu_custom_call" | custom-call | tf_op jit(solution)/shard_map/voxel_weights/pallas_call | solution.py:374
  26.5 1.5 %two_substeps.1 = (f32[8,4,24,256]{3,2,1,0:T(8,128)S(1)}, f32[8,4,24,256]{3,2,1,0:T(8,128)S(1)}, f32[8,4,24,256]{3,2,1,0:T(8,128)S(1)}, f32[8,4,24,256]{3,2,1,0:T(8,128)S(1)}) custom-call(f32[8,4,24,256]{3,2,1,0:T(8,128)S(1)} %get-tuple-element.76.refs_0_, f32[8,4,24,256]{3,2,1,0:T(8,128)S(1)} %get-tuple-element.75.refs_1_, ...), custom_call_target="tpu_custom_call" | custom-call | flops 11796480 | bytes 12582912 | tf_op jit(solution)/shard_map/two_substeps/pallas_call | solution.py:323
  28.1 0.0 collective-permute-done.2.refs_4_
  28.1 4.5 %collective-permute-done.3.refs_5_ = f32[4,48,256]{2,1,0:T(8,128)S(1)} collective-permute-done((f32[4,48,256]{2,1,0:T(8,128)S(1)}, f32[4,48,256]{2,1,0:T(8,128)S(1)}, u32[]{:S(2)}, u32[]{:S(2)}) %collective-permute-start.3) | collective-permute-done | bytes 196640 | tf_op jit(solution)/shard_map/ppermute | solution.py:639
  32.6 1.6 %collective-permute-done.5.refs_14_.refs_6_ = f32[8,4,24,256]{3,2,1,0:T(8,128)S(1)} collective-permute-done((f32[8,4,24,256]{3,2,1,0:T(8,128)S(1)}, f32[8,4,24,256]{3,2,1,0:T(8,128)S(1)}, u32[]{:S(2)}, u32[]{:S(2)}) %collective-permute-start.5) | collective-permute-done | bytes 786464 | tf_op jit(solution)/shard_map/ppermute | solution.py:617
  34.2 2.6 %last_steps.1 = (f32[8,4,24,256]{3,2,1,0:T(8,128)S(1)}, f32[4,48,256]{2,1,0:T(8,128)S(1)}, f32[4,48,256]{2,1,0:T(8,128)S(1)}, f32[8,4,24,256]{3,2,1,0:T(8,128)S(...) custom-call(f32[8,4,24,256]{3,2,1,0:T(8,128)S(1)} %get-tuple-element, ...), custom_call_target="tpu_custom_call" | custom-call | flops 23592960 | bytes 25165824 | tf_op jit(solution)/shard_map/last_steps/pallas_call | solution.py:323
  36.8 1.6 %collective-permute-start.7 = (f32[6,4,24,256]{3,2,1,0:T(8,128)S(1)}, f32[6,4,24,256]{3,2,1,0:T(8,128)S(1)}, u32[]{:S(2)}, u32[]{:S(2)}) collective-permute-start(f32[6,4,24,256]{3,2,1,0:T(8,128)S(1)} %get-tuple-element.47.refs_0_.refs_12_), channel_id=1, source_target_pairs={{0,16},{8,24},{16,0},{24,8},{1,17},{9,25},{17,1},{25,9},{2,18},{10... | collective-permute-start | bytes 1769480 | tf_op jit(solution)/shard_map/ppermute | solution.py:617
  38.4 4.4 %collective-permute-start.8 = (f32[4,48,256]{2,1,0:T(8,128)S(1)}, f32[4,48,256]{2,1,0:T(8,128)S(1)}, u32[]{:S(2)}, u32[]{:S(2)}) collective-permute-start(f32[4,48,256]{2,1,0:T(8,128)S(1)} %get-tuple-element.50), channel_id=1, source_target_pairs={{0,1},{1,2},{2,3},{3,4},{4,5},{5,6},{6,7},{8,9},{9,10},{10,11},{11... | collective-permute-start | bytes 589832 | tf_op jit(solution)/shard_map/ppermute | solution.py:639
  42.8 1.5 %collective-permute-start.9 = (f32[4,48,256]{2,1,0:T(8,128)S(1)}, f32[4,48,256]{2,1,0:T(8,128)S(1)}, u32[]{:S(2)}, u32[]{:S(2)}) collective-permute-start(f32[4,48,256]{2,1,0:T(8,128)S(1)} %get-tuple-element.51), channel_id=1, source_target_pairs={{1,0},{2,1},{3,2},{4,3},{5,4},{6,5},{7,6},{9,8},{10,9},{11,10},{12... | collective-permute-start | bytes 589832 | tf_op jit(solution)/shard_map/ppermute | solution.py:639
  44.3 0.1 collective-permute-start.6
  44.4 1.6 %collective-permute-done.8.refs_2_.refs_5_ = f32[4,48,256]{2,1,0:T(8,128)S(1)} collective-permute-done((f32[4,48,256]{2,1,0:T(8,128)S(1)}, f32[4,48,256]{2,1,0:T(8,128)S(1)}, u32[]{:S(2)}, u32[]{:S(2)}) %collective-permute-start.8) | collective-permute-done | bytes 196640 | tf_op jit(solution)/shard_map/ppermute | solution.py:639
  46.0 7.0 %collective-permute-done.9.refs_3_.refs_6_ = f32[4,48,256]{2,1,0:T(8,128)S(1)} collective-permute-done((f32[4,48,256]{2,1,0:T(8,128)S(1)}, f32[4,48,256]{2,1,0:T(8,128)S(1)}, u32[]{:S(2)}, u32[]{:S(2)}) %collective-permute-start.9) | collective-permute-done | bytes 196640 | tf_op jit(solution)/shard_map/ppermute | solution.py:639
  52.9 0.1 last_ends.1
  53.1 0.0 collective-permute-done.7.refs_2_.refs_14_
  53.1 0.1 collective-permute-start.10
  53.1 0.6 collective-permute-start.12
  53.7 0.2 collective-permute-start.11
  53.9 1.2 %collective-permute-done.10.refs_3_.refs_15_ = f32[6,4,24,256]{3,2,1,0:T(8,128)S(1)} collective-permute-done((f32[6,4,24,256]{3,2,1,0:T(8,128)S(1)}, f32[6,4,24,256]{3,2,1,0:T(8,128)S(1)}, u32[]{:S(2)}, u32[]{:S(2)}) %collective-permute-start.10) | collective-permute-done | bytes 589856 | tf_op jit(solution)/shard_map/ppermute | solution.py:617
  55.1 3.0 %gram.2.refs_0_ = f32[2,96,128]{2,1,0:T(8,128)S(1)} custom-call(s32[4]{0:T(128)S(1)} %copy-done.6, f32[2,32,256]{2,1,0:T(8,128)S(1)} %get-tuple-element.36.refs_11_.omega, f32[2,32,256]{2,1,0:T(8,128)S(1)} %get-tuple-element.37.refs_12_.eta, f32[6,4,24,256]{3,2,1,0:T(8,128)S(1)} %get-tuple-element.47.refs_0_.refs_12_, ...), custom_call_target="tpu_custom_call" | custom-call | tf_op jit(solution)/shard_map/gram/pallas_call | solution.py:438
  58.1 2.3 %collective-permute-done.12.refs_3_.refs_18_ = f32[2,4,24,256]{3,2,1,0:T(8,128)S(1)} collective-permute-done((f32[2,4,24,256]{3,2,1,0:T(8,128)S(1)}, f32[2,4,24,256]{3,2,1,0:T(8,128)S(1)}, u32[]{:S(2)}, u32[]{:S(2)}) %collective-permute-start.12) | collective-permute-done | bytes 196640 | tf_op jit(solution)/shard_map/ppermute | solution.py:617
  60.5 1.4 %collective-permute-done.13.refs_4_.refs_19_ = f32[2,4,24,256]{3,2,1,0:T(8,128)S(1)} collective-permute-done((f32[2,4,24,256]{3,2,1,0:T(8,128)S(1)}, f32[2,4,24,256]{3,2,1,0:T(8,128)S(1)}, u32[]{:S(2)}, u32[]{:S(2)}) %collective-permute-start.13) | collective-permute-done | bytes 196640 | tf_op jit(solution)/shard_map/ppermute | solution.py:617
  61.9 1.5 %gram.3 = f32[96,128]{1,0:T(8,128)S(1)} custom-call(s32[4]{0:T(128)S(1)} %copy-done.6, f32[2,32,256]{2,1,0:T(8,128)S(1)} %get-tuple-element.36.refs_11_.omega, f32[2,32,256]{2,1,0:T(8,128)S(1)} %get-tuple-element.37.refs_12_.eta, f32[2,96,128]{2,1,0:T(8,128)S(1)} %gram.2.refs_0_, f32[2,4,24,256]{3,2,1,0:T(8,128)S(1)} %get-tuple-element.52.refs_1_.refs_16_, ...), custom_call_target="tpu_custom_call" | custom-call | tf_op jit(solution)/shard_map/gram/pallas_call | solution.py:438
  63.4 2.1 %collective-permute-start.14 = (f32[96,128]{1,0:T(8,128)S(1)}, f32[96,128]{1,0:T(8,128)S(1)}, u32[]{:S(2)}, u32[]{:S(2)}) collective-permute-start(f32[96,128]{1,0:T(8,128)S(1)} %gram.3), channel_id=1, source_target_pairs={{0,1},{1,0},{2,3},{3,2},{4,5},{5,4},{6,7},{7,6},{8,9},{9,8},{10,11... | collective-permute-start | bytes 147464 | tf_op jit(solution)/shard_map/ppermute | solution.py:617
  65.5 0.5 collective-permute-start.23
  66.0 0.5 last_free.1.refs_0_
  66.5 1.1 collective-permute-done.14
  67.6 0.6 collective-permute-start.19
  68.2 3.9 %collective-permute-start.15 = (f32[96,128]{1,0:T(8,128)S(1)}, f32[96,128]{1,0:T(8,128)S(1)}, u32[]{:S(2)}, u32[]{:S(2)}) collective-permute-start(f32[96,128]{1,0:T(8,128)S(1)} %add.17), channel_id=1, source_target_pairs={{0,2},{1,3},{2,0},{3,1},{4,6},{5,7},{6,4},{7,5},{8,10},{9,11},{10,... | collective-permute-start | bytes 147464 | tf_op jit(solution)/shard_map/ppermute | solution.py:617
  72.1 2.1 %collective-permute-done.15 = f32[96,128]{1,0:T(8,128)S(1)} collective-permute-done((f32[96,128]{1,0:T(8,128)S(1)}, f32[96,128]{1,0:T(8,128)S(1)}, u32[]{:S(2)}, u32[]{:S(2)}) %collective-permute-start.15) | collective-permute-done | bytes 49184 | tf_op jit(solution)/shard_map/ppermute | solution.py:617
  74.2 4.3 %collective-permute-start.16 = (f32[96,128]{1,0:T(8,128)S(1)}, f32[96,128]{1,0:T(8,128)S(1)}, u32[]{:S(2)}, u32[]{:S(2)}) collective-permute-start(f32[96,128]{1,0:T(8,128)S(1)} %add.18), channel_id=1, source_target_pairs={{0,4},{1,5},{2,6},{3,7},{4,0},{5,1},{6,2},{7,3},{8,12},{9,13},{10,... | collective-permute-start | bytes 147464 | tf_op jit(solution)/shard_map/ppermute | solution.py:617
  78.5 2.6 %collective-permute-done.16 = f32[96,128]{1,0:T(8,128)S(1)} collective-permute-done((f32[96,128]{1,0:T(8,128)S(1)}, f32[96,128]{1,0:T(8,128)S(1)}, u32[]{:S(2)}, u32[]{:S(2)}) %collective-permute-start.16) | collective-permute-done | bytes 49184 | tf_op jit(solution)/shard_map/ppermute | solution.py:617
  81.1 0.1 collective-permute-start.17
  81.2 0.5 collective-permute-start.22
  81.7 0.1 collective-permute-start.18
  81.8 4.2 %collective-permute-done.23.refs_10_ = f32[8,4,24,256]{3,2,1,0:T(8,128)S(1)} collective-permute-done((f32[8,4,24,256]{3,2,1,0:T(8,128)S(1)}, f32[8,4,24,256]{3,2,1,0:T(8,128)S(1)}, u32[]{:S(2)}, u32[]{:S(2)}) %collective-permute-start.23) | collective-permute-done | bytes 786464 | tf_op jit(solution)/shard_map/ppermute | solution.py:617
  86.0 0.0 collective-permute-start.21
  86.0 0.0 collective-permute-done.17.other
  86.0 0.5 collective-permute-start.24
  86.5 17.9 %transforms_early.1 = (f32[96,128]{1,0:T(8,128)S(1)}, f32[96,128]{1,0:T(8,128)S(1)}) custom-call(f32[96,128]{1,0:T(8,128)S(1)} %add.19.mine, f32[96,128]{1,0:T(8,128)S(1)} %collective-permute-done.17.other), custom_call_target="tpu_custom_call" | custom-call | flops 100000000 | bytes 1000000 | tf_op jit(solution)/shard_map/transforms_early/pallas_call | solution.py:542
  104.4 0.0 collective-permute-done.19.refs_2_
  104.4 0.1 collective-permute-start.20
  104.5 6.0 %transforms_late.1.weights = f32[24,128]{1,0:T(8,128)S(1)} custom-call(f32[96,128]{1,0:T(8,128)S(1)} %get-tuple-element.55.total, f32[96,128]{1,0:T(8,128)S(1)} %get-tuple-element.56.last), custom_call_target="tpu_custom_call" | custom-call | flops 100000000 | bytes 1000000 | tf_op jit(solution)/shard_map/transforms_late/pallas_call | solution.py:542
  110.6 0.0 collective-permute-done.21.refs_7_
  110.6 5.9 %mix.1 = f32[24,4,8,4,256]{4,3,2,1,0:T(4,128)} custom-call(f32[24,128]{1,0:T(8,128)S(1)} %transforms_late.1.weights, f32[8,4,24,256]{3,2,1,0:T(8,128)S(1)} %last_free.1.refs_0_, f32[8,4,24,256]{3,2,1,0:T(8,128)S(1)} %collective-permute-done.18.refs_1_, f32[8,4,24,256]{3,2,1,0:T(8,128)S(1)} %collective-permute-done.19.refs_2_, ...), custom_call_target="tpu_custom_call" | custom-call | tf_op jit(solution)/shard_map/mix/pallas_call | solution.py:604
  (23 shorter events, 0.1 us)
Async XLA Ops:
  0.0 8.4 %copy-start.7 = (f32[24,4,8,4,256]{4,3,2,1,0:T(4,128)S(1)}, f32[24,4,8,4,256]{4,3,2,1,0:T(4,128)}, u32[]{:S(2)}) copy-start(f32[24,4,8,4,256]{4,3,2,1,0:T(4,128)} %param.8) | copy-start | bytes 9437188
  0.0 2.0 %copy-start = (f32[8,4,256]{2,1,0:T(4,128)S(1)}, f32[8,4,256]{2,1,0:T(4,128)}, u32[]{:S(2)}) copy-start(f32[8,4,256]{2,1,0:T(4,128)} %refs_9_.7) | copy-start | bytes 98308
  0.0 2.0 %copy-start.2 = (f32[8,4,256]{2,1,0:T(4,128)S(1)}, f32[8,4,256]{2,1,0:T(4,128)}, u32[]{:S(2)}) copy-start(f32[8,4,256]{2,1,0:T(4,128)} %refs_6_.1) | copy-start | bytes 98308
  0.0 2.0 %copy-start.1 = (f32[8,4,256]{2,1,0:T(4,128)S(1)}, f32[8,4,256]{2,1,0:T(4,128)}, u32[]{:S(2)}) copy-start(f32[8,4,256]{2,1,0:T(4,128)} %refs_5_.1) | copy-start | bytes 98308
  2.2 14.6 %collective-permute-start = (f32[4,56,256]{2,1,0:T(8,128)S(1)}, f32[4,56,256]{2,1,0:T(8,128)S(1)}, u32[]{:S(2)}, u32[]{:S(2)}) collective-permute-start(f32[4,56,256]{2,1,0:T(8,128)S(1)} %get-tuple-element.38), channel_id=1, source_target_pairs={{0,1},{1,2},{2,3},{3,4},{4,5},{5,6},{6,7},{8,9},{9,10},{10,11},{11... | collective-permute-start | bytes 688136 | tf_op jit(solution)/shard_map/ppermute | solution.py:639
  7.1 9.7 %collective-permute-start.1 = (f32[4,56,256]{2,1,0:T(8,128)S(1)}, f32[4,56,256]{2,1,0:T(8,128)S(1)}, u32[]{:S(2)}, u32[]{:S(2)}) collective-permute-start(f32[4,56,256]{2,1,0:T(8,128)S(1)} %get-tuple-element.39), channel_id=1, source_target_pairs={{1,0},{2,1},{3,2},{4,3},{5,4},{6,5},{7,6},{9,8},{10,9},{11,10},{12... | collective-permute-start | bytes 688136 | tf_op jit(solution)/shard_map/ppermute | solution.py:639
  10.7 21.9 %collective-permute-start.4 = (f32[8,4,24,256]{3,2,1,0:T(8,128)S(1)}, f32[8,4,24,256]{3,2,1,0:T(8,128)S(1)}, u32[]{:S(2)}, u32[]{:S(2)}) collective-permute-start(f32[8,4,24,256]{3,2,1,0:T(8,128)S(1)} %add_add_fusion.refs_4_), channel_id=1, source_target_pairs={{0,8},{8,0},{16,24},{24,16},{1,9},{9,1},{17,25},{25,17},{2,10},{10... | collective-permute-start | bytes 2359304 | tf_op jit(solution)/shard_map/ppermute | solution.py:617
  11.8 13.3 %copy-start.3 = (s32[4,2048]{1,0:T(4,128)S(1)}, s32[4,2048]{1,0:T(4,128)}, u32[]{:S(2)}) copy-start(s32[4,2048]{1,0:T(4,128)} %obs_index.1) | copy-start | bytes 98308
  11.8 13.3 %copy-start.4 = (f32[4,2048]{1,0:T(4,128)S(1)}, f32[4,2048]{1,0:T(4,128)}, u32[]{:S(2)}) copy-start(f32[4,2048]{1,0:T(4,128)} %observed.1) | copy-start | bytes 98308
  11.8 13.3 %copy-start.5 = (f32[4,2048]{1,0:T(4,128)S(1)}, f32[4,2048]{1,0:T(4,128)}, u32[]{:S(2)}) copy-start(f32[4,2048]{1,0:T(4,128)} %obs_var.1) | copy-start | bytes 98308
  11.8 13.3 %copy-start.6 = (s32[4]{0:T(128)S(1)}, s32[4]{0:T(128)}, u32[]{:S(2)}) copy-start(s32[4]{0:T(128)} %owner.5) | copy-start | bytes 52
  16.9 17.3 %collective-permute-start.5 = (f32[8,4,24,256]{3,2,1,0:T(8,128)S(1)}, f32[8,4,24,256]{3,2,1,0:T(8,128)S(1)}, u32[]{:S(2)}, u32[]{:S(2)}) collective-permute-start(f32[8,4,24,256]{3,2,1,0:T(8,128)S(1)} %add_add_fusion.refs_4_), channel_id=1, source_target_pairs={{0,16},{8,24},{16,0},{24,8},{1,17},{9,25},{17,1},{25,9},{2,18},{10... | collective-permute-start | bytes 2359304 | tf_op jit(solution)/shard_map/ppermute | solution.py:617
  19.3 8.7 %collective-permute-start.2 = (f32[4,48,256]{2,1,0:T(8,128)S(1)}, f32[4,48,256]{2,1,0:T(8,128)S(1)}, u32[]{:S(2)}, u32[]{:S(2)}) collective-permute-start(f32[4,48,256]{2,1,0:T(8,128)S(1)} %get-tuple-element.44), channel_id=1, source_target_pairs={{0,1},{1,2},{2,3},{3,4},{4,5},{5,6},{6,7},{8,9},{9,10},{10,11},{11... | collective-permute-start | bytes 589832 | tf_op jit(solution)/shard_map/ppermute | solution.py:639
  23.7 8.9 %collective-permute-start.3 = (f32[4,48,256]{2,1,0:T(8,128)S(1)}, f32[4,48,256]{2,1,0:T(8,128)S(1)}, u32[]{:S(2)}, u32[]{:S(2)}) collective-permute-start(f32[4,48,256]{2,1,0:T(8,128)S(1)} %get-tuple-element.45), channel_id=1, source_target_pairs={{1,0},{2,1},{3,2},{4,3},{5,4},{6,5},{7,6},{9,8},{10,9},{11,10},{12... | collective-permute-start | bytes 589832 | tf_op jit(solution)/shard_map/ppermute | solution.py:639
  36.8 16.3 %collective-permute-start.7 = (f32[6,4,24,256]{3,2,1,0:T(8,128)S(1)}, f32[6,4,24,256]{3,2,1,0:T(8,128)S(1)}, u32[]{:S(2)}, u32[]{:S(2)}) collective-permute-start(f32[6,4,24,256]{3,2,1,0:T(8,128)S(1)} %get-tuple-element.47.refs_0_.refs_12_), channel_id=1, source_target_pairs={{0,16},{8,24},{16,0},{24,8},{1,17},{9,25},{17,1},{25,9},{2,18},{10... | collective-permute-start | bytes 1769480 | tf_op jit(solution)/shard_map/ppermute | solution.py:617
  38.4 7.6 %collective-permute-start.8 = (f32[4,48,256]{2,1,0:T(8,128)S(1)}, f32[4,48,256]{2,1,0:T(8,128)S(1)}, u32[]{:S(2)}, u32[]{:S(2)}) collective-permute-start(f32[4,48,256]{2,1,0:T(8,128)S(1)} %get-tuple-element.50), channel_id=1, source_target_pairs={{0,1},{1,2},{2,3},{3,4},{4,5},{5,6},{6,7},{8,9},{9,10},{10,11},{11... | collective-permute-start | bytes 589832 | tf_op jit(solution)/shard_map/ppermute | solution.py:639
  42.8 10.1 %collective-permute-start.9 = (f32[4,48,256]{2,1,0:T(8,128)S(1)}, f32[4,48,256]{2,1,0:T(8,128)S(1)}, u32[]{:S(2)}, u32[]{:S(2)}) collective-permute-start(f32[4,48,256]{2,1,0:T(8,128)S(1)} %get-tuple-element.51), channel_id=1, source_target_pairs={{1,0},{2,1},{3,2},{4,3},{5,4},{6,5},{7,6},{9,8},{10,9},{11,10},{12... | collective-permute-start | bytes 589832 | tf_op jit(solution)/shard_map/ppermute | solution.py:639
  44.3 9.6 %collective-permute-start.6 = (f32[6,4,24,256]{3,2,1,0:T(8,128)S(1)}, f32[6,4,24,256]{3,2,1,0:T(8,128)S(1)}, u32[]{:S(2)}, u32[]{:S(2)}) collective-permute-start(f32[6,4,24,256]{3,2,1,0:T(8,128)S(1)} %get-tuple-element.47.refs_0_.refs_12_), channel_id=1, source_target_pairs={{0,8},{8,0},{16,24},{24,16},{1,9},{9,1},{17,25},{25,17},{2,10},{10... | collective-permute-start | bytes 1769480 | tf_op jit(solution)/shard_map/ppermute | solution.py:617
  53.1 2.1 %collective-permute-start.10 = (f32[6,4,24,256]{3,2,1,0:T(8,128)S(1)}, f32[6,4,24,256]{3,2,1,0:T(8,128)S(1)}, u32[]{:S(2)}, u32[]{:S(2)}) collective-permute-start(f32[6,4,24,256]{3,2,1,0:T(8,128)S(1)} %collective-permute-done.7.refs_2_.refs_14_), channel_id=1, source_target_pairs={{0,8},{8,0},{16,24},{24,16},{1,9},{9,1},{17,25},{25,17},{2,10},{10... | collective-permute-start | bytes 1769480 | tf_op jit(solution)/shard_map/ppermute | solution.py:617
  53.1 7.3 %collective-permute-start.12 = (f32[2,4,24,256]{3,2,1,0:T(8,128)S(1)}, f32[2,4,24,256]{3,2,1,0:T(8,128)S(1)}, u32[]{:S(2)}, u32[]{:S(2)}) collective-permute-start(f32[2,4,24,256]{3,2,1,0:T(8,128)S(1)} %get-tuple-element.52.refs_1_.refs_16_), channel_id=1, source_target_pairs={{0,16},{8,24},{16,0},{24,8},{1,17},{9,25},{17,1},{25,9},{2,18},{10... | collective-permute-start | bytes 589832 | tf_op jit(solution)/shard_map/ppermute | solution.py:617
  53.7 6.8 %collective-permute-start.11 = (f32[2,4,24,256]{3,2,1,0:T(8,128)S(1)}, f32[2,4,24,256]{3,2,1,0:T(8,128)S(1)}, u32[]{:S(2)}, u32[]{:S(2)}) collective-permute-start(f32[2,4,24,256]{3,2,1,0:T(8,128)S(1)} %get-tuple-element.52.refs_1_.refs_16_), channel_id=1, source_target_pairs={{0,8},{8,0},{16,24},{24,16},{1,9},{9,1},{17,25},{25,17},{2,10},{10... | collective-permute-start | bytes 589832 | tf_op jit(solution)/shard_map/ppermute | solution.py:617
  60.5 1.4 %collective-permute-start.13 = (f32[2,4,24,256]{3,2,1,0:T(8,128)S(1)}, f32[2,4,24,256]{3,2,1,0:T(8,128)S(1)}, u32[]{:S(2)}, u32[]{:S(2)}) collective-permute-start(f32[2,4,24,256]{3,2,1,0:T(8,128)S(1)} %collective-permute-done.12.refs_3_.refs_18_), channel_id=1, source_target_pairs={{0,8},{8,0},{16,24},{24,16},{1,9},{9,1},{17,25},{25,17},{2,10},{10... | collective-permute-start | bytes 589832 | tf_op jit(solution)/shard_map/ppermute | solution.py:617
  63.4 4.2 %collective-permute-start.14 = (f32[96,128]{1,0:T(8,128)S(1)}, f32[96,128]{1,0:T(8,128)S(1)}, u32[]{:S(2)}, u32[]{:S(2)}) collective-permute-start(f32[96,128]{1,0:T(8,128)S(1)} %gram.3), channel_id=1, source_target_pairs={{0,1},{1,0},{2,3},{3,2},{4,5},{5,4},{6,7},{7,6},{8,9},{9,8},{10,11... | collective-permute-start | bytes 147464 | tf_op jit(solution)/shard_map/ppermute | solution.py:617
  65.5 20.4 %collective-permute-start.23 = (f32[8,4,24,256]{3,2,1,0:T(8,128)S(1)}, f32[8,4,24,256]{3,2,1,0:T(8,128)S(1)}, u32[]{:S(2)}, u32[]{:S(2)}) collective-permute-start(f32[8,4,24,256]{3,2,1,0:T(8,128)S(1)} %get-tuple-element.65.refs_8_), channel_id=1, source_target_pairs={{0,16},{8,24},{16,0},{24,8},{1,17},{9,25},{17,1},{25,9},{2,18},{10... | collective-permute-start | bytes 2359304 | tf_op jit(solution)/shard_map/ppermute | solution.py:617
  67.6 36.8 %collective-permute-start.19 = (f32[8,4,24,256]{3,2,1,0:T(8,128)S(1)}, f32[8,4,24,256]{3,2,1,0:T(8,128)S(1)}, u32[]{:S(2)}, u32[]{:S(2)}) collective-permute-start(f32[8,4,24,256]{3,2,1,0:T(8,128)S(1)} %last_free.1.refs_0_), channel_id=1, source_target_pairs={{0,16},{8,24},{16,0},{24,8},{1,17},{9,25},{17,1},{25,9},{2,18},{10... | collective-permute-start | bytes 2359304 | tf_op jit(solution)/shard_map/ppermute | solution.py:617
  68.2 6.0 %collective-permute-start.15 = (f32[96,128]{1,0:T(8,128)S(1)}, f32[96,128]{1,0:T(8,128)S(1)}, u32[]{:S(2)}, u32[]{:S(2)}) collective-permute-start(f32[96,128]{1,0:T(8,128)S(1)} %add.17), channel_id=1, source_target_pairs={{0,2},{1,3},{2,0},{3,1},{4,6},{5,7},{6,4},{7,5},{8,10},{9,11},{10,... | collective-permute-start | bytes 147464 | tf_op jit(solution)/shard_map/ppermute | solution.py:617
  74.2 6.9 %collective-permute-start.16 = (f32[96,128]{1,0:T(8,128)S(1)}, f32[96,128]{1,0:T(8,128)S(1)}, u32[]{:S(2)}, u32[]{:S(2)}) collective-permute-start(f32[96,128]{1,0:T(8,128)S(1)} %add.18), channel_id=1, source_target_pairs={{0,4},{1,5},{2,6},{3,7},{4,0},{5,1},{6,2},{7,3},{8,12},{9,13},{10,... | collective-permute-start | bytes 147464 | tf_op jit(solution)/shard_map/ppermute | solution.py:617
  81.1 4.9 %collective-permute-start.17 = (f32[96,128]{1,0:T(8,128)S(1)}, f32[96,128]{1,0:T(8,128)S(1)}, u32[]{:S(2)}, u32[]{:S(2)}) collective-permute-start(f32[96,128]{1,0:T(8,128)S(1)} %add.19.mine), channel_id=1, source_target_pairs={{0,8},{8,0},{16,24},{24,16},{1,9},{9,1},{17,25},{25,17},{2,10},{10... | collective-permute-start | bytes 147464 | tf_op jit(solution)/shard_map/ppermute | solution.py:617
  81.2 29.4 %collective-permute-start.22 = (f32[8,4,24,256]{3,2,1,0:T(8,128)S(1)}, f32[8,4,24,256]{3,2,1,0:T(8,128)S(1)}, u32[]{:S(2)}, u32[]{:S(2)}) collective-permute-start(f32[8,4,24,256]{3,2,1,0:T(8,128)S(1)} %get-tuple-element.65.refs_8_), channel_id=1, source_target_pairs={{0,8},{8,0},{16,24},{24,16},{1,9},{9,1},{17,25},{25,17},{2,10},{10... | collective-permute-start | bytes 2359304 | tf_op jit(solution)/shard_map/ppermute | solution.py:617
  81.7 28.9 %collective-permute-start.18 = (f32[8,4,24,256]{3,2,1,0:T(8,128)S(1)}, f32[8,4,24,256]{3,2,1,0:T(8,128)S(1)}, u32[]{:S(2)}, u32[]{:S(2)}) collective-permute-start(f32[8,4,24,256]{3,2,1,0:T(8,128)S(1)} %last_free.1.refs_0_), channel_id=1, source_target_pairs={{0,8},{8,0},{16,24},{24,16},{1,9},{9,1},{17,25},{25,17},{2,10},{10... | collective-permute-start | bytes 2359304 | tf_op jit(solution)/shard_map/ppermute | solution.py:617
  86.0 24.6 %collective-permute-start.21 = (f32[8,4,24,256]{3,2,1,0:T(8,128)S(1)}, f32[8,4,24,256]{3,2,1,0:T(8,128)S(1)}, u32[]{:S(2)}, u32[]{:S(2)}) collective-permute-start(f32[8,4,24,256]{3,2,1,0:T(8,128)S(1)} %collective-permute-done.5.refs_14_.refs_6_), channel_id=1, source_target_pairs={{0,8},{8,0},{16,24},{24,16},{1,9},{9,1},{17,25},{25,17},{2,10},{10... | collective-permute-start | bytes 2359304 | tf_op jit(solution)/shard_map/ppermute | solution.py:617
  86.0 24.6 %collective-permute-start.24 = (f32[8,4,24,256]{3,2,1,0:T(8,128)S(1)}, f32[8,4,24,256]{3,2,1,0:T(8,128)S(1)}, u32[]{:S(2)}, u32[]{:S(2)}) collective-permute-start(f32[8,4,24,256]{3,2,1,0:T(8,128)S(1)} %collective-permute-done.23.refs_10_), channel_id=1, source_target_pairs={{0,8},{8,0},{16,24},{24,16},{1,9},{9,1},{17,25},{25,17},{2,10},{10... | collective-permute-start | bytes 2359304 | tf_op jit(solution)/shard_map/ppermute | solution.py:617
  104.4 6.2 %collective-permute-start.20 = (f32[8,4,24,256]{3,2,1,0:T(8,128)S(1)}, f32[8,4,24,256]{3,2,1,0:T(8,128)S(1)}, u32[]{:S(2)}, u32[]{:S(2)}) collective-permute-start(f32[8,4,24,256]{3,2,1,0:T(8,128)S(1)} %collective-permute-done.19.refs_2_), channel_id=1, source_target_pairs={{0,8},{8,0},{16,24},{24,16},{1,9},{9,1},{17,25},{25,17},{2,10},{10... | collective-permute-start | bytes 2359304 | tf_op jit(solution)/shard_map/ppermute | solution.py:617

commit v11 on v10

--- a/solution.py
+++ b/solution.py
@@ -562,22 +562,15 @@
     ]
     members = blocks * free[0].shape[2]
     high, low = split(weights[:, :members])
-    high, low = high.astype(f32), low.astype(f32)
-    both = jnp.concatenate(
-        [
-            jnp.concatenate([high, high], axis=1),
-            jnp.concatenate([low, jnp.zeros_like(low)], axis=1),
-        ],
-        axis=0,
-    ).astype(bf16)
+    both = jnp.concatenate([high.astype(f32), low.astype(f32)], axis=0).astype(bf16)
+    mul = functools.partial(jnp.dot, preferred_element_type=f32)
 
     def mixed(held, x, z):
         parts = [array[x, z] for array in held]
         values = parts[0] if blocks == 1 else jnp.concatenate(parts, axis=0)
-        out = jnp.dot(
-            both, jnp.concatenate(split(values), axis=0), preferred_element_type=f32
-        )
-        return out[:rows] + out[rows:]
+        value_high, value_low = split(values)
+        upper = mul(both, value_high)
+        return upper[:rows] + (upper[rows:] + mul(high, value_low))
 
     def plane(tracer, at):
         for z in range(nz):
@@ -707,7 +700,7 @@
         [whole, payload, payload, whole, inner, whole, inner, (3, *end)],
         4 * cells,
         scratch=[whole] * 7,
-        ready=(omega, eta, *conserved[1:]),
+        ready=(omega, eta),
     )
     tracer = collect(tracer)
     around = halos(first, last)
@@ -717,6 +710,7 @@
         [free, ends, *around, *coefficients],
         [end] * 3,
         cells // nx,
+        ready=conserved[1:],
     )
     tracer = complete(tracer, tracer_ends)
     tracer_ends = collect(tracer_ends)
@@ -736,7 +730,6 @@
     free = collect(free, half)
     half = total_over(half, "space", 2)
     other = swap(half, "member", 1)
-    internal = complete(internal, half)
     square = (members, LANES)
     total, extended = transform_call(
         early_kernel,
@@ -745,6 +738,7 @@
         [(batches, members, LANES)],
         [half, other],
     )
+    internal = complete(internal, total)
     free = complete(free, total)
     (weights,) = transform_call(
         functools.partial(late_kernel, offsets=offsets, blocks=blocks, rows=rows),

time: 117 us -> 119 us (1.017)
  Pallas kernels: 41.6 us -> 37.8 us
  starting transfers between devices: 34.5 us -> 37.7 us
  waiting for transfers between devices: 33.8 us -> 36.2 us
    ppermute x19, waiting for transfers between devices: 16.5 us -> 21.2 us  [swap(): return lax.ppermute(x, axis, [(k, k ^ bit) for k in range(count)])]
    ppermute x3, waiting for transfers between devices: 11.5 us -> 7.73 us  [halos(): lax.ppermute(first, 'space', backward)]
    pallas_call x2, Pallas kernels: 4.5 us -> 1.25 us  [gram(): pl.pallas_call(functools.partial(gram_kernel, offsets=offsets, planes=pla...]
    ppermute x19, starting transfers between devices: 16.7 us -> 19.9 us  [swap(): return lax.ppermute(x, axis, [(k, k ^ bit) for k in range(count)])]
    ppermute x3, waiting for transfers between devices: 5.74 us -> 7.22 us  [halos(): lax.ppermute(last, 'space', forward)]
  transfers between devices with their start and end apart: 25 -> 25, of which waited for: 12 -> 12; matrix products, arithmetic and copies ran while one was open for 4% -> 4% of each run, Pallas kernels for 27% -> 26%
where the time goes in v11:
time: 119 us; the launch traced here: 118 us
  Pallas kernels  37.8 us (32%)
  starting transfers between devices  37.7 us (32%)
  waiting for transfers between devices  36.2 us (30%)
  local copies, waits for them, and re-layouts  4.89 us (4%)
  other arithmetic  1.29 us (1%)
    pallas_call x2, Pallas kernels, transform_call(): pl.pallas_call(kernel, out_shape=[jax.ShapeDtypeStruct(shape, f32) for sh...  23.9 us
    ppermute x19, waiting for transfers between devices, swap(): return lax.ppermute(x, axis, [(k, k ^ bit) for k in range(count)])  21.2 us
    ppermute x19, starting transfers between devices, swap(): return lax.ppermute(x, axis, [(k, k ^ bit) for k in range(count)])  19.9 us
    ppermute x3, starting transfers between devices, halos(): lax.ppermute(last, 'space', forward)  13.8 us
    ppermute x3, waiting for transfers between devices, halos(): lax.ppermute(first, 'space', backward)  7.73 us
    ppermute x3, waiting for transfers between devices, halos(): lax.ppermute(last, 'space', forward)  7.22 us
    pallas_call x6, Pallas kernels, forecast_call(): pl.pallas_call(body, out_shape=[jax.ShapeDtypeStruct(shape, f32) for shap...  5.91 us
    pallas_call x1, Pallas kernels, mix(): pl.pallas_call(functools.partial(mix_kernel, blocks=blocks), grid=(nx,),...  5.25 us
  transfers between devices with their start and end apart: 25, of which 12 were waited for; matrix products, arithmetic and copies ran while one was open for 4% of the time, Pallas kernels for 26%

profile of v11, /device:TPU:0, one launch (start us, length us, event | category | flops | bytes accessed | tf_op | source)
XLA Modules:
  0.0 118.1 jit_solution(6556160152743800756)
XLA Ops:
  0.0 1.6 %fusion = (f32[24,3,2,4,256]{4,3,2,1,0:T(4,128)S(1)}, f32[24,3,2,4,256]{4,3,2,1,0:T(4,128)S(1)}) fusion(f32[24,4,8,4,256]{4,3,2,1,0:T(4,128)} %param.8), kind=kLoop, calls=%fused_computation.7 | loop fusion | bytes 2359296 | tf_op jit(solution)/shard_map/slice | solution.py:667
  1.6 0.4 copy_bitcast_fusion.4
  2.0 0.2 first_edges.1
  2.2 4.9 %collective-permute-start = (f32[4,56,256]{2,1,0:T(8,128)S(1)}, f32[4,56,256]{2,1,0:T(8,128)S(1)}, u32[]{:S(2)}, u32[]{:S(2)}) collective-permute-start(f32[4,56,256]{2,1,0:T(8,128)S(1)} %get-tuple-element.38), channel_id=1, source_target_pairs={{0,1},{1,2},{2,3},{3,4},{4,5},{5,6},{6,7},{8,9},{9,10},{10,11},{11... | collective-permute-start | bytes 688136 | tf_op jit(solution)/shard_map/ppermute | solution.py:632
  7.1 1.3 %collective-permute-start.1 = (f32[4,56,256]{2,1,0:T(8,128)S(1)}, f32[4,56,256]{2,1,0:T(8,128)S(1)}, u32[]{:S(2)}, u32[]{:S(2)}) collective-permute-start(f32[4,56,256]{2,1,0:T(8,128)S(1)} %get-tuple-element.39), channel_id=1, source_target_pairs={{1,0},{2,1},{3,2},{4,3},{5,4},{6,5},{7,6},{9,8},{10,9},{11,10},{12... | collective-permute-start | bytes 688136 | tf_op jit(solution)/shard_map/ppermute | solution.py:632
  8.4 1.0 fusion.1
  9.5 0.9 copy_bitcast_fusion
  10.4 0.9 copy_bitcast_fusion.2
  11.3 5.5 %collective-permute-done.refs_4_.refs_6_.refs_7_ = f32[4,56,256]{2,1,0:T(8,128)S(1)} collective-permute-done((f32[4,56,256]{2,1,0:T(8,128)S(1)}, f32[4,56,256]{2,1,0:T(8,128)S(1)}, u32[]{:S(2)}, u32[]{:S(2)}) %collective-permute-start) | collective-permute-done | bytes 229408 | tf_op jit(solution)/shard_map/ppermute | solution.py:632
  16.9 0.0 collective-permute-done.1.refs_5_.refs_7_.refs_8_
  16.9 0.0 copy-start.6
  16.9 1.0 next_edges.1
  17.9 4.4 %collective-permute-start.2 = (f32[4,48,256]{2,1,0:T(8,128)S(1)}, f32[4,48,256]{2,1,0:T(8,128)S(1)}, u32[]{:S(2)}, u32[]{:S(2)}) collective-permute-start(f32[4,48,256]{2,1,0:T(8,128)S(1)} %get-tuple-element.44), channel_id=1, source_target_pairs={{0,1},{1,2},{2,3},{3,4},{4,5},{5,6},{6,7},{8,9},{9,10},{10,11},{11... | collective-permute-start | bytes 589832 | tf_op jit(solution)/shard_map/ppermute | solution.py:632
  22.3 1.3 %collective-permute-start.3 = (f32[4,48,256]{2,1,0:T(8,128)S(1)}, f32[4,48,256]{2,1,0:T(8,128)S(1)}, u32[]{:S(2)}, u32[]{:S(2)}) collective-permute-start(f32[4,48,256]{2,1,0:T(8,128)S(1)} %get-tuple-element.45), channel_id=1, source_target_pairs={{1,0},{2,1},{3,2},{4,3},{5,4},{6,5},{7,6},{9,8},{10,9},{11,10},{12... | collective-permute-start | bytes 589832 | tf_op jit(solution)/shard_map/ppermute | solution.py:632
  23.6 1.3 %add_add_fusion.refs_4_ = f32[8,4,24,256]{3,2,1,0:T(8,128)S(1)} fusion(f32[24,1,8,4,256]{4,3,2,1,0:T(4,128)S(1)} %get-tuple-element.71, f32[24,1,8,4,256]{4,3,2,1,0:T(4,128)S(1)} %get-tuple-element.70, f32[24,1,8,4,256]{4,3,2,1,0:T(4,128)S(1)} %get-tuple-element.69), kind=kLoop, calls=%fused_computation.4 | loop fusion | flops 393216 | bytes 3145728 | tf_op jit(solution)/shard_map/add | solution.py:678
  24.8 0.1 collective-permute-start.8
  24.9 1.6 %collective-permute-start.9 = (f32[8,4,24,256]{3,2,1,0:T(8,128)S(1)}, f32[8,4,24,256]{3,2,1,0:T(8,128)S(1)}, u32[]{:S(2)}, u32[]{:S(2)}) collective-permute-start(f32[8,4,24,256]{3,2,1,0:T(8,128)S(1)} %add_add_fusion.refs_4_), channel_id=1, source_target_pairs={{0,16},{8,24},{16,0},{24,8},{1,17},{9,25},{17,1},{25,9},{2,18},{10... | collective-permute-start | bytes 2359304 | tf_op jit(solution)/shard_map/ppermute | solution.py:610
  26.5 1.4 %voxel_weights.1 = (f32[2,32,256]{2,1,0:T(8,128)S(1)}, f32[2,32,256]{2,1,0:T(8,128)S(1)}) custom-call(s32[4]{0:T(128)S(1)} %copy-done.6, s32[4,2048]{1,0:T(4,128)S(1)} %copy-done.3, f32[4,2048]{1,0:T(4,128)S(1)} %copy-done.4, f32[4,2048]{1,0:T(4,128)S(1)} %copy-done.5), custom_call_target="tpu_custom_call" | custom-call | tf_op jit(solution)/shard_map/voxel_weights/pallas_call | solution.py:374
  27.9 1.5 %two_substeps.1 = (f32[8,4,24,256]{3,2,1,0:T(8,128)S(1)}, f32[8,4,24,256]{3,2,1,0:T(8,128)S(1)}, f32[8,4,24,256]{3,2,1,0:T(8,128)S(1)}, f32[8,4,24,256]{3,2,1,0:T(8,128)S(1)}) custom-call(f32[8,4,24,256]{3,2,1,0:T(8,128)S(1)} %get-tuple-element.76.refs_0_, f32[8,4,24,256]{3,2,1,0:T(8,128)S(1)} %get-tuple-element.75.refs_1_, ...), custom_call_target="tpu_custom_call" | custom-call | flops 11796480 | bytes 12582912 | tf_op jit(solution)/shard_map/two_substeps/pallas_call | solution.py:323
  29.5 0.0 collective-permute-done.2.refs_4_
  29.5 1.9 %collective-permute-done.3.refs_5_ = f32[4,48,256]{2,1,0:T(8,128)S(1)} collective-permute-done((f32[4,48,256]{2,1,0:T(8,128)S(1)}, f32[4,48,256]{2,1,0:T(8,128)S(1)}, u32[]{:S(2)}, u32[]{:S(2)}) %collective-permute-start.3) | collective-permute-done | bytes 196640 | tf_op jit(solution)/shard_map/ppermute | solution.py:632
  31.4 2.6 %last_steps.1 = (f32[8,4,24,256]{3,2,1,0:T(8,128)S(1)}, f32[4,48,256]{2,1,0:T(8,128)S(1)}, f32[4,48,256]{2,1,0:T(8,128)S(1)}, f32[8,4,24,256]{3,2,1,0:T(8,128)S(...) custom-call(f32[8,4,24,256]{3,2,1,0:T(8,128)S(1)} %get-tuple-element, ...), custom_call_target="tpu_custom_call" | custom-call | flops 23592960 | bytes 25165824 | tf_op jit(solution)/shard_map/last_steps/pallas_call | solution.py:323
  34.0 1.6 %collective-permute-start.5 = (f32[6,4,24,256]{3,2,1,0:T(8,128)S(1)}, f32[6,4,24,256]{3,2,1,0:T(8,128)S(1)}, u32[]{:S(2)}, u32[]{:S(2)}) collective-permute-start(f32[6,4,24,256]{3,2,1,0:T(8,128)S(1)} %get-tuple-element.46.refs_0_.refs_12_), channel_id=1, source_target_pairs={{0,16},{8,24},{16,0},{24,8},{1,17},{9,25},{17,1},{25,9},{2,18},{10... | collective-permute-start | bytes 1769480 | tf_op jit(solution)/shard_map/ppermute | solution.py:610
  35.6 4.5 %collective-permute-start.6 = (f32[4,48,256]{2,1,0:T(8,128)S(1)}, f32[4,48,256]{2,1,0:T(8,128)S(1)}, u32[]{:S(2)}, u32[]{:S(2)}) collective-permute-start(f32[4,48,256]{2,1,0:T(8,128)S(1)} %get-tuple-element.49), channel_id=1, source_target_pairs={{0,1},{1,2},{2,3},{3,4},{4,5},{5,6},{6,7},{8,9},{9,10},{10,11},{11... | collective-permute-start | bytes 589832 | tf_op jit(solution)/shard_map/ppermute | solution.py:632
  40.1 1.5 %collective-permute-start.7 = (f32[4,48,256]{2,1,0:T(8,128)S(1)}, f32[4,48,256]{2,1,0:T(8,128)S(1)}, u32[]{:S(2)}, u32[]{:S(2)}) collective-permute-start(f32[4,48,256]{2,1,0:T(8,128)S(1)} %get-tuple-element.50), channel_id=1, source_target_pairs={{1,0},{2,1},{3,2},{4,3},{5,4},{6,5},{7,6},{9,8},{10,9},{11,10},{12... | collective-permute-start | bytes 589832 | tf_op jit(solution)/shard_map/ppermute | solution.py:632
  41.6 1.7 %collective-permute-done.6.refs_2_.refs_5_ = f32[4,48,256]{2,1,0:T(8,128)S(1)} collective-permute-done((f32[4,48,256]{2,1,0:T(8,128)S(1)}, f32[4,48,256]{2,1,0:T(8,128)S(1)}, u32[]{:S(2)}, u32[]{:S(2)}) %collective-permute-start.6) | collective-permute-done | bytes 196640 | tf_op jit(solution)/shard_map/ppermute | solution.py:632
  43.3 0.0 collective-permute-start.4
  43.3 5.8 %collective-permute-done.7.refs_3_.refs_6_ = f32[4,48,256]{2,1,0:T(8,128)S(1)} collective-permute-done((f32[4,48,256]{2,1,0:T(8,128)S(1)}, f32[4,48,256]{2,1,0:T(8,128)S(1)}, u32[]{:S(2)}, u32[]{:S(2)}) %collective-permute-start.7) | collective-permute-done | bytes 196640 | tf_op jit(solution)/shard_map/ppermute | solution.py:632
  49.1 0.0 collective-permute-done.8.refs_7_.refs_5_
  49.1 0.0 collective-permute-done.9.refs_8_.refs_6_
  49.1 0.1 last_ends.1
  49.3 8.3 %collective-permute-done.5.refs_2_.refs_14_ = f32[6,4,24,256]{3,2,1,0:T(8,128)S(1)} collective-permute-done((f32[6,4,24,256]{3,2,1,0:T(8,128)S(1)}, f32[6,4,24,256]{3,2,1,0:T(8,128)S(1)}, u32[]{:S(2)}, u32[]{:S(2)}) %collective-permute-start.5) | collective-permute-done | bytes 589856 | tf_op jit(solution)/shard_map/ppermute | solution.py:610
  57.5 0.0 collective-permute-start.10
  57.5 1.5 %collective-permute-start.12 = (f32[2,4,24,256]{3,2,1,0:T(8,128)S(1)}, f32[2,4,24,256]{3,2,1,0:T(8,128)S(1)}, u32[]{:S(2)}, u32[]{:S(2)}) collective-permute-start(f32[2,4,24,256]{3,2,1,0:T(8,128)S(1)} %get-tuple-element.52.refs_1_.refs_16_), channel_id=1, source_target_pairs={{0,16},{8,24},{16,0},{24,8},{1,17},{9,25},{17,1},{25,9},{2,18},{10... | collective-permute-start | bytes 589832 | tf_op jit(solution)/shard_map/ppermute | solution.py:610
  59.0 0.2 collective-permute-start.11
  59.3 0.2 collective-permute-done.10.refs_3_.refs_15_
  59.5 0.6 gram.2.refs_0_
  60.1 4.7 %collective-permute-done.12.refs_3_.refs_18_ = f32[2,4,24,256]{3,2,1,0:T(8,128)S(1)} collective-permute-done((f32[2,4,24,256]{3,2,1,0:T(8,128)S(1)}, f32[2,4,24,256]{3,2,1,0:T(8,128)S(1)}, u32[]{:S(2)}, u32[]{:S(2)}) %collective-permute-start.12) | collective-permute-done | bytes 196640 | tf_op jit(solution)/shard_map/ppermute | solution.py:610
  64.8 0.0 collective-permute-start.13
  64.8 1.4 %collective-permute-done.13.refs_4_.refs_19_ = f32[2,4,24,256]{3,2,1,0:T(8,128)S(1)} collective-permute-done((f32[2,4,24,256]{3,2,1,0:T(8,128)S(1)}, f32[2,4,24,256]{3,2,1,0:T(8,128)S(1)}, u32[]{:S(2)}, u32[]{:S(2)}) %collective-permute-start.13) | collective-permute-done | bytes 196640 | tf_op jit(solution)/shard_map/ppermute | solution.py:610
  66.3 0.7 gram.3
  67.0 3.1 %collective-permute-start.14 = (f32[96,128]{1,0:T(8,128)S(1)}, f32[96,128]{1,0:T(8,128)S(1)}, u32[]{:S(2)}, u32[]{:S(2)}) collective-permute-start(f32[96,128]{1,0:T(8,128)S(1)} %gram.3), channel_id=1, source_target_pairs={{0,1},{1,0},{2,3},{3,2},{4,5},{5,4},{6,7},{7,6},{8,9},{9,8},{10,11... | collective-permute-start | bytes 147464 | tf_op jit(solution)/shard_map/ppermute | solution.py:610
  70.1 0.5 last_free.1.refs_0_
  70.6 1.6 %collective-permute-start.23 = (f32[8,4,24,256]{3,2,1,0:T(8,128)S(1)}, f32[8,4,24,256]{3,2,1,0:T(8,128)S(1)}, u32[]{:S(2)}, u32[]{:S(2)}) collective-permute-start(f32[8,4,24,256]{3,2,1,0:T(8,128)S(1)} %get-tuple-element.65.refs_8_), channel_id=1, source_target_pairs={{0,16},{8,24},{16,0},{24,8},{1,17},{9,25},{17,1},{25,9},{2,18},{10... | collective-permute-start | bytes 2359304 | tf_op jit(solution)/shard_map/ppermute | solution.py:610
  72.2 0.0 collective-permute-done.14
  72.2 1.6 %collective-permute-start.19 = (f32[8,4,24,256]{3,2,1,0:T(8,128)S(1)}, f32[8,4,24,256]{3,2,1,0:T(8,128)S(1)}, u32[]{:S(2)}, u32[]{:S(2)}) collective-permute-start(f32[8,4,24,256]{3,2,1,0:T(8,128)S(1)} %last_free.1.refs_0_), channel_id=1, source_target_pairs={{0,16},{8,24},{16,0},{24,8},{1,17},{9,25},{17,1},{25,9},{2,18},{10... | collective-permute-start | bytes 2359304 | tf_op jit(solution)/shard_map/ppermute | solution.py:610
  73.7 4.0 %collective-permute-start.15 = (f32[96,128]{1,0:T(8,128)S(1)}, f32[96,128]{1,0:T(8,128)S(1)}, u32[]{:S(2)}, u32[]{:S(2)}) collective-permute-start(f32[96,128]{1,0:T(8,128)S(1)} %add.17), channel_id=1, source_target_pairs={{0,2},{1,3},{2,0},{3,1},{4,6},{5,7},{6,4},{7,5},{8,10},{9,11},{10,... | collective-permute-start | bytes 147464 | tf_op jit(solution)/shard_map/ppermute | solution.py:610
  77.7 2.1 %collective-permute-done.15 = f32[96,128]{1,0:T(8,128)S(1)} collective-permute-done((f32[96,128]{1,0:T(8,128)S(1)}, f32[96,128]{1,0:T(8,128)S(1)}, u32[]{:S(2)}, u32[]{:S(2)}) %collective-permute-start.15) | collective-permute-done | bytes 49184 | tf_op jit(solution)/shard_map/ppermute | solution.py:610
  79.8 3.4 %collective-permute-start.16 = (f32[96,128]{1,0:T(8,128)S(1)}, f32[96,128]{1,0:T(8,128)S(1)}, u32[]{:S(2)}, u32[]{:S(2)}) collective-permute-start(f32[96,128]{1,0:T(8,128)S(1)} %add.18), channel_id=1, source_target_pairs={{0,4},{1,5},{2,6},{3,7},{4,0},{5,1},{6,2},{7,3},{8,12},{9,13},{10,... | collective-permute-start | bytes 147464 | tf_op jit(solution)/shard_map/ppermute | solution.py:610
  83.2 2.1 %collective-permute-done.16 = f32[96,128]{1,0:T(8,128)S(1)} collective-permute-done((f32[96,128]{1,0:T(8,128)S(1)}, f32[96,128]{1,0:T(8,128)S(1)}, u32[]{:S(2)}, u32[]{:S(2)}) %collective-permute-start.16) | collective-permute-done | bytes 49184 | tf_op jit(solution)/shard_map/ppermute | solution.py:610
  85.3 0.1 collective-permute-start.17
  85.3 0.5 collective-permute-start.22
  85.8 0.1 collective-permute-start.18
  85.9 0.6 collective-permute-done.17.other
  86.6 0.2 collective-permute-start.21
  86.7 17.9 %transforms_early.1 = (f32[96,128]{1,0:T(8,128)S(1)}, f32[96,128]{1,0:T(8,128)S(1)}) custom-call(f32[96,128]{1,0:T(8,128)S(1)} %add.19.mine, f32[96,128]{1,0:T(8,128)S(1)} %collective-permute-done.17.other), custom_call_target="tpu_custom_call" | custom-call | flops 100000000 | bytes 1000000 | tf_op jit(solution)/shard_map/transforms_early/pallas_call | solution.py:542
  104.7 0.0 collective-permute-done.23.refs_10_
  104.7 0.4 collective-permute-start.24
  105.1 1.7 %collective-permute-done.19.refs_2_ = f32[8,4,24,256]{3,2,1,0:T(8,128)S(1)} collective-permute-done((f32[8,4,24,256]{3,2,1,0:T(8,128)S(1)}, f32[8,4,24,256]{3,2,1,0:T(8,128)S(1)}, u32[]{:S(2)}, u32[]{:S(2)}) %collective-permute-start.19) | collective-permute-done | bytes 786464 | tf_op jit(solution)/shard_map/ppermute | solution.py:610
  106.8 0.0 collective-permute-start.20
  106.8 6.0 %transforms_late.1.weights = f32[24,128]{1,0:T(8,128)S(1)} custom-call(f32[96,128]{1,0:T(8,128)S(1)} %get-tuple-element.55.total, f32[96,128]{1,0:T(8,128)S(1)} %get-tuple-element.56.last), custom_call_target="tpu_custom_call" | custom-call | flops 100000000 | bytes 1000000 | tf_op jit(solution)/shard_map/transforms_late/pallas_call | solution.py:542
  112.9 0.0 collective-permute-done.18.refs_1_
  112.9 0.0 collective-permute-done.24.refs_11_
  112.9 5.3 %mix.1 = f32[24,4,8,4,256]{4,3,2,1,0:T(4,128)} custom-call(f32[24,128]{1,0:T(8,128)S(1)} %transforms_late.1.weights, f32[8,4,24,256]{3,2,1,0:T(8,128)S(1)} %last_free.1.refs_0_, f32[8,4,24,256]{3,2,1,0:T(8,128)S(1)} %collective-permute-done.18.refs_1_, f32[8,4,24,256]{3,2,1,0:T(8,128)S(1)} %collective-permute-done.19.refs_2_, ...), custom_call_target="tpu_custom_call" | custom-call | tf_op jit(solution)/shard_map/mix/pallas_call | solution.py:597
  (23 shorter events, 0.1 us)
Async XLA Ops:
  0.0 8.4 %copy-start.7 = (f32[24,4,8,4,256]{4,3,2,1,0:T(4,128)S(1)}, f32[24,4,8,4,256]{4,3,2,1,0:T(4,128)}, u32[]{:S(2)}) copy-start(f32[24,4,8,4,256]{4,3,2,1,0:T(4,128)} %param.8) | copy-start | bytes 9437188
  0.0 2.0 %copy-start = (f32[8,4,256]{2,1,0:T(4,128)S(1)}, f32[8,4,256]{2,1,0:T(4,128)}, u32[]{:S(2)}) copy-start(f32[8,4,256]{2,1,0:T(4,128)} %refs_9_.7) | copy-start | bytes 98308
  0.0 2.0 %copy-start.2 = (f32[8,4,256]{2,1,0:T(4,128)S(1)}, f32[8,4,256]{2,1,0:T(4,128)}, u32[]{:S(2)}) copy-start(f32[8,4,256]{2,1,0:T(4,128)} %refs_6_.1) | copy-start | bytes 98308
  0.0 2.0 %copy-start.1 = (f32[8,4,256]{2,1,0:T(4,128)S(1)}, f32[8,4,256]{2,1,0:T(4,128)}, u32[]{:S(2)}) copy-start(f32[8,4,256]{2,1,0:T(4,128)} %refs_5_.1) | copy-start | bytes 98308
  2.2 14.6 %collective-permute-start = (f32[4,56,256]{2,1,0:T(8,128)S(1)}, f32[4,56,256]{2,1,0:T(8,128)S(1)}, u32[]{:S(2)}, u32[]{:S(2)}) collective-permute-start(f32[4,56,256]{2,1,0:T(8,128)S(1)} %get-tuple-element.38), channel_id=1, source_target_pairs={{0,1},{1,2},{2,3},{3,4},{4,5},{5,6},{6,7},{8,9},{9,10},{10,11},{11... | collective-permute-start | bytes 688136 | tf_op jit(solution)/shard_map/ppermute | solution.py:632
  7.1 9.7 %collective-permute-start.1 = (f32[4,56,256]{2,1,0:T(8,128)S(1)}, f32[4,56,256]{2,1,0:T(8,128)S(1)}, u32[]{:S(2)}, u32[]{:S(2)}) collective-permute-start(f32[4,56,256]{2,1,0:T(8,128)S(1)} %get-tuple-element.39), channel_id=1, source_target_pairs={{1,0},{2,1},{3,2},{4,3},{5,4},{6,5},{7,6},{9,8},{10,9},{11,10},{12... | collective-permute-start | bytes 688136 | tf_op jit(solution)/shard_map/ppermute | solution.py:632
  16.9 9.6 %copy-start.3 = (s32[4,2048]{1,0:T(4,128)S(1)}, s32[4,2048]{1,0:T(4,128)}, u32[]{:S(2)}) copy-start(s32[4,2048]{1,0:T(4,128)} %obs_index.1) | copy-start | bytes 98308
  16.9 9.6 %copy-start.4 = (f32[4,2048]{1,0:T(4,128)S(1)}, f32[4,2048]{1,0:T(4,128)}, u32[]{:S(2)}) copy-start(f32[4,2048]{1,0:T(4,128)} %observed.1) | copy-start | bytes 98308
  16.9 9.6 %copy-start.5 = (f32[4,2048]{1,0:T(4,128)S(1)}, f32[4,2048]{1,0:T(4,128)}, u32[]{:S(2)}) copy-start(f32[4,2048]{1,0:T(4,128)} %obs_var.1) | copy-start | bytes 98308
  16.9 9.6 %copy-start.6 = (s32[4]{0:T(128)S(1)}, s32[4]{0:T(128)}, u32[]{:S(2)}) copy-start(s32[4]{0:T(128)} %owner.5) | copy-start | bytes 52
  17.9 11.6 %collective-permute-start.2 = (f32[4,48,256]{2,1,0:T(8,128)S(1)}, f32[4,48,256]{2,1,0:T(8,128)S(1)}, u32[]{:S(2)}, u32[]{:S(2)}) collective-permute-start(f32[4,48,256]{2,1,0:T(8,128)S(1)} %get-tuple-element.44), channel_id=1, source_target_pairs={{0,1},{1,2},{2,3},{3,4},{4,5},{5,6},{6,7},{8,9},{9,10},{10,11},{11... | collective-permute-start | bytes 589832 | tf_op jit(solution)/shard_map/ppermute | solution.py:632
  22.3 9.1 %collective-permute-start.3 = (f32[4,48,256]{2,1,0:T(8,128)S(1)}, f32[4,48,256]{2,1,0:T(8,128)S(1)}, u32[]{:S(2)}, u32[]{:S(2)}) collective-permute-start(f32[4,48,256]{2,1,0:T(8,128)S(1)} %get-tuple-element.45), channel_id=1, source_target_pairs={{1,0},{2,1},{3,2},{4,3},{5,4},{6,5},{7,6},{9,8},{10,9},{11,10},{12... | collective-permute-start | bytes 589832 | tf_op jit(solution)/shard_map/ppermute | solution.py:632
  24.8 24.3 %collective-permute-start.8 = (f32[8,4,24,256]{3,2,1,0:T(8,128)S(1)}, f32[8,4,24,256]{3,2,1,0:T(8,128)S(1)}, u32[]{:S(2)}, u32[]{:S(2)}) collective-permute-start(f32[8,4,24,256]{3,2,1,0:T(8,128)S(1)} %add_add_fusion.refs_4_), channel_id=1, source_target_pairs={{0,8},{8,0},{16,24},{24,16},{1,9},{9,1},{17,25},{25,17},{2,10},{10... | collective-permute-start | bytes 2359304 | tf_op jit(solution)/shard_map/ppermute | solution.py:610
  24.9 24.2 %collective-permute-start.9 = (f32[8,4,24,256]{3,2,1,0:T(8,128)S(1)}, f32[8,4,24,256]{3,2,1,0:T(8,128)S(1)}, u32[]{:S(2)}, u32[]{:S(2)}) collective-permute-start(f32[8,4,24,256]{3,2,1,0:T(8,128)S(1)} %add_add_fusion.refs_4_), channel_id=1, source_target_pairs={{0,16},{8,24},{16,0},{24,8},{1,17},{9,25},{17,1},{25,9},{2,18},{10... | collective-permute-start | bytes 2359304 | tf_op jit(solution)/shard_map/ppermute | solution.py:610
  34.0 23.5 %collective-permute-start.5 = (f32[6,4,24,256]{3,2,1,0:T(8,128)S(1)}, f32[6,4,24,256]{3,2,1,0:T(8,128)S(1)}, u32[]{:S(2)}, u32[]{:S(2)}) collective-permute-start(f32[6,4,24,256]{3,2,1,0:T(8,128)S(1)} %get-tuple-element.46.refs_0_.refs_12_), channel_id=1, source_target_pairs={{0,16},{8,24},{16,0},{24,8},{1,17},{9,25},{17,1},{25,9},{2,18},{10... | collective-permute-start | bytes 1769480 | tf_op jit(solution)/shard_map/ppermute | solution.py:610
  35.6 7.7 %collective-permute-start.6 = (f32[4,48,256]{2,1,0:T(8,128)S(1)}, f32[4,48,256]{2,1,0:T(8,128)S(1)}, u32[]{:S(2)}, u32[]{:S(2)}) collective-permute-start(f32[4,48,256]{2,1,0:T(8,128)S(1)} %get-tuple-element.49), channel_id=1, source_target_pairs={{0,1},{1,2},{2,3},{3,4},{4,5},{5,6},{6,7},{8,9},{9,10},{10,11},{11... | collective-permute-start | bytes 589832 | tf_op jit(solution)/shard_map/ppermute | solution.py:632
  40.1 9.0 %collective-permute-start.7 = (f32[4,48,256]{2,1,0:T(8,128)S(1)}, f32[4,48,256]{2,1,0:T(8,128)S(1)}, u32[]{:S(2)}, u32[]{:S(2)}) collective-permute-start(f32[4,48,256]{2,1,0:T(8,128)S(1)} %get-tuple-element.50), channel_id=1, source_target_pairs={{1,0},{2,1},{3,2},{4,3},{5,4},{6,5},{7,6},{9,8},{10,9},{11,10},{12... | collective-permute-start | bytes 589832 | tf_op jit(solution)/shard_map/ppermute | solution.py:632
  43.3 16.0 %collective-permute-start.4 = (f32[6,4,24,256]{3,2,1,0:T(8,128)S(1)}, f32[6,4,24,256]{3,2,1,0:T(8,128)S(1)}, u32[]{:S(2)}, u32[]{:S(2)}) collective-permute-start(f32[6,4,24,256]{3,2,1,0:T(8,128)S(1)} %get-tuple-element.46.refs_0_.refs_12_), channel_id=1, source_target_pairs={{0,8},{8,0},{16,24},{24,16},{1,9},{9,1},{17,25},{25,17},{2,10},{10... | collective-permute-start | bytes 1769480 | tf_op jit(solution)/shard_map/ppermute | solution.py:610
  57.5 2.0 %collective-permute-start.10 = (f32[6,4,24,256]{3,2,1,0:T(8,128)S(1)}, f32[6,4,24,256]{3,2,1,0:T(8,128)S(1)}, u32[]{:S(2)}, u32[]{:S(2)}) collective-permute-start(f32[6,4,24,256]{3,2,1,0:T(8,128)S(1)} %collective-permute-done.5.refs_2_.refs_14_), channel_id=1, source_target_pairs={{0,8},{8,0},{16,24},{24,16},{1,9},{9,1},{17,25},{25,17},{2,10},{10... | collective-permute-start | bytes 1769480 | tf_op jit(solution)/shard_map/ppermute | solution.py:610
  57.5 7.3 %collective-permute-start.12 = (f32[2,4,24,256]{3,2,1,0:T(8,128)S(1)}, f32[2,4,24,256]{3,2,1,0:T(8,128)S(1)}, u32[]{:S(2)}, u32[]{:S(2)}) collective-permute-start(f32[2,4,24,256]{3,2,1,0:T(8,128)S(1)} %get-tuple-element.52.refs_1_.refs_16_), channel_id=1, source_target_pairs={{0,16},{8,24},{16,0},{24,8},{1,17},{9,25},{17,1},{25,9},{2,18},{10... | collective-permute-start | bytes 589832 | tf_op jit(solution)/shard_map/ppermute | solution.py:610
  59.0 5.8 %collective-permute-start.11 = (f32[2,4,24,256]{3,2,1,0:T(8,128)S(1)}, f32[2,4,24,256]{3,2,1,0:T(8,128)S(1)}, u32[]{:S(2)}, u32[]{:S(2)}) collective-permute-start(f32[2,4,24,256]{3,2,1,0:T(8,128)S(1)} %get-tuple-element.52.refs_1_.refs_16_), channel_id=1, source_target_pairs={{0,8},{8,0},{16,24},{24,16},{1,9},{9,1},{17,25},{25,17},{2,10},{10... | collective-permute-start | bytes 589832 | tf_op jit(solution)/shard_map/ppermute | solution.py:610
  64.8 1.4 %collective-permute-start.13 = (f32[2,4,24,256]{3,2,1,0:T(8,128)S(1)}, f32[2,4,24,256]{3,2,1,0:T(8,128)S(1)}, u32[]{:S(2)}, u32[]{:S(2)}) collective-permute-start(f32[2,4,24,256]{3,2,1,0:T(8,128)S(1)} %collective-permute-done.12.refs_3_.refs_18_), channel_id=1, source_target_pairs={{0,8},{8,0},{16,24},{24,16},{1,9},{9,1},{17,25},{25,17},{2,10},{10... | collective-permute-start | bytes 589832 | tf_op jit(solution)/shard_map/ppermute | solution.py:610
  67.0 5.2 %collective-permute-start.14 = (f32[96,128]{1,0:T(8,128)S(1)}, f32[96,128]{1,0:T(8,128)S(1)}, u32[]{:S(2)}, u32[]{:S(2)}) collective-permute-start(f32[96,128]{1,0:T(8,128)S(1)} %gram.3), channel_id=1, source_target_pairs={{0,1},{1,0},{2,3},{3,2},{4,5},{5,4},{6,7},{7,6},{8,9},{9,8},{10,11... | collective-permute-start | bytes 147464 | tf_op jit(solution)/shard_map/ppermute | solution.py:610
  70.6 34.1 %collective-permute-start.23 = (f32[8,4,24,256]{3,2,1,0:T(8,128)S(1)}, f32[8,4,24,256]{3,2,1,0:T(8,128)S(1)}, u32[]{:S(2)}, u32[]{:S(2)}) collective-permute-start(f32[8,4,24,256]{3,2,1,0:T(8,128)S(1)} %get-tuple-element.65.refs_8_), channel_id=1, source_target_pairs={{0,16},{8,24},{16,0},{24,8},{1,17},{9,25},{17,1},{25,9},{2,18},{10... | collective-permute-start | bytes 2359304 | tf_op jit(solution)/shard_map/ppermute | solution.py:610
  72.2 34.6 %collective-permute-start.19 = (f32[8,4,24,256]{3,2,1,0:T(8,128)S(1)}, f32[8,4,24,256]{3,2,1,0:T(8,128)S(1)}, u32[]{:S(2)}, u32[]{:S(2)}) collective-permute-start(f32[8,4,24,256]{3,2,1,0:T(8,128)S(1)} %last_free.1.refs_0_), channel_id=1, source_target_pairs={{0,16},{8,24},{16,0},{24,8},{1,17},{9,25},{17,1},{25,9},{2,18},{10... | collective-permute-start | bytes 2359304 | tf_op jit(solution)/shard_map/ppermute | solution.py:610
  73.7 6.1 %collective-permute-start.15 = (f32[96,128]{1,0:T(8,128)S(1)}, f32[96,128]{1,0:T(8,128)S(1)}, u32[]{:S(2)}, u32[]{:S(2)}) collective-permute-start(f32[96,128]{1,0:T(8,128)S(1)} %add.17), channel_id=1, source_target_pairs={{0,2},{1,3},{2,0},{3,1},{4,6},{5,7},{6,4},{7,5},{8,10},{9,11},{10,... | collective-permute-start | bytes 147464 | tf_op jit(solution)/shard_map/ppermute | solution.py:610
  79.8 5.5 %collective-permute-start.16 = (f32[96,128]{1,0:T(8,128)S(1)}, f32[96,128]{1,0:T(8,128)S(1)}, u32[]{:S(2)}, u32[]{:S(2)}) collective-permute-start(f32[96,128]{1,0:T(8,128)S(1)} %add.18), channel_id=1, source_target_pairs={{0,4},{1,5},{2,6},{3,7},{4,0},{5,1},{6,2},{7,3},{8,12},{9,13},{10,... | collective-permute-start | bytes 147464 | tf_op jit(solution)/shard_map/ppermute | solution.py:610
  85.3 1.3 %collective-permute-start.17 = (f32[96,128]{1,0:T(8,128)S(1)}, f32[96,128]{1,0:T(8,128)S(1)}, u32[]{:S(2)}, u32[]{:S(2)}) collective-permute-start(f32[96,128]{1,0:T(8,128)S(1)} %add.19.mine), channel_id=1, source_target_pairs={{0,8},{8,0},{16,24},{24,16},{1,9},{9,1},{17,25},{25,17},{2,10},{10... | collective-permute-start | bytes 147464 | tf_op jit(solution)/shard_map/ppermute | solution.py:610
  85.3 27.5 %collective-permute-start.22 = (f32[8,4,24,256]{3,2,1,0:T(8,128)S(1)}, f32[8,4,24,256]{3,2,1,0:T(8,128)S(1)}, u32[]{:S(2)}, u32[]{:S(2)}) collective-permute-start(f32[8,4,24,256]{3,2,1,0:T(8,128)S(1)} %get-tuple-element.65.refs_8_), channel_id=1, source_target_pairs={{0,8},{8,0},{16,24},{24,16},{1,9},{9,1},{17,25},{25,17},{2,10},{10... | collective-permute-start | bytes 2359304 | tf_op jit(solution)/shard_map/ppermute | solution.py:610
  85.8 27.0 %collective-permute-start.18 = (f32[8,4,24,256]{3,2,1,0:T(8,128)S(1)}, f32[8,4,24,256]{3,2,1,0:T(8,128)S(1)}, u32[]{:S(2)}, u32[]{:S(2)}) collective-permute-start(f32[8,4,24,256]{3,2,1,0:T(8,128)S(1)} %last_free.1.refs_0_), channel_id=1, source_target_pairs={{0,8},{8,0},{16,24},{24,16},{1,9},{9,1},{17,25},{25,17},{2,10},{10... | collective-permute-start | bytes 2359304 | tf_op jit(solution)/shard_map/ppermute | solution.py:610
  86.6 26.3 %collective-permute-start.21 = (f32[8,4,24,256]{3,2,1,0:T(8,128)S(1)}, f32[8,4,24,256]{3,2,1,0:T(8,128)S(1)}, u32[]{:S(2)}, u32[]{:S(2)}) collective-permute-start(f32[8,4,24,256]{3,2,1,0:T(8,128)S(1)} %collective-permute-done.9.refs_8_.refs_6_), channel_id=1, source_target_pairs={{0,8},{8,0},{16,24},{24,16},{1,9},{9,1},{17,25},{25,17},{2,10},{10... | collective-permute-start | bytes 2359304 | tf_op jit(solution)/shard_map/ppermute | solution.py:610
  104.7 8.2 %collective-permute-start.24 = (f32[8,4,24,256]{3,2,1,0:T(8,128)S(1)}, f32[8,4,24,256]{3,2,1,0:T(8,128)S(1)}, u32[]{:S(2)}, u32[]{:S(2)}) collective-permute-start(f32[8,4,24,256]{3,2,1,0:T(8,128)S(1)} %collective-permute-done.23.refs_10_), channel_id=1, source_target_pairs={{0,8},{8,0},{16,24},{24,16},{1,9},{9,1},{17,25},{25,17},{2,10},{10... | collective-permute-start | bytes 2359304 | tf_op jit(solution)/shard_map/ppermute | solution.py:610
  106.8 6.1 %collective-permute-start.20 = (f32[8,4,24,256]{3,2,1,0:T(8,128)S(1)}, f32[8,4,24,256]{3,2,1,0:T(8,128)S(1)}, u32[]{:S(2)}, u32[]{:S(2)}) collective-permute-start(f32[8,4,24,256]{3,2,1,0:T(8,128)S(1)} %collective-permute-done.19.refs_2_), channel_id=1, source_target_pairs={{0,8},{8,0},{16,24},{24,16},{1,9},{9,1},{17,25},{25,17},{2,10},{10... | collective-permute-start | bytes 2359304 | tf_op jit(solution)/shard_map/ppermute | solution.py:610

commit v12 on v11

--- a/solution.py
+++ b/solution.py
@@ -224,11 +224,16 @@
     )
 
 
+def nz_part(a):
+    return a.shape[1] // 2
+
+
 def last_steps_kernel(
     a, r, c, i, low, high, low_first, high_first, diffusivity, binding, source, *refs
 ):
     *outs, m0, m1, m2, m3, later_r, later_c, later_i = refs
-    before, first, last, free, tracer, inside, add, ends = outs
+    before, first, last, free, tracer, inside_low, inside_high, add, ends = outs
+    part = nz_part(a)
     nx, nz, members, _ = a.shape
     coefficients = (diffusivity, binding, source)
     two_substeps_kernel(
@@ -268,7 +273,7 @@
             back, _, complexed, internal = react(
                 free[x, z], m1[x, z], m2[x, z], m3[x, z], binding[x, row, :]
             )
-            inside[x, z] = internal
+            (inside_low if z < part else inside_high)[x, z % part] = internal
             if 0 < x < nx - 1:
                 tracer[x - 1, z] = complexed + internal
                 add[x - 1, z] = back + source[x, row, :]
@@ -557,9 +562,10 @@
     *sources, out = refs
     rows, _, _, nz, _ = out.shape
     x, nx = pl.program_id(0), pl.num_programs(0)
-    free, conserved, internal, tracer, tracer_ends = [
+    free, conserved, inside_low, inside_high, tracer, tracer_ends = [
         sources[k : k + blocks] for k in range(0, len(sources), blocks)
     ]
+    part = nz_part(free[0])
     members = blocks * free[0].shape[2]
     high, low = split(weights[:, :members])
     both = jnp.concatenate([high.astype(f32), low.astype(f32)], axis=0).astype(bf16)
@@ -575,7 +581,7 @@
     def plane(tracer, at):
         for z in range(nz):
             bound = mixed(tracer, at, z)
-            inside = mixed(internal, x, z)
+            inside = mixed(inside_low if z < part else inside_high, x, z % part)
             out[:, 0, 0, z, :] = mixed(free, x, z)
             out[:, 1, 0, z, :] = mixed(conserved, x, z) - bound
             out[:, 2, 0, z, :] = bound - inside
@@ -680,7 +686,7 @@
         owner, obs_index, observed, obs_var, batches // 2, nx * nz, ny
     )
     around = origin = halos(*edges)
-    conserved = collect(conserved, *around, *fields)
+    conserved = collect(conserved)
     payload = (nz, 2 * rows, ny)
     for step in range(SUBSTEPS // 2 - 2):
         inputs = [*fields, *around, *origin, *coefficients]
@@ -692,15 +698,15 @@
         fields = forecast_call(
             two_substeps_kernel, "two_substeps", inputs, [whole] * 4, 2 * cells, scratch=[whole] * 4
         )
-    inner, end = (nx - 2, nz, rows, ny), (2, nz, rows, ny)
-    before, first, last, free, tracer, internal, add, ends = forecast_call(
+    inner, end, part = (nx - 2, nz, rows, ny), (2, nz, rows, ny), (nx, nz // 2, rows, ny)
+    before, first, last, free, tracer, inside_low, inside_high, add, ends = forecast_call(
         last_steps_kernel,
         "last_steps",
         [*fields, *around, *origin, *coefficients],
-        [whole, payload, payload, whole, inner, whole, inner, (3, *end)],
+        [whole, payload, payload, whole, inner, part, part, inner, (3, *end)],
         4 * cells,
         scratch=[whole] * 7,
-        ready=(omega, eta),
+        ready=(omega, eta, *conserved[1:]),
     )
     tracer = collect(tracer)
     around = halos(first, last)
@@ -710,7 +716,6 @@
         [free, ends, *around, *coefficients],
         [end] * 3,
         cells // nx,
-        ready=conserved[1:],
     )
     tracer = complete(tracer, tracer_ends)
     tracer_ends = collect(tracer_ends)
@@ -724,11 +729,14 @@
         [whole],
         cells,
     )
-    internal = collect(internal, across(tracer_ends))
+    inside_low = collect(inside_low, across(tracer_ends), begun)
     half = gram(owner, omega, eta, begun, tracer_ends, offsets, (0, nx - 1))
     half = half + swap(half, "space", 1)
+    half = half + swap(half, "space", 2)
+    half = tie(half, across(inside_low))
+    inside_high = collect(inside_high, half)
     free = collect(free, half)
-    half = total_over(half, "space", 2)
+    half = total_over(half, "space", 4)
     other = swap(half, "member", 1)
     square = (members, LANES)
     total, extended = transform_call(
@@ -738,7 +746,8 @@
         [(batches, members, LANES)],
         [half, other],
     )
-    internal = complete(internal, total)
+    inside_low = complete(inside_low, total)
+    inside_high = complete(inside_high, total)
     free = complete(free, total)
     (weights,) = transform_call(
         functools.partial(late_kernel, offsets=offsets, blocks=blocks, rows=rows),
@@ -749,7 +758,7 @@
     )
     if blocks == 1:
         weights = lax.dynamic_slice(weights, (member * rows, 0), (rows, LANES))
-    held = free + conserved + internal + tracer + tracer_ends
+    held = free + conserved + inside_low + inside_high + tracer + tracer_ends
     return mix(weights, held, blocks, ensemble.shape)
 
 

time: 119 us -> 110 us (0.924)
  waiting for transfers between devices: 36.2 us -> 26.3 us
  Pallas kernels: 37.8 us -> 41.2 us
  starting transfers between devices: 37.7 us -> 35.6 us
    ppermute x19 -> x22, waiting for transfers between devices: 21.2 us -> 11.3 us  [swap(): return lax.ppermute(x, axis, [(k, k ^ bit) for k in range(count)])]
    pallas_call x2, Pallas kernels: 1.25 us -> 4.68 us  [gram(): pl.pallas_call(functools.partial(gram_kernel, offsets=offsets, planes=pla...]
    ppermute x3, waiting for transfers between devices: 7.73 us -> 10.7 us  [halos(): lax.ppermute(first, 'space', backward)]
    ppermute x3, waiting for transfers between devices: 7.22 us -> 4.34 us  [halos(): lax.ppermute(last, 'space', forward)]
    ppermute x19 -> x22, starting transfers between devices: 19.9 us -> 17.9 us  [swap(): return lax.ppermute(x, axis, [(k, k ^ bit) for k in range(count)])]
  transfers between devices with their start and end apart: 25 -> 28, of which waited for: 12 -> 12; matrix products, arithmetic and copies ran while one was open for 4% -> 4% of each run, Pallas kernels for 26% -> 30%
where the time goes in v12:
time: 110 us
  Pallas kernels  41.2 us (37%)
  starting transfers between devices  35.6 us (32%)
  waiting for transfers between devices  26.3 us (24%)
  local copies, waits for them, and re-layouts  4.89 us (4%)
  other arithmetic  1.29 us (1%)
    pallas_call x2, Pallas kernels, transform_call(): pl.pallas_call(kernel, out_shape=[jax.ShapeDtypeStruct(shape, f32) for sh...  23.9 us
    ppermute x22, starting transfers between devices, swap(): return lax.ppermute(x, axis, [(k, k ^ bit) for k in range(count)])  17.9 us
    ppermute x3, starting transfers between devices, halos(): lax.ppermute(last, 'space', forward)  13.8 us
    ppermute x22, waiting for transfers between devices, swap(): return lax.ppermute(x, axis, [(k, k ^ bit) for k in range(count)])  11.3 us
    ppermute x3, waiting for transfers between devices, halos(): lax.ppermute(first, 'space', backward)  10.7 us
    pallas_call x6, Pallas kernels, forecast_call(): pl.pallas_call(body, out_shape=[jax.ShapeDtypeStruct(shape, f32) for shap...  5.91 us
    pallas_call x1, Pallas kernels, mix(): pl.pallas_call(functools.partial(mix_kernel, blocks=blocks), grid=(nx,),...  5.27 us
    pallas_call x2, Pallas kernels, gram(): pl.pallas_call(functools.partial(gram_kernel, offsets=offsets, planes=pla...  4.68 us
  transfers between devices with their start and end apart: 28, of which 12 were waited for; matrix products, arithmetic and copies ran while one was open for 4% of the time, Pallas kernels for 30%

profile of v12, /device:TPU:0, one launch (start us, length us, event | category | flops | bytes accessed | tf_op | source)
XLA Modules:
  0.0 109.7 jit_solution(15571649890837718651)
XLA Ops:
  0.0 1.6 %fusion = (f32[24,3,2,4,256]{4,3,2,1,0:T(4,128)S(1)}, f32[24,3,2,4,256]{4,3,2,1,0:T(4,128)S(1)}) fusion(f32[24,4,8,4,256]{4,3,2,1,0:T(4,128)} %param.8), kind=kLoop, calls=%fused_computation.7 | loop fusion | bytes 2359296 | tf_op jit(solution)/shard_map/slice | solution.py:673
  1.6 0.4 copy_bitcast_fusion.4
  2.0 0.2 first_edges.1
  2.2 4.9 %collective-permute-start = (f32[4,56,256]{2,1,0:T(8,128)S(1)}, f32[4,56,256]{2,1,0:T(8,128)S(1)}, u32[]{:S(2)}, u32[]{:S(2)}) collective-permute-start(f32[4,56,256]{2,1,0:T(8,128)S(1)} %get-tuple-element.41), channel_id=1, source_target_pairs={{0,1},{1,2},{2,3},{3,4},{4,5},{5,6},{6,7},{8,9},{9,10},{10,11},{11... | collective-permute-start | bytes 688136 | tf_op jit(solution)/shard_map/ppermute | solution.py:638
  7.1 1.3 %collective-permute-start.1 = (f32[4,56,256]{2,1,0:T(8,128)S(1)}, f32[4,56,256]{2,1,0:T(8,128)S(1)}, u32[]{:S(2)}, u32[]{:S(2)}) collective-permute-start(f32[4,56,256]{2,1,0:T(8,128)S(1)} %get-tuple-element.42), channel_id=1, source_target_pairs={{1,0},{2,1},{3,2},{4,3},{5,4},{6,5},{7,6},{9,8},{10,9},{11,10},{12... | collective-permute-start | bytes 688136 | tf_op jit(solution)/shard_map/ppermute | solution.py:638
  8.4 1.0 fusion.1
  9.5 1.3 %add_add_fusion.refs_4_ = f32[8,4,24,256]{3,2,1,0:T(8,128)S(1)} fusion(f32[24,1,8,4,256]{4,3,2,1,0:T(4,128)S(1)} %get-tuple-element.77, f32[24,1,8,4,256]{4,3,2,1,0:T(4,128)S(1)} %get-tuple-element.76, f32[24,1,8,4,256]{4,3,2,1,0:T(4,128)S(1)} %get-tuple-element.75), kind=kLoop, calls=%fused_computation.4 | loop fusion | flops 393216 | bytes 3145728 | tf_op jit(solution)/shard_map/add | solution.py:684
  10.7 0.1 collective-permute-start.4
  10.8 1.6 %collective-permute-start.5 = (f32[8,4,24,256]{3,2,1,0:T(8,128)S(1)}, f32[8,4,24,256]{3,2,1,0:T(8,128)S(1)}, u32[]{:S(2)}, u32[]{:S(2)}) collective-permute-start(f32[8,4,24,256]{3,2,1,0:T(8,128)S(1)} %add_add_fusion.refs_4_), channel_id=1, source_target_pairs={{0,16},{8,24},{16,0},{24,8},{1,17},{9,25},{17,1},{25,9},{2,18},{10... | collective-permute-start | bytes 2359304 | tf_op jit(solution)/shard_map/ppermute | solution.py:616
  12.4 0.9 copy_bitcast_fusion
  13.3 0.0 copy-start.3
  13.3 0.0 copy-start.4
  13.4 0.0 copy-start.5
  13.4 0.0 copy-start.6
  13.4 0.9 copy_bitcast_fusion.2
  14.3 2.6 %collective-permute-done.refs_4_.refs_6_.refs_7_ = f32[4,56,256]{2,1,0:T(8,128)S(1)} collective-permute-done((f32[4,56,256]{2,1,0:T(8,128)S(1)}, f32[4,56,256]{2,1,0:T(8,128)S(1)}, u32[]{:S(2)}, u32[]{:S(2)}) %collective-permute-start) | collective-permute-done | bytes 229408 | tf_op jit(solution)/shard_map/ppermute | solution.py:638
  16.9 1.0 next_edges.1
  17.8 4.4 %collective-permute-start.2 = (f32[4,48,256]{2,1,0:T(8,128)S(1)}, f32[4,48,256]{2,1,0:T(8,128)S(1)}, u32[]{:S(2)}, u32[]{:S(2)}) collective-permute-start(f32[4,48,256]{2,1,0:T(8,128)S(1)} %get-tuple-element.47), channel_id=1, source_target_pairs={{0,1},{1,2},{2,3},{3,4},{4,5},{5,6},{6,7},{8,9},{9,10},{10,11},{11... | collective-permute-start | bytes 589832 | tf_op jit(solution)/shard_map/ppermute | solution.py:638
  22.2 1.3 %collective-permute-start.3 = (f32[4,48,256]{2,1,0:T(8,128)S(1)}, f32[4,48,256]{2,1,0:T(8,128)S(1)}, u32[]{:S(2)}, u32[]{:S(2)}) collective-permute-start(f32[4,48,256]{2,1,0:T(8,128)S(1)} %get-tuple-element.48), channel_id=1, source_target_pairs={{1,0},{2,1},{3,2},{4,3},{5,4},{6,5},{7,6},{9,8},{10,9},{11,10},{12... | collective-permute-start | bytes 589832 | tf_op jit(solution)/shard_map/ppermute | solution.py:638
  23.6 1.4 %voxel_weights.1 = (f32[2,32,256]{2,1,0:T(8,128)S(1)}, f32[2,32,256]{2,1,0:T(8,128)S(1)}) custom-call(s32[4]{0:T(128)S(1)} %copy-done.6, s32[4,2048]{1,0:T(4,128)S(1)} %copy-done.3, f32[4,2048]{1,0:T(4,128)S(1)} %copy-done.4, f32[4,2048]{1,0:T(4,128)S(1)} %copy-done.5), custom_call_target="tpu_custom_call" | custom-call | tf_op jit(solution)/shard_map/voxel_weights/pallas_call | solution.py:379
  25.0 1.5 %two_substeps.1 = (f32[8,4,24,256]{3,2,1,0:T(8,128)S(1)}, f32[8,4,24,256]{3,2,1,0:T(8,128)S(1)}, f32[8,4,24,256]{3,2,1,0:T(8,128)S(1)}, f32[8,4,24,256]{3,2,1,0:T(8,128)S(1)}) custom-call(f32[8,4,24,256]{3,2,1,0:T(8,128)S(1)} %get-tuple-element.82.refs_0_, f32[8,4,24,256]{3,2,1,0:T(8,128)S(1)} %get-tuple-element.81.refs_1_, ...), custom_call_target="tpu_custom_call" | custom-call | flops 11796480 | bytes 12582912 | tf_op jit(solution)/shard_map/two_substeps/pallas_call | solution.py:328
  26.6 4.8 %collective-permute-done.3.refs_5_ = f32[4,48,256]{2,1,0:T(8,128)S(1)} collective-permute-done((f32[4,48,256]{2,1,0:T(8,128)S(1)}, f32[4,48,256]{2,1,0:T(8,128)S(1)}, u32[]{:S(2)}, u32[]{:S(2)}) %collective-permute-start.3) | collective-permute-done | bytes 196640 | tf_op jit(solution)/shard_map/ppermute | solution.py:638
  31.4 0.0 collective-permute-done.4.refs_13_.refs_5_
  31.4 2.6 %last_steps.1 = (f32[8,4,24,256]{3,2,1,0:T(8,128)S(1)}, f32[4,48,256]{2,1,0:T(8,128)S(1)}, f32[4,48,256]{2,1,0:T(8,128)S(1)}, f32[8,4,24,256]{3,2,1,0:T(8,128)S(...) custom-call(f32[8,4,24,256]{3,2,1,0:T(8,128)S(1)} %get-tuple-element, ...), custom_call_target="tpu_custom_call" | custom-call | flops 23592960 | bytes 25165824 | tf_op jit(solution)/shard_map/last_steps/pallas_call | solution.py:328
  34.0 1.6 %collective-permute-start.7 = (f32[6,4,24,256]{3,2,1,0:T(8,128)S(1)}, f32[6,4,24,256]{3,2,1,0:T(8,128)S(1)}, u32[]{:S(2)}, u32[]{:S(2)}) collective-permute-start(f32[6,4,24,256]{3,2,1,0:T(8,128)S(1)} %get-tuple-element.49.refs_0_.refs_16_), channel_id=1, source_target_pairs={{0,16},{8,24},{16,0},{24,8},{1,17},{9,25},{17,1},{25,9},{2,18},{10... | collective-permute-start | bytes 1769480 | tf_op jit(solution)/shard_map/ppermute | solution.py:616
  35.6 4.5 %collective-permute-start.8 = (f32[4,48,256]{2,1,0:T(8,128)S(1)}, f32[4,48,256]{2,1,0:T(8,128)S(1)}, u32[]{:S(2)}, u32[]{:S(2)}) collective-permute-start(f32[4,48,256]{2,1,0:T(8,128)S(1)} %get-tuple-element.52), channel_id=1, source_target_pairs={{0,1},{1,2},{2,3},{3,4},{4,5},{5,6},{6,7},{8,9},{9,10},{10,11},{11... | collective-permute-start | bytes 589832 | tf_op jit(solution)/shard_map/ppermute | solution.py:638
  40.1 1.3 %collective-permute-start.9 = (f32[4,48,256]{2,1,0:T(8,128)S(1)}, f32[4,48,256]{2,1,0:T(8,128)S(1)}, u32[]{:S(2)}, u32[]{:S(2)}) collective-permute-start(f32[4,48,256]{2,1,0:T(8,128)S(1)} %get-tuple-element.53), channel_id=1, source_target_pairs={{1,0},{2,1},{3,2},{4,3},{5,4},{6,5},{7,6},{9,8},{10,9},{11,10},{12... | collective-permute-start | bytes 589832 | tf_op jit(solution)/shard_map/ppermute | solution.py:638
  41.4 0.1 collective-permute-start.6
  41.5 1.8 %collective-permute-done.8.refs_2_.refs_5_ = f32[4,48,256]{2,1,0:T(8,128)S(1)} collective-permute-done((f32[4,48,256]{2,1,0:T(8,128)S(1)}, f32[4,48,256]{2,1,0:T(8,128)S(1)}, u32[]{:S(2)}, u32[]{:S(2)}) %collective-permute-start.8) | collective-permute-done | bytes 196640 | tf_op jit(solution)/shard_map/ppermute | solution.py:638
  43.3 5.8 %collective-permute-done.9.refs_3_.refs_6_ = f32[4,48,256]{2,1,0:T(8,128)S(1)} collective-permute-done((f32[4,48,256]{2,1,0:T(8,128)S(1)}, f32[4,48,256]{2,1,0:T(8,128)S(1)}, u32[]{:S(2)}, u32[]{:S(2)}) %collective-permute-start.9) | collective-permute-done | bytes 196640 | tf_op jit(solution)/shard_map/ppermute | solution.py:638
  49.1 0.1 last_ends.1
  49.2 0.0 collective-permute-done.7.refs_2_.refs_18_
  49.2 0.1 collective-permute-start.10
  49.3 0.7 collective-permute-start.12
  50.0 1.3 %collective-permute-done.10.refs_3_.refs_19_ = f32[6,4,24,256]{3,2,1,0:T(8,128)S(1)} collective-permute-done((f32[6,4,24,256]{3,2,1,0:T(8,128)S(1)}, f32[6,4,24,256]{3,2,1,0:T(8,128)S(1)}, u32[]{:S(2)}, u32[]{:S(2)}) %collective-permute-start.10) | collective-permute-done | bytes 589856 | tf_op jit(solution)/shard_map/ppermute | solution.py:616
  51.3 3.2 %gram.2.refs_0_ = f32[2,96,128]{2,1,0:T(8,128)S(1)} custom-call(s32[4]{0:T(128)S(1)} %copy-done.6, f32[2,32,256]{2,1,0:T(8,128)S(1)} %get-tuple-element.39.refs_11_.omega, f32[2,32,256]{2,1,0:T(8,128)S(1)} %get-tuple-element.40.refs_12_.eta, f32[6,4,24,256]{3,2,1,0:T(8,128)S(1)} %get-tuple-element.49.refs_0_.refs_16_, ...), custom_call_target="tpu_custom_call" | custom-call | tf_op jit(solution)/shard_map/gram/pallas_call | solution.py:443
  54.5 2.1 %collective-permute-done.12.refs_3_.refs_22_ = f32[2,4,24,256]{3,2,1,0:T(8,128)S(1)} collective-permute-done((f32[2,4,24,256]{3,2,1,0:T(8,128)S(1)}, f32[2,4,24,256]{3,2,1,0:T(8,128)S(1)}, u32[]{:S(2)}, u32[]{:S(2)}) %collective-permute-start.12) | collective-permute-done | bytes 196640 | tf_op jit(solution)/shard_map/ppermute | solution.py:616
  56.6 0.7 collective-permute-start.16
  57.3 0.5 collective-permute-start.13
  57.8 0.9 collective-permute-done.11.refs_2_.refs_21_
  58.8 0.3 collective-permute-done.13.refs_4_.refs_23_
  59.0 1.5 %gram.3 = f32[96,128]{1,0:T(8,128)S(1)} custom-call(s32[4]{0:T(128)S(1)} %copy-done.6, f32[2,32,256]{2,1,0:T(8,128)S(1)} %get-tuple-element.39.refs_11_.omega, f32[2,32,256]{2,1,0:T(8,128)S(1)} %get-tuple-element.40.refs_12_.eta, f32[2,96,128]{2,1,0:T(8,128)S(1)} %gram.2.refs_0_, f32[2,4,24,256]{3,2,1,0:T(8,128)S(1)} %get-tuple-element.54.refs_1_.refs_20_, ...), custom_call_target="tpu_custom_call" | custom-call | tf_op jit(solution)/shard_map/gram/pallas_call | solution.py:443
  60.5 1.8 %collective-permute-start.14 = (f32[96,128]{1,0:T(8,128)S(1)}, f32[96,128]{1,0:T(8,128)S(1)}, u32[]{:S(2)}, u32[]{:S(2)}) collective-permute-start(f32[96,128]{1,0:T(8,128)S(1)} %gram.3), channel_id=1, source_target_pairs={{0,1},{1,0},{2,3},{3,2},{4,5},{5,4},{6,7},{7,6},{8,9},{9,8},{10,11... | collective-permute-start | bytes 147464 | tf_op jit(solution)/shard_map/ppermute | solution.py:616
  62.3 2.4 %collective-permute-done.14 = f32[96,128]{1,0:T(8,128)S(1)} collective-permute-done((f32[96,128]{1,0:T(8,128)S(1)}, f32[96,128]{1,0:T(8,128)S(1)}, u32[]{:S(2)}, u32[]{:S(2)}) %collective-permute-start.14) | collective-permute-done | bytes 49184 | tf_op jit(solution)/shard_map/ppermute | solution.py:616
  64.7 3.8 %collective-permute-start.15 = (f32[96,128]{1,0:T(8,128)S(1)}, f32[96,128]{1,0:T(8,128)S(1)}, u32[]{:S(2)}, u32[]{:S(2)}) collective-permute-start(f32[96,128]{1,0:T(8,128)S(1)} %add.17), channel_id=1, source_target_pairs={{0,2},{1,3},{2,0},{3,1},{4,6},{5,7},{6,4},{7,5},{8,10},{9,11},{10,... | collective-permute-start | bytes 147464 | tf_op jit(solution)/shard_map/ppermute | solution.py:616
  68.5 0.5 last_free.1.refs_0_
  69.0 1.6 %collective-permute-done.15 = f32[96,128]{1,0:T(8,128)S(1)} collective-permute-done((f32[96,128]{1,0:T(8,128)S(1)}, f32[96,128]{1,0:T(8,128)S(1)}, u32[]{:S(2)}, u32[]{:S(2)}) %collective-permute-start.15) | collective-permute-done | bytes 49184 | tf_op jit(solution)/shard_map/ppermute | solution.py:616
  70.6 0.6 collective-permute-start.20
  71.2 1.5 %collective-permute-start.26 = (f32[8,2,24,256]{3,2,1,0:T(8,128)S(1)}, f32[8,2,24,256]{3,2,1,0:T(8,128)S(1)}, u32[]{:S(2)}, u32[]{:S(2)}) collective-permute-start(f32[8,2,24,256]{3,2,1,0:T(8,128)S(1)} %get-tuple-element.71.refs_12_), channel_id=1, source_target_pairs={{0,16},{8,24},{16,0},{24,8},{1,17},{9,25},{17,1},{25,9},{2,18},{10... | collective-permute-start | bytes 1179656 | tf_op jit(solution)/shard_map/ppermute | solution.py:616
  72.7 3.0 %collective-permute-start.17 = (f32[96,128]{1,0:T(8,128)S(1)}, f32[96,128]{1,0:T(8,128)S(1)}, u32[]{:S(2)}, u32[]{:S(2)}) collective-permute-start(f32[96,128]{1,0:T(8,128)S(1)} %add.18), channel_id=1, source_target_pairs={{0,4},{1,5},{2,6},{3,7},{4,0},{5,1},{6,2},{7,3},{8,12},{9,13},{10,... | collective-permute-start | bytes 147464 | tf_op jit(solution)/shard_map/ppermute | solution.py:616
  75.8 2.1 %collective-permute-done.17 = f32[96,128]{1,0:T(8,128)S(1)} collective-permute-done((f32[96,128]{1,0:T(8,128)S(1)}, f32[96,128]{1,0:T(8,128)S(1)}, u32[]{:S(2)}, u32[]{:S(2)}) %collective-permute-start.17) | collective-permute-done | bytes 49184 | tf_op jit(solution)/shard_map/ppermute | solution.py:616
  77.8 0.1 collective-permute-start.18
  77.9 0.5 collective-permute-start.23
  78.4 0.1 collective-permute-start.25
  78.5 0.6 collective-permute-done.18.other
  79.1 0.2 collective-permute-start.19
  79.3 17.9 %transforms_early.1 = (f32[96,128]{1,0:T(8,128)S(1)}, f32[96,128]{1,0:T(8,128)S(1)}) custom-call(f32[96,128]{1,0:T(8,128)S(1)} %add.19.mine, f32[96,128]{1,0:T(8,128)S(1)} %collective-permute-done.18.other), custom_call_target="tpu_custom_call" | custom-call | flops 100000000 | bytes 1000000 | tf_op jit(solution)/shard_map/transforms_early/pallas_call | solution.py:547
  97.2 0.0 collective-permute-done.20.refs_2_
  97.2 0.4 collective-permute-start.22
  97.6 0.2 collective-permute-start.21
  97.8 0.4 collective-permute-start.24
  98.2 0.2 collective-permute-start.27
  98.3 6.0 %transforms_late.1.weights = f32[24,128]{1,0:T(8,128)S(1)} custom-call(f32[96,128]{1,0:T(8,128)S(1)} %get-tuple-element.60.total, f32[96,128]{1,0:T(8,128)S(1)} %get-tuple-element.61.last), custom_call_target="tpu_custom_call" | custom-call | flops 100000000 | bytes 1000000 | tf_op jit(solution)/shard_map/transforms_late/pallas_call | solution.py:547
  104.4 5.3 %mix.1 = f32[24,4,8,4,256]{4,3,2,1,0:T(4,128)} custom-call(f32[24,128]{1,0:T(8,128)S(1)} %transforms_late.1.weights, f32[8,4,24,256]{3,2,1,0:T(8,128)S(1)} %last_free.1.refs_0_, f32[8,4,24,256]{3,2,1,0:T(8,128)S(1)} %collective-permute-done.19.refs_1_, f32[8,4,24,256]{3,2,1,0:T(8,128)S(1)} %collective-permute-done.20.refs_2_, ...), custom_call_target="tpu_custom_call" | custom-call | tf_op jit(solution)/shard_map/mix/pallas_call | solution.py:603
  (29 shorter events, 0.1 us)
Async XLA Ops:
  0.0 8.4 %copy-start.7 = (f32[24,4,8,4,256]{4,3,2,1,0:T(4,128)S(1)}, f32[24,4,8,4,256]{4,3,2,1,0:T(4,128)}, u32[]{:S(2)}) copy-start(f32[24,4,8,4,256]{4,3,2,1,0:T(4,128)} %param.8) | copy-start | bytes 9437188
  0.0 2.0 %copy-start = (f32[8,4,256]{2,1,0:T(4,128)S(1)}, f32[8,4,256]{2,1,0:T(4,128)}, u32[]{:S(2)}) copy-start(f32[8,4,256]{2,1,0:T(4,128)} %refs_9_.7) | copy-start | bytes 98308
  0.0 2.0 %copy-start.2 = (f32[8,4,256]{2,1,0:T(4,128)S(1)}, f32[8,4,256]{2,1,0:T(4,128)}, u32[]{:S(2)}) copy-start(f32[8,4,256]{2,1,0:T(4,128)} %refs_6_.1) | copy-start | bytes 98308
  0.0 2.0 %copy-start.1 = (f32[8,4,256]{2,1,0:T(4,128)S(1)}, f32[8,4,256]{2,1,0:T(4,128)}, u32[]{:S(2)}) copy-start(f32[8,4,256]{2,1,0:T(4,128)} %refs_5_.1) | copy-start | bytes 98308
  2.2 14.6 %collective-permute-start = (f32[4,56,256]{2,1,0:T(8,128)S(1)}, f32[4,56,256]{2,1,0:T(8,128)S(1)}, u32[]{:S(2)}, u32[]{:S(2)}) collective-permute-start(f32[4,56,256]{2,1,0:T(8,128)S(1)} %get-tuple-element.41), channel_id=1, source_target_pairs={{0,1},{1,2},{2,3},{3,4},{4,5},{5,6},{6,7},{8,9},{9,10},{10,11},{11... | collective-permute-start | bytes 688136 | tf_op jit(solution)/shard_map/ppermute | solution.py:638
  7.1 9.7 %collective-permute-start.1 = (f32[4,56,256]{2,1,0:T(8,128)S(1)}, f32[4,56,256]{2,1,0:T(8,128)S(1)}, u32[]{:S(2)}, u32[]{:S(2)}) collective-permute-start(f32[4,56,256]{2,1,0:T(8,128)S(1)} %get-tuple-element.42), channel_id=1, source_target_pairs={{1,0},{2,1},{3,2},{4,3},{5,4},{6,5},{7,6},{9,8},{10,9},{11,10},{12... | collective-permute-start | bytes 688136 | tf_op jit(solution)/shard_map/ppermute | solution.py:638
  10.7 20.6 %collective-permute-start.4 = (f32[8,4,24,256]{3,2,1,0:T(8,128)S(1)}, f32[8,4,24,256]{3,2,1,0:T(8,128)S(1)}, u32[]{:S(2)}, u32[]{:S(2)}) collective-permute-start(f32[8,4,24,256]{3,2,1,0:T(8,128)S(1)} %add_add_fusion.refs_4_), channel_id=1, source_target_pairs={{0,8},{8,0},{16,24},{24,16},{1,9},{9,1},{17,25},{25,17},{2,10},{10... | collective-permute-start | bytes 2359304 | tf_op jit(solution)/shard_map/ppermute | solution.py:616
  10.8 20.5 %collective-permute-start.5 = (f32[8,4,24,256]{3,2,1,0:T(8,128)S(1)}, f32[8,4,24,256]{3,2,1,0:T(8,128)S(1)}, u32[]{:S(2)}, u32[]{:S(2)}) collective-permute-start(f32[8,4,24,256]{3,2,1,0:T(8,128)S(1)} %add_add_fusion.refs_4_), channel_id=1, source_target_pairs={{0,16},{8,24},{16,0},{24,8},{1,17},{9,25},{17,1},{25,9},{2,18},{10... | collective-permute-start | bytes 2359304 | tf_op jit(solution)/shard_map/ppermute | solution.py:616
  13.3 10.2 %copy-start.3 = (s32[4,2048]{1,0:T(4,128)S(1)}, s32[4,2048]{1,0:T(4,128)}, u32[]{:S(2)}) copy-start(s32[4,2048]{1,0:T(4,128)} %obs_index.1) | copy-start | bytes 98308
  13.3 10.2 %copy-start.4 = (f32[4,2048]{1,0:T(4,128)S(1)}, f32[4,2048]{1,0:T(4,128)}, u32[]{:S(2)}) copy-start(f32[4,2048]{1,0:T(4,128)} %observed.1) | copy-start | bytes 98308
  13.4 10.2 %copy-start.5 = (f32[4,2048]{1,0:T(4,128)S(1)}, f32[4,2048]{1,0:T(4,128)}, u32[]{:S(2)}) copy-start(f32[4,2048]{1,0:T(4,128)} %obs_var.1) | copy-start | bytes 98308
  13.4 10.2 %copy-start.6 = (s32[4]{0:T(128)S(1)}, s32[4]{0:T(128)}, u32[]{:S(2)}) copy-start(s32[4]{0:T(128)} %owner.5) | copy-start | bytes 52
  17.8 8.7 %collective-permute-start.2 = (f32[4,48,256]{2,1,0:T(8,128)S(1)}, f32[4,48,256]{2,1,0:T(8,128)S(1)}, u32[]{:S(2)}, u32[]{:S(2)}) collective-permute-start(f32[4,48,256]{2,1,0:T(8,128)S(1)} %get-tuple-element.47), channel_id=1, source_target_pairs={{0,1},{1,2},{2,3},{3,4},{4,5},{5,6},{6,7},{8,9},{9,10},{10,11},{11... | collective-permute-start | bytes 589832 | tf_op jit(solution)/shard_map/ppermute | solution.py:638
  22.2 9.1 %collective-permute-start.3 = (f32[4,48,256]{2,1,0:T(8,128)S(1)}, f32[4,48,256]{2,1,0:T(8,128)S(1)}, u32[]{:S(2)}, u32[]{:S(2)}) collective-permute-start(f32[4,48,256]{2,1,0:T(8,128)S(1)} %get-tuple-element.48), channel_id=1, source_target_pairs={{1,0},{2,1},{3,2},{4,3},{5,4},{6,5},{7,6},{9,8},{10,9},{11,10},{12... | collective-permute-start | bytes 589832 | tf_op jit(solution)/shard_map/ppermute | solution.py:638
  34.0 15.2 %collective-permute-start.7 = (f32[6,4,24,256]{3,2,1,0:T(8,128)S(1)}, f32[6,4,24,256]{3,2,1,0:T(8,128)S(1)}, u32[]{:S(2)}, u32[]{:S(2)}) collective-permute-start(f32[6,4,24,256]{3,2,1,0:T(8,128)S(1)} %get-tuple-element.49.refs_0_.refs_16_), channel_id=1, source_target_pairs={{0,16},{8,24},{16,0},{24,8},{1,17},{9,25},{17,1},{25,9},{2,18},{10... | collective-permute-start | bytes 1769480 | tf_op jit(solution)/shard_map/ppermute | solution.py:616
  35.6 7.7 %collective-permute-start.8 = (f32[4,48,256]{2,1,0:T(8,128)S(1)}, f32[4,48,256]{2,1,0:T(8,128)S(1)}, u32[]{:S(2)}, u32[]{:S(2)}) collective-permute-start(f32[4,48,256]{2,1,0:T(8,128)S(1)} %get-tuple-element.52), channel_id=1, source_target_pairs={{0,1},{1,2},{2,3},{3,4},{4,5},{5,6},{6,7},{8,9},{9,10},{10,11},{11... | collective-permute-start | bytes 589832 | tf_op jit(solution)/shard_map/ppermute | solution.py:638
  40.1 9.0 %collective-permute-start.9 = (f32[4,48,256]{2,1,0:T(8,128)S(1)}, f32[4,48,256]{2,1,0:T(8,128)S(1)}, u32[]{:S(2)}, u32[]{:S(2)}) collective-permute-start(f32[4,48,256]{2,1,0:T(8,128)S(1)} %get-tuple-element.53), channel_id=1, source_target_pairs={{1,0},{2,1},{3,2},{4,3},{5,4},{6,5},{7,6},{9,8},{10,9},{11,10},{12... | collective-permute-start | bytes 589832 | tf_op jit(solution)/shard_map/ppermute | solution.py:638
  41.4 8.6 %collective-permute-start.6 = (f32[6,4,24,256]{3,2,1,0:T(8,128)S(1)}, f32[6,4,24,256]{3,2,1,0:T(8,128)S(1)}, u32[]{:S(2)}, u32[]{:S(2)}) collective-permute-start(f32[6,4,24,256]{3,2,1,0:T(8,128)S(1)} %get-tuple-element.49.refs_0_.refs_16_), channel_id=1, source_target_pairs={{0,8},{8,0},{16,24},{24,16},{1,9},{9,1},{17,25},{25,17},{2,10},{10... | collective-permute-start | bytes 1769480 | tf_op jit(solution)/shard_map/ppermute | solution.py:616
  49.2 2.1 %collective-permute-start.10 = (f32[6,4,24,256]{3,2,1,0:T(8,128)S(1)}, f32[6,4,24,256]{3,2,1,0:T(8,128)S(1)}, u32[]{:S(2)}, u32[]{:S(2)}) collective-permute-start(f32[6,4,24,256]{3,2,1,0:T(8,128)S(1)} %collective-permute-done.7.refs_2_.refs_18_), channel_id=1, source_target_pairs={{0,8},{8,0},{16,24},{24,16},{1,9},{9,1},{17,25},{25,17},{2,10},{10... | collective-permute-start | bytes 1769480 | tf_op jit(solution)/shard_map/ppermute | solution.py:616
  49.3 7.3 %collective-permute-start.12 = (f32[2,4,24,256]{3,2,1,0:T(8,128)S(1)}, f32[2,4,24,256]{3,2,1,0:T(8,128)S(1)}, u32[]{:S(2)}, u32[]{:S(2)}) collective-permute-start(f32[2,4,24,256]{3,2,1,0:T(8,128)S(1)} %get-tuple-element.54.refs_1_.refs_20_), channel_id=1, source_target_pairs={{0,16},{8,24},{16,0},{24,8},{1,17},{9,25},{17,1},{25,9},{2,18},{10... | collective-permute-start | bytes 589832 | tf_op jit(solution)/shard_map/ppermute | solution.py:616
  56.6 14.0 %collective-permute-start.16 = (f32[8,2,24,256]{3,2,1,0:T(8,128)S(1)}, f32[8,2,24,256]{3,2,1,0:T(8,128)S(1)}, u32[]{:S(2)}, u32[]{:S(2)}) collective-permute-start(f32[8,2,24,256]{3,2,1,0:T(8,128)S(1)} %get-tuple-element.58.refs_8_), channel_id=1, source_target_pairs={{0,16},{8,24},{16,0},{24,8},{1,17},{9,25},{17,1},{25,9},{2,18},{10... | collective-permute-start | bytes 1179656 | tf_op jit(solution)/shard_map/ppermute | solution.py:616
  57.3 1.4 %collective-permute-start.11 = (f32[2,4,24,256]{3,2,1,0:T(8,128)S(1)}, f32[2,4,24,256]{3,2,1,0:T(8,128)S(1)}, u32[]{:S(2)}, u32[]{:S(2)}) collective-permute-start(f32[2,4,24,256]{3,2,1,0:T(8,128)S(1)} %get-tuple-element.54.refs_1_.refs_20_), channel_id=1, source_target_pairs={{0,8},{8,0},{16,24},{24,16},{1,9},{9,1},{17,25},{25,17},{2,10},{10... | collective-permute-start | bytes 589832 | tf_op jit(solution)/shard_map/ppermute | solution.py:616
  57.3 1.7 %collective-permute-start.13 = (f32[2,4,24,256]{3,2,1,0:T(8,128)S(1)}, f32[2,4,24,256]{3,2,1,0:T(8,128)S(1)}, u32[]{:S(2)}, u32[]{:S(2)}) collective-permute-start(f32[2,4,24,256]{3,2,1,0:T(8,128)S(1)} %collective-permute-done.12.refs_3_.refs_22_), channel_id=1, source_target_pairs={{0,8},{8,0},{16,24},{24,16},{1,9},{9,1},{17,25},{25,17},{2,10},{10... | collective-permute-start | bytes 589832 | tf_op jit(solution)/shard_map/ppermute | solution.py:616
  60.5 4.2 %collective-permute-start.14 = (f32[96,128]{1,0:T(8,128)S(1)}, f32[96,128]{1,0:T(8,128)S(1)}, u32[]{:S(2)}, u32[]{:S(2)}) collective-permute-start(f32[96,128]{1,0:T(8,128)S(1)} %gram.3), channel_id=1, source_target_pairs={{0,1},{1,0},{2,3},{3,2},{4,5},{5,4},{6,7},{7,6},{8,9},{9,8},{10,11... | collective-permute-start | bytes 147464 | tf_op jit(solution)/shard_map/ppermute | solution.py:616
  64.7 5.9 %collective-permute-start.15 = (f32[96,128]{1,0:T(8,128)S(1)}, f32[96,128]{1,0:T(8,128)S(1)}, u32[]{:S(2)}, u32[]{:S(2)}) collective-permute-start(f32[96,128]{1,0:T(8,128)S(1)} %add.17), channel_id=1, source_target_pairs={{0,2},{1,3},{2,0},{3,1},{4,6},{5,7},{6,4},{7,5},{8,10},{9,11},{10,... | collective-permute-start | bytes 147464 | tf_op jit(solution)/shard_map/ppermute | solution.py:616
  70.6 26.6 %collective-permute-start.20 = (f32[8,4,24,256]{3,2,1,0:T(8,128)S(1)}, f32[8,4,24,256]{3,2,1,0:T(8,128)S(1)}, u32[]{:S(2)}, u32[]{:S(2)}) collective-permute-start(f32[8,4,24,256]{3,2,1,0:T(8,128)S(1)} %last_free.1.refs_0_), channel_id=1, source_target_pairs={{0,16},{8,24},{16,0},{24,8},{1,17},{9,25},{17,1},{25,9},{2,18},{10... | collective-permute-start | bytes 2359304 | tf_op jit(solution)/shard_map/ppermute | solution.py:616
  71.2 26.4 %collective-permute-start.26 = (f32[8,2,24,256]{3,2,1,0:T(8,128)S(1)}, f32[8,2,24,256]{3,2,1,0:T(8,128)S(1)}, u32[]{:S(2)}, u32[]{:S(2)}) collective-permute-start(f32[8,2,24,256]{3,2,1,0:T(8,128)S(1)} %get-tuple-element.71.refs_12_), channel_id=1, source_target_pairs={{0,16},{8,24},{16,0},{24,8},{1,17},{9,25},{17,1},{25,9},{2,18},{10... | collective-permute-start | bytes 1179656 | tf_op jit(solution)/shard_map/ppermute | solution.py:616
  72.7 5.1 %collective-permute-start.17 = (f32[96,128]{1,0:T(8,128)S(1)}, f32[96,128]{1,0:T(8,128)S(1)}, u32[]{:S(2)}, u32[]{:S(2)}) collective-permute-start(f32[96,128]{1,0:T(8,128)S(1)} %add.18), channel_id=1, source_target_pairs={{0,4},{1,5},{2,6},{3,7},{4,0},{5,1},{6,2},{7,3},{8,12},{9,13},{10,... | collective-permute-start | bytes 147464 | tf_op jit(solution)/shard_map/ppermute | solution.py:616
  77.8 1.3 %collective-permute-start.18 = (f32[96,128]{1,0:T(8,128)S(1)}, f32[96,128]{1,0:T(8,128)S(1)}, u32[]{:S(2)}, u32[]{:S(2)}) collective-permute-start(f32[96,128]{1,0:T(8,128)S(1)} %add.19.mine), channel_id=1, source_target_pairs={{0,8},{8,0},{16,24},{24,16},{1,9},{9,1},{17,25},{25,17},{2,10},{10... | collective-permute-start | bytes 147464 | tf_op jit(solution)/shard_map/ppermute | solution.py:616
  77.9 19.9 %collective-permute-start.23 = (f32[8,2,24,256]{3,2,1,0:T(8,128)S(1)}, f32[8,2,24,256]{3,2,1,0:T(8,128)S(1)}, u32[]{:S(2)}, u32[]{:S(2)}) collective-permute-start(f32[8,2,24,256]{3,2,1,0:T(8,128)S(1)} %get-tuple-element.58.refs_8_), channel_id=1, source_target_pairs={{0,8},{8,0},{16,24},{24,16},{1,9},{9,1},{17,25},{25,17},{2,10},{10... | collective-permute-start | bytes 1179656 | tf_op jit(solution)/shard_map/ppermute | solution.py:616
  78.4 19.8 %collective-permute-start.25 = (f32[8,2,24,256]{3,2,1,0:T(8,128)S(1)}, f32[8,2,24,256]{3,2,1,0:T(8,128)S(1)}, u32[]{:S(2)}, u32[]{:S(2)}) collective-permute-start(f32[8,2,24,256]{3,2,1,0:T(8,128)S(1)} %get-tuple-element.71.refs_12_), channel_id=1, source_target_pairs={{0,8},{8,0},{16,24},{24,16},{1,9},{9,1},{17,25},{25,17},{2,10},{10... | collective-permute-start | bytes 1179656 | tf_op jit(solution)/shard_map/ppermute | solution.py:616
  79.1 25.3 %collective-permute-start.19 = (f32[8,4,24,256]{3,2,1,0:T(8,128)S(1)}, f32[8,4,24,256]{3,2,1,0:T(8,128)S(1)}, u32[]{:S(2)}, u32[]{:S(2)}) collective-permute-start(f32[8,4,24,256]{3,2,1,0:T(8,128)S(1)} %last_free.1.refs_0_), channel_id=1, source_target_pairs={{0,8},{8,0},{16,24},{24,16},{1,9},{9,1},{17,25},{25,17},{2,10},{10... | collective-permute-start | bytes 2359304 | tf_op jit(solution)/shard_map/ppermute | solution.py:616
  97.2 7.1 %collective-permute-start.22 = (f32[8,4,24,256]{3,2,1,0:T(8,128)S(1)}, f32[8,4,24,256]{3,2,1,0:T(8,128)S(1)}, u32[]{:S(2)}, u32[]{:S(2)}) collective-permute-start(f32[8,4,24,256]{3,2,1,0:T(8,128)S(1)} %collective-permute-done.5.refs_14_.refs_6_), channel_id=1, source_target_pairs={{0,8},{8,0},{16,24},{24,16},{1,9},{9,1},{17,25},{25,17},{2,10},{10... | collective-permute-start | bytes 2359304 | tf_op jit(solution)/shard_map/ppermute | solution.py:616
  97.6 6.8 %collective-permute-start.21 = (f32[8,4,24,256]{3,2,1,0:T(8,128)S(1)}, f32[8,4,24,256]{3,2,1,0:T(8,128)S(1)}, u32[]{:S(2)}, u32[]{:S(2)}) collective-permute-start(f32[8,4,24,256]{3,2,1,0:T(8,128)S(1)} %collective-permute-done.20.refs_2_), channel_id=1, source_target_pairs={{0,8},{8,0},{16,24},{24,16},{1,9},{9,1},{17,25},{25,17},{2,10},{10... | collective-permute-start | bytes 2359304 | tf_op jit(solution)/shard_map/ppermute | solution.py:616
  97.8 6.6 %collective-permute-start.24 = (f32[8,2,24,256]{3,2,1,0:T(8,128)S(1)}, f32[8,2,24,256]{3,2,1,0:T(8,128)S(1)}, u32[]{:S(2)}, u32[]{:S(2)}) collective-permute-start(f32[8,2,24,256]{3,2,1,0:T(8,128)S(1)} %collective-permute-done.16.refs_10_), channel_id=1, source_target_pairs={{0,8},{8,0},{16,24},{24,16},{1,9},{9,1},{17,25},{25,17},{2,10},{10... | collective-permute-start | bytes 1179656 | tf_op jit(solution)/shard_map/ppermute | solution.py:616
  98.2 6.2 %collective-permute-start.27 = (f32[8,2,24,256]{3,2,1,0:T(8,128)S(1)}, f32[8,2,24,256]{3,2,1,0:T(8,128)S(1)}, u32[]{:S(2)}, u32[]{:S(2)}) collective-permute-start(f32[8,2,24,256]{3,2,1,0:T(8,128)S(1)} %collective-permute-done.26.refs_14_), channel_id=1, source_target_pairs={{0,8},{8,0},{16,24},{24,16},{1,9},{9,1},{17,25},{25,17},{2,10},{10... | collective-permute-start | bytes 1179656 | tf_op jit(solution)/shard_map/ppermute | solution.py:616

commit v13 on v11

--- a/solution.py
+++ b/solution.py
@@ -610,7 +610,8 @@
     return lax.ppermute(x, axis, [(k, k ^ bit) for k in range(count)])
 
 
-def total_over(x, axis, bit):
+def total_over(x, axis):
+    bit = 1
     while bit < lax.axis_size(axis):
         x = x + swap(x, axis, bit)
         bit *= 2
@@ -680,7 +681,7 @@
         owner, obs_index, observed, obs_var, batches // 2, nx * nz, ny
     )
     around = origin = halos(*edges)
-    conserved = collect(conserved, *around, *fields)
+    conserved = collect(conserved)
     payload = (nz, 2 * rows, ny)
     for step in range(SUBSTEPS // 2 - 2):
         inputs = [*fields, *around, *origin, *coefficients]
@@ -700,7 +701,7 @@
         [whole, payload, payload, whole, inner, whole, inner, (3, *end)],
         4 * cells,
         scratch=[whole] * 7,
-        ready=(omega, eta),
+        ready=(omega, eta, *conserved[1:]),
     )
     tracer = collect(tracer)
     around = halos(first, last)
@@ -710,7 +711,6 @@
         [free, ends, *around, *coefficients],
         [end] * 3,
         cells // nx,
-        ready=conserved[1:],
     )
     tracer = complete(tracer, tracer_ends)
     tracer_ends = collect(tracer_ends)
@@ -724,12 +724,12 @@
         [whole],
         cells,
     )
-    internal = collect(internal, across(tracer_ends))
+    internal = collect(internal, across(tracer_ends), begun)
     half = gram(owner, omega, eta, begun, tracer_ends, offsets, (0, nx - 1))
-    half = half + swap(half, "space", 1)
+    half = tie(total_over(half, "space"), across(internal))
     free = collect(free, half)
-    half = total_over(half, "space", 2)
     other = swap(half, "member", 1)
+    internal = complete(internal, half)
     square = (members, LANES)
     total, extended = transform_call(
         early_kernel,
@@ -738,7 +738,6 @@
         [(batches, members, LANES)],
         [half, other],
     )
-    internal = complete(internal, total)
     free = complete(free, total)
     (weights,) = transform_call(
         functools.partial(late_kernel, offsets=offsets, blocks=blocks, rows=rows),

time: 119 us -> 110 us (0.924); the launches traced: 118 us -> 108 us
  waiting for transfers between devices: 36.2 us -> 28.1 us
  starting transfers between devices: 37.7 us -> 34.9 us
    ppermute x19, waiting for transfers between devices: 21.2 us -> 13.1 us  [swap(): return lax.ppermute(x, axis, [(k, k ^ bit) for k in range(count)])]
    ppermute x3, waiting for transfers between devices: 7.73 us -> 10.7 us  [halos(): lax.ppermute(first, 'space', backward)]
    ppermute x3, waiting for transfers between devices: 7.22 us -> 4.34 us  [halos(): lax.ppermute(last, 'space', forward)]
    ppermute x19, starting transfers between devices: 19.9 us -> 17.3 us  [swap(): return lax.ppermute(x, axis, [(k, k ^ bit) for k in range(count)])]
  transfers between devices with their start and end apart: 25 -> 25, of which waited for: 12 -> 12; matrix products, arithmetic and copies ran while one was open for 4% -> 4% of each run, Pallas kernels for 26% -> 28%
where the time goes in v13:
time: 110 us; the launch traced here: 108 us
  Pallas kernels  38 us (35%)
  starting transfers between devices  34.9 us (32%)
  waiting for transfers between devices  28.1 us (26%)
  local copies, waits for them, and re-layouts  4.89 us (4%)
  other arithmetic  1.29 us (1%)
    pallas_call x2, Pallas kernels, transform_call(): pl.pallas_call(kernel, out_shape=[jax.ShapeDtypeStruct(shape, f32) for sh...  23.9 us
    ppermute x19, starting transfers between devices, swap(): return lax.ppermute(x, axis, [(k, k ^ bit) for k in range(count)])  17.3 us
    ppermute x3, starting transfers between devices, halos(): lax.ppermute(last, 'space', forward)  13.8 us
    ppermute x19, waiting for transfers between devices, swap(): return lax.ppermute(x, axis, [(k, k ^ bit) for k in range(count)])  13.1 us
    ppermute x3, waiting for transfers between devices, halos(): lax.ppermute(first, 'space', backward)  10.7 us
    pallas_call x6, Pallas kernels, forecast_call(): pl.pallas_call(body, out_shape=[jax.ShapeDtypeStruct(shape, f32) for shap...  5.91 us
    pallas_call x1, Pallas kernels, mix(): pl.pallas_call(functools.partial(mix_kernel, blocks=blocks), grid=(nx,),...  5.25 us
    ppermute x3, waiting for transfers between devices, halos(): lax.ppermute(last, 'space', forward)  4.34 us
  transfers between devices with their start and end apart: 25, of which 12 were waited for; matrix products, arithmetic and copies ran while one was open for 4% of the time, Pallas kernels for 28%

profile of v13, /device:TPU:0, one launch (start us, length us, event | category | flops | bytes accessed | tf_op | source)
XLA Modules:
  0.0 107.6 jit_solution(18215874967701172174)
XLA Ops:
  0.0 1.6 %fusion = (f32[24,3,2,4,256]{4,3,2,1,0:T(4,128)S(1)}, f32[24,3,2,4,256]{4,3,2,1,0:T(4,128)S(1)}) fusion(f32[24,4,8,4,256]{4,3,2,1,0:T(4,128)} %param.8), kind=kLoop, calls=%fused_computation.7 | loop fusion | bytes 2359296 | tf_op jit(solution)/shard_map/slice | solution.py:668
  1.6 0.4 copy_bitcast_fusion.4
  2.0 0.2 first_edges.1
  2.2 4.9 %collective-permute-start = (f32[4,56,256]{2,1,0:T(8,128)S(1)}, f32[4,56,256]{2,1,0:T(8,128)S(1)}, u32[]{:S(2)}, u32[]{:S(2)}) collective-permute-start(f32[4,56,256]{2,1,0:T(8,128)S(1)} %get-tuple-element.38), channel_id=1, source_target_pairs={{0,1},{1,2},{2,3},{3,4},{4,5},{5,6},{6,7},{8,9},{9,10},{10,11},{11... | collective-permute-start | bytes 688136 | tf_op jit(solution)/shard_map/ppermute | solution.py:633
  7.1 1.3 %collective-permute-start.1 = (f32[4,56,256]{2,1,0:T(8,128)S(1)}, f32[4,56,256]{2,1,0:T(8,128)S(1)}, u32[]{:S(2)}, u32[]{:S(2)}) collective-permute-start(f32[4,56,256]{2,1,0:T(8,128)S(1)} %get-tuple-element.39), channel_id=1, source_target_pairs={{1,0},{2,1},{3,2},{4,3},{5,4},{6,5},{7,6},{9,8},{10,9},{11,10},{12... | collective-permute-start | bytes 688136 | tf_op jit(solution)/shard_map/ppermute | solution.py:633
  8.4 1.0 fusion.1
  9.5 1.3 %add_add_fusion.refs_4_ = f32[8,4,24,256]{3,2,1,0:T(8,128)S(1)} fusion(f32[24,1,8,4,256]{4,3,2,1,0:T(4,128)S(1)} %get-tuple-element.71, f32[24,1,8,4,256]{4,3,2,1,0:T(4,128)S(1)} %get-tuple-element.70, f32[24,1,8,4,256]{4,3,2,1,0:T(4,128)S(1)} %get-tuple-element.69), kind=kLoop, calls=%fused_computation.4 | loop fusion | flops 393216 | bytes 3145728 | tf_op jit(solution)/shard_map/add | solution.py:679
  10.7 0.1 collective-permute-start.4
  10.8 1.6 %collective-permute-start.5 = (f32[8,4,24,256]{3,2,1,0:T(8,128)S(1)}, f32[8,4,24,256]{3,2,1,0:T(8,128)S(1)}, u32[]{:S(2)}, u32[]{:S(2)}) collective-permute-start(f32[8,4,24,256]{3,2,1,0:T(8,128)S(1)} %add_add_fusion.refs_4_), channel_id=1, source_target_pairs={{0,16},{8,24},{16,0},{24,8},{1,17},{9,25},{17,1},{25,9},{2,18},{10... | collective-permute-start | bytes 2359304 | tf_op jit(solution)/shard_map/ppermute | solution.py:610
  12.4 0.9 copy_bitcast_fusion
  13.3 0.0 copy-start.3
  13.3 0.0 copy-start.4
  13.4 0.0 copy-start.5
  13.4 0.0 copy-start.6
  13.4 0.9 copy_bitcast_fusion.2
  14.3 2.6 %collective-permute-done.refs_4_.refs_6_.refs_7_ = f32[4,56,256]{2,1,0:T(8,128)S(1)} collective-permute-done((f32[4,56,256]{2,1,0:T(8,128)S(1)}, f32[4,56,256]{2,1,0:T(8,128)S(1)}, u32[]{:S(2)}, u32[]{:S(2)}) %collective-permute-start) | collective-permute-done | bytes 229408 | tf_op jit(solution)/shard_map/ppermute | solution.py:633
  16.9 1.0 next_edges.1
  17.8 4.4 %collective-permute-start.2 = (f32[4,48,256]{2,1,0:T(8,128)S(1)}, f32[4,48,256]{2,1,0:T(8,128)S(1)}, u32[]{:S(2)}, u32[]{:S(2)}) collective-permute-start(f32[4,48,256]{2,1,0:T(8,128)S(1)} %get-tuple-element.44), channel_id=1, source_target_pairs={{0,1},{1,2},{2,3},{3,4},{4,5},{5,6},{6,7},{8,9},{9,10},{10,11},{11... | collective-permute-start | bytes 589832 | tf_op jit(solution)/shard_map/ppermute | solution.py:633
  22.2 1.3 %collective-permute-start.3 = (f32[4,48,256]{2,1,0:T(8,128)S(1)}, f32[4,48,256]{2,1,0:T(8,128)S(1)}, u32[]{:S(2)}, u32[]{:S(2)}) collective-permute-start(f32[4,48,256]{2,1,0:T(8,128)S(1)} %get-tuple-element.45), channel_id=1, source_target_pairs={{1,0},{2,1},{3,2},{4,3},{5,4},{6,5},{7,6},{9,8},{10,9},{11,10},{12... | collective-permute-start | bytes 589832 | tf_op jit(solution)/shard_map/ppermute | solution.py:633
  23.6 1.4 %voxel_weights.1 = (f32[2,32,256]{2,1,0:T(8,128)S(1)}, f32[2,32,256]{2,1,0:T(8,128)S(1)}) custom-call(s32[4]{0:T(128)S(1)} %copy-done.6, s32[4,2048]{1,0:T(4,128)S(1)} %copy-done.3, f32[4,2048]{1,0:T(4,128)S(1)} %copy-done.4, f32[4,2048]{1,0:T(4,128)S(1)} %copy-done.5), custom_call_target="tpu_custom_call" | custom-call | tf_op jit(solution)/shard_map/voxel_weights/pallas_call | solution.py:374
  25.0 1.5 %two_substeps.1 = (f32[8,4,24,256]{3,2,1,0:T(8,128)S(1)}, f32[8,4,24,256]{3,2,1,0:T(8,128)S(1)}, f32[8,4,24,256]{3,2,1,0:T(8,128)S(1)}, f32[8,4,24,256]{3,2,1,0:T(8,128)S(1)}) custom-call(f32[8,4,24,256]{3,2,1,0:T(8,128)S(1)} %get-tuple-element.76.refs_0_, f32[8,4,24,256]{3,2,1,0:T(8,128)S(1)} %get-tuple-element.75.refs_1_, ...), custom_call_target="tpu_custom_call" | custom-call | flops 11796480 | bytes 12582912 | tf_op jit(solution)/shard_map/two_substeps/pallas_call | solution.py:323
  26.5 0.0 collective-permute-done.2.refs_4_
  26.6 4.8 %collective-permute-done.3.refs_5_ = f32[4,48,256]{2,1,0:T(8,128)S(1)} collective-permute-done((f32[4,48,256]{2,1,0:T(8,128)S(1)}, f32[4,48,256]{2,1,0:T(8,128)S(1)}, u32[]{:S(2)}, u32[]{:S(2)}) %collective-permute-start.3) | collective-permute-done | bytes 196640 | tf_op jit(solution)/shard_map/ppermute | solution.py:633
  31.4 0.0 collective-permute-done.5.refs_14_.refs_6_
  31.4 0.0 collective-permute-done.4.refs_13_.refs_5_
  31.4 2.6 %last_steps.1 = (f32[8,4,24,256]{3,2,1,0:T(8,128)S(1)}, f32[4,48,256]{2,1,0:T(8,128)S(1)}, f32[4,48,256]{2,1,0:T(8,128)S(1)}, f32[8,4,24,256]{3,2,1,0:T(8,128)S(...) custom-call(f32[8,4,24,256]{3,2,1,0:T(8,128)S(1)} %get-tuple-element, ...), custom_call_target="tpu_custom_call" | custom-call | flops 23592960 | bytes 25165824 | tf_op jit(solution)/shard_map/last_steps/pallas_call | solution.py:323
  34.0 1.6 %collective-permute-start.7 = (f32[6,4,24,256]{3,2,1,0:T(8,128)S(1)}, f32[6,4,24,256]{3,2,1,0:T(8,128)S(1)}, u32[]{:S(2)}, u32[]{:S(2)}) collective-permute-start(f32[6,4,24,256]{3,2,1,0:T(8,128)S(1)} %get-tuple-element.46.refs_0_.refs_12_), channel_id=1, source_target_pairs={{0,16},{8,24},{16,0},{24,8},{1,17},{9,25},{17,1},{25,9},{2,18},{10... | collective-permute-start | bytes 1769480 | tf_op jit(solution)/shard_map/ppermute | solution.py:610
  35.6 4.5 %collective-permute-start.8 = (f32[4,48,256]{2,1,0:T(8,128)S(1)}, f32[4,48,256]{2,1,0:T(8,128)S(1)}, u32[]{:S(2)}, u32[]{:S(2)}) collective-permute-start(f32[4,48,256]{2,1,0:T(8,128)S(1)} %get-tuple-element.49), channel_id=1, source_target_pairs={{0,1},{1,2},{2,3},{3,4},{4,5},{5,6},{6,7},{8,9},{9,10},{10,11},{11... | collective-permute-start | bytes 589832 | tf_op jit(solution)/shard_map/ppermute | solution.py:633
  40.1 1.3 %collective-permute-start.9 = (f32[4,48,256]{2,1,0:T(8,128)S(1)}, f32[4,48,256]{2,1,0:T(8,128)S(1)}, u32[]{:S(2)}, u32[]{:S(2)}) collective-permute-start(f32[4,48,256]{2,1,0:T(8,128)S(1)} %get-tuple-element.50), channel_id=1, source_target_pairs={{1,0},{2,1},{3,2},{4,3},{5,4},{6,5},{7,6},{9,8},{10,9},{11,10},{12... | collective-permute-start | bytes 589832 | tf_op jit(solution)/shard_map/ppermute | solution.py:633
  41.4 0.1 collective-permute-start.6
  41.5 1.8 %collective-permute-done.8.refs_2_.refs_5_ = f32[4,48,256]{2,1,0:T(8,128)S(1)} collective-permute-done((f32[4,48,256]{2,1,0:T(8,128)S(1)}, f32[4,48,256]{2,1,0:T(8,128)S(1)}, u32[]{:S(2)}, u32[]{:S(2)}) %collective-permute-start.8) | collective-permute-done | bytes 196640 | tf_op jit(solution)/shard_map/ppermute | solution.py:633
  43.3 5.8 %collective-permute-done.9.refs_3_.refs_6_ = f32[4,48,256]{2,1,0:T(8,128)S(1)} collective-permute-done((f32[4,48,256]{2,1,0:T(8,128)S(1)}, f32[4,48,256]{2,1,0:T(8,128)S(1)}, u32[]{:S(2)}, u32[]{:S(2)}) %collective-permute-start.9) | collective-permute-done | bytes 196640 | tf_op jit(solution)/shard_map/ppermute | solution.py:633
  49.1 0.1 last_ends.1
  49.2 0.0 collective-permute-done.7.refs_2_.refs_14_
  49.2 0.1 collective-permute-start.10
  49.3 0.7 collective-permute-start.12
  50.0 0.0 collective-permute-done.6.refs_1_.refs_13_
  50.0 1.3 %collective-permute-done.10.refs_3_.refs_15_ = f32[6,4,24,256]{3,2,1,0:T(8,128)S(1)} collective-permute-done((f32[6,4,24,256]{3,2,1,0:T(8,128)S(1)}, f32[6,4,24,256]{3,2,1,0:T(8,128)S(1)}, u32[]{:S(2)}, u32[]{:S(2)}) %collective-permute-start.10) | collective-permute-done | bytes 589856 | tf_op jit(solution)/shard_map/ppermute | solution.py:610
  51.3 0.7 gram.2.refs_0_
  52.1 4.6 %collective-permute-done.12.refs_3_.refs_18_ = f32[2,4,24,256]{3,2,1,0:T(8,128)S(1)} collective-permute-done((f32[2,4,24,256]{3,2,1,0:T(8,128)S(1)}, f32[2,4,24,256]{3,2,1,0:T(8,128)S(1)}, u32[]{:S(2)}, u32[]{:S(2)}) %collective-permute-start.12) | collective-permute-done | bytes 196640 | tf_op jit(solution)/shard_map/ppermute | solution.py:610
  56.6 0.7 collective-permute-start.17
  57.3 0.5 collective-permute-start.13
  57.8 0.9 collective-permute-done.11.refs_2_.refs_17_
  58.8 0.3 collective-permute-done.13.refs_4_.refs_19_
  59.0 0.7 gram.3
  59.7 2.6 %collective-permute-start.14 = (f32[96,128]{1,0:T(8,128)S(1)}, f32[96,128]{1,0:T(8,128)S(1)}, u32[]{:S(2)}, u32[]{:S(2)}) collective-permute-start(f32[96,128]{1,0:T(8,128)S(1)} %gram.3), channel_id=1, source_target_pairs={{0,1},{1,0},{2,3},{3,2},{4,5},{5,4},{6,7},{7,6},{8,9},{9,8},{10,11... | collective-permute-start | bytes 147464 | tf_op jit(solution)/shard_map/ppermute | solution.py:610
  62.3 2.2 %collective-permute-done.14 = f32[96,128]{1,0:T(8,128)S(1)} collective-permute-done((f32[96,128]{1,0:T(8,128)S(1)}, f32[96,128]{1,0:T(8,128)S(1)}, u32[]{:S(2)}, u32[]{:S(2)}) %collective-permute-start.14) | collective-permute-done | bytes 49184 | tf_op jit(solution)/shard_map/ppermute | solution.py:610
  64.5 4.0 %collective-permute-start.15 = (f32[96,128]{1,0:T(8,128)S(1)}, f32[96,128]{1,0:T(8,128)S(1)}, u32[]{:S(2)}, u32[]{:S(2)}) collective-permute-start(f32[96,128]{1,0:T(8,128)S(1)} %add.17), channel_id=1, source_target_pairs={{0,2},{1,3},{2,0},{3,1},{4,6},{5,7},{6,4},{7,5},{8,10},{9,11},{10,... | collective-permute-start | bytes 147464 | tf_op jit(solution)/shard_map/ppermute | solution.py:610
  68.5 2.1 %collective-permute-done.15 = f32[96,128]{1,0:T(8,128)S(1)} collective-permute-done((f32[96,128]{1,0:T(8,128)S(1)}, f32[96,128]{1,0:T(8,128)S(1)}, u32[]{:S(2)}, u32[]{:S(2)}) %collective-permute-start.15) | collective-permute-done | bytes 49184 | tf_op jit(solution)/shard_map/ppermute | solution.py:610
  70.6 3.1 %collective-permute-start.16 = (f32[96,128]{1,0:T(8,128)S(1)}, f32[96,128]{1,0:T(8,128)S(1)}, u32[]{:S(2)}, u32[]{:S(2)}) collective-permute-start(f32[96,128]{1,0:T(8,128)S(1)} %add.18), channel_id=1, source_target_pairs={{0,4},{1,5},{2,6},{3,7},{4,0},{5,1},{6,2},{7,3},{8,12},{9,13},{10,... | collective-permute-start | bytes 147464 | tf_op jit(solution)/shard_map/ppermute | solution.py:610
  73.7 0.5 last_free.1.refs_0_
  74.2 1.6 %collective-permute-done.16 = f32[96,128]{1,0:T(8,128)S(1)} collective-permute-done((f32[96,128]{1,0:T(8,128)S(1)}, f32[96,128]{1,0:T(8,128)S(1)}, u32[]{:S(2)}, u32[]{:S(2)}) %collective-permute-start.16) | collective-permute-done | bytes 49184 | tf_op jit(solution)/shard_map/ppermute | solution.py:610
  75.8 0.0 collective-permute-done.17.refs_10_
  75.8 0.7 collective-permute-start.20
  76.5 0.0 collective-permute-start.18
  76.5 0.5 collective-permute-start.23
  77.0 0.5 collective-permute-start.22
  77.5 0.2 collective-permute-done.18.other
  77.7 0.2 collective-permute-start.24
  77.9 17.9 %transforms_early.1 = (f32[96,128]{1,0:T(8,128)S(1)}, f32[96,128]{1,0:T(8,128)S(1)}) custom-call(f32[96,128]{1,0:T(8,128)S(1)} %add.19.mine, f32[96,128]{1,0:T(8,128)S(1)} %collective-permute-done.18.other), custom_call_target="tpu_custom_call" | custom-call | flops 100000000 | bytes 1000000 | tf_op jit(solution)/shard_map/transforms_early/pallas_call | solution.py:542
  95.8 0.0 collective-permute-done.20.refs_2_
  95.8 0.4 collective-permute-start.21
  96.2 6.0 %transforms_late.1.weights = f32[24,128]{1,0:T(8,128)S(1)} custom-call(f32[96,128]{1,0:T(8,128)S(1)} %get-tuple-element.57.total, f32[96,128]{1,0:T(8,128)S(1)} %get-tuple-element.58.last), custom_call_target="tpu_custom_call" | custom-call | flops 100000000 | bytes 1000000 | tf_op jit(solution)/shard_map/transforms_late/pallas_call | solution.py:542
  102.3 5.3 %mix.1 = f32[24,4,8,4,256]{4,3,2,1,0:T(4,128)} custom-call(f32[24,128]{1,0:T(8,128)S(1)} %transforms_late.1.weights, f32[8,4,24,256]{3,2,1,0:T(8,128)S(1)} %last_free.1.refs_0_, f32[8,4,24,256]{3,2,1,0:T(8,128)S(1)} %collective-permute-done.19.refs_1_, f32[8,4,24,256]{3,2,1,0:T(8,128)S(1)} %collective-permute-done.20.refs_2_, ...), custom_call_target="tpu_custom_call" | custom-call | tf_op jit(solution)/shard_map/mix/pallas_call | solution.py:597
  (23 shorter events, 0.1 us)
Async XLA Ops:
  0.0 8.4 %copy-start.7 = (f32[24,4,8,4,256]{4,3,2,1,0:T(4,128)S(1)}, f32[24,4,8,4,256]{4,3,2,1,0:T(4,128)}, u32[]{:S(2)}) copy-start(f32[24,4,8,4,256]{4,3,2,1,0:T(4,128)} %param.8) | copy-start | bytes 9437188
  0.0 2.0 %copy-start = (f32[8,4,256]{2,1,0:T(4,128)S(1)}, f32[8,4,256]{2,1,0:T(4,128)}, u32[]{:S(2)}) copy-start(f32[8,4,256]{2,1,0:T(4,128)} %refs_9_.7) | copy-start | bytes 98308
  0.0 2.0 %copy-start.2 = (f32[8,4,256]{2,1,0:T(4,128)S(1)}, f32[8,4,256]{2,1,0:T(4,128)}, u32[]{:S(2)}) copy-start(f32[8,4,256]{2,1,0:T(4,128)} %refs_6_.1) | copy-start | bytes 98308
  0.0 2.0 %copy-start.1 = (f32[8,4,256]{2,1,0:T(4,128)S(1)}, f32[8,4,256]{2,1,0:T(4,128)}, u32[]{:S(2)}) copy-start(f32[8,4,256]{2,1,0:T(4,128)} %refs_5_.1) | copy-start | bytes 98308
  2.2 14.6 %collective-permute-start = (f32[4,56,256]{2,1,0:T(8,128)S(1)}, f32[4,56,256]{2,1,0:T(8,128)S(1)}, u32[]{:S(2)}, u32[]{:S(2)}) collective-permute-start(f32[4,56,256]{2,1,0:T(8,128)S(1)} %get-tuple-element.38), channel_id=1, source_target_pairs={{0,1},{1,2},{2,3},{3,4},{4,5},{5,6},{6,7},{8,9},{9,10},{10,11},{11... | collective-permute-start | bytes 688136 | tf_op jit(solution)/shard_map/ppermute | solution.py:633
  7.1 9.7 %collective-permute-start.1 = (f32[4,56,256]{2,1,0:T(8,128)S(1)}, f32[4,56,256]{2,1,0:T(8,128)S(1)}, u32[]{:S(2)}, u32[]{:S(2)}) collective-permute-start(f32[4,56,256]{2,1,0:T(8,128)S(1)} %get-tuple-element.39), channel_id=1, source_target_pairs={{1,0},{2,1},{3,2},{4,3},{5,4},{6,5},{7,6},{9,8},{10,9},{11,10},{12... | collective-permute-start | bytes 688136 | tf_op jit(solution)/shard_map/ppermute | solution.py:633
  10.7 20.6 %collective-permute-start.4 = (f32[8,4,24,256]{3,2,1,0:T(8,128)S(1)}, f32[8,4,24,256]{3,2,1,0:T(8,128)S(1)}, u32[]{:S(2)}, u32[]{:S(2)}) collective-permute-start(f32[8,4,24,256]{3,2,1,0:T(8,128)S(1)} %add_add_fusion.refs_4_), channel_id=1, source_target_pairs={{0,8},{8,0},{16,24},{24,16},{1,9},{9,1},{17,25},{25,17},{2,10},{10... | collective-permute-start | bytes 2359304 | tf_op jit(solution)/shard_map/ppermute | solution.py:610
  10.8 20.5 %collective-permute-start.5 = (f32[8,4,24,256]{3,2,1,0:T(8,128)S(1)}, f32[8,4,24,256]{3,2,1,0:T(8,128)S(1)}, u32[]{:S(2)}, u32[]{:S(2)}) collective-permute-start(f32[8,4,24,256]{3,2,1,0:T(8,128)S(1)} %add_add_fusion.refs_4_), channel_id=1, source_target_pairs={{0,16},{8,24},{16,0},{24,8},{1,17},{9,25},{17,1},{25,9},{2,18},{10... | collective-permute-start | bytes 2359304 | tf_op jit(solution)/shard_map/ppermute | solution.py:610
  13.3 10.2 %copy-start.3 = (s32[4,2048]{1,0:T(4,128)S(1)}, s32[4,2048]{1,0:T(4,128)}, u32[]{:S(2)}) copy-start(s32[4,2048]{1,0:T(4,128)} %obs_index.1) | copy-start | bytes 98308
  13.3 10.2 %copy-start.4 = (f32[4,2048]{1,0:T(4,128)S(1)}, f32[4,2048]{1,0:T(4,128)}, u32[]{:S(2)}) copy-start(f32[4,2048]{1,0:T(4,128)} %observed.1) | copy-start | bytes 98308
  13.4 10.2 %copy-start.5 = (f32[4,2048]{1,0:T(4,128)S(1)}, f32[4,2048]{1,0:T(4,128)}, u32[]{:S(2)}) copy-start(f32[4,2048]{1,0:T(4,128)} %obs_var.1) | copy-start | bytes 98308
  13.4 10.2 %copy-start.6 = (s32[4]{0:T(128)S(1)}, s32[4]{0:T(128)}, u32[]{:S(2)}) copy-start(s32[4]{0:T(128)} %owner.5) | copy-start | bytes 52
  17.8 8.7 %collective-permute-start.2 = (f32[4,48,256]{2,1,0:T(8,128)S(1)}, f32[4,48,256]{2,1,0:T(8,128)S(1)}, u32[]{:S(2)}, u32[]{:S(2)}) collective-permute-start(f32[4,48,256]{2,1,0:T(8,128)S(1)} %get-tuple-element.44), channel_id=1, source_target_pairs={{0,1},{1,2},{2,3},{3,4},{4,5},{5,6},{6,7},{8,9},{9,10},{10,11},{11... | collective-permute-start | bytes 589832 | tf_op jit(solution)/shard_map/ppermute | solution.py:633
  22.2 9.1 %collective-permute-start.3 = (f32[4,48,256]{2,1,0:T(8,128)S(1)}, f32[4,48,256]{2,1,0:T(8,128)S(1)}, u32[]{:S(2)}, u32[]{:S(2)}) collective-permute-start(f32[4,48,256]{2,1,0:T(8,128)S(1)} %get-tuple-element.45), channel_id=1, source_target_pairs={{1,0},{2,1},{3,2},{4,3},{5,4},{6,5},{7,6},{9,8},{10,9},{11,10},{12... | collective-permute-start | bytes 589832 | tf_op jit(solution)/shard_map/ppermute | solution.py:633
  34.0 15.2 %collective-permute-start.7 = (f32[6,4,24,256]{3,2,1,0:T(8,128)S(1)}, f32[6,4,24,256]{3,2,1,0:T(8,128)S(1)}, u32[]{:S(2)}, u32[]{:S(2)}) collective-permute-start(f32[6,4,24,256]{3,2,1,0:T(8,128)S(1)} %get-tuple-element.46.refs_0_.refs_12_), channel_id=1, source_target_pairs={{0,16},{8,24},{16,0},{24,8},{1,17},{9,25},{17,1},{25,9},{2,18},{10... | collective-permute-start | bytes 1769480 | tf_op jit(solution)/shard_map/ppermute | solution.py:610
  35.6 7.7 %collective-permute-start.8 = (f32[4,48,256]{2,1,0:T(8,128)S(1)}, f32[4,48,256]{2,1,0:T(8,128)S(1)}, u32[]{:S(2)}, u32[]{:S(2)}) collective-permute-start(f32[4,48,256]{2,1,0:T(8,128)S(1)} %get-tuple-element.49), channel_id=1, source_target_pairs={{0,1},{1,2},{2,3},{3,4},{4,5},{5,6},{6,7},{8,9},{9,10},{10,11},{11... | collective-permute-start | bytes 589832 | tf_op jit(solution)/shard_map/ppermute | solution.py:633
  40.1 9.0 %collective-permute-start.9 = (f32[4,48,256]{2,1,0:T(8,128)S(1)}, f32[4,48,256]{2,1,0:T(8,128)S(1)}, u32[]{:S(2)}, u32[]{:S(2)}) collective-permute-start(f32[4,48,256]{2,1,0:T(8,128)S(1)} %get-tuple-element.50), channel_id=1, source_target_pairs={{1,0},{2,1},{3,2},{4,3},{5,4},{6,5},{7,6},{9,8},{10,9},{11,10},{12... | collective-permute-start | bytes 589832 | tf_op jit(solution)/shard_map/ppermute | solution.py:633
  41.4 8.6 %collective-permute-start.6 = (f32[6,4,24,256]{3,2,1,0:T(8,128)S(1)}, f32[6,4,24,256]{3,2,1,0:T(8,128)S(1)}, u32[]{:S(2)}, u32[]{:S(2)}) collective-permute-start(f32[6,4,24,256]{3,2,1,0:T(8,128)S(1)} %get-tuple-element.46.refs_0_.refs_12_), channel_id=1, source_target_pairs={{0,8},{8,0},{16,24},{24,16},{1,9},{9,1},{17,25},{25,17},{2,10},{10... | collective-permute-start | bytes 1769480 | tf_op jit(solution)/shard_map/ppermute | solution.py:610
  49.2 2.1 %collective-permute-start.10 = (f32[6,4,24,256]{3,2,1,0:T(8,128)S(1)}, f32[6,4,24,256]{3,2,1,0:T(8,128)S(1)}, u32[]{:S(2)}, u32[]{:S(2)}) collective-permute-start(f32[6,4,24,256]{3,2,1,0:T(8,128)S(1)} %collective-permute-done.7.refs_2_.refs_14_), channel_id=1, source_target_pairs={{0,8},{8,0},{16,24},{24,16},{1,9},{9,1},{17,25},{25,17},{2,10},{10... | collective-permute-start | bytes 1769480 | tf_op jit(solution)/shard_map/ppermute | solution.py:610
  49.3 7.3 %collective-permute-start.12 = (f32[2,4,24,256]{3,2,1,0:T(8,128)S(1)}, f32[2,4,24,256]{3,2,1,0:T(8,128)S(1)}, u32[]{:S(2)}, u32[]{:S(2)}) collective-permute-start(f32[2,4,24,256]{3,2,1,0:T(8,128)S(1)} %get-tuple-element.51.refs_1_.refs_16_), channel_id=1, source_target_pairs={{0,16},{8,24},{16,0},{24,8},{1,17},{9,25},{17,1},{25,9},{2,18},{10... | collective-permute-start | bytes 589832 | tf_op jit(solution)/shard_map/ppermute | solution.py:610
  56.6 19.1 %collective-permute-start.17 = (f32[8,4,24,256]{3,2,1,0:T(8,128)S(1)}, f32[8,4,24,256]{3,2,1,0:T(8,128)S(1)}, u32[]{:S(2)}, u32[]{:S(2)}) collective-permute-start(f32[8,4,24,256]{3,2,1,0:T(8,128)S(1)} %get-tuple-element.55.refs_8_), channel_id=1, source_target_pairs={{0,16},{8,24},{16,0},{24,8},{1,17},{9,25},{17,1},{25,9},{2,18},{10... | collective-permute-start | bytes 2359304 | tf_op jit(solution)/shard_map/ppermute | solution.py:610
  57.3 1.4 %collective-permute-start.11 = (f32[2,4,24,256]{3,2,1,0:T(8,128)S(1)}, f32[2,4,24,256]{3,2,1,0:T(8,128)S(1)}, u32[]{:S(2)}, u32[]{:S(2)}) collective-permute-start(f32[2,4,24,256]{3,2,1,0:T(8,128)S(1)} %get-tuple-element.51.refs_1_.refs_16_), channel_id=1, source_target_pairs={{0,8},{8,0},{16,24},{24,16},{1,9},{9,1},{17,25},{25,17},{2,10},{10... | collective-permute-start | bytes 589832 | tf_op jit(solution)/shard_map/ppermute | solution.py:610
  57.3 1.7 %collective-permute-start.13 = (f32[2,4,24,256]{3,2,1,0:T(8,128)S(1)}, f32[2,4,24,256]{3,2,1,0:T(8,128)S(1)}, u32[]{:S(2)}, u32[]{:S(2)}) collective-permute-start(f32[2,4,24,256]{3,2,1,0:T(8,128)S(1)} %collective-permute-done.12.refs_3_.refs_18_), channel_id=1, source_target_pairs={{0,8},{8,0},{16,24},{24,16},{1,9},{9,1},{17,25},{25,17},{2,10},{10... | collective-permute-start | bytes 589832 | tf_op jit(solution)/shard_map/ppermute | solution.py:610
  59.7 4.8 %collective-permute-start.14 = (f32[96,128]{1,0:T(8,128)S(1)}, f32[96,128]{1,0:T(8,128)S(1)}, u32[]{:S(2)}, u32[]{:S(2)}) collective-permute-start(f32[96,128]{1,0:T(8,128)S(1)} %gram.3), channel_id=1, source_target_pairs={{0,1},{1,0},{2,3},{3,2},{4,5},{5,4},{6,7},{7,6},{8,9},{9,8},{10,11... | collective-permute-start | bytes 147464 | tf_op jit(solution)/shard_map/ppermute | solution.py:610
  64.5 6.1 %collective-permute-start.15 = (f32[96,128]{1,0:T(8,128)S(1)}, f32[96,128]{1,0:T(8,128)S(1)}, u32[]{:S(2)}, u32[]{:S(2)}) collective-permute-start(f32[96,128]{1,0:T(8,128)S(1)} %add.17), channel_id=1, source_target_pairs={{0,2},{1,3},{2,0},{3,1},{4,6},{5,7},{6,4},{7,5},{8,10},{9,11},{10,... | collective-permute-start | bytes 147464 | tf_op jit(solution)/shard_map/ppermute | solution.py:610
  70.6 5.2 %collective-permute-start.16 = (f32[96,128]{1,0:T(8,128)S(1)}, f32[96,128]{1,0:T(8,128)S(1)}, u32[]{:S(2)}, u32[]{:S(2)}) collective-permute-start(f32[96,128]{1,0:T(8,128)S(1)} %add.18), channel_id=1, source_target_pairs={{0,4},{1,5},{2,6},{3,7},{4,0},{5,1},{6,2},{7,3},{8,12},{9,13},{10,... | collective-permute-start | bytes 147464 | tf_op jit(solution)/shard_map/ppermute | solution.py:610
  75.8 20.0 %collective-permute-start.20 = (f32[8,4,24,256]{3,2,1,0:T(8,128)S(1)}, f32[8,4,24,256]{3,2,1,0:T(8,128)S(1)}, u32[]{:S(2)}, u32[]{:S(2)}) collective-permute-start(f32[8,4,24,256]{3,2,1,0:T(8,128)S(1)} %last_free.1.refs_0_), channel_id=1, source_target_pairs={{0,16},{8,24},{16,0},{24,8},{1,17},{9,25},{17,1},{25,9},{2,18},{10... | collective-permute-start | bytes 2359304 | tf_op jit(solution)/shard_map/ppermute | solution.py:610
  76.5 1.2 %collective-permute-start.18 = (f32[96,128]{1,0:T(8,128)S(1)}, f32[96,128]{1,0:T(8,128)S(1)}, u32[]{:S(2)}, u32[]{:S(2)}) collective-permute-start(f32[96,128]{1,0:T(8,128)S(1)} %add.19.mine), channel_id=1, source_target_pairs={{0,8},{8,0},{16,24},{24,16},{1,9},{9,1},{17,25},{25,17},{2,10},{10... | collective-permute-start | bytes 147464 | tf_op jit(solution)/shard_map/ppermute | solution.py:610
  76.5 25.8 %collective-permute-start.23 = (f32[8,4,24,256]{3,2,1,0:T(8,128)S(1)}, f32[8,4,24,256]{3,2,1,0:T(8,128)S(1)}, u32[]{:S(2)}, u32[]{:S(2)}) collective-permute-start(f32[8,4,24,256]{3,2,1,0:T(8,128)S(1)} %get-tuple-element.55.refs_8_), channel_id=1, source_target_pairs={{0,8},{8,0},{16,24},{24,16},{1,9},{9,1},{17,25},{25,17},{2,10},{10... | collective-permute-start | bytes 2359304 | tf_op jit(solution)/shard_map/ppermute | solution.py:610
  77.0 25.3 %collective-permute-start.19 = (f32[8,4,24,256]{3,2,1,0:T(8,128)S(1)}, f32[8,4,24,256]{3,2,1,0:T(8,128)S(1)}, u32[]{:S(2)}, u32[]{:S(2)}) collective-permute-start(f32[8,4,24,256]{3,2,1,0:T(8,128)S(1)} %last_free.1.refs_0_), channel_id=1, source_target_pairs={{0,8},{8,0},{16,24},{24,16},{1,9},{9,1},{17,25},{25,17},{2,10},{10... | collective-permute-start | bytes 2359304 | tf_op jit(solution)/shard_map/ppermute | solution.py:610
  77.0 25.3 %collective-permute-start.22 = (f32[8,4,24,256]{3,2,1,0:T(8,128)S(1)}, f32[8,4,24,256]{3,2,1,0:T(8,128)S(1)}, u32[]{:S(2)}, u32[]{:S(2)}) collective-permute-start(f32[8,4,24,256]{3,2,1,0:T(8,128)S(1)} %collective-permute-done.5.refs_14_.refs_6_), channel_id=1, source_target_pairs={{0,8},{8,0},{16,24},{24,16},{1,9},{9,1},{17,25},{25,17},{2,10},{10... | collective-permute-start | bytes 2359304 | tf_op jit(solution)/shard_map/ppermute | solution.py:610
  77.7 24.6 %collective-permute-start.24 = (f32[8,4,24,256]{3,2,1,0:T(8,128)S(1)}, f32[8,4,24,256]{3,2,1,0:T(8,128)S(1)}, u32[]{:S(2)}, u32[]{:S(2)}) collective-permute-start(f32[8,4,24,256]{3,2,1,0:T(8,128)S(1)} %collective-permute-done.17.refs_10_), channel_id=1, source_target_pairs={{0,8},{8,0},{16,24},{24,16},{1,9},{9,1},{17,25},{25,17},{2,10},{10... | collective-permute-start | bytes 2359304 | tf_op jit(solution)/shard_map/ppermute | solution.py:610
  95.8 6.5 %collective-permute-start.21 = (f32[8,4,24,256]{3,2,1,0:T(8,128)S(1)}, f32[8,4,24,256]{3,2,1,0:T(8,128)S(1)}, u32[]{:S(2)}, u32[]{:S(2)}) collective-permute-start(f32[8,4,24,256]{3,2,1,0:T(8,128)S(1)} %collective-permute-done.20.refs_2_), channel_id=1, source_target_pairs={{0,8},{8,0},{16,24},{24,16},{1,9},{9,1},{17,25},{25,17},{2,10},{10... | collective-permute-start | bytes 2359304 | tf_op jit(solution)/shard_map/ppermute | solution.py:610

commit v14 on v13

--- a/solution.py
+++ b/solution.py
@@ -717,18 +717,20 @@
     conserved = complete(conserved, tracer_ends[0])
     begun = gram(owner, omega, eta, None, tracer, offsets, (1, 1))
     tracer_ends = complete(tracer_ends, begun)
+    internal = collect(internal, across(tracer_ends), begun)
     (free,) = forecast_call(
         last_free_kernel,
         "last_free",
         [before, free, free_ends, add, add_ends, *around, *origin, diffusivity],
         [whole],
         cells,
-    )
-    internal = collect(internal, across(tracer_ends), begun)
+        ready=[*conserved[3:], *internal[1:2]] if blocks > 1 else (),
+    )
     half = gram(owner, omega, eta, begun, tracer_ends, offsets, (0, nx - 1))
-    half = tie(total_over(half, "space"), across(internal))
+    half = total_over(half, "space")
+    other = swap(half, "member", 1)
+    half = tie(half, other, across(internal))
     free = collect(free, half)
-    other = swap(half, "member", 1)
     internal = complete(internal, half)
     square = (members, LANES)
     total, extended = transform_call(

time: 110 us -> 109 us (level); the launches traced: 108 us -> 109 us
  Pallas kernels: 38 us -> 41.2 us
  starting transfers between devices: 34.9 us -> 33.4 us
    pallas_call x2, Pallas kernels: 1.43 us -> 4.5 us  [gram(): pl.pallas_call(functools.partial(gram_kernel, offsets=offsets, planes=pla...]
    ppermute x19, starting transfers between devices: 17.3 us -> 15.5 us  [swap(): return lax.ppermute(x, axis, [(k, k ^ bit) for k in range(count)])]
  transfers between devices with their start and end apart: 25 -> 25, of which waited for: 12 -> 13; matrix products, arithmetic and copies ran while one was open for 4% -> 4% of each run, Pallas kernels for 28% -> 30%
where the time goes in v14:
time: 109 us
  Pallas kernels  41.2 us (38%)
  starting transfers between devices  33.4 us (31%)
  waiting for transfers between devices  27.7 us (25%)
  local copies, waits for them, and re-layouts  4.89 us (4%)
  other arithmetic  1.29 us (1%)
    pallas_call x2, Pallas kernels, transform_call(): pl.pallas_call(kernel, out_shape=[jax.ShapeDtypeStruct(shape, f32) for sh...  24 us
    ppermute x19, starting transfers between devices, swap(): return lax.ppermute(x, axis, [(k, k ^ bit) for k in range(count)])  15.5 us
    ppermute x3, starting transfers between devices, halos(): lax.ppermute(last, 'space', forward)  13.8 us
    ppermute x19, waiting for transfers between devices, swap(): return lax.ppermute(x, axis, [(k, k ^ bit) for k in range(count)])  12.9 us
    ppermute x3, waiting for transfers between devices, halos(): lax.ppermute(first, 'space', backward)  10.7 us
    pallas_call x6, Pallas kernels, forecast_call(): pl.pallas_call(body, out_shape=[jax.ShapeDtypeStruct(shape, f32) for shap...  6.02 us
    pallas_call x1, Pallas kernels, mix(): pl.pallas_call(functools.partial(mix_kernel, blocks=blocks), grid=(nx,),...  5.26 us
    pallas_call x2, Pallas kernels, gram(): pl.pallas_call(functools.partial(gram_kernel, offsets=offsets, planes=pla...  4.5 us
  transfers between devices with their start and end apart: 25, of which 13 were waited for; matrix products, arithmetic and copies ran while one was open for 4% of the time, Pallas kernels for 30%

profile of v14, /device:TPU:0, one launch (start us, length us, event | category | flops | bytes accessed | tf_op | source)
XLA Modules:
  0.0 108.8 jit_solution(16017281694307139903)
XLA Ops:
  0.0 1.6 %fusion = (f32[24,3,2,4,256]{4,3,2,1,0:T(4,128)S(1)}, f32[24,3,2,4,256]{4,3,2,1,0:T(4,128)S(1)}) fusion(f32[24,4,8,4,256]{4,3,2,1,0:T(4,128)} %param.8), kind=kLoop, calls=%fused_computation.7 | loop fusion | bytes 2359296 | tf_op jit(solution)/shard_map/slice | solution.py:668
  1.6 0.4 copy_bitcast_fusion.4
  2.0 0.2 first_edges.1
  2.2 4.9 %collective-permute-start = (f32[4,56,256]{2,1,0:T(8,128)S(1)}, f32[4,56,256]{2,1,0:T(8,128)S(1)}, u32[]{:S(2)}, u32[]{:S(2)}) collective-permute-start(f32[4,56,256]{2,1,0:T(8,128)S(1)} %get-tuple-element.38), channel_id=1, source_target_pairs={{0,1},{1,2},{2,3},{3,4},{4,5},{5,6},{6,7},{8,9},{9,10},{10,11},{11... | collective-permute-start | bytes 688136 | tf_op jit(solution)/shard_map/ppermute | solution.py:633
  7.1 1.3 %collective-permute-start.1 = (f32[4,56,256]{2,1,0:T(8,128)S(1)}, f32[4,56,256]{2,1,0:T(8,128)S(1)}, u32[]{:S(2)}, u32[]{:S(2)}) collective-permute-start(f32[4,56,256]{2,1,0:T(8,128)S(1)} %get-tuple-element.39), channel_id=1, source_target_pairs={{1,0},{2,1},{3,2},{4,3},{5,4},{6,5},{7,6},{9,8},{10,9},{11,10},{12... | collective-permute-start | bytes 688136 | tf_op jit(solution)/shard_map/ppermute | solution.py:633
  8.4 1.0 fusion.1
  9.5 1.3 %add_add_fusion.refs_4_ = f32[8,4,24,256]{3,2,1,0:T(8,128)S(1)} fusion(f32[24,1,8,4,256]{4,3,2,1,0:T(4,128)S(1)} %get-tuple-element.71, f32[24,1,8,4,256]{4,3,2,1,0:T(4,128)S(1)} %get-tuple-element.70, f32[24,1,8,4,256]{4,3,2,1,0:T(4,128)S(1)} %get-tuple-element.69), kind=kLoop, calls=%fused_computation.4 | loop fusion | flops 393216 | bytes 3145728 | tf_op jit(solution)/shard_map/add | solution.py:679
  10.7 0.1 collective-permute-start.4
  10.8 1.6 %collective-permute-start.5 = (f32[8,4,24,256]{3,2,1,0:T(8,128)S(1)}, f32[8,4,24,256]{3,2,1,0:T(8,128)S(1)}, u32[]{:S(2)}, u32[]{:S(2)}) collective-permute-start(f32[8,4,24,256]{3,2,1,0:T(8,128)S(1)} %add_add_fusion.refs_4_), channel_id=1, source_target_pairs={{0,16},{8,24},{16,0},{24,8},{1,17},{9,25},{17,1},{25,9},{2,18},{10... | collective-permute-start | bytes 2359304 | tf_op jit(solution)/shard_map/ppermute | solution.py:610
  12.4 0.9 copy_bitcast_fusion
  13.3 0.0 copy-start.3
  13.3 0.0 copy-start.4
  13.4 0.0 copy-start.5
  13.4 0.0 copy-start.6
  13.4 0.9 copy_bitcast_fusion.2
  14.3 2.6 %collective-permute-done.refs_4_.refs_6_.refs_7_ = f32[4,56,256]{2,1,0:T(8,128)S(1)} collective-permute-done((f32[4,56,256]{2,1,0:T(8,128)S(1)}, f32[4,56,256]{2,1,0:T(8,128)S(1)}, u32[]{:S(2)}, u32[]{:S(2)}) %collective-permute-start) | collective-permute-done | bytes 229408 | tf_op jit(solution)/shard_map/ppermute | solution.py:633
  16.9 0.0 collective-permute-done.1.refs_5_.refs_7_.refs_8_
  16.9 1.0 next_edges.1
  17.8 4.4 %collective-permute-start.2 = (f32[4,48,256]{2,1,0:T(8,128)S(1)}, f32[4,48,256]{2,1,0:T(8,128)S(1)}, u32[]{:S(2)}, u32[]{:S(2)}) collective-permute-start(f32[4,48,256]{2,1,0:T(8,128)S(1)} %get-tuple-element.44), channel_id=1, source_target_pairs={{0,1},{1,2},{2,3},{3,4},{4,5},{5,6},{6,7},{8,9},{9,10},{10,11},{11... | collective-permute-start | bytes 589832 | tf_op jit(solution)/shard_map/ppermute | solution.py:633
  22.2 1.3 %collective-permute-start.3 = (f32[4,48,256]{2,1,0:T(8,128)S(1)}, f32[4,48,256]{2,1,0:T(8,128)S(1)}, u32[]{:S(2)}, u32[]{:S(2)}) collective-permute-start(f32[4,48,256]{2,1,0:T(8,128)S(1)} %get-tuple-element.45), channel_id=1, source_target_pairs={{1,0},{2,1},{3,2},{4,3},{5,4},{6,5},{7,6},{9,8},{10,9},{11,10},{12... | collective-permute-start | bytes 589832 | tf_op jit(solution)/shard_map/ppermute | solution.py:633
  23.6 1.4 %voxel_weights.1 = (f32[2,32,256]{2,1,0:T(8,128)S(1)}, f32[2,32,256]{2,1,0:T(8,128)S(1)}) custom-call(s32[4]{0:T(128)S(1)} %copy-done.6, s32[4,2048]{1,0:T(4,128)S(1)} %copy-done.3, f32[4,2048]{1,0:T(4,128)S(1)} %copy-done.4, f32[4,2048]{1,0:T(4,128)S(1)} %copy-done.5), custom_call_target="tpu_custom_call" | custom-call | tf_op jit(solution)/shard_map/voxel_weights/pallas_call | solution.py:374
  25.0 1.5 %two_substeps.1 = (f32[8,4,24,256]{3,2,1,0:T(8,128)S(1)}, f32[8,4,24,256]{3,2,1,0:T(8,128)S(1)}, f32[8,4,24,256]{3,2,1,0:T(8,128)S(1)}, f32[8,4,24,256]{3,2,1,0:T(8,128)S(1)}) custom-call(f32[8,4,24,256]{3,2,1,0:T(8,128)S(1)} %get-tuple-element.76.refs_0_, f32[8,4,24,256]{3,2,1,0:T(8,128)S(1)} %get-tuple-element.75.refs_1_, ...), custom_call_target="tpu_custom_call" | custom-call | flops 11796480 | bytes 12582912 | tf_op jit(solution)/shard_map/two_substeps/pallas_call | solution.py:323
  26.5 0.0 collective-permute-done.2.refs_4_
  26.5 4.8 %collective-permute-done.3.refs_5_ = f32[4,48,256]{2,1,0:T(8,128)S(1)} collective-permute-done((f32[4,48,256]{2,1,0:T(8,128)S(1)}, f32[4,48,256]{2,1,0:T(8,128)S(1)}, u32[]{:S(2)}, u32[]{:S(2)}) %collective-permute-start.3) | collective-permute-done | bytes 196640 | tf_op jit(solution)/shard_map/ppermute | solution.py:633
  31.4 2.7 %last_steps.1 = (f32[8,4,24,256]{3,2,1,0:T(8,128)S(1)}, f32[4,48,256]{2,1,0:T(8,128)S(1)}, f32[4,48,256]{2,1,0:T(8,128)S(1)}, f32[8,4,24,256]{3,2,1,0:T(8,128)S(...) custom-call(f32[8,4,24,256]{3,2,1,0:T(8,128)S(1)} %get-tuple-element, ...), custom_call_target="tpu_custom_call" | custom-call | flops 23592960 | bytes 25165824 | tf_op jit(solution)/shard_map/last_steps/pallas_call | solution.py:323
  34.1 1.6 %collective-permute-start.7 = (f32[6,4,24,256]{3,2,1,0:T(8,128)S(1)}, f32[6,4,24,256]{3,2,1,0:T(8,128)S(1)}, u32[]{:S(2)}, u32[]{:S(2)}) collective-permute-start(f32[6,4,24,256]{3,2,1,0:T(8,128)S(1)} %get-tuple-element.46.refs_0_.refs_12_), channel_id=1, source_target_pairs={{0,16},{8,24},{16,0},{24,8},{1,17},{9,25},{17,1},{25,9},{2,18},{10... | collective-permute-start | bytes 1769480 | tf_op jit(solution)/shard_map/ppermute | solution.py:610
  35.7 4.5 %collective-permute-start.8 = (f32[4,48,256]{2,1,0:T(8,128)S(1)}, f32[4,48,256]{2,1,0:T(8,128)S(1)}, u32[]{:S(2)}, u32[]{:S(2)}) collective-permute-start(f32[4,48,256]{2,1,0:T(8,128)S(1)} %get-tuple-element.49), channel_id=1, source_target_pairs={{0,1},{1,2},{2,3},{3,4},{4,5},{5,6},{6,7},{8,9},{9,10},{10,11},{11... | collective-permute-start | bytes 589832 | tf_op jit(solution)/shard_map/ppermute | solution.py:633
  40.2 1.5 %collective-permute-start.9 = (f32[4,48,256]{2,1,0:T(8,128)S(1)}, f32[4,48,256]{2,1,0:T(8,128)S(1)}, u32[]{:S(2)}, u32[]{:S(2)}) collective-permute-start(f32[4,48,256]{2,1,0:T(8,128)S(1)} %get-tuple-element.50), channel_id=1, source_target_pairs={{1,0},{2,1},{3,2},{4,3},{5,4},{6,5},{7,6},{9,8},{10,9},{11,10},{12... | collective-permute-start | bytes 589832 | tf_op jit(solution)/shard_map/ppermute | solution.py:633
  41.7 0.1 collective-permute-start.6
  41.8 1.6 %collective-permute-done.8.refs_2_.refs_5_ = f32[4,48,256]{2,1,0:T(8,128)S(1)} collective-permute-done((f32[4,48,256]{2,1,0:T(8,128)S(1)}, f32[4,48,256]{2,1,0:T(8,128)S(1)}, u32[]{:S(2)}, u32[]{:S(2)}) %collective-permute-start.8) | collective-permute-done | bytes 196640 | tf_op jit(solution)/shard_map/ppermute | solution.py:633
  43.4 5.8 %collective-permute-done.9.refs_3_.refs_6_ = f32[4,48,256]{2,1,0:T(8,128)S(1)} collective-permute-done((f32[4,48,256]{2,1,0:T(8,128)S(1)}, f32[4,48,256]{2,1,0:T(8,128)S(1)}, u32[]{:S(2)}, u32[]{:S(2)}) %collective-permute-start.9) | collective-permute-done | bytes 196640 | tf_op jit(solution)/shard_map/ppermute | solution.py:633
  49.2 0.1 last_ends.1
  49.3 0.0 collective-permute-done.7.refs_2_.refs_14_
  49.3 0.1 collective-permute-start.10
  49.4 0.7 collective-permute-start.12
  50.1 0.2 collective-permute-start.20
  50.3 0.3 collective-permute-start.19
  50.6 0.8 collective-permute-done.10.refs_3_.refs_15_
  51.4 3.0 %gram.2.refs_0_ = f32[2,96,128]{2,1,0:T(8,128)S(1)} custom-call(s32[4]{0:T(128)S(1)} %copy-done.6, f32[2,32,256]{2,1,0:T(8,128)S(1)} %get-tuple-element.36.refs_11_.omega, f32[2,32,256]{2,1,0:T(8,128)S(1)} %get-tuple-element.37.refs_12_.eta, f32[6,4,24,256]{3,2,1,0:T(8,128)S(1)} %get-tuple-element.46.refs_0_.refs_12_, ...), custom_call_target="tpu_custom_call" | custom-call | tf_op jit(solution)/shard_map/gram/pallas_call | solution.py:438
  54.4 2.3 %collective-permute-done.12.refs_3_.refs_18_ = f32[2,4,24,256]{3,2,1,0:T(8,128)S(1)} collective-permute-done((f32[2,4,24,256]{3,2,1,0:T(8,128)S(1)}, f32[2,4,24,256]{3,2,1,0:T(8,128)S(1)}, u32[]{:S(2)}, u32[]{:S(2)}) %collective-permute-start.12) | collective-permute-done | bytes 196640 | tf_op jit(solution)/shard_map/ppermute | solution.py:610
  56.7 0.7 collective-permute-start.18
  57.4 0.5 collective-permute-start.13
  57.9 0.9 collective-permute-done.11.refs_2_.refs_17_
  58.8 0.3 collective-permute-done.13.refs_4_.refs_19_
  59.1 1.5 %gram.3 = f32[96,128]{1,0:T(8,128)S(1)} custom-call(s32[4]{0:T(128)S(1)} %copy-done.6, f32[2,32,256]{2,1,0:T(8,128)S(1)} %get-tuple-element.36.refs_11_.omega, f32[2,32,256]{2,1,0:T(8,128)S(1)} %get-tuple-element.37.refs_12_.eta, f32[2,96,128]{2,1,0:T(8,128)S(1)} %gram.2.refs_0_, f32[2,4,24,256]{3,2,1,0:T(8,128)S(1)} %get-tuple-element.51.refs_1_.refs_16_, ...), custom_call_target="tpu_custom_call" | custom-call | tf_op jit(solution)/shard_map/gram/pallas_call | solution.py:438
  60.6 1.8 %collective-permute-start.14 = (f32[96,128]{1,0:T(8,128)S(1)}, f32[96,128]{1,0:T(8,128)S(1)}, u32[]{:S(2)}, u32[]{:S(2)}) collective-permute-start(f32[96,128]{1,0:T(8,128)S(1)} %gram.3), channel_id=1, source_target_pairs={{0,1},{1,0},{2,3},{3,2},{4,5},{5,4},{6,7},{7,6},{8,9},{9,8},{10,11... | collective-permute-start | bytes 147464 | tf_op jit(solution)/shard_map/ppermute | solution.py:610
  62.4 2.4 %collective-permute-done.14 = f32[96,128]{1,0:T(8,128)S(1)} collective-permute-done((f32[96,128]{1,0:T(8,128)S(1)}, f32[96,128]{1,0:T(8,128)S(1)}, u32[]{:S(2)}, u32[]{:S(2)}) %collective-permute-start.14) | collective-permute-done | bytes 49184 | tf_op jit(solution)/shard_map/ppermute | solution.py:610
  64.8 4.3 %collective-permute-start.15 = (f32[96,128]{1,0:T(8,128)S(1)}, f32[96,128]{1,0:T(8,128)S(1)}, u32[]{:S(2)}, u32[]{:S(2)}) collective-permute-start(f32[96,128]{1,0:T(8,128)S(1)} %add.17), channel_id=1, source_target_pairs={{0,2},{1,3},{2,0},{3,1},{4,6},{5,7},{6,4},{7,5},{8,10},{9,11},{10,... | collective-permute-start | bytes 147464 | tf_op jit(solution)/shard_map/ppermute | solution.py:610
  69.1 2.1 %collective-permute-done.15 = f32[96,128]{1,0:T(8,128)S(1)} collective-permute-done((f32[96,128]{1,0:T(8,128)S(1)}, f32[96,128]{1,0:T(8,128)S(1)}, u32[]{:S(2)}, u32[]{:S(2)}) %collective-permute-start.15) | collective-permute-done | bytes 49184 | tf_op jit(solution)/shard_map/ppermute | solution.py:610
  71.2 2.6 %collective-permute-start.16 = (f32[96,128]{1,0:T(8,128)S(1)}, f32[96,128]{1,0:T(8,128)S(1)}, u32[]{:S(2)}, u32[]{:S(2)}) collective-permute-start(f32[96,128]{1,0:T(8,128)S(1)} %add.18), channel_id=1, source_target_pairs={{0,4},{1,5},{2,6},{3,7},{4,0},{5,1},{6,2},{7,3},{8,12},{9,13},{10,... | collective-permute-start | bytes 147464 | tf_op jit(solution)/shard_map/ppermute | solution.py:610
  73.8 2.8 %collective-permute-done.16 = f32[96,128]{1,0:T(8,128)S(1)} collective-permute-done((f32[96,128]{1,0:T(8,128)S(1)}, f32[96,128]{1,0:T(8,128)S(1)}, u32[]{:S(2)}, u32[]{:S(2)}) %collective-permute-start.16) | collective-permute-done | bytes 49184 | tf_op jit(solution)/shard_map/ppermute | solution.py:610
  76.6 0.1 collective-permute-start.17
  76.6 0.0 collective-permute-done.20.refs_11_.refs_9_
  76.7 0.5 last_free.1.refs_0_
  77.2 0.7 collective-permute-done.17.other
  77.9 0.0 collective-permute-done.18.refs_10_
  77.9 0.5 collective-permute-start.22
  78.4 0.5 collective-permute-start.24
  78.9 17.9 %transforms_early.1 = (f32[96,128]{1,0:T(8,128)S(1)}, f32[96,128]{1,0:T(8,128)S(1)}) custom-call(f32[96,128]{1,0:T(8,128)S(1)} %add.19.mine, f32[96,128]{1,0:T(8,128)S(1)} %collective-permute-done.17.other), custom_call_target="tpu_custom_call" | custom-call | flops 100000000 | bytes 1000000 | tf_op jit(solution)/shard_map/transforms_early/pallas_call | solution.py:542
  96.8 0.7 collective-permute-done.22.refs_2_
  97.5 6.0 %transforms_late.1.weights = f32[24,128]{1,0:T(8,128)S(1)} custom-call(f32[96,128]{1,0:T(8,128)S(1)} %get-tuple-element.57.total, f32[96,128]{1,0:T(8,128)S(1)} %get-tuple-element.58.last), custom_call_target="tpu_custom_call" | custom-call | flops 100000000 | bytes 1000000 | tf_op jit(solution)/shard_map/transforms_late/pallas_call | solution.py:542
  103.5 0.0 collective-permute-done.24.refs_11_
  103.5 0.0 collective-permute-done.23.refs_3_
  103.5 5.3 %mix.1 = f32[24,4,8,4,256]{4,3,2,1,0:T(4,128)} custom-call(f32[24,128]{1,0:T(8,128)S(1)} %transforms_late.1.weights, f32[8,4,24,256]{3,2,1,0:T(8,128)S(1)} %last_free.1.refs_0_, f32[8,4,24,256]{3,2,1,0:T(8,128)S(1)} %collective-permute-done.21.refs_1_, f32[8,4,24,256]{3,2,1,0:T(8,128)S(1)} %collective-permute-done.22.refs_2_, ...), custom_call_target="tpu_custom_call" | custom-call | tf_op jit(solution)/shard_map/mix/pallas_call | solution.py:597
  (23 shorter events, 0.1 us)
Async XLA Ops:
  0.0 8.4 %copy-start.7 = (f32[24,4,8,4,256]{4,3,2,1,0:T(4,128)S(1)}, f32[24,4,8,4,256]{4,3,2,1,0:T(4,128)}, u32[]{:S(2)}) copy-start(f32[24,4,8,4,256]{4,3,2,1,0:T(4,128)} %param.8) | copy-start | bytes 9437188
  0.0 2.0 %copy-start = (f32[8,4,256]{2,1,0:T(4,128)S(1)}, f32[8,4,256]{2,1,0:T(4,128)}, u32[]{:S(2)}) copy-start(f32[8,4,256]{2,1,0:T(4,128)} %refs_9_.7) | copy-start | bytes 98308
  0.0 2.0 %copy-start.2 = (f32[8,4,256]{2,1,0:T(4,128)S(1)}, f32[8,4,256]{2,1,0:T(4,128)}, u32[]{:S(2)}) copy-start(f32[8,4,256]{2,1,0:T(4,128)} %refs_6_.1) | copy-start | bytes 98308
  0.0 2.0 %copy-start.1 = (f32[8,4,256]{2,1,0:T(4,128)S(1)}, f32[8,4,256]{2,1,0:T(4,128)}, u32[]{:S(2)}) copy-start(f32[8,4,256]{2,1,0:T(4,128)} %refs_5_.1) | copy-start | bytes 98308
  2.2 14.6 %collective-permute-start = (f32[4,56,256]{2,1,0:T(8,128)S(1)}, f32[4,56,256]{2,1,0:T(8,128)S(1)}, u32[]{:S(2)}, u32[]{:S(2)}) collective-permute-start(f32[4,56,256]{2,1,0:T(8,128)S(1)} %get-tuple-element.38), channel_id=1, source_target_pairs={{0,1},{1,2},{2,3},{3,4},{4,5},{5,6},{6,7},{8,9},{9,10},{10,11},{11... | collective-permute-start | bytes 688136 | tf_op jit(solution)/shard_map/ppermute | solution.py:633
  7.1 9.7 %collective-permute-start.1 = (f32[4,56,256]{2,1,0:T(8,128)S(1)}, f32[4,56,256]{2,1,0:T(8,128)S(1)}, u32[]{:S(2)}, u32[]{:S(2)}) collective-permute-start(f32[4,56,256]{2,1,0:T(8,128)S(1)} %get-tuple-element.39), channel_id=1, source_target_pairs={{1,0},{2,1},{3,2},{4,3},{5,4},{6,5},{7,6},{9,8},{10,9},{11,10},{12... | collective-permute-start | bytes 688136 | tf_op jit(solution)/shard_map/ppermute | solution.py:633
  10.7 20.6 %collective-permute-start.4 = (f32[8,4,24,256]{3,2,1,0:T(8,128)S(1)}, f32[8,4,24,256]{3,2,1,0:T(8,128)S(1)}, u32[]{:S(2)}, u32[]{:S(2)}) collective-permute-start(f32[8,4,24,256]{3,2,1,0:T(8,128)S(1)} %add_add_fusion.refs_4_), channel_id=1, source_target_pairs={{0,8},{8,0},{16,24},{24,16},{1,9},{9,1},{17,25},{25,17},{2,10},{10... | collective-permute-start | bytes 2359304 | tf_op jit(solution)/shard_map/ppermute | solution.py:610
  10.8 20.5 %collective-permute-start.5 = (f32[8,4,24,256]{3,2,1,0:T(8,128)S(1)}, f32[8,4,24,256]{3,2,1,0:T(8,128)S(1)}, u32[]{:S(2)}, u32[]{:S(2)}) collective-permute-start(f32[8,4,24,256]{3,2,1,0:T(8,128)S(1)} %add_add_fusion.refs_4_), channel_id=1, source_target_pairs={{0,16},{8,24},{16,0},{24,8},{1,17},{9,25},{17,1},{25,9},{2,18},{10... | collective-permute-start | bytes 2359304 | tf_op jit(solution)/shard_map/ppermute | solution.py:610
  13.3 10.2 %copy-start.3 = (s32[4,2048]{1,0:T(4,128)S(1)}, s32[4,2048]{1,0:T(4,128)}, u32[]{:S(2)}) copy-start(s32[4,2048]{1,0:T(4,128)} %obs_index.1) | copy-start | bytes 98308
  13.3 10.2 %copy-start.4 = (f32[4,2048]{1,0:T(4,128)S(1)}, f32[4,2048]{1,0:T(4,128)}, u32[]{:S(2)}) copy-start(f32[4,2048]{1,0:T(4,128)} %observed.1) | copy-start | bytes 98308
  13.4 10.2 %copy-start.5 = (f32[4,2048]{1,0:T(4,128)S(1)}, f32[4,2048]{1,0:T(4,128)}, u32[]{:S(2)}) copy-start(f32[4,2048]{1,0:T(4,128)} %obs_var.1) | copy-start | bytes 98308
  13.4 10.2 %copy-start.6 = (s32[4]{0:T(128)S(1)}, s32[4]{0:T(128)}, u32[]{:S(2)}) copy-start(s32[4]{0:T(128)} %owner.5) | copy-start | bytes 52
  17.8 8.7 %collective-permute-start.2 = (f32[4,48,256]{2,1,0:T(8,128)S(1)}, f32[4,48,256]{2,1,0:T(8,128)S(1)}, u32[]{:S(2)}, u32[]{:S(2)}) collective-permute-start(f32[4,48,256]{2,1,0:T(8,128)S(1)} %get-tuple-element.44), channel_id=1, source_target_pairs={{0,1},{1,2},{2,3},{3,4},{4,5},{5,6},{6,7},{8,9},{9,10},{10,11},{11... | collective-permute-start | bytes 589832 | tf_op jit(solution)/shard_map/ppermute | solution.py:633
  22.2 9.1 %collective-permute-start.3 = (f32[4,48,256]{2,1,0:T(8,128)S(1)}, f32[4,48,256]{2,1,0:T(8,128)S(1)}, u32[]{:S(2)}, u32[]{:S(2)}) collective-permute-start(f32[4,48,256]{2,1,0:T(8,128)S(1)} %get-tuple-element.45), channel_id=1, source_target_pairs={{1,0},{2,1},{3,2},{4,3},{5,4},{6,5},{7,6},{9,8},{10,9},{11,10},{12... | collective-permute-start | bytes 589832 | tf_op jit(solution)/shard_map/ppermute | solution.py:633
  34.1 15.2 %collective-permute-start.7 = (f32[6,4,24,256]{3,2,1,0:T(8,128)S(1)}, f32[6,4,24,256]{3,2,1,0:T(8,128)S(1)}, u32[]{:S(2)}, u32[]{:S(2)}) collective-permute-start(f32[6,4,24,256]{3,2,1,0:T(8,128)S(1)} %get-tuple-element.46.refs_0_.refs_12_), channel_id=1, source_target_pairs={{0,16},{8,24},{16,0},{24,8},{1,17},{9,25},{17,1},{25,9},{2,18},{10... | collective-permute-start | bytes 1769480 | tf_op jit(solution)/shard_map/ppermute | solution.py:610
  35.7 7.7 %collective-permute-start.8 = (f32[4,48,256]{2,1,0:T(8,128)S(1)}, f32[4,48,256]{2,1,0:T(8,128)S(1)}, u32[]{:S(2)}, u32[]{:S(2)}) collective-permute-start(f32[4,48,256]{2,1,0:T(8,128)S(1)} %get-tuple-element.49), channel_id=1, source_target_pairs={{0,1},{1,2},{2,3},{3,4},{4,5},{5,6},{6,7},{8,9},{9,10},{10,11},{11... | collective-permute-start | bytes 589832 | tf_op jit(solution)/shard_map/ppermute | solution.py:633
  40.2 9.0 %collective-permute-start.9 = (f32[4,48,256]{2,1,0:T(8,128)S(1)}, f32[4,48,256]{2,1,0:T(8,128)S(1)}, u32[]{:S(2)}, u32[]{:S(2)}) collective-permute-start(f32[4,48,256]{2,1,0:T(8,128)S(1)} %get-tuple-element.50), channel_id=1, source_target_pairs={{1,0},{2,1},{3,2},{4,3},{5,4},{6,5},{7,6},{9,8},{10,9},{11,10},{12... | collective-permute-start | bytes 589832 | tf_op jit(solution)/shard_map/ppermute | solution.py:633
  41.7 8.9 %collective-permute-start.6 = (f32[6,4,24,256]{3,2,1,0:T(8,128)S(1)}, f32[6,4,24,256]{3,2,1,0:T(8,128)S(1)}, u32[]{:S(2)}, u32[]{:S(2)}) collective-permute-start(f32[6,4,24,256]{3,2,1,0:T(8,128)S(1)} %get-tuple-element.46.refs_0_.refs_12_), channel_id=1, source_target_pairs={{0,8},{8,0},{16,24},{24,16},{1,9},{9,1},{17,25},{25,17},{2,10},{10... | collective-permute-start | bytes 1769480 | tf_op jit(solution)/shard_map/ppermute | solution.py:610
  49.3 2.1 %collective-permute-start.10 = (f32[6,4,24,256]{3,2,1,0:T(8,128)S(1)}, f32[6,4,24,256]{3,2,1,0:T(8,128)S(1)}, u32[]{:S(2)}, u32[]{:S(2)}) collective-permute-start(f32[6,4,24,256]{3,2,1,0:T(8,128)S(1)} %collective-permute-done.7.refs_2_.refs_14_), channel_id=1, source_target_pairs={{0,8},{8,0},{16,24},{24,16},{1,9},{9,1},{17,25},{25,17},{2,10},{10... | collective-permute-start | bytes 1769480 | tf_op jit(solution)/shard_map/ppermute | solution.py:610
  49.4 7.3 %collective-permute-start.12 = (f32[2,4,24,256]{3,2,1,0:T(8,128)S(1)}, f32[2,4,24,256]{3,2,1,0:T(8,128)S(1)}, u32[]{:S(2)}, u32[]{:S(2)}) collective-permute-start(f32[2,4,24,256]{3,2,1,0:T(8,128)S(1)} %get-tuple-element.51.refs_1_.refs_16_), channel_id=1, source_target_pairs={{0,16},{8,24},{16,0},{24,8},{1,17},{9,25},{17,1},{25,9},{2,18},{10... | collective-permute-start | bytes 589832 | tf_op jit(solution)/shard_map/ppermute | solution.py:610
  50.1 26.6 %collective-permute-start.20 = (f32[8,4,24,256]{3,2,1,0:T(8,128)S(1)}, f32[8,4,24,256]{3,2,1,0:T(8,128)S(1)}, u32[]{:S(2)}, u32[]{:S(2)}) collective-permute-start(f32[8,4,24,256]{3,2,1,0:T(8,128)S(1)} %get-tuple-element.55.refs_8_), channel_id=1, source_target_pairs={{0,8},{8,0},{16,24},{24,16},{1,9},{9,1},{17,25},{25,17},{2,10},{10... | collective-permute-start | bytes 2359304 | tf_op jit(solution)/shard_map/ppermute | solution.py:610
  50.3 26.3 %collective-permute-start.19 = (f32[8,4,24,256]{3,2,1,0:T(8,128)S(1)}, f32[8,4,24,256]{3,2,1,0:T(8,128)S(1)}, u32[]{:S(2)}, u32[]{:S(2)}) collective-permute-start(f32[8,4,24,256]{3,2,1,0:T(8,128)S(1)} %collective-permute-done.5.refs_14_.refs_6_), channel_id=1, source_target_pairs={{0,8},{8,0},{16,24},{24,16},{1,9},{9,1},{17,25},{25,17},{2,10},{10... | collective-permute-start | bytes 2359304 | tf_op jit(solution)/shard_map/ppermute | solution.py:610
  56.7 21.1 %collective-permute-start.18 = (f32[8,4,24,256]{3,2,1,0:T(8,128)S(1)}, f32[8,4,24,256]{3,2,1,0:T(8,128)S(1)}, u32[]{:S(2)}, u32[]{:S(2)}) collective-permute-start(f32[8,4,24,256]{3,2,1,0:T(8,128)S(1)} %get-tuple-element.55.refs_8_), channel_id=1, source_target_pairs={{0,16},{8,24},{16,0},{24,8},{1,17},{9,25},{17,1},{25,9},{2,18},{10... | collective-permute-start | bytes 2359304 | tf_op jit(solution)/shard_map/ppermute | solution.py:610
  57.4 1.4 %collective-permute-start.11 = (f32[2,4,24,256]{3,2,1,0:T(8,128)S(1)}, f32[2,4,24,256]{3,2,1,0:T(8,128)S(1)}, u32[]{:S(2)}, u32[]{:S(2)}) collective-permute-start(f32[2,4,24,256]{3,2,1,0:T(8,128)S(1)} %get-tuple-element.51.refs_1_.refs_16_), channel_id=1, source_target_pairs={{0,8},{8,0},{16,24},{24,16},{1,9},{9,1},{17,25},{25,17},{2,10},{10... | collective-permute-start | bytes 589832 | tf_op jit(solution)/shard_map/ppermute | solution.py:610
  57.4 1.7 %collective-permute-start.13 = (f32[2,4,24,256]{3,2,1,0:T(8,128)S(1)}, f32[2,4,24,256]{3,2,1,0:T(8,128)S(1)}, u32[]{:S(2)}, u32[]{:S(2)}) collective-permute-start(f32[2,4,24,256]{3,2,1,0:T(8,128)S(1)} %collective-permute-done.12.refs_3_.refs_18_), channel_id=1, source_target_pairs={{0,8},{8,0},{16,24},{24,16},{1,9},{9,1},{17,25},{25,17},{2,10},{10... | collective-permute-start | bytes 589832 | tf_op jit(solution)/shard_map/ppermute | solution.py:610
  60.6 4.2 %collective-permute-start.14 = (f32[96,128]{1,0:T(8,128)S(1)}, f32[96,128]{1,0:T(8,128)S(1)}, u32[]{:S(2)}, u32[]{:S(2)}) collective-permute-start(f32[96,128]{1,0:T(8,128)S(1)} %gram.3), channel_id=1, source_target_pairs={{0,1},{1,0},{2,3},{3,2},{4,5},{5,4},{6,7},{7,6},{8,9},{9,8},{10,11... | collective-permute-start | bytes 147464 | tf_op jit(solution)/shard_map/ppermute | solution.py:610
  64.8 6.4 %collective-permute-start.15 = (f32[96,128]{1,0:T(8,128)S(1)}, f32[96,128]{1,0:T(8,128)S(1)}, u32[]{:S(2)}, u32[]{:S(2)}) collective-permute-start(f32[96,128]{1,0:T(8,128)S(1)} %add.17), channel_id=1, source_target_pairs={{0,2},{1,3},{2,0},{3,1},{4,6},{5,7},{6,4},{7,5},{8,10},{9,11},{10,... | collective-permute-start | bytes 147464 | tf_op jit(solution)/shard_map/ppermute | solution.py:610
  71.2 5.4 %collective-permute-start.16 = (f32[96,128]{1,0:T(8,128)S(1)}, f32[96,128]{1,0:T(8,128)S(1)}, u32[]{:S(2)}, u32[]{:S(2)}) collective-permute-start(f32[96,128]{1,0:T(8,128)S(1)} %add.18), channel_id=1, source_target_pairs={{0,4},{1,5},{2,6},{3,7},{4,0},{5,1},{6,2},{7,3},{8,12},{9,13},{10,... | collective-permute-start | bytes 147464 | tf_op jit(solution)/shard_map/ppermute | solution.py:610
  76.6 1.3 %collective-permute-start.17 = (f32[96,128]{1,0:T(8,128)S(1)}, f32[96,128]{1,0:T(8,128)S(1)}, u32[]{:S(2)}, u32[]{:S(2)}) collective-permute-start(f32[96,128]{1,0:T(8,128)S(1)} %add.19.mine), channel_id=1, source_target_pairs={{0,8},{8,0},{16,24},{24,16},{1,9},{9,1},{17,25},{25,17},{2,10},{10... | collective-permute-start | bytes 147464 | tf_op jit(solution)/shard_map/ppermute | solution.py:610
  77.9 19.6 %collective-permute-start.22 = (f32[8,4,24,256]{3,2,1,0:T(8,128)S(1)}, f32[8,4,24,256]{3,2,1,0:T(8,128)S(1)}, u32[]{:S(2)}, u32[]{:S(2)}) collective-permute-start(f32[8,4,24,256]{3,2,1,0:T(8,128)S(1)} %last_free.1.refs_0_), channel_id=1, source_target_pairs={{0,16},{8,24},{16,0},{24,8},{1,17},{9,25},{17,1},{25,9},{2,18},{10... | collective-permute-start | bytes 2359304 | tf_op jit(solution)/shard_map/ppermute | solution.py:610
  78.4 25.1 %collective-permute-start.21 = (f32[8,4,24,256]{3,2,1,0:T(8,128)S(1)}, f32[8,4,24,256]{3,2,1,0:T(8,128)S(1)}, u32[]{:S(2)}, u32[]{:S(2)}) collective-permute-start(f32[8,4,24,256]{3,2,1,0:T(8,128)S(1)} %last_free.1.refs_0_), channel_id=1, source_target_pairs={{0,8},{8,0},{16,24},{24,16},{1,9},{9,1},{17,25},{25,17},{2,10},{10... | collective-permute-start | bytes 2359304 | tf_op jit(solution)/shard_map/ppermute | solution.py:610
  78.4 25.2 %collective-permute-start.24 = (f32[8,4,24,256]{3,2,1,0:T(8,128)S(1)}, f32[8,4,24,256]{3,2,1,0:T(8,128)S(1)}, u32[]{:S(2)}, u32[]{:S(2)}) collective-permute-start(f32[8,4,24,256]{3,2,1,0:T(8,128)S(1)} %collective-permute-done.18.refs_10_), channel_id=1, source_target_pairs={{0,8},{8,0},{16,24},{24,16},{1,9},{9,1},{17,25},{25,17},{2,10},{10... | collective-permute-start | bytes 2359304 | tf_op jit(solution)/shard_map/ppermute | solution.py:610
  97.5 6.1 %collective-permute-start.23 = (f32[8,4,24,256]{3,2,1,0:T(8,128)S(1)}, f32[8,4,24,256]{3,2,1,0:T(8,128)S(1)}, u32[]{:S(2)}, u32[]{:S(2)}) collective-permute-start(f32[8,4,24,256]{3,2,1,0:T(8,128)S(1)} %collective-permute-done.22.refs_2_), channel_id=1, source_target_pairs={{0,8},{8,0},{16,24},{24,16},{1,9},{9,1},{17,25},{25,17},{2,10},{10... | collective-permute-start | bytes 2359304 | tf_op jit(solution)/shard_map/ppermute | solution.py:610

commit v15 on v14

--- a/solution.py
+++ b/solution.py
@@ -556,7 +556,9 @@
 def mix_kernel(weights, *refs, blocks):
     *sources, out = refs
     rows, _, _, nz, _ = out.shape
-    x, nx = pl.program_id(0), pl.num_programs(0)
+    step, steps = pl.program_id(0), pl.num_programs(0)
+    planes = out.shape[2]
+    nx = steps * planes
     free, conserved, internal, tracer, tracer_ends = [
         sources[k : k + blocks] for k in range(0, len(sources), blocks)
     ]
@@ -572,33 +574,36 @@
         upper = mul(both, value_high)
         return upper[:rows] + (upper[rows:] + mul(high, value_low))
 
-    def plane(tracer, at):
+    def plane(tracer, at, x, k):
         for z in range(nz):
             bound = mixed(tracer, at, z)
             inside = mixed(internal, x, z)
-            out[:, 0, 0, z, :] = mixed(free, x, z)
-            out[:, 1, 0, z, :] = mixed(conserved, x, z) - bound
-            out[:, 2, 0, z, :] = bound - inside
-            out[:, 3, 0, z, :] = inside
-
-    at_end = (x == 0) | (x == nx - 1)
-
-    @pl.when(at_end)
-    def _():
-        plane(tracer_ends, x // (nx - 1))
-
-    @pl.when(jnp.logical_not(at_end))
-    def _():
-        plane(tracer, x - 1)
+            out[:, 0, k, z, :] = mixed(free, x, z)
+            out[:, 1, k, z, :] = mixed(conserved, x, z) - bound
+            out[:, 2, k, z, :] = bound - inside
+            out[:, 3, k, z, :] = inside
+
+    for k in range(planes):
+        x = step * planes + k
+        at_end = (x == 0) | (x == nx - 1)
+
+        @pl.when(at_end)
+        def _(x=x, k=k):
+            plane(tracer_ends, x // (nx - 1), x, k)
+
+        @pl.when(jnp.logical_not(at_end))
+        def _(x=x, k=k):
+            plane(tracer, x - 1, x, k)
 
 
 def mix(weights, sources, blocks, shape):
     rows, species, nx, nz, ny = shape
+    planes = 2 if nx % 2 == 0 else 1
     return pl.pallas_call(
         functools.partial(mix_kernel, blocks=blocks),
-        grid=(nx,),
+        grid=(nx // planes,),
         in_specs=[VMEM] * (1 + len(sources)),
-        out_specs=pl.BlockSpec((rows, species, 1, nz, ny), lambda x: (0, 0, x, 0, 0)),
+        out_specs=pl.BlockSpec((rows, species, planes, nz, ny), lambda x: (0, 0, x, 0, 0)),
         out_shape=jax.ShapeDtypeStruct(shape, f32),
         compiler_params=pltpu.CompilerParams(vmem_limit_bytes=SCOPED),
         name="mix",
@@ -610,9 +615,11 @@
     return lax.ppermute(x, axis, [(k, k ^ bit) for k in range(count)])
 
 
-def total_over(x, axis):
+def total_over(x, axis, before_last):
     bit = 1
     while bit < lax.axis_size(axis):
+        if 2 * bit >= lax.axis_size(axis):
+            x = lax.optimization_barrier((x, *before_last))[0]
         x = x + swap(x, axis, bit)
         bit *= 2
     return x
@@ -641,8 +648,11 @@
         def offsets(position, j):
             return jnp.bitwise_xor(position, j) * rows
 
+        def beside_core(x):
+            return [x, swap(x, "member", 1)]
+
         def collect(x, *after):
-            return [x, swap(x, "member", 1), swap(tie(x, *after), "member", 2)]
+            return [*beside_core(x), swap(tie(x, *after), "member", 2)]
 
         def complete(held, *after):
             return [*held, swap(lax.optimization_barrier((held[2], *after))[0], "member", 1)]
@@ -651,6 +661,9 @@
 
         def offsets(position, j):
             return 0
+
+        def beside_core(x):
+            return [x]
 
         def collect(x, *after):
             return [lax.all_gather(x, "member", axis=2, tiled=True)]
@@ -727,10 +740,11 @@
         ready=[*conserved[3:], *internal[1:2]] if blocks > 1 else (),
     )
     half = gram(owner, omega, eta, begun, tracer_ends, offsets, (0, nx - 1))
-    half = total_over(half, "space")
+    held = beside_core(free)
+    half = total_over(half, "space", held)
     other = swap(half, "member", 1)
     half = tie(half, other, across(internal))
-    free = collect(free, half)
+    free = [*held, swap(tie(free, half), "member", 2)] if blocks > 1 else collect(free)
     internal = complete(internal, half)
     square = (members, LANES)
     total, extended = transform_call(

time: 109 us -> 108 us (level)
  Pallas kernels: 41.2 us -> 37.3 us
  waiting for transfers between devices: 27.7 us -> 30.3 us
    pallas_call x2, Pallas kernels: 4.5 us -> 1.25 us  [gram(): pl.pallas_call(functools.partial(gram_kernel, offsets=offsets, planes=pla...]
    ppermute x19, waiting for transfers between devices: 12.9 us -> 15.5 us  [swap(): return lax.ppermute(x, axis, [(k, k ^ bit) for k in range(count)])]
  transfers between devices with their start and end apart: 25 -> 25, of which waited for: 13 -> 15; matrix products, arithmetic and copies ran while one was open for 4% -> 4% of each run, Pallas kernels for 30% -> 27%
where the time goes in v15:
time: 108 us
  Pallas kernels  37.3 us (35%)
  starting transfers between devices  34.1 us (32%)
  waiting for transfers between devices  30.3 us (28%)
  local copies, waits for them, and re-layouts  4.89 us (5%)
  other arithmetic  1.29 us (1%)
    pallas_call x2, Pallas kernels, transform_call(): pl.pallas_call(kernel, out_shape=[jax.ShapeDtypeStruct(shape, f32) for sh...  23.9 us
    ppermute x19, starting transfers between devices, swap(): return lax.ppermute(x, axis, [(k, k ^ bit) for k in range(count)])  16.2 us
    ppermute x19, waiting for transfers between devices, swap(): return lax.ppermute(x, axis, [(k, k ^ bit) for k in range(count)])  15.5 us
    ppermute x3, starting transfers between devices, halos(): lax.ppermute(last, 'space', forward)  13.8 us
    ppermute x3, waiting for transfers between devices, halos(): lax.ppermute(first, 'space', backward)  10.7 us
    pallas_call x6, Pallas kernels, forecast_call(): pl.pallas_call(body, out_shape=[jax.ShapeDtypeStruct(shape, f32) for shap...  6.01 us
    pallas_call x1, Pallas kernels, mix(): pl.pallas_call(functools.partial(mix_kernel, blocks=blocks), grid=(nx //...  4.63 us
    ppermute x3, waiting for transfers between devices, halos(): lax.ppermute(last, 'space', forward)  4.16 us
  transfers between devices with their start and end apart: 25, of which 15 were waited for; matrix products, arithmetic and copies ran while one was open for 4% of the time, Pallas kernels for 27%

profile of v15, /device:TPU:0, one launch (start us, length us, event | category | flops | bytes accessed | tf_op | source)
XLA Modules:
  0.0 108.2 jit_solution(14126765496953849594)
XLA Ops:
  0.0 1.6 %fusion = (f32[24,3,2,4,256]{4,3,2,1,0:T(4,128)S(1)}, f32[24,3,2,4,256]{4,3,2,1,0:T(4,128)S(1)}) fusion(f32[24,4,8,4,256]{4,3,2,1,0:T(4,128)} %param.8), kind=kLoop, calls=%fused_computation.7 | loop fusion | bytes 2359296 | tf_op jit(solution)/shard_map/slice | solution.py:681
  1.6 0.4 copy_bitcast_fusion.4
  2.0 0.2 first_edges.1
  2.2 4.9 %collective-permute-start = (f32[4,56,256]{2,1,0:T(8,128)S(1)}, f32[4,56,256]{2,1,0:T(8,128)S(1)}, u32[]{:S(2)}, u32[]{:S(2)}) collective-permute-start(f32[4,56,256]{2,1,0:T(8,128)S(1)} %get-tuple-element.39), channel_id=1, source_target_pairs={{0,1},{1,2},{2,3},{3,4},{4,5},{5,6},{6,7},{8,9},{9,10},{10,11},{11... | collective-permute-start | bytes 688136 | tf_op jit(solution)/shard_map/ppermute | solution.py:640
  7.1 1.3 %collective-permute-start.1 = (f32[4,56,256]{2,1,0:T(8,128)S(1)}, f32[4,56,256]{2,1,0:T(8,128)S(1)}, u32[]{:S(2)}, u32[]{:S(2)}) collective-permute-start(f32[4,56,256]{2,1,0:T(8,128)S(1)} %get-tuple-element.40), channel_id=1, source_target_pairs={{1,0},{2,1},{3,2},{4,3},{5,4},{6,5},{7,6},{9,8},{10,9},{11,10},{12... | collective-permute-start | bytes 688136 | tf_op jit(solution)/shard_map/ppermute | solution.py:640
  8.4 1.0 fusion.1
  9.5 1.3 %add_add_fusion.refs_4_ = f32[8,4,24,256]{3,2,1,0:T(8,128)S(1)} fusion(f32[24,1,8,4,256]{4,3,2,1,0:T(4,128)S(1)} %get-tuple-element.73, f32[24,1,8,4,256]{4,3,2,1,0:T(4,128)S(1)} %get-tuple-element.72, f32[24,1,8,4,256]{4,3,2,1,0:T(4,128)S(1)} %get-tuple-element.71), kind=kLoop, calls=%fused_computation.4 | loop fusion | flops 393216 | bytes 3145728 | tf_op jit(solution)/shard_map/add | solution.py:692
  10.7 0.1 collective-permute-start.4
  10.8 1.6 %collective-permute-start.5 = (f32[8,4,24,256]{3,2,1,0:T(8,128)S(1)}, f32[8,4,24,256]{3,2,1,0:T(8,128)S(1)}, u32[]{:S(2)}, u32[]{:S(2)}) collective-permute-start(f32[8,4,24,256]{3,2,1,0:T(8,128)S(1)} %add_add_fusion.refs_4_), channel_id=1, source_target_pairs={{0,16},{8,24},{16,0},{24,8},{1,17},{9,25},{17,1},{25,9},{2,18},{10... | collective-permute-start | bytes 2359304 | tf_op jit(solution)/shard_map/ppermute | solution.py:615
  12.4 0.9 copy_bitcast_fusion
  13.3 0.0 copy-start.3
  13.3 0.0 copy-start.4
  13.4 0.0 copy-start.5
  13.4 0.0 copy-start.6
  13.4 0.9 copy_bitcast_fusion.2
  14.3 2.6 %collective-permute-done.refs_4_.refs_6_.refs_7_ = f32[4,56,256]{2,1,0:T(8,128)S(1)} collective-permute-done((f32[4,56,256]{2,1,0:T(8,128)S(1)}, f32[4,56,256]{2,1,0:T(8,128)S(1)}, u32[]{:S(2)}, u32[]{:S(2)}) %collective-permute-start) | collective-permute-done | bytes 229408 | tf_op jit(solution)/shard_map/ppermute | solution.py:640
  16.9 0.0 collective-permute-done.1.refs_5_.refs_7_.refs_8_
  16.9 1.0 next_edges.1
  17.8 4.4 %collective-permute-start.2 = (f32[4,48,256]{2,1,0:T(8,128)S(1)}, f32[4,48,256]{2,1,0:T(8,128)S(1)}, u32[]{:S(2)}, u32[]{:S(2)}) collective-permute-start(f32[4,48,256]{2,1,0:T(8,128)S(1)} %get-tuple-element.45), channel_id=1, source_target_pairs={{0,1},{1,2},{2,3},{3,4},{4,5},{5,6},{6,7},{8,9},{9,10},{10,11},{11... | collective-permute-start | bytes 589832 | tf_op jit(solution)/shard_map/ppermute | solution.py:640
  22.2 1.3 %collective-permute-start.3 = (f32[4,48,256]{2,1,0:T(8,128)S(1)}, f32[4,48,256]{2,1,0:T(8,128)S(1)}, u32[]{:S(2)}, u32[]{:S(2)}) collective-permute-start(f32[4,48,256]{2,1,0:T(8,128)S(1)} %get-tuple-element.46), channel_id=1, source_target_pairs={{1,0},{2,1},{3,2},{4,3},{5,4},{6,5},{7,6},{9,8},{10,9},{11,10},{12... | collective-permute-start | bytes 589832 | tf_op jit(solution)/shard_map/ppermute | solution.py:640
  23.6 1.4 %voxel_weights.1 = (f32[2,32,256]{2,1,0:T(8,128)S(1)}, f32[2,32,256]{2,1,0:T(8,128)S(1)}) custom-call(s32[4]{0:T(128)S(1)} %copy-done.6, s32[4,2048]{1,0:T(4,128)S(1)} %copy-done.3, f32[4,2048]{1,0:T(4,128)S(1)} %copy-done.4, f32[4,2048]{1,0:T(4,128)S(1)} %copy-done.5), custom_call_target="tpu_custom_call" | custom-call | tf_op jit(solution)/shard_map/voxel_weights/pallas_call | solution.py:374
  25.0 1.5 %two_substeps.1 = (f32[8,4,24,256]{3,2,1,0:T(8,128)S(1)}, f32[8,4,24,256]{3,2,1,0:T(8,128)S(1)}, f32[8,4,24,256]{3,2,1,0:T(8,128)S(1)}, f32[8,4,24,256]{3,2,1,0:T(8,128)S(1)}) custom-call(f32[8,4,24,256]{3,2,1,0:T(8,128)S(1)} %get-tuple-element.78.refs_0_, f32[8,4,24,256]{3,2,1,0:T(8,128)S(1)} %get-tuple-element.77.refs_1_, ...), custom_call_target="tpu_custom_call" | custom-call | flops 11796480 | bytes 12582912 | tf_op jit(solution)/shard_map/two_substeps/pallas_call | solution.py:323
  26.5 0.0 collective-permute-done.2.refs_4_
  26.5 4.8 %collective-permute-done.3.refs_5_ = f32[4,48,256]{2,1,0:T(8,128)S(1)} collective-permute-done((f32[4,48,256]{2,1,0:T(8,128)S(1)}, f32[4,48,256]{2,1,0:T(8,128)S(1)}, u32[]{:S(2)}, u32[]{:S(2)}) %collective-permute-start.3) | collective-permute-done | bytes 196640 | tf_op jit(solution)/shard_map/ppermute | solution.py:640
  31.4 0.0 collective-permute-done.5.refs_14_.refs_6_
  31.4 0.0 collective-permute-done.4.refs_13_.refs_5_
  31.4 2.7 %last_steps.1 = (f32[8,4,24,256]{3,2,1,0:T(8,128)S(1)}, f32[4,48,256]{2,1,0:T(8,128)S(1)}, f32[4,48,256]{2,1,0:T(8,128)S(1)}, f32[8,4,24,256]{3,2,1,0:T(8,128)S(...) custom-call(f32[8,4,24,256]{3,2,1,0:T(8,128)S(1)} %get-tuple-element, ...), custom_call_target="tpu_custom_call" | custom-call | flops 23592960 | bytes 25165824 | tf_op jit(solution)/shard_map/last_steps/pallas_call | solution.py:323
  34.1 1.6 %collective-permute-start.7 = (f32[6,4,24,256]{3,2,1,0:T(8,128)S(1)}, f32[6,4,24,256]{3,2,1,0:T(8,128)S(1)}, u32[]{:S(2)}, u32[]{:S(2)}) collective-permute-start(f32[6,4,24,256]{3,2,1,0:T(8,128)S(1)} %get-tuple-element.47.refs_0_.refs_12_), channel_id=1, source_target_pairs={{0,16},{8,24},{16,0},{24,8},{1,17},{9,25},{17,1},{25,9},{2,18},{10... | collective-permute-start | bytes 1769480 | tf_op jit(solution)/shard_map/ppermute | solution.py:615
  35.7 4.5 %collective-permute-start.8 = (f32[4,48,256]{2,1,0:T(8,128)S(1)}, f32[4,48,256]{2,1,0:T(8,128)S(1)}, u32[]{:S(2)}, u32[]{:S(2)}) collective-permute-start(f32[4,48,256]{2,1,0:T(8,128)S(1)} %get-tuple-element.50), channel_id=1, source_target_pairs={{0,1},{1,2},{2,3},{3,4},{4,5},{5,6},{6,7},{8,9},{9,10},{10,11},{11... | collective-permute-start | bytes 589832 | tf_op jit(solution)/shard_map/ppermute | solution.py:640
  40.2 1.5 %collective-permute-start.9 = (f32[4,48,256]{2,1,0:T(8,128)S(1)}, f32[4,48,256]{2,1,0:T(8,128)S(1)}, u32[]{:S(2)}, u32[]{:S(2)}) collective-permute-start(f32[4,48,256]{2,1,0:T(8,128)S(1)} %get-tuple-element.51), channel_id=1, source_target_pairs={{1,0},{2,1},{3,2},{4,3},{5,4},{6,5},{7,6},{9,8},{10,9},{11,10},{12... | collective-permute-start | bytes 589832 | tf_op jit(solution)/shard_map/ppermute | solution.py:640
  41.7 0.1 collective-permute-start.17
  41.8 1.6 %collective-permute-done.8.refs_2_.refs_5_ = f32[4,48,256]{2,1,0:T(8,128)S(1)} collective-permute-done((f32[4,48,256]{2,1,0:T(8,128)S(1)}, f32[4,48,256]{2,1,0:T(8,128)S(1)}, u32[]{:S(2)}, u32[]{:S(2)}) %collective-permute-start.8) | collective-permute-done | bytes 196640 | tf_op jit(solution)/shard_map/ppermute | solution.py:640
  43.4 5.8 %collective-permute-done.9.refs_3_.refs_6_ = f32[4,48,256]{2,1,0:T(8,128)S(1)} collective-permute-done((f32[4,48,256]{2,1,0:T(8,128)S(1)}, f32[4,48,256]{2,1,0:T(8,128)S(1)}, u32[]{:S(2)}, u32[]{:S(2)}) %collective-permute-start.9) | collective-permute-done | bytes 196640 | tf_op jit(solution)/shard_map/ppermute | solution.py:640
  49.2 0.1 last_ends.1
  49.3 0.1 collective-permute-start.16
  49.4 0.5 collective-permute-start.6
  49.9 0.1 collective-permute-start.10
  50.0 0.5 collective-permute-start.12
  50.5 0.0 collective-permute-done.17.refs_11_.refs_9_
  50.5 1.2 %collective-permute-done.16.refs_10_.refs_7_ = f32[8,4,24,256]{3,2,1,0:T(8,128)S(1)} collective-permute-done((f32[8,4,24,256]{3,2,1,0:T(8,128)S(1)}, f32[8,4,24,256]{3,2,1,0:T(8,128)S(1)}, u32[]{:S(2)}, u32[]{:S(2)}) %collective-permute-start.16) | collective-permute-done | bytes 786464 | tf_op jit(solution)/shard_map/ppermute | solution.py:615
  51.7 0.5 last_free.1.refs_0_
  52.2 0.2 collective-permute-start.18
  52.4 0.1 collective-permute-done.6.refs_1_.refs_13_
  52.5 0.8 collective-permute-done.10.refs_3_.refs_15_
  53.4 0.6 gram.2.refs_0_
  53.9 3.3 %collective-permute-done.12.refs_3_.refs_18_ = f32[2,4,24,256]{3,2,1,0:T(8,128)S(1)} collective-permute-done((f32[2,4,24,256]{3,2,1,0:T(8,128)S(1)}, f32[2,4,24,256]{3,2,1,0:T(8,128)S(1)}, u32[]{:S(2)}, u32[]{:S(2)}) %collective-permute-start.12) | collective-permute-done | bytes 196640 | tf_op jit(solution)/shard_map/ppermute | solution.py:615
  57.2 0.5 collective-permute-start.21
  57.7 0.5 collective-permute-start.13
  58.3 0.9 collective-permute-done.11.refs_2_.refs_17_
  59.2 0.3 collective-permute-done.13.refs_4_.refs_19_
  59.5 0.7 gram.3
  60.2 3.5 %collective-permute-start.14 = (f32[96,128]{1,0:T(8,128)S(1)}, f32[96,128]{1,0:T(8,128)S(1)}, u32[]{:S(2)}, u32[]{:S(2)}) collective-permute-start(f32[96,128]{1,0:T(8,128)S(1)} %gram.3), channel_id=1, source_target_pairs={{0,1},{1,0},{2,3},{3,2},{4,5},{5,4},{6,7},{7,6},{8,9},{9,8},{10,11... | collective-permute-start | bytes 147464 | tf_op jit(solution)/shard_map/ppermute | solution.py:615
  63.7 2.1 %collective-permute-done.14 = f32[96,128]{1,0:T(8,128)S(1)} collective-permute-done((f32[96,128]{1,0:T(8,128)S(1)}, f32[96,128]{1,0:T(8,128)S(1)}, u32[]{:S(2)}, u32[]{:S(2)}) %collective-permute-start.14) | collective-permute-done | bytes 49184 | tf_op jit(solution)/shard_map/ppermute | solution.py:615
  65.7 3.3 %collective-permute-start.15 = (f32[96,128]{1,0:T(8,128)S(1)}, f32[96,128]{1,0:T(8,128)S(1)}, u32[]{:S(2)}, u32[]{:S(2)}) collective-permute-start(f32[96,128]{1,0:T(8,128)S(1)} %add.17), channel_id=1, source_target_pairs={{0,2},{1,3},{2,0},{3,1},{4,6},{5,7},{6,4},{7,5},{8,10},{9,11},{10,... | collective-permute-start | bytes 147464 | tf_op jit(solution)/shard_map/ppermute | solution.py:615
  69.1 2.1 %collective-permute-done.15 = f32[96,128]{1,0:T(8,128)S(1)} collective-permute-done((f32[96,128]{1,0:T(8,128)S(1)}, f32[96,128]{1,0:T(8,128)S(1)}, u32[]{:S(2)}, u32[]{:S(2)}) %collective-permute-start.15) | collective-permute-done | bytes 49184 | tf_op jit(solution)/shard_map/ppermute | solution.py:615
  71.2 2.6 %collective-permute-start.19 = (f32[96,128]{1,0:T(8,128)S(1)}, f32[96,128]{1,0:T(8,128)S(1)}, u32[]{:S(2)}, u32[]{:S(2)}) collective-permute-start(f32[96,128]{1,0:T(8,128)S(1)} %add.18), channel_id=1, source_target_pairs={{0,4},{1,5},{2,6},{3,7},{4,0},{5,1},{6,2},{7,3},{8,12},{9,13},{10,... | collective-permute-start | bytes 147464 | tf_op jit(solution)/shard_map/ppermute | solution.py:615
  73.8 2.8 %collective-permute-done.19 = f32[96,128]{1,0:T(8,128)S(1)} collective-permute-done((f32[96,128]{1,0:T(8,128)S(1)}, f32[96,128]{1,0:T(8,128)S(1)}, u32[]{:S(2)}, u32[]{:S(2)}) %collective-permute-start.19) | collective-permute-done | bytes 49184 | tf_op jit(solution)/shard_map/ppermute | solution.py:615
  76.6 0.1 collective-permute-start.20
  76.7 1.2 %collective-permute-done.20.other = f32[96,128]{1,0:T(8,128)S(1)} collective-permute-done((f32[96,128]{1,0:T(8,128)S(1)}, f32[96,128]{1,0:T(8,128)S(1)}, u32[]{:S(2)}, u32[]{:S(2)}) %collective-permute-start.20) | collective-permute-done | bytes 49184 | tf_op jit(solution)/shard_map/ppermute | solution.py:615
  77.9 1.0 collective-permute-start.22
  78.9 17.9 %transforms_early.1 = (f32[96,128]{1,0:T(8,128)S(1)}, f32[96,128]{1,0:T(8,128)S(1)}) custom-call(f32[96,128]{1,0:T(8,128)S(1)} %add.19.mine, f32[96,128]{1,0:T(8,128)S(1)} %collective-permute-done.20.other), custom_call_target="tpu_custom_call" | custom-call | flops 100000000 | bytes 1000000 | tf_op jit(solution)/shard_map/transforms_early/pallas_call | solution.py:542
  96.8 0.7 collective-permute-done.22.refs_2_
  97.5 6.0 %transforms_late.1.weights = f32[24,128]{1,0:T(8,128)S(1)} custom-call(f32[96,128]{1,0:T(8,128)S(1)} %get-tuple-element.64.total, f32[96,128]{1,0:T(8,128)S(1)} %get-tuple-element.65.last), custom_call_target="tpu_custom_call" | custom-call | flops 100000000 | bytes 1000000 | tf_op jit(solution)/shard_map/transforms_late/pallas_call | solution.py:542
  103.5 4.6 %mix.1 = f32[24,4,8,4,256]{4,3,2,1,0:T(4,128)} custom-call(f32[24,128]{1,0:T(8,128)S(1)} %transforms_late.1.weights, f32[8,4,24,256]{3,2,1,0:T(8,128)S(1)} %last_free.1.refs_0_, f32[8,4,24,256]{3,2,1,0:T(8,128)S(1)} %collective-permute-done.18.refs_1_, f32[8,4,24,256]{3,2,1,0:T(8,128)S(1)} %collective-permute-done.22.refs_2_, ...), custom_call_target="tpu_custom_call" | custom-call | tf_op jit(solution)/shard_map/mix/pallas_call | solution.py:602
  (23 shorter events, 0.1 us)
Async XLA Ops:
  0.0 8.4 %copy-start.7 = (f32[24,4,8,4,256]{4,3,2,1,0:T(4,128)S(1)}, f32[24,4,8,4,256]{4,3,2,1,0:T(4,128)}, u32[]{:S(2)}) copy-start(f32[24,4,8,4,256]{4,3,2,1,0:T(4,128)} %param.8) | copy-start | bytes 9437188
  0.0 2.0 %copy-start = (f32[8,4,256]{2,1,0:T(4,128)S(1)}, f32[8,4,256]{2,1,0:T(4,128)}, u32[]{:S(2)}) copy-start(f32[8,4,256]{2,1,0:T(4,128)} %refs_9_.7) | copy-start | bytes 98308
  0.0 2.0 %copy-start.2 = (f32[8,4,256]{2,1,0:T(4,128)S(1)}, f32[8,4,256]{2,1,0:T(4,128)}, u32[]{:S(2)}) copy-start(f32[8,4,256]{2,1,0:T(4,128)} %refs_6_.1) | copy-start | bytes 98308
  0.0 2.0 %copy-start.1 = (f32[8,4,256]{2,1,0:T(4,128)S(1)}, f32[8,4,256]{2,1,0:T(4,128)}, u32[]{:S(2)}) copy-start(f32[8,4,256]{2,1,0:T(4,128)} %refs_5_.1) | copy-start | bytes 98308
  2.2 14.6 %collective-permute-start = (f32[4,56,256]{2,1,0:T(8,128)S(1)}, f32[4,56,256]{2,1,0:T(8,128)S(1)}, u32[]{:S(2)}, u32[]{:S(2)}) collective-permute-start(f32[4,56,256]{2,1,0:T(8,128)S(1)} %get-tuple-element.39), channel_id=1, source_target_pairs={{0,1},{1,2},{2,3},{3,4},{4,5},{5,6},{6,7},{8,9},{9,10},{10,11},{11... | collective-permute-start | bytes 688136 | tf_op jit(solution)/shard_map/ppermute | solution.py:640
  7.1 9.7 %collective-permute-start.1 = (f32[4,56,256]{2,1,0:T(8,128)S(1)}, f32[4,56,256]{2,1,0:T(8,128)S(1)}, u32[]{:S(2)}, u32[]{:S(2)}) collective-permute-start(f32[4,56,256]{2,1,0:T(8,128)S(1)} %get-tuple-element.40), channel_id=1, source_target_pairs={{1,0},{2,1},{3,2},{4,3},{5,4},{6,5},{7,6},{9,8},{10,9},{11,10},{12... | collective-permute-start | bytes 688136 | tf_op jit(solution)/shard_map/ppermute | solution.py:640
  10.7 20.6 %collective-permute-start.4 = (f32[8,4,24,256]{3,2,1,0:T(8,128)S(1)}, f32[8,4,24,256]{3,2,1,0:T(8,128)S(1)}, u32[]{:S(2)}, u32[]{:S(2)}) collective-permute-start(f32[8,4,24,256]{3,2,1,0:T(8,128)S(1)} %add_add_fusion.refs_4_), channel_id=1, source_target_pairs={{0,8},{8,0},{16,24},{24,16},{1,9},{9,1},{17,25},{25,17},{2,10},{10... | collective-permute-start | bytes 2359304 | tf_op jit(solution)/shard_map/ppermute | solution.py:615
  10.8 20.5 %collective-permute-start.5 = (f32[8,4,24,256]{3,2,1,0:T(8,128)S(1)}, f32[8,4,24,256]{3,2,1,0:T(8,128)S(1)}, u32[]{:S(2)}, u32[]{:S(2)}) collective-permute-start(f32[8,4,24,256]{3,2,1,0:T(8,128)S(1)} %add_add_fusion.refs_4_), channel_id=1, source_target_pairs={{0,16},{8,24},{16,0},{24,8},{1,17},{9,25},{17,1},{25,9},{2,18},{10... | collective-permute-start | bytes 2359304 | tf_op jit(solution)/shard_map/ppermute | solution.py:615
  13.3 10.2 %copy-start.3 = (s32[4,2048]{1,0:T(4,128)S(1)}, s32[4,2048]{1,0:T(4,128)}, u32[]{:S(2)}) copy-start(s32[4,2048]{1,0:T(4,128)} %obs_index.1) | copy-start | bytes 98308
  13.3 10.2 %copy-start.4 = (f32[4,2048]{1,0:T(4,128)S(1)}, f32[4,2048]{1,0:T(4,128)}, u32[]{:S(2)}) copy-start(f32[4,2048]{1,0:T(4,128)} %observed.1) | copy-start | bytes 98308
  13.4 10.2 %copy-start.5 = (f32[4,2048]{1,0:T(4,128)S(1)}, f32[4,2048]{1,0:T(4,128)}, u32[]{:S(2)}) copy-start(f32[4,2048]{1,0:T(4,128)} %obs_var.1) | copy-start | bytes 98308
  13.4 10.2 %copy-start.6 = (s32[4]{0:T(128)S(1)}, s32[4]{0:T(128)}, u32[]{:S(2)}) copy-start(s32[4]{0:T(128)} %owner.5) | copy-start | bytes 52
  17.8 8.7 %collective-permute-start.2 = (f32[4,48,256]{2,1,0:T(8,128)S(1)}, f32[4,48,256]{2,1,0:T(8,128)S(1)}, u32[]{:S(2)}, u32[]{:S(2)}) collective-permute-start(f32[4,48,256]{2,1,0:T(8,128)S(1)} %get-tuple-element.45), channel_id=1, source_target_pairs={{0,1},{1,2},{2,3},{3,4},{4,5},{5,6},{6,7},{8,9},{9,10},{10,11},{11... | collective-permute-start | bytes 589832 | tf_op jit(solution)/shard_map/ppermute | solution.py:640
  22.2 9.1 %collective-permute-start.3 = (f32[4,48,256]{2,1,0:T(8,128)S(1)}, f32[4,48,256]{2,1,0:T(8,128)S(1)}, u32[]{:S(2)}, u32[]{:S(2)}) collective-permute-start(f32[4,48,256]{2,1,0:T(8,128)S(1)} %get-tuple-element.46), channel_id=1, source_target_pairs={{1,0},{2,1},{3,2},{4,3},{5,4},{6,5},{7,6},{9,8},{10,9},{11,10},{12... | collective-permute-start | bytes 589832 | tf_op jit(solution)/shard_map/ppermute | solution.py:640
  34.1 15.8 %collective-permute-start.7 = (f32[6,4,24,256]{3,2,1,0:T(8,128)S(1)}, f32[6,4,24,256]{3,2,1,0:T(8,128)S(1)}, u32[]{:S(2)}, u32[]{:S(2)}) collective-permute-start(f32[6,4,24,256]{3,2,1,0:T(8,128)S(1)} %get-tuple-element.47.refs_0_.refs_12_), channel_id=1, source_target_pairs={{0,16},{8,24},{16,0},{24,8},{1,17},{9,25},{17,1},{25,9},{2,18},{10... | collective-permute-start | bytes 1769480 | tf_op jit(solution)/shard_map/ppermute | solution.py:615
  35.7 7.7 %collective-permute-start.8 = (f32[4,48,256]{2,1,0:T(8,128)S(1)}, f32[4,48,256]{2,1,0:T(8,128)S(1)}, u32[]{:S(2)}, u32[]{:S(2)}) collective-permute-start(f32[4,48,256]{2,1,0:T(8,128)S(1)} %get-tuple-element.50), channel_id=1, source_target_pairs={{0,1},{1,2},{2,3},{3,4},{4,5},{5,6},{6,7},{8,9},{9,10},{10,11},{11... | collective-permute-start | bytes 589832 | tf_op jit(solution)/shard_map/ppermute | solution.py:640
  40.2 9.0 %collective-permute-start.9 = (f32[4,48,256]{2,1,0:T(8,128)S(1)}, f32[4,48,256]{2,1,0:T(8,128)S(1)}, u32[]{:S(2)}, u32[]{:S(2)}) collective-permute-start(f32[4,48,256]{2,1,0:T(8,128)S(1)} %get-tuple-element.51), channel_id=1, source_target_pairs={{1,0},{2,1},{3,2},{4,3},{5,4},{6,5},{7,6},{9,8},{10,9},{11,10},{12... | collective-permute-start | bytes 589832 | tf_op jit(solution)/shard_map/ppermute | solution.py:640
  41.7 8.8 %collective-permute-start.17 = (f32[8,4,24,256]{3,2,1,0:T(8,128)S(1)}, f32[8,4,24,256]{3,2,1,0:T(8,128)S(1)}, u32[]{:S(2)}, u32[]{:S(2)}) collective-permute-start(f32[8,4,24,256]{3,2,1,0:T(8,128)S(1)} %get-tuple-element.62.refs_8_), channel_id=1, source_target_pairs={{0,8},{8,0},{16,24},{24,16},{1,9},{9,1},{17,25},{25,17},{2,10},{10... | collective-permute-start | bytes 2359304 | tf_op jit(solution)/shard_map/ppermute | solution.py:615
  49.3 2.4 %collective-permute-start.16 = (f32[8,4,24,256]{3,2,1,0:T(8,128)S(1)}, f32[8,4,24,256]{3,2,1,0:T(8,128)S(1)}, u32[]{:S(2)}, u32[]{:S(2)}) collective-permute-start(f32[8,4,24,256]{3,2,1,0:T(8,128)S(1)} %collective-permute-done.5.refs_14_.refs_6_), channel_id=1, source_target_pairs={{0,8},{8,0},{16,24},{24,16},{1,9},{9,1},{17,25},{25,17},{2,10},{10... | collective-permute-start | bytes 2359304 | tf_op jit(solution)/shard_map/ppermute | solution.py:615
  49.4 3.1 %collective-permute-start.6 = (f32[6,4,24,256]{3,2,1,0:T(8,128)S(1)}, f32[6,4,24,256]{3,2,1,0:T(8,128)S(1)}, u32[]{:S(2)}, u32[]{:S(2)}) collective-permute-start(f32[6,4,24,256]{3,2,1,0:T(8,128)S(1)} %get-tuple-element.47.refs_0_.refs_12_), channel_id=1, source_target_pairs={{0,8},{8,0},{16,24},{24,16},{1,9},{9,1},{17,25},{25,17},{2,10},{10... | collective-permute-start | bytes 1769480 | tf_op jit(solution)/shard_map/ppermute | solution.py:615
  49.9 3.5 %collective-permute-start.10 = (f32[6,4,24,256]{3,2,1,0:T(8,128)S(1)}, f32[6,4,24,256]{3,2,1,0:T(8,128)S(1)}, u32[]{:S(2)}, u32[]{:S(2)}) collective-permute-start(f32[6,4,24,256]{3,2,1,0:T(8,128)S(1)} %collective-permute-done.7.refs_2_.refs_14_), channel_id=1, source_target_pairs={{0,8},{8,0},{16,24},{24,16},{1,9},{9,1},{17,25},{25,17},{2,10},{10... | collective-permute-start | bytes 1769480 | tf_op jit(solution)/shard_map/ppermute | solution.py:615
  50.0 7.3 %collective-permute-start.12 = (f32[2,4,24,256]{3,2,1,0:T(8,128)S(1)}, f32[2,4,24,256]{3,2,1,0:T(8,128)S(1)}, u32[]{:S(2)}, u32[]{:S(2)}) collective-permute-start(f32[2,4,24,256]{3,2,1,0:T(8,128)S(1)} %get-tuple-element.52.refs_1_.refs_16_), channel_id=1, source_target_pairs={{0,16},{8,24},{16,0},{24,8},{1,17},{9,25},{17,1},{25,9},{2,18},{10... | collective-permute-start | bytes 589832 | tf_op jit(solution)/shard_map/ppermute | solution.py:615
  52.2 19.0 %collective-permute-start.18 = (f32[8,4,24,256]{3,2,1,0:T(8,128)S(1)}, f32[8,4,24,256]{3,2,1,0:T(8,128)S(1)}, u32[]{:S(2)}, u32[]{:S(2)}) collective-permute-start(f32[8,4,24,256]{3,2,1,0:T(8,128)S(1)} %last_free.1.refs_0_), channel_id=1, source_target_pairs={{0,8},{8,0},{16,24},{24,16},{1,9},{9,1},{17,25},{25,17},{2,10},{10... | collective-permute-start | bytes 2359304 | tf_op jit(solution)/shard_map/ppermute | solution.py:615
  57.2 20.6 %collective-permute-start.21 = (f32[8,4,24,256]{3,2,1,0:T(8,128)S(1)}, f32[8,4,24,256]{3,2,1,0:T(8,128)S(1)}, u32[]{:S(2)}, u32[]{:S(2)}) collective-permute-start(f32[8,4,24,256]{3,2,1,0:T(8,128)S(1)} %get-tuple-element.62.refs_8_), channel_id=1, source_target_pairs={{0,16},{8,24},{16,0},{24,8},{1,17},{9,25},{17,1},{25,9},{2,18},{10... | collective-permute-start | bytes 2359304 | tf_op jit(solution)/shard_map/ppermute | solution.py:615
  57.7 1.4 %collective-permute-start.11 = (f32[2,4,24,256]{3,2,1,0:T(8,128)S(1)}, f32[2,4,24,256]{3,2,1,0:T(8,128)S(1)}, u32[]{:S(2)}, u32[]{:S(2)}) collective-permute-start(f32[2,4,24,256]{3,2,1,0:T(8,128)S(1)} %get-tuple-element.52.refs_1_.refs_16_), channel_id=1, source_target_pairs={{0,8},{8,0},{16,24},{24,16},{1,9},{9,1},{17,25},{25,17},{2,10},{10... | collective-permute-start | bytes 589832 | tf_op jit(solution)/shard_map/ppermute | solution.py:615
  57.7 1.7 %collective-permute-start.13 = (f32[2,4,24,256]{3,2,1,0:T(8,128)S(1)}, f32[2,4,24,256]{3,2,1,0:T(8,128)S(1)}, u32[]{:S(2)}, u32[]{:S(2)}) collective-permute-start(f32[2,4,24,256]{3,2,1,0:T(8,128)S(1)} %collective-permute-done.12.refs_3_.refs_18_), channel_id=1, source_target_pairs={{0,8},{8,0},{16,24},{24,16},{1,9},{9,1},{17,25},{25,17},{2,10},{10... | collective-permute-start | bytes 589832 | tf_op jit(solution)/shard_map/ppermute | solution.py:615
  60.2 5.6 %collective-permute-start.14 = (f32[96,128]{1,0:T(8,128)S(1)}, f32[96,128]{1,0:T(8,128)S(1)}, u32[]{:S(2)}, u32[]{:S(2)}) collective-permute-start(f32[96,128]{1,0:T(8,128)S(1)} %gram.3), channel_id=1, source_target_pairs={{0,1},{1,0},{2,3},{3,2},{4,5},{5,4},{6,7},{7,6},{8,9},{9,8},{10,11... | collective-permute-start | bytes 147464 | tf_op jit(solution)/shard_map/ppermute | solution.py:615
  65.7 5.4 %collective-permute-start.15 = (f32[96,128]{1,0:T(8,128)S(1)}, f32[96,128]{1,0:T(8,128)S(1)}, u32[]{:S(2)}, u32[]{:S(2)}) collective-permute-start(f32[96,128]{1,0:T(8,128)S(1)} %add.17), channel_id=1, source_target_pairs={{0,2},{1,3},{2,0},{3,1},{4,6},{5,7},{6,4},{7,5},{8,10},{9,11},{10,... | collective-permute-start | bytes 147464 | tf_op jit(solution)/shard_map/ppermute | solution.py:615
  71.2 5.4 %collective-permute-start.19 = (f32[96,128]{1,0:T(8,128)S(1)}, f32[96,128]{1,0:T(8,128)S(1)}, u32[]{:S(2)}, u32[]{:S(2)}) collective-permute-start(f32[96,128]{1,0:T(8,128)S(1)} %add.18), channel_id=1, source_target_pairs={{0,4},{1,5},{2,6},{3,7},{4,0},{5,1},{6,2},{7,3},{8,12},{9,13},{10,... | collective-permute-start | bytes 147464 | tf_op jit(solution)/shard_map/ppermute | solution.py:615
  76.6 1.3 %collective-permute-start.20 = (f32[96,128]{1,0:T(8,128)S(1)}, f32[96,128]{1,0:T(8,128)S(1)}, u32[]{:S(2)}, u32[]{:S(2)}) collective-permute-start(f32[96,128]{1,0:T(8,128)S(1)} %add.19.mine), channel_id=1, source_target_pairs={{0,8},{8,0},{16,24},{24,16},{1,9},{9,1},{17,25},{25,17},{2,10},{10... | collective-permute-start | bytes 147464 | tf_op jit(solution)/shard_map/ppermute | solution.py:615
  77.9 19.6 %collective-permute-start.22 = (f32[8,4,24,256]{3,2,1,0:T(8,128)S(1)}, f32[8,4,24,256]{3,2,1,0:T(8,128)S(1)}, u32[]{:S(2)}, u32[]{:S(2)}) collective-permute-start(f32[8,4,24,256]{3,2,1,0:T(8,128)S(1)} %last_free.1.refs_0_), channel_id=1, source_target_pairs={{0,16},{8,24},{16,0},{24,8},{1,17},{9,25},{17,1},{25,9},{2,18},{10... | collective-permute-start | bytes 2359304 | tf_op jit(solution)/shard_map/ppermute | solution.py:615
  78.9 24.6 %collective-permute-start.24 = (f32[8,4,24,256]{3,2,1,0:T(8,128)S(1)}, f32[8,4,24,256]{3,2,1,0:T(8,128)S(1)}, u32[]{:S(2)}, u32[]{:S(2)}) collective-permute-start(f32[8,4,24,256]{3,2,1,0:T(8,128)S(1)} %collective-permute-done.21.refs_10_), channel_id=1, source_target_pairs={{0,8},{8,0},{16,24},{24,16},{1,9},{9,1},{17,25},{25,17},{2,10},{10... | collective-permute-start | bytes 2359304 | tf_op jit(solution)/shard_map/ppermute | solution.py:615
  97.5 6.1 %collective-permute-start.23 = (f32[8,4,24,256]{3,2,1,0:T(8,128)S(1)}, f32[8,4,24,256]{3,2,1,0:T(8,128)S(1)}, u32[]{:S(2)}, u32[]{:S(2)}) collective-permute-start(f32[8,4,24,256]{3,2,1,0:T(8,128)S(1)} %collective-permute-done.22.refs_2_), channel_id=1, source_target_pairs={{0,8},{8,0},{16,24},{24,16},{1,9},{9,1},{17,25},{25,17},{2,10},{10... | collective-permute-start | bytes 2359304 | tf_op jit(solution)/shard_map/ppermute | solution.py:615

commit v16 on v15

--- a/solution.py
+++ b/solution.py
@@ -598,7 +598,7 @@
 
 def mix(weights, sources, blocks, shape):
     rows, species, nx, nz, ny = shape
-    planes = 2 if nx % 2 == 0 else 1
+    planes = next(count for count in (4, 2, 1) if nx % count == 0)
     return pl.pallas_call(
         functools.partial(mix_kernel, blocks=blocks),
         grid=(nx // planes,),

time: 108 us -> 109 us (level)
  Pallas kernels: 37.3 us -> 41 us
  waiting for transfers between devices: 30.3 us -> 27.9 us
    pallas_call x2, Pallas kernels: 1.25 us -> 4.49 us  [gram(): pl.pallas_call(functools.partial(gram_kernel, offsets=offsets, planes=pla...]
    ppermute x19, waiting for transfers between devices: 15.5 us -> 13.1 us  [swap(): return lax.ppermute(x, axis, [(k, k ^ bit) for k in range(count)])]
  transfers between devices with their start and end apart: 25 -> 25, of which waited for: 15 -> 15; matrix products, arithmetic and copies ran while one was open for 4% -> 4% of each run, Pallas kernels for 27% -> 30%
where the time goes in v16:
time: 109 us
  Pallas kernels  41 us (38%)
  starting transfers between devices  33.2 us (30%)
  waiting for transfers between devices  27.9 us (26%)
  local copies, waits for them, and re-layouts  4.89 us (4%)
  other arithmetic  1.29 us (1%)
    pallas_call x2, Pallas kernels, transform_call(): pl.pallas_call(kernel, out_shape=[jax.ShapeDtypeStruct(shape, f32) for sh...  23.9 us
    ppermute x19, starting transfers between devices, swap(): return lax.ppermute(x, axis, [(k, k ^ bit) for k in range(count)])  15.3 us
    ppermute x3, starting transfers between devices, halos(): lax.ppermute(last, 'space', forward)  13.8 us
    ppermute x19, waiting for transfers between devices, swap(): return lax.ppermute(x, axis, [(k, k ^ bit) for k in range(count)])  13.1 us
    ppermute x3, waiting for transfers between devices, halos(): lax.ppermute(first, 'space', backward)  10.7 us
    pallas_call x6, Pallas kernels, forecast_call(): pl.pallas_call(body, out_shape=[jax.ShapeDtypeStruct(shape, f32) for shap...  6.01 us
    pallas_call x1, Pallas kernels, mix(): pl.pallas_call(functools.partial(mix_kernel, blocks=blocks), grid=(nx //...  5.15 us
    pallas_call x2, Pallas kernels, gram(): pl.pallas_call(functools.partial(gram_kernel, offsets=offsets, planes=pla...  4.49 us
  transfers between devices with their start and end apart: 25, of which 15 were waited for; matrix products, arithmetic and copies ran while one was open for 4% of the time, Pallas kernels for 30%

profile of v16, /device:TPU:0, one launch (start us, length us, event | category | flops | bytes accessed | tf_op | source)
XLA Modules:
  0.0 108.6 jit_solution(4709566179623802179)
XLA Ops:
  0.0 1.6 %fusion = (f32[24,3,2,4,256]{4,3,2,1,0:T(4,128)S(1)}, f32[24,3,2,4,256]{4,3,2,1,0:T(4,128)S(1)}) fusion(f32[24,4,8,4,256]{4,3,2,1,0:T(4,128)} %param.8), kind=kLoop, calls=%fused_computation.7 | loop fusion | bytes 2359296 | tf_op jit(solution)/shard_map/slice | solution.py:681
  1.6 0.4 copy_bitcast_fusion.4
  2.0 0.2 first_edges.1
  2.2 4.9 %collective-permute-start = (f32[4,56,256]{2,1,0:T(8,128)S(1)}, f32[4,56,256]{2,1,0:T(8,128)S(1)}, u32[]{:S(2)}, u32[]{:S(2)}) collective-permute-start(f32[4,56,256]{2,1,0:T(8,128)S(1)} %get-tuple-element.39), channel_id=1, source_target_pairs={{0,1},{1,2},{2,3},{3,4},{4,5},{5,6},{6,7},{8,9},{9,10},{10,11},{11... | collective-permute-start | bytes 688136 | tf_op jit(solution)/shard_map/ppermute | solution.py:640
  7.1 1.3 %collective-permute-start.1 = (f32[4,56,256]{2,1,0:T(8,128)S(1)}, f32[4,56,256]{2,1,0:T(8,128)S(1)}, u32[]{:S(2)}, u32[]{:S(2)}) collective-permute-start(f32[4,56,256]{2,1,0:T(8,128)S(1)} %get-tuple-element.40), channel_id=1, source_target_pairs={{1,0},{2,1},{3,2},{4,3},{5,4},{6,5},{7,6},{9,8},{10,9},{11,10},{12... | collective-permute-start | bytes 688136 | tf_op jit(solution)/shard_map/ppermute | solution.py:640
  8.4 1.0 fusion.1
  9.5 1.3 %add_add_fusion.refs_4_ = f32[8,4,24,256]{3,2,1,0:T(8,128)S(1)} fusion(f32[24,1,8,4,256]{4,3,2,1,0:T(4,128)S(1)} %get-tuple-element.73, f32[24,1,8,4,256]{4,3,2,1,0:T(4,128)S(1)} %get-tuple-element.72, f32[24,1,8,4,256]{4,3,2,1,0:T(4,128)S(1)} %get-tuple-element.71), kind=kLoop, calls=%fused_computation.4 | loop fusion | flops 393216 | bytes 3145728 | tf_op jit(solution)/shard_map/add | solution.py:692
  10.7 0.1 collective-permute-start.4
  10.8 1.6 %collective-permute-start.5 = (f32[8,4,24,256]{3,2,1,0:T(8,128)S(1)}, f32[8,4,24,256]{3,2,1,0:T(8,128)S(1)}, u32[]{:S(2)}, u32[]{:S(2)}) collective-permute-start(f32[8,4,24,256]{3,2,1,0:T(8,128)S(1)} %add_add_fusion.refs_4_), channel_id=1, source_target_pairs={{0,16},{8,24},{16,0},{24,8},{1,17},{9,25},{17,1},{25,9},{2,18},{10... | collective-permute-start | bytes 2359304 | tf_op jit(solution)/shard_map/ppermute | solution.py:615
  12.4 0.9 copy_bitcast_fusion
  13.3 0.0 copy-start.3
  13.3 0.0 copy-start.4
  13.4 0.0 copy-start.5
  13.4 0.0 copy-start.6
  13.4 0.9 copy_bitcast_fusion.2
  14.3 2.6 %collective-permute-done.refs_4_.refs_6_.refs_7_ = f32[4,56,256]{2,1,0:T(8,128)S(1)} collective-permute-done((f32[4,56,256]{2,1,0:T(8,128)S(1)}, f32[4,56,256]{2,1,0:T(8,128)S(1)}, u32[]{:S(2)}, u32[]{:S(2)}) %collective-permute-start) | collective-permute-done | bytes 229408 | tf_op jit(solution)/shard_map/ppermute | solution.py:640
  16.9 1.0 next_edges.1
  17.8 4.4 %collective-permute-start.2 = (f32[4,48,256]{2,1,0:T(8,128)S(1)}, f32[4,48,256]{2,1,0:T(8,128)S(1)}, u32[]{:S(2)}, u32[]{:S(2)}) collective-permute-start(f32[4,48,256]{2,1,0:T(8,128)S(1)} %get-tuple-element.45), channel_id=1, source_target_pairs={{0,1},{1,2},{2,3},{3,4},{4,5},{5,6},{6,7},{8,9},{9,10},{10,11},{11... | collective-permute-start | bytes 589832 | tf_op jit(solution)/shard_map/ppermute | solution.py:640
  22.2 1.3 %collective-permute-start.3 = (f32[4,48,256]{2,1,0:T(8,128)S(1)}, f32[4,48,256]{2,1,0:T(8,128)S(1)}, u32[]{:S(2)}, u32[]{:S(2)}) collective-permute-start(f32[4,48,256]{2,1,0:T(8,128)S(1)} %get-tuple-element.46), channel_id=1, source_target_pairs={{1,0},{2,1},{3,2},{4,3},{5,4},{6,5},{7,6},{9,8},{10,9},{11,10},{12... | collective-permute-start | bytes 589832 | tf_op jit(solution)/shard_map/ppermute | solution.py:640
  23.6 1.4 %voxel_weights.1 = (f32[2,32,256]{2,1,0:T(8,128)S(1)}, f32[2,32,256]{2,1,0:T(8,128)S(1)}) custom-call(s32[4]{0:T(128)S(1)} %copy-done.6, s32[4,2048]{1,0:T(4,128)S(1)} %copy-done.3, f32[4,2048]{1,0:T(4,128)S(1)} %copy-done.4, f32[4,2048]{1,0:T(4,128)S(1)} %copy-done.5), custom_call_target="tpu_custom_call" | custom-call | tf_op jit(solution)/shard_map/voxel_weights/pallas_call | solution.py:374
  25.0 1.5 %two_substeps.1 = (f32[8,4,24,256]{3,2,1,0:T(8,128)S(1)}, f32[8,4,24,256]{3,2,1,0:T(8,128)S(1)}, f32[8,4,24,256]{3,2,1,0:T(8,128)S(1)}, f32[8,4,24,256]{3,2,1,0:T(8,128)S(1)}) custom-call(f32[8,4,24,256]{3,2,1,0:T(8,128)S(1)} %get-tuple-element.78.refs_0_, f32[8,4,24,256]{3,2,1,0:T(8,128)S(1)} %get-tuple-element.77.refs_1_, ...), custom_call_target="tpu_custom_call" | custom-call | flops 11796480 | bytes 12582912 | tf_op jit(solution)/shard_map/two_substeps/pallas_call | solution.py:323
  26.5 0.0 collective-permute-done.2.refs_4_
  26.5 4.8 %collective-permute-done.3.refs_5_ = f32[4,48,256]{2,1,0:T(8,128)S(1)} collective-permute-done((f32[4,48,256]{2,1,0:T(8,128)S(1)}, f32[4,48,256]{2,1,0:T(8,128)S(1)}, u32[]{:S(2)}, u32[]{:S(2)}) %collective-permute-start.3) | collective-permute-done | bytes 196640 | tf_op jit(solution)/shard_map/ppermute | solution.py:640
  31.4 2.7 %last_steps.1 = (f32[8,4,24,256]{3,2,1,0:T(8,128)S(1)}, f32[4,48,256]{2,1,0:T(8,128)S(1)}, f32[4,48,256]{2,1,0:T(8,128)S(1)}, f32[8,4,24,256]{3,2,1,0:T(8,128)S(...) custom-call(f32[8,4,24,256]{3,2,1,0:T(8,128)S(1)} %get-tuple-element, ...), custom_call_target="tpu_custom_call" | custom-call | flops 23592960 | bytes 25165824 | tf_op jit(solution)/shard_map/last_steps/pallas_call | solution.py:323
  34.1 1.6 %collective-permute-start.7 = (f32[6,4,24,256]{3,2,1,0:T(8,128)S(1)}, f32[6,4,24,256]{3,2,1,0:T(8,128)S(1)}, u32[]{:S(2)}, u32[]{:S(2)}) collective-permute-start(f32[6,4,24,256]{3,2,1,0:T(8,128)S(1)} %get-tuple-element.47.refs_0_.refs_12_), channel_id=1, source_target_pairs={{0,16},{8,24},{16,0},{24,8},{1,17},{9,25},{17,1},{25,9},{2,18},{10... | collective-permute-start | bytes 1769480 | tf_op jit(solution)/shard_map/ppermute | solution.py:615
  35.7 4.5 %collective-permute-start.8 = (f32[4,48,256]{2,1,0:T(8,128)S(1)}, f32[4,48,256]{2,1,0:T(8,128)S(1)}, u32[]{:S(2)}, u32[]{:S(2)}) collective-permute-start(f32[4,48,256]{2,1,0:T(8,128)S(1)} %get-tuple-element.50), channel_id=1, source_target_pairs={{0,1},{1,2},{2,3},{3,4},{4,5},{5,6},{6,7},{8,9},{9,10},{10,11},{11... | collective-permute-start | bytes 589832 | tf_op jit(solution)/shard_map/ppermute | solution.py:640
  40.2 1.5 %collective-permute-start.9 = (f32[4,48,256]{2,1,0:T(8,128)S(1)}, f32[4,48,256]{2,1,0:T(8,128)S(1)}, u32[]{:S(2)}, u32[]{:S(2)}) collective-permute-start(f32[4,48,256]{2,1,0:T(8,128)S(1)} %get-tuple-element.51), channel_id=1, source_target_pairs={{1,0},{2,1},{3,2},{4,3},{5,4},{6,5},{7,6},{9,8},{10,9},{11,10},{12... | collective-permute-start | bytes 589832 | tf_op jit(solution)/shard_map/ppermute | solution.py:640
  41.7 0.1 collective-permute-start.17
  41.8 1.6 %collective-permute-done.8.refs_2_.refs_5_ = f32[4,48,256]{2,1,0:T(8,128)S(1)} collective-permute-done((f32[4,48,256]{2,1,0:T(8,128)S(1)}, f32[4,48,256]{2,1,0:T(8,128)S(1)}, u32[]{:S(2)}, u32[]{:S(2)}) %collective-permute-start.8) | collective-permute-done | bytes 196640 | tf_op jit(solution)/shard_map/ppermute | solution.py:640
  43.4 5.8 %collective-permute-done.9.refs_3_.refs_6_ = f32[4,48,256]{2,1,0:T(8,128)S(1)} collective-permute-done((f32[4,48,256]{2,1,0:T(8,128)S(1)}, f32[4,48,256]{2,1,0:T(8,128)S(1)}, u32[]{:S(2)}, u32[]{:S(2)}) %collective-permute-start.9) | collective-permute-done | bytes 196640 | tf_op jit(solution)/shard_map/ppermute | solution.py:640
  49.2 0.1 last_ends.1
  49.3 0.1 collective-permute-start.16
  49.4 0.5 collective-permute-start.6
  49.9 0.0 collective-permute-done.7.refs_2_.refs_14_
  49.9 0.1 collective-permute-start.10
  50.0 0.5 collective-permute-start.12
  50.5 1.2 %collective-permute-done.16.refs_10_.refs_7_ = f32[8,4,24,256]{3,2,1,0:T(8,128)S(1)} collective-permute-done((f32[8,4,24,256]{3,2,1,0:T(8,128)S(1)}, f32[8,4,24,256]{3,2,1,0:T(8,128)S(1)}, u32[]{:S(2)}, u32[]{:S(2)}) %collective-permute-start.16) | collective-permute-done | bytes 786464 | tf_op jit(solution)/shard_map/ppermute | solution.py:615
  51.7 0.5 last_free.1.refs_0_
  52.2 0.2 collective-permute-start.18
  52.4 0.1 collective-permute-done.6.refs_1_.refs_13_
  52.5 0.8 collective-permute-done.10.refs_3_.refs_15_
  53.4 3.0 %gram.2.refs_0_ = f32[2,96,128]{2,1,0:T(8,128)S(1)} custom-call(s32[4]{0:T(128)S(1)} %copy-done.6, f32[2,32,256]{2,1,0:T(8,128)S(1)} %get-tuple-element.37.refs_11_.omega, f32[2,32,256]{2,1,0:T(8,128)S(1)} %get-tuple-element.38.refs_12_.eta, f32[6,4,24,256]{3,2,1,0:T(8,128)S(1)} %get-tuple-element.47.refs_0_.refs_12_, ...), custom_call_target="tpu_custom_call" | custom-call | tf_op jit(solution)/shard_map/gram/pallas_call | solution.py:438
  56.4 0.9 collective-permute-done.12.refs_3_.refs_18_
  57.2 0.5 collective-permute-start.21
  57.7 0.5 collective-permute-start.13
  58.3 0.9 collective-permute-done.11.refs_2_.refs_17_
  59.2 0.3 collective-permute-done.13.refs_4_.refs_19_
  59.5 1.5 %gram.3 = f32[96,128]{1,0:T(8,128)S(1)} custom-call(s32[4]{0:T(128)S(1)} %copy-done.6, f32[2,32,256]{2,1,0:T(8,128)S(1)} %get-tuple-element.37.refs_11_.omega, f32[2,32,256]{2,1,0:T(8,128)S(1)} %get-tuple-element.38.refs_12_.eta, f32[2,96,128]{2,1,0:T(8,128)S(1)} %gram.2.refs_0_, f32[2,4,24,256]{3,2,1,0:T(8,128)S(1)} %get-tuple-element.52.refs_1_.refs_16_, ...), custom_call_target="tpu_custom_call" | custom-call | tf_op jit(solution)/shard_map/gram/pallas_call | solution.py:438
  61.0 1.9 %collective-permute-start.14 = (f32[96,128]{1,0:T(8,128)S(1)}, f32[96,128]{1,0:T(8,128)S(1)}, u32[]{:S(2)}, u32[]{:S(2)}) collective-permute-start(f32[96,128]{1,0:T(8,128)S(1)} %gram.3), channel_id=1, source_target_pairs={{0,1},{1,0},{2,3},{3,2},{4,5},{5,4},{6,7},{7,6},{8,9},{9,8},{10,11... | collective-permute-start | bytes 147464 | tf_op jit(solution)/shard_map/ppermute | solution.py:615
  62.9 2.3 %collective-permute-done.14 = f32[96,128]{1,0:T(8,128)S(1)} collective-permute-done((f32[96,128]{1,0:T(8,128)S(1)}, f32[96,128]{1,0:T(8,128)S(1)}, u32[]{:S(2)}, u32[]{:S(2)}) %collective-permute-start.14) | collective-permute-done | bytes 49184 | tf_op jit(solution)/shard_map/ppermute | solution.py:615
  65.1 3.5 %collective-permute-start.15 = (f32[96,128]{1,0:T(8,128)S(1)}, f32[96,128]{1,0:T(8,128)S(1)}, u32[]{:S(2)}, u32[]{:S(2)}) collective-permute-start(f32[96,128]{1,0:T(8,128)S(1)} %add.17), channel_id=1, source_target_pairs={{0,2},{1,3},{2,0},{3,1},{4,6},{5,7},{6,4},{7,5},{8,10},{9,11},{10,... | collective-permute-start | bytes 147464 | tf_op jit(solution)/shard_map/ppermute | solution.py:615
  68.6 2.1 %collective-permute-done.15 = f32[96,128]{1,0:T(8,128)S(1)} collective-permute-done((f32[96,128]{1,0:T(8,128)S(1)}, f32[96,128]{1,0:T(8,128)S(1)}, u32[]{:S(2)}, u32[]{:S(2)}) %collective-permute-start.15) | collective-permute-done | bytes 49184 | tf_op jit(solution)/shard_map/ppermute | solution.py:615
  70.7 0.0 collective-permute-done.18.refs_1_
  70.7 3.1 %collective-permute-start.19 = (f32[96,128]{1,0:T(8,128)S(1)}, f32[96,128]{1,0:T(8,128)S(1)}, u32[]{:S(2)}, u32[]{:S(2)}) collective-permute-start(f32[96,128]{1,0:T(8,128)S(1)} %add.18), channel_id=1, source_target_pairs={{0,4},{1,5},{2,6},{3,7},{4,0},{5,1},{6,2},{7,3},{8,12},{9,13},{10,... | collective-permute-start | bytes 147464 | tf_op jit(solution)/shard_map/ppermute | solution.py:615
  73.8 2.6 %collective-permute-done.19 = f32[96,128]{1,0:T(8,128)S(1)} collective-permute-done((f32[96,128]{1,0:T(8,128)S(1)}, f32[96,128]{1,0:T(8,128)S(1)}, u32[]{:S(2)}, u32[]{:S(2)}) %collective-permute-start.19) | collective-permute-done | bytes 49184 | tf_op jit(solution)/shard_map/ppermute | solution.py:615
  76.5 0.1 collective-permute-start.20
  76.5 1.2 %collective-permute-done.20.other = f32[96,128]{1,0:T(8,128)S(1)} collective-permute-done((f32[96,128]{1,0:T(8,128)S(1)}, f32[96,128]{1,0:T(8,128)S(1)}, u32[]{:S(2)}, u32[]{:S(2)}) %collective-permute-start.20) | collective-permute-done | bytes 49184 | tf_op jit(solution)/shard_map/ppermute | solution.py:615
  77.7 0.0 collective-permute-done.21.refs_10_
  77.7 1.0 collective-permute-start.22
  78.8 0.0 collective-permute-start.24
  78.8 17.9 %transforms_early.1 = (f32[96,128]{1,0:T(8,128)S(1)}, f32[96,128]{1,0:T(8,128)S(1)}) custom-call(f32[96,128]{1,0:T(8,128)S(1)} %add.19.mine, f32[96,128]{1,0:T(8,128)S(1)} %collective-permute-done.20.other), custom_call_target="tpu_custom_call" | custom-call | flops 100000000 | bytes 1000000 | tf_op jit(solution)/shard_map/transforms_early/pallas_call | solution.py:542
  96.7 0.7 collective-permute-done.22.refs_2_
  97.4 6.0 %transforms_late.1.weights = f32[24,128]{1,0:T(8,128)S(1)} custom-call(f32[96,128]{1,0:T(8,128)S(1)} %get-tuple-element.64.total, f32[96,128]{1,0:T(8,128)S(1)} %get-tuple-element.65.last), custom_call_target="tpu_custom_call" | custom-call | flops 100000000 | bytes 1000000 | tf_op jit(solution)/shard_map/transforms_late/pallas_call | solution.py:542
  103.4 5.2 %mix.1 = f32[24,4,8,4,256]{4,3,2,1,0:T(4,128)} custom-call(f32[24,128]{1,0:T(8,128)S(1)} %transforms_late.1.weights, f32[8,4,24,256]{3,2,1,0:T(8,128)S(1)} %last_free.1.refs_0_, f32[8,4,24,256]{3,2,1,0:T(8,128)S(1)} %collective-permute-done.18.refs_1_, f32[8,4,24,256]{3,2,1,0:T(8,128)S(1)} %collective-permute-done.22.refs_2_, ...), custom_call_target="tpu_custom_call" | custom-call | tf_op jit(solution)/shard_map/mix/pallas_call | solution.py:602
  (23 shorter events, 0.1 us)
Async XLA Ops:
  0.0 8.4 %copy-start.7 = (f32[24,4,8,4,256]{4,3,2,1,0:T(4,128)S(1)}, f32[24,4,8,4,256]{4,3,2,1,0:T(4,128)}, u32[]{:S(2)}) copy-start(f32[24,4,8,4,256]{4,3,2,1,0:T(4,128)} %param.8) | copy-start | bytes 9437188
  0.0 2.0 %copy-start = (f32[8,4,256]{2,1,0:T(4,128)S(1)}, f32[8,4,256]{2,1,0:T(4,128)}, u32[]{:S(2)}) copy-start(f32[8,4,256]{2,1,0:T(4,128)} %refs_9_.7) | copy-start | bytes 98308
  0.0 2.0 %copy-start.2 = (f32[8,4,256]{2,1,0:T(4,128)S(1)}, f32[8,4,256]{2,1,0:T(4,128)}, u32[]{:S(2)}) copy-start(f32[8,4,256]{2,1,0:T(4,128)} %refs_6_.1) | copy-start | bytes 98308
  0.0 2.0 %copy-start.1 = (f32[8,4,256]{2,1,0:T(4,128)S(1)}, f32[8,4,256]{2,1,0:T(4,128)}, u32[]{:S(2)}) copy-start(f32[8,4,256]{2,1,0:T(4,128)} %refs_5_.1) | copy-start | bytes 98308
  2.2 14.6 %collective-permute-start = (f32[4,56,256]{2,1,0:T(8,128)S(1)}, f32[4,56,256]{2,1,0:T(8,128)S(1)}, u32[]{:S(2)}, u32[]{:S(2)}) collective-permute-start(f32[4,56,256]{2,1,0:T(8,128)S(1)} %get-tuple-element.39), channel_id=1, source_target_pairs={{0,1},{1,2},{2,3},{3,4},{4,5},{5,6},{6,7},{8,9},{9,10},{10,11},{11... | collective-permute-start | bytes 688136 | tf_op jit(solution)/shard_map/ppermute | solution.py:640
  7.1 9.7 %collective-permute-start.1 = (f32[4,56,256]{2,1,0:T(8,128)S(1)}, f32[4,56,256]{2,1,0:T(8,128)S(1)}, u32[]{:S(2)}, u32[]{:S(2)}) collective-permute-start(f32[4,56,256]{2,1,0:T(8,128)S(1)} %get-tuple-element.40), channel_id=1, source_target_pairs={{1,0},{2,1},{3,2},{4,3},{5,4},{6,5},{7,6},{9,8},{10,9},{11,10},{12... | collective-permute-start | bytes 688136 | tf_op jit(solution)/shard_map/ppermute | solution.py:640
  10.7 20.6 %collective-permute-start.4 = (f32[8,4,24,256]{3,2,1,0:T(8,128)S(1)}, f32[8,4,24,256]{3,2,1,0:T(8,128)S(1)}, u32[]{:S(2)}, u32[]{:S(2)}) collective-permute-start(f32[8,4,24,256]{3,2,1,0:T(8,128)S(1)} %add_add_fusion.refs_4_), channel_id=1, source_target_pairs={{0,8},{8,0},{16,24},{24,16},{1,9},{9,1},{17,25},{25,17},{2,10},{10... | collective-permute-start | bytes 2359304 | tf_op jit(solution)/shard_map/ppermute | solution.py:615
  10.8 20.5 %collective-permute-start.5 = (f32[8,4,24,256]{3,2,1,0:T(8,128)S(1)}, f32[8,4,24,256]{3,2,1,0:T(8,128)S(1)}, u32[]{:S(2)}, u32[]{:S(2)}) collective-permute-start(f32[8,4,24,256]{3,2,1,0:T(8,128)S(1)} %add_add_fusion.refs_4_), channel_id=1, source_target_pairs={{0,16},{8,24},{16,0},{24,8},{1,17},{9,25},{17,1},{25,9},{2,18},{10... | collective-permute-start | bytes 2359304 | tf_op jit(solution)/shard_map/ppermute | solution.py:615
  13.3 10.2 %copy-start.3 = (s32[4,2048]{1,0:T(4,128)S(1)}, s32[4,2048]{1,0:T(4,128)}, u32[]{:S(2)}) copy-start(s32[4,2048]{1,0:T(4,128)} %obs_index.1) | copy-start | bytes 98308
  13.3 10.2 %copy-start.4 = (f32[4,2048]{1,0:T(4,128)S(1)}, f32[4,2048]{1,0:T(4,128)}, u32[]{:S(2)}) copy-start(f32[4,2048]{1,0:T(4,128)} %observed.1) | copy-start | bytes 98308
  13.4 10.2 %copy-start.5 = (f32[4,2048]{1,0:T(4,128)S(1)}, f32[4,2048]{1,0:T(4,128)}, u32[]{:S(2)}) copy-start(f32[4,2048]{1,0:T(4,128)} %obs_var.1) | copy-start | bytes 98308
  13.4 10.2 %copy-start.6 = (s32[4]{0:T(128)S(1)}, s32[4]{0:T(128)}, u32[]{:S(2)}) copy-start(s32[4]{0:T(128)} %owner.5) | copy-start | bytes 52
  17.8 8.7 %collective-permute-start.2 = (f32[4,48,256]{2,1,0:T(8,128)S(1)}, f32[4,48,256]{2,1,0:T(8,128)S(1)}, u32[]{:S(2)}, u32[]{:S(2)}) collective-permute-start(f32[4,48,256]{2,1,0:T(8,128)S(1)} %get-tuple-element.45), channel_id=1, source_target_pairs={{0,1},{1,2},{2,3},{3,4},{4,5},{5,6},{6,7},{8,9},{9,10},{10,11},{11... | collective-permute-start | bytes 589832 | tf_op jit(solution)/shard_map/ppermute | solution.py:640
  22.2 9.1 %collective-permute-start.3 = (f32[4,48,256]{2,1,0:T(8,128)S(1)}, f32[4,48,256]{2,1,0:T(8,128)S(1)}, u32[]{:S(2)}, u32[]{:S(2)}) collective-permute-start(f32[4,48,256]{2,1,0:T(8,128)S(1)} %get-tuple-element.46), channel_id=1, source_target_pairs={{1,0},{2,1},{3,2},{4,3},{5,4},{6,5},{7,6},{9,8},{10,9},{11,10},{12... | collective-permute-start | bytes 589832 | tf_op jit(solution)/shard_map/ppermute | solution.py:640
  34.1 15.8 %collective-permute-start.7 = (f32[6,4,24,256]{3,2,1,0:T(8,128)S(1)}, f32[6,4,24,256]{3,2,1,0:T(8,128)S(1)}, u32[]{:S(2)}, u32[]{:S(2)}) collective-permute-start(f32[6,4,24,256]{3,2,1,0:T(8,128)S(1)} %get-tuple-element.47.refs_0_.refs_12_), channel_id=1, source_target_pairs={{0,16},{8,24},{16,0},{24,8},{1,17},{9,25},{17,1},{25,9},{2,18},{10... | collective-permute-start | bytes 1769480 | tf_op jit(solution)/shard_map/ppermute | solution.py:615
  35.7 7.7 %collective-permute-start.8 = (f32[4,48,256]{2,1,0:T(8,128)S(1)}, f32[4,48,256]{2,1,0:T(8,128)S(1)}, u32[]{:S(2)}, u32[]{:S(2)}) collective-permute-start(f32[4,48,256]{2,1,0:T(8,128)S(1)} %get-tuple-element.50), channel_id=1, source_target_pairs={{0,1},{1,2},{2,3},{3,4},{4,5},{5,6},{6,7},{8,9},{9,10},{10,11},{11... | collective-permute-start | bytes 589832 | tf_op jit(solution)/shard_map/ppermute | solution.py:640
  40.2 9.0 %collective-permute-start.9 = (f32[4,48,256]{2,1,0:T(8,128)S(1)}, f32[4,48,256]{2,1,0:T(8,128)S(1)}, u32[]{:S(2)}, u32[]{:S(2)}) collective-permute-start(f32[4,48,256]{2,1,0:T(8,128)S(1)} %get-tuple-element.51), channel_id=1, source_target_pairs={{1,0},{2,1},{3,2},{4,3},{5,4},{6,5},{7,6},{9,8},{10,9},{11,10},{12... | collective-permute-start | bytes 589832 | tf_op jit(solution)/shard_map/ppermute | solution.py:640
  41.7 8.8 %collective-permute-start.17 = (f32[8,4,24,256]{3,2,1,0:T(8,128)S(1)}, f32[8,4,24,256]{3,2,1,0:T(8,128)S(1)}, u32[]{:S(2)}, u32[]{:S(2)}) collective-permute-start(f32[8,4,24,256]{3,2,1,0:T(8,128)S(1)} %get-tuple-element.62.refs_8_), channel_id=1, source_target_pairs={{0,8},{8,0},{16,24},{24,16},{1,9},{9,1},{17,25},{25,17},{2,10},{10... | collective-permute-start | bytes 2359304 | tf_op jit(solution)/shard_map/ppermute | solution.py:615
  49.3 2.4 %collective-permute-start.16 = (f32[8,4,24,256]{3,2,1,0:T(8,128)S(1)}, f32[8,4,24,256]{3,2,1,0:T(8,128)S(1)}, u32[]{:S(2)}, u32[]{:S(2)}) collective-permute-start(f32[8,4,24,256]{3,2,1,0:T(8,128)S(1)} %collective-permute-done.5.refs_14_.refs_6_), channel_id=1, source_target_pairs={{0,8},{8,0},{16,24},{24,16},{1,9},{9,1},{17,25},{25,17},{2,10},{10... | collective-permute-start | bytes 2359304 | tf_op jit(solution)/shard_map/ppermute | solution.py:615
  49.4 3.1 %collective-permute-start.6 = (f32[6,4,24,256]{3,2,1,0:T(8,128)S(1)}, f32[6,4,24,256]{3,2,1,0:T(8,128)S(1)}, u32[]{:S(2)}, u32[]{:S(2)}) collective-permute-start(f32[6,4,24,256]{3,2,1,0:T(8,128)S(1)} %get-tuple-element.47.refs_0_.refs_12_), channel_id=1, source_target_pairs={{0,8},{8,0},{16,24},{24,16},{1,9},{9,1},{17,25},{25,17},{2,10},{10... | collective-permute-start | bytes 1769480 | tf_op jit(solution)/shard_map/ppermute | solution.py:615
  49.9 3.5 %collective-permute-start.10 = (f32[6,4,24,256]{3,2,1,0:T(8,128)S(1)}, f32[6,4,24,256]{3,2,1,0:T(8,128)S(1)}, u32[]{:S(2)}, u32[]{:S(2)}) collective-permute-start(f32[6,4,24,256]{3,2,1,0:T(8,128)S(1)} %collective-permute-done.7.refs_2_.refs_14_), channel_id=1, source_target_pairs={{0,8},{8,0},{16,24},{24,16},{1,9},{9,1},{17,25},{25,17},{2,10},{10... | collective-permute-start | bytes 1769480 | tf_op jit(solution)/shard_map/ppermute | solution.py:615
  50.0 7.3 %collective-permute-start.12 = (f32[2,4,24,256]{3,2,1,0:T(8,128)S(1)}, f32[2,4,24,256]{3,2,1,0:T(8,128)S(1)}, u32[]{:S(2)}, u32[]{:S(2)}) collective-permute-start(f32[2,4,24,256]{3,2,1,0:T(8,128)S(1)} %get-tuple-element.52.refs_1_.refs_16_), channel_id=1, source_target_pairs={{0,16},{8,24},{16,0},{24,8},{1,17},{9,25},{17,1},{25,9},{2,18},{10... | collective-permute-start | bytes 589832 | tf_op jit(solution)/shard_map/ppermute | solution.py:615
  52.2 18.5 %collective-permute-start.18 = (f32[8,4,24,256]{3,2,1,0:T(8,128)S(1)}, f32[8,4,24,256]{3,2,1,0:T(8,128)S(1)}, u32[]{:S(2)}, u32[]{:S(2)}) collective-permute-start(f32[8,4,24,256]{3,2,1,0:T(8,128)S(1)} %last_free.1.refs_0_), channel_id=1, source_target_pairs={{0,8},{8,0},{16,24},{24,16},{1,9},{9,1},{17,25},{25,17},{2,10},{10... | collective-permute-start | bytes 2359304 | tf_op jit(solution)/shard_map/ppermute | solution.py:615
  57.2 20.5 %collective-permute-start.21 = (f32[8,4,24,256]{3,2,1,0:T(8,128)S(1)}, f32[8,4,24,256]{3,2,1,0:T(8,128)S(1)}, u32[]{:S(2)}, u32[]{:S(2)}) collective-permute-start(f32[8,4,24,256]{3,2,1,0:T(8,128)S(1)} %get-tuple-element.62.refs_8_), channel_id=1, source_target_pairs={{0,16},{8,24},{16,0},{24,8},{1,17},{9,25},{17,1},{25,9},{2,18},{10... | collective-permute-start | bytes 2359304 | tf_op jit(solution)/shard_map/ppermute | solution.py:615
  57.7 1.4 %collective-permute-start.11 = (f32[2,4,24,256]{3,2,1,0:T(8,128)S(1)}, f32[2,4,24,256]{3,2,1,0:T(8,128)S(1)}, u32[]{:S(2)}, u32[]{:S(2)}) collective-permute-start(f32[2,4,24,256]{3,2,1,0:T(8,128)S(1)} %get-tuple-element.52.refs_1_.refs_16_), channel_id=1, source_target_pairs={{0,8},{8,0},{16,24},{24,16},{1,9},{9,1},{17,25},{25,17},{2,10},{10... | collective-permute-start | bytes 589832 | tf_op jit(solution)/shard_map/ppermute | solution.py:615
  57.7 1.7 %collective-permute-start.13 = (f32[2,4,24,256]{3,2,1,0:T(8,128)S(1)}, f32[2,4,24,256]{3,2,1,0:T(8,128)S(1)}, u32[]{:S(2)}, u32[]{:S(2)}) collective-permute-start(f32[2,4,24,256]{3,2,1,0:T(8,128)S(1)} %collective-permute-done.12.refs_3_.refs_18_), channel_id=1, source_target_pairs={{0,8},{8,0},{16,24},{24,16},{1,9},{9,1},{17,25},{25,17},{2,10},{10... | collective-permute-start | bytes 589832 | tf_op jit(solution)/shard_map/ppermute | solution.py:615
  61.0 4.2 %collective-permute-start.14 = (f32[96,128]{1,0:T(8,128)S(1)}, f32[96,128]{1,0:T(8,128)S(1)}, u32[]{:S(2)}, u32[]{:S(2)}) collective-permute-start(f32[96,128]{1,0:T(8,128)S(1)} %gram.3), channel_id=1, source_target_pairs={{0,1},{1,0},{2,3},{3,2},{4,5},{5,4},{6,7},{7,6},{8,9},{9,8},{10,11... | collective-permute-start | bytes 147464 | tf_op jit(solution)/shard_map/ppermute | solution.py:615
  65.1 5.6 %collective-permute-start.15 = (f32[96,128]{1,0:T(8,128)S(1)}, f32[96,128]{1,0:T(8,128)S(1)}, u32[]{:S(2)}, u32[]{:S(2)}) collective-permute-start(f32[96,128]{1,0:T(8,128)S(1)} %add.17), channel_id=1, source_target_pairs={{0,2},{1,3},{2,0},{3,1},{4,6},{5,7},{6,4},{7,5},{8,10},{9,11},{10,... | collective-permute-start | bytes 147464 | tf_op jit(solution)/shard_map/ppermute | solution.py:615
  70.7 5.7 %collective-permute-start.19 = (f32[96,128]{1,0:T(8,128)S(1)}, f32[96,128]{1,0:T(8,128)S(1)}, u32[]{:S(2)}, u32[]{:S(2)}) collective-permute-start(f32[96,128]{1,0:T(8,128)S(1)} %add.18), channel_id=1, source_target_pairs={{0,4},{1,5},{2,6},{3,7},{4,0},{5,1},{6,2},{7,3},{8,12},{9,13},{10,... | collective-permute-start | bytes 147464 | tf_op jit(solution)/shard_map/ppermute | solution.py:615
  76.5 1.3 %collective-permute-start.20 = (f32[96,128]{1,0:T(8,128)S(1)}, f32[96,128]{1,0:T(8,128)S(1)}, u32[]{:S(2)}, u32[]{:S(2)}) collective-permute-start(f32[96,128]{1,0:T(8,128)S(1)} %add.19.mine), channel_id=1, source_target_pairs={{0,8},{8,0},{16,24},{24,16},{1,9},{9,1},{17,25},{25,17},{2,10},{10... | collective-permute-start | bytes 147464 | tf_op jit(solution)/shard_map/ppermute | solution.py:615
  77.7 19.6 %collective-permute-start.22 = (f32[8,4,24,256]{3,2,1,0:T(8,128)S(1)}, f32[8,4,24,256]{3,2,1,0:T(8,128)S(1)}, u32[]{:S(2)}, u32[]{:S(2)}) collective-permute-start(f32[8,4,24,256]{3,2,1,0:T(8,128)S(1)} %last_free.1.refs_0_), channel_id=1, source_target_pairs={{0,16},{8,24},{16,0},{24,8},{1,17},{9,25},{17,1},{25,9},{2,18},{10... | collective-permute-start | bytes 2359304 | tf_op jit(solution)/shard_map/ppermute | solution.py:615
  78.8 24.6 %collective-permute-start.24 = (f32[8,4,24,256]{3,2,1,0:T(8,128)S(1)}, f32[8,4,24,256]{3,2,1,0:T(8,128)S(1)}, u32[]{:S(2)}, u32[]{:S(2)}) collective-permute-start(f32[8,4,24,256]{3,2,1,0:T(8,128)S(1)} %collective-permute-done.21.refs_10_), channel_id=1, source_target_pairs={{0,8},{8,0},{16,24},{24,16},{1,9},{9,1},{17,25},{25,17},{2,10},{10... | collective-permute-start | bytes 2359304 | tf_op jit(solution)/shard_map/ppermute | solution.py:615
  97.4 6.1 %collective-permute-start.23 = (f32[8,4,24,256]{3,2,1,0:T(8,128)S(1)}, f32[8,4,24,256]{3,2,1,0:T(8,128)S(1)}, u32[]{:S(2)}, u32[]{:S(2)}) collective-permute-start(f32[8,4,24,256]{3,2,1,0:T(8,128)S(1)} %collective-permute-done.22.refs_2_), channel_id=1, source_target_pairs={{0,8},{8,0},{16,24},{24,16},{1,9},{9,1},{17,25},{25,17},{2,10},{10... | collective-permute-start | bytes 2359304 | tf_op jit(solution)/shard_map/ppermute | solution.py:615
